TPU v7x, 512 devices: a whole 4x8x8 slice. The times are simulated.
512 devices in a mesh: dp: 32 (over x, z_lo, core), mp: 16 (over z_hi, y).
Axes of the slice: x: 4, y: 8, z: 8 (z_hi: 2, z_lo: 4; z = z_hi * 4 + z_lo), core: 2. Of those that a mesh axis runs over, the one named last changes fastest.
Arguments:
- inputs: bfloat16 [2, 4096, 8192], P(None, 'dp'), may hold values from -100 to 100, as said below
- weight: bfloat16 [8192, 4096], P('dp', 'mp'), may hold values from -0.0625 to 0.0625
Outputs:
- weight_gradient: float32 [8192, 4096], P('dp', 'mp')
Inputs may be any that keep to these rules, and one draw needn't show every extreme that they name: `inputs`: bfloat16 activations of two views of the same images.
All inputs are finite; a program needn't handle non-finite values.
Results may differ from a plain program's by a relative error of at most 0.0075.
Values may be sent and summed in bfloat16 or wider, within the bound.
No kernel may reach another device: no remote copies, remote signals or barrier semaphores. Data moves between devices by JAX's collectives and lax.ppermute only.
A program may use at most 64 MiB of HBM per device.

v0:
```python
import jax
import jax.numpy as jnp
from jax import lax
from jax.sharding import PartitionSpec as P

epsilon = 1e-05
redundancy_weight = 0.0051
loss_scale = 512.0


def per_device(inputs, weight):
    views, images, width = inputs.shape
    data_count = lax.axis_size("dp")
    total = images * data_count
    data_index = lax.axis_index("dp")
    model_index = lax.axis_index("mp")
    local_feat = weight.shape[1]
    block_feat = local_feat // data_count
    input_column_block = lax.all_to_all(inputs, "dp", split_axis=2, concat_axis=1, tiled=True)
    projected = jnp.einsum(
        "vbk,ke->vbe",
        inputs,
        lax.all_gather(weight, "dp", axis=0, tiled=True),
        preferred_element_type=jnp.float32,
    )
    average = lax.psum(jnp.sum(projected, axis=1), "dp") / total
    centered = projected - average[:, None, :]
    variance = lax.psum(jnp.sum(centered * centered, axis=1), "dp") / total
    inverse = lax.rsqrt(variance + epsilon)
    normed = (centered * inverse[:, None, :]).astype(jnp.bfloat16)
    gathered_a = lax.all_gather(normed[0].T, "dp", axis=1, tiled=True)
    split_b = lax.all_to_all(normed[1].T, "dp", split_axis=0, concat_axis=1, tiled=True)
    columns_b = lax.all_gather(split_b, "mp", axis=0, tiled=True)
    correlation = (
        lax.dot_general(
            gathered_a, columns_b, (((1,), (1,)), ((), ())), preferred_element_type=jnp.float32
        )
        / total
    )
    row_ids = model_index * local_feat + lax.broadcasted_iota(jnp.int32, (local_feat, 1), 0)
    col_local = lax.broadcasted_iota(jnp.int32, (1, columns_b.shape[0]), 1)
    col_ids = (
        col_local // block_feat * local_feat + data_index * block_feat + col_local % block_feat
    )
    diagonal = (row_ids == col_ids).astype(jnp.float32)
    grad_corr = (
        loss_scale
        * (
            2.0 * redundancy_weight * correlation
            + diagonal * (2.0 * (correlation - 1.0) - 2.0 * redundancy_weight * correlation)
        )
    ).astype(jnp.bfloat16)
    reduced_b = lax.psum_scatter(
        (
            lax.dot_general(
                grad_corr, gathered_a, (((0,), (0,)), ((), ())), preferred_element_type=jnp.float32
            )
            / total
        ).astype(jnp.bfloat16),
        "mp",
        scatter_dimension=0,
        tiled=True,
    ).astype(jnp.float32)
    own_b = lax.all_to_all(reduced_b, "dp", split_axis=1, concat_axis=0, tiled=True).T
    own_a = lax.psum_scatter(
        (
            lax.dot_general(
                columns_b, grad_corr, (((0,), (1,)), ((), ())), preferred_element_type=jnp.float32
            )
            / total
        ).astype(jnp.bfloat16),
        "dp",
        scatter_dimension=0,
        tiled=True,
    ).astype(jnp.float32)
    grads = jnp.stack([own_a, own_b])
    normalized_wide_rows = normed.astype(jnp.float32)
    sum_grad, sum_cross = lax.psum(
        (jnp.sum(grads, axis=1), jnp.sum(grads * normalized_wide_rows, axis=1)), "dp"
    )
    grad_proj = (
        (
            grads
            - sum_grad[:, None, :] / total
            - normalized_wide_rows * (sum_cross[:, None, :] / total)
        )
        * inverse[:, None, :]
    ).astype(jnp.bfloat16)
    complete_gradients = lax.all_gather(grad_proj, "dp", axis=1, tiled=True)
    return jnp.einsum(
        "fju,fjh->uh", input_column_block, complete_gradients, preferred_element_type=jnp.float32
    )


def solution(mesh):
    placed = (P(None, "dp", None), P("dp", "mp"))
    return jax.shard_map(
        per_device, mesh=mesh, in_specs=placed, out_specs=P("dp", "mp"), check_vma=False
    )
```

profile of v0, /device:TPU:1, one launch (start us, length us, event | category | flops | bytes accessed | tf_op | source)
XLA Modules:
  0.0 915.2 jit_solution(3237158250383194473)
XLA Ops:
  6.5 0.7 all-gather.5.cloned.1.call-update
  7.3 74.1 %all-gather.5.cloned.1.call-done = bf16[8192,256]{1,0:T(8,128)(2,1)} async-done(((bf16[256,256]{1,0:T(8,128)(2,1)}), bf16[8192,256]{1,0:T(8,128)(2,1)}) %all-gather.5.cloned.1.call-update) | async-done | bytes 4194320 | tf_op jit(solution)/shard_map/all_gather | solution.py:23
  81.4 4.7 fusion.42
  86.1 67.0 %psum.28 = f32[2,256]{1,0:T(2,128)S(1)} all-reduce(f32[2,256]{1,0:T(2,128)S(1)} %get-tuple-element.11), channel_id=1, replica_groups=mesh['dp'=32,'mp'=16] {'dp'}, use_global_device_ids=true, to_apply=%region_1.0 | all-reduce | flops 512 | bytes 4096 | tf_op jit(solution)/shard_map/psum | solution.py:26
  153.2 70.1 %psum.29 = f32[2,256]{1,0:T(2,128)S(1)} all-reduce(f32[2,256]{1,0:T(2,128)S(1)} %multiply_reduce_fusion), channel_id=1, replica_groups=mesh['dp'=32,'mp'=16] {'dp'}, use_global_device_ids=true, to_apply=%region_3.0 | all-reduce | flops 512 | bytes 4096 | tf_op jit(solution)/shard_map/psum | solution.py:28
  224.2 11.9 %all_to_all.60 = bf16[32,8,128]{2,1,0:T(8,128)(2,1)} all-to-all(bf16[32,8,128]{2,1,0:T(8,128)(2,1)S(1)} %bitcast.49), channel_id=1, replica_groups=mesh['dp'=32,'mp'=16] {'dp'}, dimensions={0} | all-to-all | bytes 131072 | tf_op jit(solution)/shard_map/all_to_all | solution.py:32
  236.9 86.3 %all-gather.7.cloned.1.call-done = bf16[128,4096]{1,0:T(8,128)(2,1)} async-done(((bf16[8,4096]{1,0:T(8,128)(2,1)}), bf16[128,4096]{1,0:T(8,128)(2,1)}) %all-gather.7.cloned.1.call-update) | async-done | bytes 1048592 | tf_op jit(solution)/shard_map/all_gather | solution.py:33
  323.2 63.5 %all-gather.9.cloned.1.call-done = bf16[256,4096]{0,1:T(8,128)(2,1)} async-done(((bf16[256,128]{0,1:T(8,128)(2,1)}), bf16[256,4096]{0,1:T(8,128)(2,1)}) %all-gather.9.cloned.1.call-update) | async-done | bytes 2097168 | tf_op jit(solution)/shard_map/all_gather | solution.py:31
  386.6 2.6 fusion.43
  389.2 3.5 fusion.1
  392.8 2.2 fusion
  395.0 212.7 %reduce-scatter.5.cloned.1.call-done = bf16[8,4096]{1,0:T(8,128)(2,1)} async-done(((bf16[128,4096]{1,0:T(8,128)(2,1)}), bf16[8,4096]{1,0:T(8,128)(2,1)}) %reduce-scatter.5.cloned.1.call-update) | async-done | bytes 65552 | tf_op jit(solution)/shard_map/reduce_scatter | solution.py:53
  607.7 1.5 bitcast_convert_fusion
  609.2 10.5 %all-to-all-start.1 = ((f32[8,32,128]{2,0,1:T(8,128)}), f32[8,32,128]{2,0,1:T(8,128)S(1)}, u32[]{:S(2)}, u32[]{:S(2)}) async-start(f32[8,32,128]{2,0,1:T(8,128)} %bitcast_convert_fusion), calls=%async_computation.3 | async-start | bytes 262144 | tf_op jit(solution)/shard_map/all_to_all | solution.py:64
  619.7 11.2 %copy.14 = bf16[2,128,8192]{1,0,2:T(2,128)(2,1)} copy(bf16[2,128,8192]{2,1,0:T(8,128)(2,1)} %param.2) | data formatting | bytes 8388608 | tf_op args[0]
  630.9 7.7 all-to-all-start.2
  638.8 124.3 %reduce-scatter.3.cloned.1.call-done = bf16[128,256]{1,0:T(8,128)(2,1)} async-done(((bf16[4096,256]{1,0:T(8,128)(2,1)}), bf16[128,256]{1,0:T(8,128)(2,1)}) %reduce-scatter.3.cloned.1.call-update) | async-done | bytes 65552 | tf_op jit(solution)/shard_map/reduce_scatter | solution.py:65
  763.1 0.8 bitcast_convert_fusion.1
  764.1 72.8 %all-reduce = (f32[2,256]{1,0:T(2,128)S(1)}, f32[2,256]{1,0:T(2,128)S(1)}) all-reduce(f32[2,256]{1,0:T(2,128)S(1)} %get-tuple-element.6, f32[2,256]{1,0:T(2,128)S(1)} %get-tuple-element.5), channel_id=1, replica_groups=mesh['dp'=32,'mp'=16] {'dp'}, use_global_device_ids=true, to_apply=%region_9.10 | all-reduce | flops 1024 | bytes 8192 | tf_op jit(solution)/shard_map/psum | solution.py:78
  836.9 0.7 fusion.7
  837.6 11.2 %copy.15 = bf16[2,128,32,256]{3,1,2,0:T(8,128)(2,1)} copy(bf16[2,128,32,256]{1,0,3,2:T(2,128)(2,1)} %bitcast.14) | data formatting | bytes 8388608 | tf_op jit(solution)/shard_map/all_to_all | solution.py:19
  848.8 54.0 %all-gather.11.cloned.1.call-done = bf16[2,4096,256]{2,1,0:T(8,128)(2,1)} async-done(((bf16[2,128,256]{2,1,0:T(8,128)(2,1)}), bf16[2,4096,256]{2,1,0:T(8,128)(2,1)}) %all-gather.11.cloned.1.call-update) | async-done | bytes 4194320 | tf_op jit(solution)/shard_map/all_gather | solution.py:89
  902.8 4.7 convolution_bitcast_fusion
  907.5 0.8 copy.17
  (26 shorter events, 2.0 us)
Async XLA Ops:
  6.5 74.9 %all-gather.5.cloned.1.call-start = ((), (), s32[]{:S(2)}) async-start(), calls=%async_computation.5 | async-start | bytes 4325376 | tf_op jit(solution)/shard_map/all_gather | solution.py:23
  7.3 315.9 %all-gather.7.cloned.1.call-start = ((), (), s32[]{:S(2)}) async-start(), calls=%async_computation.6 | async-start | bytes 1114112 | tf_op jit(solution)/shard_map/all_gather | solution.py:33
  236.0 150.6 %all-gather.9.cloned.1.call-start = ((), (), s32[]{:S(2)}) async-start(), calls=%async_computation.7 | async-start | bytes 2162688 | tf_op jit(solution)/shard_map/all_gather | solution.py:31
  236.8 371.0 %reduce-scatter.5.cloned.1.call-start = ((), (), s32[]{:S(2)}) async-start(), calls=%async_computation.9 | async-start | bytes 1114112 | tf_op jit(solution)/shard_map/reduce_scatter | solution.py:53
  323.2 69.6 %copy-start = (bf16[128,4096]{1,0:T(8,128)(2,1)S(1)}, bf16[128,4096]{1,0:T(8,128)(2,1)}, u32[]{:S(2)}) copy-start(bf16[128,4096]{1,0:T(8,128)(2,1)} %all-gather.7.cloned.1.call-done) | copy-start | bytes 3145732
  392.7 370.4 %reduce-scatter.3.cloned.1.call-start = ((), (), s32[]{:S(2)}) async-start(), calls=%async_computation.8 | async-start | bytes 2162688 | tf_op jit(solution)/shard_map/reduce_scatter | solution.py:65
  609.2 21.7 %all-to-all-start.1 = ((f32[8,32,128]{2,0,1:T(8,128)}), f32[8,32,128]{2,0,1:T(8,128)S(1)}, u32[]{:S(2)}, u32[]{:S(2)}) async-start(f32[8,32,128]{2,0,1:T(8,128)} %bitcast_convert_fusion), calls=%async_computation.3 | async-start | bytes 262144 | tf_op jit(solution)/shard_map/all_to_all | solution.py:64
  630.9 206.7 %all-to-all-start.2 = ((bf16[2,128,8192]{1,0,2:T(2,128)(2,1)}), bf16[2,128,8192]{1,0,2:T(2,128)(2,1)}, u32[]{:S(2)}, u32[]{:S(2)}) async-start(bf16[2,128,8192]{1,0,2:T(2,128)(2,1)} %copy.14), calls=%async_computation.4 | async-start | bytes 8388608 | tf_op jit(solution)/shard_map/all_to_all | solution.py:19
  638.7 264.1 %all-gather.11.cloned.1.call-start = ((), (), s32[]{:S(2)}) async-start(), calls=%async_computation.10 | async-start | bytes 4325376 | tf_op jit(solution)/shard_map/all_gather | solution.py:89
Sparse Core Ops, SparseCore 0:
  9.5 71.8 all-gather.4
  236.2 86.9 all-gather.6
  325.3 61.2 all-gather.8
  392.9 214.8 reduce-scatter.4
  610.6 152.4 reduce-scatter.2
  837.7 65.0 all-gather.10
where the time goes:
time: 916 us; the launch traced here: 915 us
  waiting for transfers between devices  616 us (67%)
  blocking collectives  222 us (24%)
  local copies, waits for them, and re-layouts  24 us (3%)
  starting transfers between devices  18.4 us (2%)
  matrix products  17.7 us (2%)
  between operations  13.6 us (1%)
    reduce_scatter x1, waiting for transfers between devices, per_device(): lax.psum_scatter((lax.dot_general(grad_corr, gathered_a, (((0,), (0,)), (...  213 us
    reduce_scatter x1, waiting for transfers between devices, per_device(): lax.psum_scatter((lax.dot_general(columns_b, grad_corr, (((0,), (1,)), ((...  124 us
    all_gather x1, waiting for transfers between devices, per_device(): columns_b = lax.all_gather(split_b, 'mp', axis=0, tiled=True)  86.3 us
    all_gather x1, waiting for transfers between devices, per_device(): lax.all_gather(weight, 'dp', axis=0, tiled=True)  74.1 us
    psum x1, blocking collectives, per_device(): lax.psum((jnp.sum(grads, axis=1), jnp.sum(grads * normalized_wide_rows, a...  72.8 us
    psum x1, blocking collectives, per_device(): variance = lax.psum(jnp.sum(centered * centered, axis=1), 'dp') / total  70.1 us
    psum x1, blocking collectives, per_device(): average = lax.psum(jnp.sum(projected, axis=1), 'dp') / total  67 us
    all_gather x1, waiting for transfers between devices, per_device(): gathered_a = lax.all_gather(normed[0].T, 'dp', axis=1, tiled=True)  63.5 us
  transfers between devices with their start and end apart: 8, of which 6 were waited for; matrix products, arithmetic and copies ran while one was open for 3% of the time, Pallas kernels for 0%

commit v1 on v0

v1 whole, which is shorter than its diff:
```python
import jax
import jax.numpy as jnp
from jax import lax
from jax.sharding import PartitionSpec as P

epsilon = 1e-05
redundancy_weight = 0.0051
loss_scale = 512.0


def spread(block, axis, count):
    copies = jnp.broadcast_to(block[None], (count,) + block.shape)
    return lax.all_to_all(copies, axis, split_axis=0, concat_axis=0)


def per_device(inputs, weight):
    views, images, width = inputs.shape
    dp = lax.axis_size("dp")
    mp = lax.axis_size("mp")
    total = images * dp
    data_index = lax.axis_index("dp")
    feat = weight.shape[1]
    block = feat // dp
    rows = width // dp

    pieces = inputs.reshape(views, images, dp, rows).transpose(2, 0, 1, 3)
    columns = lax.all_to_all(pieces, "dp", split_axis=0, concat_axis=0)

    full_weight = lax.all_gather(weight, "dp", axis=0, tiled=True)
    projected = lax.dot_general(
        full_weight,
        inputs.reshape(views * images, width),
        (((0,), (1,)), ((), ())),
        preferred_element_type=jnp.float32,
    )
    own = lax.all_to_all(
        projected.reshape(dp, block, views * images), "dp", split_axis=0, concat_axis=0
    ).reshape(dp, block, views, images)
    average = jnp.sum(own, axis=(0, 3), keepdims=True) / total
    centered = own - average
    variance = jnp.sum(centered * centered, axis=(0, 3), keepdims=True) / total
    inverse = lax.rsqrt(variance + epsilon)
    normed = (centered * inverse).astype(jnp.bfloat16)
    first = normed[:, :, 0].transpose(1, 0, 2).reshape(block, total)
    second = normed[:, :, 1].transpose(1, 0, 2).reshape(block, total)

    rows_a = lax.all_gather(first, "dp", axis=0, tiled=True)
    columns_b = spread(second, "mp", mp).reshape(mp * block, total)
    correlation = (
        lax.dot_general(rows_a, columns_b, (((1,), (1,)), ((), ())), preferred_element_type=jnp.float32)
        / total
    )
    row_ids = lax.broadcasted_iota(jnp.int32, (feat, 1), 0)
    column = lax.broadcasted_iota(jnp.int32, (1, mp * block), 1)
    own_columns = column // block == lax.axis_index("mp")
    diagonal = (own_columns & (row_ids == data_index * block + column % block)).astype(jnp.float32)
    grad_corr = (
        loss_scale
        * (
            2.0 * redundancy_weight * correlation
            + diagonal * (2.0 * (correlation - 1.0) - 2.0 * redundancy_weight * correlation)
        )
    ).astype(jnp.bfloat16)
    terms_b = (
        lax.dot_general(grad_corr, rows_a, (((0,), (0,)), ((), ())), preferred_element_type=jnp.float32)
        / total
    ).astype(jnp.bfloat16)
    terms_a = (
        lax.dot_general(grad_corr, columns_b, (((1,), (0,)), ((), ())), preferred_element_type=jnp.float32)
        / total
    ).astype(jnp.bfloat16)
    terms_a = lax.all_to_all(terms_a.reshape(dp, block, total), "dp", split_axis=0, concat_axis=0)
    terms_b = lax.all_to_all(terms_b.reshape(mp, block, total), "mp", split_axis=0, concat_axis=0)
    grads = jnp.stack(
        [
            jnp.sum(terms.astype(jnp.float32), axis=0).reshape(block, dp, images)
            for terms in (terms_a, terms_b)
        ],
        axis=2,
    )
    wide = normed.transpose(1, 0, 2, 3).astype(jnp.float32)
    grad_mean = jnp.sum(grads, axis=(1, 3), keepdims=True) / total
    cross_mean = jnp.sum(grads * wide, axis=(1, 3), keepdims=True) / total
    grad_proj = (
        (grads - grad_mean - wide * cross_mean) * inverse.transpose(1, 0, 2, 3)
    ).astype(jnp.bfloat16)
    gathered = lax.all_gather(
        grad_proj.reshape(block, dp * views * images), "dp", axis=0, tiled=True
    )
    return lax.dot_general(
        columns.reshape(dp * views * images, rows),
        gathered,
        (((0,), (1,)), ((), ())),
        preferred_element_type=jnp.float32,
    )


def solution(mesh):
    placed = (P(None, "dp", None), P("dp", "mp"))
    return jax.shard_map(
        per_device, mesh=mesh, in_specs=placed, out_specs=P("dp", "mp"), check_vma=False
    )
```

time: 916 us -> 434 us (0.47)
  waiting for transfers between devices: 616 us -> 319 us
  blocking collectives: 222 us -> 16.5 us
  starting transfers between devices: 18.4 us -> 39.8 us
    reduce_scatter x2 -> x0, waiting for transfers between devices: 337 us -> none  [the longest x1 213 us: per_device(): lax.psum_scatter((lax.dot_general(grad_corr, gathered_a, (((0,), (0,)), (...]
    psum x3 -> x0, blocking collectives: 210 us -> none  [the longest x1 72.8 us: per_device(): lax.psum((jnp.sum(grads, axis=1), jnp.sum(grads * normalized_wide_rows, a...]
    all_to_all x2 -> x4, waiting for transfers between devices: 0.01 us -> 208 us  [the longest x1 114 us: per_device(): columns = lax.all_to_all(pieces, 'dp', split_axis=0, concat_axis=0)]
    all_gather x4 -> x3, waiting for transfers between devices: 278 us -> 110 us  [the longest x1 74.1 us: per_device(): full_weight = lax.all_gather(weight, 'dp', axis=0, tiled=True)]
    all_to_all x2 -> x4, starting transfers between devices: 18.2 us -> 39.7 us  [the longest x1 15.5 us: per_device(): lax.all_to_all(terms_b.reshape(mp, block, total), 'mp', split_axis=0, con...]
  transfers between devices with their start and end apart: 8 -> 7, of which waited for: 6 -> 6; matrix products, arithmetic and copies ran while one was open for 3% -> 5% of each run, Pallas kernels for 0% -> 0%
where the time goes in v1:
time: 434 us; the launch traced here: 433 us
  waiting for transfers between devices  319 us (74%)
  starting transfers between devices  39.8 us (9%)
  local copies, waits for them, and re-layouts  27.5 us (6%)
  blocking collectives  16.5 us (4%)
  matrix products  15.5 us (4%)
  between operations  13.2 us (3%)
    all_to_all x1, waiting for transfers between devices, per_device(): columns = lax.all_to_all(pieces, 'dp', split_axis=0, concat_axis=0)  114 us
    all_gather x1, waiting for transfers between devices, per_device(): full_weight = lax.all_gather(weight, 'dp', axis=0, tiled=True)  74.1 us
    all_to_all x1, waiting for transfers between devices, per_device(): lax.all_to_all(terms_a.reshape(dp, block, total), 'dp', split_axis=0, con...  38.6 us
    all_gather x1, waiting for transfers between devices, per_device(): rows_a = lax.all_gather(first, 'dp', axis=0, tiled=True)  36.1 us
    all_to_all x1, waiting for transfers between devices, spread(): return lax.all_to_all(copies, axis, split_axis=0, concat_axis=0)  29.4 us
    all_to_all x1, waiting for transfers between devices, per_device(): lax.all_to_all(terms_b.reshape(mp, block, total), 'mp', split_axis=0, con...  26 us
    all_to_all x1, blocking collectives, per_device(): lax.all_to_all(projected.reshape(dp, block, views * images), 'dp', split_...  16.5 us
    all_to_all x1, starting transfers between devices, per_device(): lax.all_to_all(terms_b.reshape(mp, block, total), 'mp', split_axis=0, con...  15.5 us
  transfers between devices with their start and end apart: 7, of which 6 were waited for; matrix products, arithmetic and copies ran while one was open for 5% of the time, Pallas kernels for 0%

profile of v1, /device:TPU:1, one launch (start us, length us, event | category | flops | bytes accessed | tf_op | source)
XLA Modules:
  0.0 433.2 jit_solution(7139761078906354555)
XLA Ops:
  7.3 74.1 %all-gather.4.cloned.1.call-done = bf16[8192,256]{1,0:T(8,128)(2,1)} async-done(((bf16[256,256]{1,0:T(8,128)(2,1)}), bf16[8192,256]{1,0:T(8,128)(2,1)}) %all-gather.4.cloned.1.call-update) | async-done | bytes 4194320 | tf_op jit(solution)/shard_map/all_gather | solution.py:29
  81.4 6.4 %copy.16 = bf16[256,8192]{1,0:T(8,128)(2,1)} copy(bf16[256,8192]{0,1:T(8,128)(2,1)} %bitcast.71) | data formatting | bytes 8388608 | tf_op jit(solution)/shard_map/dot_general | solution.py:30
  87.8 4.7 %fusion.4 = f32[32,8,256]{2,1,0:T(8,128)S(1)} fusion(bf16[256,8192,1]{1,0,2:T(8,128)(2,1)} %bitcast.69, bf16[256,8192]{1,0:T(8,128)(2,1)} %copy.16), kind=kOutput, calls=%fused_computation.6 | convolution fusion | flops 1073741824 | bytes 8650752 | tf_op jit(solution)/shard_map/dot_general | solution.py:30
  92.6 16.5 %all_to_all.25 = f32[32,8,256]{2,1,0:T(8,128)S(1)} all-to-all(f32[32,8,256]{2,1,0:T(8,128)S(1)} %fusion.4), channel_id=1, replica_groups=mesh['dp'=32,'mp'=16] {'dp'}, dimensions={0} | all-to-all | bytes 524288 | tf_op jit(solution)/shard_map/all_to_all | solution.py:36
  110.2 1.1 broadcast_in_dim.5
  111.3 10.2 %all-to-all-start.1 = ((bf16[16,8,4096]{2,1,0:T(8,128)(2,1)}), bf16[16,8,4096]{2,1,0:T(8,128)(2,1)S(1)}, u32[]{:S(2)}, u32[]{:S(2)}) async-start(bf16[16,8,4096]{2,1,0:T(8,128)(2,1)} %broadcast_in_dim.5), calls=%async_computation.1 | async-start | bytes 2097152 | tf_op jit(solution)/shard_map/all_to_all | solution.py:13
  121.5 29.4 %all-to-all-done.1 = bf16[16,8,4096]{2,1,0:T(8,128)(2,1)S(1)} async-done(((bf16[16,8,4096]{2,1,0:T(8,128)(2,1)}), bf16[16,8,4096]{2,1,0:T(8,128)(2,1)S(1)}, u32[]{:S(2)}, u32[]{:S(2)}) %all-to-all-start.1) | async-done | bytes 1048608 | tf_op jit(solution)/shard_map/all_to_all | solution.py:13
  150.9 36.1 %all-gather.6.cloned.1.call-done = bf16[256,4096]{1,0:T(8,128)(2,1)} async-done(((bf16[8,4096]{1,0:T(8,128)(2,1)}), bf16[256,4096]{1,0:T(8,128)(2,1)}) %all-gather.6.cloned.1.call-update) | async-done | bytes 2097168 | tf_op jit(solution)/shard_map/all_gather | solution.py:47
  187.0 2.4 fusion.7
  189.4 1.5 fusion.3
  190.9 15.5 %all-to-all-start.3 = ((bf16[16,8,4096]{2,1,0:T(8,128)(2,1)}), bf16[16,8,4096]{2,1,0:T(8,128)(2,1)S(1)}, u32[]{:S(2)}, u32[]{:S(2)}) async-start(bf16[16,8,4096]{2,1,0:T(8,128)(2,1)} %fusion.3), calls=%async_computation.3 | async-start | bytes 2097152 | tf_op jit(solution)/shard_map/all_to_all | solution.py:73
  206.5 2.1 fusion.1
  208.6 26.0 %all-to-all-done.3 = bf16[16,8,4096]{2,1,0:T(8,128)(2,1)S(1)} async-done(((bf16[16,8,4096]{2,1,0:T(8,128)(2,1)}), bf16[16,8,4096]{2,1,0:T(8,128)(2,1)S(1)}, u32[]{:S(2)}, u32[]{:S(2)}) %all-to-all-start.3) | async-done | bytes 1048608 | tf_op jit(solution)/shard_map/all_to_all | solution.py:73
  234.6 1.0 copy-done.1
  235.5 8.7 %all-to-all-start.2 = ((bf16[32,8,4096]{2,1,0:T(8,128)(2,1)}), bf16[32,8,4096]{2,1,0:T(8,128)(2,1)S(1)}, u32[]{:S(2)}, u32[]{:S(2)}) async-start(bf16[32,8,4096]{2,1,0:T(8,128)(2,1)} %fusion.1), calls=%async_computation.2 | async-start | bytes 4194304 | tf_op jit(solution)/shard_map/all_to_all | solution.py:72
  244.2 6.4 %copy.17 = bf16[2,128,8192]{1,2,0:T(8,128)(2,1)} copy(bf16[2,128,8192]{2,1,0:T(8,128)(2,1)} %param.2) | data formatting | bytes 8388608 | tf_op args[0]
  250.6 4.7 %copy.18 = bf16[32,2,128,256]{2,3,1,0:T(8,128)(2,1)} copy(bf16[32,2,128,256]{2,3,0,1:T(8,128)(2,1)} %bitcast.70) | data formatting | bytes 8388608 | tf_op jit(solution)/shard_map/transpose | solution.py:26
  255.5 38.6 %all-to-all-done.2 = bf16[32,8,4096]{2,1,0:T(8,128)(2,1)S(1)} async-done(((bf16[32,8,4096]{2,1,0:T(8,128)(2,1)}), bf16[32,8,4096]{2,1,0:T(8,128)(2,1)S(1)}, u32[]{:S(2)}, u32[]{:S(2)}) %all-to-all-start.2) | async-done | bytes 2097184 | tf_op jit(solution)/shard_map/all_to_all | solution.py:72
  294.0 5.3 %all-to-all-start.4 = ((bf16[32,2,128,256]{2,3,1,0:T(8,128)(2,1)}), bf16[32,2,128,256]{2,3,1,0:T(8,128)(2,1)}, u32[]{:S(2)}, u32[]{:S(2)}) async-start(bf16[32,2,128,256]{2,3,1,0:T(8,128)(2,1)} %copy.18), calls=%async_computation.4 | async-start | bytes 8388608 | tf_op jit(solution)/shard_map/all_to_all | solution.py:27
  299.9 0.8 fusion.12
  300.7 114.0 %all-to-all-done.4 = bf16[32,2,128,256]{2,3,1,0:T(8,128)(2,1)} async-done(((bf16[32,2,128,256]{2,3,1,0:T(8,128)(2,1)}), bf16[32,2,128,256]{2,3,1,0:T(8,128)(2,1)}, u32[]{:S(2)}, u32[]{:S(2)}) %all-to-all-start.4) | async-done | bytes 4194336 | tf_op jit(solution)/shard_map/all_to_all | solution.py:27
  414.7 6.4 %copy.19 = bf16[32,2,128,256]{3,2,1,0:T(8,128)(2,1)} copy(bf16[32,2,128,256]{2,3,1,0:T(8,128)(2,1)} %all-to-all-done.4) | data formatting | bytes 8388608 | tf_op jit(solution)/shard_map/all_to_all | solution.py:27
  421.1 4.7 %convolution_bitcast_fusion = f32[256,256]{0,1:T(8,128)S(1)} fusion(bf16[256,8192]{1,0:T(8,128)(2,1)} %all-gather.8.cloned.1.call-done, bf16[8192,256]{1,0:T(8,128)(2,1)} %bitcast.72), kind=kOutput, calls=%fused_computation.10 | convolution fusion | flops 1073741824 | bytes 8650752 | tf_op jit(solution)/shard_map/dot_general | solution.py:90
  425.8 0.8 copy.20
  (27 shorter events, 2.6 us)
Async XLA Ops:
  6.5 74.9 %all-gather.4.cloned.1.call-start = ((), (), s32[]{:S(2)}) async-start(), calls=%async_computation.5 | async-start | bytes 4325376 | tf_op jit(solution)/shard_map/all_gather | solution.py:29
  7.3 179.7 %all-gather.6.cloned.1.call-start = ((), (), s32[]{:S(2)}) async-start(), calls=%async_computation.6 | async-start | bytes 2162688 | tf_op jit(solution)/shard_map/all_gather | solution.py:47
  111.3 39.6 %all-to-all-start.1 = ((bf16[16,8,4096]{2,1,0:T(8,128)(2,1)}), bf16[16,8,4096]{2,1,0:T(8,128)(2,1)S(1)}, u32[]{:S(2)}, u32[]{:S(2)}) async-start(bf16[16,8,4096]{2,1,0:T(8,128)(2,1)} %broadcast_in_dim.5), calls=%async_computation.1 | async-start | bytes 2097152 | tf_op jit(solution)/shard_map/all_to_all | solution.py:13
  187.0 2.5 copy-start
  190.9 43.6 %all-to-all-start.3 = ((bf16[16,8,4096]{2,1,0:T(8,128)(2,1)}), bf16[16,8,4096]{2,1,0:T(8,128)(2,1)S(1)}, u32[]{:S(2)}, u32[]{:S(2)}) async-start(bf16[16,8,4096]{2,1,0:T(8,128)(2,1)} %fusion.3), calls=%async_computation.3 | async-start | bytes 2097152 | tf_op jit(solution)/shard_map/all_to_all | solution.py:73
  234.6 1.0 copy-start.1
  235.5 58.5 %all-to-all-start.2 = ((bf16[32,8,4096]{2,1,0:T(8,128)(2,1)}), bf16[32,8,4096]{2,1,0:T(8,128)(2,1)S(1)}, u32[]{:S(2)}, u32[]{:S(2)}) async-start(bf16[32,8,4096]{2,1,0:T(8,128)(2,1)} %fusion.1), calls=%async_computation.2 | async-start | bytes 4194304 | tf_op jit(solution)/shard_map/all_to_all | solution.py:72
  250.6 4.7 %copy-start.2 = (bf16[16,8,4096]{2,1,0:T(8,128)(2,1)S(1)}, bf16[16,8,4096]{2,1,0:T(8,128)(2,1)}, u32[]{:S(2)}) copy-start(bf16[16,8,4096]{2,1,0:T(8,128)(2,1)} %copy-done.1) | copy-start | bytes 3145732
  294.0 120.7 %all-to-all-start.4 = ((bf16[32,2,128,256]{2,3,1,0:T(8,128)(2,1)}), bf16[32,2,128,256]{2,3,1,0:T(8,128)(2,1)}, u32[]{:S(2)}, u32[]{:S(2)}) async-start(bf16[32,2,128,256]{2,3,1,0:T(8,128)(2,1)} %copy.18), calls=%async_computation.4 | async-start | bytes 8388608 | tf_op jit(solution)/shard_map/all_to_all | solution.py:27
  299.4 121.8 %all-gather.8.cloned.1.call-start = ((), (), s32[]{:S(2)}) async-start(), calls=%async_computation.7 | async-start | bytes 4325376 | tf_op jit(solution)/shard_map/all_gather | solution.py:87
Sparse Core Ops, SparseCore 0:
  9.5 71.8 all-gather.3
  110.3 76.5 all-gather.5
  302.3 104.3 all-gather.7

commit v2 on v1

v2 whole, which is shorter than its diff:
```python
import jax
import jax.numpy as jnp
from jax import lax
from jax.experimental import pallas as pl
from jax.experimental.pallas import tpu as pltpu
from jax.sharding import PartitionSpec as P

epsilon = 1e-05
redundancy_weight = 0.0051
loss_scale = 512.0
DP = 32
MP = 16
Y = 8


def swap(array, step):
    return lax.ppermute(array, "dp", [(i, i ^ step) for i in range(DP)])


def gather_dp(block):
    along_z = jnp.stack([block] + [swap(block, 2 * k) for k in (1, 2, 3)])
    along_x = jnp.stack([along_z] + [swap(along_z, 8 * k) for k in (1, 2, 3)])
    return along_x, swap(along_x, 1)


def add_dp(own, other):
    both = (own + swap(other, 1).astype(jnp.float32)).astype(jnp.bfloat16)
    parts = [both[0]] + [swap(both[k], 8 * k) for k in (1, 2, 3)]
    along_x = sum(part.astype(jnp.float32) for part in parts).astype(jnp.bfloat16)
    parts = [along_x[0]] + [swap(along_x[k], 2 * k) for k in (1, 2, 3)]
    return sum(part.astype(jnp.float32) for part in parts)


def copy_kernel(order_ref, source_ref, out_ref):
    out_ref[...] = source_ref[...]


def take_columns(array, order, width):
    rows, columns = array.shape
    return pl.pallas_call(
        copy_kernel,
        grid_spec=pltpu.PrefetchScalarGridSpec(
            num_scalar_prefetch=1,
            grid=(columns // width,),
            in_specs=[pl.BlockSpec((rows, width), lambda k, order: (0, order[k]))],
            out_specs=pl.BlockSpec((rows, width), lambda k, order: (0, k)),
        ),
        out_shape=jax.ShapeDtypeStruct(array.shape, array.dtype),
    )(order, array)


def weight_kernel(order_ref, own_ref, other_ref, columns_ref, out_ref, total_ref, placed_ref):
    step = pl.program_id(0)
    half = own_ref.shape[0]

    @pl.when(step == 0)
    def _():
        total_ref[...] = jnp.zeros_like(total_ref)

    total_ref[:half] += jnp.dot(own_ref[...], columns_ref[...], preferred_element_type=jnp.float32)
    total_ref[half:] += jnp.dot(other_ref[...], columns_ref[...], preferred_element_type=jnp.float32)

    @pl.when(step == pl.num_programs(0) - 1)
    def _():
        for block in range(DP):
            start = pl.multiple_of(order_ref[block] * 8, 8)
            placed_ref[block * 8 : block * 8 + 8] = total_ref[pl.ds(start, 8)]
        out_ref[...] = placed_ref[...].T


def weight_gradient(order, own, other, columns):
    depth, rows = columns.shape
    half = own.shape[0]
    tile = 1024
    return pl.pallas_call(
        weight_kernel,
        grid_spec=pltpu.PrefetchScalarGridSpec(
            num_scalar_prefetch=1,
            grid=(depth // tile,),
            in_specs=[
                pl.BlockSpec((half, tile), lambda k, order: (0, k)),
                pl.BlockSpec((half, tile), lambda k, order: (0, k)),
                pl.BlockSpec((tile, rows), lambda k, order: (k, 0)),
            ],
            out_specs=pl.BlockSpec((rows, 2 * half), lambda k, order: (0, 0)),
            scratch_shapes=[
                pltpu.VMEM((2 * half, rows), jnp.float32),
                pltpu.VMEM((2 * half, rows), jnp.float32),
            ],
        ),
        out_shape=jax.ShapeDtypeStruct((rows, 2 * half), jnp.float32),
    )(order, own, other, columns)


def per_device(inputs, weight):
    views, images, width = inputs.shape
    total = images * DP
    data_index = lax.axis_index("dp")
    model_index = lax.axis_index("mp")
    feat = weight.shape[1]
    block = feat // DP
    rows = width // DP
    flat = inputs.reshape(views * images, width)

    place = jnp.arange(DP, dtype=jnp.int32)
    distance = (place >> 4) | ((place >> 2) & 3) << 3 | (place & 3) << 1
    order = data_index ^ distance
    relative = place ^ data_index
    position = (relative & 1) << 4 | (relative >> 3) << 2 | ((relative >> 1) & 3)

    share = views * images // Y
    mine = lax.dynamic_slice_in_dim(flat, lax.rem(model_index, Y) * share, share, axis=0)
    pieces = mine.reshape(share, DP, rows).transpose(1, 0, 2)
    slices = lax.all_to_all(pieces, "dp", split_axis=0, concat_axis=0)

    weight_own, weight_other = gather_dp(weight)
    ordered = take_columns(flat, order, rows)
    projected = lax.dot_general(
        weight_own.reshape(width // 2, feat),
        ordered[:, : width // 2],
        (((0,), (1,)), ((), ())),
        preferred_element_type=jnp.float32,
    ) + lax.dot_general(
        weight_other.reshape(width // 2, feat),
        ordered[:, width // 2 :],
        (((0,), (1,)), ((), ())),
        preferred_element_type=jnp.float32,
    )
    projected, slices = lax.optimization_barrier((projected, slices))
    groups = [list(range(Y)), list(range(Y, MP))]
    columns = lax.all_gather(slices, "mp", axis=0, axis_index_groups=groups)
    columns = columns.reshape(views, Y // views, DP, share, rows).transpose(0, 2, 1, 3, 4)
    columns = columns.reshape(views * total, rows)

    own = lax.all_to_all(
        projected.reshape(DP, block, views * images), "dp", split_axis=0, concat_axis=0
    ).reshape(DP, block, views, images)
    average = jnp.sum(own, axis=(0, 3), keepdims=True) / total
    centered = own - average
    variance = jnp.sum(centered * centered, axis=(0, 3), keepdims=True) / total
    inverse = lax.rsqrt(variance + epsilon)
    normed = (centered * inverse).astype(jnp.bfloat16).transpose(2, 1, 0, 3).reshape(views, block, total)
    inverse = inverse.reshape(block, views).T[:, :, None]

    copies = jnp.broadcast_to(normed[1][None], (MP, block, total))
    columns_b = lax.all_to_all(copies, "mp", split_axis=0, concat_axis=0).reshape(MP * block, total)
    rows_own, rows_other = (part.reshape(feat // 2, total) for part in gather_dp(normed[0]))

    def gradient_of(rows_a, with_diagonal):
        correlation = (
            lax.dot_general(rows_a, columns_b, (((1,), (1,)), ((), ())), preferred_element_type=jnp.float32)
            / total
        )
        inner = 2.0 * redundancy_weight * correlation
        if with_diagonal:
            row = lax.broadcasted_iota(jnp.int32, correlation.shape, 0)
            column = lax.broadcasted_iota(jnp.int32, correlation.shape, 1)
            diagonal = (row < block) & (column == model_index * block + row)
            inner = inner + diagonal.astype(jnp.float32) * (2.0 * (correlation - 1.0) - inner)
        return (loss_scale * inner).astype(jnp.bfloat16)

    corr_own = gradient_of(rows_own, True)
    corr_other = gradient_of(rows_other, False)
    corr_own, columns = lax.optimization_barrier((corr_own, columns))

    def times(lhs, rhs, dims):
        return lax.dot_general(lhs, rhs, (dims, ((), ())), preferred_element_type=jnp.float32) / total

    terms_other = times(corr_other, columns_b, ((1,), (0,))).astype(jnp.bfloat16)
    terms_b = (
        times(corr_own, rows_own, ((0,), (0,))) + times(corr_other, rows_other, ((0,), (0,)))
    ).astype(jnp.bfloat16)
    terms_own = times(corr_own, columns_b, ((1,), (0,)))
    terms_b = lax.all_to_all(terms_b.reshape(MP, block, total), "mp", split_axis=0, concat_axis=0)
    shape = (4, 4, block, total)
    grads = jnp.stack(
        [
            add_dp(terms_own.reshape(shape), terms_other.reshape(shape)),
            jnp.sum(terms_b.astype(jnp.float32), axis=0),
        ]
    )
    wide = normed.astype(jnp.float32)
    grad_mean = jnp.sum(grads, axis=2, keepdims=True) / total
    cross_mean = jnp.sum(grads * wide, axis=2, keepdims=True) / total
    grad_proj = ((grads - grad_mean - wide * cross_mean) * inverse).astype(jnp.bfloat16)
    grad_proj = grad_proj.transpose(1, 0, 2).reshape(block, views * total)
    grad_own, grad_other = gather_dp(grad_proj)
    return weight_gradient(
        position,
        grad_own.reshape(feat // 2, views * total),
        grad_other.reshape(feat // 2, views * total),
        columns,
    )


def solution(mesh):
    placed = (P(None, "dp", None), P("dp", "mp"))
    return jax.shard_map(
        per_device, mesh=mesh, in_specs=placed, out_specs=P("dp", "mp"), check_vma=False
    )
```

time: 434 us -> 310 us (0.71)
  waiting for transfers between devices: 319 us -> 110 us
  starting transfers between devices: 39.8 us -> 110 us
  Pallas kernels: 0 us -> 26.9 us
  local copies, waits for them, and re-layouts: 27.5 us -> 12.4 us
  matrix products: 15.5 us -> 9.22 us
  other arithmetic: 1.82 us -> 6.6 us
    all_to_all x4 -> x3, waiting for transfers between devices: 208 us -> 20.1 us  [the longest x1 20.1 us: per_device(): lax.all_to_all(copies, 'mp', split_axis=0, concat_axis=0)]
    all_gather x3 -> x1, waiting for transfers between devices: 110 us -> 0.01 us  [per_device(): columns = lax.all_gather(slices, 'mp', axis=0, axis_index_groups=groups)]
    ppermute x0 -> x28, waiting for transfers between devices: none -> 90.2 us  [swap(): return lax.ppermute(array, 'dp', [(i, i ^ step) for i in range(DP)])]
    ppermute x0 -> x28, starting transfers between devices: none -> 87.3 us  [swap(): return lax.ppermute(array, 'dp', [(i, i ^ step) for i in range(DP)])]
    pallas_call x0 -> x2, Pallas kernels: none -> 26.9 us  [the longest x1 18.7 us: take_columns(): pl.pallas_call(copy_kernel, grid_spec=pltpu.PrefetchScalarGridSpec(num_sc...]
    all_to_all x4 -> x3, starting transfers between devices: 39.7 us -> 22.3 us  [the longest x1 12.4 us: per_device(): lax.all_to_all(copies, 'mp', split_axis=0, concat_axis=0)]
    dot_general x2 -> x0, local copies, waits for them, and re-layouts: 7.22 us -> none  [the longest x1 6.38 us: per_device(): lax.dot_general(full_weight, inputs.reshape(views * images, width), (((0,...]
    all_to_all x1 -> x0, local copies, waits for them, and re-layouts: 6.42 us -> none  [per_device(): columns = lax.all_to_all(pieces, 'dp', split_axis=0, concat_axis=0)]
  transfers between devices with their start and end apart: 7 -> 32, of which waited for: 6 -> 19; matrix products, arithmetic and copies ran while one was open for 5% -> 7% of each run, Pallas kernels for 0% -> 6%
where the time goes in v2:
time: 310 us; the launch traced here: 308 us
  starting transfers between devices  110 us (35%)
  waiting for transfers between devices  110 us (35%)
  Pallas kernels  26.9 us (9%)
  blocking collectives  18.8 us (6%)
  between operations  13.9 us (4%)
  local copies, waits for them, and re-layouts  12.4 us (4%)
  matrix products  9.22 us (3%)
  other arithmetic  6.6 us (2%)
    ppermute x28, waiting for transfers between devices, swap(): return lax.ppermute(array, 'dp', [(i, i ^ step) for i in range(DP)])  90.2 us
    ppermute x28, starting transfers between devices, swap(): return lax.ppermute(array, 'dp', [(i, i ^ step) for i in range(DP)])  87.3 us
    all_to_all x1, waiting for transfers between devices, per_device(): lax.all_to_all(copies, 'mp', split_axis=0, concat_axis=0)  20.1 us
    all_to_all x1, blocking collectives, per_device(): lax.all_to_all(projected.reshape(DP, block, views * images), 'dp', split_...  18.8 us
    pallas_call x1, Pallas kernels, take_columns(): pl.pallas_call(copy_kernel, grid_spec=pltpu.PrefetchScalarGridSpec(num_sc...  18.7 us
    all_to_all x1, starting transfers between devices, per_device(): lax.all_to_all(copies, 'mp', split_axis=0, concat_axis=0)  12.4 us
    pallas_call x1, Pallas kernels, weight_gradient(): pl.pallas_call(weight_kernel, grid_spec=pltpu.PrefetchScalarGridSpec(num_...  8.19 us
    all_to_all x1, starting transfers between devices, per_device(): slices = lax.all_to_all(pieces, 'dp', split_axis=0, concat_axis=0)  6.26 us
  transfers between devices with their start and end apart: 32, of which 19 were waited for; matrix products, arithmetic and copies ran while one was open for 7% of the time, Pallas kernels for 6%

profile of v2, /device:TPU:1, one launch (start us, length us, event | category | flops | bytes accessed | tf_op | source)
XLA Modules:
  0.0 307.7 jit_solution(7026179922733945043)
XLA Ops:
  6.5 4.8 %collective-permute-start = (bf16[256,256]{1,0:T(8,128)(2,1)}, bf16[256,256]{1,0:T(8,128)(2,1)S(1)}, u32[]{:S(2)}, u32[]{:S(2)}) collective-permute-start(bf16[256,256]{1,0:T(8,128)(2,1)} %param.3), channel_id=1, source_target_pairs={{0,32},{16,48},{32,0},{48,16},{64,96},{80,112},{96,64},{112,80},{1... | collective-permute-start | bytes 393224 | tf_op jit(solution)/shard_map/ppermute | solution.py:17
  11.4 5.5 %collective-permute-start.2 = (bf16[256,256]{1,0:T(8,128)(2,1)}, bf16[256,256]{1,0:T(8,128)(2,1)S(1)}, u32[]{:S(2)}, u32[]{:S(2)}) collective-permute-start(bf16[256,256]{1,0:T(8,128)(2,1)} %param.3), channel_id=1, source_target_pairs={{0,96},{16,112},{32,64},{48,80},{64,32},{80,48},{96,0},{112,16},{1... | collective-permute-start | bytes 393224 | tf_op jit(solution)/shard_map/ppermute | solution.py:17
  20.5 8.9 %collective-permute-done.1 = bf16[256,256]{1,0:T(8,128)(2,1)S(1)} collective-permute-done((bf16[256,256]{1,0:T(8,128)(2,1)}, bf16[256,256]{1,0:T(8,128)(2,1)S(1)}, u32[]{:S(2)}, u32[]{:S(2)}) %collective-permute-start.1) | collective-permute-done | bytes 131104 | tf_op jit(solution)/shard_map/ppermute | solution.py:17
  30.4 4.4 %collective-permute-start.4 = (bf16[4,256,256]{2,1,0:T(8,128)(2,1)S(1)}, bf16[4,256,256]{2,1,0:T(8,128)(2,1)S(1)}, u32[]{:S(2)}, u32[]{:S(2)}) collective-permute-start(bf16[4,256,256]{2,1,0:T(8,128)(2,1)S(1)} %get-tuple-element.21), channel_id=1, source_target_pairs={{0,256},{16,272},{32,288},{48,304},{64,320},{80,336},{96,352},{112... | collective-permute-start | bytes 1572872 | tf_op jit(solution)/shard_map/ppermute | solution.py:17
  39.5 6.4 %collective-permute-done.4 = bf16[4,256,256]{2,1,0:T(8,128)(2,1)S(1)} collective-permute-done((bf16[4,256,256]{2,1,0:T(8,128)(2,1)S(1)}, bf16[4,256,256]{2,1,0:T(8,128)(2,1)S(1)}, u32[]{:S(2)}, u32[]{:S(2)}) %collective-permute-start.4) | collective-permute-done | bytes 524320 | tf_op jit(solution)/shard_map/ppermute | solution.py:17
  45.9 11.5 %collective-permute-done.3 = bf16[4,256,256]{2,1,0:T(8,128)(2,1)S(1)} collective-permute-done((bf16[4,256,256]{2,1,0:T(8,128)(2,1)S(1)}, bf16[4,256,256]{2,1,0:T(8,128)(2,1)S(1)}, u32[]{:S(2)}, u32[]{:S(2)}) %collective-permute-start.3) | collective-permute-done | bytes 524320 | tf_op jit(solution)/shard_map/ppermute | solution.py:17
  63.9 6.3 %all-to-all-start = ((bf16[32,32,256]{2,1,0:T(8,128)(2,1)}), bf16[32,32,256]{2,1,0:T(8,128)(2,1)S(1)}, u32[]{:S(2)}, u32[]{:S(2)}) async-start(bf16[32,32,256]{2,1,0:T(8,128)(2,1)} %copy.25), calls=%async_computation | async-start | bytes 1048576 | tf_op jit(solution)/shard_map/all_to_all | solution.py:114
  70.8 18.7 %shard_map.28 = bf16[256,8192]{1,0:T(8,128)(2,1)} custom-call(s32[32]{0:T(128)} %fusion.39.order_ref, bf16[256,8192]{1,0:T(8,128)(2,1)} %bitcast.147), custom_call_target="tpu_custom_call" | custom-call | tf_op jit(solution)/shard_map/pallas_call | solution.py:40
  94.5 18.8 %all_to_all.20 = f32[32,8,256]{2,1,0:T(8,128)S(1)} all-to-all(f32[32,8,256]{2,1,0:T(8,128)S(1)} %bitcast.168), channel_id=1, replica_groups=mesh['dp'=32,'mp'=16] {'dp'}, dimensions={0} | all-to-all | bytes 524288 | tf_op jit(solution)/shard_map/all_to_all | solution.py:135
  118.8 4.3 %collective-permute-start.7 = (bf16[8,4096]{1,0:T(8,128)(2,1)S(1)}, bf16[8,4096]{1,0:T(8,128)(2,1)S(1)}, u32[]{:S(2)}, u32[]{:S(2)}) collective-permute-start(bf16[8,4096]{1,0:T(8,128)(2,1)S(1)} %get-tuple-element.30), channel_id=1, source_target_pairs={{0,32},{16,48},{32,0},{48,16},{64,96},{80,112},{96,64},{112,80},{1... | collective-permute-start | bytes 196616 | tf_op jit(solution)/shard_map/ppermute | solution.py:17
  124.1 12.4 %all-to-all-start.2 = ((bf16[16,8,4096]{2,1,0:T(8,128)(2,1)}), bf16[16,8,4096]{2,1,0:T(8,128)(2,1)S(1)}, u32[]{:S(2)}, u32[]{:S(2)}) async-start(bf16[16,8,4096]{2,1,0:T(8,128)(2,1)} %broadcast_in_dim.5), calls=%async_computation.2 | async-start | bytes 2097152 | tf_op jit(solution)/shard_map/all_to_all | solution.py:146
  146.7 4.6 %collective-permute-done.10 = bf16[4,8,4096]{2,1,0:T(8,128)(2,1)S(1)} collective-permute-done((bf16[4,8,4096]{2,1,0:T(8,128)(2,1)S(1)}, bf16[4,8,4096]{2,1,0:T(8,128)(2,1)S(1)}, u32[]{:S(2)}, u32[]{:S(2)}) %collective-permute-start.10) | collective-permute-done | bytes 262176 | tf_op jit(solution)/shard_map/ppermute | solution.py:17
  159.2 20.1 %all-to-all-done.2 = bf16[16,8,4096]{2,1,0:T(8,128)(2,1)S(1)} async-done(((bf16[16,8,4096]{2,1,0:T(8,128)(2,1)}), bf16[16,8,4096]{2,1,0:T(8,128)(2,1)S(1)}, u32[]{:S(2)}, u32[]{:S(2)}) %all-to-all-start.2) | async-done | bytes 1048608 | tf_op jit(solution)/shard_map/all_to_all | solution.py:146
  181.8 3.9 %collective-permute-start.14 = (bf16[4,4,8,4096]{3,2,1,0:T(8,128)(2,1)}, bf16[4,4,8,4096]{3,2,1,0:T(8,128)(2,1)}, u32[]{:S(2)}, u32[]{:S(2)}) collective-permute-start(bf16[4,4,8,4096]{3,2,1,0:T(8,128)(2,1)} %bitcast.35), channel_id=1, source_target_pairs={{0,16},{16,0},{32,48},{48,32},{64,80},{80,64},{96,112},{112,96},{1... | collective-permute-start | bytes 3145736 | tf_op jit(solution)/shard_map/ppermute | solution.py:17
  186.8 4.8 %copy.26 = bf16[2,32,4,32,256]{4,3,2,1,0:T(8,128)(2,1)} copy(bf16[2,32,4,32,256]{4,3,1,2,0:T(8,128)(2,1)} %bitcast.150) | data formatting | bytes 8388608 | tf_op jit(solution)/shard_map/transpose | solution.py:132
  199.6 3.9 %collective-permute-start.16 = (bf16[4,8,4096]{2,1,0:T(8,128)(2,1)}, bf16[4,8,4096]{2,1,0:T(8,128)(2,1)}, u32[]{:S(2)}, u32[]{:S(2)}) collective-permute-start(bf16[4,8,4096]{2,1,0:T(8,128)(2,1)} %get-tuple-element.17), channel_id=1, source_target_pairs={{0,256},{16,272},{32,288},{48,304},{64,320},{80,336},{96,352},{112... | collective-permute-start | bytes 786440 | tf_op jit(solution)/shard_map/ppermute | solution.py:17
  209.2 4.0 %collective-permute-done.17 = bf16[4,8,4096]{2,1,0:T(8,128)(2,1)} collective-permute-done((bf16[4,8,4096]{2,1,0:T(8,128)(2,1)}, bf16[4,8,4096]{2,1,0:T(8,128)(2,1)}, u32[]{:S(2)}, u32[]{:S(2)}) %collective-permute-start.17) | collective-permute-done | bytes 262176 | tf_op jit(solution)/shard_map/ppermute | solution.py:17
  222.9 9.7 %collective-permute-done.18 = bf16[8,4096]{1,0:T(8,128)(2,1)S(1)} collective-permute-done((bf16[8,4096]{1,0:T(8,128)(2,1)S(1)}, bf16[8,4096]{1,0:T(8,128)(2,1)S(1)}, u32[]{:S(2)}, u32[]{:S(2)}) %collective-permute-start.18) | collective-permute-done | bytes 65568 | tf_op jit(solution)/shard_map/ppermute | solution.py:17
  232.5 4.8 %collective-permute-done.20 = bf16[8,4096]{1,0:T(8,128)(2,1)S(1)} collective-permute-done((bf16[8,4096]{1,0:T(8,128)(2,1)S(1)}, bf16[8,4096]{1,0:T(8,128)(2,1)S(1)}, u32[]{:S(2)}, u32[]{:S(2)}) %collective-permute-start.20) | collective-permute-done | bytes 65568 | tf_op jit(solution)/shard_map/ppermute | solution.py:17
  241.5 3.9 %collective-permute-start.23 = (bf16[8,8192]{1,0:T(8,128)(2,1)S(1)}, bf16[8,8192]{1,0:T(8,128)(2,1)S(1)}, u32[]{:S(2)}, u32[]{:S(2)}) collective-permute-start(bf16[8,8192]{1,0:T(8,128)(2,1)S(1)} %bitcast.158), channel_id=1, source_target_pairs={{0,96},{16,112},{32,64},{48,80},{64,32},{80,48},{96,0},{112,16},{1... | collective-permute-start | bytes 393224 | tf_op jit(solution)/shard_map/ppermute | solution.py:17
  250.8 5.5 %collective-permute-done.22 = bf16[8,8192]{1,0:T(8,128)(2,1)S(1)} collective-permute-done((bf16[8,8192]{1,0:T(8,128)(2,1)S(1)}, bf16[8,8192]{1,0:T(8,128)(2,1)S(1)}, u32[]{:S(2)}, u32[]{:S(2)}) %collective-permute-start.22) | collective-permute-done | bytes 131104 | tf_op jit(solution)/shard_map/ppermute | solution.py:17
  265.4 6.2 %collective-permute-done.25 = bf16[4,8,8192]{2,1,0:T(8,128)(2,1)S(1)} collective-permute-done((bf16[4,8,8192]{2,1,0:T(8,128)(2,1)S(1)}, bf16[4,8,8192]{2,1,0:T(8,128)(2,1)S(1)}, u32[]{:S(2)}, u32[]{:S(2)}) %collective-permute-start.25) | collective-permute-done | bytes 524320 | tf_op jit(solution)/shard_map/ppermute | solution.py:17
  271.5 9.9 %collective-permute-done.24 = bf16[4,8,8192]{2,1,0:T(8,128)(2,1)S(1)} collective-permute-done((bf16[4,8,8192]{2,1,0:T(8,128)(2,1)S(1)}, bf16[4,8,8192]{2,1,0:T(8,128)(2,1)S(1)}, u32[]{:S(2)}, u32[]{:S(2)}) %collective-permute-start.24) | collective-permute-done | bytes 524320 | tf_op jit(solution)/shard_map/ppermute | solution.py:17
  292.7 8.2 %shard_map.29 = f32[256,256]{1,0:T(8,128)} custom-call(s32[32]{0:T(128)} %and_or_fusion.order_ref, bf16[128,8192]{1,0:T(8,128)(2,1)} %bitcast.144, bf16[128,8192]{1,0:T(8,128)(2,1)} %bitcast.151, bf16[8192,256]{1,0:T(8,128)(2,1)} %bitcast.141), custom_call_target="tpu_custom_call" | custom-call | tf_op jit(solution)/shard_map/pallas_call | solution.py:75
  (102 shorter events, 102.5 us)
Async XLA Ops:
  6.5 12.6 %collective-permute-start = (bf16[256,256]{1,0:T(8,128)(2,1)}, bf16[256,256]{1,0:T(8,128)(2,1)S(1)}, u32[]{:S(2)}, u32[]{:S(2)}) collective-permute-start(bf16[256,256]{1,0:T(8,128)(2,1)} %param.3), channel_id=1, source_target_pairs={{0,32},{16,48},{32,0},{48,16},{64,96},{80,112},{96,64},{112,80},{1... | collective-permute-start | bytes 393224 | tf_op jit(solution)/shard_map/ppermute | solution.py:17
  16.9 12.5 %collective-permute-start.1 = (bf16[256,256]{1,0:T(8,128)(2,1)}, bf16[256,256]{1,0:T(8,128)(2,1)S(1)}, u32[]{:S(2)}, u32[]{:S(2)}) collective-permute-start(bf16[256,256]{1,0:T(8,128)(2,1)} %param.3), channel_id=1, source_target_pairs={{0,64},{16,80},{32,96},{48,112},{64,0},{80,16},{96,32},{112,48},{1... | collective-permute-start | bytes 393224 | tf_op jit(solution)/shard_map/ppermute | solution.py:17
  30.4 15.4 %collective-permute-start.4 = (bf16[4,256,256]{2,1,0:T(8,128)(2,1)S(1)}, bf16[4,256,256]{2,1,0:T(8,128)(2,1)S(1)}, u32[]{:S(2)}, u32[]{:S(2)}) collective-permute-start(bf16[4,256,256]{2,1,0:T(8,128)(2,1)S(1)} %get-tuple-element.21), channel_id=1, source_target_pairs={{0,256},{16,272},{32,288},{48,304},{64,320},{80,336},{96,352},{112... | collective-permute-start | bytes 1572872 | tf_op jit(solution)/shard_map/ppermute | solution.py:17
  34.8 22.5 %collective-permute-start.3 = (bf16[4,256,256]{2,1,0:T(8,128)(2,1)S(1)}, bf16[4,256,256]{2,1,0:T(8,128)(2,1)S(1)}, u32[]{:S(2)}, u32[]{:S(2)}) collective-permute-start(bf16[4,256,256]{2,1,0:T(8,128)(2,1)S(1)} %get-tuple-element.21), channel_id=1, source_target_pairs={{0,128},{16,144},{32,160},{48,176},{64,192},{80,208},{96,224},{112... | collective-permute-start | bytes 1572872 | tf_op jit(solution)/shard_map/ppermute | solution.py:17
  37.0 21.9 %collective-permute-start.5 = (bf16[4,256,256]{2,1,0:T(8,128)(2,1)S(1)}, bf16[4,256,256]{2,1,0:T(8,128)(2,1)S(1)}, u32[]{:S(2)}, u32[]{:S(2)}) collective-permute-start(bf16[4,256,256]{2,1,0:T(8,128)(2,1)S(1)} %get-tuple-element.21), channel_id=1, source_target_pairs={{0,384},{16,400},{32,416},{48,432},{64,448},{80,464},{96,480},{112... | collective-permute-start | bytes 1572872 | tf_op jit(solution)/shard_map/ppermute | solution.py:17
  59.2 30.2 %collective-permute-start.6 = (bf16[4,4,256,256]{3,2,1,0:T(8,128)(2,1)S(1)}, bf16[4,4,256,256]{3,2,1,0:T(8,128)(2,1)}, u32[]{:S(2)}, u32[]{:S(2)}) collective-permute-start(bf16[4,4,256,256]{3,2,1,0:T(8,128)(2,1)S(1)} %pad_maximum_fusion), channel_id=1, source_target_pairs={{0,16},{16,0},{32,48},{48,32},{64,80},{80,64},{96,112},{112,96},{1... | collective-permute-start | bytes 6291464 | tf_op jit(solution)/shard_map/ppermute | solution.py:17
  63.9 29.7 %all-to-all-start = ((bf16[32,32,256]{2,1,0:T(8,128)(2,1)}), bf16[32,32,256]{2,1,0:T(8,128)(2,1)S(1)}, u32[]{:S(2)}, u32[]{:S(2)}) async-start(bf16[32,32,256]{2,1,0:T(8,128)(2,1)} %copy.25), calls=%async_computation | async-start | bytes 1048576 | tf_op jit(solution)/shard_map/all_to_all | solution.py:114
  70.2 116.6 %all-gather.3.cloned.1.call-start = ((), (), s32[]{:S(2)}) async-start(), calls=%async_computation.4 | async-start | bytes 4718592 | tf_op jit(solution)/shard_map/all_gather | solution.py:131
  113.8 22.8 %collective-permute-start.9 = (bf16[8,4096]{1,0:T(8,128)(2,1)S(1)}, bf16[8,4096]{1,0:T(8,128)(2,1)S(1)}, u32[]{:S(2)}, u32[]{:S(2)}) collective-permute-start(bf16[8,4096]{1,0:T(8,128)(2,1)S(1)} %get-tuple-element.30), channel_id=1, source_target_pairs={{0,96},{16,112},{32,64},{48,80},{64,32},{80,48},{96,0},{112,16},{1... | collective-permute-start | bytes 196616 | tf_op jit(solution)/shard_map/ppermute | solution.py:17
  116.8 19.7 %collective-permute-start.8 = (bf16[8,4096]{1,0:T(8,128)(2,1)S(1)}, bf16[8,4096]{1,0:T(8,128)(2,1)S(1)}, u32[]{:S(2)}, u32[]{:S(2)}) collective-permute-start(bf16[8,4096]{1,0:T(8,128)(2,1)S(1)} %get-tuple-element.30), channel_id=1, source_target_pairs={{0,64},{16,80},{32,96},{48,112},{64,0},{80,16},{96,32},{112,48},{1... | collective-permute-start | bytes 196616 | tf_op jit(solution)/shard_map/ppermute | solution.py:17
  118.8 17.8 %collective-permute-start.7 = (bf16[8,4096]{1,0:T(8,128)(2,1)S(1)}, bf16[8,4096]{1,0:T(8,128)(2,1)S(1)}, u32[]{:S(2)}, u32[]{:S(2)}) collective-permute-start(bf16[8,4096]{1,0:T(8,128)(2,1)S(1)} %get-tuple-element.30), channel_id=1, source_target_pairs={{0,32},{16,48},{32,0},{48,16},{64,96},{80,112},{96,64},{112,80},{1... | collective-permute-start | bytes 196616 | tf_op jit(solution)/shard_map/ppermute | solution.py:17
  124.1 55.2 %all-to-all-start.2 = ((bf16[16,8,4096]{2,1,0:T(8,128)(2,1)}), bf16[16,8,4096]{2,1,0:T(8,128)(2,1)S(1)}, u32[]{:S(2)}, u32[]{:S(2)}) async-start(bf16[16,8,4096]{2,1,0:T(8,128)(2,1)} %broadcast_in_dim.5), calls=%async_computation.2 | async-start | bytes 2097152 | tf_op jit(solution)/shard_map/all_to_all | solution.py:146
  139.8 11.5 %collective-permute-start.10 = (bf16[4,8,4096]{2,1,0:T(8,128)(2,1)S(1)}, bf16[4,8,4096]{2,1,0:T(8,128)(2,1)S(1)}, u32[]{:S(2)}, u32[]{:S(2)}) collective-permute-start(bf16[4,8,4096]{2,1,0:T(8,128)(2,1)S(1)} %get-tuple-element.28), channel_id=1, source_target_pairs={{0,128},{16,144},{32,160},{48,176},{64,192},{80,208},{96,224},{112... | collective-permute-start | bytes 786440 | tf_op jit(solution)/shard_map/ppermute | solution.py:17
  141.9 11.7 %collective-permute-start.12 = (bf16[4,8,4096]{2,1,0:T(8,128)(2,1)S(1)}, bf16[4,8,4096]{2,1,0:T(8,128)(2,1)S(1)}, u32[]{:S(2)}, u32[]{:S(2)}) collective-permute-start(bf16[4,8,4096]{2,1,0:T(8,128)(2,1)S(1)} %get-tuple-element.28), channel_id=1, source_target_pairs={{0,384},{16,400},{32,416},{48,432},{64,448},{80,464},{96,480},{112... | collective-permute-start | bytes 786440 | tf_op jit(solution)/shard_map/ppermute | solution.py:17
  194.5 14.6 %collective-permute-start.15 = (bf16[4,8,4096]{2,1,0:T(8,128)(2,1)}, bf16[4,8,4096]{2,1,0:T(8,128)(2,1)}, u32[]{:S(2)}, u32[]{:S(2)}) collective-permute-start(bf16[4,8,4096]{2,1,0:T(8,128)(2,1)} %get-tuple-element.15), channel_id=1, source_target_pairs={{0,128},{16,144},{32,160},{48,176},{64,192},{80,208},{96,224},{112... | collective-permute-start | bytes 786440 | tf_op jit(solution)/shard_map/ppermute | solution.py:17
  196.5 16.6 %collective-permute-start.17 = (bf16[4,8,4096]{2,1,0:T(8,128)(2,1)}, bf16[4,8,4096]{2,1,0:T(8,128)(2,1)}, u32[]{:S(2)}, u32[]{:S(2)}) collective-permute-start(bf16[4,8,4096]{2,1,0:T(8,128)(2,1)} %get-tuple-element.16), channel_id=1, source_target_pairs={{0,384},{16,400},{32,416},{48,432},{64,448},{80,464},{96,480},{112... | collective-permute-start | bytes 786440 | tf_op jit(solution)/shard_map/ppermute | solution.py:17
  199.6 13.5 %collective-permute-start.16 = (bf16[4,8,4096]{2,1,0:T(8,128)(2,1)}, bf16[4,8,4096]{2,1,0:T(8,128)(2,1)}, u32[]{:S(2)}, u32[]{:S(2)}) collective-permute-start(bf16[4,8,4096]{2,1,0:T(8,128)(2,1)} %get-tuple-element.17), channel_id=1, source_target_pairs={{0,256},{16,272},{32,288},{48,304},{64,320},{80,336},{96,352},{112... | collective-permute-start | bytes 786440 | tf_op jit(solution)/shard_map/ppermute | solution.py:17
  205.5 35.5 %all-to-all-start.3 = ((bf16[16,8,4096]{2,1,0:T(8,128)(2,1)}), bf16[16,8,4096]{2,1,0:T(8,128)(2,1)S(1)}, u32[]{:S(2)}, u32[]{:S(2)}) async-start(bf16[16,8,4096]{2,1,0:T(8,128)(2,1)} %fusion.3), calls=%async_computation.3 | async-start | bytes 2097152 | tf_op jit(solution)/shard_map/all_to_all | solution.py:174
  214.5 18.1 %collective-permute-start.18 = (bf16[8,4096]{1,0:T(8,128)(2,1)S(1)}, bf16[8,4096]{1,0:T(8,128)(2,1)S(1)}, u32[]{:S(2)}, u32[]{:S(2)}) collective-permute-start(bf16[8,4096]{1,0:T(8,128)(2,1)S(1)} %get-tuple-element.24), channel_id=1, source_target_pairs={{0,32},{16,48},{32,0},{48,16},{64,96},{80,112},{96,64},{112,80},{1... | collective-permute-start | bytes 196616 | tf_op jit(solution)/shard_map/ppermute | solution.py:17
  216.4 21.0 %collective-permute-start.20 = (bf16[8,4096]{1,0:T(8,128)(2,1)S(1)}, bf16[8,4096]{1,0:T(8,128)(2,1)S(1)}, u32[]{:S(2)}, u32[]{:S(2)}) collective-permute-start(bf16[8,4096]{1,0:T(8,128)(2,1)S(1)} %get-tuple-element.25), channel_id=1, source_target_pairs={{0,96},{16,112},{32,64},{48,80},{64,32},{80,48},{96,0},{112,16},{1... | collective-permute-start | bytes 196616 | tf_op jit(solution)/shard_map/ppermute | solution.py:17
  219.6 21.4 %collective-permute-start.19 = (bf16[8,4096]{1,0:T(8,128)(2,1)S(1)}, bf16[8,4096]{1,0:T(8,128)(2,1)S(1)}, u32[]{:S(2)}, u32[]{:S(2)}) collective-permute-start(bf16[8,4096]{1,0:T(8,128)(2,1)S(1)} %get-tuple-element.26), channel_id=1, source_target_pairs={{0,64},{16,80},{32,96},{48,112},{64,0},{80,16},{96,32},{112,48},{1... | collective-permute-start | bytes 196616 | tf_op jit(solution)/shard_map/ppermute | solution.py:17
  256.4 15.2 %collective-permute-start.25 = (bf16[4,8,8192]{2,1,0:T(8,128)(2,1)S(1)}, bf16[4,8,8192]{2,1,0:T(8,128)(2,1)S(1)}, u32[]{:S(2)}, u32[]{:S(2)}) collective-permute-start(bf16[4,8,8192]{2,1,0:T(8,128)(2,1)S(1)} %get-tuple-element.19), channel_id=1, source_target_pairs={{0,256},{16,272},{32,288},{48,304},{64,320},{80,336},{96,352},{112... | collective-permute-start | bytes 1572872 | tf_op jit(solution)/shard_map/ppermute | solution.py:17
  259.4 22.1 %collective-permute-start.24 = (bf16[4,8,8192]{2,1,0:T(8,128)(2,1)S(1)}, bf16[4,8,8192]{2,1,0:T(8,128)(2,1)S(1)}, u32[]{:S(2)}, u32[]{:S(2)}) collective-permute-start(bf16[4,8,8192]{2,1,0:T(8,128)(2,1)S(1)} %get-tuple-element.19), channel_id=1, source_target_pairs={{0,128},{16,144},{32,160},{48,176},{64,192},{80,208},{96,224},{112... | collective-permute-start | bytes 1572872 | tf_op jit(solution)/shard_map/ppermute | solution.py:17
  262.0 22.8 %collective-permute-start.26 = (bf16[4,8,8192]{2,1,0:T(8,128)(2,1)S(1)}, bf16[4,8,8192]{2,1,0:T(8,128)(2,1)S(1)}, u32[]{:S(2)}, u32[]{:S(2)}) collective-permute-start(bf16[4,8,8192]{2,1,0:T(8,128)(2,1)S(1)} %get-tuple-element.19), channel_id=1, source_target_pairs={{0,384},{16,400},{32,416},{48,432},{64,448},{80,464},{96,480},{112... | collective-permute-start | bytes 1572872 | tf_op jit(solution)/shard_map/ppermute | solution.py:17
  (16 other events, 110.7 us)
Sparse Core Ops, SparseCore 0:
  94.6 80.7 all-gather.2

commit v3 on v2

--- a/solution.py
+++ b/solution.py
@@ -1,3 +1,5 @@
+import functools
+
 import jax
 import jax.numpy as jnp
 from jax import lax
@@ -31,65 +33,90 @@
     return sum(part.astype(jnp.float32) for part in parts)
 
 
-def copy_kernel(order_ref, source_ref, out_ref):
-    out_ref[...] = source_ref[...]
-
-
-def take_columns(array, order, width):
-    rows, columns = array.shape
+def project_kernel(last, order_ref, inputs_ref, weight_ref, *refs):
+    out_ref = refs[-1]
+    blocks, depth, _ = weight_ref.shape
+    result = refs[0][...] if last else None
+    for k in range(blocks):
+        columns = pl.ds(pl.multiple_of(order_ref[k] * depth, depth), depth)
+        part = jnp.dot(inputs_ref[:, columns], weight_ref[k], preferred_element_type=jnp.float32)
+        result = part if result is None else result + part
+    out_ref[...] = result.T if last else result
+
+
+def project(order, inputs, weight, before=None):
+    rows, feat = inputs.shape[0], weight.shape[2]
+    operands = (inputs, weight) if before is None else (inputs, weight, before)
     return pl.pallas_call(
-        copy_kernel,
-        grid_spec=pltpu.PrefetchScalarGridSpec(
-            num_scalar_prefetch=1,
-            grid=(columns // width,),
-            in_specs=[pl.BlockSpec((rows, width), lambda k, order: (0, order[k]))],
-            out_specs=pl.BlockSpec((rows, width), lambda k, order: (0, k)),
+        functools.partial(project_kernel, before is not None),
+        in_specs=[pl.BlockSpec(memory_space=pltpu.SMEM)]
+        + [pl.BlockSpec(memory_space=pltpu.VMEM)] * len(operands),
+        out_specs=pl.BlockSpec(memory_space=pltpu.VMEM),
+        out_shape=jax.ShapeDtypeStruct((rows, feat) if before is None else (feat, rows), jnp.float32),
+        compiler_params=pltpu.CompilerParams(vmem_limit_bytes=32 * 1024 * 1024),
+        cost_estimate=pl.CostEstimate(
+            flops=2 * rows * feat * weight.shape[0] * weight.shape[1],
+            bytes_accessed=6 * 1024 * 1024,
+            transcendentals=0,
         ),
-        out_shape=jax.ShapeDtypeStruct(array.shape, array.dtype),
-    )(order, array)
-
-
-def weight_kernel(order_ref, own_ref, other_ref, columns_ref, out_ref, total_ref, placed_ref):
-    step = pl.program_id(0)
-    half = own_ref.shape[0]
+    )(order, *operands)
+
+
+def weight_kernel(last, grad_ref, columns_ref, *refs):
+    total_ref = refs[-1]
+    step = pl.program_id(0) * pl.num_programs(1) + pl.program_id(1)
 
     @pl.when(step == 0)
     def _():
         total_ref[...] = jnp.zeros_like(total_ref)
 
-    total_ref[:half] += jnp.dot(own_ref[...], columns_ref[...], preferred_element_type=jnp.float32)
-    total_ref[half:] += jnp.dot(other_ref[...], columns_ref[...], preferred_element_type=jnp.float32)
-
-    @pl.when(step == pl.num_programs(0) - 1)
-    def _():
-        for block in range(DP):
-            start = pl.multiple_of(order_ref[block] * 8, 8)
-            placed_ref[block * 8 : block * 8 + 8] = total_ref[pl.ds(start, 8)]
-        out_ref[...] = placed_ref[...].T
-
-
-def weight_gradient(order, own, other, columns):
-    depth, rows = columns.shape
-    half = own.shape[0]
-    tile = 1024
+    quarters, devices, share, rows = columns_ref.shape
+    pieces = [columns_ref[:, d].reshape(quarters * share, rows) for d in range(devices)]
+    columns = jnp.concatenate(pieces, axis=0)
+    total_ref[...] += jnp.dot(grad_ref[...], columns, preferred_element_type=jnp.float32)
+
+    if last:
+        position_ref, own_ref, out_ref, placed_ref = refs[:4]
+        half = own_ref.shape[0]
+
+        @pl.when(step == pl.num_programs(0) * pl.num_programs(1) - 1)
+        def _():
+            placed_ref[:half] = own_ref[...]
+            placed_ref[half:] = total_ref[...]
+            blocks = [
+                placed_ref[pl.ds(pl.multiple_of(position_ref[block] * 8, 8), 8)] for block in range(DP)
+            ]
+            out_ref[...] = jnp.concatenate(blocks, axis=0).T
+
+
+def weight_half(grad, columns, position=None, own=None):
+    half, depth = grad.shape
+    slices, devices, share, rows = columns.shape
+    quarters, group = slices // 2, 8
+    last = own is not None
+    in_specs = [
+        pl.BlockSpec((half, group * quarters * share), lambda v, d: (0, v * (devices // group) + d)),
+        pl.BlockSpec((quarters, group, share, rows), lambda v, d: (v, d, 0, 0)),
+    ]
+    scratch = [pltpu.VMEM((half, rows), jnp.float32)]
+    if last:
+        in_specs += [
+            pl.BlockSpec(memory_space=pltpu.SMEM),
+            pl.BlockSpec((half, rows), lambda v, d: (0, 0)),
+        ]
+        scratch = [pltpu.VMEM((2 * half, rows), jnp.float32)] + scratch
     return pl.pallas_call(
-        weight_kernel,
-        grid_spec=pltpu.PrefetchScalarGridSpec(
-            num_scalar_prefetch=1,
-            grid=(depth // tile,),
-            in_specs=[
-                pl.BlockSpec((half, tile), lambda k, order: (0, k)),
-                pl.BlockSpec((half, tile), lambda k, order: (0, k)),
-                pl.BlockSpec((tile, rows), lambda k, order: (k, 0)),
-            ],
-            out_specs=pl.BlockSpec((rows, 2 * half), lambda k, order: (0, 0)),
-            scratch_shapes=[
-                pltpu.VMEM((2 * half, rows), jnp.float32),
-                pltpu.VMEM((2 * half, rows), jnp.float32),
-            ],
+        functools.partial(weight_kernel, last),
+        grid=(2, devices // group),
+        in_specs=in_specs,
+        out_specs=pl.BlockSpec((rows, 2 * half) if last else (half, rows), lambda v, d: (0, 0)),
+        out_shape=jax.ShapeDtypeStruct((rows, 2 * half) if last else (half, rows), jnp.float32),
+        scratch_shapes=scratch if last else [],
+        compiler_params=pltpu.CompilerParams(vmem_limit_bytes=32 * 1024 * 1024),
+        cost_estimate=pl.CostEstimate(
+            flops=2 * half * depth * rows, bytes_accessed=6 * 1024 * 1024, transcendentals=0
         ),
-        out_shape=jax.ShapeDtypeStruct((rows, 2 * half), jnp.float32),
-    )(order, own, other, columns)
+    )(grad, columns, *((position, own) if last else ()))
 
 
 def per_device(inputs, weight):
@@ -113,24 +140,13 @@
     pieces = mine.reshape(share, DP, rows).transpose(1, 0, 2)
     slices = lax.all_to_all(pieces, "dp", split_axis=0, concat_axis=0)
 
-    weight_own, weight_other = gather_dp(weight)
-    ordered = take_columns(flat, order, rows)
-    projected = lax.dot_general(
-        weight_own.reshape(width // 2, feat),
-        ordered[:, : width // 2],
-        (((0,), (1,)), ((), ())),
-        preferred_element_type=jnp.float32,
-    ) + lax.dot_general(
-        weight_other.reshape(width // 2, feat),
-        ordered[:, width // 2 :],
-        (((0,), (1,)), ((), ())),
-        preferred_element_type=jnp.float32,
-    )
-    projected, slices = lax.optimization_barrier((projected, slices))
-    groups = [list(range(Y)), list(range(Y, MP))]
-    columns = lax.all_gather(slices, "mp", axis=0, axis_index_groups=groups)
-    columns = columns.reshape(views, Y // views, DP, share, rows).transpose(0, 2, 1, 3, 4)
-    columns = columns.reshape(views * total, rows)
+    along_z = jnp.stack([weight] + [swap(weight, 2 * k) for k in (1, 2, 3)])
+    weight_own = jnp.stack([along_z] + [swap(along_z, 8 * k) for k in (1, 2, 3)])
+    weight_own, slices = lax.optimization_barrier((weight_own, slices))
+    weight_other = swap(weight_own, 1)
+    half = (DP // 2, rows, feat)
+    projected = project(order[: DP // 2], flat, weight_own.reshape(half))
+    projected = project(order[DP // 2 :], flat, weight_other.reshape(half), projected)
 
     own = lax.all_to_all(
         projected.reshape(DP, block, views * images), "dp", split_axis=0, concat_axis=0
@@ -161,7 +177,6 @@
 
     corr_own = gradient_of(rows_own, True)
     corr_other = gradient_of(rows_other, False)
-    corr_own, columns = lax.optimization_barrier((corr_own, columns))
 
     def times(lhs, rhs, dims):
         return lax.dot_general(lhs, rhs, (dims, ((), ())), preferred_element_type=jnp.float32) / total
@@ -172,6 +187,9 @@
     ).astype(jnp.bfloat16)
     terms_own = times(corr_own, columns_b, ((1,), (0,)))
     terms_b = lax.all_to_all(terms_b.reshape(MP, block, total), "mp", split_axis=0, concat_axis=0)
+    terms_b, slices = lax.optimization_barrier((terms_b, slices))
+    groups = [list(range(Y)), list(range(Y, MP))]
+    columns = lax.all_gather(slices, "mp", axis=0, axis_index_groups=groups)
     shape = (4, 4, block, total)
     grads = jnp.stack(
         [
@@ -185,12 +203,8 @@
     grad_proj = ((grads - grad_mean - wide * cross_mean) * inverse).astype(jnp.bfloat16)
     grad_proj = grad_proj.transpose(1, 0, 2).reshape(block, views * total)
     grad_own, grad_other = gather_dp(grad_proj)
-    return weight_gradient(
-        position,
-        grad_own.reshape(feat // 2, views * total),
-        grad_other.reshape(feat // 2, views * total),
-        columns,
-    )
+    part = weight_half(grad_own.reshape(feat // 2, views * total), columns)
+    return weight_half(grad_other.reshape(feat // 2, views * total), columns, position, part)
 
 
 def solution(mesh):

time: 310 us -> 291 us (0.939)
  Pallas kernels: 26.9 us -> 12.3 us
  starting transfers between devices: 110 us -> 123 us
  waiting for transfers between devices: 110 us -> 102 us
  matrix products: 9.22 us -> 4.6 us
  local copies, waits for them, and re-layouts: 12.4 us -> 8.93 us
    all_to_all x1, waiting for transfers between devices: 20.1 us -> 2.7 us  [per_device(): lax.all_to_all(copies, 'mp', split_axis=0, concat_axis=0)]
    all_to_all x1, waiting for transfers between devices: 0.01 us -> 17.3 us  [per_device(): lax.all_to_all(terms_b.reshape(MP, block, total), 'mp', split_axis=0, con...]
    pallas_call x2 -> x4, Pallas kernels: 26.9 us -> 12.3 us  [the longest x2 8.66 us: weight_half(): pl.pallas_call(functools.partial(weight_kernel, last), grid=(2, devices /...]
    ppermute x28, waiting for transfers between devices: 90.2 us -> 81.9 us  [swap(): return lax.ppermute(array, 'dp', [(i, i ^ step) for i in range(DP)])]
    ppermute x28, starting transfers between devices: 87.3 us -> 92.7 us  [swap(): return lax.ppermute(array, 'dp', [(i, i ^ step) for i in range(DP)])]
    all_to_all x1, starting transfers between devices: 6.26 us -> 11.4 us  [per_device(): slices = lax.all_to_all(pieces, 'dp', split_axis=0, concat_axis=0)]
    transpose x1 -> x0, local copies, waits for them, and re-layouts: 4.8 us -> none  [per_device(): columns.reshape(views, Y // views, DP, share, rows).transpose(0, 2, 1, 3, 4)]
    dot_general x2 -> x0, matrix products: 3.91 us -> none  [the longest x1 3.13 us: per_device(): lax.dot_general(weight_other.reshape(width // 2, feat), ordered[:, width...]
  transfers between devices with their start and end apart: 32 -> 32, of which waited for: 19 -> 17; matrix products, arithmetic and copies ran while one was open for 7% -> 3% of each run, Pallas kernels for 6% -> 1%
where the time goes in v3:
time: 291 us; the launch traced here: 286 us
  starting transfers between devices  123 us (42%)
  waiting for transfers between devices  102 us (35%)
  blocking collectives  16.6 us (6%)
  between operations  14 us (5%)
  Pallas kernels  12.3 us (4%)
  local copies, waits for them, and re-layouts  8.93 us (3%)
  matrix products  4.6 us (2%)
  other arithmetic  4.41 us (2%)
    ppermute x28, starting transfers between devices, swap(): return lax.ppermute(array, 'dp', [(i, i ^ step) for i in range(DP)])  92.7 us
    ppermute x28, waiting for transfers between devices, swap(): return lax.ppermute(array, 'dp', [(i, i ^ step) for i in range(DP)])  81.9 us
    all_to_all x1, waiting for transfers between devices, per_device(): lax.all_to_all(terms_b.reshape(MP, block, total), 'mp', split_axis=0, con...  17.3 us
    all_to_all x1, blocking collectives, per_device(): lax.all_to_all(projected.reshape(DP, block, views * images), 'dp', split_...  16.6 us
    all_to_all x1, starting transfers between devices, per_device(): lax.all_to_all(copies, 'mp', split_axis=0, concat_axis=0)  12.7 us
    all_to_all x1, starting transfers between devices, per_device(): slices = lax.all_to_all(pieces, 'dp', split_axis=0, concat_axis=0)  11.4 us
    pallas_call x2, Pallas kernels, weight_half(): pl.pallas_call(functools.partial(weight_kernel, last), grid=(2, devices /...  8.66 us
    all_to_all x1, starting transfers between devices, per_device(): lax.all_to_all(terms_b.reshape(MP, block, total), 'mp', split_axis=0, con...  6.45 us
  transfers between devices with their start and end apart: 32, of which 17 were waited for; matrix products, arithmetic and copies ran while one was open for 3% of the time, Pallas kernels for 1%

profile of v3, /device:TPU:1, one launch (start us, length us, event | category | flops | bytes accessed | tf_op | source)
XLA Modules:
  0.0 286.1 jit_solution(18006167149576236605)
XLA Ops:
  8.9 11.4 %all-to-all-start = ((bf16[32,32,256]{2,1,0:T(8,128)(2,1)}), bf16[32,32,256]{2,1,0:T(8,128)(2,1)S(1)}, u32[]{:S(2)}, u32[]{:S(2)}) async-start(bf16[32,32,256]{2,1,0:T(8,128)(2,1)} %copy.18), calls=%async_computation | async-start | bytes 1048576 | tf_op jit(solution)/shard_map/all_to_all | solution.py:141
  32.5 10.6 %collective-permute-done.1 = bf16[256,256]{1,0:T(8,128)(2,1)S(1)} collective-permute-done((bf16[256,256]{1,0:T(8,128)(2,1)S(1)}, bf16[256,256]{1,0:T(8,128)(2,1)S(1)}, u32[]{:S(2)}, u32[]{:S(2)}) %collective-permute-start.1) | collective-permute-done | bytes 131104 | tf_op jit(solution)/shard_map/ppermute | solution.py:19
  46.3 4.4 %collective-permute-start.4 = (bf16[4,256,256]{2,1,0:T(8,128)(2,1)S(1)}, bf16[4,256,256]{2,1,0:T(8,128)(2,1)S(1)}, u32[]{:S(2)}, u32[]{:S(2)}) collective-permute-start(bf16[4,256,256]{2,1,0:T(8,128)(2,1)S(1)} %get-tuple-element.21), channel_id=1, source_target_pairs={{0,256},{16,272},{32,288},{48,304},{64,320},{80,336},{96,352},{112... | collective-permute-start | bytes 1572872 | tf_op jit(solution)/shard_map/ppermute | solution.py:19
  52.8 4.4 %collective-permute-done.3 = bf16[4,256,256]{2,1,0:T(8,128)(2,1)S(1)} collective-permute-done((bf16[4,256,256]{2,1,0:T(8,128)(2,1)S(1)}, bf16[4,256,256]{2,1,0:T(8,128)(2,1)S(1)}, u32[]{:S(2)}, u32[]{:S(2)}) %collective-permute-start.3) | collective-permute-done | bytes 524320 | tf_op jit(solution)/shard_map/ppermute | solution.py:19
  57.1 13.5 %collective-permute-done.4 = bf16[4,256,256]{2,1,0:T(8,128)(2,1)S(1)} collective-permute-done((bf16[4,256,256]{2,1,0:T(8,128)(2,1)S(1)}, bf16[4,256,256]{2,1,0:T(8,128)(2,1)S(1)}, u32[]{:S(2)}, u32[]{:S(2)}) %collective-permute-start.4) | collective-permute-done | bytes 524320 | tf_op jit(solution)/shard_map/ppermute | solution.py:19
  70.6 5.9 %collective-permute-done.5 = bf16[4,256,256]{2,1,0:T(8,128)(2,1)S(1)} collective-permute-done((bf16[4,256,256]{2,1,0:T(8,128)(2,1)S(1)}, bf16[4,256,256]{2,1,0:T(8,128)(2,1)S(1)}, u32[]{:S(2)}, u32[]{:S(2)}) %collective-permute-start.5) | collective-permute-done | bytes 524320 | tf_op jit(solution)/shard_map/ppermute | solution.py:19
  76.8 4.7 %collective-permute-start.6 = (bf16[4,4,256,256]{3,2,1,0:T(8,128)(2,1)S(1)}, bf16[4,4,256,256]{3,2,1,0:T(8,128)(2,1)}, u32[]{:S(2)}, u32[]{:S(2)}) collective-permute-start(bf16[4,4,256,256]{3,2,1,0:T(8,128)(2,1)S(1)} %pad_maximum_fusion), channel_id=1, source_target_pairs={{0,16},{16,0},{32,48},{48,32},{64,80},{80,64},{96,112},{112,96},{1... | collective-permute-start | bytes 6291464 | tf_op jit(solution)/shard_map/ppermute | solution.py:19
  87.8 16.6 %all_to_all.20 = f32[32,8,256]{2,1,0:T(8,128)S(1)} all-to-all(f32[32,8,256]{2,1,0:T(8,128)S(1)} %bitcast.143), channel_id=1, replica_groups=mesh['dp'=32,'mp'=16] {'dp'}, dimensions={0} | all-to-all | bytes 524288 | tf_op jit(solution)/shard_map/all_to_all | solution.py:151
  110.2 4.0 %collective-permute-start.9 = (bf16[8,4096]{1,0:T(8,128)(2,1)S(1)}, bf16[8,4096]{1,0:T(8,128)(2,1)S(1)}, u32[]{:S(2)}, u32[]{:S(2)}) collective-permute-start(bf16[8,4096]{1,0:T(8,128)(2,1)S(1)} %get-tuple-element.30), channel_id=1, source_target_pairs={{0,96},{16,112},{32,64},{48,80},{64,32},{80,48},{96,0},{112,16},{1... | collective-permute-start | bytes 196616 | tf_op jit(solution)/shard_map/ppermute | solution.py:19
  115.3 12.7 %all-to-all-start.2 = ((bf16[16,8,4096]{2,1,0:T(8,128)(2,1)}), bf16[16,8,4096]{2,1,0:T(8,128)(2,1)S(1)}, u32[]{:S(2)}, u32[]{:S(2)}) async-start(bf16[16,8,4096]{2,1,0:T(8,128)(2,1)} %broadcast_in_dim.5), calls=%async_computation.2 | async-start | bytes 2097152 | tf_op jit(solution)/shard_map/all_to_all | solution.py:162
  137.7 5.5 %collective-permute-done.11 = bf16[4,8,4096]{2,1,0:T(8,128)(2,1)S(1)} collective-permute-done((bf16[4,8,4096]{2,1,0:T(8,128)(2,1)S(1)}, bf16[4,8,4096]{2,1,0:T(8,128)(2,1)S(1)}, u32[]{:S(2)}, u32[]{:S(2)}) %collective-permute-start.11) | collective-permute-done | bytes 262176 | tf_op jit(solution)/shard_map/ppermute | solution.py:19
  143.2 6.4 %collective-permute-done.12 = bf16[4,8,4096]{2,1,0:T(8,128)(2,1)S(1)} collective-permute-done((bf16[4,8,4096]{2,1,0:T(8,128)(2,1)S(1)}, bf16[4,8,4096]{2,1,0:T(8,128)(2,1)S(1)}, u32[]{:S(2)}, u32[]{:S(2)}) %collective-permute-start.12) | collective-permute-done | bytes 262176 | tf_op jit(solution)/shard_map/ppermute | solution.py:19
  159.2 4.6 %collective-permute-start.14 = (bf16[4,4,8,4096]{3,2,1,0:T(8,128)(2,1)}, bf16[4,4,8,4096]{3,2,1,0:T(8,128)(2,1)}, u32[]{:S(2)}, u32[]{:S(2)}) collective-permute-start(bf16[4,4,8,4096]{3,2,1,0:T(8,128)(2,1)} %bitcast.32), channel_id=1, source_target_pairs={{0,16},{16,0},{32,48},{48,32},{64,80},{80,64},{96,112},{112,96},{1... | collective-permute-start | bytes 3145736 | tf_op jit(solution)/shard_map/ppermute | solution.py:19
  166.3 6.5 %all-to-all-start.3 = ((bf16[16,8,4096]{2,1,0:T(8,128)(2,1)}), bf16[16,8,4096]{2,1,0:T(8,128)(2,1)S(1)}, u32[]{:S(2)}, u32[]{:S(2)}) async-start(bf16[16,8,4096]{2,1,0:T(8,128)(2,1)} %fusion.3), calls=%async_computation.3 | async-start | bytes 2097152 | tf_op jit(solution)/shard_map/all_to_all | solution.py:189
  177.5 4.7 %collective-permute-start.16 = (bf16[4,8,4096]{2,1,0:T(8,128)(2,1)}, bf16[4,8,4096]{2,1,0:T(8,128)(2,1)S(1)}, u32[]{:S(2)}, u32[]{:S(2)}) collective-permute-start(bf16[4,8,4096]{2,1,0:T(8,128)(2,1)} %get-tuple-element.17), channel_id=1, source_target_pairs={{0,256},{16,272},{32,288},{48,304},{64,320},{80,336},{96,352},{112... | collective-permute-start | bytes 786440 | tf_op jit(solution)/shard_map/ppermute | solution.py:19
  185.2 17.3 %all-to-all-done.3 = bf16[16,8,4096]{2,1,0:T(8,128)(2,1)S(1)} async-done(((bf16[16,8,4096]{2,1,0:T(8,128)(2,1)}), bf16[16,8,4096]{2,1,0:T(8,128)(2,1)S(1)}, u32[]{:S(2)}, u32[]{:S(2)}) %all-to-all-start.3) | async-done | bytes 1048608 | tf_op jit(solution)/shard_map/all_to_all | solution.py:189
  207.5 5.4 %collective-permute-start.20 = (bf16[8,4096]{1,0:T(8,128)(2,1)S(1)}, bf16[8,4096]{1,0:T(8,128)(2,1)S(1)}, u32[]{:S(2)}, u32[]{:S(2)}) collective-permute-start(bf16[8,4096]{1,0:T(8,128)(2,1)S(1)} %get-tuple-element.25), channel_id=1, source_target_pairs={{0,96},{16,112},{32,64},{48,80},{64,32},{80,48},{96,0},{112,16},{1... | collective-permute-start | bytes 196616 | tf_op jit(solution)/shard_map/ppermute | solution.py:19
  217.1 5.4 %collective-permute-start.22 = (bf16[8,8192]{1,0:T(8,128)(2,1)S(1)}, bf16[8,8192]{1,0:T(8,128)(2,1)S(1)}, u32[]{:S(2)}, u32[]{:S(2)}) collective-permute-start(bf16[8,8192]{1,0:T(8,128)(2,1)S(1)} %bitcast.155), channel_id=1, source_target_pairs={{0,64},{16,80},{32,96},{48,112},{64,0},{80,16},{96,32},{112,48},{1... | collective-permute-start | bytes 393224 | tf_op jit(solution)/shard_map/ppermute | solution.py:19
  226.6 4.2 %collective-permute-done.23 = bf16[8,8192]{1,0:T(8,128)(2,1)S(1)} collective-permute-done((bf16[8,8192]{1,0:T(8,128)(2,1)S(1)}, bf16[8,8192]{1,0:T(8,128)(2,1)S(1)}, u32[]{:S(2)}, u32[]{:S(2)}) %collective-permute-start.23) | collective-permute-done | bytes 131104 | tf_op jit(solution)/shard_map/ppermute | solution.py:19
  233.8 4.1 %collective-permute-start.25 = (bf16[4,8,8192]{2,1,0:T(8,128)(2,1)S(1)}, bf16[4,8,8192]{2,1,0:T(8,128)(2,1)S(1)}, u32[]{:S(2)}, u32[]{:S(2)}) collective-permute-start(bf16[4,8,8192]{2,1,0:T(8,128)(2,1)S(1)} %get-tuple-element.19), channel_id=1, source_target_pairs={{0,256},{16,272},{32,288},{48,304},{64,320},{80,336},{96,352},{112... | collective-permute-start | bytes 1572872 | tf_op jit(solution)/shard_map/ppermute | solution.py:19
  241.3 12.8 %collective-permute-done.25 = bf16[4,8,8192]{2,1,0:T(8,128)(2,1)S(1)} collective-permute-done((bf16[4,8,8192]{2,1,0:T(8,128)(2,1)S(1)}, bf16[4,8,8192]{2,1,0:T(8,128)(2,1)S(1)}, u32[]{:S(2)}, u32[]{:S(2)}) %collective-permute-start.25) | collective-permute-done | bytes 524320 | tf_op jit(solution)/shard_map/ppermute | solution.py:19
  254.1 8.6 %collective-permute-done.26 = bf16[4,8,8192]{2,1,0:T(8,128)(2,1)S(1)} collective-permute-done((bf16[4,8,8192]{2,1,0:T(8,128)(2,1)S(1)}, bf16[4,8,8192]{2,1,0:T(8,128)(2,1)S(1)}, u32[]{:S(2)}, u32[]{:S(2)}) %collective-permute-start.26) | collective-permute-done | bytes 524320 | tf_op jit(solution)/shard_map/ppermute | solution.py:19
  262.9 5.4 %collective-permute-start.27 = (bf16[4,4,8,8192]{3,2,1,0:T(8,128)(2,1)S(1)}, bf16[4,4,8,8192]{3,2,1,0:T(8,128)(2,1)}, u32[]{:S(2)}, u32[]{:S(2)}) collective-permute-start(bf16[4,4,8,8192]{3,2,1,0:T(8,128)(2,1)S(1)} %pad_maximum_fusion.1), channel_id=1, source_target_pairs={{0,16},{16,0},{32,48},{48,32},{64,80},{80,64},{96,112},{112,96},{1... | collective-permute-start | bytes 6291464 | tf_op jit(solution)/shard_map/ppermute | solution.py:19
  273.1 6.1 %shard_map.31 = f32[256,256]{1,0:T(8,128)} custom-call(bf16[128,8192]{1,0:T(8,128)(2,1)} %bitcast.61.grad_ref, bf16[8,32,32,256]{3,2,1,0:T(8,128)(2,1)S(1)} %bitcast.140, s32[32]{0:T(128)S(1)} %and_or_fusion.refs_0_, f32[128,256]{1,0:T(8,128)S(1)} %shard_map.30.refs_1_), custom_call_target="tpu_custom_call" | custom-call | flops 536870912 | bytes 6291456 | tf_op jit(solution)/shard_map/pallas_call | solution.py:108
  (98 shorter events, 87.1 us)
Async XLA Ops:
  8.9 67.9 %all-to-all-start = ((bf16[32,32,256]{2,1,0:T(8,128)(2,1)}), bf16[32,32,256]{2,1,0:T(8,128)(2,1)S(1)}, u32[]{:S(2)}, u32[]{:S(2)}) async-start(bf16[32,32,256]{2,1,0:T(8,128)(2,1)} %copy.18), calls=%async_computation | async-start | bytes 1048576 | tf_op jit(solution)/shard_map/all_to_all | solution.py:141
  20.3 12.2 %collective-permute-start = (bf16[256,256]{1,0:T(8,128)(2,1)S(1)}, bf16[256,256]{1,0:T(8,128)(2,1)S(1)}, u32[]{:S(2)}, u32[]{:S(2)}) collective-permute-start(bf16[256,256]{1,0:T(8,128)(2,1)S(1)} %copy-done.5), channel_id=1, source_target_pairs={{0,32},{16,48},{32,0},{48,16},{64,96},{80,112},{96,64},{112,80},{1... | collective-permute-start | bytes 393224 | tf_op jit(solution)/shard_map/ppermute | solution.py:19
  23.6 19.5 %collective-permute-start.1 = (bf16[256,256]{1,0:T(8,128)(2,1)S(1)}, bf16[256,256]{1,0:T(8,128)(2,1)S(1)}, u32[]{:S(2)}, u32[]{:S(2)}) collective-permute-start(bf16[256,256]{1,0:T(8,128)(2,1)S(1)} %copy-done.5), channel_id=1, source_target_pairs={{0,64},{16,80},{32,96},{48,112},{64,0},{80,16},{96,32},{112,48},{1... | collective-permute-start | bytes 393224 | tf_op jit(solution)/shard_map/ppermute | solution.py:19
  27.6 15.5 %collective-permute-start.2 = (bf16[256,256]{1,0:T(8,128)(2,1)S(1)}, bf16[256,256]{1,0:T(8,128)(2,1)S(1)}, u32[]{:S(2)}, u32[]{:S(2)}) collective-permute-start(bf16[256,256]{1,0:T(8,128)(2,1)S(1)} %copy-done.5), channel_id=1, source_target_pairs={{0,96},{16,112},{32,64},{48,80},{64,32},{80,48},{96,0},{112,16},{1... | collective-permute-start | bytes 393224 | tf_op jit(solution)/shard_map/ppermute | solution.py:19
  43.1 14.0 %collective-permute-start.3 = (bf16[4,256,256]{2,1,0:T(8,128)(2,1)S(1)}, bf16[4,256,256]{2,1,0:T(8,128)(2,1)S(1)}, u32[]{:S(2)}, u32[]{:S(2)}) collective-permute-start(bf16[4,256,256]{2,1,0:T(8,128)(2,1)S(1)} %get-tuple-element.21), channel_id=1, source_target_pairs={{0,128},{16,144},{32,160},{48,176},{64,192},{80,208},{96,224},{112... | collective-permute-start | bytes 1572872 | tf_op jit(solution)/shard_map/ppermute | solution.py:19
  46.3 24.3 %collective-permute-start.4 = (bf16[4,256,256]{2,1,0:T(8,128)(2,1)S(1)}, bf16[4,256,256]{2,1,0:T(8,128)(2,1)S(1)}, u32[]{:S(2)}, u32[]{:S(2)}) collective-permute-start(bf16[4,256,256]{2,1,0:T(8,128)(2,1)S(1)} %get-tuple-element.21), channel_id=1, source_target_pairs={{0,256},{16,272},{32,288},{48,304},{64,320},{80,336},{96,352},{112... | collective-permute-start | bytes 1572872 | tf_op jit(solution)/shard_map/ppermute | solution.py:19
  50.6 25.9 %collective-permute-start.5 = (bf16[4,256,256]{2,1,0:T(8,128)(2,1)S(1)}, bf16[4,256,256]{2,1,0:T(8,128)(2,1)S(1)}, u32[]{:S(2)}, u32[]{:S(2)}) collective-permute-start(bf16[4,256,256]{2,1,0:T(8,128)(2,1)S(1)} %get-tuple-element.21), channel_id=1, source_target_pairs={{0,384},{16,400},{32,416},{48,432},{64,448},{80,464},{96,480},{112... | collective-permute-start | bytes 1572872 | tf_op jit(solution)/shard_map/ppermute | solution.py:19
  104.9 23.1 %collective-permute-start.7 = (bf16[8,4096]{1,0:T(8,128)(2,1)S(1)}, bf16[8,4096]{1,0:T(8,128)(2,1)S(1)}, u32[]{:S(2)}, u32[]{:S(2)}) collective-permute-start(bf16[8,4096]{1,0:T(8,128)(2,1)S(1)} %get-tuple-element.30), channel_id=1, source_target_pairs={{0,32},{16,48},{32,0},{48,16},{64,96},{80,112},{96,64},{112,80},{1... | collective-permute-start | bytes 196616 | tf_op jit(solution)/shard_map/ppermute | solution.py:19
  106.9 21.1 %collective-permute-start.8 = (bf16[8,4096]{1,0:T(8,128)(2,1)S(1)}, bf16[8,4096]{1,0:T(8,128)(2,1)S(1)}, u32[]{:S(2)}, u32[]{:S(2)}) collective-permute-start(bf16[8,4096]{1,0:T(8,128)(2,1)S(1)} %get-tuple-element.30), channel_id=1, source_target_pairs={{0,64},{16,80},{32,96},{48,112},{64,0},{80,16},{96,32},{112,48},{1... | collective-permute-start | bytes 196616 | tf_op jit(solution)/shard_map/ppermute | solution.py:19
  110.2 17.8 %collective-permute-start.9 = (bf16[8,4096]{1,0:T(8,128)(2,1)S(1)}, bf16[8,4096]{1,0:T(8,128)(2,1)S(1)}, u32[]{:S(2)}, u32[]{:S(2)}) collective-permute-start(bf16[8,4096]{1,0:T(8,128)(2,1)S(1)} %get-tuple-element.30), channel_id=1, source_target_pairs={{0,96},{16,112},{32,64},{48,80},{64,32},{80,48},{96,0},{112,16},{1... | collective-permute-start | bytes 196616 | tf_op jit(solution)/shard_map/ppermute | solution.py:19
  115.3 42.0 %all-to-all-start.2 = ((bf16[16,8,4096]{2,1,0:T(8,128)(2,1)}), bf16[16,8,4096]{2,1,0:T(8,128)(2,1)S(1)}, u32[]{:S(2)}, u32[]{:S(2)}) async-start(bf16[16,8,4096]{2,1,0:T(8,128)(2,1)} %broadcast_in_dim.5), calls=%async_computation.2 | async-start | bytes 2097152 | tf_op jit(solution)/shard_map/all_to_all | solution.py:162
  128.1 9.6 %collective-permute-start.10 = (bf16[4,8,4096]{2,1,0:T(8,128)(2,1)S(1)}, bf16[4,8,4096]{2,1,0:T(8,128)(2,1)S(1)}, u32[]{:S(2)}, u32[]{:S(2)}) collective-permute-start(bf16[4,8,4096]{2,1,0:T(8,128)(2,1)S(1)} %get-tuple-element.28), channel_id=1, source_target_pairs={{0,128},{16,144},{32,160},{48,176},{64,192},{80,208},{96,224},{112... | collective-permute-start | bytes 786440 | tf_op jit(solution)/shard_map/ppermute | solution.py:19
  130.3 12.9 %collective-permute-start.11 = (bf16[4,8,4096]{2,1,0:T(8,128)(2,1)S(1)}, bf16[4,8,4096]{2,1,0:T(8,128)(2,1)S(1)}, u32[]{:S(2)}, u32[]{:S(2)}) collective-permute-start(bf16[4,8,4096]{2,1,0:T(8,128)(2,1)S(1)} %get-tuple-element.28), channel_id=1, source_target_pairs={{0,256},{16,272},{32,288},{48,304},{64,320},{80,336},{96,352},{112... | collective-permute-start | bytes 786440 | tf_op jit(solution)/shard_map/ppermute | solution.py:19
  134.0 15.6 %collective-permute-start.12 = (bf16[4,8,4096]{2,1,0:T(8,128)(2,1)S(1)}, bf16[4,8,4096]{2,1,0:T(8,128)(2,1)S(1)}, u32[]{:S(2)}, u32[]{:S(2)}) collective-permute-start(bf16[4,8,4096]{2,1,0:T(8,128)(2,1)S(1)} %get-tuple-element.28), channel_id=1, source_target_pairs={{0,384},{16,400},{32,416},{48,432},{64,448},{80,464},{96,480},{112... | collective-permute-start | bytes 786440 | tf_op jit(solution)/shard_map/ppermute | solution.py:19
  159.2 14.0 %collective-permute-start.14 = (bf16[4,4,8,4096]{3,2,1,0:T(8,128)(2,1)}, bf16[4,4,8,4096]{3,2,1,0:T(8,128)(2,1)}, u32[]{:S(2)}, u32[]{:S(2)}) collective-permute-start(bf16[4,4,8,4096]{3,2,1,0:T(8,128)(2,1)} %bitcast.32), channel_id=1, source_target_pairs={{0,16},{16,0},{32,48},{48,32},{64,80},{80,64},{96,112},{112,96},{1... | collective-permute-start | bytes 3145736 | tf_op jit(solution)/shard_map/ppermute | solution.py:19
  166.3 36.2 %all-to-all-start.3 = ((bf16[16,8,4096]{2,1,0:T(8,128)(2,1)}), bf16[16,8,4096]{2,1,0:T(8,128)(2,1)S(1)}, u32[]{:S(2)}, u32[]{:S(2)}) async-start(bf16[16,8,4096]{2,1,0:T(8,128)(2,1)} %fusion.3), calls=%async_computation.3 | async-start | bytes 2097152 | tf_op jit(solution)/shard_map/all_to_all | solution.py:189
  172.7 95.6 %all-gather.3.cloned.1.call-start = ((), (), s32[]{:S(2)}) async-start(), calls=%async_computation.4 | async-start | bytes 4718592 | tf_op jit(solution)/shard_map/all_gather | solution.py:192
  175.6 26.9 %collective-permute-start.15 = (bf16[4,8,4096]{2,1,0:T(8,128)(2,1)}, bf16[4,8,4096]{2,1,0:T(8,128)(2,1)S(1)}, u32[]{:S(2)}, u32[]{:S(2)}) collective-permute-start(bf16[4,8,4096]{2,1,0:T(8,128)(2,1)} %get-tuple-element.15), channel_id=1, source_target_pairs={{0,128},{16,144},{32,160},{48,176},{64,192},{80,208},{96,224},{112... | collective-permute-start | bytes 786440 | tf_op jit(solution)/shard_map/ppermute | solution.py:19
  177.5 25.0 %collective-permute-start.16 = (bf16[4,8,4096]{2,1,0:T(8,128)(2,1)}, bf16[4,8,4096]{2,1,0:T(8,128)(2,1)S(1)}, u32[]{:S(2)}, u32[]{:S(2)}) collective-permute-start(bf16[4,8,4096]{2,1,0:T(8,128)(2,1)} %get-tuple-element.17), channel_id=1, source_target_pairs={{0,256},{16,272},{32,288},{48,304},{64,320},{80,336},{96,352},{112... | collective-permute-start | bytes 786440 | tf_op jit(solution)/shard_map/ppermute | solution.py:19
  182.2 20.3 %collective-permute-start.17 = (bf16[4,8,4096]{2,1,0:T(8,128)(2,1)S(1)}, bf16[4,8,4096]{2,1,0:T(8,128)(2,1)}, u32[]{:S(2)}, u32[]{:S(2)}) collective-permute-start(bf16[4,8,4096]{2,1,0:T(8,128)(2,1)S(1)} %get-tuple-element.16), channel_id=1, source_target_pairs={{0,384},{16,400},{32,416},{48,432},{64,448},{80,464},{96,480},{112... | collective-permute-start | bytes 786440 | tf_op jit(solution)/shard_map/ppermute | solution.py:19
  230.9 10.3 %collective-permute-start.24 = (bf16[4,8,8192]{2,1,0:T(8,128)(2,1)S(1)}, bf16[4,8,8192]{2,1,0:T(8,128)(2,1)S(1)}, u32[]{:S(2)}, u32[]{:S(2)}) collective-permute-start(bf16[4,8,8192]{2,1,0:T(8,128)(2,1)S(1)} %get-tuple-element.19), channel_id=1, source_target_pairs={{0,128},{16,144},{32,160},{48,176},{64,192},{80,208},{96,224},{112... | collective-permute-start | bytes 1572872 | tf_op jit(solution)/shard_map/ppermute | solution.py:19
  233.8 20.3 %collective-permute-start.25 = (bf16[4,8,8192]{2,1,0:T(8,128)(2,1)S(1)}, bf16[4,8,8192]{2,1,0:T(8,128)(2,1)S(1)}, u32[]{:S(2)}, u32[]{:S(2)}) collective-permute-start(bf16[4,8,8192]{2,1,0:T(8,128)(2,1)S(1)} %get-tuple-element.19), channel_id=1, source_target_pairs={{0,256},{16,272},{32,288},{48,304},{64,320},{80,336},{96,352},{112... | collective-permute-start | bytes 1572872 | tf_op jit(solution)/shard_map/ppermute | solution.py:19
  237.9 24.8 %collective-permute-start.26 = (bf16[4,8,8192]{2,1,0:T(8,128)(2,1)S(1)}, bf16[4,8,8192]{2,1,0:T(8,128)(2,1)S(1)}, u32[]{:S(2)}, u32[]{:S(2)}) collective-permute-start(bf16[4,8,8192]{2,1,0:T(8,128)(2,1)S(1)} %get-tuple-element.19), channel_id=1, source_target_pairs={{0,384},{16,400},{32,416},{48,432},{64,448},{80,464},{96,480},{112... | collective-permute-start | bytes 1572872 | tf_op jit(solution)/shard_map/ppermute | solution.py:19
  262.9 10.2 %collective-permute-start.27 = (bf16[4,4,8,8192]{3,2,1,0:T(8,128)(2,1)S(1)}, bf16[4,4,8,8192]{3,2,1,0:T(8,128)(2,1)}, u32[]{:S(2)}, u32[]{:S(2)}) collective-permute-start(bf16[4,4,8,8192]{3,2,1,0:T(8,128)(2,1)S(1)} %pad_maximum_fusion.1), channel_id=1, source_target_pairs={{0,16},{16,0},{32,48},{48,32},{64,80},{80,64},{96,112},{112,96},{1... | collective-permute-start | bytes 6291464 | tf_op jit(solution)/shard_map/ppermute | solution.py:19
  (14 other events, 98.1 us)
Sparse Core Ops, SparseCore 0:
  202.6 55.4 all-gather.2

commit v4 on v3

--- a/solution.py
+++ b/solution.py
@@ -13,10 +13,15 @@
 DP = 32
 MP = 16
 Y = 8
+GROUPS = [list(range(Y)), list(range(Y, MP))]
 
 
 def swap(array, step):
     return lax.ppermute(array, "dp", [(i, i ^ step) for i in range(DP)])
+
+
+def partner(array):
+    return lax.ppermute(array, "mp", [(i, i ^ Y) for i in range(MP)])
 
 
 def gather_dp(block):
@@ -25,12 +30,13 @@
     return along_x, swap(along_x, 1)
 
 
-def add_dp(own, other):
+def add_dp(own, other, later):
     both = (own + swap(other, 1).astype(jnp.float32)).astype(jnp.bfloat16)
     parts = [both[0]] + [swap(both[k], 8 * k) for k in (1, 2, 3)]
     along_x = sum(part.astype(jnp.float32) for part in parts).astype(jnp.bfloat16)
+    along_x, later = lax.optimization_barrier((along_x, later))
     parts = [along_x[0]] + [swap(along_x[k], 2 * k) for k in (1, 2, 3)]
-    return sum(part.astype(jnp.float32) for part in parts)
+    return sum(part.astype(jnp.float32) for part in parts), later
 
 
 def project_kernel(last, order_ref, inputs_ref, weight_ref, *refs):
@@ -138,11 +144,8 @@
     share = views * images // Y
     mine = lax.dynamic_slice_in_dim(flat, lax.rem(model_index, Y) * share, share, axis=0)
     pieces = mine.reshape(share, DP, rows).transpose(1, 0, 2)
-    slices = lax.all_to_all(pieces, "dp", split_axis=0, concat_axis=0)
-
     along_z = jnp.stack([weight] + [swap(weight, 2 * k) for k in (1, 2, 3)])
     weight_own = jnp.stack([along_z] + [swap(along_z, 8 * k) for k in (1, 2, 3)])
-    weight_own, slices = lax.optimization_barrier((weight_own, slices))
     weight_other = swap(weight_own, 1)
     half = (DP // 2, rows, feat)
     projected = project(order[: DP // 2], flat, weight_own.reshape(half))
@@ -158,9 +161,12 @@
     normed = (centered * inverse).astype(jnp.bfloat16).transpose(2, 1, 0, 3).reshape(views, block, total)
     inverse = inverse.reshape(block, views).T[:, :, None]
 
-    copies = jnp.broadcast_to(normed[1][None], (MP, block, total))
-    columns_b = lax.all_to_all(copies, "mp", split_axis=0, concat_axis=0).reshape(MP * block, total)
-    rows_own, rows_other = (part.reshape(feat // 2, total) for part in gather_dp(normed[0]))
+    first, second, pieces = lax.optimization_barrier((normed[0], normed[1], pieces))
+    slices = lax.all_to_all(pieces, "dp", split_axis=0, concat_axis=0)
+    pair = jnp.stack([second, partner(second)])
+    columns_b = lax.all_gather(pair, "mp", axis=0, axis_index_groups=GROUPS)
+    columns_b = columns_b.reshape(MP * block, total)
+    rows_own, rows_other = (part.reshape(feat // 2, total) for part in gather_dp(first))
 
     def gradient_of(rows_a, with_diagonal):
         correlation = (
@@ -171,12 +177,13 @@
         if with_diagonal:
             row = lax.broadcasted_iota(jnp.int32, correlation.shape, 0)
             column = lax.broadcasted_iota(jnp.int32, correlation.shape, 1)
-            diagonal = (row < block) & (column == model_index * block + row)
+            diagonal = (row < block) & (column == lax.rem(model_index, Y) * 2 * block + row)
             inner = inner + diagonal.astype(jnp.float32) * (2.0 * (correlation - 1.0) - inner)
         return (loss_scale * inner).astype(jnp.bfloat16)
 
     corr_own = gradient_of(rows_own, True)
     corr_other = gradient_of(rows_other, False)
+    corr_other, slices = lax.optimization_barrier((corr_other, slices))
 
     def times(lhs, rhs, dims):
         return lax.dot_general(lhs, rhs, (dims, ((), ())), preferred_element_type=jnp.float32) / total
@@ -186,17 +193,15 @@
         times(corr_own, rows_own, ((0,), (0,))) + times(corr_other, rows_other, ((0,), (0,)))
     ).astype(jnp.bfloat16)
     terms_own = times(corr_own, columns_b, ((1,), (0,)))
-    terms_b = lax.all_to_all(terms_b.reshape(MP, block, total), "mp", split_axis=0, concat_axis=0)
-    terms_b, slices = lax.optimization_barrier((terms_b, slices))
-    groups = [list(range(Y)), list(range(Y, MP))]
-    columns = lax.all_gather(slices, "mp", axis=0, axis_index_groups=groups)
+    terms_b = lax.all_to_all(
+        terms_b.reshape(Y, 2, block, total), "mp", split_axis=0, concat_axis=0, axis_index_groups=GROUPS
+    )
     shape = (4, 4, block, total)
-    grads = jnp.stack(
-        [
-            add_dp(terms_own.reshape(shape), terms_other.reshape(shape)),
-            jnp.sum(terms_b.astype(jnp.float32), axis=0),
-        ]
-    )
+    grad_a, slices = add_dp(terms_own.reshape(shape), terms_other.reshape(shape), slices)
+    columns = lax.all_gather(slices, "mp", axis=0, axis_index_groups=GROUPS)
+    terms_b = jnp.sum(terms_b.astype(jnp.float32), axis=0)
+    grad_b = terms_b[0] + partner(terms_b[1].astype(jnp.bfloat16)).astype(jnp.float32)
+    grads = jnp.stack([grad_a, grad_b])
     wide = normed.astype(jnp.float32)
     grad_mean = jnp.sum(grads, axis=2, keepdims=True) / total
     cross_mean = jnp.sum(grads * wide, axis=2, keepdims=True) / total

time: 291 us -> 285 us (0.979); the launches traced: 286 us -> 284 us
  waiting for transfers between devices: 102 us -> 125 us
  blocking collectives: 16.6 us -> 0 us
  starting transfers between devices: 123 us -> 113 us
    all_to_all x1 -> x0, blocking collectives: 16.6 us -> none  [per_device(): lax.all_to_all(projected.reshape(DP, block, views * images), 'dp', split_...]
    all_to_all x2, waiting for transfers between devices: 20 us -> 35.1 us  [the longest x1 25.1 us: per_device(): lax.all_to_all(terms_b.reshape(Y, 2, block, total), 'mp', split_axis=0, c...]
    ppermute x28, waiting for transfers between devices: 81.9 us -> 68.3 us  [swap(): return lax.ppermute(array, 'dp', [(i, i ^ step) for i in range(DP)])]
    all_to_all x1, waiting for transfers between devices: 0.01 us -> 10.5 us  [per_device(): slices = lax.all_to_all(pieces, 'dp', split_axis=0, concat_axis=0)]
    ppermute x0 -> x2, starting transfers between devices: none -> 9.6 us  [partner(): return lax.ppermute(array, 'mp', [(i, i ^ Y) for i in range(MP)])]
    ppermute x28, starting transfers between devices: 92.7 us -> 85.4 us  [swap(): return lax.ppermute(array, 'dp', [(i, i ^ step) for i in range(DP)])]
    all_to_all x1, starting transfers between devices: 11.4 us -> 4.4 us  [per_device(): slices = lax.all_to_all(pieces, 'dp', split_axis=0, concat_axis=0)]
    ppermute x0 -> x2, waiting for transfers between devices: none -> 6.92 us  [partner(): return lax.ppermute(array, 'mp', [(i, i ^ Y) for i in range(MP)])]
  transfers between devices with their start and end apart: 32 -> 35, of which waited for: 17 -> 22; matrix products, arithmetic and copies ran while one was open for 3% -> 3% of each run, Pallas kernels for 1% -> 1%
where the time goes in v4:
time: 285 us; the launch traced here: 284 us
  waiting for transfers between devices  125 us (44%)
  starting transfers between devices  113 us (40%)
  between operations  14 us (5%)
  Pallas kernels  13 us (5%)
  local copies, waits for them, and re-layouts  7.67 us (3%)
  matrix products  5.99 us (2%)
  other arithmetic  5.13 us (2%)
    ppermute x28, starting transfers between devices, swap(): return lax.ppermute(array, 'dp', [(i, i ^ step) for i in range(DP)])  85.4 us
    ppermute x28, waiting for transfers between devices, swap(): return lax.ppermute(array, 'dp', [(i, i ^ step) for i in range(DP)])  68.3 us
    all_to_all x1, waiting for transfers between devices, per_device(): lax.all_to_all(terms_b.reshape(Y, 2, block, total), 'mp', split_axis=0, c...  25.1 us
    all_to_all x1, waiting for transfers between devices, per_device(): slices = lax.all_to_all(pieces, 'dp', split_axis=0, concat_axis=0)  10.5 us
    all_to_all x1, waiting for transfers between devices, per_device(): lax.all_to_all(projected.reshape(DP, block, views * images), 'dp', split_...  10 us
    ppermute x2, starting transfers between devices, partner(): return lax.ppermute(array, 'mp', [(i, i ^ Y) for i in range(MP)])  9.6 us
    pallas_call x2, Pallas kernels, weight_half(): pl.pallas_call(functools.partial(weight_kernel, last), grid=(2, devices /...  8.66 us
    ppermute x2, waiting for transfers between devices, partner(): return lax.ppermute(array, 'mp', [(i, i ^ Y) for i in range(MP)])  6.92 us
  transfers between devices with their start and end apart: 35, of which 22 were waited for; matrix products, arithmetic and copies ran while one was open for 3% of the time, Pallas kernels for 1%

profile of v4, /device:TPU:1, one launch (start us, length us, event | category | flops | bytes accessed | tf_op | source)
XLA Modules:
  0.0 283.9 jit_solution(2891724717178597830)
XLA Ops:
  6.5 4.8 %collective-permute-start = (bf16[256,256]{1,0:T(8,128)(2,1)}, bf16[256,256]{1,0:T(8,128)(2,1)S(1)}, u32[]{:S(2)}, u32[]{:S(2)}) collective-permute-start(bf16[256,256]{1,0:T(8,128)(2,1)} %param.3), channel_id=1, source_target_pairs={{0,32},{16,48},{32,0},{48,16},{64,96},{80,112},{96,64},{112,80},{1... | collective-permute-start | bytes 393224 | tf_op jit(solution)/shard_map/ppermute | solution.py:20
  11.4 5.5 %collective-permute-start.2 = (bf16[256,256]{1,0:T(8,128)(2,1)}, bf16[256,256]{1,0:T(8,128)(2,1)S(1)}, u32[]{:S(2)}, u32[]{:S(2)}) collective-permute-start(bf16[256,256]{1,0:T(8,128)(2,1)} %param.3), channel_id=1, source_target_pairs={{0,96},{16,112},{32,64},{48,80},{64,32},{80,48},{96,0},{112,16},{1... | collective-permute-start | bytes 393224 | tf_op jit(solution)/shard_map/ppermute | solution.py:20
  20.5 8.9 %collective-permute-done.1 = bf16[256,256]{1,0:T(8,128)(2,1)S(1)} collective-permute-done((bf16[256,256]{1,0:T(8,128)(2,1)}, bf16[256,256]{1,0:T(8,128)(2,1)S(1)}, u32[]{:S(2)}, u32[]{:S(2)}) %collective-permute-start.1) | collective-permute-done | bytes 131104 | tf_op jit(solution)/shard_map/ppermute | solution.py:20
  30.4 4.4 %collective-permute-start.4 = (bf16[4,256,256]{2,1,0:T(8,128)(2,1)S(1)}, bf16[4,256,256]{2,1,0:T(8,128)(2,1)S(1)}, u32[]{:S(2)}, u32[]{:S(2)}) collective-permute-start(bf16[4,256,256]{2,1,0:T(8,128)(2,1)S(1)} %get-tuple-element.25), channel_id=1, source_target_pairs={{0,256},{16,272},{32,288},{48,304},{64,320},{80,336},{96,352},{112... | collective-permute-start | bytes 1572872 | tf_op jit(solution)/shard_map/ppermute | solution.py:20
  39.5 6.4 %collective-permute-done.4 = bf16[4,256,256]{2,1,0:T(8,128)(2,1)S(1)} collective-permute-done((bf16[4,256,256]{2,1,0:T(8,128)(2,1)S(1)}, bf16[4,256,256]{2,1,0:T(8,128)(2,1)S(1)}, u32[]{:S(2)}, u32[]{:S(2)}) %collective-permute-start.4) | collective-permute-done | bytes 524320 | tf_op jit(solution)/shard_map/ppermute | solution.py:20
  45.9 11.5 %collective-permute-done.3 = bf16[4,256,256]{2,1,0:T(8,128)(2,1)S(1)} collective-permute-done((bf16[4,256,256]{2,1,0:T(8,128)(2,1)S(1)}, bf16[4,256,256]{2,1,0:T(8,128)(2,1)S(1)}, u32[]{:S(2)}, u32[]{:S(2)}) %collective-permute-start.3) | collective-permute-done | bytes 524320 | tf_op jit(solution)/shard_map/ppermute | solution.py:20
  68.6 6.5 %all-to-all-start = ((f32[32,8,256]{2,1,0:T(8,128)}), f32[32,8,256]{2,1,0:T(8,128)S(1)}, u32[]{:S(2)}, u32[]{:S(2)}) async-start(f32[32,8,256]{2,1,0:T(8,128)} %bitcast.11), calls=%async_computation | async-start | bytes 524288 | tf_op jit(solution)/shard_map/all_to_all | solution.py:154
  76.4 10.0 %all-to-all-done = f32[32,8,256]{2,1,0:T(8,128)S(1)} async-done(((f32[32,8,256]{2,1,0:T(8,128)}), f32[32,8,256]{2,1,0:T(8,128)S(1)}, u32[]{:S(2)}, u32[]{:S(2)}) %all-to-all-start) | async-done | bytes 262176 | tf_op jit(solution)/shard_map/all_to_all | solution.py:154
  86.9 7.7 %collective-permute-start.13 = (bf16[8,4096]{1,0:T(8,128)(2,1)S(1)}, bf16[8,4096]{1,0:T(8,128)(2,1)S(1)}, u32[]{:S(2)}, u32[]{:S(2)}) collective-permute-start(bf16[8,4096]{1,0:T(8,128)(2,1)S(1)} %get-tuple-element.13), channel_id=1, source_target_pairs={{0,8},{1,9},{2,10},{3,11},{4,12},{5,13},{6,14},{7,15},{8,0},{9,1},... | collective-permute-start | bytes 196616 | tf_op jit(solution)/shard_map/ppermute | solution.py:24
  99.6 4.3 %collective-permute-start.7 = (bf16[8,4096]{1,0:T(8,128)(2,1)S(1)}, bf16[8,4096]{1,0:T(8,128)(2,1)S(1)}, u32[]{:S(2)}, u32[]{:S(2)}) collective-permute-start(bf16[8,4096]{1,0:T(8,128)(2,1)S(1)} %get-tuple-element.12), channel_id=1, source_target_pairs={{0,32},{16,48},{32,0},{48,16},{64,96},{80,112},{96,64},{112,80},{1... | collective-permute-start | bytes 196616 | tf_op jit(solution)/shard_map/ppermute | solution.py:20
  117.0 5.0 %collective-permute-done.10 = bf16[4,8,4096]{2,1,0:T(8,128)(2,1)S(1)} collective-permute-done((bf16[4,8,4096]{2,1,0:T(8,128)(2,1)S(1)}, bf16[4,8,4096]{2,1,0:T(8,128)(2,1)S(1)}, u32[]{:S(2)}, u32[]{:S(2)}) %collective-permute-start.10) | collective-permute-done | bytes 262176 | tf_op jit(solution)/shard_map/ppermute | solution.py:20
  128.1 4.4 %all-to-all-start.1 = ((bf16[32,32,256]{2,1,0:T(8,128)(2,1)}), bf16[32,32,256]{2,1,0:T(8,128)(2,1)}, u32[]{:S(2)}, u32[]{:S(2)}) async-start(bf16[32,32,256]{2,1,0:T(8,128)(2,1)} %copy.15), calls=%async_computation.1 | async-start | bytes 1048576 | tf_op jit(solution)/shard_map/all_to_all | solution.py:165
  132.6 4.6 %all-gather.5.cloned.1.call-done = bf16[16,8,4096]{2,1,0:T(8,128)(2,1)} async-done(((bf16[2,8,4096]{2,1,0:T(8,128)(2,1)}), bf16[16,8,4096]{2,1,0:T(8,128)(2,1)}) %all-gather.5.cloned.1.call-update) | async-done | bytes 1048592 | tf_op jit(solution)/shard_map/all_gather | solution.py:167
  138.9 10.5 %all-to-all-done.1 = bf16[32,32,256]{2,1,0:T(8,128)(2,1)} async-done(((bf16[32,32,256]{2,1,0:T(8,128)(2,1)}), bf16[32,32,256]{2,1,0:T(8,128)(2,1)}, u32[]{:S(2)}, u32[]{:S(2)}) %all-to-all-start.1) | async-done | bytes 524320 | tf_op jit(solution)/shard_map/all_to_all | solution.py:165
  168.5 6.8 %all-to-all-start.2 = ((bf16[8,2,8,4096]{3,2,1,0:T(8,128)(2,1)}), bf16[8,2,8,4096]{3,2,1,0:T(8,128)(2,1)S(1)}, u32[]{:S(2)}, u32[]{:S(2)}) async-start(bf16[8,2,8,4096]{3,2,1,0:T(8,128)(2,1)} %bitcast.44), calls=%async_computation.2 | async-start | bytes 2097152 | tf_op jit(solution)/shard_map/all_to_all | solution.py:196
  185.2 25.1 %all-to-all-done.2 = bf16[8,2,8,4096]{3,2,1,0:T(8,128)(2,1)S(1)} async-done(((bf16[8,2,8,4096]{3,2,1,0:T(8,128)(2,1)}), bf16[8,2,8,4096]{3,2,1,0:T(8,128)(2,1)S(1)}, u32[]{:S(2)}, u32[]{:S(2)}) %all-to-all-start.2) | async-done | bytes 1048608 | tf_op jit(solution)/shard_map/all_to_all | solution.py:196
  212.4 6.9 %collective-permute-done.22 = bf16[8,4096]{1,0:T(8,128)(2,1)S(1)} collective-permute-done((bf16[8,4096]{1,0:T(8,128)(2,1)S(1)}, bf16[8,4096]{1,0:T(8,128)(2,1)S(1)}, u32[]{:S(2)}, u32[]{:S(2)}) %collective-permute-start.22) | collective-permute-done | bytes 65568 | tf_op jit(solution)/shard_map/ppermute | solution.py:24
  223.7 5.4 %collective-permute-start.23 = (bf16[8,8192]{1,0:T(8,128)(2,1)S(1)}, bf16[8,8192]{1,0:T(8,128)(2,1)S(1)}, u32[]{:S(2)}, u32[]{:S(2)}) collective-permute-start(bf16[8,8192]{1,0:T(8,128)(2,1)S(1)} %bitcast.161), channel_id=1, source_target_pairs={{0,32},{16,48},{32,0},{48,16},{64,96},{80,112},{96,64},{112,80},{1... | collective-permute-start | bytes 393224 | tf_op jit(solution)/shard_map/ppermute | solution.py:20
  229.1 5.8 %collective-permute-done.24 = bf16[8,8192]{1,0:T(8,128)(2,1)S(1)} collective-permute-done((bf16[8,8192]{1,0:T(8,128)(2,1)S(1)}, bf16[8,8192]{1,0:T(8,128)(2,1)S(1)}, u32[]{:S(2)}, u32[]{:S(2)}) %collective-permute-start.24) | collective-permute-done | bytes 131104 | tf_op jit(solution)/shard_map/ppermute | solution.py:20
  239.1 4.9 %collective-permute-start.28 = (bf16[4,8,8192]{2,1,0:T(8,128)(2,1)S(1)}, bf16[4,8,8192]{2,1,0:T(8,128)(2,1)S(1)}, u32[]{:S(2)}, u32[]{:S(2)}) collective-permute-start(bf16[4,8,8192]{2,1,0:T(8,128)(2,1)S(1)} %get-tuple-element.23), channel_id=1, source_target_pairs={{0,384},{16,400},{32,416},{48,432},{64,448},{80,464},{96,480},{112... | collective-permute-start | bytes 1572872 | tf_op jit(solution)/shard_map/ppermute | solution.py:20
  244.0 6.0 %collective-permute-done.27 = bf16[4,8,8192]{2,1,0:T(8,128)(2,1)S(1)} collective-permute-done((bf16[4,8,8192]{2,1,0:T(8,128)(2,1)S(1)}, bf16[4,8,8192]{2,1,0:T(8,128)(2,1)S(1)}, u32[]{:S(2)}, u32[]{:S(2)}) %collective-permute-start.27) | collective-permute-done | bytes 524320 | tf_op jit(solution)/shard_map/ppermute | solution.py:20
  250.1 8.5 %collective-permute-done.26 = bf16[4,8,8192]{2,1,0:T(8,128)(2,1)S(1)} collective-permute-done((bf16[4,8,8192]{2,1,0:T(8,128)(2,1)S(1)}, bf16[4,8,8192]{2,1,0:T(8,128)(2,1)S(1)}, u32[]{:S(2)}, u32[]{:S(2)}) %collective-permute-start.26) | collective-permute-done | bytes 524320 | tf_op jit(solution)/shard_map/ppermute | solution.py:20
  258.6 4.9 %collective-permute-done.28 = bf16[4,8,8192]{2,1,0:T(8,128)(2,1)S(1)} collective-permute-done((bf16[4,8,8192]{2,1,0:T(8,128)(2,1)S(1)}, bf16[4,8,8192]{2,1,0:T(8,128)(2,1)S(1)}, u32[]{:S(2)}, u32[]{:S(2)}) %collective-permute-start.28) | collective-permute-done | bytes 524320 | tf_op jit(solution)/shard_map/ppermute | solution.py:20
  271.0 6.1 %shard_map.31 = f32[256,256]{1,0:T(8,128)} custom-call(bf16[128,8192]{1,0:T(8,128)(2,1)} %bitcast.63.grad_ref, bf16[8,32,32,256]{3,2,1,0:T(8,128)(2,1)S(1)} %bitcast.149, s32[32]{0:T(128)S(1)} %and_or_fusion.refs_0_, f32[128,256]{1,0:T(8,128)S(1)} %shard_map.30.refs_1_), custom_call_target="tpu_custom_call" | custom-call | flops 536870912 | bytes 6291456 | tf_op jit(solution)/shard_map/pallas_call | solution.py:114
  (100 shorter events, 95.0 us)
Async XLA Ops:
  6.5 12.6 %collective-permute-start = (bf16[256,256]{1,0:T(8,128)(2,1)}, bf16[256,256]{1,0:T(8,128)(2,1)S(1)}, u32[]{:S(2)}, u32[]{:S(2)}) collective-permute-start(bf16[256,256]{1,0:T(8,128)(2,1)} %param.3), channel_id=1, source_target_pairs={{0,32},{16,48},{32,0},{48,16},{64,96},{80,112},{96,64},{112,80},{1... | collective-permute-start | bytes 393224 | tf_op jit(solution)/shard_map/ppermute | solution.py:20
  16.9 12.5 %collective-permute-start.1 = (bf16[256,256]{1,0:T(8,128)(2,1)}, bf16[256,256]{1,0:T(8,128)(2,1)S(1)}, u32[]{:S(2)}, u32[]{:S(2)}) collective-permute-start(bf16[256,256]{1,0:T(8,128)(2,1)} %param.3), channel_id=1, source_target_pairs={{0,64},{16,80},{32,96},{48,112},{64,0},{80,16},{96,32},{112,48},{1... | collective-permute-start | bytes 393224 | tf_op jit(solution)/shard_map/ppermute | solution.py:20
  30.4 15.4 %collective-permute-start.4 = (bf16[4,256,256]{2,1,0:T(8,128)(2,1)S(1)}, bf16[4,256,256]{2,1,0:T(8,128)(2,1)S(1)}, u32[]{:S(2)}, u32[]{:S(2)}) collective-permute-start(bf16[4,256,256]{2,1,0:T(8,128)(2,1)S(1)} %get-tuple-element.25), channel_id=1, source_target_pairs={{0,256},{16,272},{32,288},{48,304},{64,320},{80,336},{96,352},{112... | collective-permute-start | bytes 1572872 | tf_op jit(solution)/shard_map/ppermute | solution.py:20
  34.8 22.5 %collective-permute-start.3 = (bf16[4,256,256]{2,1,0:T(8,128)(2,1)S(1)}, bf16[4,256,256]{2,1,0:T(8,128)(2,1)S(1)}, u32[]{:S(2)}, u32[]{:S(2)}) collective-permute-start(bf16[4,256,256]{2,1,0:T(8,128)(2,1)S(1)} %get-tuple-element.25), channel_id=1, source_target_pairs={{0,128},{16,144},{32,160},{48,176},{64,192},{80,208},{96,224},{112... | collective-permute-start | bytes 1572872 | tf_op jit(solution)/shard_map/ppermute | solution.py:20
  37.0 21.9 %collective-permute-start.5 = (bf16[4,256,256]{2,1,0:T(8,128)(2,1)S(1)}, bf16[4,256,256]{2,1,0:T(8,128)(2,1)S(1)}, u32[]{:S(2)}, u32[]{:S(2)}) collective-permute-start(bf16[4,256,256]{2,1,0:T(8,128)(2,1)S(1)} %get-tuple-element.25), channel_id=1, source_target_pairs={{0,384},{16,400},{32,416},{48,432},{64,448},{80,464},{96,480},{112... | collective-permute-start | bytes 1572872 | tf_op jit(solution)/shard_map/ppermute | solution.py:20
  68.6 17.8 %all-to-all-start = ((f32[32,8,256]{2,1,0:T(8,128)}), f32[32,8,256]{2,1,0:T(8,128)S(1)}, u32[]{:S(2)}, u32[]{:S(2)}) async-start(f32[32,8,256]{2,1,0:T(8,128)} %bitcast.11), calls=%async_computation | async-start | bytes 524288 | tf_op jit(solution)/shard_map/all_to_all | solution.py:154
  75.1 62.0 %all-gather.5.cloned.1.call-start = ((), (), s32[]{:S(2)}) async-start(), calls=%async_computation.3 | async-start | bytes 1179648 | tf_op jit(solution)/shard_map/all_gather | solution.py:167
  86.9 17.0 %collective-permute-start.13 = (bf16[8,4096]{1,0:T(8,128)(2,1)S(1)}, bf16[8,4096]{1,0:T(8,128)(2,1)S(1)}, u32[]{:S(2)}, u32[]{:S(2)}) collective-permute-start(bf16[8,4096]{1,0:T(8,128)(2,1)S(1)} %get-tuple-element.13), channel_id=1, source_target_pairs={{0,8},{1,9},{2,10},{3,11},{4,12},{5,13},{6,14},{7,15},{8,0},{9,1},... | collective-permute-start | bytes 196616 | tf_op jit(solution)/shard_map/ppermute | solution.py:24
  108.6 13.4 %collective-permute-start.10 = (bf16[4,8,4096]{2,1,0:T(8,128)(2,1)S(1)}, bf16[4,8,4096]{2,1,0:T(8,128)(2,1)S(1)}, u32[]{:S(2)}, u32[]{:S(2)}) collective-permute-start(bf16[4,8,4096]{2,1,0:T(8,128)(2,1)S(1)} %get-tuple-element.34), channel_id=1, source_target_pairs={{0,128},{16,144},{32,160},{48,176},{64,192},{80,208},{96,224},{112... | collective-permute-start | bytes 786440 | tf_op jit(solution)/shard_map/ppermute | solution.py:20
  112.3 11.5 %collective-permute-start.12 = (bf16[4,8,4096]{2,1,0:T(8,128)(2,1)S(1)}, bf16[4,8,4096]{2,1,0:T(8,128)(2,1)S(1)}, u32[]{:S(2)}, u32[]{:S(2)}) collective-permute-start(bf16[4,8,4096]{2,1,0:T(8,128)(2,1)S(1)} %get-tuple-element.34), channel_id=1, source_target_pairs={{0,384},{16,400},{32,416},{48,432},{64,448},{80,464},{96,480},{112... | collective-permute-start | bytes 786440 | tf_op jit(solution)/shard_map/ppermute | solution.py:20
  128.1 21.2 %all-to-all-start.1 = ((bf16[32,32,256]{2,1,0:T(8,128)(2,1)}), bf16[32,32,256]{2,1,0:T(8,128)(2,1)}, u32[]{:S(2)}, u32[]{:S(2)}) async-start(bf16[32,32,256]{2,1,0:T(8,128)(2,1)} %copy.15), calls=%async_computation.1 | async-start | bytes 1048576 | tf_op jit(solution)/shard_map/all_to_all | solution.py:165
  158.0 17.3 %collective-permute-start.16 = (bf16[4,8,4096]{2,1,0:T(8,128)(2,1)}, bf16[4,8,4096]{2,1,0:T(8,128)(2,1)S(1)}, u32[]{:S(2)}, u32[]{:S(2)}) collective-permute-start(bf16[4,8,4096]{2,1,0:T(8,128)(2,1)} %get-tuple-element.19), channel_id=1, source_target_pairs={{0,128},{16,144},{32,160},{48,176},{64,192},{80,208},{96,224},{112... | collective-permute-start | bytes 786440 | tf_op jit(solution)/shard_map/ppermute | solution.py:20
  160.2 16.4 %collective-permute-start.18 = (bf16[4,8,4096]{2,1,0:T(8,128)(2,1)}, bf16[4,8,4096]{2,1,0:T(8,128)(2,1)S(1)}, u32[]{:S(2)}, u32[]{:S(2)}) collective-permute-start(bf16[4,8,4096]{2,1,0:T(8,128)(2,1)} %get-tuple-element.20), channel_id=1, source_target_pairs={{0,384},{16,400},{32,416},{48,432},{64,448},{80,464},{96,480},{112... | collective-permute-start | bytes 786440 | tf_op jit(solution)/shard_map/ppermute | solution.py:20
  163.2 13.4 %collective-permute-start.17 = (bf16[4,8,4096]{2,1,0:T(8,128)(2,1)S(1)}, bf16[4,8,4096]{2,1,0:T(8,128)(2,1)S(1)}, u32[]{:S(2)}, u32[]{:S(2)}) collective-permute-start(bf16[4,8,4096]{2,1,0:T(8,128)(2,1)S(1)} %get-tuple-element.21), channel_id=1, source_target_pairs={{0,256},{16,272},{32,288},{48,304},{64,320},{80,336},{96,352},{112... | collective-permute-start | bytes 786440 | tf_op jit(solution)/shard_map/ppermute | solution.py:20
  168.5 41.8 %all-to-all-start.2 = ((bf16[8,2,8,4096]{3,2,1,0:T(8,128)(2,1)}), bf16[8,2,8,4096]{3,2,1,0:T(8,128)(2,1)S(1)}, u32[]{:S(2)}, u32[]{:S(2)}) async-start(bf16[8,2,8,4096]{3,2,1,0:T(8,128)(2,1)} %bitcast.44), calls=%async_computation.2 | async-start | bytes 2097152 | tf_op jit(solution)/shard_map/all_to_all | solution.py:196
  175.3 91.0 %all-gather.7.cloned.1.call-start = ((), (), s32[]{:S(2)}) async-start(), calls=%async_computation.4 | async-start | bytes 4718592 | tf_op jit(solution)/shard_map/all_gather | solution.py:201
  176.8 35.6 %collective-permute-start.19 = (bf16[8,4096]{1,0:T(8,128)(2,1)S(1)}, bf16[8,4096]{1,0:T(8,128)(2,1)S(1)}, u32[]{:S(2)}, u32[]{:S(2)}) collective-permute-start(bf16[8,4096]{1,0:T(8,128)(2,1)S(1)} %get-tuple-element.30), channel_id=1, source_target_pairs={{0,32},{16,48},{32,0},{48,16},{64,96},{80,112},{96,64},{112,80},{1... | collective-permute-start | bytes 196616 | tf_op jit(solution)/shard_map/ppermute | solution.py:20
  178.7 33.6 %collective-permute-start.21 = (bf16[8,4096]{1,0:T(8,128)(2,1)S(1)}, bf16[8,4096]{1,0:T(8,128)(2,1)S(1)}, u32[]{:S(2)}, u32[]{:S(2)}) collective-permute-start(bf16[8,4096]{1,0:T(8,128)(2,1)S(1)} %get-tuple-element.31), channel_id=1, source_target_pairs={{0,96},{16,112},{32,64},{48,80},{64,32},{80,48},{96,0},{112,16},{1... | collective-permute-start | bytes 196616 | tf_op jit(solution)/shard_map/ppermute | solution.py:20
  181.6 30.7 %collective-permute-start.20 = (bf16[8,4096]{1,0:T(8,128)(2,1)S(1)}, bf16[8,4096]{1,0:T(8,128)(2,1)S(1)}, u32[]{:S(2)}, u32[]{:S(2)}) collective-permute-start(bf16[8,4096]{1,0:T(8,128)(2,1)S(1)} %get-tuple-element.32), channel_id=1, source_target_pairs={{0,64},{16,80},{32,96},{48,112},{64,0},{80,16},{96,32},{112,48},{1... | collective-permute-start | bytes 196616 | tf_op jit(solution)/shard_map/ppermute | solution.py:20
  221.7 13.2 %collective-permute-start.24 = (bf16[8,8192]{1,0:T(8,128)(2,1)S(1)}, bf16[8,8192]{1,0:T(8,128)(2,1)S(1)}, u32[]{:S(2)}, u32[]{:S(2)}) collective-permute-start(bf16[8,8192]{1,0:T(8,128)(2,1)S(1)} %bitcast.160), channel_id=1, source_target_pairs={{0,64},{16,80},{32,96},{48,112},{64,0},{80,16},{96,32},{112,48},{1... | collective-permute-start | bytes 393224 | tf_op jit(solution)/shard_map/ppermute | solution.py:20
  223.7 11.3 %collective-permute-start.23 = (bf16[8,8192]{1,0:T(8,128)(2,1)S(1)}, bf16[8,8192]{1,0:T(8,128)(2,1)S(1)}, u32[]{:S(2)}, u32[]{:S(2)}) collective-permute-start(bf16[8,8192]{1,0:T(8,128)(2,1)S(1)} %bitcast.161), channel_id=1, source_target_pairs={{0,32},{16,48},{32,0},{48,16},{64,96},{80,112},{96,64},{112,80},{1... | collective-permute-start | bytes 393224 | tf_op jit(solution)/shard_map/ppermute | solution.py:20
  235.0 15.0 %collective-permute-start.27 = (bf16[4,8,8192]{2,1,0:T(8,128)(2,1)S(1)}, bf16[4,8,8192]{2,1,0:T(8,128)(2,1)S(1)}, u32[]{:S(2)}, u32[]{:S(2)}) collective-permute-start(bf16[4,8,8192]{2,1,0:T(8,128)(2,1)S(1)} %get-tuple-element.23), channel_id=1, source_target_pairs={{0,256},{16,272},{32,288},{48,304},{64,320},{80,336},{96,352},{112... | collective-permute-start | bytes 1572872 | tf_op jit(solution)/shard_map/ppermute | solution.py:20
  237.0 21.6 %collective-permute-start.26 = (bf16[4,8,8192]{2,1,0:T(8,128)(2,1)S(1)}, bf16[4,8,8192]{2,1,0:T(8,128)(2,1)S(1)}, u32[]{:S(2)}, u32[]{:S(2)}) collective-permute-start(bf16[4,8,8192]{2,1,0:T(8,128)(2,1)S(1)} %get-tuple-element.23), channel_id=1, source_target_pairs={{0,128},{16,144},{32,160},{48,176},{64,192},{80,208},{96,224},{112... | collective-permute-start | bytes 1572872 | tf_op jit(solution)/shard_map/ppermute | solution.py:20
  239.1 24.4 %collective-permute-start.28 = (bf16[4,8,8192]{2,1,0:T(8,128)(2,1)S(1)}, bf16[4,8,8192]{2,1,0:T(8,128)(2,1)S(1)}, u32[]{:S(2)}, u32[]{:S(2)}) collective-permute-start(bf16[4,8,8192]{2,1,0:T(8,128)(2,1)S(1)} %get-tuple-element.23), channel_id=1, source_target_pairs={{0,384},{16,400},{32,416},{48,432},{64,448},{80,464},{96,480},{112... | collective-permute-start | bytes 1572872 | tf_op jit(solution)/shard_map/ppermute | solution.py:20
  (14 other events, 106.4 us)
Sparse Core Ops, SparseCore 0:
  104.7 32.3 all-gather.4
  178.2 63.5 all-gather.6

commit v5 on v4

--- a/solution.py
+++ b/solution.py
@@ -24,19 +24,21 @@
     return lax.ppermute(array, "mp", [(i, i ^ Y) for i in range(MP)])
 
 
-def gather_dp(block):
-    along_z = jnp.stack([block] + [swap(block, 2 * k) for k in (1, 2, 3)])
-    along_x = jnp.stack([along_z] + [swap(along_z, 8 * k) for k in (1, 2, 3)])
-    return along_x, swap(along_x, 1)
-
-
-def add_dp(own, other, later):
+def gather_z(block):
+    return jnp.stack([block] + [swap(block, 2 * k) for k in (1, 2, 3)])
+
+
+def gather_x(block):
+    return jnp.stack([block] + [swap(block, 8 * k) for k in (1, 2, 3)])
+
+
+def add_dp(own, other, *later):
     both = (own + swap(other, 1).astype(jnp.float32)).astype(jnp.bfloat16)
     parts = [both[0]] + [swap(both[k], 8 * k) for k in (1, 2, 3)]
     along_x = sum(part.astype(jnp.float32) for part in parts).astype(jnp.bfloat16)
-    along_x, later = lax.optimization_barrier((along_x, later))
+    along_x, *later = lax.optimization_barrier((along_x, *later))
     parts = [along_x[0]] + [swap(along_x[k], 2 * k) for k in (1, 2, 3)]
-    return sum(part.astype(jnp.float32) for part in parts), later
+    return sum(part.astype(jnp.float32) for part in parts), *later
 
 
 def project_kernel(last, order_ref, inputs_ref, weight_ref, *refs):
@@ -144,8 +146,7 @@
     share = views * images // Y
     mine = lax.dynamic_slice_in_dim(flat, lax.rem(model_index, Y) * share, share, axis=0)
     pieces = mine.reshape(share, DP, rows).transpose(1, 0, 2)
-    along_z = jnp.stack([weight] + [swap(weight, 2 * k) for k in (1, 2, 3)])
-    weight_own = jnp.stack([along_z] + [swap(along_z, 8 * k) for k in (1, 2, 3)])
+    weight_own = gather_x(gather_z(weight))
     weight_other = swap(weight_own, 1)
     half = (DP // 2, rows, feat)
     projected = project(order[: DP // 2], flat, weight_own.reshape(half))
@@ -162,11 +163,15 @@
     inverse = inverse.reshape(block, views).T[:, :, None]
 
     first, second, pieces = lax.optimization_barrier((normed[0], normed[1], pieces))
-    slices = lax.all_to_all(pieces, "dp", split_axis=0, concat_axis=0)
     pair = jnp.stack([second, partner(second)])
+    first, pair = lax.optimization_barrier((first, pair))
     columns_b = lax.all_gather(pair, "mp", axis=0, axis_index_groups=GROUPS)
     columns_b = columns_b.reshape(MP * block, total)
-    rows_own, rows_other = (part.reshape(feat // 2, total) for part in gather_dp(first))
+    along_z, pieces = lax.optimization_barrier((gather_z(first), pieces))
+    slices = lax.all_to_all(pieces, "dp", split_axis=0, concat_axis=0)
+    rows_own, slices = lax.optimization_barrier((gather_x(along_z), slices))
+    rows_other = swap(rows_own, 1).reshape(feat // 2, total)
+    rows_own = rows_own.reshape(feat // 2, total)
 
     def gradient_of(rows_a, with_diagonal):
         correlation = (
@@ -183,7 +188,6 @@
 
     corr_own = gradient_of(rows_own, True)
     corr_other = gradient_of(rows_other, False)
-    corr_other, slices = lax.optimization_barrier((corr_other, slices))
 
     def times(lhs, rhs, dims):
         return lax.dot_general(lhs, rhs, (dims, ((), ())), preferred_element_type=jnp.float32) / total
@@ -197,7 +201,9 @@
         terms_b.reshape(Y, 2, block, total), "mp", split_axis=0, concat_axis=0, axis_index_groups=GROUPS
     )
     shape = (4, 4, block, total)
-    grad_a, slices = add_dp(terms_own.reshape(shape), terms_other.reshape(shape), slices)
+    grad_a, terms_b, slices = add_dp(
+        terms_own.reshape(shape), terms_other.reshape(shape), terms_b, slices
+    )
     columns = lax.all_gather(slices, "mp", axis=0, axis_index_groups=GROUPS)
     terms_b = jnp.sum(terms_b.astype(jnp.float32), axis=0)
     grad_b = terms_b[0] + partner(terms_b[1].astype(jnp.bfloat16)).astype(jnp.float32)
@@ -207,7 +213,8 @@
     cross_mean = jnp.sum(grads * wide, axis=2, keepdims=True) / total
     grad_proj = ((grads - grad_mean - wide * cross_mean) * inverse).astype(jnp.bfloat16)
     grad_proj = grad_proj.transpose(1, 0, 2).reshape(block, views * total)
-    grad_own, grad_other = gather_dp(grad_proj)
+    grad_own = gather_x(gather_z(grad_proj))
+    grad_other = swap(grad_own, 1)
     part = weight_half(grad_own.reshape(feat // 2, views * total), columns)
     return weight_half(grad_other.reshape(feat // 2, views * total), columns, position, part)
 

time: 285 us -> 292 us (1.025)
  starting transfers between devices: 113 us -> 122 us
  waiting for transfers between devices: 125 us -> 121 us
    all_to_all x1, waiting for transfers between devices: 25.1 us -> 8.62 us  [per_device(): lax.all_to_all(terms_b.reshape(Y, 2, block, total), 'mp', split_axis=0, c...]
    ppermute x28, waiting for transfers between devices: 68.3 us -> 83.6 us  [swap(): return lax.ppermute(array, 'dp', [(i, i ^ step) for i in range(DP)])]
    all_gather x1, waiting for transfers between devices: 4.55 us -> 15.8 us  [per_device(): columns_b = lax.all_gather(pair, 'mp', axis=0, axis_index_groups=GROUPS)]
    all_to_all x1, waiting for transfers between devices: 10.5 us -> 0.01 us  [per_device(): slices = lax.all_to_all(pieces, 'dp', split_axis=0, concat_axis=0)]
    ppermute x2, starting transfers between devices: 9.6 us -> 15.3 us  [partner(): return lax.ppermute(array, 'mp', [(i, i ^ Y) for i in range(MP)])]
    ppermute x28, starting transfers between devices: 85.4 us -> 90.6 us  [swap(): return lax.ppermute(array, 'dp', [(i, i ^ step) for i in range(DP)])]
    ppermute x2, waiting for transfers between devices: 6.92 us -> 2.4 us  [partner(): return lax.ppermute(array, 'mp', [(i, i ^ Y) for i in range(MP)])]
    unnamed x7 -> x13, local copies, waits for them, and re-layouts: 4.48 us -> 6.07 us
  transfers between devices with their start and end apart: 35 -> 35, of which waited for: 22 -> 22; matrix products, arithmetic and copies ran while one was open for 3% -> 2% of each run, Pallas kernels for 1% -> 1%
where the time goes in v5:
time: 292 us; the launch traced here: 290 us
  starting transfers between devices  122 us (42%)
  waiting for transfers between devices  121 us (41%)
  between operations  14 us (5%)
  Pallas kernels  13 us (4%)
  local copies, waits for them, and re-layouts  8.47 us (3%)
  matrix products  6.23 us (2%)
  other arithmetic  5.07 us (2%)
    ppermute x28, starting transfers between devices, swap(): return lax.ppermute(array, 'dp', [(i, i ^ step) for i in range(DP)])  90.6 us
    ppermute x28, waiting for transfers between devices, swap(): return lax.ppermute(array, 'dp', [(i, i ^ step) for i in range(DP)])  83.6 us
    all_gather x1, waiting for transfers between devices, per_device(): columns_b = lax.all_gather(pair, 'mp', axis=0, axis_index_groups=GROUPS)  15.8 us
    ppermute x2, starting transfers between devices, partner(): return lax.ppermute(array, 'mp', [(i, i ^ Y) for i in range(MP)])  15.3 us
    all_to_all x1, waiting for transfers between devices, per_device(): lax.all_to_all(projected.reshape(DP, block, views * images), 'dp', split_...  10.1 us
    pallas_call x2, Pallas kernels, weight_half(): pl.pallas_call(functools.partial(weight_kernel, last), grid=(2, devices /...  8.66 us
    all_to_all x1, waiting for transfers between devices, per_device(): lax.all_to_all(terms_b.reshape(Y, 2, block, total), 'mp', split_axis=0, c...  8.62 us
    all_to_all x1, starting transfers between devices, per_device(): lax.all_to_all(projected.reshape(DP, block, views * images), 'dp', split_...  6.52 us
  transfers between devices with their start and end apart: 35, of which 22 were waited for; matrix products, arithmetic and copies ran while one was open for 2% of the time, Pallas kernels for 1%

profile of v5, /device:TPU:1, one launch (start us, length us, event | category | flops | bytes accessed | tf_op | source)
XLA Modules:
  0.0 290.2 jit_solution(12008212645128391724)
XLA Ops:
  6.5 4.8 %collective-permute-start = (bf16[256,256]{1,0:T(8,128)(2,1)}, bf16[256,256]{1,0:T(8,128)(2,1)S(1)}, u32[]{:S(2)}, u32[]{:S(2)}) collective-permute-start(bf16[256,256]{1,0:T(8,128)(2,1)} %param.3), channel_id=1, source_target_pairs={{0,32},{16,48},{32,0},{48,16},{64,96},{80,112},{96,64},{112,80},{1... | collective-permute-start | bytes 393224 | tf_op jit(solution)/shard_map/ppermute | solution.py:20
  11.4 5.5 %collective-permute-start.2 = (bf16[256,256]{1,0:T(8,128)(2,1)}, bf16[256,256]{1,0:T(8,128)(2,1)S(1)}, u32[]{:S(2)}, u32[]{:S(2)}) collective-permute-start(bf16[256,256]{1,0:T(8,128)(2,1)} %param.3), channel_id=1, source_target_pairs={{0,96},{16,112},{32,64},{48,80},{64,32},{80,48},{96,0},{112,16},{1... | collective-permute-start | bytes 393224 | tf_op jit(solution)/shard_map/ppermute | solution.py:20
  20.5 8.9 %collective-permute-done.1 = bf16[256,256]{1,0:T(8,128)(2,1)S(1)} collective-permute-done((bf16[256,256]{1,0:T(8,128)(2,1)}, bf16[256,256]{1,0:T(8,128)(2,1)S(1)}, u32[]{:S(2)}, u32[]{:S(2)}) %collective-permute-start.1) | collective-permute-done | bytes 131104 | tf_op jit(solution)/shard_map/ppermute | solution.py:20
  30.4 4.4 %collective-permute-start.4 = (bf16[4,256,256]{2,1,0:T(8,128)(2,1)S(1)}, bf16[4,256,256]{2,1,0:T(8,128)(2,1)S(1)}, u32[]{:S(2)}, u32[]{:S(2)}) collective-permute-start(bf16[4,256,256]{2,1,0:T(8,128)(2,1)S(1)} %get-tuple-element.35), channel_id=1, source_target_pairs={{0,256},{16,272},{32,288},{48,304},{64,320},{80,336},{96,352},{112... | collective-permute-start | bytes 1572872 | tf_op jit(solution)/shard_map/ppermute | solution.py:20
  39.5 6.4 %collective-permute-done.4 = bf16[4,256,256]{2,1,0:T(8,128)(2,1)S(1)} collective-permute-done((bf16[4,256,256]{2,1,0:T(8,128)(2,1)S(1)}, bf16[4,256,256]{2,1,0:T(8,128)(2,1)S(1)}, u32[]{:S(2)}, u32[]{:S(2)}) %collective-permute-start.4) | collective-permute-done | bytes 524320 | tf_op jit(solution)/shard_map/ppermute | solution.py:20
  45.9 11.5 %collective-permute-done.3 = bf16[4,256,256]{2,1,0:T(8,128)(2,1)S(1)} collective-permute-done((bf16[4,256,256]{2,1,0:T(8,128)(2,1)S(1)}, bf16[4,256,256]{2,1,0:T(8,128)(2,1)S(1)}, u32[]{:S(2)}, u32[]{:S(2)}) %collective-permute-start.3) | collective-permute-done | bytes 524320 | tf_op jit(solution)/shard_map/ppermute | solution.py:20
  68.6 6.5 %all-to-all-start = ((f32[32,8,256]{2,1,0:T(8,128)}), f32[32,8,256]{2,1,0:T(8,128)S(1)}, u32[]{:S(2)}, u32[]{:S(2)}) async-start(f32[32,8,256]{2,1,0:T(8,128)} %bitcast.11), calls=%async_computation | async-start | bytes 524288 | tf_op jit(solution)/shard_map/all_to_all | solution.py:155
  76.3 10.1 %all-to-all-done = f32[32,8,256]{2,1,0:T(8,128)S(1)} async-done(((f32[32,8,256]{2,1,0:T(8,128)}), f32[32,8,256]{2,1,0:T(8,128)S(1)}, u32[]{:S(2)}, u32[]{:S(2)}) %all-to-all-start) | async-done | bytes 262176 | tf_op jit(solution)/shard_map/all_to_all | solution.py:155
  86.9 7.7 %collective-permute-start.7 = (bf16[8,4096]{1,0:T(8,128)(2,1)S(1)}, bf16[8,4096]{1,0:T(8,128)(2,1)S(1)}, u32[]{:S(2)}, u32[]{:S(2)}) collective-permute-start(bf16[8,4096]{1,0:T(8,128)(2,1)S(1)} %get-tuple-element.18), channel_id=1, source_target_pairs={{0,8},{1,9},{2,10},{3,11},{4,12},{5,13},{6,14},{7,15},{8,0},{9,1},... | collective-permute-start | bytes 196616 | tf_op jit(solution)/shard_map/ppermute | solution.py:24
  110.5 5.4 %all-to-all-start.1 = ((bf16[32,32,256]{2,1,0:T(8,128)(2,1)}), bf16[32,32,256]{2,1,0:T(8,128)(2,1)S(1)}, u32[]{:S(2)}, u32[]{:S(2)}) async-start(bf16[32,32,256]{2,1,0:T(8,128)(2,1)} %copy.15), calls=%async_computation.1 | async-start | bytes 1048576 | tf_op jit(solution)/shard_map/all_to_all | solution.py:171
  116.7 4.6 %collective-permute-start.13 = (bf16[4,8,4096]{2,1,0:T(8,128)(2,1)S(1)}, bf16[4,8,4096]{2,1,0:T(8,128)(2,1)S(1)}, u32[]{:S(2)}, u32[]{:S(2)}) collective-permute-start(bf16[4,8,4096]{2,1,0:T(8,128)(2,1)S(1)} %pad_maximum_fusion.5), channel_id=1, source_target_pairs={{0,384},{16,400},{32,416},{48,432},{64,448},{80,464},{96,480},{112... | collective-permute-start | bytes 786440 | tf_op jit(solution)/shard_map/ppermute | solution.py:20
  125.7 10.9 %collective-permute-done.13 = bf16[4,8,4096]{2,1,0:T(8,128)(2,1)S(1)} collective-permute-done((bf16[4,8,4096]{2,1,0:T(8,128)(2,1)S(1)}, bf16[4,8,4096]{2,1,0:T(8,128)(2,1)S(1)}, u32[]{:S(2)}, u32[]{:S(2)}) %collective-permute-start.13) | collective-permute-done | bytes 262176 | tf_op jit(solution)/shard_map/ppermute | solution.py:20
  141.3 15.8 %all-gather.5.cloned.1.call-done = bf16[16,8,4096]{2,1,0:T(8,128)(2,1)} async-done(((bf16[2,8,4096]{2,1,0:T(8,128)(2,1)}), bf16[16,8,4096]{2,1,0:T(8,128)(2,1)}) %all-gather.5.cloned.1.call-update) | async-done | bytes 1048592 | tf_op jit(solution)/shard_map/all_gather | solution.py:168
  160.6 6.8 %collective-permute-start.15 = (bf16[4,4,8,4096]{3,2,1,0:T(8,128)(2,1)}, bf16[4,4,8,4096]{3,2,1,0:T(8,128)(2,1)}, u32[]{:S(2)}, u32[]{:S(2)}) collective-permute-start(bf16[4,4,8,4096]{3,2,1,0:T(8,128)(2,1)} %bitcast.34), channel_id=1, source_target_pairs={{0,16},{16,0},{32,48},{48,32},{64,80},{80,64},{96,112},{112,96},{1... | collective-permute-start | bytes 3145736 | tf_op jit(solution)/shard_map/ppermute | solution.py:20
  171.0 4.2 %all-to-all-start.2 = ((bf16[8,2,8,4096]{3,2,1,0:T(8,128)(2,1)}), bf16[8,2,8,4096]{3,2,1,0:T(8,128)(2,1)S(1)}, u32[]{:S(2)}, u32[]{:S(2)}) async-start(bf16[8,2,8,4096]{3,2,1,0:T(8,128)(2,1)} %bitcast.154), calls=%async_computation.2 | async-start | bytes 2097152 | tf_op jit(solution)/shard_map/all_to_all | solution.py:200
  186.2 9.4 %collective-permute-done.18 = bf16[4,8,4096]{2,1,0:T(8,128)(2,1)S(1)} collective-permute-done((bf16[4,8,4096]{2,1,0:T(8,128)(2,1)S(1)}, bf16[4,8,4096]{2,1,0:T(8,128)(2,1)S(1)}, u32[]{:S(2)}, u32[]{:S(2)}) %collective-permute-start.18) | collective-permute-done | bytes 262176 | tf_op jit(solution)/shard_map/ppermute | solution.py:20
  195.8 8.6 %all-to-all-done.2 = bf16[8,2,8,4096]{3,2,1,0:T(8,128)(2,1)S(1)} async-done(((bf16[8,2,8,4096]{3,2,1,0:T(8,128)(2,1)}), bf16[8,2,8,4096]{3,2,1,0:T(8,128)(2,1)S(1)}, u32[]{:S(2)}, u32[]{:S(2)}) %all-to-all-start.2) | async-done | bytes 1048608 | tf_op jit(solution)/shard_map/all_to_all | solution.py:200
  204.6 7.6 %collective-permute-start.22 = (bf16[8,4096]{1,0:T(8,128)(2,1)S(1)}, bf16[8,4096]{1,0:T(8,128)(2,1)S(1)}, u32[]{:S(2)}, u32[]{:S(2)}) collective-permute-start(bf16[8,4096]{1,0:T(8,128)(2,1)S(1)} %fusion.26), channel_id=1, source_target_pairs={{0,8},{1,9},{2,10},{3,11},{4,12},{5,13},{6,14},{7,15},{8,0},{9,1},... | collective-permute-start | bytes 196616 | tf_op jit(solution)/shard_map/ppermute | solution.py:24
  231.0 4.3 %collective-permute-start.23 = (bf16[8,8192]{1,0:T(8,128)(2,1)S(1)}, bf16[8,8192]{1,0:T(8,128)(2,1)S(1)}, u32[]{:S(2)}, u32[]{:S(2)}) collective-permute-start(bf16[8,8192]{1,0:T(8,128)(2,1)S(1)} %bitcast.162), channel_id=1, source_target_pairs={{0,32},{16,48},{32,0},{48,16},{64,96},{80,112},{96,64},{112,80},{1... | collective-permute-start | bytes 393224 | tf_op jit(solution)/shard_map/ppermute | solution.py:20
  235.3 5.8 %collective-permute-done.24 = bf16[8,8192]{1,0:T(8,128)(2,1)S(1)} collective-permute-done((bf16[8,8192]{1,0:T(8,128)(2,1)S(1)}, bf16[8,8192]{1,0:T(8,128)(2,1)S(1)}, u32[]{:S(2)}, u32[]{:S(2)}) %collective-permute-start.24) | collective-permute-done | bytes 131104 | tf_op jit(solution)/shard_map/ppermute | solution.py:20
  241.2 4.6 %collective-permute-start.27 = (bf16[4,8,8192]{2,1,0:T(8,128)(2,1)S(1)}, bf16[4,8,8192]{2,1,0:T(8,128)(2,1)S(1)}, u32[]{:S(2)}, u32[]{:S(2)}) collective-permute-start(bf16[4,8,8192]{2,1,0:T(8,128)(2,1)S(1)} %get-tuple-element.33), channel_id=1, source_target_pairs={{0,256},{16,272},{32,288},{48,304},{64,320},{80,336},{96,352},{112... | collective-permute-start | bytes 1572872 | tf_op jit(solution)/shard_map/ppermute | solution.py:20
  250.3 6.0 %collective-permute-done.27 = bf16[4,8,8192]{2,1,0:T(8,128)(2,1)S(1)} collective-permute-done((bf16[4,8,8192]{2,1,0:T(8,128)(2,1)S(1)}, bf16[4,8,8192]{2,1,0:T(8,128)(2,1)S(1)}, u32[]{:S(2)}, u32[]{:S(2)}) %collective-permute-start.27) | collective-permute-done | bytes 524320 | tf_op jit(solution)/shard_map/ppermute | solution.py:20
  256.3 11.1 %collective-permute-done.26 = bf16[4,8,8192]{2,1,0:T(8,128)(2,1)S(1)} collective-permute-done((bf16[4,8,8192]{2,1,0:T(8,128)(2,1)S(1)}, bf16[4,8,8192]{2,1,0:T(8,128)(2,1)S(1)}, u32[]{:S(2)}, u32[]{:S(2)}) %collective-permute-start.26) | collective-permute-done | bytes 524320 | tf_op jit(solution)/shard_map/ppermute | solution.py:20
  277.2 6.1 %shard_map.31 = f32[256,256]{1,0:T(8,128)} custom-call(bf16[128,8192]{1,0:T(8,128)(2,1)} %bitcast.63.grad_ref, bf16[8,32,32,256]{3,2,1,0:T(8,128)(2,1)S(1)} %bitcast.148, s32[32]{0:T(128)S(1)} %and_or_fusion.refs_0_, f32[128,256]{1,0:T(8,128)S(1)} %shard_map.30.refs_1_), custom_call_target="tpu_custom_call" | custom-call | flops 536870912 | bytes 6291456 | tf_op jit(solution)/shard_map/pallas_call | solution.py:116
  (106 shorter events, 99.1 us)
Async XLA Ops:
  6.5 12.6 %collective-permute-start = (bf16[256,256]{1,0:T(8,128)(2,1)}, bf16[256,256]{1,0:T(8,128)(2,1)S(1)}, u32[]{:S(2)}, u32[]{:S(2)}) collective-permute-start(bf16[256,256]{1,0:T(8,128)(2,1)} %param.3), channel_id=1, source_target_pairs={{0,32},{16,48},{32,0},{48,16},{64,96},{80,112},{96,64},{112,80},{1... | collective-permute-start | bytes 393224 | tf_op jit(solution)/shard_map/ppermute | solution.py:20
  16.9 12.5 %collective-permute-start.1 = (bf16[256,256]{1,0:T(8,128)(2,1)}, bf16[256,256]{1,0:T(8,128)(2,1)S(1)}, u32[]{:S(2)}, u32[]{:S(2)}) collective-permute-start(bf16[256,256]{1,0:T(8,128)(2,1)} %param.3), channel_id=1, source_target_pairs={{0,64},{16,80},{32,96},{48,112},{64,0},{80,16},{96,32},{112,48},{1... | collective-permute-start | bytes 393224 | tf_op jit(solution)/shard_map/ppermute | solution.py:20
  30.4 15.4 %collective-permute-start.4 = (bf16[4,256,256]{2,1,0:T(8,128)(2,1)S(1)}, bf16[4,256,256]{2,1,0:T(8,128)(2,1)S(1)}, u32[]{:S(2)}, u32[]{:S(2)}) collective-permute-start(bf16[4,256,256]{2,1,0:T(8,128)(2,1)S(1)} %get-tuple-element.35), channel_id=1, source_target_pairs={{0,256},{16,272},{32,288},{48,304},{64,320},{80,336},{96,352},{112... | collective-permute-start | bytes 1572872 | tf_op jit(solution)/shard_map/ppermute | solution.py:20
  34.8 22.5 %collective-permute-start.3 = (bf16[4,256,256]{2,1,0:T(8,128)(2,1)S(1)}, bf16[4,256,256]{2,1,0:T(8,128)(2,1)S(1)}, u32[]{:S(2)}, u32[]{:S(2)}) collective-permute-start(bf16[4,256,256]{2,1,0:T(8,128)(2,1)S(1)} %get-tuple-element.35), channel_id=1, source_target_pairs={{0,128},{16,144},{32,160},{48,176},{64,192},{80,208},{96,224},{112... | collective-permute-start | bytes 1572872 | tf_op jit(solution)/shard_map/ppermute | solution.py:20
  37.0 21.9 %collective-permute-start.5 = (bf16[4,256,256]{2,1,0:T(8,128)(2,1)S(1)}, bf16[4,256,256]{2,1,0:T(8,128)(2,1)S(1)}, u32[]{:S(2)}, u32[]{:S(2)}) collective-permute-start(bf16[4,256,256]{2,1,0:T(8,128)(2,1)S(1)} %get-tuple-element.35), channel_id=1, source_target_pairs={{0,384},{16,400},{32,416},{48,432},{64,448},{80,464},{96,480},{112... | collective-permute-start | bytes 1572872 | tf_op jit(solution)/shard_map/ppermute | solution.py:20
  68.6 17.8 %all-to-all-start = ((f32[32,8,256]{2,1,0:T(8,128)}), f32[32,8,256]{2,1,0:T(8,128)S(1)}, u32[]{:S(2)}, u32[]{:S(2)}) async-start(f32[32,8,256]{2,1,0:T(8,128)} %bitcast.11), calls=%async_computation | async-start | bytes 524288 | tf_op jit(solution)/shard_map/all_to_all | solution.py:155
  86.9 10.1 %collective-permute-start.7 = (bf16[8,4096]{1,0:T(8,128)(2,1)S(1)}, bf16[8,4096]{1,0:T(8,128)(2,1)S(1)}, u32[]{:S(2)}, u32[]{:S(2)}) collective-permute-start(bf16[8,4096]{1,0:T(8,128)(2,1)S(1)} %get-tuple-element.18), channel_id=1, source_target_pairs={{0,8},{1,9},{2,10},{3,11},{4,12},{5,13},{6,14},{7,15},{8,0},{9,1},... | collective-permute-start | bytes 196616 | tf_op jit(solution)/shard_map/ppermute | solution.py:24
  110.5 26.9 %all-to-all-start.1 = ((bf16[32,32,256]{2,1,0:T(8,128)(2,1)}), bf16[32,32,256]{2,1,0:T(8,128)(2,1)S(1)}, u32[]{:S(2)}, u32[]{:S(2)}) async-start(bf16[32,32,256]{2,1,0:T(8,128)(2,1)} %copy.15), calls=%async_computation.1 | async-start | bytes 1048576 | tf_op jit(solution)/shard_map/all_to_all | solution.py:171
  115.9 41.2 %all-gather.5.cloned.1.call-start = ((), (), s32[]{:S(2)}) async-start(), calls=%async_computation.3 | async-start | bytes 1179648 | tf_op jit(solution)/shard_map/all_gather | solution.py:168
  116.7 19.9 %collective-permute-start.13 = (bf16[4,8,4096]{2,1,0:T(8,128)(2,1)S(1)}, bf16[4,8,4096]{2,1,0:T(8,128)(2,1)S(1)}, u32[]{:S(2)}, u32[]{:S(2)}) collective-permute-start(bf16[4,8,4096]{2,1,0:T(8,128)(2,1)S(1)} %pad_maximum_fusion.5), channel_id=1, source_target_pairs={{0,384},{16,400},{32,416},{48,432},{64,448},{80,464},{96,480},{112... | collective-permute-start | bytes 786440 | tf_op jit(solution)/shard_map/ppermute | solution.py:20
  121.2 15.3 %collective-permute-start.12 = (bf16[4,8,4096]{2,1,0:T(8,128)(2,1)S(1)}, bf16[4,8,4096]{2,1,0:T(8,128)(2,1)S(1)}, u32[]{:S(2)}, u32[]{:S(2)}) collective-permute-start(bf16[4,8,4096]{2,1,0:T(8,128)(2,1)S(1)} %pad_maximum_fusion.5), channel_id=1, source_target_pairs={{0,256},{16,272},{32,288},{48,304},{64,320},{80,336},{96,352},{112... | collective-permute-start | bytes 786440 | tf_op jit(solution)/shard_map/ppermute | solution.py:20
  123.7 13.5 %collective-permute-start.11 = (bf16[4,8,4096]{2,1,0:T(8,128)(2,1)S(1)}, bf16[4,8,4096]{2,1,0:T(8,128)(2,1)S(1)}, u32[]{:S(2)}, u32[]{:S(2)}) collective-permute-start(bf16[4,8,4096]{2,1,0:T(8,128)(2,1)S(1)} %pad_maximum_fusion.5), channel_id=1, source_target_pairs={{0,128},{16,144},{32,160},{48,176},{64,192},{80,208},{96,224},{112... | collective-permute-start | bytes 786440 | tf_op jit(solution)/shard_map/ppermute | solution.py:20
  138.1 19.0 %collective-permute-start.14 = (bf16[4,4,8,4096]{3,2,1,0:T(8,128)(2,1)S(1)}, bf16[4,4,8,4096]{3,2,1,0:T(8,128)(2,1)S(1)}, u32[]{:S(2)}, u32[]{:S(2)}) collective-permute-start(bf16[4,4,8,4096]{3,2,1,0:T(8,128)(2,1)S(1)} %pad_maximum_fusion.2), channel_id=1, source_target_pairs={{0,16},{16,0},{32,48},{48,32},{64,80},{80,64},{96,112},{112,96},{1... | collective-permute-start | bytes 3145736 | tf_op jit(solution)/shard_map/ppermute | solution.py:20
  160.6 14.6 %collective-permute-start.15 = (bf16[4,4,8,4096]{3,2,1,0:T(8,128)(2,1)}, bf16[4,4,8,4096]{3,2,1,0:T(8,128)(2,1)}, u32[]{:S(2)}, u32[]{:S(2)}) collective-permute-start(bf16[4,4,8,4096]{3,2,1,0:T(8,128)(2,1)} %bitcast.34), channel_id=1, source_target_pairs={{0,16},{16,0},{32,48},{48,32},{64,80},{80,64},{96,112},{112,96},{1... | collective-permute-start | bytes 3145736 | tf_op jit(solution)/shard_map/ppermute | solution.py:20
  171.0 33.5 %all-to-all-start.2 = ((bf16[8,2,8,4096]{3,2,1,0:T(8,128)(2,1)}), bf16[8,2,8,4096]{3,2,1,0:T(8,128)(2,1)S(1)}, u32[]{:S(2)}, u32[]{:S(2)}) async-start(bf16[8,2,8,4096]{3,2,1,0:T(8,128)(2,1)} %bitcast.154), calls=%async_computation.2 | async-start | bytes 2097152 | tf_op jit(solution)/shard_map/all_to_all | solution.py:200
  175.2 97.3 %all-gather.7.cloned.1.call-start = ((), (), s32[]{:S(2)}) async-start(), calls=%async_computation.4 | async-start | bytes 4718592 | tf_op jit(solution)/shard_map/all_gather | solution.py:207
  179.7 16.0 %collective-permute-start.18 = (bf16[4,8,4096]{2,1,0:T(8,128)(2,1)S(1)}, bf16[4,8,4096]{2,1,0:T(8,128)(2,1)S(1)}, u32[]{:S(2)}, u32[]{:S(2)}) collective-permute-start(bf16[4,8,4096]{2,1,0:T(8,128)(2,1)S(1)} %get-tuple-element.30), channel_id=1, source_target_pairs={{0,384},{16,400},{32,416},{48,432},{64,448},{80,464},{96,480},{112... | collective-permute-start | bytes 786440 | tf_op jit(solution)/shard_map/ppermute | solution.py:20
  183.4 12.3 %collective-permute-start.17 = (bf16[4,8,4096]{2,1,0:T(8,128)(2,1)S(1)}, bf16[4,8,4096]{2,1,0:T(8,128)(2,1)S(1)}, u32[]{:S(2)}, u32[]{:S(2)}) collective-permute-start(bf16[4,8,4096]{2,1,0:T(8,128)(2,1)S(1)} %get-tuple-element.31), channel_id=1, source_target_pairs={{0,256},{16,272},{32,288},{48,304},{64,320},{80,336},{96,352},{112... | collective-permute-start | bytes 786440 | tf_op jit(solution)/shard_map/ppermute | solution.py:20
  204.6 16.0 %collective-permute-start.22 = (bf16[8,4096]{1,0:T(8,128)(2,1)S(1)}, bf16[8,4096]{1,0:T(8,128)(2,1)S(1)}, u32[]{:S(2)}, u32[]{:S(2)}) collective-permute-start(bf16[8,4096]{1,0:T(8,128)(2,1)S(1)} %fusion.26), channel_id=1, source_target_pairs={{0,8},{1,9},{2,10},{3,11},{4,12},{5,13},{6,14},{7,15},{8,0},{9,1},... | collective-permute-start | bytes 196616 | tf_op jit(solution)/shard_map/ppermute | solution.py:24
  229.0 12.1 %collective-permute-start.24 = (bf16[8,8192]{1,0:T(8,128)(2,1)S(1)}, bf16[8,8192]{1,0:T(8,128)(2,1)S(1)}, u32[]{:S(2)}, u32[]{:S(2)}) collective-permute-start(bf16[8,8192]{1,0:T(8,128)(2,1)S(1)} %bitcast.161), channel_id=1, source_target_pairs={{0,64},{16,80},{32,96},{48,112},{64,0},{80,16},{96,32},{112,48},{1... | collective-permute-start | bytes 393224 | tf_op jit(solution)/shard_map/ppermute | solution.py:20
  231.0 10.1 %collective-permute-start.23 = (bf16[8,8192]{1,0:T(8,128)(2,1)S(1)}, bf16[8,8192]{1,0:T(8,128)(2,1)S(1)}, u32[]{:S(2)}, u32[]{:S(2)}) collective-permute-start(bf16[8,8192]{1,0:T(8,128)(2,1)S(1)} %bitcast.162), channel_id=1, source_target_pairs={{0,32},{16,48},{32,0},{48,16},{64,96},{80,112},{96,64},{112,80},{1... | collective-permute-start | bytes 393224 | tf_op jit(solution)/shard_map/ppermute | solution.py:20
  241.2 15.1 %collective-permute-start.27 = (bf16[4,8,8192]{2,1,0:T(8,128)(2,1)S(1)}, bf16[4,8,8192]{2,1,0:T(8,128)(2,1)S(1)}, u32[]{:S(2)}, u32[]{:S(2)}) collective-permute-start(bf16[4,8,8192]{2,1,0:T(8,128)(2,1)S(1)} %get-tuple-element.33), channel_id=1, source_target_pairs={{0,256},{16,272},{32,288},{48,304},{64,320},{80,336},{96,352},{112... | collective-permute-start | bytes 1572872 | tf_op jit(solution)/shard_map/ppermute | solution.py:20
  245.8 21.6 %collective-permute-start.26 = (bf16[4,8,8192]{2,1,0:T(8,128)(2,1)S(1)}, bf16[4,8,8192]{2,1,0:T(8,128)(2,1)S(1)}, u32[]{:S(2)}, u32[]{:S(2)}) collective-permute-start(bf16[4,8,8192]{2,1,0:T(8,128)(2,1)S(1)} %get-tuple-element.33), channel_id=1, source_target_pairs={{0,128},{16,144},{32,160},{48,176},{64,192},{80,208},{96,224},{112... | collective-permute-start | bytes 1572872 | tf_op jit(solution)/shard_map/ppermute | solution.py:20
  248.0 21.5 %collective-permute-start.28 = (bf16[4,8,8192]{2,1,0:T(8,128)(2,1)S(1)}, bf16[4,8,8192]{2,1,0:T(8,128)(2,1)S(1)}, u32[]{:S(2)}, u32[]{:S(2)}) collective-permute-start(bf16[4,8,8192]{2,1,0:T(8,128)(2,1)S(1)} %get-tuple-element.33), channel_id=1, source_target_pairs={{0,384},{16,400},{32,416},{48,432},{64,448},{80,464},{96,480},{112... | collective-permute-start | bytes 1572872 | tf_op jit(solution)/shard_map/ppermute | solution.py:20
  (17 other events, 100.2 us)
Sparse Core Ops, SparseCore 0:
  118.8 38.2 all-gather.4
  204.7 53.2 all-gather.6

commit v6 on v5

--- a/solution.py
+++ b/solution.py
@@ -14,31 +14,27 @@
 MP = 16
 Y = 8
 GROUPS = [list(range(Y)), list(range(Y, MP))]
-
-
-def swap(array, step):
-    return lax.ppermute(array, "dp", [(i, i ^ step) for i in range(DP)])
+ALONG_X = [(8,), (16,), (24,)]
+ALONG_Z = [(2,), (4,), (6,)]
+STRIDED_Z = [(4,), (0, 8), (4, 8)]
+
+
+def swap(array, data, model=0):
+    mask = data * MP + model
+    return lax.ppermute(array, ("dp", "mp"), [(i, i ^ mask) for i in range(DP * MP)])
 
 
 def partner(array):
-    return lax.ppermute(array, "mp", [(i, i ^ Y) for i in range(MP)])
-
-
-def gather_z(block):
-    return jnp.stack([block] + [swap(block, 2 * k) for k in (1, 2, 3)])
-
-
-def gather_x(block):
-    return jnp.stack([block] + [swap(block, 8 * k) for k in (1, 2, 3)])
-
-
-def add_dp(own, other, *later):
-    both = (own + swap(other, 1).astype(jnp.float32)).astype(jnp.bfloat16)
-    parts = [both[0]] + [swap(both[k], 8 * k) for k in (1, 2, 3)]
-    along_x = sum(part.astype(jnp.float32) for part in parts).astype(jnp.bfloat16)
-    along_x, *later = lax.optimization_barrier((along_x, *later))
-    parts = [along_x[0]] + [swap(along_x[k], 2 * k) for k in (1, 2, 3)]
-    return sum(part.astype(jnp.float32) for part in parts), *later
+    return swap(array, 2)
+
+
+def gather(block, masks):
+    return jnp.stack([block] + [swap(block, *mask) for mask in masks])
+
+
+def add(blocks, masks):
+    parts = [blocks[0]] + [swap(blocks[k + 1], *mask) for k, mask in enumerate(masks)]
+    return sum(part.astype(jnp.float32) for part in parts)
 
 
 def project_kernel(last, order_ref, inputs_ref, weight_ref, *refs):
@@ -146,7 +142,7 @@
     share = views * images // Y
     mine = lax.dynamic_slice_in_dim(flat, lax.rem(model_index, Y) * share, share, axis=0)
     pieces = mine.reshape(share, DP, rows).transpose(1, 0, 2)
-    weight_own = gather_x(gather_z(weight))
+    weight_own = gather(gather(weight, ALONG_Z), ALONG_X)
     weight_other = swap(weight_own, 1)
     half = (DP // 2, rows, feat)
     projected = project(order[: DP // 2], flat, weight_own.reshape(half))
@@ -167,9 +163,11 @@
     first, pair = lax.optimization_barrier((first, pair))
     columns_b = lax.all_gather(pair, "mp", axis=0, axis_index_groups=GROUPS)
     columns_b = columns_b.reshape(MP * block, total)
-    along_z, pieces = lax.optimization_barrier((gather_z(first), pieces))
+    along_z, pieces = lax.optimization_barrier((gather(first, STRIDED_Z), pieces))
     slices = lax.all_to_all(pieces, "dp", split_axis=0, concat_axis=0)
-    rows_own, slices = lax.optimization_barrier((gather_x(along_z), slices))
+    rows_own, columns_b, slices = lax.optimization_barrier(
+        (gather(along_z, ALONG_X), columns_b, slices)
+    )
     rows_other = swap(rows_own, 1).reshape(feat // 2, total)
     rows_own = rows_own.reshape(feat // 2, total)
 
@@ -192,28 +190,30 @@
     def times(lhs, rhs, dims):
         return lax.dot_general(lhs, rhs, (dims, ((), ())), preferred_element_type=jnp.float32) / total
 
-    terms_other = times(corr_other, columns_b, ((1,), (0,))).astype(jnp.bfloat16)
     terms_b = (
         times(corr_own, rows_own, ((0,), (0,))) + times(corr_other, rows_other, ((0,), (0,)))
     ).astype(jnp.bfloat16)
-    terms_own = times(corr_own, columns_b, ((1,), (0,)))
+    corr_own, corr_other, terms_b = lax.optimization_barrier((corr_own, corr_other, terms_b))
     terms_b = lax.all_to_all(
         terms_b.reshape(Y, 2, block, total), "mp", split_axis=0, concat_axis=0, axis_index_groups=GROUPS
     )
+    terms_other = times(corr_other, columns_b, ((1,), (0,))).astype(jnp.bfloat16)
+    terms_own = times(corr_own, columns_b, ((1,), (0,)))
     shape = (4, 4, block, total)
-    grad_a, terms_b, slices = add_dp(
-        terms_own.reshape(shape), terms_other.reshape(shape), terms_b, slices
-    )
+    both = terms_own.reshape(shape) + swap(terms_other.reshape(shape), 1).astype(jnp.float32)
+    along_x = add(both.astype(jnp.bfloat16), ALONG_X).astype(jnp.bfloat16)
+    along_x, terms_b, slices = lax.optimization_barrier((along_x, terms_b, slices))
     columns = lax.all_gather(slices, "mp", axis=0, axis_index_groups=GROUPS)
     terms_b = jnp.sum(terms_b.astype(jnp.float32), axis=0)
     grad_b = terms_b[0] + partner(terms_b[1].astype(jnp.bfloat16)).astype(jnp.float32)
-    grads = jnp.stack([grad_a, grad_b])
+    grads = jnp.stack([add(along_x, STRIDED_Z), grad_b])
     wide = normed.astype(jnp.float32)
     grad_mean = jnp.sum(grads, axis=2, keepdims=True) / total
     cross_mean = jnp.sum(grads * wide, axis=2, keepdims=True) / total
     grad_proj = ((grads - grad_mean - wide * cross_mean) * inverse).astype(jnp.bfloat16)
     grad_proj = grad_proj.transpose(1, 0, 2).reshape(block, views * total)
-    grad_own = gather_x(gather_z(grad_proj))
+    grad_own = gather(gather(grad_proj, ALONG_Z), ALONG_X)
+    grad_own, columns = lax.optimization_barrier((grad_own, columns))
     grad_other = swap(grad_own, 1)
     part = weight_half(grad_own.reshape(feat // 2, views * total), columns)
     return weight_half(grad_other.reshape(feat // 2, views * total), columns, position, part)

time: 292 us -> 272 us (0.932)
  waiting for transfers between devices: 121 us -> 109 us
  starting transfers between devices: 122 us -> 119 us
    all_gather x1, waiting for transfers between devices: 15.8 us -> 0.02 us  [per_device(): columns_b = lax.all_gather(pair, 'mp', axis=0, axis_index_groups=GROUPS)]
    ppermute x30, starting transfers between devices: 106 us -> 101 us  [swap(): lax.ppermute(array, ('dp', 'mp'), [(i, i ^ mask) for i in range(DP * MP)])]
    ppermute x30, waiting for transfers between devices: 86 us -> 89.6 us  [swap(): lax.ppermute(array, ('dp', 'mp'), [(i, i ^ mask) for i in range(DP * MP)])]
    unnamed x13 -> x9, local copies, waits for them, and re-layouts: 6.07 us -> 5.14 us
  transfers between devices with their start and end apart: 35 -> 35, of which waited for: 22 -> 17; matrix products, arithmetic and copies ran while one was open for 2% -> 3% of each run, Pallas kernels for 1% -> 1%
where the time goes in v6:
time: 272 us; the launch traced here: 270 us
  starting transfers between devices  119 us (44%)
  waiting for transfers between devices  109 us (40%)
  between operations  14 us (5%)
  Pallas kernels  10.9 us (4%)
  local copies, waits for them, and re-layouts  7.53 us (3%)
  other arithmetic  5.12 us (2%)
  matrix products  4.97 us (2%)
    ppermute x30, starting transfers between devices, swap(): lax.ppermute(array, ('dp', 'mp'), [(i, i ^ mask) for i in range(DP * MP)])  101 us
    ppermute x30, waiting for transfers between devices, swap(): lax.ppermute(array, ('dp', 'mp'), [(i, i ^ mask) for i in range(DP * MP)])  89.6 us
    all_to_all x1, waiting for transfers between devices, per_device(): lax.all_to_all(projected.reshape(DP, block, views * images), 'dp', split_...  10 us
    all_to_all x1, waiting for transfers between devices, per_device(): lax.all_to_all(terms_b.reshape(Y, 2, block, total), 'mp', split_axis=0, c...  9 us
    all_to_all x1, starting transfers between devices, per_device(): lax.all_to_all(terms_b.reshape(Y, 2, block, total), 'mp', split_axis=0, c...  6.83 us
    all_to_all x1, starting transfers between devices, per_device(): lax.all_to_all(projected.reshape(DP, block, views * images), 'dp', split_...  6.7 us
    pallas_call x2, Pallas kernels, weight_half(): pl.pallas_call(functools.partial(weight_kernel, last), grid=(2, devices /...  6.54 us
  transfers between devices with their start and end apart: 35, of which 17 were waited for; matrix products, arithmetic and copies ran while one was open for 3% of the time, Pallas kernels for 1%

profile of v6, /device:TPU:1, one launch (start us, length us, event | category | flops | bytes accessed | tf_op | source)
XLA Modules:
  0.0 270.4 jit_solution(18302568771601991230)
XLA Ops:
  6.5 8.4 %collective-permute-start.2 = (bf16[256,256]{1,0:T(8,128)(2,1)}, bf16[256,256]{1,0:T(8,128)(2,1)S(1)}, u32[]{:S(2)}, u32[]{:S(2)}) collective-permute-start(bf16[256,256]{1,0:T(8,128)(2,1)} %param.3), channel_id=1, source_target_pairs={{0,96},{1,97},{2,98},{3,99},{4,100},{5,101},{6,102},{7,103},{8,104... | collective-permute-start | bytes 393224 | tf_op jit(solution)/shard_map/ppermute | solution.py:24
  19.1 6.7 %collective-permute-done.1 = bf16[256,256]{1,0:T(8,128)(2,1)S(1)} collective-permute-done((bf16[256,256]{1,0:T(8,128)(2,1)}, bf16[256,256]{1,0:T(8,128)(2,1)S(1)}, u32[]{:S(2)}, u32[]{:S(2)}) %collective-permute-start.1) | collective-permute-done | bytes 131104 | tf_op jit(solution)/shard_map/ppermute | solution.py:24
  26.9 4.8 %collective-permute-start.5 = (bf16[4,256,256]{2,1,0:T(8,128)(2,1)S(1)}, bf16[4,256,256]{2,1,0:T(8,128)(2,1)S(1)}, u32[]{:S(2)}, u32[]{:S(2)}) collective-permute-start(bf16[4,256,256]{2,1,0:T(8,128)(2,1)S(1)} %get-tuple-element.47), channel_id=1, source_target_pairs={{0,384},{1,385},{2,386},{3,387},{4,388},{5,389},{6,390},{7,391},{8... | collective-permute-start | bytes 1572872 | tf_op jit(solution)/shard_map/ppermute | solution.py:24
  36.1 17.0 %collective-permute-done.5 = bf16[4,256,256]{2,1,0:T(8,128)(2,1)S(1)} collective-permute-done((bf16[4,256,256]{2,1,0:T(8,128)(2,1)S(1)}, bf16[4,256,256]{2,1,0:T(8,128)(2,1)S(1)}, u32[]{:S(2)}, u32[]{:S(2)}) %collective-permute-start.5) | collective-permute-done | bytes 524320 | tf_op jit(solution)/shard_map/ppermute | solution.py:24
  55.7 4.8 %collective-permute-start.6 = (bf16[4,4,256,256]{3,2,1,0:T(8,128)(2,1)S(1)}, bf16[4,4,256,256]{3,2,1,0:T(8,128)(2,1)}, u32[]{:S(2)}, u32[]{:S(2)}) collective-permute-start(bf16[4,4,256,256]{3,2,1,0:T(8,128)(2,1)S(1)} %pad_maximum_fusion), channel_id=1, source_target_pairs={{0,16},{1,17},{2,18},{3,19},{4,20},{5,21},{6,22},{7,23},{8,24},{9,... | collective-permute-start | bytes 6291464 | tf_op jit(solution)/shard_map/ppermute | solution.py:24
  67.5 6.7 %all-to-all-start = ((f32[32,8,256]{2,1,0:T(8,128)}), f32[32,8,256]{2,1,0:T(8,128)S(1)}, u32[]{:S(2)}, u32[]{:S(2)}) async-start(f32[32,8,256]{2,1,0:T(8,128)} %bitcast.11), calls=%async_computation | async-start | bytes 524288 | tf_op jit(solution)/shard_map/all_to_all | solution.py:151
  75.5 10.0 %all-to-all-done = f32[32,8,256]{2,1,0:T(8,128)S(1)} async-done(((f32[32,8,256]{2,1,0:T(8,128)}), f32[32,8,256]{2,1,0:T(8,128)S(1)}, u32[]{:S(2)}, u32[]{:S(2)}) %all-to-all-start) | async-done | bytes 262176 | tf_op jit(solution)/shard_map/all_to_all | solution.py:151
  92.3 5.4 %collective-permute-start.10 = (bf16[8,4096]{1,0:T(8,128)(2,1)S(1)}, bf16[8,4096]{1,0:T(8,128)(2,1)S(1)}, u32[]{:S(2)}, u32[]{:S(2)}) collective-permute-start(bf16[8,4096]{1,0:T(8,128)(2,1)S(1)} %get-tuple-element.25), channel_id=1, source_target_pairs={{0,72},{1,73},{2,74},{3,75},{4,76},{5,77},{6,78},{7,79},{8,64},{9,... | collective-permute-start | bytes 196616 | tf_op jit(solution)/shard_map/ppermute | solution.py:24
  97.6 4.5 %collective-permute-start.9 = (bf16[8,4096]{1,0:T(8,128)(2,1)S(1)}, bf16[8,4096]{1,0:T(8,128)(2,1)S(1)}, u32[]{:S(2)}, u32[]{:S(2)}) collective-permute-start(bf16[8,4096]{1,0:T(8,128)(2,1)S(1)} %get-tuple-element.25), channel_id=1, source_target_pairs={{0,8},{1,9},{2,10},{3,11},{4,12},{5,13},{6,14},{7,15},{8,0},{9,1},... | collective-permute-start | bytes 196616 | tf_op jit(solution)/shard_map/ppermute | solution.py:24
  107.4 4.3 %collective-permute-done.8 = bf16[8,4096]{1,0:T(8,128)(2,1)S(1)} collective-permute-done((bf16[8,4096]{1,0:T(8,128)(2,1)S(1)}, bf16[8,4096]{1,0:T(8,128)(2,1)S(1)}, u32[]{:S(2)}, u32[]{:S(2)}) %collective-permute-start.8) | collective-permute-done | bytes 65568 | tf_op jit(solution)/shard_map/ppermute | solution.py:24
  112.8 4.2 %all-to-all-start.1 = ((bf16[32,32,256]{2,1,0:T(8,128)(2,1)}), bf16[32,32,256]{2,1,0:T(8,128)(2,1)S(1)}, u32[]{:S(2)}, u32[]{:S(2)}) async-start(bf16[32,32,256]{2,1,0:T(8,128)(2,1)} %copy.15), calls=%async_computation.1 | async-start | bytes 1048576 | tf_op jit(solution)/shard_map/all_to_all | solution.py:167
  117.0 4.5 %collective-permute-start.13 = (bf16[4,8,4096]{2,1,0:T(8,128)(2,1)S(1)}, bf16[4,8,4096]{2,1,0:T(8,128)(2,1)S(1)}, u32[]{:S(2)}, u32[]{:S(2)}) collective-permute-start(bf16[4,8,4096]{2,1,0:T(8,128)(2,1)S(1)} %pad_maximum_fusion.5), channel_id=1, source_target_pairs={{0,384},{1,385},{2,386},{3,387},{4,388},{5,389},{6,390},{7,391},{8... | collective-permute-start | bytes 786440 | tf_op jit(solution)/shard_map/ppermute | solution.py:24
  126.0 11.7 %collective-permute-done.13 = bf16[4,8,4096]{2,1,0:T(8,128)(2,1)S(1)} collective-permute-done((bf16[4,8,4096]{2,1,0:T(8,128)(2,1)S(1)}, bf16[4,8,4096]{2,1,0:T(8,128)(2,1)S(1)}, u32[]{:S(2)}, u32[]{:S(2)}) %collective-permute-start.13) | collective-permute-done | bytes 262176 | tf_op jit(solution)/shard_map/ppermute | solution.py:24
  148.2 6.8 %all-to-all-start.2 = ((bf16[8,2,8,4096]{3,2,1,0:T(8,128)(2,1)}), bf16[8,2,8,4096]{3,2,1,0:T(8,128)(2,1)S(1)}, u32[]{:S(2)}, u32[]{:S(2)}) async-start(bf16[8,2,8,4096]{3,2,1,0:T(8,128)(2,1)} %bitcast.39), calls=%async_computation.2 | async-start | bytes 2097152 | tf_op jit(solution)/shard_map/all_to_all | solution.py:197
  157.1 4.4 %collective-permute-start.18 = (bf16[4,8,4096]{2,1,0:T(8,128)(2,1)S(1)}, bf16[4,8,4096]{2,1,0:T(8,128)(2,1)S(1)}, u32[]{:S(2)}, u32[]{:S(2)}) collective-permute-start(bf16[4,8,4096]{2,1,0:T(8,128)(2,1)S(1)} %get-tuple-element.42), channel_id=1, source_target_pairs={{0,384},{1,385},{2,386},{3,387},{4,388},{5,389},{6,390},{7,391},{8... | collective-permute-start | bytes 786440 | tf_op jit(solution)/shard_map/ppermute | solution.py:24
  166.1 5.7 %collective-permute-done.18 = bf16[4,8,4096]{2,1,0:T(8,128)(2,1)S(1)} collective-permute-done((bf16[4,8,4096]{2,1,0:T(8,128)(2,1)S(1)}, bf16[4,8,4096]{2,1,0:T(8,128)(2,1)S(1)}, u32[]{:S(2)}, u32[]{:S(2)}) %collective-permute-start.18) | collective-permute-done | bytes 262176 | tf_op jit(solution)/shard_map/ppermute | solution.py:24
  175.3 9.0 %all-to-all-done.2 = bf16[8,2,8,4096]{3,2,1,0:T(8,128)(2,1)S(1)} async-done(((bf16[8,2,8,4096]{3,2,1,0:T(8,128)(2,1)}), bf16[8,2,8,4096]{3,2,1,0:T(8,128)(2,1)S(1)}, u32[]{:S(2)}, u32[]{:S(2)}) %all-to-all-start.2) | async-done | bytes 1048608 | tf_op jit(solution)/shard_map/all_to_all | solution.py:197
  188.0 4.1 %collective-permute-start.21 = (bf16[8,4096]{1,0:T(8,128)(2,1)S(1)}, bf16[8,4096]{1,0:T(8,128)(2,1)S(1)}, u32[]{:S(2)}, u32[]{:S(2)}) collective-permute-start(bf16[8,4096]{1,0:T(8,128)(2,1)S(1)} %get-tuple-element.53), channel_id=1, source_target_pairs={{0,72},{1,73},{2,74},{3,75},{4,76},{5,77},{6,78},{7,79},{8,64},{9,... | collective-permute-start | bytes 196616 | tf_op jit(solution)/shard_map/ppermute | solution.py:24
  192.2 4.5 %collective-permute-start.20 = (bf16[8,4096]{1,0:T(8,128)(2,1)S(1)}, bf16[8,4096]{1,0:T(8,128)(2,1)S(1)}, u32[]{:S(2)}, u32[]{:S(2)}) collective-permute-start(bf16[8,4096]{1,0:T(8,128)(2,1)S(1)} %get-tuple-element.54), channel_id=1, source_target_pairs={{0,8},{1,9},{2,10},{3,11},{4,12},{5,13},{6,14},{7,15},{8,0},{9,1},... | collective-permute-start | bytes 196616 | tf_op jit(solution)/shard_map/ppermute | solution.py:24
  201.1 4.8 %collective-permute-done.19 = bf16[8,4096]{1,0:T(8,128)(2,1)S(1)} collective-permute-done((bf16[8,4096]{1,0:T(8,128)(2,1)S(1)}, bf16[8,4096]{1,0:T(8,128)(2,1)S(1)}, u32[]{:S(2)}, u32[]{:S(2)}) %collective-permute-start.19) | collective-permute-done | bytes 65568 | tf_op jit(solution)/shard_map/ppermute | solution.py:24
  215.7 5.6 %collective-permute-done.24 = bf16[8,8192]{1,0:T(8,128)(2,1)S(1)} collective-permute-done((bf16[8,8192]{1,0:T(8,128)(2,1)S(1)}, bf16[8,8192]{1,0:T(8,128)(2,1)S(1)}, u32[]{:S(2)}, u32[]{:S(2)}) %collective-permute-start.24) | collective-permute-done | bytes 131104 | tf_op jit(solution)/shard_map/ppermute | solution.py:24
  230.4 17.2 %collective-permute-done.28 = bf16[4,8,8192]{2,1,0:T(8,128)(2,1)S(1)} collective-permute-done((bf16[4,8,8192]{2,1,0:T(8,128)(2,1)S(1)}, bf16[4,8,8192]{2,1,0:T(8,128)(2,1)S(1)}, u32[]{:S(2)}, u32[]{:S(2)}) %collective-permute-start.28) | collective-permute-done | bytes 524320 | tf_op jit(solution)/shard_map/ppermute | solution.py:24
  250.2 4.6 %collective-permute-start.29 = (bf16[4,4,8,8192]{3,2,1,0:T(8,128)(2,1)S(1)}, bf16[4,4,8,8192]{3,2,1,0:T(8,128)(2,1)S(1)}, u32[]{:S(2)}, u32[]{:S(2)}) collective-permute-start(bf16[4,4,8,8192]{3,2,1,0:T(8,128)(2,1)S(1)} %pad_maximum_fusion.1), channel_id=1, source_target_pairs={{0,16},{1,17},{2,18},{3,19},{4,20},{5,21},{6,22},{7,23},{8,24},{9,... | collective-permute-start | bytes 6291464 | tf_op jit(solution)/shard_map/ppermute | solution.py:24
  259.6 4.0 %shard_map.31 = f32[256,256]{1,0:T(8,128)} custom-call(bf16[128,8192]{1,0:T(8,128)(2,1)S(1)} %bitcast.144, bf16[8,32,32,256]{3,2,1,0:T(8,128)(2,1)S(1)} %bitcast.141, s32[32]{0:T(128)S(1)} %and_or_fusion.refs_0_, f32[128,256]{1,0:T(8,128)S(1)} %shard_map.30.refs_1_), custom_call_target="tpu_custom_call" | custom-call | flops 536870912 | bytes 6291456 | tf_op jit(solution)/shard_map/pallas_call | solution.py:112
  (102 shorter events, 92.6 us)
Async XLA Ops:
  6.5 12.6 %collective-permute-start.2 = (bf16[256,256]{1,0:T(8,128)(2,1)}, bf16[256,256]{1,0:T(8,128)(2,1)S(1)}, u32[]{:S(2)}, u32[]{:S(2)}) collective-permute-start(bf16[256,256]{1,0:T(8,128)(2,1)} %param.3), channel_id=1, source_target_pairs={{0,96},{1,97},{2,98},{3,99},{4,100},{5,101},{6,102},{7,103},{8,104... | collective-permute-start | bytes 393224 | tf_op jit(solution)/shard_map/ppermute | solution.py:24
  15.0 10.9 %collective-permute-start.1 = (bf16[256,256]{1,0:T(8,128)(2,1)}, bf16[256,256]{1,0:T(8,128)(2,1)S(1)}, u32[]{:S(2)}, u32[]{:S(2)}) collective-permute-start(bf16[256,256]{1,0:T(8,128)(2,1)} %param.3), channel_id=1, source_target_pairs={{0,64},{1,65},{2,66},{3,67},{4,68},{5,69},{6,70},{7,71},{8,72},{9,... | collective-permute-start | bytes 393224 | tf_op jit(solution)/shard_map/ppermute | solution.py:24
  26.9 26.3 %collective-permute-start.5 = (bf16[4,256,256]{2,1,0:T(8,128)(2,1)S(1)}, bf16[4,256,256]{2,1,0:T(8,128)(2,1)S(1)}, u32[]{:S(2)}, u32[]{:S(2)}) collective-permute-start(bf16[4,256,256]{2,1,0:T(8,128)(2,1)S(1)} %get-tuple-element.47), channel_id=1, source_target_pairs={{0,384},{1,385},{2,386},{3,387},{4,388},{5,389},{6,390},{7,391},{8... | collective-permute-start | bytes 1572872 | tf_op jit(solution)/shard_map/ppermute | solution.py:24
  31.7 21.4 %collective-permute-start.4 = (bf16[4,256,256]{2,1,0:T(8,128)(2,1)S(1)}, bf16[4,256,256]{2,1,0:T(8,128)(2,1)S(1)}, u32[]{:S(2)}, u32[]{:S(2)}) collective-permute-start(bf16[4,256,256]{2,1,0:T(8,128)(2,1)S(1)} %get-tuple-element.47), channel_id=1, source_target_pairs={{0,256},{1,257},{2,258},{3,259},{4,260},{5,261},{6,262},{7,263},{8... | collective-permute-start | bytes 1572872 | tf_op jit(solution)/shard_map/ppermute | solution.py:24
  34.2 21.3 %collective-permute-start.3 = (bf16[4,256,256]{2,1,0:T(8,128)(2,1)S(1)}, bf16[4,256,256]{2,1,0:T(8,128)(2,1)S(1)}, u32[]{:S(2)}, u32[]{:S(2)}) collective-permute-start(bf16[4,256,256]{2,1,0:T(8,128)(2,1)S(1)} %get-tuple-element.47), channel_id=1, source_target_pairs={{0,128},{1,129},{2,130},{3,131},{4,132},{5,133},{6,134},{7,135},{8... | collective-permute-start | bytes 1572872 | tf_op jit(solution)/shard_map/ppermute | solution.py:24
  67.5 18.0 %all-to-all-start = ((f32[32,8,256]{2,1,0:T(8,128)}), f32[32,8,256]{2,1,0:T(8,128)S(1)}, u32[]{:S(2)}, u32[]{:S(2)}) async-start(f32[32,8,256]{2,1,0:T(8,128)} %bitcast.11), calls=%async_computation | async-start | bytes 524288 | tf_op jit(solution)/shard_map/all_to_all | solution.py:151
  74.2 63.7 %all-gather.5.cloned.1.call-start = ((), (), s32[]{:S(2)}) async-start(), calls=%async_computation.3 | async-start | bytes 1179648 | tf_op jit(solution)/shard_map/all_gather | solution.py:164
  92.3 12.1 %collective-permute-start.10 = (bf16[8,4096]{1,0:T(8,128)(2,1)S(1)}, bf16[8,4096]{1,0:T(8,128)(2,1)S(1)}, u32[]{:S(2)}, u32[]{:S(2)}) collective-permute-start(bf16[8,4096]{1,0:T(8,128)(2,1)S(1)} %get-tuple-element.25), channel_id=1, source_target_pairs={{0,72},{1,73},{2,74},{3,75},{4,76},{5,77},{6,78},{7,79},{8,64},{9,... | collective-permute-start | bytes 196616 | tf_op jit(solution)/shard_map/ppermute | solution.py:24
  97.6 9.8 %collective-permute-start.9 = (bf16[8,4096]{1,0:T(8,128)(2,1)S(1)}, bf16[8,4096]{1,0:T(8,128)(2,1)S(1)}, u32[]{:S(2)}, u32[]{:S(2)}) collective-permute-start(bf16[8,4096]{1,0:T(8,128)(2,1)S(1)} %get-tuple-element.25), channel_id=1, source_target_pairs={{0,8},{1,9},{2,10},{3,11},{4,12},{5,13},{6,14},{7,15},{8,0},{9,1},... | collective-permute-start | bytes 196616 | tf_op jit(solution)/shard_map/ppermute | solution.py:24
  112.8 25.0 %all-to-all-start.1 = ((bf16[32,32,256]{2,1,0:T(8,128)(2,1)}), bf16[32,32,256]{2,1,0:T(8,128)(2,1)S(1)}, u32[]{:S(2)}, u32[]{:S(2)}) async-start(bf16[32,32,256]{2,1,0:T(8,128)(2,1)} %copy.15), calls=%async_computation.1 | async-start | bytes 1048576 | tf_op jit(solution)/shard_map/all_to_all | solution.py:167
  117.0 20.7 %collective-permute-start.13 = (bf16[4,8,4096]{2,1,0:T(8,128)(2,1)S(1)}, bf16[4,8,4096]{2,1,0:T(8,128)(2,1)S(1)}, u32[]{:S(2)}, u32[]{:S(2)}) collective-permute-start(bf16[4,8,4096]{2,1,0:T(8,128)(2,1)S(1)} %pad_maximum_fusion.5), channel_id=1, source_target_pairs={{0,384},{1,385},{2,386},{3,387},{4,388},{5,389},{6,390},{7,391},{8... | collective-permute-start | bytes 786440 | tf_op jit(solution)/shard_map/ppermute | solution.py:24
  121.6 16.2 %collective-permute-start.12 = (bf16[4,8,4096]{2,1,0:T(8,128)(2,1)S(1)}, bf16[4,8,4096]{2,1,0:T(8,128)(2,1)S(1)}, u32[]{:S(2)}, u32[]{:S(2)}) collective-permute-start(bf16[4,8,4096]{2,1,0:T(8,128)(2,1)S(1)} %pad_maximum_fusion.5), channel_id=1, source_target_pairs={{0,256},{1,257},{2,258},{3,259},{4,260},{5,261},{6,262},{7,263},{8... | collective-permute-start | bytes 786440 | tf_op jit(solution)/shard_map/ppermute | solution.py:24
  124.0 13.7 %collective-permute-start.11 = (bf16[4,8,4096]{2,1,0:T(8,128)(2,1)S(1)}, bf16[4,8,4096]{2,1,0:T(8,128)(2,1)S(1)}, u32[]{:S(2)}, u32[]{:S(2)}) collective-permute-start(bf16[4,8,4096]{2,1,0:T(8,128)(2,1)S(1)} %pad_maximum_fusion.5), channel_id=1, source_target_pairs={{0,128},{1,129},{2,130},{3,131},{4,132},{5,133},{6,134},{7,135},{8... | collective-permute-start | bytes 786440 | tf_op jit(solution)/shard_map/ppermute | solution.py:24
  148.2 36.1 %all-to-all-start.2 = ((bf16[8,2,8,4096]{3,2,1,0:T(8,128)(2,1)}), bf16[8,2,8,4096]{3,2,1,0:T(8,128)(2,1)S(1)}, u32[]{:S(2)}, u32[]{:S(2)}) async-start(bf16[8,2,8,4096]{3,2,1,0:T(8,128)(2,1)} %bitcast.39), calls=%async_computation.2 | async-start | bytes 2097152 | tf_op jit(solution)/shard_map/all_to_all | solution.py:197
  155.0 95.1 %all-gather.7.cloned.1.call-start = ((), (), s32[]{:S(2)}) async-start(), calls=%async_computation.4 | async-start | bytes 4718592 | tf_op jit(solution)/shard_map/all_gather | solution.py:206
  157.1 14.7 %collective-permute-start.18 = (bf16[4,8,4096]{2,1,0:T(8,128)(2,1)S(1)}, bf16[4,8,4096]{2,1,0:T(8,128)(2,1)S(1)}, u32[]{:S(2)}, u32[]{:S(2)}) collective-permute-start(bf16[4,8,4096]{2,1,0:T(8,128)(2,1)S(1)} %get-tuple-element.42), channel_id=1, source_target_pairs={{0,384},{1,385},{2,386},{3,387},{4,388},{5,389},{6,390},{7,391},{8... | collective-permute-start | bytes 786440 | tf_op jit(solution)/shard_map/ppermute | solution.py:24
  161.5 10.3 %collective-permute-start.17 = (bf16[4,8,4096]{2,1,0:T(8,128)(2,1)S(1)}, bf16[4,8,4096]{2,1,0:T(8,128)(2,1)S(1)}, u32[]{:S(2)}, u32[]{:S(2)}) collective-permute-start(bf16[4,8,4096]{2,1,0:T(8,128)(2,1)S(1)} %get-tuple-element.43), channel_id=1, source_target_pairs={{0,256},{1,257},{2,258},{3,259},{4,260},{5,261},{6,262},{7,263},{8... | collective-permute-start | bytes 786440 | tf_op jit(solution)/shard_map/ppermute | solution.py:24
  163.9 11.2 %collective-permute-start.16 = (bf16[4,8,4096]{2,1,0:T(8,128)(2,1)S(1)}, bf16[4,8,4096]{2,1,0:T(8,128)(2,1)S(1)}, u32[]{:S(2)}, u32[]{:S(2)}) collective-permute-start(bf16[4,8,4096]{2,1,0:T(8,128)(2,1)S(1)} %get-tuple-element.41), channel_id=1, source_target_pairs={{0,128},{1,129},{2,130},{3,131},{4,132},{5,133},{6,134},{7,135},{8... | collective-permute-start | bytes 786440 | tf_op jit(solution)/shard_map/ppermute | solution.py:24
  184.5 15.0 %collective-permute-start.22 = (bf16[8,4096]{1,0:T(8,128)(2,1)S(1)}, bf16[8,4096]{1,0:T(8,128)(2,1)S(1)}, u32[]{:S(2)}, u32[]{:S(2)}) collective-permute-start(bf16[8,4096]{1,0:T(8,128)(2,1)S(1)} %fusion.21), channel_id=1, source_target_pairs={{0,32},{1,33},{2,34},{3,35},{4,36},{5,37},{6,38},{7,39},{8,40},{9,... | collective-permute-start | bytes 196616 | tf_op jit(solution)/shard_map/ppermute | solution.py:24
  188.0 11.4 %collective-permute-start.21 = (bf16[8,4096]{1,0:T(8,128)(2,1)S(1)}, bf16[8,4096]{1,0:T(8,128)(2,1)S(1)}, u32[]{:S(2)}, u32[]{:S(2)}) collective-permute-start(bf16[8,4096]{1,0:T(8,128)(2,1)S(1)} %get-tuple-element.53), channel_id=1, source_target_pairs={{0,72},{1,73},{2,74},{3,75},{4,76},{5,77},{6,78},{7,79},{8,64},{9,... | collective-permute-start | bytes 196616 | tf_op jit(solution)/shard_map/ppermute | solution.py:24
  209.8 11.5 %collective-permute-start.24 = (bf16[8,8192]{1,0:T(8,128)(2,1)S(1)}, bf16[8,8192]{1,0:T(8,128)(2,1)S(1)}, u32[]{:S(2)}, u32[]{:S(2)}) collective-permute-start(bf16[8,8192]{1,0:T(8,128)(2,1)S(1)} %bitcast.159), channel_id=1, source_target_pairs={{0,64},{1,65},{2,66},{3,67},{4,68},{5,69},{6,70},{7,71},{8,72},{9,... | collective-permute-start | bytes 393224 | tf_op jit(solution)/shard_map/ppermute | solution.py:24
  221.4 26.2 %collective-permute-start.28 = (bf16[4,8,8192]{2,1,0:T(8,128)(2,1)S(1)}, bf16[4,8,8192]{2,1,0:T(8,128)(2,1)S(1)}, u32[]{:S(2)}, u32[]{:S(2)}) collective-permute-start(bf16[4,8,8192]{2,1,0:T(8,128)(2,1)S(1)} %get-tuple-element.45), channel_id=1, source_target_pairs={{0,384},{1,385},{2,386},{3,387},{4,388},{5,389},{6,390},{7,391},{8... | collective-permute-start | bytes 1572872 | tf_op jit(solution)/shard_map/ppermute | solution.py:24
  225.4 22.2 %collective-permute-start.27 = (bf16[4,8,8192]{2,1,0:T(8,128)(2,1)S(1)}, bf16[4,8,8192]{2,1,0:T(8,128)(2,1)S(1)}, u32[]{:S(2)}, u32[]{:S(2)}) collective-permute-start(bf16[4,8,8192]{2,1,0:T(8,128)(2,1)S(1)} %get-tuple-element.45), channel_id=1, source_target_pairs={{0,256},{1,257},{2,258},{3,259},{4,260},{5,261},{6,262},{7,263},{8... | collective-permute-start | bytes 1572872 | tf_op jit(solution)/shard_map/ppermute | solution.py:24
  228.1 21.8 %collective-permute-start.26 = (bf16[4,8,8192]{2,1,0:T(8,128)(2,1)S(1)}, bf16[4,8,8192]{2,1,0:T(8,128)(2,1)S(1)}, u32[]{:S(2)}, u32[]{:S(2)}) collective-permute-start(bf16[4,8,8192]{2,1,0:T(8,128)(2,1)S(1)} %get-tuple-element.45), channel_id=1, source_target_pairs={{0,128},{1,129},{2,130},{3,131},{4,132},{5,133},{6,134},{7,135},{8... | collective-permute-start | bytes 1572872 | tf_op jit(solution)/shard_map/ppermute | solution.py:24
  (15 other events, 102.6 us)
Sparse Core Ops, SparseCore 0:
  92.4 37.2 all-gather.4
  184.4 50.7 all-gather.6

commit v7 on v6

v7 whole, which is shorter than its diff:
```python
import functools

import jax
import jax.numpy as jnp
from jax import lax
from jax.experimental import pallas as pl
from jax.experimental.pallas import tpu as pltpu
from jax.sharding import PartitionSpec as P

epsilon = 1e-05
redundancy_weight = 0.0051
loss_scale = 512.0
DP = 32
MP = 16
Y = 8
GROUPS = [list(range(Y)), list(range(Y, MP))]
ALONG_X = [(8,), (16,), (24,)]
ARRIVAL = (0, 1, 3, 2)
ALONG_Z = [(2,), (4,), (6,)]
STRIDED_Z = [(4,), (0, 8), (4, 8)]


def swap(array, data, model=0):
    mask = data * MP + model
    return lax.ppermute(array, ("dp", "mp"), [(i, i ^ mask) for i in range(DP * MP)])


def partner(array):
    return swap(array, 2)


def gather(block, masks):
    return jnp.stack([block] + [swap(block, *mask) for mask in masks])


def add(blocks, masks):
    parts = [blocks[0]] + [swap(blocks[k + 1], *mask) for k, mask in enumerate(masks)]
    return sum(part.astype(jnp.float32) for part in parts)


def project_kernel(first, last, order_ref, inputs_ref, own_ref, other_ref, *refs):
    out_ref = refs[-1]
    blocks, depth, _ = own_ref.shape
    result = None if first else refs[0][...]
    for core, weight_ref in enumerate((own_ref, other_ref)):
        for k in range(blocks):
            start = pl.multiple_of(order_ref[core * blocks + k] * depth, depth)
            part = jnp.dot(
                inputs_ref[:, pl.ds(start, depth)], weight_ref[k], preferred_element_type=jnp.float32
            )
            result = part if result is None else result + part
    out_ref[...] = result.T if last else result


def project(order, inputs, own, other, before=None, last=False):
    rows, feat = inputs.shape[0], own.shape[2]
    operands = (inputs, own, other) if before is None else (inputs, own, other, before)
    return pl.pallas_call(
        functools.partial(project_kernel, before is None, last),
        in_specs=[pl.BlockSpec(memory_space=pltpu.SMEM)]
        + [pl.BlockSpec(memory_space=pltpu.VMEM)] * len(operands),
        out_specs=pl.BlockSpec(memory_space=pltpu.VMEM),
        out_shape=jax.ShapeDtypeStruct((feat, rows) if last else (rows, feat), jnp.float32),
        compiler_params=pltpu.CompilerParams(vmem_limit_bytes=32 * 1024 * 1024),
        cost_estimate=pl.CostEstimate(
            flops=4 * rows * feat * own.shape[0] * own.shape[1],
            bytes_accessed=2 * 1024 * 1024,
            transcendentals=0,
        ),
    )(order, *operands)


def weight_kernel(own_ref, other_ref, columns_ref, *refs):
    *before, total_ref = refs
    step = pl.program_id(0) * pl.num_programs(1) + pl.program_id(1)
    half = own_ref.shape[0]

    @pl.when(step == 0)
    def _():
        total_ref[...] = jnp.zeros_like(total_ref)

    quarters, devices, share, rows = columns_ref.shape
    pieces = [columns_ref[:, d].reshape(quarters * share, rows) for d in range(devices)]
    columns = jnp.concatenate(pieces, axis=0)
    grad = jnp.concatenate([own_ref[...], other_ref[...]], axis=0)
    total_ref[...] += jnp.dot(grad, columns, preferred_element_type=jnp.float32)

    if before:
        position_ref, *parts, out_ref, placed_ref = before

        @pl.when(step == pl.num_programs(0) * pl.num_programs(1) - 1)
        def _():
            for k, part in enumerate(parts + [total_ref]):
                placed_ref[2 * half * k : 2 * half * (k + 1)] = part[...]
            blocks = [
                placed_ref[pl.ds(pl.multiple_of(position_ref[block] * 8, 8), 8)] for block in range(DP)
            ]
            out_ref[...] = jnp.concatenate(blocks, axis=0).T


def weight_part(own, other, columns, position=None, parts=()):
    half, depth = own.shape
    slices, devices, share, rows = columns.shape
    quarters, group = slices // 2, 8
    features = 2 * half * (len(parts) + 1)
    grad_spec = pl.BlockSpec(
        (half, group * quarters * share), lambda v, d: (0, v * (devices // group) + d)
    )
    in_specs = [
        grad_spec,
        grad_spec,
        pl.BlockSpec((quarters, group, share, rows), lambda v, d: (v, d, 0, 0)),
    ]
    scratch = []
    if parts:
        in_specs.append(pl.BlockSpec(memory_space=pltpu.SMEM))
        in_specs += [pl.BlockSpec((2 * half, rows), lambda v, d: (0, 0))] * len(parts)
        scratch = [pltpu.VMEM((features, rows), jnp.float32), pltpu.VMEM((2 * half, rows), jnp.float32)]
    shape = (rows, features) if parts else (2 * half, rows)
    return pl.pallas_call(
        weight_kernel,
        grid=(2, devices // group),
        in_specs=in_specs,
        out_specs=pl.BlockSpec(shape, lambda v, d: (0, 0)),
        out_shape=jax.ShapeDtypeStruct(shape, jnp.float32),
        scratch_shapes=scratch,
        compiler_params=pltpu.CompilerParams(vmem_limit_bytes=32 * 1024 * 1024),
        cost_estimate=pl.CostEstimate(
            flops=4 * half * depth * rows, bytes_accessed=5 * 1024 * 1024, transcendentals=0
        ),
    )(own, other, columns, *((position, *parts) if parts else ()))


def per_device(inputs, weight):
    views, images, width = inputs.shape
    total = images * DP
    data_index = lax.axis_index("dp")
    model_index = lax.axis_index("mp")
    feat = weight.shape[1]
    block = feat // DP
    rows = width // DP
    flat = inputs.reshape(views * images, width)

    place = jnp.arange(DP, dtype=jnp.int32)
    order = data_index ^ ((place >> 3) << 3 | (place & 3) << 1 | ((place >> 2) & 1))
    relative = place ^ data_index
    position = (relative >> 3) << 3 | (relative & 1) << 2 | ((relative >> 1) & 3)

    share = views * images // Y
    mine = lax.dynamic_slice_in_dim(flat, lax.rem(model_index, Y) * share, share, axis=0)
    pieces = mine.reshape(share, DP, rows).transpose(1, 0, 2)
    along_z = gather(weight, ALONG_Z)
    parts = [along_z] + [swap(along_z, *mask) for mask in ALONG_X]
    projected = None
    for k in ARRIVAL:
        projected = project(
            order[8 * k : 8 * k + 8], flat, parts[k], swap(parts[k], 1), projected, k == ARRIVAL[-1]
        )

    own = lax.all_to_all(
        projected.reshape(DP, block, views * images), "dp", split_axis=0, concat_axis=0
    ).reshape(DP, block, views, images)
    average = jnp.sum(own, axis=(0, 3), keepdims=True) / total
    centered = own - average
    variance = jnp.sum(centered * centered, axis=(0, 3), keepdims=True) / total
    inverse = lax.rsqrt(variance + epsilon)
    normed = (centered * inverse).astype(jnp.bfloat16).transpose(2, 1, 0, 3).reshape(views, block, total)
    inverse = inverse.reshape(block, views).T[:, :, None]

    first, second, pieces = lax.optimization_barrier((normed[0], normed[1], pieces))
    pair = jnp.stack([second, partner(second)])
    first, pair = lax.optimization_barrier((first, pair))
    columns_b = lax.all_gather(pair, "mp", axis=0, axis_index_groups=GROUPS)
    columns_b = columns_b.reshape(MP * block, total)
    along_z, pieces = lax.optimization_barrier((gather(first, STRIDED_Z), pieces))
    slices = lax.all_to_all(pieces, "dp", split_axis=0, concat_axis=0)
    rows_own, columns_b, slices = lax.optimization_barrier(
        (gather(along_z, ALONG_X), columns_b, slices)
    )
    rows_other = swap(rows_own, 1).reshape(feat // 2, total)
    rows_own = rows_own.reshape(feat // 2, total)

    def gradient_of(rows_a, with_diagonal):
        correlation = (
            lax.dot_general(rows_a, columns_b, (((1,), (1,)), ((), ())), preferred_element_type=jnp.float32)
            / total
        )
        inner = 2.0 * redundancy_weight * correlation
        if with_diagonal:
            row = lax.broadcasted_iota(jnp.int32, correlation.shape, 0)
            column = lax.broadcasted_iota(jnp.int32, correlation.shape, 1)
            diagonal = (row < block) & (column == lax.rem(model_index, Y) * 2 * block + row)
            inner = inner + diagonal.astype(jnp.float32) * (2.0 * (correlation - 1.0) - inner)
        return (loss_scale * inner).astype(jnp.bfloat16)

    corr_own = gradient_of(rows_own, True)
    corr_other = gradient_of(rows_other, False)

    def times(lhs, rhs, dims):
        return lax.dot_general(lhs, rhs, (dims, ((), ())), preferred_element_type=jnp.float32) / total

    half = (feat // 2, Y, 2, block)
    sides = [
        corr.reshape(half).transpose(2, 0, 1, 3).reshape(2, feat // 2, Y * block)
        for corr in (corr_own, corr_other)
    ]
    terms_b = [
        times(sides[0][k], rows_own, ((0,), (0,))) + times(sides[1][k], rows_other, ((0,), (0,)))
        for k in (0, 1)
    ]
    away = terms_b[1].astype(jnp.bfloat16)
    corr_own, corr_other, away = lax.optimization_barrier((corr_own, corr_other, away))
    terms_b = (terms_b[0] + partner(away).astype(jnp.float32)).astype(jnp.bfloat16)
    terms_b = lax.all_to_all(
        terms_b.reshape(Y, block, total), "mp", split_axis=0, concat_axis=0, axis_index_groups=GROUPS
    )
    terms_b, slices = lax.optimization_barrier((terms_b, slices))
    columns = lax.all_gather(slices, "mp", axis=0, axis_index_groups=GROUPS)
    grad_b = jnp.sum(terms_b.astype(jnp.float32), axis=0)
    terms_other = times(corr_other, columns_b, ((1,), (0,))).astype(jnp.bfloat16)
    terms_own = times(corr_own, columns_b, ((1,), (0,)))
    shape = (4, 4, block, total)
    both = terms_own.reshape(shape) + swap(terms_other.reshape(shape), 1).astype(jnp.float32)
    along_x = add(both.astype(jnp.bfloat16), ALONG_X).astype(jnp.bfloat16)
    grads = jnp.stack([add(along_x, STRIDED_Z), grad_b])
    wide = normed.astype(jnp.float32)
    grad_mean = jnp.sum(grads, axis=2, keepdims=True) / total
    cross_mean = jnp.sum(grads * wide, axis=2, keepdims=True) / total
    grad_proj = ((grads - grad_mean - wide * cross_mean) * inverse).astype(jnp.bfloat16)
    grad_proj = grad_proj.transpose(1, 0, 2).reshape(block, views * total)
    along_z = gather(grad_proj, ALONG_Z)
    parts = [along_z] + [swap(along_z, *mask) for mask in ALONG_X]
    shape = (4 * block, views * total)
    pairs = [(part.reshape(shape), swap(part, 1).reshape(shape)) for part in parts]
    products = [weight_part(*pairs[k], columns) for k in ARRIVAL[:-1]]
    turn = sum(jnp.where(position // 8 == k, place, 0) for place, k in enumerate(ARRIVAL))
    position = turn * 8 + position % 8
    return weight_part(*pairs[ARRIVAL[-1]], columns, position, products)


def solution(mesh):
    placed = (P(None, "dp", None), P("dp", "mp"))
    return jax.shard_map(
        per_device, mesh=mesh, in_specs=placed, out_specs=P("dp", "mp"), check_vma=False
    )
```

time: 272 us -> 300 us (1.10)
  starting transfers between devices: 119 us -> 155 us
  waiting for transfers between devices: 109 us -> 88.6 us
  Pallas kernels: 10.9 us -> 21 us
    ppermute x30 -> x36, starting transfers between devices: 101 us -> 138 us  [swap(): lax.ppermute(array, ('dp', 'mp'), [(i, i ^ mask) for i in range(DP * MP)])]
    ppermute x30 -> x36, waiting for transfers between devices: 89.6 us -> 62 us  [swap(): lax.ppermute(array, ('dp', 'mp'), [(i, i ^ mask) for i in range(DP * MP)])]
    pallas_call x4 -> x8, Pallas kernels: 10.9 us -> 21 us  [the longest x4 15.3 us: weight_part(): pl.pallas_call(weight_kernel, grid=(2, devices // group), in_specs=in_spe...]
    all_to_all x1, waiting for transfers between devices: 9 us -> 16.5 us  [per_device(): lax.all_to_all(terms_b.reshape(Y, block, total), 'mp', split_axis=0, conc...]
  transfers between devices with their start and end apart: 35 -> 41, of which waited for: 17 -> 17; matrix products, arithmetic and copies ran while one was open for 3% -> 4% of each run, Pallas kernels for 1% -> 5%
where the time goes in v7:
time: 300 us; the launch traced here: 298 us
  starting transfers between devices  155 us (52%)
  waiting for transfers between devices  88.6 us (30%)
  Pallas kernels  21 us (7%)
  between operations  14.1 us (5%)
  local copies, waits for them, and re-layouts  6.89 us (2%)
  matrix products  6.12 us (2%)
  other arithmetic  5.51 us (2%)
    ppermute x36, starting transfers between devices, swap(): lax.ppermute(array, ('dp', 'mp'), [(i, i ^ mask) for i in range(DP * MP)])  138 us
    ppermute x36, waiting for transfers between devices, swap(): lax.ppermute(array, ('dp', 'mp'), [(i, i ^ mask) for i in range(DP * MP)])  62 us
    all_to_all x1, waiting for transfers between devices, per_device(): lax.all_to_all(terms_b.reshape(Y, block, total), 'mp', split_axis=0, conc...  16.5 us
    pallas_call x4, Pallas kernels, weight_part(): pl.pallas_call(weight_kernel, grid=(2, devices // group), in_specs=in_spe...  15.3 us
    all_to_all x1, waiting for transfers between devices, per_device(): lax.all_to_all(projected.reshape(DP, block, views * images), 'dp', split_...  10 us
    all_to_all x1, starting transfers between devices, per_device(): lax.all_to_all(terms_b.reshape(Y, block, total), 'mp', split_axis=0, conc...  6.82 us
  transfers between devices with their start and end apart: 41, of which 17 were waited for; matrix products, arithmetic and copies ran while one was open for 4% of the time, Pallas kernels for 5%

profile of v7, /device:TPU:1, one launch (start us, length us, event | category | flops | bytes accessed | tf_op | source)
XLA Modules:
  0.0 297.5 jit_solution(10446148959899401713)
XLA Ops:
  6.5 8.4 %collective-permute-start.2 = (bf16[256,256]{1,0:T(8,128)(2,1)}, bf16[256,256]{1,0:T(8,128)(2,1)S(1)}, u32[]{:S(2)}, u32[]{:S(2)}) collective-permute-start(bf16[256,256]{1,0:T(8,128)(2,1)} %param.3), channel_id=1, source_target_pairs={{0,96},{1,97},{2,98},{3,99},{4,100},{5,101},{6,102},{7,103},{8,104... | collective-permute-start | bytes 393224 | tf_op jit(solution)/shard_map/ppermute | solution.py:25
  19.1 6.7 %collective-permute-done.1 = bf16[256,256]{1,0:T(8,128)(2,1)S(1)} collective-permute-done((bf16[256,256]{1,0:T(8,128)(2,1)}, bf16[256,256]{1,0:T(8,128)(2,1)S(1)}, u32[]{:S(2)}, u32[]{:S(2)}) %collective-permute-start.1) | collective-permute-done | bytes 131104 | tf_op jit(solution)/shard_map/ppermute | solution.py:25
  40.6 6.9 %collective-permute-start.8 = (bf16[4,256,256]{2,1,0:T(8,128)(2,1)S(1)}, bf16[4,256,256]{2,1,0:T(8,128)(2,1)}, u32[]{:S(2)}, u32[]{:S(2)}) collective-permute-start(bf16[4,256,256]{2,1,0:T(8,128)(2,1)S(1)} %collective-permute-done.7.own_ref), channel_id=1, source_target_pairs={{0,16},{1,17},{2,18},{3,19},{4,20},{5,21},{6,22},{7,23},{8,24},{9,... | collective-permute-start | bytes 1572872 | tf_op jit(solution)/shard_map/ppermute | solution.py:25
  47.5 7.4 %collective-permute-done.5.own_ref = bf16[4,256,256]{2,1,0:T(8,128)(2,1)S(1)} collective-permute-done((bf16[4,256,256]{2,1,0:T(8,128)(2,1)S(1)}, bf16[4,256,256]{2,1,0:T(8,128)(2,1)S(1)}, u32[]{:S(2)}, u32[]{:S(2)}) %collective-permute-start.5) | collective-permute-done | bytes 524320 | tf_op jit(solution)/shard_map/ppermute | solution.py:25
  54.9 6.1 %collective-permute-start.6 = (bf16[4,256,256]{2,1,0:T(8,128)(2,1)S(1)}, bf16[4,256,256]{2,1,0:T(8,128)(2,1)S(1)}, u32[]{:S(2)}, u32[]{:S(2)}) collective-permute-start(bf16[4,256,256]{2,1,0:T(8,128)(2,1)S(1)} %collective-permute-done.5.own_ref), channel_id=1, source_target_pairs={{0,16},{1,17},{2,18},{3,19},{4,20},{5,21},{6,22},{7,23},{8,24},{9,... | collective-permute-start | bytes 1572872 | tf_op jit(solution)/shard_map/ppermute | solution.py:25
  71.0 5.7 %all-to-all-start = ((f32[32,8,256]{2,1,0:T(8,128)}), f32[32,8,256]{2,1,0:T(8,128)S(1)}, u32[]{:S(2)}, u32[]{:S(2)}) async-start(f32[32,8,256]{2,1,0:T(8,128)} %bitcast.5), calls=%async_computation | async-start | bytes 524288 | tf_op jit(solution)/shard_map/all_to_all | solution.py:160
  78.0 10.0 %all-to-all-done = f32[32,8,256]{2,1,0:T(8,128)S(1)} async-done(((f32[32,8,256]{2,1,0:T(8,128)}), f32[32,8,256]{2,1,0:T(8,128)S(1)}, u32[]{:S(2)}, u32[]{:S(2)}) %all-to-all-start) | async-done | bytes 262176 | tf_op jit(solution)/shard_map/all_to_all | solution.py:160
  94.8 5.4 %collective-permute-start.13 = (bf16[8,4096]{1,0:T(8,128)(2,1)S(1)}, bf16[8,4096]{1,0:T(8,128)(2,1)S(1)}, u32[]{:S(2)}, u32[]{:S(2)}) collective-permute-start(bf16[8,4096]{1,0:T(8,128)(2,1)S(1)} %get-tuple-element.22), channel_id=1, source_target_pairs={{0,72},{1,73},{2,74},{3,75},{4,76},{5,77},{6,78},{7,79},{8,64},{9,... | collective-permute-start | bytes 196616 | tf_op jit(solution)/shard_map/ppermute | solution.py:25
  100.2 4.5 %collective-permute-start.12 = (bf16[8,4096]{1,0:T(8,128)(2,1)S(1)}, bf16[8,4096]{1,0:T(8,128)(2,1)S(1)}, u32[]{:S(2)}, u32[]{:S(2)}) collective-permute-start(bf16[8,4096]{1,0:T(8,128)(2,1)S(1)} %get-tuple-element.22), channel_id=1, source_target_pairs={{0,8},{1,9},{2,10},{3,11},{4,12},{5,13},{6,14},{7,15},{8,0},{9,1},... | collective-permute-start | bytes 196616 | tf_op jit(solution)/shard_map/ppermute | solution.py:25
  109.9 4.3 %collective-permute-done.11 = bf16[8,4096]{1,0:T(8,128)(2,1)S(1)} collective-permute-done((bf16[8,4096]{1,0:T(8,128)(2,1)S(1)}, bf16[8,4096]{1,0:T(8,128)(2,1)S(1)}, u32[]{:S(2)}, u32[]{:S(2)}) %collective-permute-start.11) | collective-permute-done | bytes 65568 | tf_op jit(solution)/shard_map/ppermute | solution.py:25
  115.4 4.2 %all-to-all-start.1 = ((bf16[32,32,256]{2,1,0:T(8,128)(2,1)}), bf16[32,32,256]{2,1,0:T(8,128)(2,1)S(1)}, u32[]{:S(2)}, u32[]{:S(2)}) async-start(bf16[32,32,256]{2,1,0:T(8,128)(2,1)} %copy.15), calls=%async_computation.1 | async-start | bytes 1048576 | tf_op jit(solution)/shard_map/all_to_all | solution.py:176
  119.6 4.5 %collective-permute-start.16 = (bf16[4,8,4096]{2,1,0:T(8,128)(2,1)S(1)}, bf16[4,8,4096]{2,1,0:T(8,128)(2,1)S(1)}, u32[]{:S(2)}, u32[]{:S(2)}) collective-permute-start(bf16[4,8,4096]{2,1,0:T(8,128)(2,1)S(1)} %pad_maximum_fusion.3), channel_id=1, source_target_pairs={{0,384},{1,385},{2,386},{3,387},{4,388},{5,389},{6,390},{7,391},{8... | collective-permute-start | bytes 786440 | tf_op jit(solution)/shard_map/ppermute | solution.py:25
  128.6 11.7 %collective-permute-done.16 = bf16[4,8,4096]{2,1,0:T(8,128)(2,1)S(1)} collective-permute-done((bf16[4,8,4096]{2,1,0:T(8,128)(2,1)S(1)}, bf16[4,8,4096]{2,1,0:T(8,128)(2,1)S(1)}, u32[]{:S(2)}, u32[]{:S(2)}) %collective-permute-start.16) | collective-permute-done | bytes 262176 | tf_op jit(solution)/shard_map/ppermute | solution.py:25
  154.4 7.5 %collective-permute-done.25 = bf16[64,4096]{1,0:T(8,128)(2,1)S(1)} collective-permute-done((bf16[64,4096]{1,0:T(8,128)(2,1)S(1)}, bf16[64,4096]{1,0:T(8,128)(2,1)S(1)}, u32[]{:S(2)}, u32[]{:S(2)}) %collective-permute-start.25) | collective-permute-done | bytes 524320 | tf_op jit(solution)/shard_map/ppermute | solution.py:25
  163.1 6.8 %all-to-all-start.2 = ((bf16[8,8,4096]{2,1,0:T(8,128)(2,1)}), bf16[8,8,4096]{2,1,0:T(8,128)(2,1)}, u32[]{:S(2)}, u32[]{:S(2)}) async-start(bf16[8,8,4096]{2,1,0:T(8,128)(2,1)} %fusion.6), calls=%async_computation.2 | async-start | bytes 1048576 | tf_op jit(solution)/shard_map/all_to_all | solution.py:214
  170.4 16.5 %all-to-all-done.2 = bf16[8,8,4096]{2,1,0:T(8,128)(2,1)} async-done(((bf16[8,8,4096]{2,1,0:T(8,128)(2,1)}), bf16[8,8,4096]{2,1,0:T(8,128)(2,1)}, u32[]{:S(2)}, u32[]{:S(2)}) %all-to-all-start.2) | async-done | bytes 524320 | tf_op jit(solution)/shard_map/all_to_all | solution.py:214
  200.9 4.8 %collective-permute-done.19 = bf16[4,8,4096]{2,1,0:T(8,128)(2,1)S(1)} collective-permute-done((bf16[4,8,4096]{2,1,0:T(8,128)(2,1)S(1)}, bf16[4,8,4096]{2,1,0:T(8,128)(2,1)S(1)}, u32[]{:S(2)}, u32[]{:S(2)}) %collective-permute-start.19) | collective-permute-done | bytes 262176 | tf_op jit(solution)/shard_map/ppermute | solution.py:25
  209.6 4.5 %collective-permute-start.23 = (bf16[8,4096]{1,0:T(8,128)(2,1)S(1)}, bf16[8,4096]{1,0:T(8,128)(2,1)S(1)}, u32[]{:S(2)}, u32[]{:S(2)}) collective-permute-start(bf16[8,4096]{1,0:T(8,128)(2,1)S(1)} %get-tuple-element.44), channel_id=1, source_target_pairs={{0,8},{1,9},{2,10},{3,11},{4,12},{5,13},{6,14},{7,15},{8,0},{9,1},... | collective-permute-start | bytes 196616 | tf_op jit(solution)/shard_map/ppermute | solution.py:25
  228.3 4.5 %collective-permute-start.26 = (bf16[8,8192]{1,0:T(8,128)(2,1)S(1)}, bf16[8,8192]{1,0:T(8,128)(2,1)S(1)}, u32[]{:S(2)}, u32[]{:S(2)}) collective-permute-start(bf16[8,8192]{1,0:T(8,128)(2,1)S(1)} %bitcast.175), channel_id=1, source_target_pairs={{0,32},{1,33},{2,34},{3,35},{4,36},{5,37},{6,38},{7,39},{8,40},{9,... | collective-permute-start | bytes 393224 | tf_op jit(solution)/shard_map/ppermute | solution.py:25
  246.7 6.7 %collective-permute-start.31 = (bf16[4,8,8192]{2,1,0:T(8,128)(2,1)S(1)}, bf16[4,8,8192]{2,1,0:T(8,128)(2,1)S(1)}, u32[]{:S(2)}, u32[]{:S(2)}) collective-permute-start(bf16[4,8,8192]{2,1,0:T(8,128)(2,1)S(1)} %get-tuple-element.39), channel_id=1, source_target_pairs={{0,16},{1,17},{2,18},{3,19},{4,20},{5,21},{6,22},{7,23},{8,24},{9,... | collective-permute-start | bytes 1572872 | tf_op jit(solution)/shard_map/ppermute | solution.py:25
  253.4 6.6 %collective-permute-start.33 = (bf16[4,8,8192]{2,1,0:T(8,128)(2,1)S(1)}, bf16[4,8,8192]{2,1,0:T(8,128)(2,1)}, u32[]{:S(2)}, u32[]{:S(2)}) collective-permute-start(bf16[4,8,8192]{2,1,0:T(8,128)(2,1)S(1)} %collective-permute-done.32), channel_id=1, source_target_pairs={{0,16},{1,17},{2,18},{3,19},{4,20},{5,21},{6,22},{7,23},{8,24},{9,... | collective-permute-start | bytes 1572872 | tf_op jit(solution)/shard_map/ppermute | solution.py:25
  260.0 11.1 %collective-permute-start.35 = (bf16[4,8,8192]{2,1,0:T(8,128)(2,1)S(1)}, bf16[4,8,8192]{2,1,0:T(8,128)(2,1)}, u32[]{:S(2)}, u32[]{:S(2)}) collective-permute-start(bf16[4,8,8192]{2,1,0:T(8,128)(2,1)S(1)} %collective-permute-done.34), channel_id=1, source_target_pairs={{0,16},{1,17},{2,18},{3,19},{4,20},{5,21},{6,22},{7,23},{8,24},{9,... | collective-permute-start | bytes 1572872 | tf_op jit(solution)/shard_map/ppermute | solution.py:25
  277.6 4.6 %shard_map.33.refs_2_ = f32[64,256]{1,0:T(8,128)S(1)} custom-call(bf16[32,8192]{1,0:T(8,128)(2,1)S(1)} %bitcast.154, bf16[32,8192]{1,0:T(8,128)(2,1)} %bitcast.67.other_ref, bf16[8,32,32,256]{3,2,1,0:T(8,128)(2,1)S(1)} %bitcast.148), custom_call_target="tpu_custom_call" | custom-call | flops 268435456 | bytes 5242880 | tf_op jit(solution)/shard_map/pallas_call | solution.py:120
  282.3 4.6 %shard_map.34.refs_3_ = f32[64,256]{1,0:T(8,128)S(1)} custom-call(bf16[32,8192]{1,0:T(8,128)(2,1)S(1)} %bitcast.153, bf16[32,8192]{1,0:T(8,128)(2,1)} %bitcast.69.other_ref, bf16[8,32,32,256]{3,2,1,0:T(8,128)(2,1)S(1)} %bitcast.149), custom_call_target="tpu_custom_call" | custom-call | flops 268435456 | bytes 5242880 | tf_op jit(solution)/shard_map/pallas_call | solution.py:120
  (116 shorter events, 119.2 us)
Async XLA Ops:
  6.5 12.6 %collective-permute-start.2 = (bf16[256,256]{1,0:T(8,128)(2,1)}, bf16[256,256]{1,0:T(8,128)(2,1)S(1)}, u32[]{:S(2)}, u32[]{:S(2)}) collective-permute-start(bf16[256,256]{1,0:T(8,128)(2,1)} %param.3), channel_id=1, source_target_pairs={{0,96},{1,97},{2,98},{3,99},{4,100},{5,101},{6,102},{7,103},{8,104... | collective-permute-start | bytes 393224 | tf_op jit(solution)/shard_map/ppermute | solution.py:25
  26.8 13.8 %collective-permute-start.7 = (bf16[4,256,256]{2,1,0:T(8,128)(2,1)S(1)}, bf16[4,256,256]{2,1,0:T(8,128)(2,1)S(1)}, u32[]{:S(2)}, u32[]{:S(2)}) collective-permute-start(bf16[4,256,256]{2,1,0:T(8,128)(2,1)S(1)} %pad_maximum_fusion.1.own_ref), channel_id=1, source_target_pairs={{0,128},{1,129},{2,130},{3,131},{4,132},{5,133},{6,134},{7,135},{8... | collective-permute-start | bytes 1572872 | tf_op jit(solution)/shard_map/ppermute | solution.py:25
  30.4 24.5 %collective-permute-start.5 = (bf16[4,256,256]{2,1,0:T(8,128)(2,1)S(1)}, bf16[4,256,256]{2,1,0:T(8,128)(2,1)S(1)}, u32[]{:S(2)}, u32[]{:S(2)}) collective-permute-start(bf16[4,256,256]{2,1,0:T(8,128)(2,1)S(1)} %pad_maximum_fusion.1.own_ref), channel_id=1, source_target_pairs={{0,384},{1,385},{2,386},{3,387},{4,388},{5,389},{6,390},{7,391},{8... | collective-permute-start | bytes 1572872 | tf_op jit(solution)/shard_map/ppermute | solution.py:25
  34.2 26.9 %collective-permute-start.3 = (bf16[4,256,256]{2,1,0:T(8,128)(2,1)S(1)}, bf16[4,256,256]{2,1,0:T(8,128)(2,1)S(1)}, u32[]{:S(2)}, u32[]{:S(2)}) collective-permute-start(bf16[4,256,256]{2,1,0:T(8,128)(2,1)S(1)} %pad_maximum_fusion.1.own_ref), channel_id=1, source_target_pairs={{0,256},{1,257},{2,258},{3,259},{4,260},{5,261},{6,262},{7,263},{8... | collective-permute-start | bytes 1572872 | tf_op jit(solution)/shard_map/ppermute | solution.py:25
  36.7 26.3 %collective-permute-start.9 = (bf16[4,256,256]{2,1,0:T(8,128)(2,1)S(1)}, bf16[4,256,256]{2,1,0:T(8,128)(2,1)}, u32[]{:S(2)}, u32[]{:S(2)}) collective-permute-start(bf16[4,256,256]{2,1,0:T(8,128)(2,1)S(1)} %pad_maximum_fusion.1.own_ref), channel_id=1, source_target_pairs={{0,16},{1,17},{2,18},{3,19},{4,20},{5,21},{6,22},{7,23},{8,24},{9,... | collective-permute-start | bytes 1572872 | tf_op jit(solution)/shard_map/ppermute | solution.py:25
  40.6 26.1 %collective-permute-start.8 = (bf16[4,256,256]{2,1,0:T(8,128)(2,1)S(1)}, bf16[4,256,256]{2,1,0:T(8,128)(2,1)}, u32[]{:S(2)}, u32[]{:S(2)}) collective-permute-start(bf16[4,256,256]{2,1,0:T(8,128)(2,1)S(1)} %collective-permute-done.7.own_ref), channel_id=1, source_target_pairs={{0,16},{1,17},{2,18},{3,19},{4,20},{5,21},{6,22},{7,23},{8,24},{9,... | collective-permute-start | bytes 1572872 | tf_op jit(solution)/shard_map/ppermute | solution.py:25
  54.9 13.4 %collective-permute-start.6 = (bf16[4,256,256]{2,1,0:T(8,128)(2,1)S(1)}, bf16[4,256,256]{2,1,0:T(8,128)(2,1)S(1)}, u32[]{:S(2)}, u32[]{:S(2)}) collective-permute-start(bf16[4,256,256]{2,1,0:T(8,128)(2,1)S(1)} %collective-permute-done.5.own_ref), channel_id=1, source_target_pairs={{0,16},{1,17},{2,18},{3,19},{4,20},{5,21},{6,22},{7,23},{8,24},{9,... | collective-permute-start | bytes 1572872 | tf_op jit(solution)/shard_map/ppermute | solution.py:25
  71.0 17.0 %all-to-all-start = ((f32[32,8,256]{2,1,0:T(8,128)}), f32[32,8,256]{2,1,0:T(8,128)S(1)}, u32[]{:S(2)}, u32[]{:S(2)}) async-start(f32[32,8,256]{2,1,0:T(8,128)} %bitcast.5), calls=%async_computation | async-start | bytes 524288 | tf_op jit(solution)/shard_map/all_to_all | solution.py:160
  76.8 63.7 %all-gather.5.cloned.1.call-start = ((), (), s32[]{:S(2)}) async-start(), calls=%async_computation.3 | async-start | bytes 1179648 | tf_op jit(solution)/shard_map/all_gather | solution.py:173
  115.4 25.0 %all-to-all-start.1 = ((bf16[32,32,256]{2,1,0:T(8,128)(2,1)}), bf16[32,32,256]{2,1,0:T(8,128)(2,1)S(1)}, u32[]{:S(2)}, u32[]{:S(2)}) async-start(bf16[32,32,256]{2,1,0:T(8,128)(2,1)} %copy.15), calls=%async_computation.1 | async-start | bytes 1048576 | tf_op jit(solution)/shard_map/all_to_all | solution.py:176
  119.6 20.7 %collective-permute-start.16 = (bf16[4,8,4096]{2,1,0:T(8,128)(2,1)S(1)}, bf16[4,8,4096]{2,1,0:T(8,128)(2,1)S(1)}, u32[]{:S(2)}, u32[]{:S(2)}) collective-permute-start(bf16[4,8,4096]{2,1,0:T(8,128)(2,1)S(1)} %pad_maximum_fusion.3), channel_id=1, source_target_pairs={{0,384},{1,385},{2,386},{3,387},{4,388},{5,389},{6,390},{7,391},{8... | collective-permute-start | bytes 786440 | tf_op jit(solution)/shard_map/ppermute | solution.py:25
  124.1 16.2 %collective-permute-start.15 = (bf16[4,8,4096]{2,1,0:T(8,128)(2,1)S(1)}, bf16[4,8,4096]{2,1,0:T(8,128)(2,1)S(1)}, u32[]{:S(2)}, u32[]{:S(2)}) collective-permute-start(bf16[4,8,4096]{2,1,0:T(8,128)(2,1)S(1)} %pad_maximum_fusion.3), channel_id=1, source_target_pairs={{0,256},{1,257},{2,258},{3,259},{4,260},{5,261},{6,262},{7,263},{8... | collective-permute-start | bytes 786440 | tf_op jit(solution)/shard_map/ppermute | solution.py:25
  126.6 13.7 %collective-permute-start.14 = (bf16[4,8,4096]{2,1,0:T(8,128)(2,1)S(1)}, bf16[4,8,4096]{2,1,0:T(8,128)(2,1)S(1)}, u32[]{:S(2)}, u32[]{:S(2)}) collective-permute-start(bf16[4,8,4096]{2,1,0:T(8,128)(2,1)S(1)} %pad_maximum_fusion.3), channel_id=1, source_target_pairs={{0,128},{1,129},{2,130},{3,131},{4,132},{5,133},{6,134},{7,135},{8... | collective-permute-start | bytes 786440 | tf_op jit(solution)/shard_map/ppermute | solution.py:25
  146.5 15.4 %collective-permute-start.25 = (bf16[64,4096]{1,0:T(8,128)(2,1)S(1)}, bf16[64,4096]{1,0:T(8,128)(2,1)S(1)}, u32[]{:S(2)}, u32[]{:S(2)}) collective-permute-start(bf16[64,4096]{1,0:T(8,128)(2,1)S(1)} %fusion.5), channel_id=1, source_target_pairs={{0,32},{1,33},{2,34},{3,35},{4,36},{5,37},{6,38},{7,39},{8,40},{9,... | collective-permute-start | bytes 1572872 | tf_op jit(solution)/shard_map/ppermute | solution.py:25
  151.9 35.0 %collective-permute-start.18 = (bf16[4,4,8,4096]{3,2,1,0:T(8,128)(2,1)}, bf16[4,4,8,4096]{3,2,1,0:T(8,128)(2,1)}, u32[]{:S(2)}, u32[]{:S(2)}) collective-permute-start(bf16[4,4,8,4096]{3,2,1,0:T(8,128)(2,1)} %bitcast.34), channel_id=1, source_target_pairs={{0,16},{1,17},{2,18},{3,19},{4,20},{5,21},{6,22},{7,23},{8,24},{9,... | collective-permute-start | bytes 3145736 | tf_op jit(solution)/shard_map/ppermute | solution.py:25
  163.1 23.8 %all-to-all-start.2 = ((bf16[8,8,4096]{2,1,0:T(8,128)(2,1)}), bf16[8,8,4096]{2,1,0:T(8,128)(2,1)}, u32[]{:S(2)}, u32[]{:S(2)}) async-start(bf16[8,8,4096]{2,1,0:T(8,128)(2,1)} %fusion.6), calls=%async_computation.2 | async-start | bytes 1048576 | tf_op jit(solution)/shard_map/all_to_all | solution.py:214
  169.9 103.2 %all-gather.7.cloned.1.call-start = ((), (), s32[]{:S(2)}) async-start(), calls=%async_computation.4 | async-start | bytes 4718592 | tf_op jit(solution)/shard_map/all_gather | solution.py:218
  237.5 15.9 %collective-permute-start.32 = (bf16[4,8,8192]{2,1,0:T(8,128)(2,1)S(1)}, bf16[4,8,8192]{2,1,0:T(8,128)(2,1)S(1)}, u32[]{:S(2)}, u32[]{:S(2)}) collective-permute-start(bf16[4,8,8192]{2,1,0:T(8,128)(2,1)S(1)} %get-tuple-element.39), channel_id=1, source_target_pairs={{0,128},{1,129},{2,130},{3,131},{4,132},{5,133},{6,134},{7,135},{8... | collective-permute-start | bytes 1572872 | tf_op jit(solution)/shard_map/ppermute | solution.py:25
  240.5 19.5 %collective-permute-start.34 = (bf16[4,8,8192]{2,1,0:T(8,128)(2,1)S(1)}, bf16[4,8,8192]{2,1,0:T(8,128)(2,1)S(1)}, u32[]{:S(2)}, u32[]{:S(2)}) collective-permute-start(bf16[4,8,8192]{2,1,0:T(8,128)(2,1)S(1)} %get-tuple-element.39), channel_id=1, source_target_pairs={{0,384},{1,385},{2,386},{3,387},{4,388},{5,389},{6,390},{7,391},{8... | collective-permute-start | bytes 1572872 | tf_op jit(solution)/shard_map/ppermute | solution.py:25
  244.2 26.9 %collective-permute-start.29 = (bf16[4,8,8192]{2,1,0:T(8,128)(2,1)S(1)}, bf16[4,8,8192]{2,1,0:T(8,128)(2,1)S(1)}, u32[]{:S(2)}, u32[]{:S(2)}) collective-permute-start(bf16[4,8,8192]{2,1,0:T(8,128)(2,1)S(1)} %get-tuple-element.39), channel_id=1, source_target_pairs={{0,256},{1,257},{2,258},{3,259},{4,260},{5,261},{6,262},{7,263},{8... | collective-permute-start | bytes 1572872 | tf_op jit(solution)/shard_map/ppermute | solution.py:25
  246.7 26.4 %collective-permute-start.31 = (bf16[4,8,8192]{2,1,0:T(8,128)(2,1)S(1)}, bf16[4,8,8192]{2,1,0:T(8,128)(2,1)S(1)}, u32[]{:S(2)}, u32[]{:S(2)}) collective-permute-start(bf16[4,8,8192]{2,1,0:T(8,128)(2,1)S(1)} %get-tuple-element.39), channel_id=1, source_target_pairs={{0,16},{1,17},{2,18},{3,19},{4,20},{5,21},{6,22},{7,23},{8,24},{9,... | collective-permute-start | bytes 1572872 | tf_op jit(solution)/shard_map/ppermute | solution.py:25
  253.4 24.2 %collective-permute-start.33 = (bf16[4,8,8192]{2,1,0:T(8,128)(2,1)S(1)}, bf16[4,8,8192]{2,1,0:T(8,128)(2,1)}, u32[]{:S(2)}, u32[]{:S(2)}) collective-permute-start(bf16[4,8,8192]{2,1,0:T(8,128)(2,1)S(1)} %collective-permute-done.32), channel_id=1, source_target_pairs={{0,16},{1,17},{2,18},{3,19},{4,20},{5,21},{6,22},{7,23},{8,24},{9,... | collective-permute-start | bytes 1572872 | tf_op jit(solution)/shard_map/ppermute | solution.py:25
  260.0 22.2 %collective-permute-start.35 = (bf16[4,8,8192]{2,1,0:T(8,128)(2,1)S(1)}, bf16[4,8,8192]{2,1,0:T(8,128)(2,1)}, u32[]{:S(2)}, u32[]{:S(2)}) collective-permute-start(bf16[4,8,8192]{2,1,0:T(8,128)(2,1)S(1)} %collective-permute-done.34), channel_id=1, source_target_pairs={{0,16},{1,17},{2,18},{3,19},{4,20},{5,21},{6,22},{7,23},{8,24},{9,... | collective-permute-start | bytes 1572872 | tf_op jit(solution)/shard_map/ppermute | solution.py:25
  271.1 15.8 %collective-permute-start.30 = (bf16[4,8,8192]{2,1,0:T(8,128)(2,1)S(1)}, bf16[4,8,8192]{2,1,0:T(8,128)(2,1)S(1)}, u32[]{:S(2)}, u32[]{:S(2)}) collective-permute-start(bf16[4,8,8192]{2,1,0:T(8,128)(2,1)S(1)} %collective-permute-done.29), channel_id=1, source_target_pairs={{0,16},{1,17},{2,18},{3,19},{4,20},{5,21},{6,22},{7,23},{8,24},{9,... | collective-permute-start | bytes 1572872 | tf_op jit(solution)/shard_map/ppermute | solution.py:25
  (21 other events, 166.8 us)
Sparse Core Ops, SparseCore 0:
  94.9 37.2 all-gather.4
  187.0 51.4 all-gather.6

commit v8 on v6

--- a/solution.py
+++ b/solution.py
@@ -28,13 +28,18 @@
     return swap(array, 2)
 
 
-def gather(block, masks):
-    return jnp.stack([block] + [swap(block, *mask) for mask in masks])
-
-
-def add(blocks, masks):
+def gather(block, masks, *later):
+    parts = [block] + [swap(block, *mask) for mask in masks]
+    if later:
+        parts[1], *later = lax.optimization_barrier((parts[1], *later))
+    return jnp.stack(parts), *later
+
+
+def add(blocks, masks, *later):
     parts = [blocks[0]] + [swap(blocks[k + 1], *mask) for k, mask in enumerate(masks)]
-    return sum(part.astype(jnp.float32) for part in parts)
+    if later:
+        parts[1], *later = lax.optimization_barrier((parts[1], *later))
+    return sum(part.astype(jnp.float32) for part in parts), *later
 
 
 def project_kernel(last, order_ref, inputs_ref, weight_ref, *refs):
@@ -142,7 +147,7 @@
     share = views * images // Y
     mine = lax.dynamic_slice_in_dim(flat, lax.rem(model_index, Y) * share, share, axis=0)
     pieces = mine.reshape(share, DP, rows).transpose(1, 0, 2)
-    weight_own = gather(gather(weight, ALONG_Z), ALONG_X)
+    weight_own = gather(gather(weight, ALONG_Z)[0], ALONG_X)[0]
     weight_other = swap(weight_own, 1)
     half = (DP // 2, rows, feat)
     projected = project(order[: DP // 2], flat, weight_own.reshape(half))
@@ -163,11 +168,9 @@
     first, pair = lax.optimization_barrier((first, pair))
     columns_b = lax.all_gather(pair, "mp", axis=0, axis_index_groups=GROUPS)
     columns_b = columns_b.reshape(MP * block, total)
-    along_z, pieces = lax.optimization_barrier((gather(first, STRIDED_Z), pieces))
+    rows_own, pieces = gather(gather(first, STRIDED_Z)[0], ALONG_X, pieces)
     slices = lax.all_to_all(pieces, "dp", split_axis=0, concat_axis=0)
-    rows_own, columns_b, slices = lax.optimization_barrier(
-        (gather(along_z, ALONG_X), columns_b, slices)
-    )
+    rows_own, columns_b = lax.optimization_barrier((rows_own, columns_b))
     rows_other = swap(rows_own, 1).reshape(feat // 2, total)
     rows_own = rows_own.reshape(feat // 2, total)
 
@@ -190,30 +193,36 @@
     def times(lhs, rhs, dims):
         return lax.dot_general(lhs, rhs, (dims, ((), ())), preferred_element_type=jnp.float32) / total
 
-    terms_b = (
-        times(corr_own, rows_own, ((0,), (0,))) + times(corr_other, rows_other, ((0,), (0,)))
-    ).astype(jnp.bfloat16)
-    corr_own, corr_other, terms_b = lax.optimization_barrier((corr_own, corr_other, terms_b))
+    half = (feat // 2, Y, 2, block)
+    sides = [
+        corr.reshape(half).transpose(2, 0, 1, 3).reshape(2, feat // 2, Y * block)
+        for corr in (corr_own, corr_other)
+    ]
+    terms_b = [
+        times(sides[0][k], rows_own, ((0,), (0,))) + times(sides[1][k], rows_other, ((0,), (0,)))
+        for k in (0, 1)
+    ]
+    away = terms_b[1].astype(jnp.bfloat16)
+    corr_own, corr_other, away = lax.optimization_barrier((corr_own, corr_other, away))
+    terms_b = (terms_b[0] + partner(away).astype(jnp.float32)).astype(jnp.bfloat16)
+    terms_b, slices = lax.optimization_barrier((terms_b, slices))
     terms_b = lax.all_to_all(
-        terms_b.reshape(Y, 2, block, total), "mp", split_axis=0, concat_axis=0, axis_index_groups=GROUPS
+        terms_b.reshape(Y, block, total), "mp", split_axis=0, concat_axis=0, axis_index_groups=GROUPS
     )
     terms_other = times(corr_other, columns_b, ((1,), (0,))).astype(jnp.bfloat16)
     terms_own = times(corr_own, columns_b, ((1,), (0,)))
     shape = (4, 4, block, total)
     both = terms_own.reshape(shape) + swap(terms_other.reshape(shape), 1).astype(jnp.float32)
-    along_x = add(both.astype(jnp.bfloat16), ALONG_X).astype(jnp.bfloat16)
-    along_x, terms_b, slices = lax.optimization_barrier((along_x, terms_b, slices))
+    along_x = add(both.astype(jnp.bfloat16), ALONG_X)[0].astype(jnp.bfloat16)
+    grad_a, terms_b, slices = add(along_x, STRIDED_Z, terms_b, slices)
     columns = lax.all_gather(slices, "mp", axis=0, axis_index_groups=GROUPS)
-    terms_b = jnp.sum(terms_b.astype(jnp.float32), axis=0)
-    grad_b = terms_b[0] + partner(terms_b[1].astype(jnp.bfloat16)).astype(jnp.float32)
-    grads = jnp.stack([add(along_x, STRIDED_Z), grad_b])
+    grads = jnp.stack([grad_a, jnp.sum(terms_b.astype(jnp.float32), axis=0)])
     wide = normed.astype(jnp.float32)
     grad_mean = jnp.sum(grads, axis=2, keepdims=True) / total
     cross_mean = jnp.sum(grads * wide, axis=2, keepdims=True) / total
     grad_proj = ((grads - grad_mean - wide * cross_mean) * inverse).astype(jnp.bfloat16)
     grad_proj = grad_proj.transpose(1, 0, 2).reshape(block, views * total)
-    grad_own = gather(gather(grad_proj, ALONG_Z), ALONG_X)
-    grad_own, columns = lax.optimization_barrier((grad_own, columns))
+    grad_own, columns = gather(gather(grad_proj, ALONG_Z)[0], ALONG_X, columns)
     grad_other = swap(grad_own, 1)
     part = weight_half(grad_own.reshape(feat // 2, views * total), columns)
     return weight_half(grad_other.reshape(feat // 2, views * total), columns, position, part)

time: 272 us -> 280 us (1.029)
  starting transfers between devices: 119 us -> 125 us
    ppermute x30, starting transfers between devices: 101 us -> 106 us  [swap(): lax.ppermute(array, ('dp', 'mp'), [(i, i ^ mask) for i in range(DP * MP)])]
    all_gather x1, waiting for transfers between devices: 0.02 us -> 4.21 us  [per_device(): columns = lax.all_gather(slices, 'mp', axis=0, axis_index_groups=GROUPS)]
    ppermute x30, waiting for transfers between devices: 89.6 us -> 86 us  [swap(): lax.ppermute(array, ('dp', 'mp'), [(i, i ^ mask) for i in range(DP * MP)])]
    all_to_all x1, starting transfers between devices: 4.18 us -> 7.72 us  [per_device(): slices = lax.all_to_all(pieces, 'dp', split_axis=0, concat_axis=0)]
  transfers between devices with their start and end apart: 35 -> 35, of which waited for: 17 -> 20; matrix products, arithmetic and copies ran while one was open for 3% -> 4% of each run, Pallas kernels for 1% -> 1%
where the time goes in v8:
time: 280 us; the launch traced here: 279 us
  starting transfers between devices  125 us (45%)
  waiting for transfers between devices  110 us (39%)
  between operations  14 us (5%)
  Pallas kernels  10.9 us (4%)
  local copies, waits for them, and re-layouts  7.05 us (3%)
  matrix products  6.88 us (2%)
  other arithmetic  5.05 us (2%)
    ppermute x30, starting transfers between devices, swap(): lax.ppermute(array, ('dp', 'mp'), [(i, i ^ mask) for i in range(DP * MP)])  106 us
    ppermute x30, waiting for transfers between devices, swap(): lax.ppermute(array, ('dp', 'mp'), [(i, i ^ mask) for i in range(DP * MP)])  86 us
    all_to_all x1, waiting for transfers between devices, per_device(): lax.all_to_all(terms_b.reshape(Y, block, total), 'mp', split_axis=0, conc...  10.7 us
    all_to_all x1, waiting for transfers between devices, per_device(): lax.all_to_all(projected.reshape(DP, block, views * images), 'dp', split_...  9.22 us
    all_to_all x1, starting transfers between devices, per_device(): slices = lax.all_to_all(pieces, 'dp', split_axis=0, concat_axis=0)  7.72 us
    all_to_all x1, starting transfers between devices, per_device(): lax.all_to_all(projected.reshape(DP, block, views * images), 'dp', split_...  6.7 us
    pallas_call x2, Pallas kernels, weight_half(): pl.pallas_call(functools.partial(weight_kernel, last), grid=(2, devices /...  6.53 us
  transfers between devices with their start and end apart: 35, of which 20 were waited for; matrix products, arithmetic and copies ran while one was open for 4% of the time, Pallas kernels for 1%

profile of v8, /device:TPU:1, one launch (start us, length us, event | category | flops | bytes accessed | tf_op | source)
XLA Modules:
  0.0 278.9 jit_solution(16613154493347222620)
XLA Ops:
  6.5 8.4 %collective-permute-start.2 = (bf16[256,256]{1,0:T(8,128)(2,1)}, bf16[256,256]{1,0:T(8,128)(2,1)S(1)}, u32[]{:S(2)}, u32[]{:S(2)}) collective-permute-start(bf16[256,256]{1,0:T(8,128)(2,1)} %param.3), channel_id=1, source_target_pairs={{0,96},{1,97},{2,98},{3,99},{4,100},{5,101},{6,102},{7,103},{8,104... | collective-permute-start | bytes 393224 | tf_op jit(solution)/shard_map/ppermute | solution.py:24
  19.1 6.7 %collective-permute-done.1 = bf16[256,256]{1,0:T(8,128)(2,1)S(1)} collective-permute-done((bf16[256,256]{1,0:T(8,128)(2,1)}, bf16[256,256]{1,0:T(8,128)(2,1)S(1)}, u32[]{:S(2)}, u32[]{:S(2)}) %collective-permute-start.1) | collective-permute-done | bytes 131104 | tf_op jit(solution)/shard_map/ppermute | solution.py:24
  26.9 4.8 %collective-permute-start.5 = (bf16[4,256,256]{2,1,0:T(8,128)(2,1)S(1)}, bf16[4,256,256]{2,1,0:T(8,128)(2,1)S(1)}, u32[]{:S(2)}, u32[]{:S(2)}) collective-permute-start(bf16[4,256,256]{2,1,0:T(8,128)(2,1)S(1)} %get-tuple-element.49), channel_id=1, source_target_pairs={{0,384},{1,385},{2,386},{3,387},{4,388},{5,389},{6,390},{7,391},{8... | collective-permute-start | bytes 1572872 | tf_op jit(solution)/shard_map/ppermute | solution.py:24
  36.1 17.0 %collective-permute-done.5 = bf16[4,256,256]{2,1,0:T(8,128)(2,1)S(1)} collective-permute-done((bf16[4,256,256]{2,1,0:T(8,128)(2,1)S(1)}, bf16[4,256,256]{2,1,0:T(8,128)(2,1)S(1)}, u32[]{:S(2)}, u32[]{:S(2)}) %collective-permute-start.5) | collective-permute-done | bytes 524320 | tf_op jit(solution)/shard_map/ppermute | solution.py:24
  55.7 4.8 %collective-permute-start.6 = (bf16[4,4,256,256]{3,2,1,0:T(8,128)(2,1)S(1)}, bf16[4,4,256,256]{3,2,1,0:T(8,128)(2,1)}, u32[]{:S(2)}, u32[]{:S(2)}) collective-permute-start(bf16[4,4,256,256]{3,2,1,0:T(8,128)(2,1)S(1)} %pad_maximum_fusion), channel_id=1, source_target_pairs={{0,16},{1,17},{2,18},{3,19},{4,20},{5,21},{6,22},{7,23},{8,24},{9,... | collective-permute-start | bytes 6291464 | tf_op jit(solution)/shard_map/ppermute | solution.py:24
  67.5 6.7 %all-to-all-start = ((f32[32,8,256]{2,1,0:T(8,128)}), f32[32,8,256]{2,1,0:T(8,128)S(1)}, u32[]{:S(2)}, u32[]{:S(2)}) async-start(f32[32,8,256]{2,1,0:T(8,128)} %bitcast.11), calls=%async_computation | async-start | bytes 524288 | tf_op jit(solution)/shard_map/all_to_all | solution.py:156
  76.3 9.2 %all-to-all-done = f32[32,8,256]{2,1,0:T(8,128)S(1)} async-done(((f32[32,8,256]{2,1,0:T(8,128)}), f32[32,8,256]{2,1,0:T(8,128)S(1)}, u32[]{:S(2)}, u32[]{:S(2)}) %all-to-all-start) | async-done | bytes 262176 | tf_op jit(solution)/shard_map/all_to_all | solution.py:156
  92.3 5.4 %collective-permute-start.10 = (bf16[8,4096]{1,0:T(8,128)(2,1)S(1)}, bf16[8,4096]{1,0:T(8,128)(2,1)S(1)}, u32[]{:S(2)}, u32[]{:S(2)}) collective-permute-start(bf16[8,4096]{1,0:T(8,128)(2,1)S(1)} %get-tuple-element.26), channel_id=1, source_target_pairs={{0,72},{1,73},{2,74},{3,75},{4,76},{5,77},{6,78},{7,79},{8,64},{9,... | collective-permute-start | bytes 196616 | tf_op jit(solution)/shard_map/ppermute | solution.py:24
  97.6 4.5 %collective-permute-start.9 = (bf16[8,4096]{1,0:T(8,128)(2,1)S(1)}, bf16[8,4096]{1,0:T(8,128)(2,1)S(1)}, u32[]{:S(2)}, u32[]{:S(2)}) collective-permute-start(bf16[8,4096]{1,0:T(8,128)(2,1)S(1)} %get-tuple-element.26), channel_id=1, source_target_pairs={{0,8},{1,9},{2,10},{3,11},{4,12},{5,13},{6,14},{7,15},{8,0},{9,1},... | collective-permute-start | bytes 196616 | tf_op jit(solution)/shard_map/ppermute | solution.py:24
  107.4 4.3 %collective-permute-done.8 = bf16[8,4096]{1,0:T(8,128)(2,1)S(1)} collective-permute-done((bf16[8,4096]{1,0:T(8,128)(2,1)S(1)}, bf16[8,4096]{1,0:T(8,128)(2,1)S(1)}, u32[]{:S(2)}, u32[]{:S(2)}) %collective-permute-start.8) | collective-permute-done | bytes 65568 | tf_op jit(solution)/shard_map/ppermute | solution.py:24
  121.3 8.7 %collective-permute-done.13 = bf16[4,8,4096]{2,1,0:T(8,128)(2,1)S(1)} collective-permute-done((bf16[4,8,4096]{2,1,0:T(8,128)(2,1)S(1)}, bf16[4,8,4096]{2,1,0:T(8,128)(2,1)S(1)}, u32[]{:S(2)}, u32[]{:S(2)}) %collective-permute-start.13) | collective-permute-done | bytes 262176 | tf_op jit(solution)/shard_map/ppermute | solution.py:24
  130.1 6.1 %collective-permute-start.14 = (bf16[4,4,8,4096]{3,2,1,0:T(8,128)(2,1)S(1)}, bf16[4,4,8,4096]{3,2,1,0:T(8,128)(2,1)S(1)}, u32[]{:S(2)}, u32[]{:S(2)}) collective-permute-start(bf16[4,4,8,4096]{3,2,1,0:T(8,128)(2,1)S(1)} %pad_maximum_fusion.2), channel_id=1, source_target_pairs={{0,16},{1,17},{2,18},{3,19},{4,20},{5,21},{6,22},{7,23},{8,24},{9,... | collective-permute-start | bytes 3145736 | tf_op jit(solution)/shard_map/ppermute | solution.py:24
  144.9 7.7 %all-to-all-start.1 = ((bf16[32,32,256]{2,1,0:T(8,128)(2,1)}), bf16[32,32,256]{2,1,0:T(8,128)(2,1)}, u32[]{:S(2)}, u32[]{:S(2)}) async-start(bf16[32,32,256]{2,1,0:T(8,128)(2,1)} %copy.15), calls=%async_computation.1 | async-start | bytes 1048576 | tf_op jit(solution)/shard_map/all_to_all | solution.py:172
  159.8 4.3 %collective-permute-start.18 = (bf16[4,8,4096]{2,1,0:T(8,128)(2,1)}, bf16[4,8,4096]{2,1,0:T(8,128)(2,1)S(1)}, u32[]{:S(2)}, u32[]{:S(2)}) collective-permute-start(bf16[4,8,4096]{2,1,0:T(8,128)(2,1)} %get-tuple-element.44), channel_id=1, source_target_pairs={{0,384},{1,385},{2,386},{3,387},{4,388},{5,389},{6,390},{7,391},{8... | collective-permute-start | bytes 786440 | tf_op jit(solution)/shard_map/ppermute | solution.py:24
  168.7 5.7 %collective-permute-done.20 = bf16[64,4096]{1,0:T(8,128)(2,1)S(1)} collective-permute-done((bf16[64,4096]{1,0:T(8,128)(2,1)S(1)}, bf16[64,4096]{1,0:T(8,128)(2,1)S(1)}, u32[]{:S(2)}, u32[]{:S(2)}) %collective-permute-start.20) | collective-permute-done | bytes 524320 | tf_op jit(solution)/shard_map/ppermute | solution.py:24
  175.6 4.2 %all-to-all-start.2 = ((bf16[8,8,4096]{2,1,0:T(8,128)(2,1)}), bf16[8,8,4096]{2,1,0:T(8,128)(2,1)S(1)}, u32[]{:S(2)}, u32[]{:S(2)}) async-start(bf16[8,8,4096]{2,1,0:T(8,128)(2,1)} %bitcast.51), calls=%async_computation.2 | async-start | bytes 1048576 | tf_op jit(solution)/shard_map/all_to_all | solution.py:209
  186.7 10.7 %all-to-all-done.2 = bf16[8,8,4096]{2,1,0:T(8,128)(2,1)S(1)} async-done(((bf16[8,8,4096]{2,1,0:T(8,128)(2,1)}), bf16[8,8,4096]{2,1,0:T(8,128)(2,1)S(1)}, u32[]{:S(2)}, u32[]{:S(2)}) %all-to-all-start.2) | async-done | bytes 524320 | tf_op jit(solution)/shard_map/all_to_all | solution.py:209
  197.4 5.1 %collective-permute-start.22 = (bf16[8,4096]{1,0:T(8,128)(2,1)S(1)}, bf16[8,4096]{1,0:T(8,128)(2,1)S(1)}, u32[]{:S(2)}, u32[]{:S(2)}) collective-permute-start(bf16[8,4096]{1,0:T(8,128)(2,1)S(1)} %get-tuple-element.53), channel_id=1, source_target_pairs={{0,72},{1,73},{2,74},{3,75},{4,76},{5,77},{6,78},{7,79},{8,64},{9,... | collective-permute-start | bytes 196616 | tf_op jit(solution)/shard_map/ppermute | solution.py:24
  206.7 5.4 %collective-permute-done.21 = bf16[8,4096]{1,0:T(8,128)(2,1)S(1)} collective-permute-done((bf16[8,4096]{1,0:T(8,128)(2,1)S(1)}, bf16[8,4096]{1,0:T(8,128)(2,1)S(1)}, u32[]{:S(2)}, u32[]{:S(2)}) %collective-permute-start.21) | collective-permute-done | bytes 65568 | tf_op jit(solution)/shard_map/ppermute | solution.py:24
  214.8 4.6 %collective-permute-start.24 = (bf16[8,8192]{1,0:T(8,128)(2,1)S(1)}, bf16[8,8192]{1,0:T(8,128)(2,1)S(1)}, u32[]{:S(2)}, u32[]{:S(2)}) collective-permute-start(bf16[8,8192]{1,0:T(8,128)(2,1)S(1)} %bitcast.172), channel_id=1, source_target_pairs={{0,64},{1,65},{2,66},{3,67},{4,68},{5,69},{6,70},{7,71},{8,72},{9,... | collective-permute-start | bytes 393224 | tf_op jit(solution)/shard_map/ppermute | solution.py:24
  221.9 7.7 %collective-permute-done.24 = bf16[8,8192]{1,0:T(8,128)(2,1)S(1)} collective-permute-done((bf16[8,8192]{1,0:T(8,128)(2,1)S(1)}, bf16[8,8192]{1,0:T(8,128)(2,1)S(1)}, u32[]{:S(2)}, u32[]{:S(2)}) %collective-permute-start.24) | collective-permute-done | bytes 131104 | tf_op jit(solution)/shard_map/ppermute | solution.py:24
  239.1 5.3 %collective-permute-done.26 = bf16[4,8,8192]{2,1,0:T(8,128)(2,1)S(1)} collective-permute-done((bf16[4,8,8192]{2,1,0:T(8,128)(2,1)S(1)}, bf16[4,8,8192]{2,1,0:T(8,128)(2,1)S(1)}, u32[]{:S(2)}, u32[]{:S(2)}) %collective-permute-start.26) | collective-permute-done | bytes 524320 | tf_op jit(solution)/shard_map/ppermute | solution.py:24
  244.4 4.2 %all-gather.7.cloned.1.call-done = bf16[256,32,256]{2,1,0:T(8,128)(2,1)} async-done(((bf16[32,32,256]{2,1,0:T(8,128)(2,1)}), bf16[256,32,256]{2,1,0:T(8,128)(2,1)}) %all-gather.7.cloned.1.call-update) | async-done | bytes 4194320 | tf_op jit(solution)/shard_map/all_gather | solution.py:218
  248.6 11.4 %collective-permute-done.28 = bf16[4,8,8192]{2,1,0:T(8,128)(2,1)S(1)} collective-permute-done((bf16[4,8,8192]{2,1,0:T(8,128)(2,1)S(1)}, bf16[4,8,8192]{2,1,0:T(8,128)(2,1)S(1)}, u32[]{:S(2)}, u32[]{:S(2)}) %collective-permute-start.28) | collective-permute-done | bytes 524320 | tf_op jit(solution)/shard_map/ppermute | solution.py:24
  (104 shorter events, 101.8 us)
Async XLA Ops:
  6.5 12.6 %collective-permute-start.2 = (bf16[256,256]{1,0:T(8,128)(2,1)}, bf16[256,256]{1,0:T(8,128)(2,1)S(1)}, u32[]{:S(2)}, u32[]{:S(2)}) collective-permute-start(bf16[256,256]{1,0:T(8,128)(2,1)} %param.3), channel_id=1, source_target_pairs={{0,96},{1,97},{2,98},{3,99},{4,100},{5,101},{6,102},{7,103},{8,104... | collective-permute-start | bytes 393224 | tf_op jit(solution)/shard_map/ppermute | solution.py:24
  15.0 10.9 %collective-permute-start.1 = (bf16[256,256]{1,0:T(8,128)(2,1)}, bf16[256,256]{1,0:T(8,128)(2,1)S(1)}, u32[]{:S(2)}, u32[]{:S(2)}) collective-permute-start(bf16[256,256]{1,0:T(8,128)(2,1)} %param.3), channel_id=1, source_target_pairs={{0,64},{1,65},{2,66},{3,67},{4,68},{5,69},{6,70},{7,71},{8,72},{9,... | collective-permute-start | bytes 393224 | tf_op jit(solution)/shard_map/ppermute | solution.py:24
  26.9 26.3 %collective-permute-start.5 = (bf16[4,256,256]{2,1,0:T(8,128)(2,1)S(1)}, bf16[4,256,256]{2,1,0:T(8,128)(2,1)S(1)}, u32[]{:S(2)}, u32[]{:S(2)}) collective-permute-start(bf16[4,256,256]{2,1,0:T(8,128)(2,1)S(1)} %get-tuple-element.49), channel_id=1, source_target_pairs={{0,384},{1,385},{2,386},{3,387},{4,388},{5,389},{6,390},{7,391},{8... | collective-permute-start | bytes 1572872 | tf_op jit(solution)/shard_map/ppermute | solution.py:24
  31.7 21.4 %collective-permute-start.4 = (bf16[4,256,256]{2,1,0:T(8,128)(2,1)S(1)}, bf16[4,256,256]{2,1,0:T(8,128)(2,1)S(1)}, u32[]{:S(2)}, u32[]{:S(2)}) collective-permute-start(bf16[4,256,256]{2,1,0:T(8,128)(2,1)S(1)} %get-tuple-element.49), channel_id=1, source_target_pairs={{0,256},{1,257},{2,258},{3,259},{4,260},{5,261},{6,262},{7,263},{8... | collective-permute-start | bytes 1572872 | tf_op jit(solution)/shard_map/ppermute | solution.py:24
  34.2 21.3 %collective-permute-start.3 = (bf16[4,256,256]{2,1,0:T(8,128)(2,1)S(1)}, bf16[4,256,256]{2,1,0:T(8,128)(2,1)S(1)}, u32[]{:S(2)}, u32[]{:S(2)}) collective-permute-start(bf16[4,256,256]{2,1,0:T(8,128)(2,1)S(1)} %get-tuple-element.49), channel_id=1, source_target_pairs={{0,128},{1,129},{2,130},{3,131},{4,132},{5,133},{6,134},{7,135},{8... | collective-permute-start | bytes 1572872 | tf_op jit(solution)/shard_map/ppermute | solution.py:24
  67.5 18.0 %all-to-all-start = ((f32[32,8,256]{2,1,0:T(8,128)}), f32[32,8,256]{2,1,0:T(8,128)S(1)}, u32[]{:S(2)}, u32[]{:S(2)}) async-start(f32[32,8,256]{2,1,0:T(8,128)} %bitcast.11), calls=%async_computation | async-start | bytes 524288 | tf_op jit(solution)/shard_map/all_to_all | solution.py:156
  74.2 55.9 %all-gather.5.cloned.1.call-start = ((), (), s32[]{:S(2)}) async-start(), calls=%async_computation.3 | async-start | bytes 1179648 | tf_op jit(solution)/shard_map/all_gather | solution.py:169
  92.3 12.1 %collective-permute-start.10 = (bf16[8,4096]{1,0:T(8,128)(2,1)S(1)}, bf16[8,4096]{1,0:T(8,128)(2,1)S(1)}, u32[]{:S(2)}, u32[]{:S(2)}) collective-permute-start(bf16[8,4096]{1,0:T(8,128)(2,1)S(1)} %get-tuple-element.26), channel_id=1, source_target_pairs={{0,72},{1,73},{2,74},{3,75},{4,76},{5,77},{6,78},{7,79},{8,64},{9,... | collective-permute-start | bytes 196616 | tf_op jit(solution)/shard_map/ppermute | solution.py:24
  97.6 9.8 %collective-permute-start.9 = (bf16[8,4096]{1,0:T(8,128)(2,1)S(1)}, bf16[8,4096]{1,0:T(8,128)(2,1)S(1)}, u32[]{:S(2)}, u32[]{:S(2)}) collective-permute-start(bf16[8,4096]{1,0:T(8,128)(2,1)S(1)} %get-tuple-element.26), channel_id=1, source_target_pairs={{0,8},{1,9},{2,10},{3,11},{4,12},{5,13},{6,14},{7,15},{8,0},{9,1},... | collective-permute-start | bytes 196616 | tf_op jit(solution)/shard_map/ppermute | solution.py:24
  114.1 15.9 %collective-permute-start.13 = (bf16[4,8,4096]{2,1,0:T(8,128)(2,1)S(1)}, bf16[4,8,4096]{2,1,0:T(8,128)(2,1)S(1)}, u32[]{:S(2)}, u32[]{:S(2)}) collective-permute-start(bf16[4,8,4096]{2,1,0:T(8,128)(2,1)S(1)} %get-tuple-element.56), channel_id=1, source_target_pairs={{0,384},{1,385},{2,386},{3,387},{4,388},{5,389},{6,390},{7,391},{8... | collective-permute-start | bytes 786440 | tf_op jit(solution)/shard_map/ppermute | solution.py:24
  116.6 13.4 %collective-permute-start.12 = (bf16[4,8,4096]{2,1,0:T(8,128)(2,1)S(1)}, bf16[4,8,4096]{2,1,0:T(8,128)(2,1)S(1)}, u32[]{:S(2)}, u32[]{:S(2)}) collective-permute-start(bf16[4,8,4096]{2,1,0:T(8,128)(2,1)S(1)} %get-tuple-element.56), channel_id=1, source_target_pairs={{0,256},{1,257},{2,258},{3,259},{4,260},{5,261},{6,262},{7,263},{8... | collective-permute-start | bytes 786440 | tf_op jit(solution)/shard_map/ppermute | solution.py:24
  141.5 15.9 %collective-permute-start.15 = (bf16[4,4,8,4096]{3,2,1,0:T(8,128)(2,1)}, bf16[4,4,8,4096]{3,2,1,0:T(8,128)(2,1)}, u32[]{:S(2)}, u32[]{:S(2)}) collective-permute-start(bf16[4,4,8,4096]{3,2,1,0:T(8,128)(2,1)} %bitcast.40), channel_id=1, source_target_pairs={{0,16},{1,17},{2,18},{3,19},{4,20},{5,21},{6,22},{7,23},{8,24},{9,... | collective-permute-start | bytes 3145736 | tf_op jit(solution)/shard_map/ppermute | solution.py:24
  144.9 30.7 %all-to-all-start.1 = ((bf16[32,32,256]{2,1,0:T(8,128)(2,1)}), bf16[32,32,256]{2,1,0:T(8,128)(2,1)}, u32[]{:S(2)}, u32[]{:S(2)}) async-start(bf16[32,32,256]{2,1,0:T(8,128)(2,1)} %copy.15), calls=%async_computation.1 | async-start | bytes 1048576 | tf_op jit(solution)/shard_map/all_to_all | solution.py:172
  153.7 20.8 %collective-permute-start.20 = (bf16[64,4096]{1,0:T(8,128)(2,1)S(1)}, bf16[64,4096]{1,0:T(8,128)(2,1)S(1)}, u32[]{:S(2)}, u32[]{:S(2)}) collective-permute-start(bf16[64,4096]{1,0:T(8,128)(2,1)S(1)} %copy-done.4), channel_id=1, source_target_pairs={{0,32},{1,33},{2,34},{3,35},{4,36},{5,37},{6,38},{7,39},{8,40},{9,... | collective-permute-start | bytes 1572872 | tf_op jit(solution)/shard_map/ppermute | solution.py:24
  159.8 20.1 %collective-permute-start.18 = (bf16[4,8,4096]{2,1,0:T(8,128)(2,1)}, bf16[4,8,4096]{2,1,0:T(8,128)(2,1)S(1)}, u32[]{:S(2)}, u32[]{:S(2)}) collective-permute-start(bf16[4,8,4096]{2,1,0:T(8,128)(2,1)} %get-tuple-element.44), channel_id=1, source_target_pairs={{0,384},{1,385},{2,386},{3,387},{4,388},{5,389},{6,390},{7,391},{8... | collective-permute-start | bytes 786440 | tf_op jit(solution)/shard_map/ppermute | solution.py:24
  164.1 15.8 %collective-permute-start.17 = (bf16[4,8,4096]{2,1,0:T(8,128)(2,1)}, bf16[4,8,4096]{2,1,0:T(8,128)(2,1)S(1)}, u32[]{:S(2)}, u32[]{:S(2)}) collective-permute-start(bf16[4,8,4096]{2,1,0:T(8,128)(2,1)} %get-tuple-element.45), channel_id=1, source_target_pairs={{0,256},{1,257},{2,258},{3,259},{4,260},{5,261},{6,262},{7,263},{8... | collective-permute-start | bytes 786440 | tf_op jit(solution)/shard_map/ppermute | solution.py:24
  166.5 13.3 %collective-permute-start.16 = (bf16[4,8,4096]{2,1,0:T(8,128)(2,1)S(1)}, bf16[4,8,4096]{2,1,0:T(8,128)(2,1)S(1)}, u32[]{:S(2)}, u32[]{:S(2)}) collective-permute-start(bf16[4,8,4096]{2,1,0:T(8,128)(2,1)S(1)} %get-tuple-element.43), channel_id=1, source_target_pairs={{0,128},{1,129},{2,130},{3,131},{4,132},{5,133},{6,134},{7,135},{8... | collective-permute-start | bytes 786440 | tf_op jit(solution)/shard_map/ppermute | solution.py:24
  175.6 21.7 %all-to-all-start.2 = ((bf16[8,8,4096]{2,1,0:T(8,128)(2,1)}), bf16[8,8,4096]{2,1,0:T(8,128)(2,1)S(1)}, u32[]{:S(2)}, u32[]{:S(2)}) async-start(bf16[8,8,4096]{2,1,0:T(8,128)(2,1)} %bitcast.51), calls=%async_computation.2 | async-start | bytes 1048576 | tf_op jit(solution)/shard_map/all_to_all | solution.py:209
  179.8 68.8 %all-gather.7.cloned.1.call-start = ((), (), s32[]{:S(2)}) async-start(), calls=%async_computation.4 | async-start | bytes 4718592 | tf_op jit(solution)/shard_map/all_gather | solution.py:218
  214.8 14.8 %collective-permute-start.24 = (bf16[8,8192]{1,0:T(8,128)(2,1)S(1)}, bf16[8,8192]{1,0:T(8,128)(2,1)S(1)}, u32[]{:S(2)}, u32[]{:S(2)}) collective-permute-start(bf16[8,8192]{1,0:T(8,128)(2,1)S(1)} %bitcast.172), channel_id=1, source_target_pairs={{0,64},{1,65},{2,66},{3,67},{4,68},{5,69},{6,70},{7,71},{8,72},{9,... | collective-permute-start | bytes 393224 | tf_op jit(solution)/shard_map/ppermute | solution.py:24
  219.4 10.2 %collective-permute-start.23 = (bf16[8,8192]{1,0:T(8,128)(2,1)S(1)}, bf16[8,8192]{1,0:T(8,128)(2,1)S(1)}, u32[]{:S(2)}, u32[]{:S(2)}) collective-permute-start(bf16[8,8192]{1,0:T(8,128)(2,1)S(1)} %bitcast.173), channel_id=1, source_target_pairs={{0,32},{1,33},{2,34},{3,35},{4,36},{5,37},{6,38},{7,39},{8,40},{9,... | collective-permute-start | bytes 393224 | tf_op jit(solution)/shard_map/ppermute | solution.py:24
  229.7 14.7 %collective-permute-start.26 = (bf16[4,8,8192]{2,1,0:T(8,128)(2,1)S(1)}, bf16[4,8,8192]{2,1,0:T(8,128)(2,1)S(1)}, u32[]{:S(2)}, u32[]{:S(2)}) collective-permute-start(bf16[4,8,8192]{2,1,0:T(8,128)(2,1)S(1)} %get-tuple-element.47), channel_id=1, source_target_pairs={{0,128},{1,129},{2,130},{3,131},{4,132},{5,133},{6,134},{7,135},{8... | collective-permute-start | bytes 1572872 | tf_op jit(solution)/shard_map/ppermute | solution.py:24
  233.2 26.8 %collective-permute-start.28 = (bf16[4,8,8192]{2,1,0:T(8,128)(2,1)S(1)}, bf16[4,8,8192]{2,1,0:T(8,128)(2,1)S(1)}, u32[]{:S(2)}, u32[]{:S(2)}) collective-permute-start(bf16[4,8,8192]{2,1,0:T(8,128)(2,1)S(1)} %get-tuple-element.47), channel_id=1, source_target_pairs={{0,384},{1,385},{2,386},{3,387},{4,388},{5,389},{6,390},{7,391},{8... | collective-permute-start | bytes 1572872 | tf_op jit(solution)/shard_map/ppermute | solution.py:24
  236.8 23.2 %collective-permute-start.27 = (bf16[4,8,8192]{2,1,0:T(8,128)(2,1)S(1)}, bf16[4,8,8192]{2,1,0:T(8,128)(2,1)S(1)}, u32[]{:S(2)}, u32[]{:S(2)}) collective-permute-start(bf16[4,8,8192]{2,1,0:T(8,128)(2,1)S(1)} %get-tuple-element.47), channel_id=1, source_target_pairs={{0,256},{1,257},{2,258},{3,259},{4,260},{5,261},{6,262},{7,263},{8... | collective-permute-start | bytes 1572872 | tf_op jit(solution)/shard_map/ppermute | solution.py:24
  (16 other events, 107.9 us)
Sparse Core Ops, SparseCore 0:
  92.4 37.2 all-gather.4
  197.5 51.1 all-gather.6

commit v9 on v8

--- a/solution.py
+++ b/solution.py
@@ -37,8 +37,7 @@
 
 def add(blocks, masks, *later):
     parts = [blocks[0]] + [swap(blocks[k + 1], *mask) for k, mask in enumerate(masks)]
-    if later:
-        parts[1], *later = lax.optimization_barrier((parts[1], *later))
+    *parts, later = lax.optimization_barrier((*parts, later))
     return sum(part.astype(jnp.float32) for part in parts), *later
 
 
@@ -168,9 +167,11 @@
     first, pair = lax.optimization_barrier((first, pair))
     columns_b = lax.all_gather(pair, "mp", axis=0, axis_index_groups=GROUPS)
     columns_b = columns_b.reshape(MP * block, total)
-    rows_own, pieces = gather(gather(first, STRIDED_Z)[0], ALONG_X, pieces)
+    along_z, pieces = lax.optimization_barrier((gather(first, STRIDED_Z)[0], pieces))
     slices = lax.all_to_all(pieces, "dp", split_axis=0, concat_axis=0)
-    rows_own, columns_b = lax.optimization_barrier((rows_own, columns_b))
+    rows_own, columns_b, slices = lax.optimization_barrier(
+        (gather(along_z, ALONG_X)[0], columns_b, slices)
+    )
     rows_other = swap(rows_own, 1).reshape(feat // 2, total)
     rows_own = rows_own.reshape(feat // 2, total)
 
@@ -205,7 +206,6 @@
     away = terms_b[1].astype(jnp.bfloat16)
     corr_own, corr_other, away = lax.optimization_barrier((corr_own, corr_other, away))
     terms_b = (terms_b[0] + partner(away).astype(jnp.float32)).astype(jnp.bfloat16)
-    terms_b, slices = lax.optimization_barrier((terms_b, slices))
     terms_b = lax.all_to_all(
         terms_b.reshape(Y, block, total), "mp", split_axis=0, concat_axis=0, axis_index_groups=GROUPS
     )

time: 280 us -> 265 us (0.946)
  starting transfers between devices: 125 us -> 118 us
  waiting for transfers between devices: 110 us -> 106 us
    all_gather x1, waiting for transfers between devices: 4.21 us -> 25.9 us  [per_device(): columns = lax.all_gather(slices, 'mp', axis=0, axis_index_groups=GROUPS)]
    ppermute x30, waiting for transfers between devices: 86 us -> 70.4 us  [swap(): lax.ppermute(array, ('dp', 'mp'), [(i, i ^ mask) for i in range(DP * MP)])]
    all_to_all x1, waiting for transfers between devices: 10.7 us -> 0.01 us  [per_device(): lax.all_to_all(terms_b.reshape(Y, block, total), 'mp', split_axis=0, conc...]
    ppermute x30, starting transfers between devices: 106 us -> 101 us  [swap(): lax.ppermute(array, ('dp', 'mp'), [(i, i ^ mask) for i in range(DP * MP)])]
    all_to_all x1, starting transfers between devices: 7.72 us -> 4.18 us  [per_device(): slices = lax.all_to_all(pieces, 'dp', split_axis=0, concat_axis=0)]
  transfers between devices with their start and end apart: 35 -> 35, of which waited for: 20 -> 18; matrix products, arithmetic and copies ran while one was open for 4% -> 3% of each run, Pallas kernels for 1% -> 1%
where the time goes in v9:
time: 265 us; the launch traced here: 264 us
  starting transfers between devices  118 us (45%)
  waiting for transfers between devices  106 us (40%)
  between operations  14 us (5%)
  Pallas kernels  10.9 us (4%)
  local copies, waits for them, and re-layouts  5.56 us (2%)
  matrix products  5.13 us (2%)
  other arithmetic  3.74 us (1%)
    ppermute x30, starting transfers between devices, swap(): lax.ppermute(array, ('dp', 'mp'), [(i, i ^ mask) for i in range(DP * MP)])  101 us
    ppermute x30, waiting for transfers between devices, swap(): lax.ppermute(array, ('dp', 'mp'), [(i, i ^ mask) for i in range(DP * MP)])  70.4 us
    all_gather x1, waiting for transfers between devices, per_device(): columns = lax.all_gather(slices, 'mp', axis=0, axis_index_groups=GROUPS)  25.9 us
    all_to_all x1, waiting for transfers between devices, per_device(): lax.all_to_all(projected.reshape(DP, block, views * images), 'dp', split_...  10 us
    all_to_all x1, starting transfers between devices, per_device(): lax.all_to_all(terms_b.reshape(Y, block, total), 'mp', split_axis=0, conc...  6.81 us
    all_to_all x1, starting transfers between devices, per_device(): lax.all_to_all(projected.reshape(DP, block, views * images), 'dp', split_...  6.7 us
    pallas_call x2, Pallas kernels, weight_half(): pl.pallas_call(functools.partial(weight_kernel, last), grid=(2, devices /...  6.53 us
  transfers between devices with their start and end apart: 35, of which 18 were waited for; matrix products, arithmetic and copies ran while one was open for 3% of the time, Pallas kernels for 1%

profile of v9, /device:TPU:1, one launch (start us, length us, event | category | flops | bytes accessed | tf_op | source)
XLA Modules:
  0.0 263.9 jit_solution(16253263460779539008)
XLA Ops:
  6.5 8.4 %collective-permute-start.2 = (bf16[256,256]{1,0:T(8,128)(2,1)}, bf16[256,256]{1,0:T(8,128)(2,1)S(1)}, u32[]{:S(2)}, u32[]{:S(2)}) collective-permute-start(bf16[256,256]{1,0:T(8,128)(2,1)} %param.3), channel_id=1, source_target_pairs={{0,96},{1,97},{2,98},{3,99},{4,100},{5,101},{6,102},{7,103},{8,104... | collective-permute-start | bytes 393224 | tf_op jit(solution)/shard_map/ppermute | solution.py:24
  19.1 6.7 %collective-permute-done.1 = bf16[256,256]{1,0:T(8,128)(2,1)S(1)} collective-permute-done((bf16[256,256]{1,0:T(8,128)(2,1)}, bf16[256,256]{1,0:T(8,128)(2,1)S(1)}, u32[]{:S(2)}, u32[]{:S(2)}) %collective-permute-start.1) | collective-permute-done | bytes 131104 | tf_op jit(solution)/shard_map/ppermute | solution.py:24
  26.9 4.8 %collective-permute-start.5 = (bf16[4,256,256]{2,1,0:T(8,128)(2,1)S(1)}, bf16[4,256,256]{2,1,0:T(8,128)(2,1)S(1)}, u32[]{:S(2)}, u32[]{:S(2)}) collective-permute-start(bf16[4,256,256]{2,1,0:T(8,128)(2,1)S(1)} %get-tuple-element.62), channel_id=1, source_target_pairs={{0,384},{1,385},{2,386},{3,387},{4,388},{5,389},{6,390},{7,391},{8... | collective-permute-start | bytes 1572872 | tf_op jit(solution)/shard_map/ppermute | solution.py:24
  36.1 17.0 %collective-permute-done.5 = bf16[4,256,256]{2,1,0:T(8,128)(2,1)S(1)} collective-permute-done((bf16[4,256,256]{2,1,0:T(8,128)(2,1)S(1)}, bf16[4,256,256]{2,1,0:T(8,128)(2,1)S(1)}, u32[]{:S(2)}, u32[]{:S(2)}) %collective-permute-start.5) | collective-permute-done | bytes 524320 | tf_op jit(solution)/shard_map/ppermute | solution.py:24
  55.7 4.8 %collective-permute-start.6 = (bf16[4,4,256,256]{3,2,1,0:T(8,128)(2,1)S(1)}, bf16[4,4,256,256]{3,2,1,0:T(8,128)(2,1)}, u32[]{:S(2)}, u32[]{:S(2)}) collective-permute-start(bf16[4,4,256,256]{3,2,1,0:T(8,128)(2,1)S(1)} %pad_maximum_fusion), channel_id=1, source_target_pairs={{0,16},{1,17},{2,18},{3,19},{4,20},{5,21},{6,22},{7,23},{8,24},{9,... | collective-permute-start | bytes 6291464 | tf_op jit(solution)/shard_map/ppermute | solution.py:24
  67.5 6.7 %all-to-all-start = ((f32[32,8,256]{2,1,0:T(8,128)}), f32[32,8,256]{2,1,0:T(8,128)S(1)}, u32[]{:S(2)}, u32[]{:S(2)}) async-start(f32[32,8,256]{2,1,0:T(8,128)} %bitcast.11), calls=%async_computation | async-start | bytes 524288 | tf_op jit(solution)/shard_map/all_to_all | solution.py:155
  75.5 10.0 %all-to-all-done = f32[32,8,256]{2,1,0:T(8,128)S(1)} async-done(((f32[32,8,256]{2,1,0:T(8,128)}), f32[32,8,256]{2,1,0:T(8,128)S(1)}, u32[]{:S(2)}, u32[]{:S(2)}) %all-to-all-start) | async-done | bytes 262176 | tf_op jit(solution)/shard_map/all_to_all | solution.py:155
  92.3 5.4 %collective-permute-start.10 = (bf16[8,4096]{1,0:T(8,128)(2,1)S(1)}, bf16[8,4096]{1,0:T(8,128)(2,1)S(1)}, u32[]{:S(2)}, u32[]{:S(2)}) collective-permute-start(bf16[8,4096]{1,0:T(8,128)(2,1)S(1)} %get-tuple-element.32), channel_id=1, source_target_pairs={{0,72},{1,73},{2,74},{3,75},{4,76},{5,77},{6,78},{7,79},{8,64},{9,... | collective-permute-start | bytes 196616 | tf_op jit(solution)/shard_map/ppermute | solution.py:24
  97.6 4.5 %collective-permute-start.9 = (bf16[8,4096]{1,0:T(8,128)(2,1)S(1)}, bf16[8,4096]{1,0:T(8,128)(2,1)S(1)}, u32[]{:S(2)}, u32[]{:S(2)}) collective-permute-start(bf16[8,4096]{1,0:T(8,128)(2,1)S(1)} %get-tuple-element.32), channel_id=1, source_target_pairs={{0,8},{1,9},{2,10},{3,11},{4,12},{5,13},{6,14},{7,15},{8,0},{9,1},... | collective-permute-start | bytes 196616 | tf_op jit(solution)/shard_map/ppermute | solution.py:24
  107.4 4.3 %collective-permute-done.8 = bf16[8,4096]{1,0:T(8,128)(2,1)S(1)} collective-permute-done((bf16[8,4096]{1,0:T(8,128)(2,1)S(1)}, bf16[8,4096]{1,0:T(8,128)(2,1)S(1)}, u32[]{:S(2)}, u32[]{:S(2)}) %collective-permute-start.8) | collective-permute-done | bytes 65568 | tf_op jit(solution)/shard_map/ppermute | solution.py:24
  112.9 4.2 %all-to-all-start.1 = ((bf16[32,32,256]{2,1,0:T(8,128)(2,1)}), bf16[32,32,256]{2,1,0:T(8,128)(2,1)S(1)}, u32[]{:S(2)}, u32[]{:S(2)}) async-start(bf16[32,32,256]{2,1,0:T(8,128)(2,1)} %copy.15), calls=%async_computation.1 | async-start | bytes 1048576 | tf_op jit(solution)/shard_map/all_to_all | solution.py:171
  117.0 4.5 %collective-permute-start.13 = (bf16[4,8,4096]{2,1,0:T(8,128)(2,1)S(1)}, bf16[4,8,4096]{2,1,0:T(8,128)(2,1)S(1)}, u32[]{:S(2)}, u32[]{:S(2)}) collective-permute-start(bf16[4,8,4096]{2,1,0:T(8,128)(2,1)S(1)} %pad_maximum_fusion.5), channel_id=1, source_target_pairs={{0,384},{1,385},{2,386},{3,387},{4,388},{5,389},{6,390},{7,391},{8... | collective-permute-start | bytes 786440 | tf_op jit(solution)/shard_map/ppermute | solution.py:24
  126.0 11.7 %collective-permute-done.13 = bf16[4,8,4096]{2,1,0:T(8,128)(2,1)S(1)} collective-permute-done((bf16[4,8,4096]{2,1,0:T(8,128)(2,1)S(1)}, bf16[4,8,4096]{2,1,0:T(8,128)(2,1)S(1)}, u32[]{:S(2)}, u32[]{:S(2)}) %collective-permute-start.13) | collective-permute-done | bytes 262176 | tf_op jit(solution)/shard_map/ppermute | solution.py:24
  154.1 4.5 %collective-permute-start.17 = (bf16[4,8,4096]{2,1,0:T(8,128)(2,1)}, bf16[4,8,4096]{2,1,0:T(8,128)(2,1)S(1)}, u32[]{:S(2)}, u32[]{:S(2)}) collective-permute-start(bf16[4,8,4096]{2,1,0:T(8,128)(2,1)} %get-tuple-element.56), channel_id=1, source_target_pairs={{0,256},{1,257},{2,258},{3,259},{4,260},{5,261},{6,262},{7,263},{8... | collective-permute-start | bytes 786440 | tf_op jit(solution)/shard_map/ppermute | solution.py:24
  163.6 6.8 %all-to-all-start.2 = ((bf16[8,8,4096]{2,1,0:T(8,128)(2,1)}), bf16[8,8,4096]{2,1,0:T(8,128)(2,1)S(1)}, u32[]{:S(2)}, u32[]{:S(2)}) async-start(bf16[8,8,4096]{2,1,0:T(8,128)(2,1)} %fusion.6), calls=%async_computation.2 | async-start | bytes 1048576 | tf_op jit(solution)/shard_map/all_to_all | solution.py:209
  170.5 4.4 %collective-permute-done.18 = bf16[4,8,4096]{2,1,0:T(8,128)(2,1)S(1)} collective-permute-done((bf16[4,8,4096]{2,1,0:T(8,128)(2,1)}, bf16[4,8,4096]{2,1,0:T(8,128)(2,1)S(1)}, u32[]{:S(2)}, u32[]{:S(2)}) %collective-permute-start.18) | collective-permute-done | bytes 262176 | tf_op jit(solution)/shard_map/ppermute | solution.py:24
  175.1 3.8 %collective-permute-start.19 = (bf16[8,4096]{1,0:T(8,128)(2,1)S(1)}, bf16[8,4096]{1,0:T(8,128)(2,1)S(1)}, u32[]{:S(2)}, u32[]{:S(2)}) collective-permute-start(bf16[8,4096]{1,0:T(8,128)(2,1)S(1)} %get-tuple-element.67), channel_id=1, source_target_pairs={{0,64},{1,65},{2,66},{3,67},{4,68},{5,69},{6,70},{7,71},{8,72},{9,... | collective-permute-start | bytes 196616 | tf_op jit(solution)/shard_map/ppermute | solution.py:24
  178.9 4.7 %collective-permute-start.20 = (bf16[8,4096]{1,0:T(8,128)(2,1)S(1)}, bf16[8,4096]{1,0:T(8,128)(2,1)S(1)}, u32[]{:S(2)}, u32[]{:S(2)}) collective-permute-start(bf16[8,4096]{1,0:T(8,128)(2,1)S(1)} %get-tuple-element.66), channel_id=1, source_target_pairs={{0,8},{1,9},{2,10},{3,11},{4,12},{5,13},{6,14},{7,15},{8,0},{9,1},... | collective-permute-start | bytes 196616 | tf_op jit(solution)/shard_map/ppermute | solution.py:24
  194.0 3.7 %collective-permute-start.24 = (bf16[8,8192]{1,0:T(8,128)(2,1)S(1)}, bf16[8,8192]{1,0:T(8,128)(2,1)S(1)}, u32[]{:S(2)}, u32[]{:S(2)}) collective-permute-start(bf16[8,8192]{1,0:T(8,128)(2,1)S(1)} %bitcast.164), channel_id=1, source_target_pairs={{0,64},{1,65},{2,66},{3,67},{4,68},{5,69},{6,70},{7,71},{8,72},{9,... | collective-permute-start | bytes 393224 | tf_op jit(solution)/shard_map/ppermute | solution.py:24
  200.7 6.5 %collective-permute-done.24 = bf16[8,8192]{1,0:T(8,128)(2,1)S(1)} collective-permute-done((bf16[8,8192]{1,0:T(8,128)(2,1)S(1)}, bf16[8,8192]{1,0:T(8,128)(2,1)S(1)}, u32[]{:S(2)}, u32[]{:S(2)}) %collective-permute-start.24) | collective-permute-done | bytes 131104 | tf_op jit(solution)/shard_map/ppermute | solution.py:24
  211.7 4.5 %collective-permute-start.27 = (bf16[4,8,8192]{2,1,0:T(8,128)(2,1)S(1)}, bf16[4,8,8192]{2,1,0:T(8,128)(2,1)S(1)}, u32[]{:S(2)}, u32[]{:S(2)}) collective-permute-start(bf16[4,8,8192]{2,1,0:T(8,128)(2,1)S(1)} %get-tuple-element.60), channel_id=1, source_target_pairs={{0,256},{1,257},{2,258},{3,259},{4,260},{5,261},{6,262},{7,263},{8... | collective-permute-start | bytes 1572872 | tf_op jit(solution)/shard_map/ppermute | solution.py:24
  216.2 4.1 %collective-permute-done.26 = bf16[4,8,8192]{2,1,0:T(8,128)(2,1)S(1)} collective-permute-done((bf16[4,8,8192]{2,1,0:T(8,128)(2,1)S(1)}, bf16[4,8,8192]{2,1,0:T(8,128)(2,1)S(1)}, u32[]{:S(2)}, u32[]{:S(2)}) %collective-permute-start.26) | collective-permute-done | bytes 524320 | tf_op jit(solution)/shard_map/ppermute | solution.py:24
  220.4 25.9 %all-gather.7.cloned.1.call-done = bf16[256,32,256]{2,1,0:T(8,128)(2,1)} async-done(((bf16[32,32,256]{2,1,0:T(8,128)(2,1)}), bf16[256,32,256]{2,1,0:T(8,128)(2,1)}) %all-gather.7.cloned.1.call-update) | async-done | bytes 4194320 | tf_op jit(solution)/shard_map/all_gather | solution.py:218
  253.1 4.0 %shard_map.31 = f32[256,256]{1,0:T(8,128)} custom-call(bf16[128,8192]{1,0:T(8,128)(2,1)S(1)} %bitcast.144, bf16[8,32,32,256]{3,2,1,0:T(8,128)(2,1)S(1)} %bitcast.141, s32[32]{0:T(128)S(1)} %and_or_fusion.refs_0_, f32[128,256]{1,0:T(8,128)S(1)} %shard_map.30.refs_1_), custom_call_target="tpu_custom_call" | custom-call | flops 536870912 | bytes 6291456 | tf_op jit(solution)/shard_map/pallas_call | solution.py:116
  (102 shorter events, 83.8 us)
Async XLA Ops:
  6.5 12.6 %collective-permute-start.2 = (bf16[256,256]{1,0:T(8,128)(2,1)}, bf16[256,256]{1,0:T(8,128)(2,1)S(1)}, u32[]{:S(2)}, u32[]{:S(2)}) collective-permute-start(bf16[256,256]{1,0:T(8,128)(2,1)} %param.3), channel_id=1, source_target_pairs={{0,96},{1,97},{2,98},{3,99},{4,100},{5,101},{6,102},{7,103},{8,104... | collective-permute-start | bytes 393224 | tf_op jit(solution)/shard_map/ppermute | solution.py:24
  15.0 10.9 %collective-permute-start.1 = (bf16[256,256]{1,0:T(8,128)(2,1)}, bf16[256,256]{1,0:T(8,128)(2,1)S(1)}, u32[]{:S(2)}, u32[]{:S(2)}) collective-permute-start(bf16[256,256]{1,0:T(8,128)(2,1)} %param.3), channel_id=1, source_target_pairs={{0,64},{1,65},{2,66},{3,67},{4,68},{5,69},{6,70},{7,71},{8,72},{9,... | collective-permute-start | bytes 393224 | tf_op jit(solution)/shard_map/ppermute | solution.py:24
  26.9 26.3 %collective-permute-start.5 = (bf16[4,256,256]{2,1,0:T(8,128)(2,1)S(1)}, bf16[4,256,256]{2,1,0:T(8,128)(2,1)S(1)}, u32[]{:S(2)}, u32[]{:S(2)}) collective-permute-start(bf16[4,256,256]{2,1,0:T(8,128)(2,1)S(1)} %get-tuple-element.62), channel_id=1, source_target_pairs={{0,384},{1,385},{2,386},{3,387},{4,388},{5,389},{6,390},{7,391},{8... | collective-permute-start | bytes 1572872 | tf_op jit(solution)/shard_map/ppermute | solution.py:24
  31.7 21.4 %collective-permute-start.4 = (bf16[4,256,256]{2,1,0:T(8,128)(2,1)S(1)}, bf16[4,256,256]{2,1,0:T(8,128)(2,1)S(1)}, u32[]{:S(2)}, u32[]{:S(2)}) collective-permute-start(bf16[4,256,256]{2,1,0:T(8,128)(2,1)S(1)} %get-tuple-element.62), channel_id=1, source_target_pairs={{0,256},{1,257},{2,258},{3,259},{4,260},{5,261},{6,262},{7,263},{8... | collective-permute-start | bytes 1572872 | tf_op jit(solution)/shard_map/ppermute | solution.py:24
  34.2 21.3 %collective-permute-start.3 = (bf16[4,256,256]{2,1,0:T(8,128)(2,1)S(1)}, bf16[4,256,256]{2,1,0:T(8,128)(2,1)S(1)}, u32[]{:S(2)}, u32[]{:S(2)}) collective-permute-start(bf16[4,256,256]{2,1,0:T(8,128)(2,1)S(1)} %get-tuple-element.62), channel_id=1, source_target_pairs={{0,128},{1,129},{2,130},{3,131},{4,132},{5,133},{6,134},{7,135},{8... | collective-permute-start | bytes 1572872 | tf_op jit(solution)/shard_map/ppermute | solution.py:24
  67.5 18.0 %all-to-all-start = ((f32[32,8,256]{2,1,0:T(8,128)}), f32[32,8,256]{2,1,0:T(8,128)S(1)}, u32[]{:S(2)}, u32[]{:S(2)}) async-start(f32[32,8,256]{2,1,0:T(8,128)} %bitcast.11), calls=%async_computation | async-start | bytes 524288 | tf_op jit(solution)/shard_map/all_to_all | solution.py:155
  74.2 63.7 %all-gather.5.cloned.1.call-start = ((), (), s32[]{:S(2)}) async-start(), calls=%async_computation.3 | async-start | bytes 1179648 | tf_op jit(solution)/shard_map/all_gather | solution.py:168
  92.3 12.1 %collective-permute-start.10 = (bf16[8,4096]{1,0:T(8,128)(2,1)S(1)}, bf16[8,4096]{1,0:T(8,128)(2,1)S(1)}, u32[]{:S(2)}, u32[]{:S(2)}) collective-permute-start(bf16[8,4096]{1,0:T(8,128)(2,1)S(1)} %get-tuple-element.32), channel_id=1, source_target_pairs={{0,72},{1,73},{2,74},{3,75},{4,76},{5,77},{6,78},{7,79},{8,64},{9,... | collective-permute-start | bytes 196616 | tf_op jit(solution)/shard_map/ppermute | solution.py:24
  97.6 9.8 %collective-permute-start.9 = (bf16[8,4096]{1,0:T(8,128)(2,1)S(1)}, bf16[8,4096]{1,0:T(8,128)(2,1)S(1)}, u32[]{:S(2)}, u32[]{:S(2)}) collective-permute-start(bf16[8,4096]{1,0:T(8,128)(2,1)S(1)} %get-tuple-element.32), channel_id=1, source_target_pairs={{0,8},{1,9},{2,10},{3,11},{4,12},{5,13},{6,14},{7,15},{8,0},{9,1},... | collective-permute-start | bytes 196616 | tf_op jit(solution)/shard_map/ppermute | solution.py:24
  112.9 25.0 %all-to-all-start.1 = ((bf16[32,32,256]{2,1,0:T(8,128)(2,1)}), bf16[32,32,256]{2,1,0:T(8,128)(2,1)S(1)}, u32[]{:S(2)}, u32[]{:S(2)}) async-start(bf16[32,32,256]{2,1,0:T(8,128)(2,1)} %copy.15), calls=%async_computation.1 | async-start | bytes 1048576 | tf_op jit(solution)/shard_map/all_to_all | solution.py:171
  117.0 20.7 %collective-permute-start.13 = (bf16[4,8,4096]{2,1,0:T(8,128)(2,1)S(1)}, bf16[4,8,4096]{2,1,0:T(8,128)(2,1)S(1)}, u32[]{:S(2)}, u32[]{:S(2)}) collective-permute-start(bf16[4,8,4096]{2,1,0:T(8,128)(2,1)S(1)} %pad_maximum_fusion.5), channel_id=1, source_target_pairs={{0,384},{1,385},{2,386},{3,387},{4,388},{5,389},{6,390},{7,391},{8... | collective-permute-start | bytes 786440 | tf_op jit(solution)/shard_map/ppermute | solution.py:24
  121.6 16.2 %collective-permute-start.12 = (bf16[4,8,4096]{2,1,0:T(8,128)(2,1)S(1)}, bf16[4,8,4096]{2,1,0:T(8,128)(2,1)S(1)}, u32[]{:S(2)}, u32[]{:S(2)}) collective-permute-start(bf16[4,8,4096]{2,1,0:T(8,128)(2,1)S(1)} %pad_maximum_fusion.5), channel_id=1, source_target_pairs={{0,256},{1,257},{2,258},{3,259},{4,260},{5,261},{6,262},{7,263},{8... | collective-permute-start | bytes 786440 | tf_op jit(solution)/shard_map/ppermute | solution.py:24
  124.0 13.7 %collective-permute-start.11 = (bf16[4,8,4096]{2,1,0:T(8,128)(2,1)S(1)}, bf16[4,8,4096]{2,1,0:T(8,128)(2,1)S(1)}, u32[]{:S(2)}, u32[]{:S(2)}) collective-permute-start(bf16[4,8,4096]{2,1,0:T(8,128)(2,1)S(1)} %pad_maximum_fusion.5), channel_id=1, source_target_pairs={{0,128},{1,129},{2,130},{3,131},{4,132},{5,133},{6,134},{7,135},{8... | collective-permute-start | bytes 786440 | tf_op jit(solution)/shard_map/ppermute | solution.py:24
  146.8 15.7 %collective-permute-start.22 = (bf16[64,4096]{1,0:T(8,128)(2,1)S(1)}, bf16[64,4096]{1,0:T(8,128)(2,1)S(1)}, u32[]{:S(2)}, u32[]{:S(2)}) collective-permute-start(bf16[64,4096]{1,0:T(8,128)(2,1)S(1)} %fusion.5), channel_id=1, source_target_pairs={{0,32},{1,33},{2,34},{3,35},{4,36},{5,37},{6,38},{7,39},{8,40},{9,... | collective-permute-start | bytes 1572872 | tf_op jit(solution)/shard_map/ppermute | solution.py:24
  151.9 18.5 %collective-permute-start.16 = (bf16[4,8,4096]{2,1,0:T(8,128)(2,1)}, bf16[4,8,4096]{2,1,0:T(8,128)(2,1)S(1)}, u32[]{:S(2)}, u32[]{:S(2)}) collective-permute-start(bf16[4,8,4096]{2,1,0:T(8,128)(2,1)} %get-tuple-element.57), channel_id=1, source_target_pairs={{0,128},{1,129},{2,130},{3,131},{4,132},{5,133},{6,134},{7,135},{8... | collective-permute-start | bytes 786440 | tf_op jit(solution)/shard_map/ppermute | solution.py:24
  154.1 16.4 %collective-permute-start.17 = (bf16[4,8,4096]{2,1,0:T(8,128)(2,1)}, bf16[4,8,4096]{2,1,0:T(8,128)(2,1)S(1)}, u32[]{:S(2)}, u32[]{:S(2)}) collective-permute-start(bf16[4,8,4096]{2,1,0:T(8,128)(2,1)} %get-tuple-element.56), channel_id=1, source_target_pairs={{0,256},{1,257},{2,258},{3,259},{4,260},{5,261},{6,262},{7,263},{8... | collective-permute-start | bytes 786440 | tf_op jit(solution)/shard_map/ppermute | solution.py:24
  158.6 16.3 %collective-permute-start.18 = (bf16[4,8,4096]{2,1,0:T(8,128)(2,1)}, bf16[4,8,4096]{2,1,0:T(8,128)(2,1)S(1)}, u32[]{:S(2)}, u32[]{:S(2)}) collective-permute-start(bf16[4,8,4096]{2,1,0:T(8,128)(2,1)} %get-tuple-element.55), channel_id=1, source_target_pairs={{0,384},{1,385},{2,386},{3,387},{4,388},{5,389},{6,390},{7,391},{8... | collective-permute-start | bytes 786440 | tf_op jit(solution)/shard_map/ppermute | solution.py:24
  163.6 27.2 %all-to-all-start.2 = ((bf16[8,8,4096]{2,1,0:T(8,128)(2,1)}), bf16[8,8,4096]{2,1,0:T(8,128)(2,1)S(1)}, u32[]{:S(2)}, u32[]{:S(2)}) async-start(bf16[8,8,4096]{2,1,0:T(8,128)(2,1)} %fusion.6), calls=%async_computation.2 | async-start | bytes 1048576 | tf_op jit(solution)/shard_map/all_to_all | solution.py:209
  170.4 75.8 %all-gather.7.cloned.1.call-start = ((), (), s32[]{:S(2)}) async-start(), calls=%async_computation.4 | async-start | bytes 4718592 | tf_op jit(solution)/shard_map/all_gather | solution.py:218
  175.1 11.4 %collective-permute-start.19 = (bf16[8,4096]{1,0:T(8,128)(2,1)S(1)}, bf16[8,4096]{1,0:T(8,128)(2,1)S(1)}, u32[]{:S(2)}, u32[]{:S(2)}) collective-permute-start(bf16[8,4096]{1,0:T(8,128)(2,1)S(1)} %get-tuple-element.67), channel_id=1, source_target_pairs={{0,64},{1,65},{2,66},{3,67},{4,68},{5,69},{6,70},{7,71},{8,72},{9,... | collective-permute-start | bytes 196616 | tf_op jit(solution)/shard_map/ppermute | solution.py:24
  194.0 13.1 %collective-permute-start.24 = (bf16[8,8192]{1,0:T(8,128)(2,1)S(1)}, bf16[8,8192]{1,0:T(8,128)(2,1)S(1)}, u32[]{:S(2)}, u32[]{:S(2)}) collective-permute-start(bf16[8,8192]{1,0:T(8,128)(2,1)S(1)} %bitcast.164), channel_id=1, source_target_pairs={{0,64},{1,65},{2,66},{3,67},{4,68},{5,69},{6,70},{7,71},{8,72},{9,... | collective-permute-start | bytes 393224 | tf_op jit(solution)/shard_map/ppermute | solution.py:24
  207.2 13.1 %collective-permute-start.26 = (bf16[4,8,8192]{2,1,0:T(8,128)(2,1)S(1)}, bf16[4,8,8192]{2,1,0:T(8,128)(2,1)S(1)}, u32[]{:S(2)}, u32[]{:S(2)}) collective-permute-start(bf16[4,8,8192]{2,1,0:T(8,128)(2,1)S(1)} %get-tuple-element.60), channel_id=1, source_target_pairs={{0,128},{1,129},{2,130},{3,131},{4,132},{5,133},{6,134},{7,135},{8... | collective-permute-start | bytes 1572872 | tf_op jit(solution)/shard_map/ppermute | solution.py:24
  209.2 37.1 %collective-permute-start.28 = (bf16[4,8,8192]{2,1,0:T(8,128)(2,1)S(1)}, bf16[4,8,8192]{2,1,0:T(8,128)(2,1)S(1)}, u32[]{:S(2)}, u32[]{:S(2)}) collective-permute-start(bf16[4,8,8192]{2,1,0:T(8,128)(2,1)S(1)} %get-tuple-element.60), channel_id=1, source_target_pairs={{0,384},{1,385},{2,386},{3,387},{4,388},{5,389},{6,390},{7,391},{8... | collective-permute-start | bytes 1572872 | tf_op jit(solution)/shard_map/ppermute | solution.py:24
  211.7 34.5 %collective-permute-start.27 = (bf16[4,8,8192]{2,1,0:T(8,128)(2,1)S(1)}, bf16[4,8,8192]{2,1,0:T(8,128)(2,1)S(1)}, u32[]{:S(2)}, u32[]{:S(2)}) collective-permute-start(bf16[4,8,8192]{2,1,0:T(8,128)(2,1)S(1)} %get-tuple-element.60), channel_id=1, source_target_pairs={{0,256},{1,257},{2,258},{3,259},{4,260},{5,261},{6,262},{7,263},{8... | collective-permute-start | bytes 1572872 | tf_op jit(solution)/shard_map/ppermute | solution.py:24
  (15 other events, 98.9 us)
Sparse Core Ops, SparseCore 0:
  92.4 37.2 all-gather.4
  190.9 55.2 all-gather.6

commit v10 on v9

--- a/solution.py
+++ b/solution.py
@@ -37,7 +37,7 @@
 
 def add(blocks, masks, *later):
     parts = [blocks[0]] + [swap(blocks[k + 1], *mask) for k, mask in enumerate(masks)]
-    *parts, later = lax.optimization_barrier((*parts, later))
+    parts, later = lax.optimization_barrier((parts, later))
     return sum(part.astype(jnp.float32) for part in parts), *later
 
 
@@ -146,10 +146,12 @@
     share = views * images // Y
     mine = lax.dynamic_slice_in_dim(flat, lax.rem(model_index, Y) * share, share, axis=0)
     pieces = mine.reshape(share, DP, rows).transpose(1, 0, 2)
-    weight_own = gather(gather(weight, ALONG_Z)[0], ALONG_X)[0]
+    weight_own, pieces = gather(gather(weight, ALONG_Z)[0], ALONG_X, pieces)
+    slices = lax.all_to_all(pieces, "dp", split_axis=0, concat_axis=0)
     weight_other = swap(weight_own, 1)
     half = (DP // 2, rows, feat)
     projected = project(order[: DP // 2], flat, weight_own.reshape(half))
+    projected, slices = lax.optimization_barrier((projected, slices))
     projected = project(order[DP // 2 :], flat, weight_other.reshape(half), projected)
 
     own = lax.all_to_all(
@@ -162,16 +164,14 @@
     normed = (centered * inverse).astype(jnp.bfloat16).transpose(2, 1, 0, 3).reshape(views, block, total)
     inverse = inverse.reshape(block, views).T[:, :, None]
 
-    first, second, pieces = lax.optimization_barrier((normed[0], normed[1], pieces))
+    second = normed[1]
     pair = jnp.stack([second, partner(second)])
-    first, pair = lax.optimization_barrier((first, pair))
+    first, pair = lax.optimization_barrier((normed[0], pair))
     columns_b = lax.all_gather(pair, "mp", axis=0, axis_index_groups=GROUPS)
     columns_b = columns_b.reshape(MP * block, total)
-    along_z, pieces = lax.optimization_barrier((gather(first, STRIDED_Z)[0], pieces))
-    slices = lax.all_to_all(pieces, "dp", split_axis=0, concat_axis=0)
-    rows_own, columns_b, slices = lax.optimization_barrier(
-        (gather(along_z, ALONG_X)[0], columns_b, slices)
-    )
+    rows_own = gather(gather(first, STRIDED_Z)[0], ALONG_X)[0]
+    rows_own, columns_b, slices = lax.optimization_barrier((rows_own, columns_b, slices))
+    columns = lax.all_gather(slices, "mp", axis=0, axis_index_groups=GROUPS)
     rows_other = swap(rows_own, 1).reshape(feat // 2, total)
     rows_own = rows_own.reshape(feat // 2, total)
 
@@ -214,15 +214,15 @@
     shape = (4, 4, block, total)
     both = terms_own.reshape(shape) + swap(terms_other.reshape(shape), 1).astype(jnp.float32)
     along_x = add(both.astype(jnp.bfloat16), ALONG_X)[0].astype(jnp.bfloat16)
-    grad_a, terms_b, slices = add(along_x, STRIDED_Z, terms_b, slices)
-    columns = lax.all_gather(slices, "mp", axis=0, axis_index_groups=GROUPS)
+    grad_a, terms_b = add(along_x, STRIDED_Z, terms_b)
     grads = jnp.stack([grad_a, jnp.sum(terms_b.astype(jnp.float32), axis=0)])
     wide = normed.astype(jnp.float32)
     grad_mean = jnp.sum(grads, axis=2, keepdims=True) / total
     cross_mean = jnp.sum(grads * wide, axis=2, keepdims=True) / total
     grad_proj = ((grads - grad_mean - wide * cross_mean) * inverse).astype(jnp.bfloat16)
     grad_proj = grad_proj.transpose(1, 0, 2).reshape(block, views * total)
-    grad_own, columns = gather(gather(grad_proj, ALONG_Z)[0], ALONG_X, columns)
+    along_z, columns = gather(grad_proj, ALONG_Z, columns)
+    grad_own = gather(along_z, ALONG_X)[0]
     grad_other = swap(grad_own, 1)
     part = weight_half(grad_own.reshape(feat // 2, views * total), columns)
     return weight_half(grad_other.reshape(feat // 2, views * total), columns, position, part)

time: 265 us -> 276 us (1.042)
  blocking collectives: 0 us -> 14.8 us
  starting transfers between devices: 118 us -> 115 us
    all_gather x1, waiting for transfers between devices: 25.9 us -> 6.3 us  [per_device(): columns = lax.all_gather(slices, 'mp', axis=0, axis_index_groups=GROUPS)]
    all_to_all x0 -> x1, blocking collectives: none -> 14.8 us  [per_device(): lax.all_to_all(projected.reshape(DP, block, views * images), 'dp', split_...]
    ppermute x30, waiting for transfers between devices: 70.4 us -> 85 us  [swap(): lax.ppermute(array, ('dp', 'mp'), [(i, i ^ mask) for i in range(DP * MP)])]
    all_to_all x1, waiting for transfers between devices: 0.01 us -> 13.2 us  [per_device(): slices = lax.all_to_all(pieces, 'dp', split_axis=0, concat_axis=0)]
    all_to_all x1 -> x0, waiting for transfers between devices: 10 us -> none  [per_device(): lax.all_to_all(projected.reshape(DP, block, views * images), 'dp', split_...]
    all_to_all x1 -> x0, starting transfers between devices: 6.7 us -> none  [per_device(): lax.all_to_all(projected.reshape(DP, block, views * images), 'dp', split_...]
    ppermute x30, starting transfers between devices: 101 us -> 104 us  [swap(): lax.ppermute(array, ('dp', 'mp'), [(i, i ^ mask) for i in range(DP * MP)])]
  transfers between devices with their start and end apart: 35 -> 34, of which waited for: 18 -> 19; matrix products, arithmetic and copies ran while one was open for 3% -> 3% of each run, Pallas kernels for 1% -> 1%
where the time goes in v10:
time: 276 us; the launch traced here: 275 us
  starting transfers between devices  115 us (42%)
  waiting for transfers between devices  105 us (38%)
  blocking collectives  14.8 us (5%)
  between operations  13.9 us (5%)
  Pallas kernels  10.2 us (4%)
  local copies, waits for them, and re-layouts  7.98 us (3%)
  matrix products  5.15 us (2%)
  other arithmetic  3.75 us (1%)
    ppermute x30, starting transfers between devices, swap(): lax.ppermute(array, ('dp', 'mp'), [(i, i ^ mask) for i in range(DP * MP)])  104 us
    ppermute x30, waiting for transfers between devices, swap(): lax.ppermute(array, ('dp', 'mp'), [(i, i ^ mask) for i in range(DP * MP)])  85 us
    all_to_all x1, blocking collectives, per_device(): lax.all_to_all(projected.reshape(DP, block, views * images), 'dp', split_...  14.8 us
    all_to_all x1, waiting for transfers between devices, per_device(): slices = lax.all_to_all(pieces, 'dp', split_axis=0, concat_axis=0)  13.2 us
    pallas_call x2, Pallas kernels, weight_half(): pl.pallas_call(functools.partial(weight_kernel, last), grid=(2, devices /...  6.53 us
    all_to_all x1, starting transfers between devices, per_device(): slices = lax.all_to_all(pieces, 'dp', split_axis=0, concat_axis=0)  6.44 us
    all_gather x1, waiting for transfers between devices, per_device(): columns = lax.all_gather(slices, 'mp', axis=0, axis_index_groups=GROUPS)  6.3 us
  transfers between devices with their start and end apart: 34, of which 19 were waited for; matrix products, arithmetic and copies ran while one was open for 3% of the time, Pallas kernels for 1%

profile of v10, /device:TPU:1, one launch (start us, length us, event | category | flops | bytes accessed | tf_op | source)
XLA Modules:
  0.0 274.9 jit_solution(10771514770012290331)
XLA Ops:
  6.5 8.4 %collective-permute-start.2 = (bf16[256,256]{1,0:T(8,128)(2,1)}, bf16[256,256]{1,0:T(8,128)(2,1)S(1)}, u32[]{:S(2)}, u32[]{:S(2)}) collective-permute-start(bf16[256,256]{1,0:T(8,128)(2,1)} %param.3), channel_id=1, source_target_pairs={{0,96},{1,97},{2,98},{3,99},{4,100},{5,101},{6,102},{7,103},{8,104... | collective-permute-start | bytes 393224 | tf_op jit(solution)/shard_map/ppermute | solution.py:24
  19.1 6.7 %collective-permute-done.1 = bf16[256,256]{1,0:T(8,128)(2,1)S(1)} collective-permute-done((bf16[256,256]{1,0:T(8,128)(2,1)}, bf16[256,256]{1,0:T(8,128)(2,1)S(1)}, u32[]{:S(2)}, u32[]{:S(2)}) %collective-permute-start.1) | collective-permute-done | bytes 131104 | tf_op jit(solution)/shard_map/ppermute | solution.py:24
  26.9 4.8 %collective-permute-start.5 = (bf16[4,256,256]{2,1,0:T(8,128)(2,1)S(1)}, bf16[4,256,256]{2,1,0:T(8,128)(2,1)S(1)}, u32[]{:S(2)}, u32[]{:S(2)}) collective-permute-start(bf16[4,256,256]{2,1,0:T(8,128)(2,1)S(1)} %get-tuple-element.58), channel_id=1, source_target_pairs={{0,384},{1,385},{2,386},{3,387},{4,388},{5,389},{6,390},{7,391},{8... | collective-permute-start | bytes 1572872 | tf_op jit(solution)/shard_map/ppermute | solution.py:24
  37.3 18.1 %collective-permute-done.3 = bf16[4,256,256]{2,1,0:T(8,128)(2,1)S(1)} collective-permute-done((bf16[4,256,256]{2,1,0:T(8,128)(2,1)S(1)}, bf16[4,256,256]{2,1,0:T(8,128)(2,1)S(1)}, u32[]{:S(2)}, u32[]{:S(2)}) %collective-permute-start.3) | collective-permute-done | bytes 524320 | tf_op jit(solution)/shard_map/ppermute | solution.py:24
  55.7 4.8 %collective-permute-start.6 = (bf16[4,4,256,256]{3,2,1,0:T(8,128)(2,1)S(1)}, bf16[4,4,256,256]{3,2,1,0:T(8,128)(2,1)}, u32[]{:S(2)}, u32[]{:S(2)}) collective-permute-start(bf16[4,4,256,256]{3,2,1,0:T(8,128)(2,1)S(1)} %pad_maximum_fusion), channel_id=1, source_target_pairs={{0,16},{1,17},{2,18},{3,19},{4,20},{5,21},{6,22},{7,23},{8,24},{9,... | collective-permute-start | bytes 6291464 | tf_op jit(solution)/shard_map/ppermute | solution.py:24
  61.6 6.4 %all-to-all-start = ((bf16[32,32,256]{2,1,0:T(8,128)(2,1)}), bf16[32,32,256]{2,1,0:T(8,128)(2,1)S(1)}, u32[]{:S(2)}, u32[]{:S(2)}) async-start(bf16[32,32,256]{2,1,0:T(8,128)(2,1)} %copy.14), calls=%async_computation | async-start | bytes 1048576 | tf_op jit(solution)/shard_map/all_to_all | solution.py:150
  71.7 13.2 %all-to-all-done = bf16[32,32,256]{2,1,0:T(8,128)(2,1)S(1)} async-done(((bf16[32,32,256]{2,1,0:T(8,128)(2,1)}), bf16[32,32,256]{2,1,0:T(8,128)(2,1)S(1)}, u32[]{:S(2)}, u32[]{:S(2)}) %all-to-all-start) | async-done | bytes 524320 | tf_op jit(solution)/shard_map/all_to_all | solution.py:150
  89.7 14.8 %all_to_all.15 = f32[32,8,256]{2,1,0:T(8,128)S(1)} all-to-all(f32[32,8,256]{2,1,0:T(8,128)S(1)} %bitcast.147), channel_id=1, replica_groups=mesh['dp'=32,'mp'=16] {'dp'}, dimensions={0} | all-to-all | bytes 524288 | tf_op jit(solution)/shard_map/all_to_all | solution.py:157
  111.3 5.4 %collective-permute-start.10 = (bf16[8,4096]{1,0:T(8,128)(2,1)S(1)}, bf16[8,4096]{1,0:T(8,128)(2,1)S(1)}, u32[]{:S(2)}, u32[]{:S(2)}) collective-permute-start(bf16[8,4096]{1,0:T(8,128)(2,1)S(1)} %get-tuple-element.31), channel_id=1, source_target_pairs={{0,72},{1,73},{2,74},{3,75},{4,76},{5,77},{6,78},{7,79},{8,64},{9,... | collective-permute-start | bytes 196616 | tf_op jit(solution)/shard_map/ppermute | solution.py:24
  116.6 4.5 %collective-permute-start.9 = (bf16[8,4096]{1,0:T(8,128)(2,1)S(1)}, bf16[8,4096]{1,0:T(8,128)(2,1)S(1)}, u32[]{:S(2)}, u32[]{:S(2)}) collective-permute-start(bf16[8,4096]{1,0:T(8,128)(2,1)S(1)} %get-tuple-element.31), channel_id=1, source_target_pairs={{0,8},{1,9},{2,10},{3,11},{4,12},{5,13},{6,14},{7,15},{8,0},{9,1},... | collective-permute-start | bytes 196616 | tf_op jit(solution)/shard_map/ppermute | solution.py:24
  126.4 4.3 %collective-permute-done.8 = bf16[8,4096]{1,0:T(8,128)(2,1)S(1)} collective-permute-done((bf16[8,4096]{1,0:T(8,128)(2,1)S(1)}, bf16[8,4096]{1,0:T(8,128)(2,1)S(1)}, u32[]{:S(2)}, u32[]{:S(2)}) %collective-permute-start.8) | collective-permute-done | bytes 65568 | tf_op jit(solution)/shard_map/ppermute | solution.py:24
  139.8 7.2 %collective-permute-done.13 = bf16[4,8,4096]{2,1,0:T(8,128)(2,1)S(1)} collective-permute-done((bf16[4,8,4096]{2,1,0:T(8,128)(2,1)S(1)}, bf16[4,8,4096]{2,1,0:T(8,128)(2,1)S(1)}, u32[]{:S(2)}, u32[]{:S(2)}) %collective-permute-start.13) | collective-permute-done | bytes 262176 | tf_op jit(solution)/shard_map/ppermute | solution.py:24
  149.5 5.7 %collective-permute-start.14 = (bf16[4,4,8,4096]{3,2,1,0:T(8,128)(2,1)S(1)}, bf16[4,4,8,4096]{3,2,1,0:T(8,128)(2,1)S(1)}, u32[]{:S(2)}, u32[]{:S(2)}) collective-permute-start(bf16[4,4,8,4096]{3,2,1,0:T(8,128)(2,1)S(1)} %pad_maximum_fusion.2), channel_id=1, source_target_pairs={{0,16},{1,17},{2,18},{3,19},{4,20},{5,21},{6,22},{7,23},{8,24},{9,... | collective-permute-start | bytes 3145736 | tf_op jit(solution)/shard_map/ppermute | solution.py:24
  169.0 4.1 %collective-permute-start.17 = (bf16[4,8,4096]{2,1,0:T(8,128)(2,1)}, bf16[4,8,4096]{2,1,0:T(8,128)(2,1)S(1)}, u32[]{:S(2)}, u32[]{:S(2)}) collective-permute-start(bf16[4,8,4096]{2,1,0:T(8,128)(2,1)} %get-tuple-element.52), channel_id=1, source_target_pairs={{0,256},{1,257},{2,258},{3,259},{4,260},{5,261},{6,262},{7,263},{8... | collective-permute-start | bytes 786440 | tf_op jit(solution)/shard_map/ppermute | solution.py:24
  177.5 4.4 %all-to-all-start.2 = ((bf16[8,8,4096]{2,1,0:T(8,128)(2,1)}), bf16[8,8,4096]{2,1,0:T(8,128)(2,1)S(1)}, u32[]{:S(2)}, u32[]{:S(2)}) async-start(bf16[8,8,4096]{2,1,0:T(8,128)(2,1)} %fusion.6), calls=%async_computation.2 | async-start | bytes 1048576 | tf_op jit(solution)/shard_map/all_to_all | solution.py:209
  183.0 6.5 %collective-permute-done.18 = bf16[4,8,4096]{2,1,0:T(8,128)(2,1)S(1)} collective-permute-done((bf16[4,8,4096]{2,1,0:T(8,128)(2,1)}, bf16[4,8,4096]{2,1,0:T(8,128)(2,1)S(1)}, u32[]{:S(2)}, u32[]{:S(2)}) %collective-permute-start.18) | collective-permute-done | bytes 262176 | tf_op jit(solution)/shard_map/ppermute | solution.py:24
  189.7 4.4 %collective-permute-start.19 = (bf16[8,4096]{1,0:T(8,128)(2,1)S(1)}, bf16[8,4096]{1,0:T(8,128)(2,1)S(1)}, u32[]{:S(2)}, u32[]{:S(2)}) collective-permute-start(bf16[8,4096]{1,0:T(8,128)(2,1)S(1)} %get-tuple-element.63), channel_id=1, source_target_pairs={{0,64},{1,65},{2,66},{3,67},{4,68},{5,69},{6,70},{7,71},{8,72},{9,... | collective-permute-start | bytes 196616 | tf_op jit(solution)/shard_map/ppermute | solution.py:24
  194.0 5.1 %collective-permute-start.20 = (bf16[8,4096]{1,0:T(8,128)(2,1)S(1)}, bf16[8,4096]{1,0:T(8,128)(2,1)S(1)}, u32[]{:S(2)}, u32[]{:S(2)}) collective-permute-start(bf16[8,4096]{1,0:T(8,128)(2,1)S(1)} %get-tuple-element.62), channel_id=1, source_target_pairs={{0,8},{1,9},{2,10},{3,11},{4,12},{5,13},{6,14},{7,15},{8,0},{9,1},... | collective-permute-start | bytes 196616 | tf_op jit(solution)/shard_map/ppermute | solution.py:24
  215.9 6.3 %all-gather.7.cloned.1.call-done = bf16[256,32,256]{2,1,0:T(8,128)(2,1)} async-done(((bf16[32,32,256]{2,1,0:T(8,128)(2,1)}), bf16[256,32,256]{2,1,0:T(8,128)(2,1)}) %all-gather.7.cloned.1.call-update) | async-done | bytes 4194320 | tf_op jit(solution)/shard_map/all_gather | solution.py:174
  222.2 4.3 %collective-permute-done.24 = bf16[8,8192]{1,0:T(8,128)(2,1)S(1)} collective-permute-done((bf16[8,8192]{1,0:T(8,128)(2,1)S(1)}, bf16[8,8192]{1,0:T(8,128)(2,1)S(1)}, u32[]{:S(2)}, u32[]{:S(2)}) %collective-permute-start.24) | collective-permute-done | bytes 131104 | tf_op jit(solution)/shard_map/ppermute | solution.py:24
  232.0 3.7 %collective-permute-start.26 = (bf16[4,8,8192]{2,1,0:T(8,128)(2,1)S(1)}, bf16[4,8,8192]{2,1,0:T(8,128)(2,1)S(1)}, u32[]{:S(2)}, u32[]{:S(2)}) collective-permute-start(bf16[4,8,8192]{2,1,0:T(8,128)(2,1)S(1)} %get-tuple-element.56), channel_id=1, source_target_pairs={{0,128},{1,129},{2,130},{3,131},{4,132},{5,133},{6,134},{7,135},{8... | collective-permute-start | bytes 1572872 | tf_op jit(solution)/shard_map/ppermute | solution.py:24
  235.6 18.0 %collective-permute-done.28 = bf16[4,8,8192]{2,1,0:T(8,128)(2,1)S(1)} collective-permute-done((bf16[4,8,8192]{2,1,0:T(8,128)(2,1)S(1)}, bf16[4,8,8192]{2,1,0:T(8,128)(2,1)S(1)}, u32[]{:S(2)}, u32[]{:S(2)}) %collective-permute-start.28) | collective-permute-done | bytes 524320 | tf_op jit(solution)/shard_map/ppermute | solution.py:24
  256.2 4.1 %collective-permute-start.29 = (bf16[4,4,8,8192]{3,2,1,0:T(8,128)(2,1)S(1)}, bf16[4,4,8,8192]{3,2,1,0:T(8,128)(2,1)S(1)}, u32[]{:S(2)}, u32[]{:S(2)}) collective-permute-start(bf16[4,4,8,8192]{3,2,1,0:T(8,128)(2,1)S(1)} %pad_maximum_fusion.1), channel_id=1, source_target_pairs={{0,16},{1,17},{2,18},{3,19},{4,20},{5,21},{6,22},{7,23},{8,24},{9,... | collective-permute-start | bytes 6291464 | tf_op jit(solution)/shard_map/ppermute | solution.py:24
  264.1 4.0 %shard_map.31 = f32[256,256]{1,0:T(8,128)} custom-call(bf16[128,8192]{1,0:T(8,128)(2,1)S(1)} %bitcast.146, bf16[8,32,32,256]{3,2,1,0:T(8,128)(2,1)S(1)} %bitcast.143, s32[32]{0:T(128)S(1)} %and_or_fusion.refs_0_, f32[128,256]{1,0:T(8,128)S(1)} %shard_map.30.refs_1_), custom_call_target="tpu_custom_call" | custom-call | flops 536870912 | bytes 6291456 | tf_op jit(solution)/shard_map/pallas_call | solution.py:116
  (103 shorter events, 91.6 us)
Async XLA Ops:
  6.5 12.6 %collective-permute-start.2 = (bf16[256,256]{1,0:T(8,128)(2,1)}, bf16[256,256]{1,0:T(8,128)(2,1)S(1)}, u32[]{:S(2)}, u32[]{:S(2)}) collective-permute-start(bf16[256,256]{1,0:T(8,128)(2,1)} %param.3), channel_id=1, source_target_pairs={{0,96},{1,97},{2,98},{3,99},{4,100},{5,101},{6,102},{7,103},{8,104... | collective-permute-start | bytes 393224 | tf_op jit(solution)/shard_map/ppermute | solution.py:24
  15.0 10.9 %collective-permute-start.1 = (bf16[256,256]{1,0:T(8,128)(2,1)}, bf16[256,256]{1,0:T(8,128)(2,1)S(1)}, u32[]{:S(2)}, u32[]{:S(2)}) collective-permute-start(bf16[256,256]{1,0:T(8,128)(2,1)} %param.3), channel_id=1, source_target_pairs={{0,64},{1,65},{2,66},{3,67},{4,68},{5,69},{6,70},{7,71},{8,72},{9,... | collective-permute-start | bytes 393224 | tf_op jit(solution)/shard_map/ppermute | solution.py:24
  26.9 28.6 %collective-permute-start.5 = (bf16[4,256,256]{2,1,0:T(8,128)(2,1)S(1)}, bf16[4,256,256]{2,1,0:T(8,128)(2,1)S(1)}, u32[]{:S(2)}, u32[]{:S(2)}) collective-permute-start(bf16[4,256,256]{2,1,0:T(8,128)(2,1)S(1)} %get-tuple-element.58), channel_id=1, source_target_pairs={{0,384},{1,385},{2,386},{3,387},{4,388},{5,389},{6,390},{7,391},{8... | collective-permute-start | bytes 1572872 | tf_op jit(solution)/shard_map/ppermute | solution.py:24
  31.7 23.7 %collective-permute-start.4 = (bf16[4,256,256]{2,1,0:T(8,128)(2,1)S(1)}, bf16[4,256,256]{2,1,0:T(8,128)(2,1)S(1)}, u32[]{:S(2)}, u32[]{:S(2)}) collective-permute-start(bf16[4,256,256]{2,1,0:T(8,128)(2,1)S(1)} %get-tuple-element.58), channel_id=1, source_target_pairs={{0,256},{1,257},{2,258},{3,259},{4,260},{5,261},{6,262},{7,263},{8... | collective-permute-start | bytes 1572872 | tf_op jit(solution)/shard_map/ppermute | solution.py:24
  34.2 21.3 %collective-permute-start.3 = (bf16[4,256,256]{2,1,0:T(8,128)(2,1)S(1)}, bf16[4,256,256]{2,1,0:T(8,128)(2,1)S(1)}, u32[]{:S(2)}, u32[]{:S(2)}) collective-permute-start(bf16[4,256,256]{2,1,0:T(8,128)(2,1)S(1)} %get-tuple-element.58), channel_id=1, source_target_pairs={{0,128},{1,129},{2,130},{3,131},{4,132},{5,133},{6,134},{7,135},{8... | collective-permute-start | bytes 1572872 | tf_op jit(solution)/shard_map/ppermute | solution.py:24
  55.7 29.2 %collective-permute-start.6 = (bf16[4,4,256,256]{3,2,1,0:T(8,128)(2,1)S(1)}, bf16[4,4,256,256]{3,2,1,0:T(8,128)(2,1)}, u32[]{:S(2)}, u32[]{:S(2)}) collective-permute-start(bf16[4,4,256,256]{3,2,1,0:T(8,128)(2,1)S(1)} %pad_maximum_fusion), channel_id=1, source_target_pairs={{0,16},{1,17},{2,18},{3,19},{4,20},{5,21},{6,22},{7,23},{8,24},{9,... | collective-permute-start | bytes 6291464 | tf_op jit(solution)/shard_map/ppermute | solution.py:24
  61.6 23.3 %all-to-all-start = ((bf16[32,32,256]{2,1,0:T(8,128)(2,1)}), bf16[32,32,256]{2,1,0:T(8,128)(2,1)S(1)}, u32[]{:S(2)}, u32[]{:S(2)}) async-start(bf16[32,32,256]{2,1,0:T(8,128)(2,1)} %copy.14), calls=%async_computation | async-start | bytes 1048576 | tf_op jit(solution)/shard_map/all_to_all | solution.py:150
  68.1 81.4 %all-gather.5.cloned.1.call-start = ((), (), s32[]{:S(2)}) async-start(), calls=%async_computation.3 | async-start | bytes 1179648 | tf_op jit(solution)/shard_map/all_gather | solution.py:170
  111.2 111.0 %all-gather.7.cloned.1.call-start = ((), (), s32[]{:S(2)}) async-start(), calls=%async_computation.4 | async-start | bytes 4718592 | tf_op jit(solution)/shard_map/all_gather | solution.py:174
  111.3 12.1 %collective-permute-start.10 = (bf16[8,4096]{1,0:T(8,128)(2,1)S(1)}, bf16[8,4096]{1,0:T(8,128)(2,1)S(1)}, u32[]{:S(2)}, u32[]{:S(2)}) collective-permute-start(bf16[8,4096]{1,0:T(8,128)(2,1)S(1)} %get-tuple-element.31), channel_id=1, source_target_pairs={{0,72},{1,73},{2,74},{3,75},{4,76},{5,77},{6,78},{7,79},{8,64},{9,... | collective-permute-start | bytes 196616 | tf_op jit(solution)/shard_map/ppermute | solution.py:24
  130.8 16.2 %collective-permute-start.13 = (bf16[4,8,4096]{2,1,0:T(8,128)(2,1)S(1)}, bf16[4,8,4096]{2,1,0:T(8,128)(2,1)S(1)}, u32[]{:S(2)}, u32[]{:S(2)}) collective-permute-start(bf16[4,8,4096]{2,1,0:T(8,128)(2,1)S(1)} %get-tuple-element.66), channel_id=1, source_target_pairs={{0,384},{1,385},{2,386},{3,387},{4,388},{5,389},{6,390},{7,391},{8... | collective-permute-start | bytes 786440 | tf_op jit(solution)/shard_map/ppermute | solution.py:24
  133.7 13.3 %collective-permute-start.12 = (bf16[4,8,4096]{2,1,0:T(8,128)(2,1)S(1)}, bf16[4,8,4096]{2,1,0:T(8,128)(2,1)S(1)}, u32[]{:S(2)}, u32[]{:S(2)}) collective-permute-start(bf16[4,8,4096]{2,1,0:T(8,128)(2,1)S(1)} %get-tuple-element.66), channel_id=1, source_target_pairs={{0,256},{1,257},{2,258},{3,259},{4,260},{5,261},{6,262},{7,263},{8... | collective-permute-start | bytes 786440 | tf_op jit(solution)/shard_map/ppermute | solution.py:24
  136.8 12.6 %collective-permute-start.11 = (bf16[4,8,4096]{2,1,0:T(8,128)(2,1)S(1)}, bf16[4,8,4096]{2,1,0:T(8,128)(2,1)S(1)}, u32[]{:S(2)}, u32[]{:S(2)}) collective-permute-start(bf16[4,8,4096]{2,1,0:T(8,128)(2,1)S(1)} %get-tuple-element.66), channel_id=1, source_target_pairs={{0,128},{1,129},{2,130},{3,131},{4,132},{5,133},{6,134},{7,135},{8... | collective-permute-start | bytes 786440 | tf_op jit(solution)/shard_map/ppermute | solution.py:24
  161.0 15.4 %collective-permute-start.22 = (bf16[64,4096]{1,0:T(8,128)(2,1)S(1)}, bf16[64,4096]{1,0:T(8,128)(2,1)S(1)}, u32[]{:S(2)}, u32[]{:S(2)}) collective-permute-start(bf16[64,4096]{1,0:T(8,128)(2,1)S(1)} %fusion.5), channel_id=1, source_target_pairs={{0,32},{1,33},{2,34},{3,35},{4,36},{5,37},{6,38},{7,39},{8,40},{9,... | collective-permute-start | bytes 1572872 | tf_op jit(solution)/shard_map/ppermute | solution.py:24
  165.7 16.2 %collective-permute-start.16 = (bf16[4,8,4096]{2,1,0:T(8,128)(2,1)}, bf16[4,8,4096]{2,1,0:T(8,128)(2,1)S(1)}, u32[]{:S(2)}, u32[]{:S(2)}) collective-permute-start(bf16[4,8,4096]{2,1,0:T(8,128)(2,1)} %get-tuple-element.53), channel_id=1, source_target_pairs={{0,128},{1,129},{2,130},{3,131},{4,132},{5,133},{6,134},{7,135},{8... | collective-permute-start | bytes 786440 | tf_op jit(solution)/shard_map/ppermute | solution.py:24
  169.0 14.1 %collective-permute-start.17 = (bf16[4,8,4096]{2,1,0:T(8,128)(2,1)}, bf16[4,8,4096]{2,1,0:T(8,128)(2,1)S(1)}, u32[]{:S(2)}, u32[]{:S(2)}) collective-permute-start(bf16[4,8,4096]{2,1,0:T(8,128)(2,1)} %get-tuple-element.52), channel_id=1, source_target_pairs={{0,256},{1,257},{2,258},{3,259},{4,260},{5,261},{6,262},{7,263},{8... | collective-permute-start | bytes 786440 | tf_op jit(solution)/shard_map/ppermute | solution.py:24
  173.1 16.4 %collective-permute-start.18 = (bf16[4,8,4096]{2,1,0:T(8,128)(2,1)}, bf16[4,8,4096]{2,1,0:T(8,128)(2,1)S(1)}, u32[]{:S(2)}, u32[]{:S(2)}) collective-permute-start(bf16[4,8,4096]{2,1,0:T(8,128)(2,1)} %get-tuple-element.51), channel_id=1, source_target_pairs={{0,384},{1,385},{2,386},{3,387},{4,388},{5,389},{6,390},{7,391},{8... | collective-permute-start | bytes 786440 | tf_op jit(solution)/shard_map/ppermute | solution.py:24
  177.5 28.9 %all-to-all-start.2 = ((bf16[8,8,4096]{2,1,0:T(8,128)(2,1)}), bf16[8,8,4096]{2,1,0:T(8,128)(2,1)S(1)}, u32[]{:S(2)}, u32[]{:S(2)}) async-start(bf16[8,8,4096]{2,1,0:T(8,128)(2,1)} %fusion.6), calls=%async_computation.2 | async-start | bytes 1048576 | tf_op jit(solution)/shard_map/all_to_all | solution.py:209
  189.7 11.5 %collective-permute-start.19 = (bf16[8,4096]{1,0:T(8,128)(2,1)S(1)}, bf16[8,4096]{1,0:T(8,128)(2,1)S(1)}, u32[]{:S(2)}, u32[]{:S(2)}) collective-permute-start(bf16[8,4096]{1,0:T(8,128)(2,1)S(1)} %get-tuple-element.63), channel_id=1, source_target_pairs={{0,64},{1,65},{2,66},{3,67},{4,68},{5,69},{6,70},{7,71},{8,72},{9,... | collective-permute-start | bytes 196616 | tf_op jit(solution)/shard_map/ppermute | solution.py:24
  210.4 11.8 %collective-permute-start.25 = (bf16[8,8192]{1,0:T(8,128)(2,1)S(1)}, bf16[8,8192]{1,0:T(8,128)(2,1)S(1)}, u32[]{:S(2)}, u32[]{:S(2)}) collective-permute-start(bf16[8,8192]{1,0:T(8,128)(2,1)S(1)} %bitcast.166), channel_id=1, source_target_pairs={{0,96},{1,97},{2,98},{3,99},{4,100},{5,101},{6,102},{7,103},{8,104... | collective-permute-start | bytes 393224 | tf_op jit(solution)/shard_map/ppermute | solution.py:24
  214.0 12.6 %collective-permute-start.24 = (bf16[8,8192]{1,0:T(8,128)(2,1)S(1)}, bf16[8,8192]{1,0:T(8,128)(2,1)S(1)}, u32[]{:S(2)}, u32[]{:S(2)}) collective-permute-start(bf16[8,8192]{1,0:T(8,128)(2,1)S(1)} %bitcast.167), channel_id=1, source_target_pairs={{0,64},{1,65},{2,66},{3,67},{4,68},{5,69},{6,70},{7,71},{8,72},{9,... | collective-permute-start | bytes 393224 | tf_op jit(solution)/shard_map/ppermute | solution.py:24
  226.6 27.0 %collective-permute-start.28 = (bf16[4,8,8192]{2,1,0:T(8,128)(2,1)S(1)}, bf16[4,8,8192]{2,1,0:T(8,128)(2,1)S(1)}, u32[]{:S(2)}, u32[]{:S(2)}) collective-permute-start(bf16[4,8,8192]{2,1,0:T(8,128)(2,1)S(1)} %get-tuple-element.56), channel_id=1, source_target_pairs={{0,384},{1,385},{2,386},{3,387},{4,388},{5,389},{6,390},{7,391},{8... | collective-permute-start | bytes 1572872 | tf_op jit(solution)/shard_map/ppermute | solution.py:24
  229.0 24.6 %collective-permute-start.27 = (bf16[4,8,8192]{2,1,0:T(8,128)(2,1)S(1)}, bf16[4,8,8192]{2,1,0:T(8,128)(2,1)S(1)}, u32[]{:S(2)}, u32[]{:S(2)}) collective-permute-start(bf16[4,8,8192]{2,1,0:T(8,128)(2,1)S(1)} %get-tuple-element.56), channel_id=1, source_target_pairs={{0,256},{1,257},{2,258},{3,259},{4,260},{5,261},{6,262},{7,263},{8... | collective-permute-start | bytes 1572872 | tf_op jit(solution)/shard_map/ppermute | solution.py:24
  232.0 23.9 %collective-permute-start.26 = (bf16[4,8,8192]{2,1,0:T(8,128)(2,1)S(1)}, bf16[4,8,8192]{2,1,0:T(8,128)(2,1)S(1)}, u32[]{:S(2)}, u32[]{:S(2)}) collective-permute-start(bf16[4,8,8192]{2,1,0:T(8,128)(2,1)S(1)} %get-tuple-element.56), channel_id=1, source_target_pairs={{0,128},{1,129},{2,130},{3,131},{4,132},{5,133},{6,134},{7,135},{8... | collective-permute-start | bytes 1572872 | tf_op jit(solution)/shard_map/ppermute | solution.py:24
  (15 other events, 96.9 us)
Sparse Core Ops, SparseCore 0:
  111.3 37.2 all-gather.4
  155.4 66.7 all-gather.6

commit v11 on v10

--- a/solution.py
+++ b/solution.py
@@ -146,12 +146,10 @@
     share = views * images // Y
     mine = lax.dynamic_slice_in_dim(flat, lax.rem(model_index, Y) * share, share, axis=0)
     pieces = mine.reshape(share, DP, rows).transpose(1, 0, 2)
-    weight_own, pieces = gather(gather(weight, ALONG_Z)[0], ALONG_X, pieces)
-    slices = lax.all_to_all(pieces, "dp", split_axis=0, concat_axis=0)
+    weight_own = gather(gather(weight, ALONG_Z)[0], ALONG_X)[0]
     weight_other = swap(weight_own, 1)
     half = (DP // 2, rows, feat)
     projected = project(order[: DP // 2], flat, weight_own.reshape(half))
-    projected, slices = lax.optimization_barrier((projected, slices))
     projected = project(order[DP // 2 :], flat, weight_other.reshape(half), projected)
 
     own = lax.all_to_all(
@@ -169,7 +167,9 @@
     first, pair = lax.optimization_barrier((normed[0], pair))
     columns_b = lax.all_gather(pair, "mp", axis=0, axis_index_groups=GROUPS)
     columns_b = columns_b.reshape(MP * block, total)
-    rows_own = gather(gather(first, STRIDED_Z)[0], ALONG_X)[0]
+    along_z, pieces = gather(first, STRIDED_Z, pieces)
+    slices = lax.all_to_all(pieces, "dp", split_axis=0, concat_axis=0)
+    rows_own = gather(along_z, ALONG_X)[0]
     rows_own, columns_b, slices = lax.optimization_barrier((rows_own, columns_b, slices))
     columns = lax.all_gather(slices, "mp", axis=0, axis_index_groups=GROUPS)
     rows_other = swap(rows_own, 1).reshape(feat // 2, total)

time: 276 us -> 269 us (0.975)
  waiting for transfers between devices: 105 us -> 97.4 us
  blocking collectives: 14.8 us -> 17.8 us
    all_to_all x1, waiting for transfers between devices: 13.2 us -> 0.01 us  [per_device(): slices = lax.all_to_all(pieces, 'dp', split_axis=0, concat_axis=0)]
    all_gather x1, waiting for transfers between devices: 0.02 us -> 3.89 us  [per_device(): columns_b = lax.all_gather(pair, 'mp', axis=0, axis_index_groups=GROUPS)]
    all_to_all x1, blocking collectives: 14.8 us -> 17.8 us  [per_device(): lax.all_to_all(projected.reshape(DP, block, views * images), 'dp', split_...]
  transfers between devices with their start and end apart: 34 -> 34, of which waited for: 19 -> 19; matrix products, arithmetic and copies ran while one was open for 3% -> 4% of each run, Pallas kernels for 1% -> 1%
where the time goes in v11:
time: 269 us; the launch traced here: 267 us
  starting transfers between devices  113 us (42%)
  waiting for transfers between devices  97.4 us (36%)
  blocking collectives  17.8 us (7%)
  between operations  14 us (5%)
  Pallas kernels  10.2 us (4%)
  local copies, waits for them, and re-layouts  5.57 us (2%)
  matrix products  5.14 us (2%)
  other arithmetic  3.75 us (1%)
    ppermute x30, starting transfers between devices, swap(): lax.ppermute(array, ('dp', 'mp'), [(i, i ^ mask) for i in range(DP * MP)])  105 us
    ppermute x30, waiting for transfers between devices, swap(): lax.ppermute(array, ('dp', 'mp'), [(i, i ^ mask) for i in range(DP * MP)])  87 us
    all_to_all x1, blocking collectives, per_device(): lax.all_to_all(projected.reshape(DP, block, views * images), 'dp', split_...  17.8 us
    pallas_call x2, Pallas kernels, weight_half(): pl.pallas_call(functools.partial(weight_kernel, last), grid=(2, devices /...  6.53 us
    all_gather x1, waiting for transfers between devices, per_device(): columns = lax.all_gather(slices, 'mp', axis=0, axis_index_groups=GROUPS)  6.46 us
  transfers between devices with their start and end apart: 34, of which 19 were waited for; matrix products, arithmetic and copies ran while one was open for 4% of the time, Pallas kernels for 1%

profile of v11, /device:TPU:1, one launch (start us, length us, event | category | flops | bytes accessed | tf_op | source)
XLA Modules:
  0.0 267.3 jit_solution(11115305077887285349)
XLA Ops:
  6.5 8.4 %collective-permute-start.2 = (bf16[256,256]{1,0:T(8,128)(2,1)}, bf16[256,256]{1,0:T(8,128)(2,1)S(1)}, u32[]{:S(2)}, u32[]{:S(2)}) collective-permute-start(bf16[256,256]{1,0:T(8,128)(2,1)} %param.3), channel_id=1, source_target_pairs={{0,96},{1,97},{2,98},{3,99},{4,100},{5,101},{6,102},{7,103},{8,104... | collective-permute-start | bytes 393224 | tf_op jit(solution)/shard_map/ppermute | solution.py:24
  19.1 6.7 %collective-permute-done.1 = bf16[256,256]{1,0:T(8,128)(2,1)S(1)} collective-permute-done((bf16[256,256]{1,0:T(8,128)(2,1)}, bf16[256,256]{1,0:T(8,128)(2,1)S(1)}, u32[]{:S(2)}, u32[]{:S(2)}) %collective-permute-start.1) | collective-permute-done | bytes 131104 | tf_op jit(solution)/shard_map/ppermute | solution.py:24
  26.9 4.8 %collective-permute-start.5 = (bf16[4,256,256]{2,1,0:T(8,128)(2,1)S(1)}, bf16[4,256,256]{2,1,0:T(8,128)(2,1)S(1)}, u32[]{:S(2)}, u32[]{:S(2)}) collective-permute-start(bf16[4,256,256]{2,1,0:T(8,128)(2,1)S(1)} %get-tuple-element.54), channel_id=1, source_target_pairs={{0,384},{1,385},{2,386},{3,387},{4,388},{5,389},{6,390},{7,391},{8... | collective-permute-start | bytes 1572872 | tf_op jit(solution)/shard_map/ppermute | solution.py:24
  36.1 17.0 %collective-permute-done.5 = bf16[4,256,256]{2,1,0:T(8,128)(2,1)S(1)} collective-permute-done((bf16[4,256,256]{2,1,0:T(8,128)(2,1)S(1)}, bf16[4,256,256]{2,1,0:T(8,128)(2,1)S(1)}, u32[]{:S(2)}, u32[]{:S(2)}) %collective-permute-start.5) | collective-permute-done | bytes 524320 | tf_op jit(solution)/shard_map/ppermute | solution.py:24
  55.7 4.8 %collective-permute-start.6 = (bf16[4,4,256,256]{3,2,1,0:T(8,128)(2,1)S(1)}, bf16[4,4,256,256]{3,2,1,0:T(8,128)(2,1)}, u32[]{:S(2)}, u32[]{:S(2)}) collective-permute-start(bf16[4,4,256,256]{3,2,1,0:T(8,128)(2,1)S(1)} %pad_maximum_fusion), channel_id=1, source_target_pairs={{0,16},{1,17},{2,18},{3,19},{4,20},{5,21},{6,22},{7,23},{8,24},{9,... | collective-permute-start | bytes 6291464 | tf_op jit(solution)/shard_map/ppermute | solution.py:24
  66.8 17.8 %all_to_all.15 = f32[32,8,256]{2,1,0:T(8,128)S(1)} all-to-all(f32[32,8,256]{2,1,0:T(8,128)S(1)} %bitcast.147), channel_id=1, replica_groups=mesh['dp'=32,'mp'=16] {'dp'}, dimensions={0} | all-to-all | bytes 524288 | tf_op jit(solution)/shard_map/all_to_all | solution.py:155
  91.3 5.3 %collective-permute-start.10 = (bf16[8,4096]{1,0:T(8,128)(2,1)S(1)}, bf16[8,4096]{1,0:T(8,128)(2,1)S(1)}, u32[]{:S(2)}, u32[]{:S(2)}) collective-permute-start(bf16[8,4096]{1,0:T(8,128)(2,1)S(1)} %get-tuple-element.26), channel_id=1, source_target_pairs={{0,72},{1,73},{2,74},{3,75},{4,76},{5,77},{6,78},{7,79},{8,64},{9,... | collective-permute-start | bytes 196616 | tf_op jit(solution)/shard_map/ppermute | solution.py:24
  96.7 4.5 %collective-permute-start.9 = (bf16[8,4096]{1,0:T(8,128)(2,1)S(1)}, bf16[8,4096]{1,0:T(8,128)(2,1)S(1)}, u32[]{:S(2)}, u32[]{:S(2)}) collective-permute-start(bf16[8,4096]{1,0:T(8,128)(2,1)S(1)} %get-tuple-element.26), channel_id=1, source_target_pairs={{0,8},{1,9},{2,10},{3,11},{4,12},{5,13},{6,14},{7,15},{8,0},{9,1},... | collective-permute-start | bytes 196616 | tf_op jit(solution)/shard_map/ppermute | solution.py:24
  104.6 6.0 %collective-permute-done.8 = bf16[8,4096]{1,0:T(8,128)(2,1)S(1)} collective-permute-done((bf16[8,4096]{1,0:T(8,128)(2,1)S(1)}, bf16[8,4096]{1,0:T(8,128)(2,1)S(1)}, u32[]{:S(2)}, u32[]{:S(2)}) %collective-permute-start.8) | collective-permute-done | bytes 65568 | tf_op jit(solution)/shard_map/ppermute | solution.py:24
  111.8 4.3 %all-to-all-start.1 = ((bf16[32,32,256]{2,1,0:T(8,128)(2,1)}), bf16[32,32,256]{2,1,0:T(8,128)(2,1)S(1)}, u32[]{:S(2)}, u32[]{:S(2)}) async-start(bf16[32,32,256]{2,1,0:T(8,128)(2,1)} %copy.15), calls=%async_computation.1 | async-start | bytes 1048576 | tf_op jit(solution)/shard_map/all_to_all | solution.py:171
  116.2 4.5 %collective-permute-start.13 = (bf16[4,8,4096]{2,1,0:T(8,128)(2,1)S(1)}, bf16[4,8,4096]{2,1,0:T(8,128)(2,1)S(1)}, u32[]{:S(2)}, u32[]{:S(2)}) collective-permute-start(bf16[4,8,4096]{2,1,0:T(8,128)(2,1)S(1)} %get-tuple-element.62), channel_id=1, source_target_pairs={{0,384},{1,385},{2,386},{3,387},{4,388},{5,389},{6,390},{7,391},{8... | collective-permute-start | bytes 786440 | tf_op jit(solution)/shard_map/ppermute | solution.py:24
  125.2 11.8 %collective-permute-done.13 = bf16[4,8,4096]{2,1,0:T(8,128)(2,1)S(1)} collective-permute-done((bf16[4,8,4096]{2,1,0:T(8,128)(2,1)S(1)}, bf16[4,8,4096]{2,1,0:T(8,128)(2,1)S(1)}, u32[]{:S(2)}, u32[]{:S(2)}) %collective-permute-start.13) | collective-permute-done | bytes 262176 | tf_op jit(solution)/shard_map/ppermute | solution.py:24
  137.2 3.9 %all-gather.5.cloned.1.call-done = bf16[16,8,4096]{2,1,0:T(8,128)(2,1)} async-done(((bf16[2,8,4096]{2,1,0:T(8,128)(2,1)}), bf16[16,8,4096]{2,1,0:T(8,128)(2,1)}) %all-gather.5.cloned.1.call-update) | async-done | bytes 1048592 | tf_op jit(solution)/shard_map/all_gather | solution.py:168
  141.0 6.6 %collective-permute-start.14 = (bf16[4,4,8,4096]{3,2,1,0:T(8,128)(2,1)S(1)}, bf16[4,4,8,4096]{3,2,1,0:T(8,128)(2,1)S(1)}, u32[]{:S(2)}, u32[]{:S(2)}) collective-permute-start(bf16[4,4,8,4096]{3,2,1,0:T(8,128)(2,1)S(1)} %pad_maximum_fusion.2), channel_id=1, source_target_pairs={{0,16},{1,17},{2,18},{3,19},{4,20},{5,21},{6,22},{7,23},{8,24},{9,... | collective-permute-start | bytes 3145736 | tf_op jit(solution)/shard_map/ppermute | solution.py:24
  161.3 4.3 %collective-permute-start.17 = (bf16[4,8,4096]{2,1,0:T(8,128)(2,1)}, bf16[4,8,4096]{2,1,0:T(8,128)(2,1)S(1)}, u32[]{:S(2)}, u32[]{:S(2)}) collective-permute-start(bf16[4,8,4096]{2,1,0:T(8,128)(2,1)} %get-tuple-element.48), channel_id=1, source_target_pairs={{0,256},{1,257},{2,258},{3,259},{4,260},{5,261},{6,262},{7,263},{8... | collective-permute-start | bytes 786440 | tf_op jit(solution)/shard_map/ppermute | solution.py:24
  169.9 4.4 %all-to-all-start.2 = ((bf16[8,8,4096]{2,1,0:T(8,128)(2,1)}), bf16[8,8,4096]{2,1,0:T(8,128)(2,1)S(1)}, u32[]{:S(2)}, u32[]{:S(2)}) async-start(bf16[8,8,4096]{2,1,0:T(8,128)(2,1)} %fusion.6), calls=%async_computation.2 | async-start | bytes 1048576 | tf_op jit(solution)/shard_map/all_to_all | solution.py:209
  175.6 6.5 %collective-permute-done.18 = bf16[4,8,4096]{2,1,0:T(8,128)(2,1)S(1)} collective-permute-done((bf16[4,8,4096]{2,1,0:T(8,128)(2,1)}, bf16[4,8,4096]{2,1,0:T(8,128)(2,1)S(1)}, u32[]{:S(2)}, u32[]{:S(2)}) %collective-permute-start.18) | collective-permute-done | bytes 262176 | tf_op jit(solution)/shard_map/ppermute | solution.py:24
  182.2 4.4 %collective-permute-start.19 = (bf16[8,4096]{1,0:T(8,128)(2,1)S(1)}, bf16[8,4096]{1,0:T(8,128)(2,1)S(1)}, u32[]{:S(2)}, u32[]{:S(2)}) collective-permute-start(bf16[8,4096]{1,0:T(8,128)(2,1)S(1)} %get-tuple-element.59), channel_id=1, source_target_pairs={{0,64},{1,65},{2,66},{3,67},{4,68},{5,69},{6,70},{7,71},{8,72},{9,... | collective-permute-start | bytes 196616 | tf_op jit(solution)/shard_map/ppermute | solution.py:24
  186.6 5.0 %collective-permute-start.20 = (bf16[8,4096]{1,0:T(8,128)(2,1)S(1)}, bf16[8,4096]{1,0:T(8,128)(2,1)S(1)}, u32[]{:S(2)}, u32[]{:S(2)}) collective-permute-start(bf16[8,4096]{1,0:T(8,128)(2,1)S(1)} %get-tuple-element.58), channel_id=1, source_target_pairs={{0,8},{1,9},{2,10},{3,11},{4,12},{5,13},{6,14},{7,15},{8,0},{9,1},... | collective-permute-start | bytes 196616 | tf_op jit(solution)/shard_map/ppermute | solution.py:24
  208.3 6.5 %all-gather.7.cloned.1.call-done = bf16[256,32,256]{2,1,0:T(8,128)(2,1)} async-done(((bf16[32,32,256]{2,1,0:T(8,128)(2,1)}), bf16[256,32,256]{2,1,0:T(8,128)(2,1)}) %all-gather.7.cloned.1.call-update) | async-done | bytes 4194320 | tf_op jit(solution)/shard_map/all_gather | solution.py:174
  214.8 4.2 %collective-permute-done.24 = bf16[8,8192]{1,0:T(8,128)(2,1)S(1)} collective-permute-done((bf16[8,8192]{1,0:T(8,128)(2,1)S(1)}, bf16[8,8192]{1,0:T(8,128)(2,1)S(1)}, u32[]{:S(2)}, u32[]{:S(2)}) %collective-permute-start.24) | collective-permute-done | bytes 131104 | tf_op jit(solution)/shard_map/ppermute | solution.py:24
  228.0 18.0 %collective-permute-done.28 = bf16[4,8,8192]{2,1,0:T(8,128)(2,1)S(1)} collective-permute-done((bf16[4,8,8192]{2,1,0:T(8,128)(2,1)S(1)}, bf16[4,8,8192]{2,1,0:T(8,128)(2,1)S(1)}, u32[]{:S(2)}, u32[]{:S(2)}) %collective-permute-start.28) | collective-permute-done | bytes 524320 | tf_op jit(solution)/shard_map/ppermute | solution.py:24
  248.6 4.1 %collective-permute-start.29 = (bf16[4,4,8,8192]{3,2,1,0:T(8,128)(2,1)S(1)}, bf16[4,4,8,8192]{3,2,1,0:T(8,128)(2,1)S(1)}, u32[]{:S(2)}, u32[]{:S(2)}) collective-permute-start(bf16[4,4,8,8192]{3,2,1,0:T(8,128)(2,1)S(1)} %pad_maximum_fusion.1), channel_id=1, source_target_pairs={{0,16},{1,17},{2,18},{3,19},{4,20},{5,21},{6,22},{7,23},{8,24},{9,... | collective-permute-start | bytes 6291464 | tf_op jit(solution)/shard_map/ppermute | solution.py:24
  256.4 4.0 %shard_map.31 = f32[256,256]{1,0:T(8,128)} custom-call(bf16[128,8192]{1,0:T(8,128)(2,1)S(1)} %bitcast.146, bf16[8,32,32,256]{3,2,1,0:T(8,128)(2,1)S(1)} %bitcast.143, s32[32]{0:T(128)S(1)} %and_or_fusion.refs_0_, f32[128,256]{1,0:T(8,128)S(1)} %shard_map.30.refs_1_), custom_call_target="tpu_custom_call" | custom-call | flops 536870912 | bytes 6291456 | tf_op jit(solution)/shard_map/pallas_call | solution.py:116
  (101 shorter events, 85.4 us)
Async XLA Ops:
  6.5 134.5 %all-gather.5.cloned.1.call-start = ((), (), s32[]{:S(2)}) async-start(), calls=%async_computation.3 | async-start | bytes 1179648 | tf_op jit(solution)/shard_map/all_gather | solution.py:168
  6.5 12.6 %collective-permute-start.2 = (bf16[256,256]{1,0:T(8,128)(2,1)}, bf16[256,256]{1,0:T(8,128)(2,1)S(1)}, u32[]{:S(2)}, u32[]{:S(2)}) collective-permute-start(bf16[256,256]{1,0:T(8,128)(2,1)} %param.3), channel_id=1, source_target_pairs={{0,96},{1,97},{2,98},{3,99},{4,100},{5,101},{6,102},{7,103},{8,104... | collective-permute-start | bytes 393224 | tf_op jit(solution)/shard_map/ppermute | solution.py:24
  15.0 10.9 %collective-permute-start.1 = (bf16[256,256]{1,0:T(8,128)(2,1)}, bf16[256,256]{1,0:T(8,128)(2,1)S(1)}, u32[]{:S(2)}, u32[]{:S(2)}) collective-permute-start(bf16[256,256]{1,0:T(8,128)(2,1)} %param.3), channel_id=1, source_target_pairs={{0,64},{1,65},{2,66},{3,67},{4,68},{5,69},{6,70},{7,71},{8,72},{9,... | collective-permute-start | bytes 393224 | tf_op jit(solution)/shard_map/ppermute | solution.py:24
  26.9 26.3 %collective-permute-start.5 = (bf16[4,256,256]{2,1,0:T(8,128)(2,1)S(1)}, bf16[4,256,256]{2,1,0:T(8,128)(2,1)S(1)}, u32[]{:S(2)}, u32[]{:S(2)}) collective-permute-start(bf16[4,256,256]{2,1,0:T(8,128)(2,1)S(1)} %get-tuple-element.54), channel_id=1, source_target_pairs={{0,384},{1,385},{2,386},{3,387},{4,388},{5,389},{6,390},{7,391},{8... | collective-permute-start | bytes 1572872 | tf_op jit(solution)/shard_map/ppermute | solution.py:24
  31.7 21.4 %collective-permute-start.4 = (bf16[4,256,256]{2,1,0:T(8,128)(2,1)S(1)}, bf16[4,256,256]{2,1,0:T(8,128)(2,1)S(1)}, u32[]{:S(2)}, u32[]{:S(2)}) collective-permute-start(bf16[4,256,256]{2,1,0:T(8,128)(2,1)S(1)} %get-tuple-element.54), channel_id=1, source_target_pairs={{0,256},{1,257},{2,258},{3,259},{4,260},{5,261},{6,262},{7,263},{8... | collective-permute-start | bytes 1572872 | tf_op jit(solution)/shard_map/ppermute | solution.py:24
  34.2 21.3 %collective-permute-start.3 = (bf16[4,256,256]{2,1,0:T(8,128)(2,1)S(1)}, bf16[4,256,256]{2,1,0:T(8,128)(2,1)S(1)}, u32[]{:S(2)}, u32[]{:S(2)}) collective-permute-start(bf16[4,256,256]{2,1,0:T(8,128)(2,1)S(1)} %get-tuple-element.54), channel_id=1, source_target_pairs={{0,128},{1,129},{2,130},{3,131},{4,132},{5,133},{6,134},{7,135},{8... | collective-permute-start | bytes 1572872 | tf_op jit(solution)/shard_map/ppermute | solution.py:24
  91.3 24.8 %collective-permute-start.10 = (bf16[8,4096]{1,0:T(8,128)(2,1)S(1)}, bf16[8,4096]{1,0:T(8,128)(2,1)S(1)}, u32[]{:S(2)}, u32[]{:S(2)}) collective-permute-start(bf16[8,4096]{1,0:T(8,128)(2,1)S(1)} %get-tuple-element.26), channel_id=1, source_target_pairs={{0,72},{1,73},{2,74},{3,75},{4,76},{5,77},{6,78},{7,79},{8,64},{9,... | collective-permute-start | bytes 196616 | tf_op jit(solution)/shard_map/ppermute | solution.py:24
  96.7 19.4 %collective-permute-start.9 = (bf16[8,4096]{1,0:T(8,128)(2,1)S(1)}, bf16[8,4096]{1,0:T(8,128)(2,1)S(1)}, u32[]{:S(2)}, u32[]{:S(2)}) collective-permute-start(bf16[8,4096]{1,0:T(8,128)(2,1)S(1)} %get-tuple-element.26), channel_id=1, source_target_pairs={{0,8},{1,9},{2,10},{3,11},{4,12},{5,13},{6,14},{7,15},{8,0},{9,1},... | collective-permute-start | bytes 196616 | tf_op jit(solution)/shard_map/ppermute | solution.py:24
  111.8 25.4 %all-to-all-start.1 = ((bf16[32,32,256]{2,1,0:T(8,128)(2,1)}), bf16[32,32,256]{2,1,0:T(8,128)(2,1)S(1)}, u32[]{:S(2)}, u32[]{:S(2)}) async-start(bf16[32,32,256]{2,1,0:T(8,128)(2,1)} %copy.15), calls=%async_computation.1 | async-start | bytes 1048576 | tf_op jit(solution)/shard_map/all_to_all | solution.py:171
  116.1 98.7 %all-gather.7.cloned.1.call-start = ((), (), s32[]{:S(2)}) async-start(), calls=%async_computation.4 | async-start | bytes 4718592 | tf_op jit(solution)/shard_map/all_gather | solution.py:174
  116.2 20.8 %collective-permute-start.13 = (bf16[4,8,4096]{2,1,0:T(8,128)(2,1)S(1)}, bf16[4,8,4096]{2,1,0:T(8,128)(2,1)S(1)}, u32[]{:S(2)}, u32[]{:S(2)}) collective-permute-start(bf16[4,8,4096]{2,1,0:T(8,128)(2,1)S(1)} %get-tuple-element.62), channel_id=1, source_target_pairs={{0,384},{1,385},{2,386},{3,387},{4,388},{5,389},{6,390},{7,391},{8... | collective-permute-start | bytes 786440 | tf_op jit(solution)/shard_map/ppermute | solution.py:24
  120.7 16.3 %collective-permute-start.12 = (bf16[4,8,4096]{2,1,0:T(8,128)(2,1)S(1)}, bf16[4,8,4096]{2,1,0:T(8,128)(2,1)S(1)}, u32[]{:S(2)}, u32[]{:S(2)}) collective-permute-start(bf16[4,8,4096]{2,1,0:T(8,128)(2,1)S(1)} %get-tuple-element.62), channel_id=1, source_target_pairs={{0,256},{1,257},{2,258},{3,259},{4,260},{5,261},{6,262},{7,263},{8... | collective-permute-start | bytes 786440 | tf_op jit(solution)/shard_map/ppermute | solution.py:24
  123.2 13.8 %collective-permute-start.11 = (bf16[4,8,4096]{2,1,0:T(8,128)(2,1)S(1)}, bf16[4,8,4096]{2,1,0:T(8,128)(2,1)S(1)}, u32[]{:S(2)}, u32[]{:S(2)}) collective-permute-start(bf16[4,8,4096]{2,1,0:T(8,128)(2,1)S(1)} %get-tuple-element.62), channel_id=1, source_target_pairs={{0,128},{1,129},{2,130},{3,131},{4,132},{5,133},{6,134},{7,135},{8... | collective-permute-start | bytes 786440 | tf_op jit(solution)/shard_map/ppermute | solution.py:24
  153.4 15.4 %collective-permute-start.22 = (bf16[64,4096]{1,0:T(8,128)(2,1)S(1)}, bf16[64,4096]{1,0:T(8,128)(2,1)S(1)}, u32[]{:S(2)}, u32[]{:S(2)}) collective-permute-start(bf16[64,4096]{1,0:T(8,128)(2,1)S(1)} %fusion.5), channel_id=1, source_target_pairs={{0,32},{1,33},{2,34},{3,35},{4,36},{5,37},{6,38},{7,39},{8,40},{9,... | collective-permute-start | bytes 1572872 | tf_op jit(solution)/shard_map/ppermute | solution.py:24
  158.2 16.1 %collective-permute-start.16 = (bf16[4,8,4096]{2,1,0:T(8,128)(2,1)}, bf16[4,8,4096]{2,1,0:T(8,128)(2,1)S(1)}, u32[]{:S(2)}, u32[]{:S(2)}) collective-permute-start(bf16[4,8,4096]{2,1,0:T(8,128)(2,1)} %get-tuple-element.49), channel_id=1, source_target_pairs={{0,128},{1,129},{2,130},{3,131},{4,132},{5,133},{6,134},{7,135},{8... | collective-permute-start | bytes 786440 | tf_op jit(solution)/shard_map/ppermute | solution.py:24
  161.3 14.2 %collective-permute-start.17 = (bf16[4,8,4096]{2,1,0:T(8,128)(2,1)}, bf16[4,8,4096]{2,1,0:T(8,128)(2,1)S(1)}, u32[]{:S(2)}, u32[]{:S(2)}) collective-permute-start(bf16[4,8,4096]{2,1,0:T(8,128)(2,1)} %get-tuple-element.48), channel_id=1, source_target_pairs={{0,256},{1,257},{2,258},{3,259},{4,260},{5,261},{6,262},{7,263},{8... | collective-permute-start | bytes 786440 | tf_op jit(solution)/shard_map/ppermute | solution.py:24
  165.7 16.4 %collective-permute-start.18 = (bf16[4,8,4096]{2,1,0:T(8,128)(2,1)}, bf16[4,8,4096]{2,1,0:T(8,128)(2,1)S(1)}, u32[]{:S(2)}, u32[]{:S(2)}) collective-permute-start(bf16[4,8,4096]{2,1,0:T(8,128)(2,1)} %get-tuple-element.47), channel_id=1, source_target_pairs={{0,384},{1,385},{2,386},{3,387},{4,388},{5,389},{6,390},{7,391},{8... | collective-permute-start | bytes 786440 | tf_op jit(solution)/shard_map/ppermute | solution.py:24
  169.9 28.9 %all-to-all-start.2 = ((bf16[8,8,4096]{2,1,0:T(8,128)(2,1)}), bf16[8,8,4096]{2,1,0:T(8,128)(2,1)S(1)}, u32[]{:S(2)}, u32[]{:S(2)}) async-start(bf16[8,8,4096]{2,1,0:T(8,128)(2,1)} %fusion.6), calls=%async_computation.2 | async-start | bytes 1048576 | tf_op jit(solution)/shard_map/all_to_all | solution.py:209
  182.2 11.5 %collective-permute-start.19 = (bf16[8,4096]{1,0:T(8,128)(2,1)S(1)}, bf16[8,4096]{1,0:T(8,128)(2,1)S(1)}, u32[]{:S(2)}, u32[]{:S(2)}) collective-permute-start(bf16[8,4096]{1,0:T(8,128)(2,1)S(1)} %get-tuple-element.59), channel_id=1, source_target_pairs={{0,64},{1,65},{2,66},{3,67},{4,68},{5,69},{6,70},{7,71},{8,72},{9,... | collective-permute-start | bytes 196616 | tf_op jit(solution)/shard_map/ppermute | solution.py:24
  203.1 11.7 %collective-permute-start.25 = (bf16[8,8192]{1,0:T(8,128)(2,1)S(1)}, bf16[8,8192]{1,0:T(8,128)(2,1)S(1)}, u32[]{:S(2)}, u32[]{:S(2)}) collective-permute-start(bf16[8,8192]{1,0:T(8,128)(2,1)S(1)} %bitcast.166), channel_id=1, source_target_pairs={{0,96},{1,97},{2,98},{3,99},{4,100},{5,101},{6,102},{7,103},{8,104... | collective-permute-start | bytes 393224 | tf_op jit(solution)/shard_map/ppermute | solution.py:24
  206.3 12.6 %collective-permute-start.24 = (bf16[8,8192]{1,0:T(8,128)(2,1)S(1)}, bf16[8,8192]{1,0:T(8,128)(2,1)S(1)}, u32[]{:S(2)}, u32[]{:S(2)}) collective-permute-start(bf16[8,8192]{1,0:T(8,128)(2,1)S(1)} %bitcast.167), channel_id=1, source_target_pairs={{0,64},{1,65},{2,66},{3,67},{4,68},{5,69},{6,70},{7,71},{8,72},{9,... | collective-permute-start | bytes 393224 | tf_op jit(solution)/shard_map/ppermute | solution.py:24
  219.0 27.0 %collective-permute-start.28 = (bf16[4,8,8192]{2,1,0:T(8,128)(2,1)S(1)}, bf16[4,8,8192]{2,1,0:T(8,128)(2,1)S(1)}, u32[]{:S(2)}, u32[]{:S(2)}) collective-permute-start(bf16[4,8,8192]{2,1,0:T(8,128)(2,1)S(1)} %get-tuple-element.52), channel_id=1, source_target_pairs={{0,384},{1,385},{2,386},{3,387},{4,388},{5,389},{6,390},{7,391},{8... | collective-permute-start | bytes 1572872 | tf_op jit(solution)/shard_map/ppermute | solution.py:24
  221.6 24.5 %collective-permute-start.27 = (bf16[4,8,8192]{2,1,0:T(8,128)(2,1)S(1)}, bf16[4,8,8192]{2,1,0:T(8,128)(2,1)S(1)}, u32[]{:S(2)}, u32[]{:S(2)}) collective-permute-start(bf16[4,8,8192]{2,1,0:T(8,128)(2,1)S(1)} %get-tuple-element.52), channel_id=1, source_target_pairs={{0,256},{1,257},{2,258},{3,259},{4,260},{5,261},{6,262},{7,263},{8... | collective-permute-start | bytes 1572872 | tf_op jit(solution)/shard_map/ppermute | solution.py:24
  224.4 23.8 %collective-permute-start.26 = (bf16[4,8,8192]{2,1,0:T(8,128)(2,1)S(1)}, bf16[4,8,8192]{2,1,0:T(8,128)(2,1)S(1)}, u32[]{:S(2)}, u32[]{:S(2)}) collective-permute-start(bf16[4,8,8192]{2,1,0:T(8,128)(2,1)S(1)} %get-tuple-element.52), channel_id=1, source_target_pairs={{0,128},{1,129},{2,130},{3,131},{4,132},{5,133},{6,134},{7,135},{8... | collective-permute-start | bytes 1572872 | tf_op jit(solution)/shard_map/ppermute | solution.py:24
  (14 other events, 100.1 us)
Sparse Core Ops, SparseCore 0:
  103.6 37.4 all-gather.4
  147.8 66.9 all-gather.6

commit v12 on v11

--- a/solution.py
+++ b/solution.py
@@ -164,12 +164,11 @@
 
     second = normed[1]
     pair = jnp.stack([second, partner(second)])
-    first, pair = lax.optimization_barrier((normed[0], pair))
+    first, pair, pieces = lax.optimization_barrier((normed[0], pair, pieces))
+    slices = lax.all_to_all(pieces, "dp", split_axis=0, concat_axis=0)
     columns_b = lax.all_gather(pair, "mp", axis=0, axis_index_groups=GROUPS)
     columns_b = columns_b.reshape(MP * block, total)
-    along_z, pieces = gather(first, STRIDED_Z, pieces)
-    slices = lax.all_to_all(pieces, "dp", split_axis=0, concat_axis=0)
-    rows_own = gather(along_z, ALONG_X)[0]
+    rows_own = gather(gather(first, STRIDED_Z)[0], ALONG_X)[0]
     rows_own, columns_b, slices = lax.optimization_barrier((rows_own, columns_b, slices))
     columns = lax.all_gather(slices, "mp", axis=0, axis_index_groups=GROUPS)
     rows_other = swap(rows_own, 1).reshape(feat // 2, total)

time: 269 us -> 257 us (0.955)
  blocking collectives: 17.8 us -> 0 us
  starting transfers between devices: 113 us -> 121 us
    all_to_all x1 -> x0, blocking collectives: 17.8 us -> none  [per_device(): lax.all_to_all(projected.reshape(DP, block, views * images), 'dp', split_...]
    all_to_all x0 -> x1, waiting for transfers between devices: none -> 11.2 us  [per_device(): lax.all_to_all(projected.reshape(DP, block, views * images), 'dp', split_...]
    ppermute x30, waiting for transfers between devices: 87 us -> 77.1 us  [swap(): lax.ppermute(array, ('dp', 'mp'), [(i, i ^ mask) for i in range(DP * MP)])]
    all_to_all x0 -> x1, starting transfers between devices: none -> 6.71 us  [per_device(): lax.all_to_all(projected.reshape(DP, block, views * images), 'dp', split_...]
    all_gather x1, waiting for transfers between devices: 3.89 us -> 0.02 us  [per_device(): columns_b = lax.all_gather(pair, 'mp', axis=0, axis_index_groups=GROUPS)]
  transfers between devices with their start and end apart: 34 -> 35, of which waited for: 19 -> 18; matrix products, arithmetic and copies ran while one was open for 4% -> 4% of each run, Pallas kernels for 1% -> 1%
where the time goes in v12:
time: 257 us; the launch traced here: 256 us
  starting transfers between devices  121 us (47%)
  waiting for transfers between devices  95.4 us (37%)
  between operations  14 us (5%)
  Pallas kernels  10.9 us (4%)
  local copies, waits for them, and re-layouts  5.57 us (2%)
  matrix products  5.15 us (2%)
  other arithmetic  3.75 us (1%)
    ppermute x30, starting transfers between devices, swap(): lax.ppermute(array, ('dp', 'mp'), [(i, i ^ mask) for i in range(DP * MP)])  102 us
    ppermute x30, waiting for transfers between devices, swap(): lax.ppermute(array, ('dp', 'mp'), [(i, i ^ mask) for i in range(DP * MP)])  77.1 us
    all_to_all x1, waiting for transfers between devices, per_device(): lax.all_to_all(projected.reshape(DP, block, views * images), 'dp', split_...  11.2 us
    all_gather x1, waiting for transfers between devices, per_device(): columns = lax.all_gather(slices, 'mp', axis=0, axis_index_groups=GROUPS)  7.06 us
    all_to_all x1, starting transfers between devices, per_device(): lax.all_to_all(projected.reshape(DP, block, views * images), 'dp', split_...  6.71 us
    pallas_call x2, Pallas kernels, weight_half(): pl.pallas_call(functools.partial(weight_kernel, last), grid=(2, devices /...  6.53 us
    all_to_all x1, starting transfers between devices, per_device(): lax.all_to_all(terms_b.reshape(Y, block, total), 'mp', split_axis=0, conc...  6.15 us
    all_to_all x1, starting transfers between devices, per_device(): slices = lax.all_to_all(pieces, 'dp', split_axis=0, concat_axis=0)  5.95 us
  transfers between devices with their start and end apart: 35, of which 18 were waited for; matrix products, arithmetic and copies ran while one was open for 4% of the time, Pallas kernels for 1%

profile of v12, /device:TPU:1, one launch (start us, length us, event | category | flops | bytes accessed | tf_op | source)
XLA Modules:
  0.0 256.1 jit_solution(14123630057215526516)
XLA Ops:
  6.5 8.4 %collective-permute-start.2 = (bf16[256,256]{1,0:T(8,128)(2,1)}, bf16[256,256]{1,0:T(8,128)(2,1)S(1)}, u32[]{:S(2)}, u32[]{:S(2)}) collective-permute-start(bf16[256,256]{1,0:T(8,128)(2,1)} %param.3), channel_id=1, source_target_pairs={{0,96},{1,97},{2,98},{3,99},{4,100},{5,101},{6,102},{7,103},{8,104... | collective-permute-start | bytes 393224 | tf_op jit(solution)/shard_map/ppermute | solution.py:24
  19.1 6.7 %collective-permute-done.1 = bf16[256,256]{1,0:T(8,128)(2,1)S(1)} collective-permute-done((bf16[256,256]{1,0:T(8,128)(2,1)}, bf16[256,256]{1,0:T(8,128)(2,1)S(1)}, u32[]{:S(2)}, u32[]{:S(2)}) %collective-permute-start.1) | collective-permute-done | bytes 131104 | tf_op jit(solution)/shard_map/ppermute | solution.py:24
  26.9 4.8 %collective-permute-start.5 = (bf16[4,256,256]{2,1,0:T(8,128)(2,1)S(1)}, bf16[4,256,256]{2,1,0:T(8,128)(2,1)S(1)}, u32[]{:S(2)}, u32[]{:S(2)}) collective-permute-start(bf16[4,256,256]{2,1,0:T(8,128)(2,1)S(1)} %get-tuple-element.52), channel_id=1, source_target_pairs={{0,384},{1,385},{2,386},{3,387},{4,388},{5,389},{6,390},{7,391},{8... | collective-permute-start | bytes 1572872 | tf_op jit(solution)/shard_map/ppermute | solution.py:24
  36.1 17.0 %collective-permute-done.5 = bf16[4,256,256]{2,1,0:T(8,128)(2,1)S(1)} collective-permute-done((bf16[4,256,256]{2,1,0:T(8,128)(2,1)S(1)}, bf16[4,256,256]{2,1,0:T(8,128)(2,1)S(1)}, u32[]{:S(2)}, u32[]{:S(2)}) %collective-permute-start.5) | collective-permute-done | bytes 524320 | tf_op jit(solution)/shard_map/ppermute | solution.py:24
  55.7 4.8 %collective-permute-start.6 = (bf16[4,4,256,256]{3,2,1,0:T(8,128)(2,1)S(1)}, bf16[4,4,256,256]{3,2,1,0:T(8,128)(2,1)}, u32[]{:S(2)}, u32[]{:S(2)}) collective-permute-start(bf16[4,4,256,256]{3,2,1,0:T(8,128)(2,1)S(1)} %pad_maximum_fusion), channel_id=1, source_target_pairs={{0,16},{1,17},{2,18},{3,19},{4,20},{5,21},{6,22},{7,23},{8,24},{9,... | collective-permute-start | bytes 6291464 | tf_op jit(solution)/shard_map/ppermute | solution.py:24
  67.5 6.7 %all-to-all-start = ((f32[32,8,256]{2,1,0:T(8,128)}), f32[32,8,256]{2,1,0:T(8,128)S(1)}, u32[]{:S(2)}, u32[]{:S(2)}) async-start(f32[32,8,256]{2,1,0:T(8,128)} %bitcast.11), calls=%async_computation | async-start | bytes 524288 | tf_op jit(solution)/shard_map/all_to_all | solution.py:155
  74.3 11.2 %all-to-all-done = f32[32,8,256]{2,1,0:T(8,128)S(1)} async-done(((f32[32,8,256]{2,1,0:T(8,128)}), f32[32,8,256]{2,1,0:T(8,128)S(1)}, u32[]{:S(2)}, u32[]{:S(2)}) %all-to-all-start) | async-done | bytes 262176 | tf_op jit(solution)/shard_map/all_to_all | solution.py:155
  92.3 5.4 %collective-permute-start.10 = (bf16[8,4096]{1,0:T(8,128)(2,1)S(1)}, bf16[8,4096]{1,0:T(8,128)(2,1)S(1)}, u32[]{:S(2)}, u32[]{:S(2)}) collective-permute-start(bf16[8,4096]{1,0:T(8,128)(2,1)S(1)} %get-tuple-element.25), channel_id=1, source_target_pairs={{0,72},{1,73},{2,74},{3,75},{4,76},{5,77},{6,78},{7,79},{8,64},{9,... | collective-permute-start | bytes 196616 | tf_op jit(solution)/shard_map/ppermute | solution.py:24
  97.6 4.5 %collective-permute-start.9 = (bf16[8,4096]{1,0:T(8,128)(2,1)S(1)}, bf16[8,4096]{1,0:T(8,128)(2,1)S(1)}, u32[]{:S(2)}, u32[]{:S(2)}) collective-permute-start(bf16[8,4096]{1,0:T(8,128)(2,1)S(1)} %get-tuple-element.25), channel_id=1, source_target_pairs={{0,8},{1,9},{2,10},{3,11},{4,12},{5,13},{6,14},{7,15},{8,0},{9,1},... | collective-permute-start | bytes 196616 | tf_op jit(solution)/shard_map/ppermute | solution.py:24
  105.4 5.9 %all-to-all-start.1 = ((bf16[32,32,256]{2,1,0:T(8,128)(2,1)}), bf16[32,32,256]{2,1,0:T(8,128)(2,1)S(1)}, u32[]{:S(2)}, u32[]{:S(2)}) async-start(bf16[32,32,256]{2,1,0:T(8,128)(2,1)} %copy.15), calls=%async_computation.1 | async-start | bytes 1048576 | tf_op jit(solution)/shard_map/all_to_all | solution.py:168
  111.8 4.3 %collective-permute-start.13 = (bf16[4,8,4096]{2,1,0:T(8,128)(2,1)S(1)}, bf16[4,8,4096]{2,1,0:T(8,128)(2,1)S(1)}, u32[]{:S(2)}, u32[]{:S(2)}) collective-permute-start(bf16[4,8,4096]{2,1,0:T(8,128)(2,1)S(1)} %get-tuple-element.60), channel_id=1, source_target_pairs={{0,384},{1,385},{2,386},{3,387},{4,388},{5,389},{6,390},{7,391},{8... | collective-permute-start | bytes 786440 | tf_op jit(solution)/shard_map/ppermute | solution.py:24
  120.8 11.4 %collective-permute-done.13 = bf16[4,8,4096]{2,1,0:T(8,128)(2,1)S(1)} collective-permute-done((bf16[4,8,4096]{2,1,0:T(8,128)(2,1)S(1)}, bf16[4,8,4096]{2,1,0:T(8,128)(2,1)S(1)}, u32[]{:S(2)}, u32[]{:S(2)}) %collective-permute-start.13) | collective-permute-done | bytes 262176 | tf_op jit(solution)/shard_map/ppermute | solution.py:24
  132.3 3.9 %collective-permute-start.14 = (bf16[4,4,8,4096]{3,2,1,0:T(8,128)(2,1)S(1)}, bf16[4,4,8,4096]{3,2,1,0:T(8,128)(2,1)S(1)}, u32[]{:S(2)}, u32[]{:S(2)}) collective-permute-start(bf16[4,4,8,4096]{3,2,1,0:T(8,128)(2,1)S(1)} %pad_maximum_fusion.2), channel_id=1, source_target_pairs={{0,16},{1,17},{2,18},{3,19},{4,20},{5,21},{6,22},{7,23},{8,24},{9,... | collective-permute-start | bytes 3145736 | tf_op jit(solution)/shard_map/ppermute | solution.py:24
  149.9 4.4 %collective-permute-start.17 = (bf16[4,8,4096]{2,1,0:T(8,128)(2,1)}, bf16[4,8,4096]{2,1,0:T(8,128)(2,1)S(1)}, u32[]{:S(2)}, u32[]{:S(2)}) collective-permute-start(bf16[4,8,4096]{2,1,0:T(8,128)(2,1)} %get-tuple-element.46), channel_id=1, source_target_pairs={{0,256},{1,257},{2,258},{3,259},{4,260},{5,261},{6,262},{7,263},{8... | collective-permute-start | bytes 786440 | tf_op jit(solution)/shard_map/ppermute | solution.py:24
  158.6 6.1 %all-to-all-start.2 = ((bf16[8,8,4096]{2,1,0:T(8,128)(2,1)}), bf16[8,8,4096]{2,1,0:T(8,128)(2,1)S(1)}, u32[]{:S(2)}, u32[]{:S(2)}) async-start(bf16[8,8,4096]{2,1,0:T(8,128)(2,1)} %fusion.6), calls=%async_computation.2 | async-start | bytes 1048576 | tf_op jit(solution)/shard_map/all_to_all | solution.py:208
  164.8 6.0 %collective-permute-done.18 = bf16[4,8,4096]{2,1,0:T(8,128)(2,1)S(1)} collective-permute-done((bf16[4,8,4096]{2,1,0:T(8,128)(2,1)}, bf16[4,8,4096]{2,1,0:T(8,128)(2,1)S(1)}, u32[]{:S(2)}, u32[]{:S(2)}) %collective-permute-start.18) | collective-permute-done | bytes 262176 | tf_op jit(solution)/shard_map/ppermute | solution.py:24
  170.9 4.5 %collective-permute-start.19 = (bf16[8,4096]{1,0:T(8,128)(2,1)S(1)}, bf16[8,4096]{1,0:T(8,128)(2,1)S(1)}, u32[]{:S(2)}, u32[]{:S(2)}) collective-permute-start(bf16[8,4096]{1,0:T(8,128)(2,1)S(1)} %get-tuple-element.57), channel_id=1, source_target_pairs={{0,64},{1,65},{2,66},{3,67},{4,68},{5,69},{6,70},{7,71},{8,72},{9,... | collective-permute-start | bytes 196616 | tf_op jit(solution)/shard_map/ppermute | solution.py:24
  175.4 5.0 %collective-permute-start.20 = (bf16[8,4096]{1,0:T(8,128)(2,1)S(1)}, bf16[8,4096]{1,0:T(8,128)(2,1)S(1)}, u32[]{:S(2)}, u32[]{:S(2)}) collective-permute-start(bf16[8,4096]{1,0:T(8,128)(2,1)S(1)} %get-tuple-element.56), channel_id=1, source_target_pairs={{0,8},{1,9},{2,10},{3,11},{4,12},{5,13},{6,14},{7,15},{8,0},{9,1},... | collective-permute-start | bytes 196616 | tf_op jit(solution)/shard_map/ppermute | solution.py:24
  191.9 3.6 %collective-permute-start.25 = (bf16[8,8192]{1,0:T(8,128)(2,1)S(1)}, bf16[8,8192]{1,0:T(8,128)(2,1)S(1)}, u32[]{:S(2)}, u32[]{:S(2)}) collective-permute-start(bf16[8,8192]{1,0:T(8,128)(2,1)S(1)} %bitcast.165), channel_id=1, source_target_pairs={{0,96},{1,97},{2,98},{3,99},{4,100},{5,101},{6,102},{7,103},{8,104... | collective-permute-start | bytes 393224 | tf_op jit(solution)/shard_map/ppermute | solution.py:24
  197.5 7.1 %all-gather.7.cloned.1.call-done = bf16[256,32,256]{2,1,0:T(8,128)(2,1)} async-done(((bf16[32,32,256]{2,1,0:T(8,128)(2,1)}), bf16[256,32,256]{2,1,0:T(8,128)(2,1)}) %all-gather.7.cloned.1.call-update) | async-done | bytes 4194320 | tf_op jit(solution)/shard_map/all_gather | solution.py:173
  207.8 3.5 %collective-permute-start.28 = (bf16[4,8,8192]{2,1,0:T(8,128)(2,1)S(1)}, bf16[4,8,8192]{2,1,0:T(8,128)(2,1)S(1)}, u32[]{:S(2)}, u32[]{:S(2)}) collective-permute-start(bf16[4,8,8192]{2,1,0:T(8,128)(2,1)S(1)} %get-tuple-element.50), channel_id=1, source_target_pairs={{0,384},{1,385},{2,386},{3,387},{4,388},{5,389},{6,390},{7,391},{8... | collective-permute-start | bytes 1572872 | tf_op jit(solution)/shard_map/ppermute | solution.py:24
  216.8 17.8 %collective-permute-done.28 = bf16[4,8,8192]{2,1,0:T(8,128)(2,1)S(1)} collective-permute-done((bf16[4,8,8192]{2,1,0:T(8,128)(2,1)S(1)}, bf16[4,8,8192]{2,1,0:T(8,128)(2,1)S(1)}, u32[]{:S(2)}, u32[]{:S(2)}) %collective-permute-start.28) | collective-permute-done | bytes 524320 | tf_op jit(solution)/shard_map/ppermute | solution.py:24
  237.2 4.3 %collective-permute-start.29 = (bf16[4,4,8,8192]{3,2,1,0:T(8,128)(2,1)S(1)}, bf16[4,4,8,8192]{3,2,1,0:T(8,128)(2,1)S(1)}, u32[]{:S(2)}, u32[]{:S(2)}) collective-permute-start(bf16[4,4,8,8192]{3,2,1,0:T(8,128)(2,1)S(1)} %pad_maximum_fusion.1), channel_id=1, source_target_pairs={{0,16},{1,17},{2,18},{3,19},{4,20},{5,21},{6,22},{7,23},{8,24},{9,... | collective-permute-start | bytes 6291464 | tf_op jit(solution)/shard_map/ppermute | solution.py:24
  245.3 4.0 %shard_map.31 = f32[256,256]{1,0:T(8,128)} custom-call(bf16[128,8192]{1,0:T(8,128)(2,1)S(1)} %bitcast.146, bf16[8,32,32,256]{3,2,1,0:T(8,128)(2,1)S(1)} %bitcast.143, s32[32]{0:T(128)S(1)} %and_or_fusion.refs_0_, f32[128,256]{1,0:T(8,128)S(1)} %shard_map.30.refs_1_), custom_call_target="tpu_custom_call" | custom-call | flops 536870912 | bytes 6291456 | tf_op jit(solution)/shard_map/pallas_call | solution.py:116
  (102 shorter events, 80.6 us)
Async XLA Ops:
  6.5 12.6 %collective-permute-start.2 = (bf16[256,256]{1,0:T(8,128)(2,1)}, bf16[256,256]{1,0:T(8,128)(2,1)S(1)}, u32[]{:S(2)}, u32[]{:S(2)}) collective-permute-start(bf16[256,256]{1,0:T(8,128)(2,1)} %param.3), channel_id=1, source_target_pairs={{0,96},{1,97},{2,98},{3,99},{4,100},{5,101},{6,102},{7,103},{8,104... | collective-permute-start | bytes 393224 | tf_op jit(solution)/shard_map/ppermute | solution.py:24
  26.9 26.3 %collective-permute-start.5 = (bf16[4,256,256]{2,1,0:T(8,128)(2,1)S(1)}, bf16[4,256,256]{2,1,0:T(8,128)(2,1)S(1)}, u32[]{:S(2)}, u32[]{:S(2)}) collective-permute-start(bf16[4,256,256]{2,1,0:T(8,128)(2,1)S(1)} %get-tuple-element.52), channel_id=1, source_target_pairs={{0,384},{1,385},{2,386},{3,387},{4,388},{5,389},{6,390},{7,391},{8... | collective-permute-start | bytes 1572872 | tf_op jit(solution)/shard_map/ppermute | solution.py:24
  31.7 21.4 %collective-permute-start.4 = (bf16[4,256,256]{2,1,0:T(8,128)(2,1)S(1)}, bf16[4,256,256]{2,1,0:T(8,128)(2,1)S(1)}, u32[]{:S(2)}, u32[]{:S(2)}) collective-permute-start(bf16[4,256,256]{2,1,0:T(8,128)(2,1)S(1)} %get-tuple-element.52), channel_id=1, source_target_pairs={{0,256},{1,257},{2,258},{3,259},{4,260},{5,261},{6,262},{7,263},{8... | collective-permute-start | bytes 1572872 | tf_op jit(solution)/shard_map/ppermute | solution.py:24
  34.2 21.3 %collective-permute-start.3 = (bf16[4,256,256]{2,1,0:T(8,128)(2,1)S(1)}, bf16[4,256,256]{2,1,0:T(8,128)(2,1)S(1)}, u32[]{:S(2)}, u32[]{:S(2)}) collective-permute-start(bf16[4,256,256]{2,1,0:T(8,128)(2,1)S(1)} %get-tuple-element.52), channel_id=1, source_target_pairs={{0,128},{1,129},{2,130},{3,131},{4,132},{5,133},{6,134},{7,135},{8... | collective-permute-start | bytes 1572872 | tf_op jit(solution)/shard_map/ppermute | solution.py:24
  67.5 18.0 %all-to-all-start = ((f32[32,8,256]{2,1,0:T(8,128)}), f32[32,8,256]{2,1,0:T(8,128)S(1)}, u32[]{:S(2)}, u32[]{:S(2)}) async-start(f32[32,8,256]{2,1,0:T(8,128)} %bitcast.11), calls=%async_computation | async-start | bytes 524288 | tf_op jit(solution)/shard_map/all_to_all | solution.py:155
  74.2 58.1 %all-gather.5.cloned.1.call-start = ((), (), s32[]{:S(2)}) async-start(), calls=%async_computation.3 | async-start | bytes 1179648 | tf_op jit(solution)/shard_map/all_gather | solution.py:169
  92.3 19.2 %collective-permute-start.10 = (bf16[8,4096]{1,0:T(8,128)(2,1)S(1)}, bf16[8,4096]{1,0:T(8,128)(2,1)S(1)}, u32[]{:S(2)}, u32[]{:S(2)}) collective-permute-start(bf16[8,4096]{1,0:T(8,128)(2,1)S(1)} %get-tuple-element.25), channel_id=1, source_target_pairs={{0,72},{1,73},{2,74},{3,75},{4,76},{5,77},{6,78},{7,79},{8,64},{9,... | collective-permute-start | bytes 196616 | tf_op jit(solution)/shard_map/ppermute | solution.py:24
  97.6 13.8 %collective-permute-start.9 = (bf16[8,4096]{1,0:T(8,128)(2,1)S(1)}, bf16[8,4096]{1,0:T(8,128)(2,1)S(1)}, u32[]{:S(2)}, u32[]{:S(2)}) collective-permute-start(bf16[8,4096]{1,0:T(8,128)(2,1)S(1)} %get-tuple-element.25), channel_id=1, source_target_pairs={{0,8},{1,9},{2,10},{3,11},{4,12},{5,13},{6,14},{7,15},{8,0},{9,1},... | collective-permute-start | bytes 196616 | tf_op jit(solution)/shard_map/ppermute | solution.py:24
  105.4 26.9 %all-to-all-start.1 = ((bf16[32,32,256]{2,1,0:T(8,128)(2,1)}), bf16[32,32,256]{2,1,0:T(8,128)(2,1)S(1)}, u32[]{:S(2)}, u32[]{:S(2)}) async-start(bf16[32,32,256]{2,1,0:T(8,128)(2,1)} %copy.15), calls=%async_computation.1 | async-start | bytes 1048576 | tf_op jit(solution)/shard_map/all_to_all | solution.py:168
  111.4 93.1 %all-gather.7.cloned.1.call-start = ((), (), s32[]{:S(2)}) async-start(), calls=%async_computation.4 | async-start | bytes 4718592 | tf_op jit(solution)/shard_map/all_gather | solution.py:173
  111.8 20.4 %collective-permute-start.13 = (bf16[4,8,4096]{2,1,0:T(8,128)(2,1)S(1)}, bf16[4,8,4096]{2,1,0:T(8,128)(2,1)S(1)}, u32[]{:S(2)}, u32[]{:S(2)}) collective-permute-start(bf16[4,8,4096]{2,1,0:T(8,128)(2,1)S(1)} %get-tuple-element.60), channel_id=1, source_target_pairs={{0,384},{1,385},{2,386},{3,387},{4,388},{5,389},{6,390},{7,391},{8... | collective-permute-start | bytes 786440 | tf_op jit(solution)/shard_map/ppermute | solution.py:24
  116.1 16.1 %collective-permute-start.12 = (bf16[4,8,4096]{2,1,0:T(8,128)(2,1)S(1)}, bf16[4,8,4096]{2,1,0:T(8,128)(2,1)S(1)}, u32[]{:S(2)}, u32[]{:S(2)}) collective-permute-start(bf16[4,8,4096]{2,1,0:T(8,128)(2,1)S(1)} %get-tuple-element.60), channel_id=1, source_target_pairs={{0,256},{1,257},{2,258},{3,259},{4,260},{5,261},{6,262},{7,263},{8... | collective-permute-start | bytes 786440 | tf_op jit(solution)/shard_map/ppermute | solution.py:24
  118.5 13.6 %collective-permute-start.11 = (bf16[4,8,4096]{2,1,0:T(8,128)(2,1)S(1)}, bf16[4,8,4096]{2,1,0:T(8,128)(2,1)S(1)}, u32[]{:S(2)}, u32[]{:S(2)}) collective-permute-start(bf16[4,8,4096]{2,1,0:T(8,128)(2,1)S(1)} %get-tuple-element.60), channel_id=1, source_target_pairs={{0,128},{1,129},{2,130},{3,131},{4,132},{5,133},{6,134},{7,135},{8... | collective-permute-start | bytes 786440 | tf_op jit(solution)/shard_map/ppermute | solution.py:24
  142.0 15.4 %collective-permute-start.22 = (bf16[64,4096]{1,0:T(8,128)(2,1)S(1)}, bf16[64,4096]{1,0:T(8,128)(2,1)S(1)}, u32[]{:S(2)}, u32[]{:S(2)}) collective-permute-start(bf16[64,4096]{1,0:T(8,128)(2,1)S(1)} %fusion.5), channel_id=1, source_target_pairs={{0,32},{1,33},{2,34},{3,35},{4,36},{5,37},{6,38},{7,39},{8,40},{9,... | collective-permute-start | bytes 1572872 | tf_op jit(solution)/shard_map/ppermute | solution.py:24
  146.8 17.9 %collective-permute-start.16 = (bf16[4,8,4096]{2,1,0:T(8,128)(2,1)}, bf16[4,8,4096]{2,1,0:T(8,128)(2,1)S(1)}, u32[]{:S(2)}, u32[]{:S(2)}) collective-permute-start(bf16[4,8,4096]{2,1,0:T(8,128)(2,1)} %get-tuple-element.47), channel_id=1, source_target_pairs={{0,128},{1,129},{2,130},{3,131},{4,132},{5,133},{6,134},{7,135},{8... | collective-permute-start | bytes 786440 | tf_op jit(solution)/shard_map/ppermute | solution.py:24
  149.9 14.8 %collective-permute-start.17 = (bf16[4,8,4096]{2,1,0:T(8,128)(2,1)}, bf16[4,8,4096]{2,1,0:T(8,128)(2,1)S(1)}, u32[]{:S(2)}, u32[]{:S(2)}) collective-permute-start(bf16[4,8,4096]{2,1,0:T(8,128)(2,1)} %get-tuple-element.46), channel_id=1, source_target_pairs={{0,256},{1,257},{2,258},{3,259},{4,260},{5,261},{6,262},{7,263},{8... | collective-permute-start | bytes 786440 | tf_op jit(solution)/shard_map/ppermute | solution.py:24
  154.3 16.4 %collective-permute-start.18 = (bf16[4,8,4096]{2,1,0:T(8,128)(2,1)}, bf16[4,8,4096]{2,1,0:T(8,128)(2,1)S(1)}, u32[]{:S(2)}, u32[]{:S(2)}) collective-permute-start(bf16[4,8,4096]{2,1,0:T(8,128)(2,1)} %get-tuple-element.45), channel_id=1, source_target_pairs={{0,384},{1,385},{2,386},{3,387},{4,388},{5,389},{6,390},{7,391},{8... | collective-permute-start | bytes 786440 | tf_op jit(solution)/shard_map/ppermute | solution.py:24
  158.6 29.3 %all-to-all-start.2 = ((bf16[8,8,4096]{2,1,0:T(8,128)(2,1)}), bf16[8,8,4096]{2,1,0:T(8,128)(2,1)S(1)}, u32[]{:S(2)}, u32[]{:S(2)}) async-start(bf16[8,8,4096]{2,1,0:T(8,128)(2,1)} %fusion.6), calls=%async_computation.2 | async-start | bytes 1048576 | tf_op jit(solution)/shard_map/all_to_all | solution.py:208
  170.9 11.7 %collective-permute-start.19 = (bf16[8,4096]{1,0:T(8,128)(2,1)S(1)}, bf16[8,4096]{1,0:T(8,128)(2,1)S(1)}, u32[]{:S(2)}, u32[]{:S(2)}) collective-permute-start(bf16[8,4096]{1,0:T(8,128)(2,1)S(1)} %get-tuple-element.57), channel_id=1, source_target_pairs={{0,64},{1,65},{2,66},{3,67},{4,68},{5,69},{6,70},{7,71},{8,72},{9,... | collective-permute-start | bytes 196616 | tf_op jit(solution)/shard_map/ppermute | solution.py:24
  191.9 12.6 %collective-permute-start.25 = (bf16[8,8192]{1,0:T(8,128)(2,1)S(1)}, bf16[8,8192]{1,0:T(8,128)(2,1)S(1)}, u32[]{:S(2)}, u32[]{:S(2)}) collective-permute-start(bf16[8,8192]{1,0:T(8,128)(2,1)S(1)} %bitcast.165), channel_id=1, source_target_pairs={{0,96},{1,97},{2,98},{3,99},{4,100},{5,101},{6,102},{7,103},{8,104... | collective-permute-start | bytes 393224 | tf_op jit(solution)/shard_map/ppermute | solution.py:24
  195.5 12.2 %collective-permute-start.24 = (bf16[8,8192]{1,0:T(8,128)(2,1)S(1)}, bf16[8,8192]{1,0:T(8,128)(2,1)S(1)}, u32[]{:S(2)}, u32[]{:S(2)}) collective-permute-start(bf16[8,8192]{1,0:T(8,128)(2,1)S(1)} %bitcast.166), channel_id=1, source_target_pairs={{0,64},{1,65},{2,66},{3,67},{4,68},{5,69},{6,70},{7,71},{8,72},{9,... | collective-permute-start | bytes 393224 | tf_op jit(solution)/shard_map/ppermute | solution.py:24
  207.8 26.8 %collective-permute-start.28 = (bf16[4,8,8192]{2,1,0:T(8,128)(2,1)S(1)}, bf16[4,8,8192]{2,1,0:T(8,128)(2,1)S(1)}, u32[]{:S(2)}, u32[]{:S(2)}) collective-permute-start(bf16[4,8,8192]{2,1,0:T(8,128)(2,1)S(1)} %get-tuple-element.50), channel_id=1, source_target_pairs={{0,384},{1,385},{2,386},{3,387},{4,388},{5,389},{6,390},{7,391},{8... | collective-permute-start | bytes 1572872 | tf_op jit(solution)/shard_map/ppermute | solution.py:24
  211.4 23.3 %collective-permute-start.27 = (bf16[4,8,8192]{2,1,0:T(8,128)(2,1)S(1)}, bf16[4,8,8192]{2,1,0:T(8,128)(2,1)S(1)}, u32[]{:S(2)}, u32[]{:S(2)}) collective-permute-start(bf16[4,8,8192]{2,1,0:T(8,128)(2,1)S(1)} %get-tuple-element.50), channel_id=1, source_target_pairs={{0,256},{1,257},{2,258},{3,259},{4,260},{5,261},{6,262},{7,263},{8... | collective-permute-start | bytes 1572872 | tf_op jit(solution)/shard_map/ppermute | solution.py:24
  214.2 22.7 %collective-permute-start.26 = (bf16[4,8,8192]{2,1,0:T(8,128)(2,1)S(1)}, bf16[4,8,8192]{2,1,0:T(8,128)(2,1)S(1)}, u32[]{:S(2)}, u32[]{:S(2)}) collective-permute-start(bf16[4,8,8192]{2,1,0:T(8,128)(2,1)S(1)} %get-tuple-element.50), channel_id=1, source_target_pairs={{0,128},{1,129},{2,130},{3,131},{4,132},{5,133},{6,134},{7,135},{8... | collective-permute-start | bytes 1572872 | tf_op jit(solution)/shard_map/ppermute | solution.py:24
  (15 other events, 102.2 us)
Sparse Core Ops, SparseCore 0:
  92.4 37.2 all-gather.4
  136.4 68.0 all-gather.6

commit v13 on v12

--- a/solution.py
+++ b/solution.py
@@ -13,7 +13,10 @@
 DP = 32
 MP = 16
 Y = 8
+X = 4
 GROUPS = [list(range(Y)), list(range(Y, MP))]
+SAME_REST = [list(range(g, DP, DP // X)) for g in range(DP // X)]
+SAME_X = [list(range(x * DP // X, (x + 1) * DP // X)) for x in range(X)]
 ALONG_X = [(8,), (16,), (24,)]
 ALONG_Z = [(2,), (4,), (6,)]
 STRIDED_Z = [(4,), (0, 8), (4, 8)]
@@ -70,61 +73,63 @@
     )(order, *operands)
 
 
-def weight_kernel(last, grad_ref, columns_ref, *refs):
-    total_ref = refs[-1]
-    step = pl.program_id(0) * pl.num_programs(1) + pl.program_id(1)
-
-    @pl.when(step == 0)
-    def _():
-        total_ref[...] = jnp.zeros_like(total_ref)
-
-    quarters, devices, share, rows = columns_ref.shape
-    pieces = [columns_ref[:, d].reshape(quarters * share, rows) for d in range(devices)]
+def weight_kernel(grad_ref, columns_ref, *refs):
+    *before, out_ref = refs
+    slices, devices, share, rows = columns_ref.shape
+    half = slices // 2
+    pieces = [
+        columns_ref[half * view : half * (view + 1), d].reshape(half * share, rows)
+        for view in range(2)
+        for d in range(devices)
+    ]
     columns = jnp.concatenate(pieces, axis=0)
-    total_ref[...] += jnp.dot(grad_ref[...], columns, preferred_element_type=jnp.float32)
-
-    if last:
-        position_ref, own_ref, out_ref, placed_ref = refs[:4]
-        half = own_ref.shape[0]
-
-        @pl.when(step == pl.num_programs(0) * pl.num_programs(1) - 1)
-        def _():
-            placed_ref[:half] = own_ref[...]
-            placed_ref[half:] = total_ref[...]
-            blocks = [
-                placed_ref[pl.ds(pl.multiple_of(position_ref[block] * 8, 8), 8)] for block in range(DP)
-            ]
-            out_ref[...] = jnp.concatenate(blocks, axis=0).T
-
-
-def weight_half(grad, columns, position=None, own=None):
+    result = jnp.dot(grad_ref[...], columns, preferred_element_type=jnp.float32)
+    if before:
+        features = result.shape[0]
+        out_ref[0, :features] = before[0][0]
+        out_ref[0, features:] = result
+    else:
+        out_ref[0] = result
+
+
+def weight_half(grad, columns, before=()):
     half, depth = grad.shape
-    slices, devices, share, rows = columns.shape
-    quarters, group = slices // 2, 8
-    last = own is not None
-    in_specs = [
-        pl.BlockSpec((half, group * quarters * share), lambda v, d: (0, v * (devices // group) + d)),
-        pl.BlockSpec((quarters, group, share, rows), lambda v, d: (v, d, 0, 0)),
-    ]
-    scratch = [pltpu.VMEM((half, rows), jnp.float32)]
-    if last:
-        in_specs += [
-            pl.BlockSpec(memory_space=pltpu.SMEM),
-            pl.BlockSpec((half, rows), lambda v, d: (0, 0)),
+    slices, devices, share, wide = columns.shape
+    rows = wide // X
+    features = half * (len(before) + 1)
+    return pl.pallas_call(
+        weight_kernel,
+        grid=(X,),
+        in_specs=[
+            pl.BlockSpec((half, depth), lambda x: (0, 0)),
+            pl.BlockSpec((slices, devices, share, rows), lambda x: (0, 0, 0, x)),
         ]
-        scratch = [pltpu.VMEM((2 * half, rows), jnp.float32)] + scratch
-    return pl.pallas_call(
-        functools.partial(weight_kernel, last),
-        grid=(2, devices // group),
-        in_specs=in_specs,
-        out_specs=pl.BlockSpec((rows, 2 * half) if last else (half, rows), lambda v, d: (0, 0)),
-        out_shape=jax.ShapeDtypeStruct((rows, 2 * half) if last else (half, rows), jnp.float32),
-        scratch_shapes=scratch if last else [],
+        + [pl.BlockSpec((1, half, rows), lambda x: (x, 0, 0))] * len(before),
+        out_specs=pl.BlockSpec((1, features, rows), lambda x: (x, 0, 0)),
+        out_shape=jax.ShapeDtypeStruct((X, features, rows), jnp.float32),
         compiler_params=pltpu.CompilerParams(vmem_limit_bytes=32 * 1024 * 1024),
         cost_estimate=pl.CostEstimate(
-            flops=2 * half * depth * rows, bytes_accessed=6 * 1024 * 1024, transcendentals=0
+            flops=2 * half * depth * wide, bytes_accessed=5 * 1024 * 1024, transcendentals=0
         ),
-    )(grad, columns, *((position, own) if last else ()))
+    )(grad, columns, *before)
+
+
+def finish_kernel(position_ref, terms_ref, out_ref, total_ref):
+    total_ref[...] = (terms_ref[0] + terms_ref[1]) + (terms_ref[2] + terms_ref[3])
+    blocks = [total_ref[pl.ds(pl.multiple_of(position_ref[j] * 8, 8), 8)] for j in range(DP)]
+    out_ref[...] = jnp.concatenate(blocks, axis=0).T
+
+
+def finish(position, terms):
+    _, features, rows = terms.shape
+    return pl.pallas_call(
+        finish_kernel,
+        in_specs=[pl.BlockSpec(memory_space=pltpu.SMEM), pl.BlockSpec(memory_space=pltpu.VMEM)],
+        out_specs=pl.BlockSpec(memory_space=pltpu.VMEM),
+        out_shape=jax.ShapeDtypeStruct((rows, features), jnp.float32),
+        scratch_shapes=[pltpu.VMEM((features, rows), jnp.float32)],
+        compiler_params=pltpu.CompilerParams(vmem_limit_bytes=32 * 1024 * 1024),
+    )(position, terms)
 
 
 def per_device(inputs, weight):
@@ -141,11 +146,11 @@
     distance = (place >> 4) | ((place >> 2) & 3) << 3 | (place & 3) << 1
     order = data_index ^ distance
     relative = place ^ data_index
-    position = (relative & 1) << 4 | (relative >> 3) << 2 | ((relative >> 1) & 3)
+    position = (relative & 1) << 4 | ((relative >> 1) & 3) << 2 | (place >> 3)
 
     share = views * images // Y
     mine = lax.dynamic_slice_in_dim(flat, lax.rem(model_index, Y) * share, share, axis=0)
-    pieces = mine.reshape(share, DP, rows).transpose(1, 0, 2)
+    pieces = mine.reshape(share, X, DP // X, rows).transpose(2, 0, 1, 3).reshape(DP // X, share, X * rows)
     weight_own = gather(gather(weight, ALONG_Z)[0], ALONG_X)[0]
     weight_other = swap(weight_own, 1)
     half = (DP // 2, rows, feat)
@@ -165,7 +170,9 @@
     second = normed[1]
     pair = jnp.stack([second, partner(second)])
     first, pair, pieces = lax.optimization_barrier((normed[0], pair, pieces))
-    slices = lax.all_to_all(pieces, "dp", split_axis=0, concat_axis=0)
+    slices = lax.all_to_all(
+        pieces, "dp", split_axis=0, concat_axis=0, axis_index_groups=SAME_X
+    )
     columns_b = lax.all_gather(pair, "mp", axis=0, axis_index_groups=GROUPS)
     columns_b = columns_b.reshape(MP * block, total)
     rows_own = gather(gather(first, STRIDED_Z)[0], ALONG_X)[0]
@@ -219,12 +226,27 @@
     grad_mean = jnp.sum(grads, axis=2, keepdims=True) / total
     cross_mean = jnp.sum(grads * wide, axis=2, keepdims=True) / total
     grad_proj = ((grads - grad_mean - wide * cross_mean) * inverse).astype(jnp.bfloat16)
-    grad_proj = grad_proj.transpose(1, 0, 2).reshape(block, views * total)
-    along_z, columns = gather(grad_proj, ALONG_Z, columns)
-    grad_own = gather(along_z, ALONG_X)[0]
+    images_x = total // X
+    depth = views * images_x
+    grad_proj = jnp.stack(
+        [
+            jnp.concatenate(
+                [grad_proj[v, :, x * images_x : (x + 1) * images_x] for v in range(views)], axis=1
+            )
+            for x in range(X)
+        ]
+    )
+    grad_proj = lax.all_to_all(
+        grad_proj, "dp", split_axis=0, concat_axis=0, axis_index_groups=SAME_REST
+    )
+    grad_own, columns = gather(grad_proj, ALONG_Z, columns)
     grad_other = swap(grad_own, 1)
-    part = weight_half(grad_own.reshape(feat // 2, views * total), columns)
-    return weight_half(grad_other.reshape(feat // 2, views * total), columns, position, part)
+    terms = weight_half(grad_own.reshape(feat // 2, depth), columns)
+    terms = weight_half(grad_other.reshape(feat // 2, depth), columns, (terms,))
+    terms = lax.all_to_all(
+        terms, "dp", split_axis=0, concat_axis=0, axis_index_groups=SAME_REST
+    )
+    return finish(position, terms)
 
 
 def solution(mesh):

time: 257 us -> 259 us (level)
  waiting for transfers between devices: 95.4 us -> 87.1 us
  blocking collectives: 0 us -> 7.26 us
    ppermute x30 -> x27, waiting for transfers between devices: 77.1 us -> 57.8 us  [swap(): lax.ppermute(array, ('dp', 'mp'), [(i, i ^ mask) for i in range(DP * MP)])]
    all_to_all x1 -> x2, waiting for transfers between devices: 0.01 us -> 15.2 us  [the longest x1 15.2 us: per_device(): lax.all_to_all(terms, 'dp', split_axis=0, concat_axis=0, axis_index_group...]
    all_to_all x0 -> x1, blocking collectives: none -> 7.26 us  [per_device(): lax.all_to_all(grad_proj, 'dp', split_axis=0, concat_axis=0, axis_index_g...]
    all_gather x1, waiting for transfers between devices: 7.06 us -> 2.8 us  [per_device(): columns = lax.all_gather(slices, 'mp', axis=0, axis_index_groups=GROUPS)]
    ppermute x30 -> x27, starting transfers between devices: 102 us -> 99.2 us  [swap(): lax.ppermute(array, ('dp', 'mp'), [(i, i ^ mask) for i in range(DP * MP)])]
    all_to_all x1 -> x2, starting transfers between devices: 5.95 us -> 8.45 us  [the longest x1 4.93 us: per_device(): lax.all_to_all(pieces, 'dp', split_axis=0, concat_axis=0, axis_index_grou...]
    pallas_call x2 -> x3, Pallas kernels: 6.53 us -> 6.11 us  [the longest x2 4.67 us: weight_half(): pl.pallas_call(weight_kernel, grid=(X,), in_specs=[pl.BlockSpec((half, de...]
  transfers between devices with their start and end apart: 35 -> 33, of which waited for: 18 -> 19; matrix products, arithmetic and copies ran while one was open for 4% -> 4% of each run, Pallas kernels for 1% -> 1%
where the time goes in v13:
time: 259 us; the launch traced here: 258 us
  starting transfers between devices  119 us (46%)
  waiting for transfers between devices  87.1 us (34%)
  between operations  14 us (5%)
  Pallas kernels  10.5 us (4%)
  local copies, waits for them, and re-layouts  8.06 us (3%)
  blocking collectives  7.26 us (3%)
  matrix products  6.98 us (3%)
  other arithmetic  4.8 us (2%)
    ppermute x27, starting transfers between devices, swap(): lax.ppermute(array, ('dp', 'mp'), [(i, i ^ mask) for i in range(DP * MP)])  99.2 us
    ppermute x27, waiting for transfers between devices, swap(): lax.ppermute(array, ('dp', 'mp'), [(i, i ^ mask) for i in range(DP * MP)])  57.8 us
    all_to_all x1, waiting for transfers between devices, per_device(): lax.all_to_all(terms, 'dp', split_axis=0, concat_axis=0, axis_index_group...  15.2 us
    all_to_all x1, waiting for transfers between devices, per_device(): lax.all_to_all(projected.reshape(DP, block, views * images), 'dp', split_...  11.2 us
    all_to_all x1, blocking collectives, per_device(): lax.all_to_all(grad_proj, 'dp', split_axis=0, concat_axis=0, axis_index_g...  7.26 us
    all_to_all x1, starting transfers between devices, per_device(): lax.all_to_all(projected.reshape(DP, block, views * images), 'dp', split_...  6.98 us
  transfers between devices with their start and end apart: 33, of which 19 were waited for; matrix products, arithmetic and copies ran while one was open for 4% of the time, Pallas kernels for 1%

profile of v13, /device:TPU:1, one launch (start us, length us, event | category | flops | bytes accessed | tf_op | source)
XLA Modules:
  0.0 257.9 jit_solution(17024130008115723460)
XLA Ops:
  6.5 4.8 %collective-permute-start = (bf16[256,256]{1,0:T(8,128)(2,1)}, bf16[256,256]{1,0:T(8,128)(2,1)S(1)}, u32[]{:S(2)}, u32[]{:S(2)}) collective-permute-start(bf16[256,256]{1,0:T(8,128)(2,1)} %param.3), channel_id=1, source_target_pairs={{0,32},{1,33},{2,34},{3,35},{4,36},{5,37},{6,38},{7,39},{8,40},{9,... | collective-permute-start | bytes 393224 | tf_op jit(solution)/shard_map/ppermute | solution.py:27
  11.4 5.8 %collective-permute-start.1 = (bf16[256,256]{1,0:T(8,128)(2,1)}, bf16[256,256]{1,0:T(8,128)(2,1)S(1)}, u32[]{:S(2)}, u32[]{:S(2)}) collective-permute-start(bf16[256,256]{1,0:T(8,128)(2,1)} %param.3), channel_id=1, source_target_pairs={{0,64},{1,65},{2,66},{3,67},{4,68},{5,69},{6,70},{7,71},{8,72},{9,... | collective-permute-start | bytes 393224 | tf_op jit(solution)/shard_map/ppermute | solution.py:27
  21.1 4.9 %collective-permute-done.2 = bf16[256,256]{1,0:T(8,128)(2,1)S(1)} collective-permute-done((bf16[256,256]{1,0:T(8,128)(2,1)}, bf16[256,256]{1,0:T(8,128)(2,1)S(1)}, u32[]{:S(2)}, u32[]{:S(2)}) %collective-permute-start.2) | collective-permute-done | bytes 131104 | tf_op jit(solution)/shard_map/ppermute | solution.py:27
  29.1 4.4 %collective-permute-start.4 = (bf16[4,256,256]{2,1,0:T(8,128)(2,1)S(1)}, bf16[4,256,256]{2,1,0:T(8,128)(2,1)S(1)}, u32[]{:S(2)}, u32[]{:S(2)}) collective-permute-start(bf16[4,256,256]{2,1,0:T(8,128)(2,1)S(1)} %get-tuple-element.50), channel_id=1, source_target_pairs={{0,256},{1,257},{2,258},{3,259},{4,260},{5,261},{6,262},{7,263},{8... | collective-permute-start | bytes 1572872 | tf_op jit(solution)/shard_map/ppermute | solution.py:27
  39.7 12.1 %collective-permute-done.4 = bf16[4,256,256]{2,1,0:T(8,128)(2,1)S(1)} collective-permute-done((bf16[4,256,256]{2,1,0:T(8,128)(2,1)S(1)}, bf16[4,256,256]{2,1,0:T(8,128)(2,1)S(1)}, u32[]{:S(2)}, u32[]{:S(2)}) %collective-permute-start.4) | collective-permute-done | bytes 524320 | tf_op jit(solution)/shard_map/ppermute | solution.py:27
  51.9 7.2 %collective-permute-done.5 = bf16[4,256,256]{2,1,0:T(8,128)(2,1)S(1)} collective-permute-done((bf16[4,256,256]{2,1,0:T(8,128)(2,1)S(1)}, bf16[4,256,256]{2,1,0:T(8,128)(2,1)S(1)}, u32[]{:S(2)}, u32[]{:S(2)}) %collective-permute-start.5) | collective-permute-done | bytes 524320 | tf_op jit(solution)/shard_map/ppermute | solution.py:27
  59.4 5.0 %collective-permute-start.6 = (bf16[4,4,256,256]{3,2,1,0:T(8,128)(2,1)S(1)}, bf16[4,4,256,256]{3,2,1,0:T(8,128)(2,1)}, u32[]{:S(2)}, u32[]{:S(2)}) collective-permute-start(bf16[4,4,256,256]{3,2,1,0:T(8,128)(2,1)S(1)} %pad_maximum_fusion), channel_id=1, source_target_pairs={{0,16},{1,17},{2,18},{3,19},{4,20},{5,21},{6,22},{7,23},{8,24},{9,... | collective-permute-start | bytes 6291464 | tf_op jit(solution)/shard_map/ppermute | solution.py:27
  71.3 7.0 %all-to-all-start = ((f32[32,8,256]{2,1,0:T(8,128)}), f32[32,8,256]{2,1,0:T(8,128)S(1)}, u32[]{:S(2)}, u32[]{:S(2)}) async-start(f32[32,8,256]{2,1,0:T(8,128)} %bitcast.11), calls=%async_computation | async-start | bytes 524288 | tf_op jit(solution)/shard_map/all_to_all | solution.py:160
  78.4 11.2 %all-to-all-done = f32[32,8,256]{2,1,0:T(8,128)S(1)} async-done(((f32[32,8,256]{2,1,0:T(8,128)}), f32[32,8,256]{2,1,0:T(8,128)S(1)}, u32[]{:S(2)}, u32[]{:S(2)}) %all-to-all-start) | async-done | bytes 262176 | tf_op jit(solution)/shard_map/all_to_all | solution.py:160
  98.7 8.3 %collective-permute-start.9 = (bf16[8,4096]{1,0:T(8,128)(2,1)S(1)}, bf16[8,4096]{1,0:T(8,128)(2,1)S(1)}, u32[]{:S(2)}, u32[]{:S(2)}) collective-permute-start(bf16[8,4096]{1,0:T(8,128)(2,1)S(1)} %get-tuple-element.25), channel_id=1, source_target_pairs={{0,8},{1,9},{2,10},{3,11},{4,12},{5,13},{6,14},{7,15},{8,0},{9,1},... | collective-permute-start | bytes 196616 | tf_op jit(solution)/shard_map/ppermute | solution.py:27
  108.9 4.9 %all-to-all-start.1 = ((bf16[8,32,1024]{2,1,0:T(8,128)(2,1)}), bf16[8,32,1024]{2,1,0:T(8,128)(2,1)S(1)}, u32[]{:S(2)}, u32[]{:S(2)}) async-start(bf16[8,32,1024]{2,1,0:T(8,128)(2,1)} %reshape.103), calls=%async_computation.1 | async-start | bytes 1048576 | tf_op jit(solution)/shard_map/all_to_all | solution.py:173
  116.5 3.6 %collective-permute-start.12 = (bf16[4,8,4096]{2,1,0:T(8,128)(2,1)S(1)}, bf16[4,8,4096]{2,1,0:T(8,128)(2,1)S(1)}, u32[]{:S(2)}, u32[]{:S(2)}) collective-permute-start(bf16[4,8,4096]{2,1,0:T(8,128)(2,1)S(1)} %get-tuple-element.58), channel_id=1, source_target_pairs={{0,256},{1,257},{2,258},{3,259},{4,260},{5,261},{6,262},{7,263},{8... | collective-permute-start | bytes 786440 | tf_op jit(solution)/shard_map/ppermute | solution.py:27
  120.1 3.7 %collective-permute-start.13 = (bf16[4,8,4096]{2,1,0:T(8,128)(2,1)S(1)}, bf16[4,8,4096]{2,1,0:T(8,128)(2,1)S(1)}, u32[]{:S(2)}, u32[]{:S(2)}) collective-permute-start(bf16[4,8,4096]{2,1,0:T(8,128)(2,1)S(1)} %get-tuple-element.58), channel_id=1, source_target_pairs={{0,384},{1,385},{2,386},{3,387},{4,388},{5,389},{6,390},{7,391},{8... | collective-permute-start | bytes 786440 | tf_op jit(solution)/shard_map/ppermute | solution.py:27
  123.8 4.3 %collective-permute-done.12 = bf16[4,8,4096]{2,1,0:T(8,128)(2,1)S(1)} collective-permute-done((bf16[4,8,4096]{2,1,0:T(8,128)(2,1)S(1)}, bf16[4,8,4096]{2,1,0:T(8,128)(2,1)S(1)}, u32[]{:S(2)}, u32[]{:S(2)}) %collective-permute-start.12) | collective-permute-done | bytes 262176 | tf_op jit(solution)/shard_map/ppermute | solution.py:27
  128.1 6.3 %collective-permute-done.13 = bf16[4,8,4096]{2,1,0:T(8,128)(2,1)S(1)} collective-permute-done((bf16[4,8,4096]{2,1,0:T(8,128)(2,1)S(1)}, bf16[4,8,4096]{2,1,0:T(8,128)(2,1)S(1)}, u32[]{:S(2)}, u32[]{:S(2)}) %collective-permute-start.13) | collective-permute-done | bytes 262176 | tf_op jit(solution)/shard_map/ppermute | solution.py:27
  134.6 6.0 %collective-permute-start.14 = (bf16[4,4,8,4096]{3,2,1,0:T(8,128)(2,1)S(1)}, bf16[4,4,8,4096]{3,2,1,0:T(8,128)(2,1)S(1)}, u32[]{:S(2)}, u32[]{:S(2)}) collective-permute-start(bf16[4,4,8,4096]{3,2,1,0:T(8,128)(2,1)S(1)} %pad_maximum_fusion.1), channel_id=1, source_target_pairs={{0,16},{1,17},{2,18},{3,19},{4,20},{5,21},{6,22},{7,23},{8,24},{9,... | collective-permute-start | bytes 3145736 | tf_op jit(solution)/shard_map/ppermute | solution.py:27
  157.6 4.2 %collective-permute-start.17 = (bf16[4,8,4096]{2,1,0:T(8,128)(2,1)}, bf16[4,8,4096]{2,1,0:T(8,128)(2,1)S(1)}, u32[]{:S(2)}, u32[]{:S(2)}) collective-permute-start(bf16[4,8,4096]{2,1,0:T(8,128)(2,1)} %get-tuple-element.46), channel_id=1, source_target_pairs={{0,256},{1,257},{2,258},{3,259},{4,260},{5,261},{6,262},{7,263},{8... | collective-permute-start | bytes 786440 | tf_op jit(solution)/shard_map/ppermute | solution.py:27
  165.5 4.5 %all-to-all-start.2 = ((bf16[8,8,4096]{2,1,0:T(8,128)(2,1)}), bf16[8,8,4096]{2,1,0:T(8,128)(2,1)S(1)}, u32[]{:S(2)}, u32[]{:S(2)}) async-start(bf16[8,8,4096]{2,1,0:T(8,128)(2,1)} %fusion.6), calls=%async_computation.2 | async-start | bytes 1048576 | tf_op jit(solution)/shard_map/all_to_all | solution.py:215
  171.7 6.5 %collective-permute-done.18 = bf16[4,8,4096]{2,1,0:T(8,128)(2,1)S(1)} collective-permute-done((bf16[4,8,4096]{2,1,0:T(8,128)(2,1)}, bf16[4,8,4096]{2,1,0:T(8,128)(2,1)S(1)}, u32[]{:S(2)}, u32[]{:S(2)}) %collective-permute-start.18) | collective-permute-done | bytes 262176 | tf_op jit(solution)/shard_map/ppermute | solution.py:27
  178.3 4.5 %collective-permute-start.19 = (bf16[8,4096]{1,0:T(8,128)(2,1)S(1)}, bf16[8,4096]{1,0:T(8,128)(2,1)S(1)}, u32[]{:S(2)}, u32[]{:S(2)}) collective-permute-start(bf16[8,4096]{1,0:T(8,128)(2,1)S(1)} %get-tuple-element.55), channel_id=1, source_target_pairs={{0,64},{1,65},{2,66},{3,67},{4,68},{5,69},{6,70},{7,71},{8,72},{9,... | collective-permute-start | bytes 196616 | tf_op jit(solution)/shard_map/ppermute | solution.py:27
  182.8 5.0 %collective-permute-start.20 = (bf16[8,4096]{1,0:T(8,128)(2,1)S(1)}, bf16[8,4096]{1,0:T(8,128)(2,1)S(1)}, u32[]{:S(2)}, u32[]{:S(2)}) collective-permute-start(bf16[8,4096]{1,0:T(8,128)(2,1)S(1)} %get-tuple-element.54), channel_id=1, source_target_pairs={{0,8},{1,9},{2,10},{3,11},{4,12},{5,13},{6,14},{7,15},{8,0},{9,1},... | collective-permute-start | bytes 196616 | tf_op jit(solution)/shard_map/ppermute | solution.py:27
  195.7 7.3 %all_to_all.25 = bf16[4,8,2048]{2,1,0:T(8,128)(2,1)S(1)} all-to-all(bf16[4,8,2048]{2,1,0:T(8,128)(2,1)S(1)} %pad_maximum_fusion.7), channel_id=1, replica_groups={{0,128,256,384},{16,144,272,400},{32,160,288,416},{48,176,304,432},{64,..., dimensions={0} | all-to-all | bytes 262144 | tf_op jit(solution)/shard_map/all_to_all | solution.py:239
  218.1 5.9 %collective-permute-start.26 = (bf16[4,4,8,2048]{3,2,1,0:T(8,128)(2,1)S(1)}, bf16[4,4,8,2048]{3,2,1,0:T(8,128)(2,1)S(1)}, u32[]{:S(2)}, u32[]{:S(2)}) collective-permute-start(bf16[4,4,8,2048]{3,2,1,0:T(8,128)(2,1)S(1)} %pad_maximum_fusion.3), channel_id=1, source_target_pairs={{0,16},{1,17},{2,18},{3,19},{4,20},{5,21},{6,22},{7,23},{8,24},{9,... | collective-permute-start | bytes 1572872 | tf_op jit(solution)/shard_map/ppermute | solution.py:27
  234.4 15.2 %all-to-all-done.4.terms_ref = f32[4,256,256]{2,1,0:T(8,128)S(1)} async-done(((f32[4,256,256]{2,1,0:T(8,128)}), f32[4,256,256]{2,1,0:T(8,128)S(1)}, u32[]{:S(2)}, u32[]{:S(2)}) %all-to-all-start.4) | async-done | bytes 1048608 | tf_op jit(solution)/shard_map/all_to_all | solution.py:246
  (106 shorter events, 91.2 us)
Async XLA Ops:
  6.5 12.6 %collective-permute-start = (bf16[256,256]{1,0:T(8,128)(2,1)}, bf16[256,256]{1,0:T(8,128)(2,1)S(1)}, u32[]{:S(2)}, u32[]{:S(2)}) collective-permute-start(bf16[256,256]{1,0:T(8,128)(2,1)} %param.3), channel_id=1, source_target_pairs={{0,32},{1,33},{2,34},{3,35},{4,36},{5,37},{6,38},{7,39},{8,40},{9,... | collective-permute-start | bytes 393224 | tf_op jit(solution)/shard_map/ppermute | solution.py:27
  11.4 9.8 %collective-permute-start.1 = (bf16[256,256]{1,0:T(8,128)(2,1)}, bf16[256,256]{1,0:T(8,128)(2,1)S(1)}, u32[]{:S(2)}, u32[]{:S(2)}) collective-permute-start(bf16[256,256]{1,0:T(8,128)(2,1)} %param.3), channel_id=1, source_target_pairs={{0,64},{1,65},{2,66},{3,67},{4,68},{5,69},{6,70},{7,71},{8,72},{9,... | collective-permute-start | bytes 393224 | tf_op jit(solution)/shard_map/ppermute | solution.py:27
  27.1 12.7 %collective-permute-start.3 = (bf16[4,256,256]{2,1,0:T(8,128)(2,1)S(1)}, bf16[4,256,256]{2,1,0:T(8,128)(2,1)S(1)}, u32[]{:S(2)}, u32[]{:S(2)}) collective-permute-start(bf16[4,256,256]{2,1,0:T(8,128)(2,1)S(1)} %get-tuple-element.50), channel_id=1, source_target_pairs={{0,128},{1,129},{2,130},{3,131},{4,132},{5,133},{6,134},{7,135},{8... | collective-permute-start | bytes 1572872 | tf_op jit(solution)/shard_map/ppermute | solution.py:27
  29.1 22.7 %collective-permute-start.4 = (bf16[4,256,256]{2,1,0:T(8,128)(2,1)S(1)}, bf16[4,256,256]{2,1,0:T(8,128)(2,1)S(1)}, u32[]{:S(2)}, u32[]{:S(2)}) collective-permute-start(bf16[4,256,256]{2,1,0:T(8,128)(2,1)S(1)} %get-tuple-element.50), channel_id=1, source_target_pairs={{0,256},{1,257},{2,258},{3,259},{4,260},{5,261},{6,262},{7,263},{8... | collective-permute-start | bytes 1572872 | tf_op jit(solution)/shard_map/ppermute | solution.py:27
  33.5 25.6 %collective-permute-start.5 = (bf16[4,256,256]{2,1,0:T(8,128)(2,1)S(1)}, bf16[4,256,256]{2,1,0:T(8,128)(2,1)S(1)}, u32[]{:S(2)}, u32[]{:S(2)}) collective-permute-start(bf16[4,256,256]{2,1,0:T(8,128)(2,1)S(1)} %get-tuple-element.50), channel_id=1, source_target_pairs={{0,384},{1,385},{2,386},{3,387},{4,388},{5,389},{6,390},{7,391},{8... | collective-permute-start | bytes 1572872 | tf_op jit(solution)/shard_map/ppermute | solution.py:27
  71.3 18.3 %all-to-all-start = ((f32[32,8,256]{2,1,0:T(8,128)}), f32[32,8,256]{2,1,0:T(8,128)S(1)}, u32[]{:S(2)}, u32[]{:S(2)}) async-start(f32[32,8,256]{2,1,0:T(8,128)} %bitcast.11), calls=%async_computation | async-start | bytes 524288 | tf_op jit(solution)/shard_map/all_to_all | solution.py:160
  78.3 56.3 %all-gather.5.cloned.1.call-start = ((), (), s32[]{:S(2)}) async-start(), calls=%async_computation.5 | async-start | bytes 1179648 | tf_op jit(solution)/shard_map/all_gather | solution.py:176
  96.3 17.5 %collective-permute-start.8 = (bf16[8,4096]{1,0:T(8,128)(2,1)S(1)}, bf16[8,4096]{1,0:T(8,128)(2,1)S(1)}, u32[]{:S(2)}, u32[]{:S(2)}) collective-permute-start(bf16[8,4096]{1,0:T(8,128)(2,1)S(1)} %get-tuple-element.25), channel_id=1, source_target_pairs={{0,64},{1,65},{2,66},{3,67},{4,68},{5,69},{6,70},{7,71},{8,72},{9,... | collective-permute-start | bytes 196616 | tf_op jit(solution)/shard_map/ppermute | solution.py:27
  98.7 15.2 %collective-permute-start.9 = (bf16[8,4096]{1,0:T(8,128)(2,1)S(1)}, bf16[8,4096]{1,0:T(8,128)(2,1)S(1)}, u32[]{:S(2)}, u32[]{:S(2)}) collective-permute-start(bf16[8,4096]{1,0:T(8,128)(2,1)S(1)} %get-tuple-element.25), channel_id=1, source_target_pairs={{0,8},{1,9},{2,10},{3,11},{4,12},{5,13},{6,14},{7,15},{8,0},{9,1},... | collective-permute-start | bytes 196616 | tf_op jit(solution)/shard_map/ppermute | solution.py:27
  108.9 25.7 %all-to-all-start.1 = ((bf16[8,32,1024]{2,1,0:T(8,128)(2,1)}), bf16[8,32,1024]{2,1,0:T(8,128)(2,1)S(1)}, u32[]{:S(2)}, u32[]{:S(2)}) async-start(bf16[8,32,1024]{2,1,0:T(8,128)(2,1)} %reshape.103), calls=%async_computation.1 | async-start | bytes 1048576 | tf_op jit(solution)/shard_map/all_to_all | solution.py:173
  113.8 101.5 %all-gather.7.cloned.1.call-start = ((), (), s32[]{:S(2)}) async-start(), calls=%async_computation.6 | async-start | bytes 4718592 | tf_op jit(solution)/shard_map/all_gather | solution.py:180
  114.2 9.6 %collective-permute-start.11 = (bf16[4,8,4096]{2,1,0:T(8,128)(2,1)S(1)}, bf16[4,8,4096]{2,1,0:T(8,128)(2,1)S(1)}, u32[]{:S(2)}, u32[]{:S(2)}) collective-permute-start(bf16[4,8,4096]{2,1,0:T(8,128)(2,1)S(1)} %get-tuple-element.58), channel_id=1, source_target_pairs={{0,128},{1,129},{2,130},{3,131},{4,132},{5,133},{6,134},{7,135},{8... | collective-permute-start | bytes 786440 | tf_op jit(solution)/shard_map/ppermute | solution.py:27
  116.5 11.6 %collective-permute-start.12 = (bf16[4,8,4096]{2,1,0:T(8,128)(2,1)S(1)}, bf16[4,8,4096]{2,1,0:T(8,128)(2,1)S(1)}, u32[]{:S(2)}, u32[]{:S(2)}) collective-permute-start(bf16[4,8,4096]{2,1,0:T(8,128)(2,1)S(1)} %get-tuple-element.58), channel_id=1, source_target_pairs={{0,256},{1,257},{2,258},{3,259},{4,260},{5,261},{6,262},{7,263},{8... | collective-permute-start | bytes 786440 | tf_op jit(solution)/shard_map/ppermute | solution.py:27
  120.1 14.3 %collective-permute-start.13 = (bf16[4,8,4096]{2,1,0:T(8,128)(2,1)S(1)}, bf16[4,8,4096]{2,1,0:T(8,128)(2,1)S(1)}, u32[]{:S(2)}, u32[]{:S(2)}) collective-permute-start(bf16[4,8,4096]{2,1,0:T(8,128)(2,1)S(1)} %get-tuple-element.58), channel_id=1, source_target_pairs={{0,384},{1,385},{2,386},{3,387},{4,388},{5,389},{6,390},{7,391},{8... | collective-permute-start | bytes 786440 | tf_op jit(solution)/shard_map/ppermute | solution.py:27
  148.3 16.1 %collective-permute-start.22 = (bf16[64,4096]{1,0:T(8,128)(2,1)}, bf16[64,4096]{1,0:T(8,128)(2,1)S(1)}, u32[]{:S(2)}, u32[]{:S(2)}) collective-permute-start(bf16[64,4096]{1,0:T(8,128)(2,1)} %fusion.5), channel_id=1, source_target_pairs={{0,32},{1,33},{2,34},{3,35},{4,36},{5,37},{6,38},{7,39},{8,40},{9,... | collective-permute-start | bytes 1572872 | tf_op jit(solution)/shard_map/ppermute | solution.py:27
  154.5 15.6 %collective-permute-start.16 = (bf16[4,8,4096]{2,1,0:T(8,128)(2,1)}, bf16[4,8,4096]{2,1,0:T(8,128)(2,1)S(1)}, u32[]{:S(2)}, u32[]{:S(2)}) collective-permute-start(bf16[4,8,4096]{2,1,0:T(8,128)(2,1)} %get-tuple-element.47), channel_id=1, source_target_pairs={{0,128},{1,129},{2,130},{3,131},{4,132},{5,133},{6,134},{7,135},{8... | collective-permute-start | bytes 786440 | tf_op jit(solution)/shard_map/ppermute | solution.py:27
  157.6 14.1 %collective-permute-start.17 = (bf16[4,8,4096]{2,1,0:T(8,128)(2,1)}, bf16[4,8,4096]{2,1,0:T(8,128)(2,1)S(1)}, u32[]{:S(2)}, u32[]{:S(2)}) collective-permute-start(bf16[4,8,4096]{2,1,0:T(8,128)(2,1)} %get-tuple-element.46), channel_id=1, source_target_pairs={{0,256},{1,257},{2,258},{3,259},{4,260},{5,261},{6,262},{7,263},{8... | collective-permute-start | bytes 786440 | tf_op jit(solution)/shard_map/ppermute | solution.py:27
  161.8 16.4 %collective-permute-start.18 = (bf16[4,8,4096]{2,1,0:T(8,128)(2,1)}, bf16[4,8,4096]{2,1,0:T(8,128)(2,1)S(1)}, u32[]{:S(2)}, u32[]{:S(2)}) collective-permute-start(bf16[4,8,4096]{2,1,0:T(8,128)(2,1)} %get-tuple-element.45), channel_id=1, source_target_pairs={{0,384},{1,385},{2,386},{3,387},{4,388},{5,389},{6,390},{7,391},{8... | collective-permute-start | bytes 786440 | tf_op jit(solution)/shard_map/ppermute | solution.py:27
  165.5 29.5 %all-to-all-start.2 = ((bf16[8,8,4096]{2,1,0:T(8,128)(2,1)}), bf16[8,8,4096]{2,1,0:T(8,128)(2,1)S(1)}, u32[]{:S(2)}, u32[]{:S(2)}) async-start(bf16[8,8,4096]{2,1,0:T(8,128)(2,1)} %fusion.6), calls=%async_computation.2 | async-start | bytes 1048576 | tf_op jit(solution)/shard_map/all_to_all | solution.py:215
  178.3 11.6 %collective-permute-start.19 = (bf16[8,4096]{1,0:T(8,128)(2,1)S(1)}, bf16[8,4096]{1,0:T(8,128)(2,1)S(1)}, u32[]{:S(2)}, u32[]{:S(2)}) collective-permute-start(bf16[8,4096]{1,0:T(8,128)(2,1)S(1)} %get-tuple-element.55), channel_id=1, source_target_pairs={{0,64},{1,65},{2,66},{3,67},{4,68},{5,69},{6,70},{7,71},{8,72},{9,... | collective-permute-start | bytes 196616 | tf_op jit(solution)/shard_map/ppermute | solution.py:27
  182.8 9.2 %collective-permute-start.20 = (bf16[8,4096]{1,0:T(8,128)(2,1)S(1)}, bf16[8,4096]{1,0:T(8,128)(2,1)S(1)}, u32[]{:S(2)}, u32[]{:S(2)}) collective-permute-start(bf16[8,4096]{1,0:T(8,128)(2,1)S(1)} %get-tuple-element.54), channel_id=1, source_target_pairs={{0,8},{1,9},{2,10},{3,11},{4,12},{5,13},{6,14},{7,15},{8,0},{9,1},... | collective-permute-start | bytes 196616 | tf_op jit(solution)/shard_map/ppermute | solution.py:27
  203.0 9.5 %collective-permute-start.23 = (bf16[4,8,2048]{2,1,0:T(8,128)(2,1)S(1)}, bf16[4,8,2048]{2,1,0:T(8,128)(2,1)S(1)}, u32[]{:S(2)}, u32[]{:S(2)}) collective-permute-start(bf16[4,8,2048]{2,1,0:T(8,128)(2,1)S(1)} %all_to_all.25), channel_id=1, source_target_pairs={{0,32},{1,33},{2,34},{3,35},{4,36},{5,37},{6,38},{7,39},{8,40},{9,... | collective-permute-start | bytes 393224 | tf_op jit(solution)/shard_map/ppermute | solution.py:27
  218.1 9.9 %collective-permute-start.26 = (bf16[4,4,8,2048]{3,2,1,0:T(8,128)(2,1)S(1)}, bf16[4,4,8,2048]{3,2,1,0:T(8,128)(2,1)S(1)}, u32[]{:S(2)}, u32[]{:S(2)}) collective-permute-start(bf16[4,4,8,2048]{3,2,1,0:T(8,128)(2,1)S(1)} %pad_maximum_fusion.3), channel_id=1, source_target_pairs={{0,16},{1,17},{2,18},{3,19},{4,20},{5,21},{6,22},{7,23},{8,24},{9,... | collective-permute-start | bytes 1572872 | tf_op jit(solution)/shard_map/ppermute | solution.py:27
  230.9 18.7 %all-to-all-start.4 = ((f32[4,256,256]{2,1,0:T(8,128)}), f32[4,256,256]{2,1,0:T(8,128)S(1)}, u32[]{:S(2)}, u32[]{:S(2)}) async-start(f32[4,256,256]{2,1,0:T(8,128)} %shard_map.31), calls=%async_computation.4 | async-start | bytes 2097152 | tf_op jit(solution)/shard_map/all_to_all | solution.py:246
  (13 other events, 81.9 us)
Sparse Core Ops, SparseCore 0:
  96.5 37.6 all-gather.4
  148.4 66.8 all-gather.6

commit v14 on v13

--- a/solution.py
+++ b/solution.py
@@ -2,6 +2,7 @@
 
 import jax
 import jax.numpy as jnp
+import numpy as np
 from jax import lax
 from jax.experimental import pallas as pl
 from jax.experimental.pallas import tpu as pltpu
@@ -17,8 +18,10 @@
 GROUPS = [list(range(Y)), list(range(Y, MP))]
 SAME_REST = [list(range(g, DP, DP // X)) for g in range(DP // X)]
 SAME_X = [list(range(x * DP // X, (x + 1) * DP // X)) for x in range(X)]
-ALONG_X = [(8,), (16,), (24,)]
-ALONG_Z = [(2,), (4,), (6,)]
+X_SLOTS = np.array([0, 2, 1, 3])
+Z_SLOTS = np.array([0, 3, 2, 1])
+ALONG_X = [(8 * int(k),) for k in X_SLOTS[1:]]
+ALONG_Z = [(2 * int(k),) for k in Z_SLOTS[1:]]
 STRIDED_Z = [(4,), (0, 8), (4, 8)]
 
 
@@ -64,7 +67,7 @@
         + [pl.BlockSpec(memory_space=pltpu.VMEM)] * len(operands),
         out_specs=pl.BlockSpec(memory_space=pltpu.VMEM),
         out_shape=jax.ShapeDtypeStruct((rows, feat) if before is None else (feat, rows), jnp.float32),
-        compiler_params=pltpu.CompilerParams(vmem_limit_bytes=32 * 1024 * 1024),
+        compiler_params=pltpu.CompilerParams(vmem_limit_bytes=16 * 1024 * 1024),
         cost_estimate=pl.CostEstimate(
             flops=2 * rows * feat * weight.shape[0] * weight.shape[1],
             bytes_accessed=6 * 1024 * 1024,
@@ -107,7 +110,7 @@
         + [pl.BlockSpec((1, half, rows), lambda x: (x, 0, 0))] * len(before),
         out_specs=pl.BlockSpec((1, features, rows), lambda x: (x, 0, 0)),
         out_shape=jax.ShapeDtypeStruct((X, features, rows), jnp.float32),
-        compiler_params=pltpu.CompilerParams(vmem_limit_bytes=32 * 1024 * 1024),
+        compiler_params=pltpu.CompilerParams(vmem_limit_bytes=16 * 1024 * 1024),
         cost_estimate=pl.CostEstimate(
             flops=2 * half * depth * wide, bytes_accessed=5 * 1024 * 1024, transcendentals=0
         ),
@@ -128,7 +131,7 @@
         out_specs=pl.BlockSpec(memory_space=pltpu.VMEM),
         out_shape=jax.ShapeDtypeStruct((rows, features), jnp.float32),
         scratch_shapes=[pltpu.VMEM((features, rows), jnp.float32)],
-        compiler_params=pltpu.CompilerParams(vmem_limit_bytes=32 * 1024 * 1024),
+        compiler_params=pltpu.CompilerParams(vmem_limit_bytes=16 * 1024 * 1024),
     )(position, terms)
 
 
@@ -142,11 +145,12 @@
     rows = width // DP
     flat = inputs.reshape(views * images, width)
 
-    place = jnp.arange(DP, dtype=jnp.int32)
-    distance = (place >> 4) | ((place >> 2) & 3) << 3 | (place & 3) << 1
-    order = data_index ^ distance
-    relative = place ^ data_index
-    position = (relative & 1) << 4 | ((relative >> 1) & 3) << 2 | (place >> 3)
+    place = np.arange(DP)
+    distance = place >> 4 | X_SLOTS[place >> 2 & 3] << 3 | Z_SLOTS[place & 3] << 1
+    order = data_index ^ jnp.asarray(distance, jnp.int32)
+    relative = data_index ^ jnp.asarray(place, jnp.int32)
+    slot = (4 - (relative >> 1 & 3)) & 3
+    position = (relative & 1) << 4 | slot << 2 | jnp.asarray(place >> 3, jnp.int32)
 
     share = views * images // Y
     mine = lax.dynamic_slice_in_dim(flat, lax.rem(model_index, Y) * share, share, axis=0)

time: 259 us -> 251 us (0.969)
  starting transfers between devices: 119 us -> 114 us
  waiting for transfers between devices: 87.1 us -> 82.8 us
    ppermute x27, waiting for transfers between devices: 57.8 us -> 45.8 us  [swap(): lax.ppermute(array, ('dp', 'mp'), [(i, i ^ mask) for i in range(DP * MP)])]
    ppermute x27, starting transfers between devices: 99.2 us -> 95.3 us  [swap(): lax.ppermute(array, ('dp', 'mp'), [(i, i ^ mask) for i in range(DP * MP)])]
    all_to_all x1, waiting for transfers between devices: 0.01 us -> 3.35 us  [per_device(): lax.all_to_all(terms_b.reshape(Y, block, total), 'mp', split_axis=0, conc...]
    all_gather x1, waiting for transfers between devices: 0.02 us -> 3.06 us  [per_device(): columns_b = lax.all_gather(pair, 'mp', axis=0, axis_index_groups=GROUPS)]
  transfers between devices with their start and end apart: 33 -> 33, of which waited for: 19 -> 20; matrix products, arithmetic and copies ran while one was open for 4% -> 4% of each run, Pallas kernels for 1% -> 1%
where the time goes in v14:
time: 251 us; the launch traced here: 250 us
  starting transfers between devices  114 us (45%)
  waiting for transfers between devices  82.8 us (33%)
  between operations  14 us (6%)
  Pallas kernels  10.5 us (4%)
  blocking collectives  8.46 us (3%)
  local copies, waits for them, and re-layouts  8.02 us (3%)
  matrix products  6.95 us (3%)
  other arithmetic  4.8 us (2%)
    ppermute x27, starting transfers between devices, swap(): lax.ppermute(array, ('dp', 'mp'), [(i, i ^ mask) for i in range(DP * MP)])  95.3 us
    ppermute x27, waiting for transfers between devices, swap(): lax.ppermute(array, ('dp', 'mp'), [(i, i ^ mask) for i in range(DP * MP)])  45.8 us
    all_to_all x1, waiting for transfers between devices, per_device(): lax.all_to_all(terms, 'dp', split_axis=0, concat_axis=0, axis_index_group...  15.2 us
    all_to_all x1, waiting for transfers between devices, per_device(): lax.all_to_all(projected.reshape(DP, block, views * images), 'dp', split_...  11.2 us
    all_to_all x1, blocking collectives, per_device(): lax.all_to_all(grad_proj, 'dp', split_axis=0, concat_axis=0, axis_index_g...  8.46 us
    all_to_all x1, starting transfers between devices, per_device(): lax.all_to_all(projected.reshape(DP, block, views * images), 'dp', split_...  6.39 us
  transfers between devices with their start and end apart: 33, of which 20 were waited for; matrix products, arithmetic and copies ran while one was open for 4% of the time, Pallas kernels for 1%

profile of v14, /device:TPU:1, one launch (start us, length us, event | category | flops | bytes accessed | tf_op | source)
XLA Modules:
  0.0 250.0 jit_solution(6226234179037782929)
XLA Ops:
  6.5 8.4 %collective-permute-start = (bf16[256,256]{1,0:T(8,128)(2,1)}, bf16[256,256]{1,0:T(8,128)(2,1)S(1)}, u32[]{:S(2)}, u32[]{:S(2)}) collective-permute-start(bf16[256,256]{1,0:T(8,128)(2,1)} %param.6), channel_id=1, source_target_pairs={{0,96},{1,97},{2,98},{3,99},{4,100},{5,101},{6,102},{7,103},{8,104... | collective-permute-start | bytes 393224 | tf_op jit(solution)/shard_map/ppermute | solution.py:30
  19.1 6.7 %collective-permute-done.1 = bf16[256,256]{1,0:T(8,128)(2,1)S(1)} collective-permute-done((bf16[256,256]{1,0:T(8,128)(2,1)}, bf16[256,256]{1,0:T(8,128)(2,1)S(1)}, u32[]{:S(2)}, u32[]{:S(2)}) %collective-permute-start.1) | collective-permute-done | bytes 131104 | tf_op jit(solution)/shard_map/ppermute | solution.py:30
  26.9 5.1 %collective-permute-start.3 = (bf16[4,256,256]{2,1,0:T(8,128)(2,1)S(1)}, bf16[4,256,256]{2,1,0:T(8,128)(2,1)S(1)}, u32[]{:S(2)}, u32[]{:S(2)}) collective-permute-start(bf16[4,256,256]{2,1,0:T(8,128)(2,1)S(1)} %get-tuple-element.50), channel_id=1, source_target_pairs={{0,256},{1,257},{2,258},{3,259},{4,260},{5,261},{6,262},{7,263},{8... | collective-permute-start | bytes 1572872 | tf_op jit(solution)/shard_map/ppermute | solution.py:30
  36.7 5.5 %collective-permute-done.3 = bf16[4,256,256]{2,1,0:T(8,128)(2,1)S(1)} collective-permute-done((bf16[4,256,256]{2,1,0:T(8,128)(2,1)S(1)}, bf16[4,256,256]{2,1,0:T(8,128)(2,1)S(1)}, u32[]{:S(2)}, u32[]{:S(2)}) %collective-permute-start.3) | collective-permute-done | bytes 524320 | tf_op jit(solution)/shard_map/ppermute | solution.py:30
  42.2 11.9 %collective-permute-done.4 = bf16[4,256,256]{2,1,0:T(8,128)(2,1)S(1)} collective-permute-done((bf16[4,256,256]{2,1,0:T(8,128)(2,1)S(1)}, bf16[4,256,256]{2,1,0:T(8,128)(2,1)S(1)}, u32[]{:S(2)}, u32[]{:S(2)}) %collective-permute-start.4) | collective-permute-done | bytes 524320 | tf_op jit(solution)/shard_map/ppermute | solution.py:30
  65.6 6.4 %all-to-all-start = ((f32[32,8,256]{2,1,0:T(8,128)}), f32[32,8,256]{2,1,0:T(8,128)S(1)}, u32[]{:S(2)}, u32[]{:S(2)}) async-start(f32[32,8,256]{2,1,0:T(8,128)} %bitcast.11), calls=%async_computation | async-start | bytes 524288 | tf_op jit(solution)/shard_map/all_to_all | solution.py:164
  72.1 11.2 %all-to-all-done = f32[32,8,256]{2,1,0:T(8,128)S(1)} async-done(((f32[32,8,256]{2,1,0:T(8,128)}), f32[32,8,256]{2,1,0:T(8,128)S(1)}, u32[]{:S(2)}, u32[]{:S(2)}) %all-to-all-start) | async-done | bytes 262176 | tf_op jit(solution)/shard_map/all_to_all | solution.py:164
  92.3 7.9 %collective-permute-start.9 = (bf16[8,4096]{1,0:T(8,128)(2,1)S(1)}, bf16[8,4096]{1,0:T(8,128)(2,1)S(1)}, u32[]{:S(2)}, u32[]{:S(2)}) collective-permute-start(bf16[8,4096]{1,0:T(8,128)(2,1)S(1)} %get-tuple-element.25), channel_id=1, source_target_pairs={{0,8},{1,9},{2,10},{3,11},{4,12},{5,13},{6,14},{7,15},{8,0},{9,1},... | collective-permute-start | bytes 196616 | tf_op jit(solution)/shard_map/ppermute | solution.py:30
  102.2 4.9 %all-to-all-start.1 = ((bf16[8,32,1024]{2,1,0:T(8,128)(2,1)}), bf16[8,32,1024]{2,1,0:T(8,128)(2,1)S(1)}, u32[]{:S(2)}, u32[]{:S(2)}) async-start(bf16[8,32,1024]{2,1,0:T(8,128)(2,1)} %reshape.103), calls=%async_computation.1 | async-start | bytes 1048576 | tf_op jit(solution)/shard_map/all_to_all | solution.py:177
  112.8 3.7 %collective-permute-start.13 = (bf16[4,8,4096]{2,1,0:T(8,128)(2,1)S(1)}, bf16[4,8,4096]{2,1,0:T(8,128)(2,1)S(1)}, u32[]{:S(2)}, u32[]{:S(2)}) collective-permute-start(bf16[4,8,4096]{2,1,0:T(8,128)(2,1)S(1)} %get-tuple-element.58), channel_id=1, source_target_pairs={{0,384},{1,385},{2,386},{3,387},{4,388},{5,389},{6,390},{7,391},{8... | collective-permute-start | bytes 786440 | tf_op jit(solution)/shard_map/ppermute | solution.py:30
  116.6 4.1 %collective-permute-done.12 = bf16[4,8,4096]{2,1,0:T(8,128)(2,1)S(1)} collective-permute-done((bf16[4,8,4096]{2,1,0:T(8,128)(2,1)S(1)}, bf16[4,8,4096]{2,1,0:T(8,128)(2,1)S(1)}, u32[]{:S(2)}, u32[]{:S(2)}) %collective-permute-start.12) | collective-permute-done | bytes 262176 | tf_op jit(solution)/shard_map/ppermute | solution.py:30
  120.6 3.6 %collective-permute-done.13 = bf16[4,8,4096]{2,1,0:T(8,128)(2,1)S(1)} collective-permute-done((bf16[4,8,4096]{2,1,0:T(8,128)(2,1)S(1)}, bf16[4,8,4096]{2,1,0:T(8,128)(2,1)S(1)}, u32[]{:S(2)}, u32[]{:S(2)}) %collective-permute-start.13) | collective-permute-done | bytes 262176 | tf_op jit(solution)/shard_map/ppermute | solution.py:30
  127.5 6.5 %collective-permute-start.14 = (bf16[4,4,8,4096]{3,2,1,0:T(8,128)(2,1)S(1)}, bf16[4,4,8,4096]{3,2,1,0:T(8,128)(2,1)S(1)}, u32[]{:S(2)}, u32[]{:S(2)}) collective-permute-start(bf16[4,4,8,4096]{3,2,1,0:T(8,128)(2,1)S(1)} %pad_maximum_fusion.1), channel_id=1, source_target_pairs={{0,16},{1,17},{2,18},{3,19},{4,20},{5,21},{6,22},{7,23},{8,24},{9,... | collective-permute-start | bytes 3145736 | tf_op jit(solution)/shard_map/ppermute | solution.py:30
  147.7 4.6 %collective-permute-start.16 = (bf16[4,8,4096]{2,1,0:T(8,128)(2,1)}, bf16[4,8,4096]{2,1,0:T(8,128)(2,1)S(1)}, u32[]{:S(2)}, u32[]{:S(2)}) collective-permute-start(bf16[4,8,4096]{2,1,0:T(8,128)(2,1)} %get-tuple-element.47), channel_id=1, source_target_pairs={{0,256},{1,257},{2,258},{3,259},{4,260},{5,261},{6,262},{7,263},{8... | collective-permute-start | bytes 786440 | tf_op jit(solution)/shard_map/ppermute | solution.py:30
  158.6 4.1 %all-to-all-start.2 = ((bf16[8,8,4096]{2,1,0:T(8,128)(2,1)}), bf16[8,8,4096]{2,1,0:T(8,128)(2,1)S(1)}, u32[]{:S(2)}, u32[]{:S(2)}) async-start(bf16[8,8,4096]{2,1,0:T(8,128)(2,1)} %fusion.6), calls=%async_computation.2 | async-start | bytes 1048576 | tf_op jit(solution)/shard_map/all_to_all | solution.py:219
  164.9 4.6 %collective-permute-start.19 = (bf16[8,4096]{1,0:T(8,128)(2,1)S(1)}, bf16[8,4096]{1,0:T(8,128)(2,1)S(1)}, u32[]{:S(2)}, u32[]{:S(2)}) collective-permute-start(bf16[8,4096]{1,0:T(8,128)(2,1)S(1)} %get-tuple-element.55), channel_id=1, source_target_pairs={{0,64},{1,65},{2,66},{3,67},{4,68},{5,69},{6,70},{7,71},{8,72},{9,... | collective-permute-start | bytes 196616 | tf_op jit(solution)/shard_map/ppermute | solution.py:30
  169.5 5.0 %collective-permute-start.20 = (bf16[8,4096]{1,0:T(8,128)(2,1)S(1)}, bf16[8,4096]{1,0:T(8,128)(2,1)S(1)}, u32[]{:S(2)}, u32[]{:S(2)}) collective-permute-start(bf16[8,4096]{1,0:T(8,128)(2,1)S(1)} %get-tuple-element.54), channel_id=1, source_target_pairs={{0,8},{1,9},{2,10},{3,11},{4,12},{5,13},{6,14},{7,15},{8,0},{9,1},... | collective-permute-start | bytes 196616 | tf_op jit(solution)/shard_map/ppermute | solution.py:30
  178.4 3.7 %collective-permute-done.21 = bf16[8,4096]{1,0:T(8,128)(2,1)S(1)} collective-permute-done((bf16[8,4096]{1,0:T(8,128)(2,1)S(1)}, bf16[8,4096]{1,0:T(8,128)(2,1)S(1)}, u32[]{:S(2)}, u32[]{:S(2)}) %collective-permute-start.21) | collective-permute-done | bytes 65568 | tf_op jit(solution)/shard_map/ppermute | solution.py:30
  186.2 8.5 %all_to_all.25 = bf16[4,8,2048]{2,1,0:T(8,128)(2,1)S(1)} all-to-all(bf16[4,8,2048]{2,1,0:T(8,128)(2,1)S(1)} %pad_maximum_fusion.7), channel_id=1, replica_groups={{0,128,256,384},{16,144,272,400},{32,160,288,416},{48,176,304,432},{64,..., dimensions={0} | all-to-all | bytes 262144 | tf_op jit(solution)/shard_map/all_to_all | solution.py:243
  194.6 5.6 %collective-permute-start.23 = (bf16[4,8,2048]{2,1,0:T(8,128)(2,1)S(1)}, bf16[4,8,2048]{2,1,0:T(8,128)(2,1)S(1)}, u32[]{:S(2)}, u32[]{:S(2)}) collective-permute-start(bf16[4,8,2048]{2,1,0:T(8,128)(2,1)S(1)} %all_to_all.25), channel_id=1, source_target_pairs={{0,96},{1,97},{2,98},{3,99},{4,100},{5,101},{6,102},{7,103},{8,104... | collective-permute-start | bytes 393224 | tf_op jit(solution)/shard_map/ppermute | solution.py:30
  204.4 4.2 %all-gather.7.cloned.1.call-done = bf16[64,32,1024]{2,1,0:T(8,128)(2,1)} async-done(((bf16[8,32,1024]{2,1,0:T(8,128)(2,1)}), bf16[64,32,1024]{2,1,0:T(8,128)(2,1)}) %all-gather.7.cloned.1.call-update) | async-done | bytes 4194320 | tf_op jit(solution)/shard_map/all_gather | solution.py:184
  211.6 4.3 %collective-permute-start.26 = (bf16[4,4,8,2048]{3,2,1,0:T(8,128)(2,1)S(1)}, bf16[4,4,8,2048]{3,2,1,0:T(8,128)(2,1)S(1)}, u32[]{:S(2)}, u32[]{:S(2)}) collective-permute-start(bf16[4,4,8,2048]{3,2,1,0:T(8,128)(2,1)S(1)} %pad_maximum_fusion.3), channel_id=1, source_target_pairs={{0,16},{1,17},{2,18},{3,19},{4,20},{5,21},{6,22},{7,23},{8,24},{9,... | collective-permute-start | bytes 1572872 | tf_op jit(solution)/shard_map/ppermute | solution.py:30
  222.8 3.6 %all-to-all-start.4 = ((f32[4,256,256]{2,1,0:T(8,128)}), f32[4,256,256]{2,1,0:T(8,128)S(1)}, u32[]{:S(2)}, u32[]{:S(2)}) async-start(f32[4,256,256]{2,1,0:T(8,128)} %shard_map.58), calls=%async_computation.4 | async-start | bytes 2097152 | tf_op jit(solution)/shard_map/all_to_all | solution.py:250
  226.5 15.2 %all-to-all-done.4.terms_ref = f32[4,256,256]{2,1,0:T(8,128)S(1)} async-done(((f32[4,256,256]{2,1,0:T(8,128)}), f32[4,256,256]{2,1,0:T(8,128)S(1)}, u32[]{:S(2)}, u32[]{:S(2)}) %all-to-all-start.4) | async-done | bytes 1048608 | tf_op jit(solution)/shard_map/all_to_all | solution.py:250
  (110 shorter events, 86.4 us)
Async XLA Ops:
  6.5 12.6 %collective-permute-start = (bf16[256,256]{1,0:T(8,128)(2,1)}, bf16[256,256]{1,0:T(8,128)(2,1)S(1)}, u32[]{:S(2)}, u32[]{:S(2)}) collective-permute-start(bf16[256,256]{1,0:T(8,128)(2,1)} %param.6), channel_id=1, source_target_pairs={{0,96},{1,97},{2,98},{3,99},{4,100},{5,101},{6,102},{7,103},{8,104... | collective-permute-start | bytes 393224 | tf_op jit(solution)/shard_map/ppermute | solution.py:30
  15.0 10.9 %collective-permute-start.1 = (bf16[256,256]{1,0:T(8,128)(2,1)}, bf16[256,256]{1,0:T(8,128)(2,1)S(1)}, u32[]{:S(2)}, u32[]{:S(2)}) collective-permute-start(bf16[256,256]{1,0:T(8,128)(2,1)} %param.6), channel_id=1, source_target_pairs={{0,64},{1,65},{2,66},{3,67},{4,68},{5,69},{6,70},{7,71},{8,72},{9,... | collective-permute-start | bytes 393224 | tf_op jit(solution)/shard_map/ppermute | solution.py:30
  26.9 15.3 %collective-permute-start.3 = (bf16[4,256,256]{2,1,0:T(8,128)(2,1)S(1)}, bf16[4,256,256]{2,1,0:T(8,128)(2,1)S(1)}, u32[]{:S(2)}, u32[]{:S(2)}) collective-permute-start(bf16[4,256,256]{2,1,0:T(8,128)(2,1)S(1)} %get-tuple-element.50), channel_id=1, source_target_pairs={{0,256},{1,257},{2,258},{3,259},{4,260},{5,261},{6,262},{7,263},{8... | collective-permute-start | bytes 1572872 | tf_op jit(solution)/shard_map/ppermute | solution.py:30
  32.0 22.1 %collective-permute-start.4 = (bf16[4,256,256]{2,1,0:T(8,128)(2,1)S(1)}, bf16[4,256,256]{2,1,0:T(8,128)(2,1)S(1)}, u32[]{:S(2)}, u32[]{:S(2)}) collective-permute-start(bf16[4,256,256]{2,1,0:T(8,128)(2,1)S(1)} %get-tuple-element.50), channel_id=1, source_target_pairs={{0,128},{1,129},{2,130},{3,131},{4,132},{5,133},{6,134},{7,135},{8... | collective-permute-start | bytes 1572872 | tf_op jit(solution)/shard_map/ppermute | solution.py:30
  34.2 21.3 %collective-permute-start.5 = (bf16[4,256,256]{2,1,0:T(8,128)(2,1)S(1)}, bf16[4,256,256]{2,1,0:T(8,128)(2,1)S(1)}, u32[]{:S(2)}, u32[]{:S(2)}) collective-permute-start(bf16[4,256,256]{2,1,0:T(8,128)(2,1)S(1)} %get-tuple-element.50), channel_id=1, source_target_pairs={{0,384},{1,385},{2,386},{3,387},{4,388},{5,389},{6,390},{7,391},{8... | collective-permute-start | bytes 1572872 | tf_op jit(solution)/shard_map/ppermute | solution.py:30
  65.6 17.7 %all-to-all-start = ((f32[32,8,256]{2,1,0:T(8,128)}), f32[32,8,256]{2,1,0:T(8,128)S(1)}, u32[]{:S(2)}, u32[]{:S(2)}) async-start(f32[32,8,256]{2,1,0:T(8,128)} %bitcast.11), calls=%async_computation | async-start | bytes 524288 | tf_op jit(solution)/shard_map/all_to_all | solution.py:164
  72.0 55.5 %all-gather.5.cloned.1.call-start = ((), (), s32[]{:S(2)}) async-start(), calls=%async_computation.5 | async-start | bytes 1179648 | tf_op jit(solution)/shard_map/all_gather | solution.py:180
  90.0 17.1 %collective-permute-start.8 = (bf16[8,4096]{1,0:T(8,128)(2,1)S(1)}, bf16[8,4096]{1,0:T(8,128)(2,1)S(1)}, u32[]{:S(2)}, u32[]{:S(2)}) collective-permute-start(bf16[8,4096]{1,0:T(8,128)(2,1)S(1)} %get-tuple-element.25), channel_id=1, source_target_pairs={{0,64},{1,65},{2,66},{3,67},{4,68},{5,69},{6,70},{7,71},{8,72},{9,... | collective-permute-start | bytes 196616 | tf_op jit(solution)/shard_map/ppermute | solution.py:30
  92.3 14.8 %collective-permute-start.9 = (bf16[8,4096]{1,0:T(8,128)(2,1)S(1)}, bf16[8,4096]{1,0:T(8,128)(2,1)S(1)}, u32[]{:S(2)}, u32[]{:S(2)}) collective-permute-start(bf16[8,4096]{1,0:T(8,128)(2,1)S(1)} %get-tuple-element.25), channel_id=1, source_target_pairs={{0,8},{1,9},{2,10},{3,11},{4,12},{5,13},{6,14},{7,15},{8,0},{9,1},... | collective-permute-start | bytes 196616 | tf_op jit(solution)/shard_map/ppermute | solution.py:30
  102.2 22.2 %all-to-all-start.1 = ((bf16[8,32,1024]{2,1,0:T(8,128)(2,1)}), bf16[8,32,1024]{2,1,0:T(8,128)(2,1)S(1)}, u32[]{:S(2)}, u32[]{:S(2)}) async-start(bf16[8,32,1024]{2,1,0:T(8,128)(2,1)} %reshape.103), calls=%async_computation.1 | async-start | bytes 1048576 | tf_op jit(solution)/shard_map/all_to_all | solution.py:177
  107.2 101.4 %all-gather.7.cloned.1.call-start = ((), (), s32[]{:S(2)}) async-start(), calls=%async_computation.6 | async-start | bytes 4718592 | tf_op jit(solution)/shard_map/all_gather | solution.py:184
  107.5 9.0 %collective-permute-start.11 = (bf16[4,8,4096]{2,1,0:T(8,128)(2,1)S(1)}, bf16[4,8,4096]{2,1,0:T(8,128)(2,1)S(1)}, u32[]{:S(2)}, u32[]{:S(2)}) collective-permute-start(bf16[4,8,4096]{2,1,0:T(8,128)(2,1)S(1)} %get-tuple-element.58), channel_id=1, source_target_pairs={{0,256},{1,257},{2,258},{3,259},{4,260},{5,261},{6,262},{7,263},{8... | collective-permute-start | bytes 786440 | tf_op jit(solution)/shard_map/ppermute | solution.py:30
  110.3 10.4 %collective-permute-start.12 = (bf16[4,8,4096]{2,1,0:T(8,128)(2,1)S(1)}, bf16[4,8,4096]{2,1,0:T(8,128)(2,1)S(1)}, u32[]{:S(2)}, u32[]{:S(2)}) collective-permute-start(bf16[4,8,4096]{2,1,0:T(8,128)(2,1)S(1)} %get-tuple-element.58), channel_id=1, source_target_pairs={{0,128},{1,129},{2,130},{3,131},{4,132},{5,133},{6,134},{7,135},{8... | collective-permute-start | bytes 786440 | tf_op jit(solution)/shard_map/ppermute | solution.py:30
  112.8 11.4 %collective-permute-start.13 = (bf16[4,8,4096]{2,1,0:T(8,128)(2,1)S(1)}, bf16[4,8,4096]{2,1,0:T(8,128)(2,1)S(1)}, u32[]{:S(2)}, u32[]{:S(2)}) collective-permute-start(bf16[4,8,4096]{2,1,0:T(8,128)(2,1)S(1)} %get-tuple-element.58), channel_id=1, source_target_pairs={{0,384},{1,385},{2,386},{3,387},{4,388},{5,389},{6,390},{7,391},{8... | collective-permute-start | bytes 786440 | tf_op jit(solution)/shard_map/ppermute | solution.py:30
  141.6 15.8 %collective-permute-start.22 = (bf16[64,4096]{1,0:T(8,128)(2,1)}, bf16[64,4096]{1,0:T(8,128)(2,1)S(1)}, u32[]{:S(2)}, u32[]{:S(2)}) collective-permute-start(bf16[64,4096]{1,0:T(8,128)(2,1)} %fusion.5), channel_id=1, source_target_pairs={{0,32},{1,33},{2,34},{3,35},{4,36},{5,37},{6,38},{7,39},{8,40},{9,... | collective-permute-start | bytes 1572872 | tf_op jit(solution)/shard_map/ppermute | solution.py:30
  147.7 14.9 %collective-permute-start.16 = (bf16[4,8,4096]{2,1,0:T(8,128)(2,1)}, bf16[4,8,4096]{2,1,0:T(8,128)(2,1)S(1)}, u32[]{:S(2)}, u32[]{:S(2)}) collective-permute-start(bf16[4,8,4096]{2,1,0:T(8,128)(2,1)} %get-tuple-element.47), channel_id=1, source_target_pairs={{0,256},{1,257},{2,258},{3,259},{4,260},{5,261},{6,262},{7,263},{8... | collective-permute-start | bytes 786440 | tf_op jit(solution)/shard_map/ppermute | solution.py:30
  152.4 12.1 %collective-permute-start.17 = (bf16[4,8,4096]{2,1,0:T(8,128)(2,1)}, bf16[4,8,4096]{2,1,0:T(8,128)(2,1)S(1)}, u32[]{:S(2)}, u32[]{:S(2)}) collective-permute-start(bf16[4,8,4096]{2,1,0:T(8,128)(2,1)} %get-tuple-element.46), channel_id=1, source_target_pairs={{0,128},{1,129},{2,130},{3,131},{4,132},{5,133},{6,134},{7,135},{8... | collective-permute-start | bytes 786440 | tf_op jit(solution)/shard_map/ppermute | solution.py:30
  154.5 10.3 %collective-permute-start.18 = (bf16[4,8,4096]{2,1,0:T(8,128)(2,1)}, bf16[4,8,4096]{2,1,0:T(8,128)(2,1)S(1)}, u32[]{:S(2)}, u32[]{:S(2)}) collective-permute-start(bf16[4,8,4096]{2,1,0:T(8,128)(2,1)} %get-tuple-element.45), channel_id=1, source_target_pairs={{0,384},{1,385},{2,386},{3,387},{4,388},{5,389},{6,390},{7,391},{8... | collective-permute-start | bytes 786440 | tf_op jit(solution)/shard_map/ppermute | solution.py:30
  158.6 27.0 %all-to-all-start.2 = ((bf16[8,8,4096]{2,1,0:T(8,128)(2,1)}), bf16[8,8,4096]{2,1,0:T(8,128)(2,1)S(1)}, u32[]{:S(2)}, u32[]{:S(2)}) async-start(bf16[8,8,4096]{2,1,0:T(8,128)(2,1)} %fusion.6), calls=%async_computation.2 | async-start | bytes 1048576 | tf_op jit(solution)/shard_map/all_to_all | solution.py:219
  164.9 11.7 %collective-permute-start.19 = (bf16[8,4096]{1,0:T(8,128)(2,1)S(1)}, bf16[8,4096]{1,0:T(8,128)(2,1)S(1)}, u32[]{:S(2)}, u32[]{:S(2)}) collective-permute-start(bf16[8,4096]{1,0:T(8,128)(2,1)S(1)} %get-tuple-element.55), channel_id=1, source_target_pairs={{0,64},{1,65},{2,66},{3,67},{4,68},{5,69},{6,70},{7,71},{8,72},{9,... | collective-permute-start | bytes 196616 | tf_op jit(solution)/shard_map/ppermute | solution.py:30
  194.6 9.7 %collective-permute-start.23 = (bf16[4,8,2048]{2,1,0:T(8,128)(2,1)S(1)}, bf16[4,8,2048]{2,1,0:T(8,128)(2,1)S(1)}, u32[]{:S(2)}, u32[]{:S(2)}) collective-permute-start(bf16[4,8,2048]{2,1,0:T(8,128)(2,1)S(1)} %all_to_all.25), channel_id=1, source_target_pairs={{0,96},{1,97},{2,98},{3,99},{4,100},{5,101},{6,102},{7,103},{8,104... | collective-permute-start | bytes 393224 | tf_op jit(solution)/shard_map/ppermute | solution.py:30
  200.2 11.3 %collective-permute-start.24 = (bf16[4,8,2048]{2,1,0:T(8,128)(2,1)S(1)}, bf16[4,8,2048]{2,1,0:T(8,128)(2,1)S(1)}, u32[]{:S(2)}, u32[]{:S(2)}) collective-permute-start(bf16[4,8,2048]{2,1,0:T(8,128)(2,1)S(1)} %all_to_all.25), channel_id=1, source_target_pairs={{0,64},{1,65},{2,66},{3,67},{4,68},{5,69},{6,70},{7,71},{8,72},{9,... | collective-permute-start | bytes 393224 | tf_op jit(solution)/shard_map/ppermute | solution.py:30
  202.1 9.4 %collective-permute-start.25 = (bf16[4,8,2048]{2,1,0:T(8,128)(2,1)S(1)}, bf16[4,8,2048]{2,1,0:T(8,128)(2,1)S(1)}, u32[]{:S(2)}, u32[]{:S(2)}) collective-permute-start(bf16[4,8,2048]{2,1,0:T(8,128)(2,1)S(1)} %all_to_all.25), channel_id=1, source_target_pairs={{0,32},{1,33},{2,34},{3,35},{4,36},{5,37},{6,38},{7,39},{8,40},{9,... | collective-permute-start | bytes 393224 | tf_op jit(solution)/shard_map/ppermute | solution.py:30
  222.8 18.9 %all-to-all-start.4 = ((f32[4,256,256]{2,1,0:T(8,128)}), f32[4,256,256]{2,1,0:T(8,128)S(1)}, u32[]{:S(2)}, u32[]{:S(2)}) async-start(f32[4,256,256]{2,1,0:T(8,128)} %shard_map.58), calls=%async_computation.4 | async-start | bytes 2097152 | tf_op jit(solution)/shard_map/all_to_all | solution.py:250
  (15 other events, 91.3 us)
Sparse Core Ops, SparseCore 0:
  90.1 37.2 all-gather.4
  141.7 66.8 all-gather.6

commit v15 on v14

--- a/solution.py
+++ b/solution.py
@@ -22,7 +22,7 @@
 Z_SLOTS = np.array([0, 3, 2, 1])
 ALONG_X = [(8 * int(k),) for k in X_SLOTS[1:]]
 ALONG_Z = [(2 * int(k),) for k in Z_SLOTS[1:]]
-STRIDED_Z = [(4,), (0, 8), (4, 8)]
+STRIDED_Z = [(0, 8), (4,), (4, 8)]
 
 
 def swap(array, data, model=0):
@@ -76,63 +76,63 @@
     )(order, *operands)
 
 
-def weight_kernel(grad_ref, columns_ref, *refs):
-    *before, out_ref = refs
-    slices, devices, share, rows = columns_ref.shape
+def weight_kernel(targets_ref, grad_ref, columns_ref, *refs):
+    before, outs = refs[:-X], refs[-X:]
+    slices, devices, share, wide = columns_ref.shape
+    rows = wide // X
     half = slices // 2
-    pieces = [
-        columns_ref[half * view : half * (view + 1), d].reshape(half * share, rows)
-        for view in range(2)
-        for d in range(devices)
-    ]
-    columns = jnp.concatenate(pieces, axis=0)
-    result = jnp.dot(grad_ref[...], columns, preferred_element_type=jnp.float32)
-    if before:
-        features = result.shape[0]
-        out_ref[0, :features] = before[0][0]
-        out_ref[0, features:] = result
-    else:
-        out_ref[0] = result
-
-
-def weight_half(grad, columns, before=()):
+    features = grad_ref.shape[0]
+    for k in range(X):
+        target = pl.ds(pl.multiple_of(targets_ref[k] * rows, rows), rows)
+        pieces = [
+            columns_ref[half * view : half * (view + 1), d, :, target].reshape(half * share, rows)
+            for view in range(2)
+            for d in range(devices)
+        ]
+        columns = jnp.concatenate(pieces, axis=0)
+        result = jnp.dot(grad_ref[...], columns, preferred_element_type=jnp.float32)
+        if before:
+            outs[k][:features] = before[k][...]
+            outs[k][features:] = result
+        else:
+            outs[k][...] = result
+
+
+def weight_half(targets, grad, columns, *before):
     half, depth = grad.shape
-    slices, devices, share, wide = columns.shape
-    rows = wide // X
-    features = half * (len(before) + 1)
+    wide = columns.shape[3]
+    features = 2 * half if before else half
+    vmem = pl.BlockSpec(memory_space=pltpu.VMEM)
     return pl.pallas_call(
         weight_kernel,
-        grid=(X,),
-        in_specs=[
-            pl.BlockSpec((half, depth), lambda x: (0, 0)),
-            pl.BlockSpec((slices, devices, share, rows), lambda x: (0, 0, 0, x)),
-        ]
-        + [pl.BlockSpec((1, half, rows), lambda x: (x, 0, 0))] * len(before),
-        out_specs=pl.BlockSpec((1, features, rows), lambda x: (x, 0, 0)),
-        out_shape=jax.ShapeDtypeStruct((X, features, rows), jnp.float32),
+        in_specs=[pl.BlockSpec(memory_space=pltpu.SMEM)] + [vmem] * (2 + len(before)),
+        out_specs=[vmem] * X,
+        out_shape=[jax.ShapeDtypeStruct((features, wide // X), jnp.float32)] * X,
         compiler_params=pltpu.CompilerParams(vmem_limit_bytes=16 * 1024 * 1024),
         cost_estimate=pl.CostEstimate(
             flops=2 * half * depth * wide, bytes_accessed=5 * 1024 * 1024, transcendentals=0
         ),
-    )(grad, columns, *before)
-
-
-def finish_kernel(position_ref, terms_ref, out_ref, total_ref):
-    total_ref[...] = (terms_ref[0] + terms_ref[1]) + (terms_ref[2] + terms_ref[3])
+    )(targets, grad, columns, *before)
+
+
+def finish_kernel(position_ref, *refs):
+    *terms, out_ref, total_ref = refs
+    total_ref[...] = (terms[0][...] + terms[1][...]) + (terms[2][...] + terms[3][...])
     blocks = [total_ref[pl.ds(pl.multiple_of(position_ref[j] * 8, 8), 8)] for j in range(DP)]
     out_ref[...] = jnp.concatenate(blocks, axis=0).T
 
 
 def finish(position, terms):
-    _, features, rows = terms.shape
+    features, rows = terms[0].shape
+    vmem = pl.BlockSpec(memory_space=pltpu.VMEM)
     return pl.pallas_call(
         finish_kernel,
-        in_specs=[pl.BlockSpec(memory_space=pltpu.SMEM), pl.BlockSpec(memory_space=pltpu.VMEM)],
-        out_specs=pl.BlockSpec(memory_space=pltpu.VMEM),
+        in_specs=[pl.BlockSpec(memory_space=pltpu.SMEM)] + [vmem] * len(terms),
+        out_specs=vmem,
         out_shape=jax.ShapeDtypeStruct((rows, features), jnp.float32),
         scratch_shapes=[pltpu.VMEM((features, rows), jnp.float32)],
         compiler_params=pltpu.CompilerParams(vmem_limit_bytes=16 * 1024 * 1024),
-    )(position, terms)
+    )(position, *terms)
 
 
 def per_device(inputs, weight):
@@ -245,12 +245,10 @@
     )
     grad_own, columns = gather(grad_proj, ALONG_Z, columns)
     grad_other = swap(grad_own, 1)
-    terms = weight_half(grad_own.reshape(feat // 2, depth), columns)
-    terms = weight_half(grad_other.reshape(feat // 2, depth), columns, (terms,))
-    terms = lax.all_to_all(
-        terms, "dp", split_axis=0, concat_axis=0, axis_index_groups=SAME_REST
-    )
-    return finish(position, terms)
+    targets = data_index >> 3 ^ jnp.asarray(X_SLOTS, jnp.int32)
+    terms = weight_half(targets, grad_own.reshape(feat // 2, depth), columns)
+    terms = weight_half(targets, grad_other.reshape(feat // 2, depth), columns, *terms)
+    return finish(position, [terms[0]] + [swap(terms[k + 1], *mask) for k, mask in enumerate(ALONG_X)])
 
 
 def solution(mesh):

time: 251 us -> 247 us (0.984)
  waiting for transfers between devices: 82.8 us -> 75.6 us
  starting transfers between devices: 114 us -> 120 us
    all_to_all x1 -> x0, waiting for transfers between devices: 15.2 us -> none  [per_device(): lax.all_to_all(terms, 'dp', split_axis=0, concat_axis=0, axis_index_group...]
    ppermute x27 -> x30, starting transfers between devices: 95.3 us -> 104 us  [swap(): lax.ppermute(array, ('dp', 'mp'), [(i, i ^ mask) for i in range(DP * MP)])]
    ppermute x27 -> x30, waiting for transfers between devices: 45.8 us -> 53.3 us  [swap(): lax.ppermute(array, ('dp', 'mp'), [(i, i ^ mask) for i in range(DP * MP)])]
    all_to_all x1 -> x0, starting transfers between devices: 3.65 us -> none  [per_device(): lax.all_to_all(terms, 'dp', split_axis=0, concat_axis=0, axis_index_group...]
  transfers between devices with their start and end apart: 33 -> 35, of which waited for: 20 -> 22; matrix products, arithmetic and copies ran while one was open for 4% -> 4% of each run, Pallas kernels for 1% -> 1%
where the time goes in v15:
time: 247 us; the launch traced here: 246 us
  starting transfers between devices  120 us (49%)
  waiting for transfers between devices  75.6 us (31%)
  between operations  14.1 us (6%)
  Pallas kernels  8.47 us (3%)
  blocking collectives  8.46 us (3%)
  local copies, waits for them, and re-layouts  8.05 us (3%)
  matrix products  6.92 us (3%)
  other arithmetic  4.8 us (2%)
    ppermute x30, starting transfers between devices, swap(): lax.ppermute(array, ('dp', 'mp'), [(i, i ^ mask) for i in range(DP * MP)])  104 us
    ppermute x30, waiting for transfers between devices, swap(): lax.ppermute(array, ('dp', 'mp'), [(i, i ^ mask) for i in range(DP * MP)])  53.3 us
    all_to_all x1, waiting for transfers between devices, per_device(): lax.all_to_all(projected.reshape(DP, block, views * images), 'dp', split_...  11.2 us
    all_to_all x1, blocking collectives, per_device(): lax.all_to_all(grad_proj, 'dp', split_axis=0, concat_axis=0, axis_index_g...  8.46 us
    all_to_all x1, starting transfers between devices, per_device(): lax.all_to_all(projected.reshape(DP, block, views * images), 'dp', split_...  6.39 us
  transfers between devices with their start and end apart: 35, of which 22 were waited for; matrix products, arithmetic and copies ran while one was open for 4% of the time, Pallas kernels for 1%

profile of v15, /device:TPU:1, one launch (start us, length us, event | category | flops | bytes accessed | tf_op | source)
XLA Modules:
  0.0 246.0 jit_solution(9028730401709658631)
XLA Ops:
  6.5 8.4 %collective-permute-start = (bf16[256,256]{1,0:T(8,128)(2,1)}, bf16[256,256]{1,0:T(8,128)(2,1)S(1)}, u32[]{:S(2)}, u32[]{:S(2)}) collective-permute-start(bf16[256,256]{1,0:T(8,128)(2,1)} %param.7), channel_id=1, source_target_pairs={{0,96},{1,97},{2,98},{3,99},{4,100},{5,101},{6,102},{7,103},{8,104... | collective-permute-start | bytes 393224 | tf_op jit(solution)/shard_map/ppermute | solution.py:30
  19.1 6.7 %collective-permute-done.1 = bf16[256,256]{1,0:T(8,128)(2,1)S(1)} collective-permute-done((bf16[256,256]{1,0:T(8,128)(2,1)}, bf16[256,256]{1,0:T(8,128)(2,1)S(1)}, u32[]{:S(2)}, u32[]{:S(2)}) %collective-permute-start.1) | collective-permute-done | bytes 131104 | tf_op jit(solution)/shard_map/ppermute | solution.py:30
  26.9 5.1 %collective-permute-start.3 = (bf16[4,256,256]{2,1,0:T(8,128)(2,1)S(1)}, bf16[4,256,256]{2,1,0:T(8,128)(2,1)S(1)}, u32[]{:S(2)}, u32[]{:S(2)}) collective-permute-start(bf16[4,256,256]{2,1,0:T(8,128)(2,1)S(1)} %get-tuple-element.66), channel_id=1, source_target_pairs={{0,256},{1,257},{2,258},{3,259},{4,260},{5,261},{6,262},{7,263},{8... | collective-permute-start | bytes 1572872 | tf_op jit(solution)/shard_map/ppermute | solution.py:30
  36.7 5.5 %collective-permute-done.3 = bf16[4,256,256]{2,1,0:T(8,128)(2,1)S(1)} collective-permute-done((bf16[4,256,256]{2,1,0:T(8,128)(2,1)S(1)}, bf16[4,256,256]{2,1,0:T(8,128)(2,1)S(1)}, u32[]{:S(2)}, u32[]{:S(2)}) %collective-permute-start.3) | collective-permute-done | bytes 524320 | tf_op jit(solution)/shard_map/ppermute | solution.py:30
  42.2 11.9 %collective-permute-done.4 = bf16[4,256,256]{2,1,0:T(8,128)(2,1)S(1)} collective-permute-done((bf16[4,256,256]{2,1,0:T(8,128)(2,1)S(1)}, bf16[4,256,256]{2,1,0:T(8,128)(2,1)S(1)}, u32[]{:S(2)}, u32[]{:S(2)}) %collective-permute-start.4) | collective-permute-done | bytes 524320 | tf_op jit(solution)/shard_map/ppermute | solution.py:30
  65.6 6.4 %all-to-all-start = ((f32[32,8,256]{2,1,0:T(8,128)}), f32[32,8,256]{2,1,0:T(8,128)S(1)}, u32[]{:S(2)}, u32[]{:S(2)}) async-start(f32[32,8,256]{2,1,0:T(8,128)} %bitcast.11), calls=%async_computation | async-start | bytes 524288 | tf_op jit(solution)/shard_map/all_to_all | solution.py:164
  72.1 11.2 %all-to-all-done = f32[32,8,256]{2,1,0:T(8,128)S(1)} async-done(((f32[32,8,256]{2,1,0:T(8,128)}), f32[32,8,256]{2,1,0:T(8,128)S(1)}, u32[]{:S(2)}, u32[]{:S(2)}) %all-to-all-start) | async-done | bytes 262176 | tf_op jit(solution)/shard_map/all_to_all | solution.py:164
  90.0 7.9 %collective-permute-start.8 = (bf16[8,4096]{1,0:T(8,128)(2,1)S(1)}, bf16[8,4096]{1,0:T(8,128)(2,1)S(1)}, u32[]{:S(2)}, u32[]{:S(2)}) collective-permute-start(bf16[8,4096]{1,0:T(8,128)(2,1)S(1)} %get-tuple-element.33), channel_id=1, source_target_pairs={{0,8},{1,9},{2,10},{3,11},{4,12},{5,13},{6,14},{7,15},{8,0},{9,1},... | collective-permute-start | bytes 196616 | tf_op jit(solution)/shard_map/ppermute | solution.py:30
  102.2 4.9 %all-to-all-start.1 = ((bf16[8,32,1024]{2,1,0:T(8,128)(2,1)}), bf16[8,32,1024]{2,1,0:T(8,128)(2,1)S(1)}, u32[]{:S(2)}, u32[]{:S(2)}) async-start(bf16[8,32,1024]{2,1,0:T(8,128)(2,1)} %reshape.103), calls=%async_computation.1 | async-start | bytes 1048576 | tf_op jit(solution)/shard_map/all_to_all | solution.py:177
  112.8 3.7 %collective-permute-start.13 = (bf16[4,8,4096]{2,1,0:T(8,128)(2,1)S(1)}, bf16[4,8,4096]{2,1,0:T(8,128)(2,1)S(1)}, u32[]{:S(2)}, u32[]{:S(2)}) collective-permute-start(bf16[4,8,4096]{2,1,0:T(8,128)(2,1)S(1)} %get-tuple-element.74), channel_id=1, source_target_pairs={{0,384},{1,385},{2,386},{3,387},{4,388},{5,389},{6,390},{7,391},{8... | collective-permute-start | bytes 786440 | tf_op jit(solution)/shard_map/ppermute | solution.py:30
  116.6 4.1 %collective-permute-done.12 = bf16[4,8,4096]{2,1,0:T(8,128)(2,1)S(1)} collective-permute-done((bf16[4,8,4096]{2,1,0:T(8,128)(2,1)S(1)}, bf16[4,8,4096]{2,1,0:T(8,128)(2,1)S(1)}, u32[]{:S(2)}, u32[]{:S(2)}) %collective-permute-start.12) | collective-permute-done | bytes 262176 | tf_op jit(solution)/shard_map/ppermute | solution.py:30
  120.7 3.6 %collective-permute-done.13 = bf16[4,8,4096]{2,1,0:T(8,128)(2,1)S(1)} collective-permute-done((bf16[4,8,4096]{2,1,0:T(8,128)(2,1)S(1)}, bf16[4,8,4096]{2,1,0:T(8,128)(2,1)S(1)}, u32[]{:S(2)}, u32[]{:S(2)}) %collective-permute-start.13) | collective-permute-done | bytes 262176 | tf_op jit(solution)/shard_map/ppermute | solution.py:30
  127.5 6.5 %collective-permute-start.14 = (bf16[4,4,8,4096]{3,2,1,0:T(8,128)(2,1)S(1)}, bf16[4,4,8,4096]{3,2,1,0:T(8,128)(2,1)S(1)}, u32[]{:S(2)}, u32[]{:S(2)}) collective-permute-start(bf16[4,4,8,4096]{3,2,1,0:T(8,128)(2,1)S(1)} %pad_maximum_fusion.1), channel_id=1, source_target_pairs={{0,16},{1,17},{2,18},{3,19},{4,20},{5,21},{6,22},{7,23},{8,24},{9,... | collective-permute-start | bytes 3145736 | tf_op jit(solution)/shard_map/ppermute | solution.py:30
  141.6 3.3 %collective-permute-start.22 = (bf16[64,4096]{1,0:T(8,128)(2,1)}, bf16[64,4096]{1,0:T(8,128)(2,1)S(1)}, u32[]{:S(2)}, u32[]{:S(2)}) collective-permute-start(bf16[64,4096]{1,0:T(8,128)(2,1)} %fusion.5), channel_id=1, source_target_pairs={{0,32},{1,33},{2,34},{3,35},{4,36},{5,37},{6,38},{7,39},{8,40},{9,... | collective-permute-start | bytes 1572872 | tf_op jit(solution)/shard_map/ppermute | solution.py:30
  147.7 4.6 %collective-permute-start.16 = (bf16[4,8,4096]{2,1,0:T(8,128)(2,1)}, bf16[4,8,4096]{2,1,0:T(8,128)(2,1)S(1)}, u32[]{:S(2)}, u32[]{:S(2)}) collective-permute-start(bf16[4,8,4096]{2,1,0:T(8,128)(2,1)} %get-tuple-element.63), channel_id=1, source_target_pairs={{0,256},{1,257},{2,258},{3,259},{4,260},{5,261},{6,262},{7,263},{8... | collective-permute-start | bytes 786440 | tf_op jit(solution)/shard_map/ppermute | solution.py:30
  158.5 4.1 %all-to-all-start.2 = ((bf16[8,8,4096]{2,1,0:T(8,128)(2,1)}), bf16[8,8,4096]{2,1,0:T(8,128)(2,1)S(1)}, u32[]{:S(2)}, u32[]{:S(2)}) async-start(bf16[8,8,4096]{2,1,0:T(8,128)(2,1)} %fusion.6), calls=%async_computation.2 | async-start | bytes 1048576 | tf_op jit(solution)/shard_map/all_to_all | solution.py:219
  164.9 6.9 %collective-permute-start.19 = (bf16[8,4096]{1,0:T(8,128)(2,1)S(1)}, bf16[8,4096]{1,0:T(8,128)(2,1)S(1)}, u32[]{:S(2)}, u32[]{:S(2)}) collective-permute-start(bf16[8,4096]{1,0:T(8,128)(2,1)S(1)} %get-tuple-element.71), channel_id=1, source_target_pairs={{0,8},{1,9},{2,10},{3,11},{4,12},{5,13},{6,14},{7,15},{8,0},{9,1},... | collective-permute-start | bytes 196616 | tf_op jit(solution)/shard_map/ppermute | solution.py:30
  181.7 3.8 %all-to-all-done.2 = bf16[8,8,4096]{2,1,0:T(8,128)(2,1)S(1)} async-done(((bf16[8,8,4096]{2,1,0:T(8,128)(2,1)}), bf16[8,8,4096]{2,1,0:T(8,128)(2,1)S(1)}, u32[]{:S(2)}, u32[]{:S(2)}) %all-to-all-start.2) | async-done | bytes 524320 | tf_op jit(solution)/shard_map/all_to_all | solution.py:219
  186.2 8.5 %all_to_all.20 = bf16[4,8,2048]{2,1,0:T(8,128)(2,1)S(1)} all-to-all(bf16[4,8,2048]{2,1,0:T(8,128)(2,1)S(1)} %pad_maximum_fusion.7), channel_id=1, replica_groups={{0,128,256,384},{16,144,272,400},{32,160,288,416},{48,176,304,432},{64,..., dimensions={0} | all-to-all | bytes 262144 | tf_op jit(solution)/shard_map/all_to_all | solution.py:243
  194.6 5.6 %collective-permute-start.23 = (bf16[4,8,2048]{2,1,0:T(8,128)(2,1)S(1)}, bf16[4,8,2048]{2,1,0:T(8,128)(2,1)S(1)}, u32[]{:S(2)}, u32[]{:S(2)}) collective-permute-start(bf16[4,8,2048]{2,1,0:T(8,128)(2,1)S(1)} %all_to_all.20), channel_id=1, source_target_pairs={{0,96},{1,97},{2,98},{3,99},{4,100},{5,101},{6,102},{7,103},{8,104... | collective-permute-start | bytes 393224 | tf_op jit(solution)/shard_map/ppermute | solution.py:30
  204.3 4.2 %all-gather.7.cloned.1.call-done = bf16[64,32,1024]{2,1,0:T(8,128)(2,1)} async-done(((bf16[8,32,1024]{2,1,0:T(8,128)(2,1)}), bf16[64,32,1024]{2,1,0:T(8,128)(2,1)}) %all-gather.7.cloned.1.call-update) | async-done | bytes 4194320 | tf_op jit(solution)/shard_map/all_gather | solution.py:184
  211.6 4.3 %collective-permute-start.26 = (bf16[4,4,8,2048]{3,2,1,0:T(8,128)(2,1)S(1)}, bf16[4,4,8,2048]{3,2,1,0:T(8,128)(2,1)S(1)}, u32[]{:S(2)}, u32[]{:S(2)}) collective-permute-start(bf16[4,4,8,2048]{3,2,1,0:T(8,128)(2,1)S(1)} %pad_maximum_fusion.3), channel_id=1, source_target_pairs={{0,16},{1,17},{2,18},{3,19},{4,20},{5,21},{6,22},{7,23},{8,24},{9,... | collective-permute-start | bytes 1572872 | tf_op jit(solution)/shard_map/ppermute | solution.py:30
  226.1 3.7 %collective-permute-start.29 = (f32[256,256]{1,0:T(8,128)S(1)}, f32[256,256]{1,0:T(8,128)S(1)}, u32[]{:S(2)}, u32[]{:S(2)}) collective-permute-start(f32[256,256]{1,0:T(8,128)S(1)} %get-tuple-element.60), channel_id=1, source_target_pairs={{0,384},{1,385},{2,386},{3,387},{4,388},{5,389},{6,390},{7,391},{8... | collective-permute-start | bytes 786440 | tf_op jit(solution)/shard_map/ppermute | solution.py:30
  232.2 4.1 %collective-permute-done.28.refs_2_ = f32[256,256]{1,0:T(8,128)S(1)} collective-permute-done((f32[256,256]{1,0:T(8,128)S(1)}, f32[256,256]{1,0:T(8,128)S(1)}, u32[]{:S(2)}, u32[]{:S(2)}) %collective-permute-start.28) | collective-permute-done | bytes 262176 | tf_op jit(solution)/shard_map/ppermute | solution.py:30
  (117 shorter events, 92.9 us)
Async XLA Ops:
  6.5 12.6 %collective-permute-start = (bf16[256,256]{1,0:T(8,128)(2,1)}, bf16[256,256]{1,0:T(8,128)(2,1)S(1)}, u32[]{:S(2)}, u32[]{:S(2)}) collective-permute-start(bf16[256,256]{1,0:T(8,128)(2,1)} %param.7), channel_id=1, source_target_pairs={{0,96},{1,97},{2,98},{3,99},{4,100},{5,101},{6,102},{7,103},{8,104... | collective-permute-start | bytes 393224 | tf_op jit(solution)/shard_map/ppermute | solution.py:30
  15.0 10.9 %collective-permute-start.1 = (bf16[256,256]{1,0:T(8,128)(2,1)}, bf16[256,256]{1,0:T(8,128)(2,1)S(1)}, u32[]{:S(2)}, u32[]{:S(2)}) collective-permute-start(bf16[256,256]{1,0:T(8,128)(2,1)} %param.7), channel_id=1, source_target_pairs={{0,64},{1,65},{2,66},{3,67},{4,68},{5,69},{6,70},{7,71},{8,72},{9,... | collective-permute-start | bytes 393224 | tf_op jit(solution)/shard_map/ppermute | solution.py:30
  26.9 15.3 %collective-permute-start.3 = (bf16[4,256,256]{2,1,0:T(8,128)(2,1)S(1)}, bf16[4,256,256]{2,1,0:T(8,128)(2,1)S(1)}, u32[]{:S(2)}, u32[]{:S(2)}) collective-permute-start(bf16[4,256,256]{2,1,0:T(8,128)(2,1)S(1)} %get-tuple-element.66), channel_id=1, source_target_pairs={{0,256},{1,257},{2,258},{3,259},{4,260},{5,261},{6,262},{7,263},{8... | collective-permute-start | bytes 1572872 | tf_op jit(solution)/shard_map/ppermute | solution.py:30
  32.0 22.1 %collective-permute-start.4 = (bf16[4,256,256]{2,1,0:T(8,128)(2,1)S(1)}, bf16[4,256,256]{2,1,0:T(8,128)(2,1)S(1)}, u32[]{:S(2)}, u32[]{:S(2)}) collective-permute-start(bf16[4,256,256]{2,1,0:T(8,128)(2,1)S(1)} %get-tuple-element.66), channel_id=1, source_target_pairs={{0,128},{1,129},{2,130},{3,131},{4,132},{5,133},{6,134},{7,135},{8... | collective-permute-start | bytes 1572872 | tf_op jit(solution)/shard_map/ppermute | solution.py:30
  34.2 21.3 %collective-permute-start.5 = (bf16[4,256,256]{2,1,0:T(8,128)(2,1)S(1)}, bf16[4,256,256]{2,1,0:T(8,128)(2,1)S(1)}, u32[]{:S(2)}, u32[]{:S(2)}) collective-permute-start(bf16[4,256,256]{2,1,0:T(8,128)(2,1)S(1)} %get-tuple-element.66), channel_id=1, source_target_pairs={{0,384},{1,385},{2,386},{3,387},{4,388},{5,389},{6,390},{7,391},{8... | collective-permute-start | bytes 1572872 | tf_op jit(solution)/shard_map/ppermute | solution.py:30
  65.6 17.7 %all-to-all-start = ((f32[32,8,256]{2,1,0:T(8,128)}), f32[32,8,256]{2,1,0:T(8,128)S(1)}, u32[]{:S(2)}, u32[]{:S(2)}) async-start(f32[32,8,256]{2,1,0:T(8,128)} %bitcast.11), calls=%async_computation | async-start | bytes 524288 | tf_op jit(solution)/shard_map/all_to_all | solution.py:164
  72.0 55.5 %all-gather.5.cloned.1.call-start = ((), (), s32[]{:S(2)}) async-start(), calls=%async_computation.4 | async-start | bytes 1179648 | tf_op jit(solution)/shard_map/all_gather | solution.py:180
  90.0 17.1 %collective-permute-start.8 = (bf16[8,4096]{1,0:T(8,128)(2,1)S(1)}, bf16[8,4096]{1,0:T(8,128)(2,1)S(1)}, u32[]{:S(2)}, u32[]{:S(2)}) collective-permute-start(bf16[8,4096]{1,0:T(8,128)(2,1)S(1)} %get-tuple-element.33), channel_id=1, source_target_pairs={{0,8},{1,9},{2,10},{3,11},{4,12},{5,13},{6,14},{7,15},{8,0},{9,1},... | collective-permute-start | bytes 196616 | tf_op jit(solution)/shard_map/ppermute | solution.py:30
  102.2 22.2 %all-to-all-start.1 = ((bf16[8,32,1024]{2,1,0:T(8,128)(2,1)}), bf16[8,32,1024]{2,1,0:T(8,128)(2,1)S(1)}, u32[]{:S(2)}, u32[]{:S(2)}) async-start(bf16[8,32,1024]{2,1,0:T(8,128)(2,1)} %reshape.103), calls=%async_computation.1 | async-start | bytes 1048576 | tf_op jit(solution)/shard_map/all_to_all | solution.py:177
  107.2 101.4 %all-gather.7.cloned.1.call-start = ((), (), s32[]{:S(2)}) async-start(), calls=%async_computation.5 | async-start | bytes 4718592 | tf_op jit(solution)/shard_map/all_gather | solution.py:184
  110.2 10.4 %collective-permute-start.12 = (bf16[4,8,4096]{2,1,0:T(8,128)(2,1)S(1)}, bf16[4,8,4096]{2,1,0:T(8,128)(2,1)S(1)}, u32[]{:S(2)}, u32[]{:S(2)}) collective-permute-start(bf16[4,8,4096]{2,1,0:T(8,128)(2,1)S(1)} %get-tuple-element.74), channel_id=1, source_target_pairs={{0,128},{1,129},{2,130},{3,131},{4,132},{5,133},{6,134},{7,135},{8... | collective-permute-start | bytes 786440 | tf_op jit(solution)/shard_map/ppermute | solution.py:30
  112.8 11.4 %collective-permute-start.13 = (bf16[4,8,4096]{2,1,0:T(8,128)(2,1)S(1)}, bf16[4,8,4096]{2,1,0:T(8,128)(2,1)S(1)}, u32[]{:S(2)}, u32[]{:S(2)}) collective-permute-start(bf16[4,8,4096]{2,1,0:T(8,128)(2,1)S(1)} %get-tuple-element.74), channel_id=1, source_target_pairs={{0,384},{1,385},{2,386},{3,387},{4,388},{5,389},{6,390},{7,391},{8... | collective-permute-start | bytes 786440 | tf_op jit(solution)/shard_map/ppermute | solution.py:30
  141.6 15.8 %collective-permute-start.22 = (bf16[64,4096]{1,0:T(8,128)(2,1)}, bf16[64,4096]{1,0:T(8,128)(2,1)S(1)}, u32[]{:S(2)}, u32[]{:S(2)}) collective-permute-start(bf16[64,4096]{1,0:T(8,128)(2,1)} %fusion.5), channel_id=1, source_target_pairs={{0,32},{1,33},{2,34},{3,35},{4,36},{5,37},{6,38},{7,39},{8,40},{9,... | collective-permute-start | bytes 1572872 | tf_op jit(solution)/shard_map/ppermute | solution.py:30
  147.7 14.9 %collective-permute-start.16 = (bf16[4,8,4096]{2,1,0:T(8,128)(2,1)}, bf16[4,8,4096]{2,1,0:T(8,128)(2,1)S(1)}, u32[]{:S(2)}, u32[]{:S(2)}) collective-permute-start(bf16[4,8,4096]{2,1,0:T(8,128)(2,1)} %get-tuple-element.63), channel_id=1, source_target_pairs={{0,256},{1,257},{2,258},{3,259},{4,260},{5,261},{6,262},{7,263},{8... | collective-permute-start | bytes 786440 | tf_op jit(solution)/shard_map/ppermute | solution.py:30
  152.3 12.1 %collective-permute-start.17 = (bf16[4,8,4096]{2,1,0:T(8,128)(2,1)}, bf16[4,8,4096]{2,1,0:T(8,128)(2,1)S(1)}, u32[]{:S(2)}, u32[]{:S(2)}) collective-permute-start(bf16[4,8,4096]{2,1,0:T(8,128)(2,1)} %get-tuple-element.62), channel_id=1, source_target_pairs={{0,128},{1,129},{2,130},{3,131},{4,132},{5,133},{6,134},{7,135},{8... | collective-permute-start | bytes 786440 | tf_op jit(solution)/shard_map/ppermute | solution.py:30
  154.5 10.3 %collective-permute-start.18 = (bf16[4,8,4096]{2,1,0:T(8,128)(2,1)}, bf16[4,8,4096]{2,1,0:T(8,128)(2,1)S(1)}, u32[]{:S(2)}, u32[]{:S(2)}) collective-permute-start(bf16[4,8,4096]{2,1,0:T(8,128)(2,1)} %get-tuple-element.61), channel_id=1, source_target_pairs={{0,384},{1,385},{2,386},{3,387},{4,388},{5,389},{6,390},{7,391},{8... | collective-permute-start | bytes 786440 | tf_op jit(solution)/shard_map/ppermute | solution.py:30
  158.5 27.0 %all-to-all-start.2 = ((bf16[8,8,4096]{2,1,0:T(8,128)(2,1)}), bf16[8,8,4096]{2,1,0:T(8,128)(2,1)S(1)}, u32[]{:S(2)}, u32[]{:S(2)}) async-start(bf16[8,8,4096]{2,1,0:T(8,128)(2,1)} %fusion.6), calls=%async_computation.2 | async-start | bytes 1048576 | tf_op jit(solution)/shard_map/all_to_all | solution.py:219
  164.9 11.7 %collective-permute-start.19 = (bf16[8,4096]{1,0:T(8,128)(2,1)S(1)}, bf16[8,4096]{1,0:T(8,128)(2,1)S(1)}, u32[]{:S(2)}, u32[]{:S(2)}) collective-permute-start(bf16[8,4096]{1,0:T(8,128)(2,1)S(1)} %get-tuple-element.71), channel_id=1, source_target_pairs={{0,8},{1,9},{2,10},{3,11},{4,12},{5,13},{6,14},{7,15},{8,0},{9,1},... | collective-permute-start | bytes 196616 | tf_op jit(solution)/shard_map/ppermute | solution.py:30
  194.6 9.7 %collective-permute-start.23 = (bf16[4,8,2048]{2,1,0:T(8,128)(2,1)S(1)}, bf16[4,8,2048]{2,1,0:T(8,128)(2,1)S(1)}, u32[]{:S(2)}, u32[]{:S(2)}) collective-permute-start(bf16[4,8,2048]{2,1,0:T(8,128)(2,1)S(1)} %all_to_all.20), channel_id=1, source_target_pairs={{0,96},{1,97},{2,98},{3,99},{4,100},{5,101},{6,102},{7,103},{8,104... | collective-permute-start | bytes 393224 | tf_op jit(solution)/shard_map/ppermute | solution.py:30
  200.2 11.3 %collective-permute-start.24 = (bf16[4,8,2048]{2,1,0:T(8,128)(2,1)S(1)}, bf16[4,8,2048]{2,1,0:T(8,128)(2,1)S(1)}, u32[]{:S(2)}, u32[]{:S(2)}) collective-permute-start(bf16[4,8,2048]{2,1,0:T(8,128)(2,1)S(1)} %all_to_all.20), channel_id=1, source_target_pairs={{0,64},{1,65},{2,66},{3,67},{4,68},{5,69},{6,70},{7,71},{8,72},{9,... | collective-permute-start | bytes 393224 | tf_op jit(solution)/shard_map/ppermute | solution.py:30
  202.1 9.4 %collective-permute-start.25 = (bf16[4,8,2048]{2,1,0:T(8,128)(2,1)S(1)}, bf16[4,8,2048]{2,1,0:T(8,128)(2,1)S(1)}, u32[]{:S(2)}, u32[]{:S(2)}) collective-permute-start(bf16[4,8,2048]{2,1,0:T(8,128)(2,1)S(1)} %all_to_all.20), channel_id=1, source_target_pairs={{0,32},{1,33},{2,34},{3,35},{4,36},{5,37},{6,38},{7,39},{8,40},{9,... | collective-permute-start | bytes 393224 | tf_op jit(solution)/shard_map/ppermute | solution.py:30
  220.8 11.3 %collective-permute-start.27 = (f32[256,256]{1,0:T(8,128)S(1)}, f32[256,256]{1,0:T(8,128)S(1)}, u32[]{:S(2)}, u32[]{:S(2)}) collective-permute-start(f32[256,256]{1,0:T(8,128)S(1)} %get-tuple-element.58), channel_id=1, source_target_pairs={{0,256},{1,257},{2,258},{3,259},{4,260},{5,261},{6,262},{7,263},{8... | collective-permute-start | bytes 786440 | tf_op jit(solution)/shard_map/ppermute | solution.py:30
  223.4 12.8 %collective-permute-start.28 = (f32[256,256]{1,0:T(8,128)S(1)}, f32[256,256]{1,0:T(8,128)S(1)}, u32[]{:S(2)}, u32[]{:S(2)}) collective-permute-start(f32[256,256]{1,0:T(8,128)S(1)} %get-tuple-element.59), channel_id=1, source_target_pairs={{0,128},{1,129},{2,130},{3,131},{4,132},{5,133},{6,134},{7,135},{8... | collective-permute-start | bytes 786440 | tf_op jit(solution)/shard_map/ppermute | solution.py:30
  226.1 11.6 %collective-permute-start.29 = (f32[256,256]{1,0:T(8,128)S(1)}, f32[256,256]{1,0:T(8,128)S(1)}, u32[]{:S(2)}, u32[]{:S(2)}) collective-permute-start(f32[256,256]{1,0:T(8,128)S(1)} %get-tuple-element.60), channel_id=1, source_target_pairs={{0,384},{1,385},{2,386},{3,387},{4,388},{5,389},{6,390},{7,391},{8... | collective-permute-start | bytes 786440 | tf_op jit(solution)/shard_map/ppermute | solution.py:30
  (18 other events, 144.3 us)
Sparse Core Ops, SparseCore 0:
  90.1 37.2 all-gather.4
  141.7 66.8 all-gather.6

commit v16 on v15

--- a/solution.py
+++ b/solution.py
@@ -16,7 +16,7 @@
 Y = 8
 X = 4
 GROUPS = [list(range(Y)), list(range(Y, MP))]
-SAME_REST = [list(range(g, DP, DP // X)) for g in range(DP // X)]
+SAME_CORE = [list(range(core, DP, 2)) for core in range(2)]
 SAME_X = [list(range(x * DP // X, (x + 1) * DP // X)) for x in range(X)]
 X_SLOTS = np.array([0, 2, 1, 3])
 Z_SLOTS = np.array([0, 3, 2, 1])
@@ -148,9 +148,7 @@
     place = np.arange(DP)
     distance = place >> 4 | X_SLOTS[place >> 2 & 3] << 3 | Z_SLOTS[place & 3] << 1
     order = data_index ^ jnp.asarray(distance, jnp.int32)
-    relative = data_index ^ jnp.asarray(place, jnp.int32)
-    slot = (4 - (relative >> 1 & 3)) & 3
-    position = (relative & 1) << 4 | slot << 2 | jnp.asarray(place >> 3, jnp.int32)
+    position = (data_index & 1 ^ jnp.asarray(place & 1, jnp.int32)) << 4 | jnp.asarray(place >> 1, jnp.int32)
 
     share = views * images // Y
     mine = lax.dynamic_slice_in_dim(flat, lax.rem(model_index, Y) * share, share, axis=0)
@@ -222,8 +220,9 @@
     terms_other = times(corr_other, columns_b, ((1,), (0,))).astype(jnp.bfloat16)
     terms_own = times(corr_own, columns_b, ((1,), (0,)))
     shape = (4, 4, block, total)
-    both = terms_own.reshape(shape) + swap(terms_other.reshape(shape), 1).astype(jnp.float32)
-    along_x = add(both.astype(jnp.bfloat16), ALONG_X)[0].astype(jnp.bfloat16)
+    terms_own, terms_other = terms_own.reshape(shape), swap(terms_other.reshape(shape), 1)
+    both = [(terms_own[k] + terms_other[k].astype(jnp.float32)).astype(jnp.bfloat16) for k in range(X)]
+    along_x = add(both, ALONG_X)[0].astype(jnp.bfloat16)
     grad_a, terms_b = add(along_x, STRIDED_Z, terms_b)
     grads = jnp.stack([grad_a, jnp.sum(terms_b.astype(jnp.float32), axis=0)])
     wide = normed.astype(jnp.float32)
@@ -232,18 +231,18 @@
     grad_proj = ((grads - grad_mean - wide * cross_mean) * inverse).astype(jnp.bfloat16)
     images_x = total // X
     depth = views * images_x
-    grad_proj = jnp.stack(
-        [
-            jnp.concatenate(
-                [grad_proj[v, :, x * images_x : (x + 1) * images_x] for v in range(views)], axis=1
-            )
-            for x in range(X)
-        ]
-    )
-    grad_proj = lax.all_to_all(
-        grad_proj, "dp", split_axis=0, concat_axis=0, axis_index_groups=SAME_REST
-    )
-    grad_own, columns = gather(grad_proj, ALONG_Z, columns)
+    blocks = [
+        jnp.concatenate([grad_proj[v, :, x * images_x : (x + 1) * images_x] for v in range(views)], axis=1)
+        for x in range(X)
+    ]
+    grad_own = lax.all_to_all(
+        jnp.stack([part for part in blocks for _ in range(DP // X // 2)]),
+        "dp",
+        split_axis=0,
+        concat_axis=0,
+        axis_index_groups=SAME_CORE,
+    )
+    grad_own, columns = lax.optimization_barrier((grad_own, columns))
     grad_other = swap(grad_own, 1)
     targets = data_index >> 3 ^ jnp.asarray(X_SLOTS, jnp.int32)
     terms = weight_half(targets, grad_own.reshape(feat // 2, depth), columns)

time: 247 us -> 252 us (1.020)
  blocking collectives: 8.46 us -> 22.8 us
  starting transfers between devices: 120 us -> 109 us
    all_to_all x1, blocking collectives: 8.46 us -> 22.8 us  [per_device(): lax.all_to_all(jnp.stack([part for part in blocks for _ in range(DP // X...]
    ppermute x30 -> x27, starting transfers between devices: 104 us -> 93.4 us  [swap(): lax.ppermute(array, ('dp', 'mp'), [(i, i ^ mask) for i in range(DP * MP)])]
    all_gather x1, waiting for transfers between devices: 4.24 us -> 11.3 us  [per_device(): columns = lax.all_gather(slices, 'mp', axis=0, axis_index_groups=GROUPS)]
    ppermute x30 -> x27, waiting for transfers between devices: 53.3 us -> 49.4 us  [swap(): lax.ppermute(array, ('dp', 'mp'), [(i, i ^ mask) for i in range(DP * MP)])]
  transfers between devices with their start and end apart: 35 -> 32, of which waited for: 22 -> 20; matrix products, arithmetic and copies ran while one was open for 4% -> 4% of each run, Pallas kernels for 1% -> 1%
where the time goes in v16:
time: 252 us; the launch traced here: 250 us
  starting transfers between devices  109 us (43%)
  waiting for transfers between devices  76.5 us (30%)
  blocking collectives  22.8 us (9%)
  between operations  14.1 us (6%)
  Pallas kernels  8.47 us (3%)
  local copies, waits for them, and re-layouts  7.16 us (3%)
  matrix products  6.93 us (3%)
  other arithmetic  5.45 us (2%)
    ppermute x27, starting transfers between devices, swap(): lax.ppermute(array, ('dp', 'mp'), [(i, i ^ mask) for i in range(DP * MP)])  93.4 us
    ppermute x27, waiting for transfers between devices, swap(): lax.ppermute(array, ('dp', 'mp'), [(i, i ^ mask) for i in range(DP * MP)])  49.4 us
    all_to_all x1, blocking collectives, per_device(): lax.all_to_all(jnp.stack([part for part in blocks for _ in range(DP // X...  22.8 us
    all_gather x1, waiting for transfers between devices, per_device(): columns = lax.all_gather(slices, 'mp', axis=0, axis_index_groups=GROUPS)  11.3 us
    all_to_all x1, waiting for transfers between devices, per_device(): lax.all_to_all(projected.reshape(DP, block, views * images), 'dp', split_...  11.2 us
    all_to_all x1, starting transfers between devices, per_device(): lax.all_to_all(projected.reshape(DP, block, views * images), 'dp', split_...  6.39 us
  transfers between devices with their start and end apart: 32, of which 20 were waited for; matrix products, arithmetic and copies ran while one was open for 4% of the time, Pallas kernels for 1%

profile of v16, /device:TPU:1, one launch (start us, length us, event | category | flops | bytes accessed | tf_op | source)
XLA Modules:
  0.0 250.5 jit_solution(7859085805225445704)
XLA Ops:
  6.5 8.4 %collective-permute-start = (bf16[256,256]{1,0:T(8,128)(2,1)}, bf16[256,256]{1,0:T(8,128)(2,1)S(1)}, u32[]{:S(2)}, u32[]{:S(2)}) collective-permute-start(bf16[256,256]{1,0:T(8,128)(2,1)} %param.7), channel_id=1, source_target_pairs={{0,96},{1,97},{2,98},{3,99},{4,100},{5,101},{6,102},{7,103},{8,104... | collective-permute-start | bytes 393224 | tf_op jit(solution)/shard_map/ppermute | solution.py:30
  19.1 6.7 %collective-permute-done.1 = bf16[256,256]{1,0:T(8,128)(2,1)S(1)} collective-permute-done((bf16[256,256]{1,0:T(8,128)(2,1)}, bf16[256,256]{1,0:T(8,128)(2,1)S(1)}, u32[]{:S(2)}, u32[]{:S(2)}) %collective-permute-start.1) | collective-permute-done | bytes 131104 | tf_op jit(solution)/shard_map/ppermute | solution.py:30
  26.9 5.1 %collective-permute-start.3 = (bf16[4,256,256]{2,1,0:T(8,128)(2,1)S(1)}, bf16[4,256,256]{2,1,0:T(8,128)(2,1)S(1)}, u32[]{:S(2)}, u32[]{:S(2)}) collective-permute-start(bf16[4,256,256]{2,1,0:T(8,128)(2,1)S(1)} %get-tuple-element.66), channel_id=1, source_target_pairs={{0,256},{1,257},{2,258},{3,259},{4,260},{5,261},{6,262},{7,263},{8... | collective-permute-start | bytes 1572872 | tf_op jit(solution)/shard_map/ppermute | solution.py:30
  36.7 5.5 %collective-permute-done.3 = bf16[4,256,256]{2,1,0:T(8,128)(2,1)S(1)} collective-permute-done((bf16[4,256,256]{2,1,0:T(8,128)(2,1)S(1)}, bf16[4,256,256]{2,1,0:T(8,128)(2,1)S(1)}, u32[]{:S(2)}, u32[]{:S(2)}) %collective-permute-start.3) | collective-permute-done | bytes 524320 | tf_op jit(solution)/shard_map/ppermute | solution.py:30
  42.2 11.9 %collective-permute-done.4 = bf16[4,256,256]{2,1,0:T(8,128)(2,1)S(1)} collective-permute-done((bf16[4,256,256]{2,1,0:T(8,128)(2,1)S(1)}, bf16[4,256,256]{2,1,0:T(8,128)(2,1)S(1)}, u32[]{:S(2)}, u32[]{:S(2)}) %collective-permute-start.4) | collective-permute-done | bytes 524320 | tf_op jit(solution)/shard_map/ppermute | solution.py:30
  62.5 3.1 %shard_map.65 = f32[256,256]{1,0:T(8,128)} custom-call(s32[16]{0:T(128)S(1)} %get-tuple-element.89.order_ref, bf16[256,8192]{1,0:T(8,128)(2,1)S(1)} %bitcast.220, bf16[16,256,256]{2,1,0:T(8,128)(2,1)} %bitcast.9.weight_ref, f32[256,256]{1,0:T(8,128)S(1)} %shard_map.64.refs_0_), custom_call_target="tpu_custom_call" | custom-call | flops 536870912 | bytes 6291456 | tf_op jit(solution)/shard_map/pallas_call | solution.py:64
  65.6 6.4 %all-to-all-start = ((f32[32,8,256]{2,1,0:T(8,128)}), f32[32,8,256]{2,1,0:T(8,128)S(1)}, u32[]{:S(2)}, u32[]{:S(2)}) async-start(f32[32,8,256]{2,1,0:T(8,128)} %bitcast.11), calls=%async_computation | async-start | bytes 524288 | tf_op jit(solution)/shard_map/all_to_all | solution.py:162
  72.1 11.2 %all-to-all-done = f32[32,8,256]{2,1,0:T(8,128)S(1)} async-done(((f32[32,8,256]{2,1,0:T(8,128)}), f32[32,8,256]{2,1,0:T(8,128)S(1)}, u32[]{:S(2)}, u32[]{:S(2)}) %all-to-all-start) | async-done | bytes 262176 | tf_op jit(solution)/shard_map/all_to_all | solution.py:162
  90.0 7.9 %collective-permute-start.8 = (bf16[8,4096]{1,0:T(8,128)(2,1)S(1)}, bf16[8,4096]{1,0:T(8,128)(2,1)S(1)}, u32[]{:S(2)}, u32[]{:S(2)}) collective-permute-start(bf16[8,4096]{1,0:T(8,128)(2,1)S(1)} %get-tuple-element.33), channel_id=1, source_target_pairs={{0,8},{1,9},{2,10},{3,11},{4,12},{5,13},{6,14},{7,15},{8,0},{9,1},... | collective-permute-start | bytes 196616 | tf_op jit(solution)/shard_map/ppermute | solution.py:30
  102.2 4.9 %all-to-all-start.1 = ((bf16[8,32,1024]{2,1,0:T(8,128)(2,1)}), bf16[8,32,1024]{2,1,0:T(8,128)(2,1)S(1)}, u32[]{:S(2)}, u32[]{:S(2)}) async-start(bf16[8,32,1024]{2,1,0:T(8,128)(2,1)} %reshape.117), calls=%async_computation.1 | async-start | bytes 1048576 | tf_op jit(solution)/shard_map/all_to_all | solution.py:175
  112.8 3.7 %collective-permute-start.13 = (bf16[4,8,4096]{2,1,0:T(8,128)(2,1)S(1)}, bf16[4,8,4096]{2,1,0:T(8,128)(2,1)S(1)}, u32[]{:S(2)}, u32[]{:S(2)}) collective-permute-start(bf16[4,8,4096]{2,1,0:T(8,128)(2,1)S(1)} %get-tuple-element.74), channel_id=1, source_target_pairs={{0,384},{1,385},{2,386},{3,387},{4,388},{5,389},{6,390},{7,391},{8... | collective-permute-start | bytes 786440 | tf_op jit(solution)/shard_map/ppermute | solution.py:30
  116.6 4.1 %collective-permute-done.12 = bf16[4,8,4096]{2,1,0:T(8,128)(2,1)S(1)} collective-permute-done((bf16[4,8,4096]{2,1,0:T(8,128)(2,1)S(1)}, bf16[4,8,4096]{2,1,0:T(8,128)(2,1)S(1)}, u32[]{:S(2)}, u32[]{:S(2)}) %collective-permute-start.12) | collective-permute-done | bytes 262176 | tf_op jit(solution)/shard_map/ppermute | solution.py:30
  120.7 3.6 %collective-permute-done.13 = bf16[4,8,4096]{2,1,0:T(8,128)(2,1)S(1)} collective-permute-done((bf16[4,8,4096]{2,1,0:T(8,128)(2,1)S(1)}, bf16[4,8,4096]{2,1,0:T(8,128)(2,1)S(1)}, u32[]{:S(2)}, u32[]{:S(2)}) %collective-permute-start.13) | collective-permute-done | bytes 262176 | tf_op jit(solution)/shard_map/ppermute | solution.py:30
  124.4 3.1 %all-gather.5.cloned.1.call-done = bf16[16,8,4096]{2,1,0:T(8,128)(2,1)} async-done(((bf16[2,8,4096]{2,1,0:T(8,128)(2,1)}), bf16[16,8,4096]{2,1,0:T(8,128)(2,1)}) %all-gather.5.cloned.1.call-update) | async-done | bytes 1048592 | tf_op jit(solution)/shard_map/all_gather | solution.py:178
  127.5 6.5 %collective-permute-start.14 = (bf16[4,4,8,4096]{3,2,1,0:T(8,128)(2,1)S(1)}, bf16[4,4,8,4096]{3,2,1,0:T(8,128)(2,1)S(1)}, u32[]{:S(2)}, u32[]{:S(2)}) collective-permute-start(bf16[4,4,8,4096]{3,2,1,0:T(8,128)(2,1)S(1)} %pad_maximum_fusion.1), channel_id=1, source_target_pairs={{0,16},{1,17},{2,18},{3,19},{4,20},{5,21},{6,22},{7,23},{8,24},{9,... | collective-permute-start | bytes 3145736 | tf_op jit(solution)/shard_map/ppermute | solution.py:30
  140.6 3.3 %collective-permute-start.22 = (bf16[64,4096]{1,0:T(8,128)(2,1)}, bf16[64,4096]{1,0:T(8,128)(2,1)}, u32[]{:S(2)}, u32[]{:S(2)}) collective-permute-start(bf16[64,4096]{1,0:T(8,128)(2,1)} %fusion.5), channel_id=1, source_target_pairs={{0,32},{1,33},{2,34},{3,35},{4,36},{5,37},{6,38},{7,39},{8,40},{9,... | collective-permute-start | bytes 1572872 | tf_op jit(solution)/shard_map/ppermute | solution.py:30
  145.4 4.6 %collective-permute-start.16 = (bf16[4,8,4096]{2,1,0:T(8,128)(2,1)}, bf16[4,8,4096]{2,1,0:T(8,128)(2,1)}, u32[]{:S(2)}, u32[]{:S(2)}) collective-permute-start(bf16[4,8,4096]{2,1,0:T(8,128)(2,1)} %get-tuple-element.63), channel_id=1, source_target_pairs={{0,256},{1,257},{2,258},{3,259},{4,260},{5,261},{6,262},{7,263},{8... | collective-permute-start | bytes 786440 | tf_op jit(solution)/shard_map/ppermute | solution.py:30
  158.3 4.2 %all-to-all-start.2 = ((bf16[8,8,4096]{2,1,0:T(8,128)(2,1)}), bf16[8,8,4096]{2,1,0:T(8,128)(2,1)S(1)}, u32[]{:S(2)}, u32[]{:S(2)}) async-start(bf16[8,8,4096]{2,1,0:T(8,128)(2,1)} %fusion.6), calls=%async_computation.2 | async-start | bytes 1048576 | tf_op jit(solution)/shard_map/all_to_all | solution.py:217
  163.9 7.6 %collective-permute-start.19 = (bf16[8,4096]{1,0:T(8,128)(2,1)S(1)}, bf16[8,4096]{1,0:T(8,128)(2,1)S(1)}, u32[]{:S(2)}, u32[]{:S(2)}) collective-permute-start(bf16[8,4096]{1,0:T(8,128)(2,1)S(1)} %get-tuple-element.71), channel_id=1, source_target_pairs={{0,8},{1,9},{2,10},{3,11},{4,12},{5,13},{6,14},{7,15},{8,0},{9,1},... | collective-permute-start | bytes 196616 | tf_op jit(solution)/shard_map/ppermute | solution.py:30
  178.5 2.9 %collective-permute-done.21 = bf16[8,4096]{1,0:T(8,128)(2,1)S(1)} collective-permute-done((bf16[8,4096]{1,0:T(8,128)(2,1)S(1)}, bf16[8,4096]{1,0:T(8,128)(2,1)S(1)}, u32[]{:S(2)}, u32[]{:S(2)}) %collective-permute-start.21) | collective-permute-done | bytes 65568 | tf_op jit(solution)/shard_map/ppermute | solution.py:30
  183.8 22.8 %all_to_all.20 = bf16[16,8,2048]{2,1,0:T(8,128)(2,1)S(1)} all-to-all(bf16[16,8,2048]{2,1,0:T(8,128)(2,1)S(1)} %constant_dynamic-update-slice_fusion), channel_id=1, replica_groups={{0,32,64,96,128,160,192,224,256,288,320,352,384,416,448,480},{16,48,80,..., dimensions={0} | all-to-all | bytes 1048576 | tf_op jit(solution)/shard_map/all_to_all | solution.py:238
  206.6 11.3 %all-gather.7.cloned.1.call-done = bf16[64,32,1024]{2,1,0:T(8,128)(2,1)} async-done(((bf16[8,32,1024]{2,1,0:T(8,128)(2,1)}), bf16[64,32,1024]{2,1,0:T(8,128)(2,1)}) %all-gather.7.cloned.1.call-update) | async-done | bytes 4194320 | tf_op jit(solution)/shard_map/all_gather | solution.py:182
  225.1 4.6 %collective-permute-start.24 = (f32[256,256]{1,0:T(8,128)S(1)}, f32[256,256]{1,0:T(8,128)S(1)}, u32[]{:S(2)}, u32[]{:S(2)}) collective-permute-start(f32[256,256]{1,0:T(8,128)S(1)} %get-tuple-element.58), channel_id=1, source_target_pairs={{0,256},{1,257},{2,258},{3,259},{4,260},{5,261},{6,262},{7,263},{8... | collective-permute-start | bytes 786440 | tf_op jit(solution)/shard_map/ppermute | solution.py:30
  236.4 5.5 %collective-permute-done.25.refs_2_ = f32[256,256]{1,0:T(8,128)S(1)} collective-permute-done((f32[256,256]{1,0:T(8,128)S(1)}, f32[256,256]{1,0:T(8,128)S(1)}, u32[]{:S(2)}, u32[]{:S(2)}) %collective-permute-start.25) | collective-permute-done | bytes 262176 | tf_op jit(solution)/shard_map/ppermute | solution.py:30
  (124 shorter events, 77.2 us)
Async XLA Ops:
  6.5 12.6 %collective-permute-start = (bf16[256,256]{1,0:T(8,128)(2,1)}, bf16[256,256]{1,0:T(8,128)(2,1)S(1)}, u32[]{:S(2)}, u32[]{:S(2)}) collective-permute-start(bf16[256,256]{1,0:T(8,128)(2,1)} %param.7), channel_id=1, source_target_pairs={{0,96},{1,97},{2,98},{3,99},{4,100},{5,101},{6,102},{7,103},{8,104... | collective-permute-start | bytes 393224 | tf_op jit(solution)/shard_map/ppermute | solution.py:30
  15.0 10.9 %collective-permute-start.1 = (bf16[256,256]{1,0:T(8,128)(2,1)}, bf16[256,256]{1,0:T(8,128)(2,1)S(1)}, u32[]{:S(2)}, u32[]{:S(2)}) collective-permute-start(bf16[256,256]{1,0:T(8,128)(2,1)} %param.7), channel_id=1, source_target_pairs={{0,64},{1,65},{2,66},{3,67},{4,68},{5,69},{6,70},{7,71},{8,72},{9,... | collective-permute-start | bytes 393224 | tf_op jit(solution)/shard_map/ppermute | solution.py:30
  16.9 9.0 %collective-permute-start.2 = (bf16[256,256]{1,0:T(8,128)(2,1)}, bf16[256,256]{1,0:T(8,128)(2,1)S(1)}, u32[]{:S(2)}, u32[]{:S(2)}) collective-permute-start(bf16[256,256]{1,0:T(8,128)(2,1)} %param.7), channel_id=1, source_target_pairs={{0,32},{1,33},{2,34},{3,35},{4,36},{5,37},{6,38},{7,39},{8,40},{9,... | collective-permute-start | bytes 393224 | tf_op jit(solution)/shard_map/ppermute | solution.py:30
  26.9 15.3 %collective-permute-start.3 = (bf16[4,256,256]{2,1,0:T(8,128)(2,1)S(1)}, bf16[4,256,256]{2,1,0:T(8,128)(2,1)S(1)}, u32[]{:S(2)}, u32[]{:S(2)}) collective-permute-start(bf16[4,256,256]{2,1,0:T(8,128)(2,1)S(1)} %get-tuple-element.66), channel_id=1, source_target_pairs={{0,256},{1,257},{2,258},{3,259},{4,260},{5,261},{6,262},{7,263},{8... | collective-permute-start | bytes 1572872 | tf_op jit(solution)/shard_map/ppermute | solution.py:30
  32.0 22.1 %collective-permute-start.4 = (bf16[4,256,256]{2,1,0:T(8,128)(2,1)S(1)}, bf16[4,256,256]{2,1,0:T(8,128)(2,1)S(1)}, u32[]{:S(2)}, u32[]{:S(2)}) collective-permute-start(bf16[4,256,256]{2,1,0:T(8,128)(2,1)S(1)} %get-tuple-element.66), channel_id=1, source_target_pairs={{0,128},{1,129},{2,130},{3,131},{4,132},{5,133},{6,134},{7,135},{8... | collective-permute-start | bytes 1572872 | tf_op jit(solution)/shard_map/ppermute | solution.py:30
  34.2 21.3 %collective-permute-start.5 = (bf16[4,256,256]{2,1,0:T(8,128)(2,1)S(1)}, bf16[4,256,256]{2,1,0:T(8,128)(2,1)S(1)}, u32[]{:S(2)}, u32[]{:S(2)}) collective-permute-start(bf16[4,256,256]{2,1,0:T(8,128)(2,1)S(1)} %get-tuple-element.66), channel_id=1, source_target_pairs={{0,384},{1,385},{2,386},{3,387},{4,388},{5,389},{6,390},{7,391},{8... | collective-permute-start | bytes 1572872 | tf_op jit(solution)/shard_map/ppermute | solution.py:30
  65.6 17.7 %all-to-all-start = ((f32[32,8,256]{2,1,0:T(8,128)}), f32[32,8,256]{2,1,0:T(8,128)S(1)}, u32[]{:S(2)}, u32[]{:S(2)}) async-start(f32[32,8,256]{2,1,0:T(8,128)} %bitcast.11), calls=%async_computation | async-start | bytes 524288 | tf_op jit(solution)/shard_map/all_to_all | solution.py:162
  72.0 55.5 %all-gather.5.cloned.1.call-start = ((), (), s32[]{:S(2)}) async-start(), calls=%async_computation.4 | async-start | bytes 1179648 | tf_op jit(solution)/shard_map/all_gather | solution.py:178
  90.0 17.1 %collective-permute-start.8 = (bf16[8,4096]{1,0:T(8,128)(2,1)S(1)}, bf16[8,4096]{1,0:T(8,128)(2,1)S(1)}, u32[]{:S(2)}, u32[]{:S(2)}) collective-permute-start(bf16[8,4096]{1,0:T(8,128)(2,1)S(1)} %get-tuple-element.33), channel_id=1, source_target_pairs={{0,8},{1,9},{2,10},{3,11},{4,12},{5,13},{6,14},{7,15},{8,0},{9,1},... | collective-permute-start | bytes 196616 | tf_op jit(solution)/shard_map/ppermute | solution.py:30
  98.0 9.2 %collective-permute-start.9 = (bf16[8,4096]{1,0:T(8,128)(2,1)S(1)}, bf16[8,4096]{1,0:T(8,128)(2,1)S(1)}, u32[]{:S(2)}, u32[]{:S(2)}) collective-permute-start(bf16[8,4096]{1,0:T(8,128)(2,1)S(1)} %get-tuple-element.33), channel_id=1, source_target_pairs={{0,64},{1,65},{2,66},{3,67},{4,68},{5,69},{6,70},{7,71},{8,72},{9,... | collective-permute-start | bytes 196616 | tf_op jit(solution)/shard_map/ppermute | solution.py:30
  102.2 22.2 %all-to-all-start.1 = ((bf16[8,32,1024]{2,1,0:T(8,128)(2,1)}), bf16[8,32,1024]{2,1,0:T(8,128)(2,1)S(1)}, u32[]{:S(2)}, u32[]{:S(2)}) async-start(bf16[8,32,1024]{2,1,0:T(8,128)(2,1)} %reshape.117), calls=%async_computation.1 | async-start | bytes 1048576 | tf_op jit(solution)/shard_map/all_to_all | solution.py:175
  107.2 110.7 %all-gather.7.cloned.1.call-start = ((), (), s32[]{:S(2)}) async-start(), calls=%async_computation.5 | async-start | bytes 4718592 | tf_op jit(solution)/shard_map/all_gather | solution.py:182
  107.6 9.0 %collective-permute-start.11 = (bf16[4,8,4096]{2,1,0:T(8,128)(2,1)S(1)}, bf16[4,8,4096]{2,1,0:T(8,128)(2,1)S(1)}, u32[]{:S(2)}, u32[]{:S(2)}) collective-permute-start(bf16[4,8,4096]{2,1,0:T(8,128)(2,1)S(1)} %get-tuple-element.74), channel_id=1, source_target_pairs={{0,256},{1,257},{2,258},{3,259},{4,260},{5,261},{6,262},{7,263},{8... | collective-permute-start | bytes 786440 | tf_op jit(solution)/shard_map/ppermute | solution.py:30
  110.2 10.4 %collective-permute-start.12 = (bf16[4,8,4096]{2,1,0:T(8,128)(2,1)S(1)}, bf16[4,8,4096]{2,1,0:T(8,128)(2,1)S(1)}, u32[]{:S(2)}, u32[]{:S(2)}) collective-permute-start(bf16[4,8,4096]{2,1,0:T(8,128)(2,1)S(1)} %get-tuple-element.74), channel_id=1, source_target_pairs={{0,128},{1,129},{2,130},{3,131},{4,132},{5,133},{6,134},{7,135},{8... | collective-permute-start | bytes 786440 | tf_op jit(solution)/shard_map/ppermute | solution.py:30
  112.8 11.4 %collective-permute-start.13 = (bf16[4,8,4096]{2,1,0:T(8,128)(2,1)S(1)}, bf16[4,8,4096]{2,1,0:T(8,128)(2,1)S(1)}, u32[]{:S(2)}, u32[]{:S(2)}) collective-permute-start(bf16[4,8,4096]{2,1,0:T(8,128)(2,1)S(1)} %get-tuple-element.74), channel_id=1, source_target_pairs={{0,384},{1,385},{2,386},{3,387},{4,388},{5,389},{6,390},{7,391},{8... | collective-permute-start | bytes 786440 | tf_op jit(solution)/shard_map/ppermute | solution.py:30
  140.6 15.6 %collective-permute-start.22 = (bf16[64,4096]{1,0:T(8,128)(2,1)}, bf16[64,4096]{1,0:T(8,128)(2,1)}, u32[]{:S(2)}, u32[]{:S(2)}) collective-permute-start(bf16[64,4096]{1,0:T(8,128)(2,1)} %fusion.5), channel_id=1, source_target_pairs={{0,32},{1,33},{2,34},{3,35},{4,36},{5,37},{6,38},{7,39},{8,40},{9,... | collective-permute-start | bytes 1572872 | tf_op jit(solution)/shard_map/ppermute | solution.py:30
  145.4 17.2 %collective-permute-start.16 = (bf16[4,8,4096]{2,1,0:T(8,128)(2,1)}, bf16[4,8,4096]{2,1,0:T(8,128)(2,1)}, u32[]{:S(2)}, u32[]{:S(2)}) collective-permute-start(bf16[4,8,4096]{2,1,0:T(8,128)(2,1)} %get-tuple-element.63), channel_id=1, source_target_pairs={{0,256},{1,257},{2,258},{3,259},{4,260},{5,261},{6,262},{7,263},{8... | collective-permute-start | bytes 786440 | tf_op jit(solution)/shard_map/ppermute | solution.py:30
  150.0 12.6 %collective-permute-start.17 = (bf16[4,8,4096]{2,1,0:T(8,128)(2,1)}, bf16[4,8,4096]{2,1,0:T(8,128)(2,1)}, u32[]{:S(2)}, u32[]{:S(2)}) collective-permute-start(bf16[4,8,4096]{2,1,0:T(8,128)(2,1)} %get-tuple-element.62), channel_id=1, source_target_pairs={{0,128},{1,129},{2,130},{3,131},{4,132},{5,133},{6,134},{7,135},{8... | collective-permute-start | bytes 786440 | tf_op jit(solution)/shard_map/ppermute | solution.py:30
  152.1 10.5 %collective-permute-start.18 = (bf16[4,8,4096]{2,1,0:T(8,128)(2,1)}, bf16[4,8,4096]{2,1,0:T(8,128)(2,1)}, u32[]{:S(2)}, u32[]{:S(2)}) collective-permute-start(bf16[4,8,4096]{2,1,0:T(8,128)(2,1)} %get-tuple-element.61), channel_id=1, source_target_pairs={{0,384},{1,385},{2,386},{3,387},{4,388},{5,389},{6,390},{7,391},{8... | collective-permute-start | bytes 786440 | tf_op jit(solution)/shard_map/ppermute | solution.py:30
  158.3 24.6 %all-to-all-start.2 = ((bf16[8,8,4096]{2,1,0:T(8,128)(2,1)}), bf16[8,8,4096]{2,1,0:T(8,128)(2,1)S(1)}, u32[]{:S(2)}, u32[]{:S(2)}) async-start(bf16[8,8,4096]{2,1,0:T(8,128)(2,1)} %fusion.6), calls=%async_computation.2 | async-start | bytes 1048576 | tf_op jit(solution)/shard_map/all_to_all | solution.py:217
  163.9 12.1 %collective-permute-start.19 = (bf16[8,4096]{1,0:T(8,128)(2,1)S(1)}, bf16[8,4096]{1,0:T(8,128)(2,1)S(1)}, u32[]{:S(2)}, u32[]{:S(2)}) collective-permute-start(bf16[8,4096]{1,0:T(8,128)(2,1)S(1)} %get-tuple-element.71), channel_id=1, source_target_pairs={{0,8},{1,9},{2,10},{3,11},{4,12},{5,13},{6,14},{7,15},{8,0},{9,1},... | collective-permute-start | bytes 196616 | tf_op jit(solution)/shard_map/ppermute | solution.py:30
  225.1 11.3 %collective-permute-start.24 = (f32[256,256]{1,0:T(8,128)S(1)}, f32[256,256]{1,0:T(8,128)S(1)}, u32[]{:S(2)}, u32[]{:S(2)}) collective-permute-start(f32[256,256]{1,0:T(8,128)S(1)} %get-tuple-element.58), channel_id=1, source_target_pairs={{0,256},{1,257},{2,258},{3,259},{4,260},{5,261},{6,262},{7,263},{8... | collective-permute-start | bytes 786440 | tf_op jit(solution)/shard_map/ppermute | solution.py:30
  229.7 12.2 %collective-permute-start.25 = (f32[256,256]{1,0:T(8,128)S(1)}, f32[256,256]{1,0:T(8,128)S(1)}, u32[]{:S(2)}, u32[]{:S(2)}) collective-permute-start(f32[256,256]{1,0:T(8,128)S(1)} %get-tuple-element.59), channel_id=1, source_target_pairs={{0,128},{1,129},{2,130},{3,131},{4,132},{5,133},{6,134},{7,135},{8... | collective-permute-start | bytes 786440 | tf_op jit(solution)/shard_map/ppermute | solution.py:30
  231.9 10.3 %collective-permute-start.26 = (f32[256,256]{1,0:T(8,128)S(1)}, f32[256,256]{1,0:T(8,128)S(1)}, u32[]{:S(2)}, u32[]{:S(2)}) collective-permute-start(f32[256,256]{1,0:T(8,128)S(1)} %get-tuple-element.60), channel_id=1, source_target_pairs={{0,384},{1,385},{2,386},{3,387},{4,388},{5,389},{6,390},{7,391},{8... | collective-permute-start | bytes 786440 | tf_op jit(solution)/shard_map/ppermute | solution.py:30
  (17 other events, 133.6 us)
Sparse Core Ops, SparseCore 0:
  90.1 37.2 all-gather.4
  155.2 62.5 all-gather.6

commit v17 on v16

--- a/solution.py
+++ b/solution.py
@@ -177,8 +177,8 @@
     )
     columns_b = lax.all_gather(pair, "mp", axis=0, axis_index_groups=GROUPS)
     columns_b = columns_b.reshape(MP * block, total)
-    rows_own = gather(gather(first, STRIDED_Z)[0], ALONG_X)[0]
-    rows_own, columns_b, slices = lax.optimization_barrier((rows_own, columns_b, slices))
+    rows_own, slices = gather(gather(first, STRIDED_Z)[0], ALONG_X, slices)
+    rows_own, columns_b = lax.optimization_barrier((rows_own, columns_b))
     columns = lax.all_gather(slices, "mp", axis=0, axis_index_groups=GROUPS)
     rows_other = swap(rows_own, 1).reshape(feat // 2, total)
     rows_own = rows_own.reshape(feat // 2, total)

time: 252 us -> 246 us (0.976)
  waiting for transfers between devices: 76.5 us -> 70.8 us
  blocking collectives: 22.8 us -> 20.2 us
    all_gather x1, waiting for transfers between devices: 11.3 us -> 0.12 us  [per_device(): columns = lax.all_gather(slices, 'mp', axis=0, axis_index_groups=GROUPS)]
    ppermute x27, waiting for transfers between devices: 49.4 us -> 54.1 us  [swap(): lax.ppermute(array, ('dp', 'mp'), [(i, i ^ mask) for i in range(DP * MP)])]
    all_to_all x1, waiting for transfers between devices: 1.49 us -> 5.32 us  [per_device(): lax.all_to_all(terms_b.reshape(Y, block, total), 'mp', split_axis=0, conc...]
    all_gather x1, waiting for transfers between devices: 3.06 us -> 0.02 us  [per_device(): columns_b = lax.all_gather(pair, 'mp', axis=0, axis_index_groups=GROUPS)]
    all_to_all x1, starting transfers between devices: 4.25 us -> 7 us  [per_device(): lax.all_to_all(terms_b.reshape(Y, block, total), 'mp', split_axis=0, conc...]
    all_to_all x1, blocking collectives: 22.8 us -> 20.2 us  [per_device(): lax.all_to_all(jnp.stack([part for part in blocks for _ in range(DP // X...]
  transfers between devices with their start and end apart: 32 -> 32, of which waited for: 20 -> 21; matrix products, arithmetic and copies ran while one was open for 4% -> 4% of each run, Pallas kernels for 1% -> 1%
where the time goes in v17:
time: 246 us; the launch traced here: 244 us
  starting transfers between devices  110 us (45%)
  waiting for transfers between devices  70.8 us (29%)
  blocking collectives  20.2 us (8%)
  between operations  14.1 us (6%)
  Pallas kernels  8.47 us (3%)
  local copies, waits for them, and re-layouts  7.16 us (3%)
  matrix products  6.95 us (3%)
  other arithmetic  6.45 us (3%)
    ppermute x27, starting transfers between devices, swap(): lax.ppermute(array, ('dp', 'mp'), [(i, i ^ mask) for i in range(DP * MP)])  92.7 us
    ppermute x27, waiting for transfers between devices, swap(): lax.ppermute(array, ('dp', 'mp'), [(i, i ^ mask) for i in range(DP * MP)])  54.1 us
    all_to_all x1, blocking collectives, per_device(): lax.all_to_all(jnp.stack([part for part in blocks for _ in range(DP // X...  20.2 us
    all_to_all x1, waiting for transfers between devices, per_device(): lax.all_to_all(projected.reshape(DP, block, views * images), 'dp', split_...  11.2 us
    all_to_all x1, starting transfers between devices, per_device(): lax.all_to_all(terms_b.reshape(Y, block, total), 'mp', split_axis=0, conc...  7 us
    all_to_all x1, starting transfers between devices, per_device(): lax.all_to_all(projected.reshape(DP, block, views * images), 'dp', split_...  6.39 us
    all_to_all x1, waiting for transfers between devices, per_device(): lax.all_to_all(terms_b.reshape(Y, block, total), 'mp', split_axis=0, conc...  5.32 us
  transfers between devices with their start and end apart: 32, of which 21 were waited for; matrix products, arithmetic and copies ran while one was open for 4% of the time, Pallas kernels for 1%

profile of v17, /device:TPU:1, one launch (start us, length us, event | category | flops | bytes accessed | tf_op | source)
XLA Modules:
  0.0 244.5 jit_solution(2740312462239011880)
XLA Ops:
  6.5 8.4 %collective-permute-start = (bf16[256,256]{1,0:T(8,128)(2,1)}, bf16[256,256]{1,0:T(8,128)(2,1)S(1)}, u32[]{:S(2)}, u32[]{:S(2)}) collective-permute-start(bf16[256,256]{1,0:T(8,128)(2,1)} %param.7), channel_id=1, source_target_pairs={{0,96},{1,97},{2,98},{3,99},{4,100},{5,101},{6,102},{7,103},{8,104... | collective-permute-start | bytes 393224 | tf_op jit(solution)/shard_map/ppermute | solution.py:30
  19.1 6.7 %collective-permute-done.1 = bf16[256,256]{1,0:T(8,128)(2,1)S(1)} collective-permute-done((bf16[256,256]{1,0:T(8,128)(2,1)}, bf16[256,256]{1,0:T(8,128)(2,1)S(1)}, u32[]{:S(2)}, u32[]{:S(2)}) %collective-permute-start.1) | collective-permute-done | bytes 131104 | tf_op jit(solution)/shard_map/ppermute | solution.py:30
  26.9 5.1 %collective-permute-start.3 = (bf16[4,256,256]{2,1,0:T(8,128)(2,1)S(1)}, bf16[4,256,256]{2,1,0:T(8,128)(2,1)S(1)}, u32[]{:S(2)}, u32[]{:S(2)}) collective-permute-start(bf16[4,256,256]{2,1,0:T(8,128)(2,1)S(1)} %get-tuple-element.68), channel_id=1, source_target_pairs={{0,256},{1,257},{2,258},{3,259},{4,260},{5,261},{6,262},{7,263},{8... | collective-permute-start | bytes 1572872 | tf_op jit(solution)/shard_map/ppermute | solution.py:30
  36.7 5.5 %collective-permute-done.3 = bf16[4,256,256]{2,1,0:T(8,128)(2,1)S(1)} collective-permute-done((bf16[4,256,256]{2,1,0:T(8,128)(2,1)S(1)}, bf16[4,256,256]{2,1,0:T(8,128)(2,1)S(1)}, u32[]{:S(2)}, u32[]{:S(2)}) %collective-permute-start.3) | collective-permute-done | bytes 524320 | tf_op jit(solution)/shard_map/ppermute | solution.py:30
  42.2 11.9 %collective-permute-done.4 = bf16[4,256,256]{2,1,0:T(8,128)(2,1)S(1)} collective-permute-done((bf16[4,256,256]{2,1,0:T(8,128)(2,1)S(1)}, bf16[4,256,256]{2,1,0:T(8,128)(2,1)S(1)}, u32[]{:S(2)}, u32[]{:S(2)}) %collective-permute-start.4) | collective-permute-done | bytes 524320 | tf_op jit(solution)/shard_map/ppermute | solution.py:30
  65.6 6.4 %all-to-all-start = ((f32[32,8,256]{2,1,0:T(8,128)}), f32[32,8,256]{2,1,0:T(8,128)S(1)}, u32[]{:S(2)}, u32[]{:S(2)}) async-start(f32[32,8,256]{2,1,0:T(8,128)} %bitcast.11), calls=%async_computation | async-start | bytes 524288 | tf_op jit(solution)/shard_map/all_to_all | solution.py:162
  72.1 11.2 %all-to-all-done = f32[32,8,256]{2,1,0:T(8,128)S(1)} async-done(((f32[32,8,256]{2,1,0:T(8,128)}), f32[32,8,256]{2,1,0:T(8,128)S(1)}, u32[]{:S(2)}, u32[]{:S(2)}) %all-to-all-start) | async-done | bytes 262176 | tf_op jit(solution)/shard_map/all_to_all | solution.py:162
  90.0 4.2 %all-to-all-start.1 = ((bf16[8,32,1024]{2,1,0:T(8,128)(2,1)}), bf16[8,32,1024]{2,1,0:T(8,128)(2,1)S(1)}, u32[]{:S(2)}, u32[]{:S(2)}) async-start(bf16[8,32,1024]{2,1,0:T(8,128)(2,1)} %reshape.117), calls=%async_computation.1 | async-start | bytes 1048576 | tf_op jit(solution)/shard_map/all_to_all | solution.py:175
  94.3 7.9 %collective-permute-start.8 = (bf16[8,4096]{1,0:T(8,128)(2,1)S(1)}, bf16[8,4096]{1,0:T(8,128)(2,1)S(1)}, u32[]{:S(2)}, u32[]{:S(2)}) collective-permute-start(bf16[8,4096]{1,0:T(8,128)(2,1)S(1)} %get-tuple-element.34), channel_id=1, source_target_pairs={{0,8},{1,9},{2,10},{3,11},{4,12},{5,13},{6,14},{7,15},{8,0},{9,1},... | collective-permute-start | bytes 196616 | tf_op jit(solution)/shard_map/ppermute | solution.py:30
  102.2 4.2 %collective-permute-start.9 = (bf16[8,4096]{1,0:T(8,128)(2,1)S(1)}, bf16[8,4096]{1,0:T(8,128)(2,1)S(1)}, u32[]{:S(2)}, u32[]{:S(2)}) collective-permute-start(bf16[8,4096]{1,0:T(8,128)(2,1)S(1)} %get-tuple-element.34), channel_id=1, source_target_pairs={{0,64},{1,65},{2,66},{3,67},{4,68},{5,69},{6,70},{7,71},{8,72},{9,... | collective-permute-start | bytes 196616 | tf_op jit(solution)/shard_map/ppermute | solution.py:30
  108.4 4.3 %collective-permute-done.8 = bf16[8,4096]{1,0:T(8,128)(2,1)S(1)} collective-permute-done((bf16[8,4096]{1,0:T(8,128)(2,1)S(1)}, bf16[8,4096]{1,0:T(8,128)(2,1)S(1)}, u32[]{:S(2)}, u32[]{:S(2)}) %collective-permute-start.8) | collective-permute-done | bytes 65568 | tf_op jit(solution)/shard_map/ppermute | solution.py:30
  119.9 3.6 %collective-permute-start.13 = (bf16[4,8,4096]{2,1,0:T(8,128)(2,1)S(1)}, bf16[4,8,4096]{2,1,0:T(8,128)(2,1)S(1)}, u32[]{:S(2)}, u32[]{:S(2)}) collective-permute-start(bf16[4,8,4096]{2,1,0:T(8,128)(2,1)S(1)} %get-tuple-element.76), channel_id=1, source_target_pairs={{0,384},{1,385},{2,386},{3,387},{4,388},{5,389},{6,390},{7,391},{8... | collective-permute-start | bytes 786440 | tf_op jit(solution)/shard_map/ppermute | solution.py:30
  124.0 4.3 %collective-permute-done.12 = bf16[4,8,4096]{2,1,0:T(8,128)(2,1)S(1)} collective-permute-done((bf16[4,8,4096]{2,1,0:T(8,128)(2,1)S(1)}, bf16[4,8,4096]{2,1,0:T(8,128)(2,1)S(1)}, u32[]{:S(2)}, u32[]{:S(2)}) %collective-permute-start.12) | collective-permute-done | bytes 262176 | tf_op jit(solution)/shard_map/ppermute | solution.py:30
  131.5 3.7 %collective-permute-start.14 = (bf16[4,4,8,4096]{3,2,1,0:T(8,128)(2,1)S(1)}, bf16[4,4,8,4096]{3,2,1,0:T(8,128)(2,1)S(1)}, u32[]{:S(2)}, u32[]{:S(2)}) collective-permute-start(bf16[4,4,8,4096]{3,2,1,0:T(8,128)(2,1)S(1)} %pad_maximum_fusion.1), channel_id=1, source_target_pairs={{0,16},{1,17},{2,18},{3,19},{4,20},{5,21},{6,22},{7,23},{8,24},{9,... | collective-permute-start | bytes 3145736 | tf_op jit(solution)/shard_map/ppermute | solution.py:30
  142.7 3.5 %collective-permute-start.22 = (bf16[64,4096]{1,0:T(8,128)(2,1)}, bf16[64,4096]{1,0:T(8,128)(2,1)S(1)}, u32[]{:S(2)}, u32[]{:S(2)}) collective-permute-start(bf16[64,4096]{1,0:T(8,128)(2,1)} %fusion.5), channel_id=1, source_target_pairs={{0,32},{1,33},{2,34},{3,35},{4,36},{5,37},{6,38},{7,39},{8,40},{9,... | collective-permute-start | bytes 1572872 | tf_op jit(solution)/shard_map/ppermute | solution.py:30
  148.9 3.3 %collective-permute-start.16 = (bf16[4,8,4096]{2,1,0:T(8,128)(2,1)}, bf16[4,8,4096]{2,1,0:T(8,128)(2,1)S(1)}, u32[]{:S(2)}, u32[]{:S(2)}) collective-permute-start(bf16[4,8,4096]{2,1,0:T(8,128)(2,1)} %get-tuple-element.65), channel_id=1, source_target_pairs={{0,256},{1,257},{2,258},{3,259},{4,260},{5,261},{6,262},{7,263},{8... | collective-permute-start | bytes 786440 | tf_op jit(solution)/shard_map/ppermute | solution.py:30
  159.7 7.0 %all-to-all-start.2 = ((bf16[8,8,4096]{2,1,0:T(8,128)(2,1)}), bf16[8,8,4096]{2,1,0:T(8,128)(2,1)S(1)}, u32[]{:S(2)}, u32[]{:S(2)}) async-start(bf16[8,8,4096]{2,1,0:T(8,128)(2,1)} %fusion.6), calls=%async_computation.2 | async-start | bytes 1048576 | tf_op jit(solution)/shard_map/all_to_all | solution.py:217
  167.9 7.1 %collective-permute-start.19 = (bf16[8,4096]{1,0:T(8,128)(2,1)S(1)}, bf16[8,4096]{1,0:T(8,128)(2,1)S(1)}, u32[]{:S(2)}, u32[]{:S(2)}) collective-permute-start(bf16[8,4096]{1,0:T(8,128)(2,1)S(1)} %get-tuple-element.73), channel_id=1, source_target_pairs={{0,8},{1,9},{2,10},{3,11},{4,12},{5,13},{6,14},{7,15},{8,0},{9,1},... | collective-permute-start | bytes 196616 | tf_op jit(solution)/shard_map/ppermute | solution.py:30
  184.3 5.3 %all-to-all-done.2 = bf16[8,8,4096]{2,1,0:T(8,128)(2,1)S(1)} async-done(((bf16[8,8,4096]{2,1,0:T(8,128)(2,1)}), bf16[8,8,4096]{2,1,0:T(8,128)(2,1)S(1)}, u32[]{:S(2)}, u32[]{:S(2)}) %all-to-all-start.2) | async-done | bytes 524320 | tf_op jit(solution)/shard_map/all_to_all | solution.py:217
  190.5 20.2 %all_to_all.20 = bf16[16,8,2048]{2,1,0:T(8,128)(2,1)S(1)} all-to-all(bf16[16,8,2048]{2,1,0:T(8,128)(2,1)S(1)} %constant_dynamic-update-slice_fusion), channel_id=1, replica_groups={{0,32,64,96,128,160,192,224,256,288,320,352,384,416,448,480},{16,48,80,..., dimensions={0} | all-to-all | bytes 1048576 | tf_op jit(solution)/shard_map/all_to_all | solution.py:238
  210.8 3.8 %collective-permute-start.23 = (bf16[16,8,2048]{2,1,0:T(8,128)(2,1)S(1)}, bf16[16,8,2048]{2,1,0:T(8,128)(2,1)S(1)}, u32[]{:S(2)}, u32[]{:S(2)}) collective-permute-start(bf16[16,8,2048]{2,1,0:T(8,128)(2,1)S(1)} %all_to_all.20), channel_id=1, source_target_pairs={{0,16},{1,17},{2,18},{3,19},{4,20},{5,21},{6,22},{7,23},{8,24},{9,... | collective-permute-start | bytes 1572872 | tf_op jit(solution)/shard_map/ppermute | solution.py:30
  219.5 3.4 %collective-permute-start.24 = (f32[256,256]{1,0:T(8,128)S(1)}, f32[256,256]{1,0:T(8,128)S(1)}, u32[]{:S(2)}, u32[]{:S(2)}) collective-permute-start(f32[256,256]{1,0:T(8,128)S(1)} %get-tuple-element.60), channel_id=1, source_target_pairs={{0,256},{1,257},{2,258},{3,259},{4,260},{5,261},{6,262},{7,263},{8... | collective-permute-start | bytes 786440 | tf_op jit(solution)/shard_map/ppermute | solution.py:30
  225.1 3.3 %collective-permute-start.26 = (f32[256,256]{1,0:T(8,128)S(1)}, f32[256,256]{1,0:T(8,128)S(1)}, u32[]{:S(2)}, u32[]{:S(2)}) collective-permute-start(f32[256,256]{1,0:T(8,128)S(1)} %get-tuple-element.62), channel_id=1, source_target_pairs={{0,384},{1,385},{2,386},{3,387},{4,388},{5,389},{6,390},{7,391},{8... | collective-permute-start | bytes 786440 | tf_op jit(solution)/shard_map/ppermute | solution.py:30
  230.8 4.5 %collective-permute-done.25.refs_2_ = f32[256,256]{1,0:T(8,128)S(1)} collective-permute-done((f32[256,256]{1,0:T(8,128)S(1)}, f32[256,256]{1,0:T(8,128)S(1)}, u32[]{:S(2)}, u32[]{:S(2)}) %collective-permute-start.25) | collective-permute-done | bytes 262176 | tf_op jit(solution)/shard_map/ppermute | solution.py:30
  (122 shorter events, 81.4 us)
Async XLA Ops:
  6.5 12.6 %collective-permute-start = (bf16[256,256]{1,0:T(8,128)(2,1)}, bf16[256,256]{1,0:T(8,128)(2,1)S(1)}, u32[]{:S(2)}, u32[]{:S(2)}) collective-permute-start(bf16[256,256]{1,0:T(8,128)(2,1)} %param.7), channel_id=1, source_target_pairs={{0,96},{1,97},{2,98},{3,99},{4,100},{5,101},{6,102},{7,103},{8,104... | collective-permute-start | bytes 393224 | tf_op jit(solution)/shard_map/ppermute | solution.py:30
  15.0 10.9 %collective-permute-start.1 = (bf16[256,256]{1,0:T(8,128)(2,1)}, bf16[256,256]{1,0:T(8,128)(2,1)S(1)}, u32[]{:S(2)}, u32[]{:S(2)}) collective-permute-start(bf16[256,256]{1,0:T(8,128)(2,1)} %param.7), channel_id=1, source_target_pairs={{0,64},{1,65},{2,66},{3,67},{4,68},{5,69},{6,70},{7,71},{8,72},{9,... | collective-permute-start | bytes 393224 | tf_op jit(solution)/shard_map/ppermute | solution.py:30
  16.9 9.0 %collective-permute-start.2 = (bf16[256,256]{1,0:T(8,128)(2,1)}, bf16[256,256]{1,0:T(8,128)(2,1)S(1)}, u32[]{:S(2)}, u32[]{:S(2)}) collective-permute-start(bf16[256,256]{1,0:T(8,128)(2,1)} %param.7), channel_id=1, source_target_pairs={{0,32},{1,33},{2,34},{3,35},{4,36},{5,37},{6,38},{7,39},{8,40},{9,... | collective-permute-start | bytes 393224 | tf_op jit(solution)/shard_map/ppermute | solution.py:30
  26.9 15.3 %collective-permute-start.3 = (bf16[4,256,256]{2,1,0:T(8,128)(2,1)S(1)}, bf16[4,256,256]{2,1,0:T(8,128)(2,1)S(1)}, u32[]{:S(2)}, u32[]{:S(2)}) collective-permute-start(bf16[4,256,256]{2,1,0:T(8,128)(2,1)S(1)} %get-tuple-element.68), channel_id=1, source_target_pairs={{0,256},{1,257},{2,258},{3,259},{4,260},{5,261},{6,262},{7,263},{8... | collective-permute-start | bytes 1572872 | tf_op jit(solution)/shard_map/ppermute | solution.py:30
  32.0 22.1 %collective-permute-start.4 = (bf16[4,256,256]{2,1,0:T(8,128)(2,1)S(1)}, bf16[4,256,256]{2,1,0:T(8,128)(2,1)S(1)}, u32[]{:S(2)}, u32[]{:S(2)}) collective-permute-start(bf16[4,256,256]{2,1,0:T(8,128)(2,1)S(1)} %get-tuple-element.68), channel_id=1, source_target_pairs={{0,128},{1,129},{2,130},{3,131},{4,132},{5,133},{6,134},{7,135},{8... | collective-permute-start | bytes 1572872 | tf_op jit(solution)/shard_map/ppermute | solution.py:30
  34.2 21.3 %collective-permute-start.5 = (bf16[4,256,256]{2,1,0:T(8,128)(2,1)S(1)}, bf16[4,256,256]{2,1,0:T(8,128)(2,1)S(1)}, u32[]{:S(2)}, u32[]{:S(2)}) collective-permute-start(bf16[4,256,256]{2,1,0:T(8,128)(2,1)S(1)} %get-tuple-element.68), channel_id=1, source_target_pairs={{0,384},{1,385},{2,386},{3,387},{4,388},{5,389},{6,390},{7,391},{8... | collective-permute-start | bytes 1572872 | tf_op jit(solution)/shard_map/ppermute | solution.py:30
  65.6 17.7 %all-to-all-start = ((f32[32,8,256]{2,1,0:T(8,128)}), f32[32,8,256]{2,1,0:T(8,128)S(1)}, u32[]{:S(2)}, u32[]{:S(2)}) async-start(f32[32,8,256]{2,1,0:T(8,128)} %bitcast.11), calls=%async_computation | async-start | bytes 524288 | tf_op jit(solution)/shard_map/all_to_all | solution.py:162
  72.0 59.5 %all-gather.5.cloned.1.call-start = ((), (), s32[]{:S(2)}) async-start(), calls=%async_computation.4 | async-start | bytes 1179648 | tf_op jit(solution)/shard_map/all_gather | solution.py:178
  90.0 34.0 %all-to-all-start.1 = ((bf16[8,32,1024]{2,1,0:T(8,128)(2,1)}), bf16[8,32,1024]{2,1,0:T(8,128)(2,1)S(1)}, u32[]{:S(2)}, u32[]{:S(2)}) async-start(bf16[8,32,1024]{2,1,0:T(8,128)(2,1)} %reshape.117), calls=%async_computation.1 | async-start | bytes 1048576 | tf_op jit(solution)/shard_map/all_to_all | solution.py:175
  94.3 116.5 %all-gather.7.cloned.1.call-start = ((), (), s32[]{:S(2)}) async-start(), calls=%async_computation.5 | async-start | bytes 4718592 | tf_op jit(solution)/shard_map/all_gather | solution.py:182
  94.3 18.4 %collective-permute-start.8 = (bf16[8,4096]{1,0:T(8,128)(2,1)S(1)}, bf16[8,4096]{1,0:T(8,128)(2,1)S(1)}, u32[]{:S(2)}, u32[]{:S(2)}) collective-permute-start(bf16[8,4096]{1,0:T(8,128)(2,1)S(1)} %get-tuple-element.34), channel_id=1, source_target_pairs={{0,8},{1,9},{2,10},{3,11},{4,12},{5,13},{6,14},{7,15},{8,0},{9,1},... | collective-permute-start | bytes 196616 | tf_op jit(solution)/shard_map/ppermute | solution.py:30
  102.2 12.2 %collective-permute-start.9 = (bf16[8,4096]{1,0:T(8,128)(2,1)S(1)}, bf16[8,4096]{1,0:T(8,128)(2,1)S(1)}, u32[]{:S(2)}, u32[]{:S(2)}) collective-permute-start(bf16[8,4096]{1,0:T(8,128)(2,1)S(1)} %get-tuple-element.34), channel_id=1, source_target_pairs={{0,64},{1,65},{2,66},{3,67},{4,68},{5,69},{6,70},{7,71},{8,72},{9,... | collective-permute-start | bytes 196616 | tf_op jit(solution)/shard_map/ppermute | solution.py:30
  114.5 9.5 %collective-permute-start.11 = (bf16[4,8,4096]{2,1,0:T(8,128)(2,1)S(1)}, bf16[4,8,4096]{2,1,0:T(8,128)(2,1)S(1)}, u32[]{:S(2)}, u32[]{:S(2)}) collective-permute-start(bf16[4,8,4096]{2,1,0:T(8,128)(2,1)S(1)} %get-tuple-element.76), channel_id=1, source_target_pairs={{0,256},{1,257},{2,258},{3,259},{4,260},{5,261},{6,262},{7,263},{8... | collective-permute-start | bytes 786440 | tf_op jit(solution)/shard_map/ppermute | solution.py:30
  117.6 10.8 %collective-permute-start.12 = (bf16[4,8,4096]{2,1,0:T(8,128)(2,1)S(1)}, bf16[4,8,4096]{2,1,0:T(8,128)(2,1)S(1)}, u32[]{:S(2)}, u32[]{:S(2)}) collective-permute-start(bf16[4,8,4096]{2,1,0:T(8,128)(2,1)S(1)} %get-tuple-element.76), channel_id=1, source_target_pairs={{0,128},{1,129},{2,130},{3,131},{4,132},{5,133},{6,134},{7,135},{8... | collective-permute-start | bytes 786440 | tf_op jit(solution)/shard_map/ppermute | solution.py:30
  119.9 11.4 %collective-permute-start.13 = (bf16[4,8,4096]{2,1,0:T(8,128)(2,1)S(1)}, bf16[4,8,4096]{2,1,0:T(8,128)(2,1)S(1)}, u32[]{:S(2)}, u32[]{:S(2)}) collective-permute-start(bf16[4,8,4096]{2,1,0:T(8,128)(2,1)S(1)} %get-tuple-element.76), channel_id=1, source_target_pairs={{0,384},{1,385},{2,386},{3,387},{4,388},{5,389},{6,390},{7,391},{8... | collective-permute-start | bytes 786440 | tf_op jit(solution)/shard_map/ppermute | solution.py:30
  142.7 15.8 %collective-permute-start.22 = (bf16[64,4096]{1,0:T(8,128)(2,1)}, bf16[64,4096]{1,0:T(8,128)(2,1)S(1)}, u32[]{:S(2)}, u32[]{:S(2)}) collective-permute-start(bf16[64,4096]{1,0:T(8,128)(2,1)} %fusion.5), channel_id=1, source_target_pairs={{0,32},{1,33},{2,34},{3,35},{4,36},{5,37},{6,38},{7,39},{8,40},{9,... | collective-permute-start | bytes 1572872 | tf_op jit(solution)/shard_map/ppermute | solution.py:30
  148.9 17.8 %collective-permute-start.16 = (bf16[4,8,4096]{2,1,0:T(8,128)(2,1)}, bf16[4,8,4096]{2,1,0:T(8,128)(2,1)S(1)}, u32[]{:S(2)}, u32[]{:S(2)}) collective-permute-start(bf16[4,8,4096]{2,1,0:T(8,128)(2,1)} %get-tuple-element.65), channel_id=1, source_target_pairs={{0,256},{1,257},{2,258},{3,259},{4,260},{5,261},{6,262},{7,263},{8... | collective-permute-start | bytes 786440 | tf_op jit(solution)/shard_map/ppermute | solution.py:30
  152.1 14.6 %collective-permute-start.17 = (bf16[4,8,4096]{2,1,0:T(8,128)(2,1)S(1)}, bf16[4,8,4096]{2,1,0:T(8,128)(2,1)}, u32[]{:S(2)}, u32[]{:S(2)}) collective-permute-start(bf16[4,8,4096]{2,1,0:T(8,128)(2,1)S(1)} %get-tuple-element.64), channel_id=1, source_target_pairs={{0,128},{1,129},{2,130},{3,131},{4,132},{5,133},{6,134},{7,135},{8... | collective-permute-start | bytes 786440 | tf_op jit(solution)/shard_map/ppermute | solution.py:30
  154.6 12.1 %collective-permute-start.18 = (bf16[4,8,4096]{2,1,0:T(8,128)(2,1)S(1)}, bf16[4,8,4096]{2,1,0:T(8,128)(2,1)}, u32[]{:S(2)}, u32[]{:S(2)}) collective-permute-start(bf16[4,8,4096]{2,1,0:T(8,128)(2,1)S(1)} %get-tuple-element.63), channel_id=1, source_target_pairs={{0,384},{1,385},{2,386},{3,387},{4,388},{5,389},{6,390},{7,391},{8... | collective-permute-start | bytes 786440 | tf_op jit(solution)/shard_map/ppermute | solution.py:30
  159.7 30.0 %all-to-all-start.2 = ((bf16[8,8,4096]{2,1,0:T(8,128)(2,1)}), bf16[8,8,4096]{2,1,0:T(8,128)(2,1)S(1)}, u32[]{:S(2)}, u32[]{:S(2)}) async-start(bf16[8,8,4096]{2,1,0:T(8,128)(2,1)} %fusion.6), calls=%async_computation.2 | async-start | bytes 1048576 | tf_op jit(solution)/shard_map/all_to_all | solution.py:217
  167.9 11.4 %collective-permute-start.19 = (bf16[8,4096]{1,0:T(8,128)(2,1)S(1)}, bf16[8,4096]{1,0:T(8,128)(2,1)S(1)}, u32[]{:S(2)}, u32[]{:S(2)}) collective-permute-start(bf16[8,4096]{1,0:T(8,128)(2,1)S(1)} %get-tuple-element.73), channel_id=1, source_target_pairs={{0,8},{1,9},{2,10},{3,11},{4,12},{5,13},{6,14},{7,15},{8,0},{9,1},... | collective-permute-start | bytes 196616 | tf_op jit(solution)/shard_map/ppermute | solution.py:30
  219.5 11.3 %collective-permute-start.24 = (f32[256,256]{1,0:T(8,128)S(1)}, f32[256,256]{1,0:T(8,128)S(1)}, u32[]{:S(2)}, u32[]{:S(2)}) collective-permute-start(f32[256,256]{1,0:T(8,128)S(1)} %get-tuple-element.60), channel_id=1, source_target_pairs={{0,256},{1,257},{2,258},{3,259},{4,260},{5,261},{6,262},{7,263},{8... | collective-permute-start | bytes 786440 | tf_op jit(solution)/shard_map/ppermute | solution.py:30
  222.9 12.4 %collective-permute-start.25 = (f32[256,256]{1,0:T(8,128)S(1)}, f32[256,256]{1,0:T(8,128)S(1)}, u32[]{:S(2)}, u32[]{:S(2)}) collective-permute-start(f32[256,256]{1,0:T(8,128)S(1)} %get-tuple-element.61), channel_id=1, source_target_pairs={{0,128},{1,129},{2,130},{3,131},{4,132},{5,133},{6,134},{7,135},{8... | collective-permute-start | bytes 786440 | tf_op jit(solution)/shard_map/ppermute | solution.py:30
  225.1 11.0 %collective-permute-start.26 = (f32[256,256]{1,0:T(8,128)S(1)}, f32[256,256]{1,0:T(8,128)S(1)}, u32[]{:S(2)}, u32[]{:S(2)}) collective-permute-start(f32[256,256]{1,0:T(8,128)S(1)} %get-tuple-element.62), channel_id=1, source_target_pairs={{0,384},{1,385},{2,386},{3,387},{4,388},{5,389},{6,390},{7,391},{8... | collective-permute-start | bytes 786440 | tf_op jit(solution)/shard_map/ppermute | solution.py:30
  (16 other events, 120.6 us)
Sparse Core Ops, SparseCore 0:
  90.1 37.1 all-gather.4
  142.8 67.8 all-gather.6

commit v18 on v17

--- a/solution.py
+++ b/solution.py
@@ -47,33 +47,35 @@
     return sum(part.astype(jnp.float32) for part in parts), *later
 
 
-def project_kernel(last, order_ref, inputs_ref, weight_ref, *refs):
+def project_kernel(last, order_ref, inputs_ref, own_ref, other_ref, *refs):
     out_ref = refs[-1]
-    blocks, depth, _ = weight_ref.shape
+    blocks, depth, _ = own_ref.shape
     result = refs[0][...] if last else None
-    for k in range(blocks):
-        columns = pl.ds(pl.multiple_of(order_ref[k] * depth, depth), depth)
-        part = jnp.dot(inputs_ref[:, columns], weight_ref[k], preferred_element_type=jnp.float32)
-        result = part if result is None else result + part
+    for core, weight_ref in enumerate((own_ref, other_ref)):
+        for k in range(blocks):
+            start = pl.multiple_of(order_ref[core * blocks + k] * depth, depth)
+            part = jnp.dot(
+                inputs_ref[:, pl.ds(start, depth)], weight_ref[k], preferred_element_type=jnp.float32
+            )
+            result = part if result is None else result + part
     out_ref[...] = result.T if last else result
 
 
-def project(order, inputs, weight, before=None):
-    rows, feat = inputs.shape[0], weight.shape[2]
-    operands = (inputs, weight) if before is None else (inputs, weight, before)
+def project(order, inputs, own, other, *before):
+    rows, feat = inputs.shape[0], own.shape[2]
+    vmem = pl.BlockSpec(memory_space=pltpu.VMEM)
     return pl.pallas_call(
-        functools.partial(project_kernel, before is not None),
-        in_specs=[pl.BlockSpec(memory_space=pltpu.SMEM)]
-        + [pl.BlockSpec(memory_space=pltpu.VMEM)] * len(operands),
-        out_specs=pl.BlockSpec(memory_space=pltpu.VMEM),
-        out_shape=jax.ShapeDtypeStruct((rows, feat) if before is None else (feat, rows), jnp.float32),
+        functools.partial(project_kernel, bool(before)),
+        in_specs=[pl.BlockSpec(memory_space=pltpu.SMEM)] + [vmem] * (3 + len(before)),
+        out_specs=vmem,
+        out_shape=jax.ShapeDtypeStruct((feat, rows) if before else (rows, feat), jnp.float32),
         compiler_params=pltpu.CompilerParams(vmem_limit_bytes=16 * 1024 * 1024),
         cost_estimate=pl.CostEstimate(
-            flops=2 * rows * feat * weight.shape[0] * weight.shape[1],
+            flops=4 * rows * feat * own.shape[0] * own.shape[1],
             bytes_accessed=6 * 1024 * 1024,
             transcendentals=0,
         ),
-    )(order, *operands)
+    )(order, inputs, own, other, *before)
 
 
 def weight_kernel(targets_ref, grad_ref, columns_ref, *refs):
@@ -147,17 +149,23 @@
 
     place = np.arange(DP)
     distance = place >> 4 | X_SLOTS[place >> 2 & 3] << 3 | Z_SLOTS[place & 3] << 1
-    order = data_index ^ jnp.asarray(distance, jnp.int32)
     position = (data_index & 1 ^ jnp.asarray(place & 1, jnp.int32)) << 4 | jnp.asarray(place >> 1, jnp.int32)
 
     share = views * images // Y
     mine = lax.dynamic_slice_in_dim(flat, lax.rem(model_index, Y) * share, share, axis=0)
     pieces = mine.reshape(share, X, DP // X, rows).transpose(2, 0, 1, 3).reshape(DP // X, share, X * rows)
-    weight_own = gather(gather(weight, ALONG_Z)[0], ALONG_X)[0]
-    weight_other = swap(weight_own, 1)
-    half = (DP // 2, rows, feat)
-    projected = project(order[: DP // 2], flat, weight_own.reshape(half))
-    projected = project(order[DP // 2 :], flat, weight_other.reshape(half), projected)
+    along_z = gather(weight, ALONG_Z)[0]
+    parts = [along_z] + [swap(along_z, *mask) for mask in ALONG_X]
+    projected = ()
+    for k in (0, 2):
+        weight_own = jnp.stack(parts[k : k + 2])
+        weight_other = swap(weight_own, 1)
+        blocks = np.concatenate([4 * k + np.arange(8), 16 + 4 * k + np.arange(8)])
+        half = (DP // 4, rows, feat)
+        order = data_index ^ jnp.asarray(distance[blocks], jnp.int32)
+        halves = weight_own.reshape(half), weight_other.reshape(half)
+        projected = (project(order, flat, *halves, *projected),)
+    projected = projected[0]
 
     own = lax.all_to_all(
         projected.reshape(DP, block, views * images), "dp", split_axis=0, concat_axis=0

time: 246 us -> 245 us (level)
  waiting for transfers between devices: 70.8 us -> 63.4 us
  starting transfers between devices: 110 us -> 117 us
    ppermute x27 -> x28, waiting for transfers between devices: 54.1 us -> 46.7 us  [swap(): lax.ppermute(array, ('dp', 'mp'), [(i, i ^ mask) for i in range(DP * MP)])]
    ppermute x27 -> x28, starting transfers between devices: 92.7 us -> 99.6 us  [swap(): lax.ppermute(array, ('dp', 'mp'), [(i, i ^ mask) for i in range(DP * MP)])]
  transfers between devices with their start and end apart: 32 -> 33, of which waited for: 21 -> 20; matrix products, arithmetic and copies ran while one was open for 4% -> 4% of each run, Pallas kernels for 1% -> 1%
where the time goes in v18:
time: 245 us; the launch traced here: 243 us
  starting transfers between devices  117 us (48%)
  waiting for transfers between devices  63.4 us (26%)
  blocking collectives  20.3 us (8%)
  between operations  14.2 us (6%)
  Pallas kernels  8.11 us (3%)
  local copies, waits for them, and re-layouts  7.08 us (3%)
  matrix products  6.93 us (3%)
  other arithmetic  6.39 us (3%)
    ppermute x28, starting transfers between devices, swap(): lax.ppermute(array, ('dp', 'mp'), [(i, i ^ mask) for i in range(DP * MP)])  99.6 us
    ppermute x28, waiting for transfers between devices, swap(): lax.ppermute(array, ('dp', 'mp'), [(i, i ^ mask) for i in range(DP * MP)])  46.7 us
    all_to_all x1, blocking collectives, per_device(): lax.all_to_all(jnp.stack([part for part in blocks for _ in range(DP // X...  20.3 us
    all_to_all x1, waiting for transfers between devices, per_device(): lax.all_to_all(projected.reshape(DP, block, views * images), 'dp', split_...  11.2 us
    all_to_all x1, starting transfers between devices, per_device(): lax.all_to_all(terms_b.reshape(Y, block, total), 'mp', split_axis=0, conc...  6.99 us
    all_to_all x1, starting transfers between devices, per_device(): lax.all_to_all(projected.reshape(DP, block, views * images), 'dp', split_...  6.13 us
    all_to_all x1, waiting for transfers between devices, per_device(): lax.all_to_all(terms_b.reshape(Y, block, total), 'mp', split_axis=0, conc...  5.32 us
  transfers between devices with their start and end apart: 33, of which 20 were waited for; matrix products, arithmetic and copies ran while one was open for 4% of the time, Pallas kernels for 1%

profile of v18, /device:TPU:1, one launch (start us, length us, event | category | flops | bytes accessed | tf_op | source)
XLA Modules:
  0.0 243.3 jit_solution(16239997592301157276)
XLA Ops:
  6.5 8.4 %collective-permute-start = (bf16[256,256]{1,0:T(8,128)(2,1)}, bf16[256,256]{1,0:T(8,128)(2,1)S(1)}, u32[]{:S(2)}, u32[]{:S(2)}) collective-permute-start(bf16[256,256]{1,0:T(8,128)(2,1)} %param.8), channel_id=1, source_target_pairs={{0,96},{1,97},{2,98},{3,99},{4,100},{5,101},{6,102},{7,103},{8,104... | collective-permute-start | bytes 393224 | tf_op jit(solution)/shard_map/ppermute | solution.py:30
  19.1 6.7 %collective-permute-done.1 = bf16[256,256]{1,0:T(8,128)(2,1)S(1)} collective-permute-done((bf16[256,256]{1,0:T(8,128)(2,1)}, bf16[256,256]{1,0:T(8,128)(2,1)S(1)}, u32[]{:S(2)}, u32[]{:S(2)}) %collective-permute-start.1) | collective-permute-done | bytes 131104 | tf_op jit(solution)/shard_map/ppermute | solution.py:30
  26.9 5.1 %collective-permute-start.6 = (bf16[4,256,256]{2,1,0:T(8,128)(2,1)S(1)}, bf16[4,256,256]{2,1,0:T(8,128)(2,1)S(1)}, u32[]{:S(2)}, u32[]{:S(2)}) collective-permute-start(bf16[4,256,256]{2,1,0:T(8,128)(2,1)S(1)} %get-tuple-element.68), channel_id=1, source_target_pairs={{0,256},{1,257},{2,258},{3,259},{4,260},{5,261},{6,262},{7,263},{8... | collective-permute-start | bytes 1572872 | tf_op jit(solution)/shard_map/ppermute | solution.py:30
  36.7 5.5 %collective-permute-done.6 = bf16[4,256,256]{2,1,0:T(8,128)(2,1)S(1)} collective-permute-done((bf16[4,256,256]{2,1,0:T(8,128)(2,1)S(1)}, bf16[4,256,256]{2,1,0:T(8,128)(2,1)S(1)}, u32[]{:S(2)}, u32[]{:S(2)}) %collective-permute-start.6) | collective-permute-done | bytes 524320 | tf_op jit(solution)/shard_map/ppermute | solution.py:30
  42.3 6.9 %collective-permute-start.7 = (bf16[2,4,256,256]{3,2,1,0:T(8,128)(2,1)S(1)}, bf16[2,4,256,256]{3,2,1,0:T(8,128)(2,1)S(1)}, u32[]{:S(2)}, u32[]{:S(2)}) collective-permute-start(bf16[2,4,256,256]{3,2,1,0:T(8,128)(2,1)S(1)} %pad_maximum_fusion.1), channel_id=1, source_target_pairs={{0,16},{1,17},{2,18},{3,19},{4,20},{5,21},{6,22},{7,23},{8,24},{9,... | collective-permute-start | bytes 3145736 | tf_op jit(solution)/shard_map/ppermute | solution.py:30
  49.2 4.9 %collective-permute-done.3 = bf16[4,256,256]{2,1,0:T(8,128)(2,1)S(1)} collective-permute-done((bf16[4,256,256]{2,1,0:T(8,128)(2,1)S(1)}, bf16[4,256,256]{2,1,0:T(8,128)(2,1)S(1)}, u32[]{:S(2)}, u32[]{:S(2)}) %collective-permute-start.3) | collective-permute-done | bytes 524320 | tf_op jit(solution)/shard_map/ppermute | solution.py:30
  64.7 6.1 %all-to-all-start = ((f32[32,8,256]{2,1,0:T(8,128)}), f32[32,8,256]{2,1,0:T(8,128)S(1)}, u32[]{:S(2)}, u32[]{:S(2)}) async-start(f32[32,8,256]{2,1,0:T(8,128)} %bitcast.13), calls=%async_computation | async-start | bytes 524288 | tf_op jit(solution)/shard_map/all_to_all | solution.py:170
  70.9 11.2 %all-to-all-done = f32[32,8,256]{2,1,0:T(8,128)S(1)} async-done(((f32[32,8,256]{2,1,0:T(8,128)}), f32[32,8,256]{2,1,0:T(8,128)S(1)}, u32[]{:S(2)}, u32[]{:S(2)}) %all-to-all-start) | async-done | bytes 262176 | tf_op jit(solution)/shard_map/all_to_all | solution.py:170
  88.9 4.2 %all-to-all-start.1 = ((bf16[8,32,1024]{2,1,0:T(8,128)(2,1)}), bf16[8,32,1024]{2,1,0:T(8,128)(2,1)S(1)}, u32[]{:S(2)}, u32[]{:S(2)}) async-start(bf16[8,32,1024]{2,1,0:T(8,128)(2,1)} %reshape.125), calls=%async_computation.1 | async-start | bytes 1048576 | tf_op jit(solution)/shard_map/all_to_all | solution.py:183
  93.1 7.9 %collective-permute-start.9 = (bf16[8,4096]{1,0:T(8,128)(2,1)S(1)}, bf16[8,4096]{1,0:T(8,128)(2,1)S(1)}, u32[]{:S(2)}, u32[]{:S(2)}) collective-permute-start(bf16[8,4096]{1,0:T(8,128)(2,1)S(1)} %get-tuple-element.34), channel_id=1, source_target_pairs={{0,8},{1,9},{2,10},{3,11},{4,12},{5,13},{6,14},{7,15},{8,0},{9,1},... | collective-permute-start | bytes 196616 | tf_op jit(solution)/shard_map/ppermute | solution.py:30
  101.1 4.2 %collective-permute-start.10 = (bf16[8,4096]{1,0:T(8,128)(2,1)S(1)}, bf16[8,4096]{1,0:T(8,128)(2,1)S(1)}, u32[]{:S(2)}, u32[]{:S(2)}) collective-permute-start(bf16[8,4096]{1,0:T(8,128)(2,1)S(1)} %get-tuple-element.34), channel_id=1, source_target_pairs={{0,64},{1,65},{2,66},{3,67},{4,68},{5,69},{6,70},{7,71},{8,72},{9,... | collective-permute-start | bytes 196616 | tf_op jit(solution)/shard_map/ppermute | solution.py:30
  107.2 4.3 %collective-permute-done.9 = bf16[8,4096]{1,0:T(8,128)(2,1)S(1)} collective-permute-done((bf16[8,4096]{1,0:T(8,128)(2,1)S(1)}, bf16[8,4096]{1,0:T(8,128)(2,1)S(1)}, u32[]{:S(2)}, u32[]{:S(2)}) %collective-permute-start.9) | collective-permute-done | bytes 65568 | tf_op jit(solution)/shard_map/ppermute | solution.py:30
  118.7 3.6 %collective-permute-start.14 = (bf16[4,8,4096]{2,1,0:T(8,128)(2,1)S(1)}, bf16[4,8,4096]{2,1,0:T(8,128)(2,1)S(1)}, u32[]{:S(2)}, u32[]{:S(2)}) collective-permute-start(bf16[4,8,4096]{2,1,0:T(8,128)(2,1)S(1)} %get-tuple-element.76), channel_id=1, source_target_pairs={{0,384},{1,385},{2,386},{3,387},{4,388},{5,389},{6,390},{7,391},{8... | collective-permute-start | bytes 786440 | tf_op jit(solution)/shard_map/ppermute | solution.py:30
  122.9 4.3 %collective-permute-done.13 = bf16[4,8,4096]{2,1,0:T(8,128)(2,1)S(1)} collective-permute-done((bf16[4,8,4096]{2,1,0:T(8,128)(2,1)S(1)}, bf16[4,8,4096]{2,1,0:T(8,128)(2,1)S(1)}, u32[]{:S(2)}, u32[]{:S(2)}) %collective-permute-start.13) | collective-permute-done | bytes 262176 | tf_op jit(solution)/shard_map/ppermute | solution.py:30
  130.3 3.7 %collective-permute-start.15 = (bf16[4,4,8,4096]{3,2,1,0:T(8,128)(2,1)S(1)}, bf16[4,4,8,4096]{3,2,1,0:T(8,128)(2,1)S(1)}, u32[]{:S(2)}, u32[]{:S(2)}) collective-permute-start(bf16[4,4,8,4096]{3,2,1,0:T(8,128)(2,1)S(1)} %pad_maximum_fusion.2), channel_id=1, source_target_pairs={{0,16},{1,17},{2,18},{3,19},{4,20},{5,21},{6,22},{7,23},{8,24},{9,... | collective-permute-start | bytes 3145736 | tf_op jit(solution)/shard_map/ppermute | solution.py:30
  141.6 3.5 %collective-permute-start.23 = (bf16[64,4096]{1,0:T(8,128)(2,1)}, bf16[64,4096]{1,0:T(8,128)(2,1)S(1)}, u32[]{:S(2)}, u32[]{:S(2)}) collective-permute-start(bf16[64,4096]{1,0:T(8,128)(2,1)} %fusion.5), channel_id=1, source_target_pairs={{0,32},{1,33},{2,34},{3,35},{4,36},{5,37},{6,38},{7,39},{8,40},{9,... | collective-permute-start | bytes 1572872 | tf_op jit(solution)/shard_map/ppermute | solution.py:30
  158.5 7.0 %all-to-all-start.2 = ((bf16[8,8,4096]{2,1,0:T(8,128)(2,1)}), bf16[8,8,4096]{2,1,0:T(8,128)(2,1)S(1)}, u32[]{:S(2)}, u32[]{:S(2)}) async-start(bf16[8,8,4096]{2,1,0:T(8,128)(2,1)} %fusion.6), calls=%async_computation.2 | async-start | bytes 1048576 | tf_op jit(solution)/shard_map/all_to_all | solution.py:225
  166.7 7.1 %collective-permute-start.20 = (bf16[8,4096]{1,0:T(8,128)(2,1)S(1)}, bf16[8,4096]{1,0:T(8,128)(2,1)S(1)}, u32[]{:S(2)}, u32[]{:S(2)}) collective-permute-start(bf16[8,4096]{1,0:T(8,128)(2,1)S(1)} %get-tuple-element.73), channel_id=1, source_target_pairs={{0,8},{1,9},{2,10},{3,11},{4,12},{5,13},{6,14},{7,15},{8,0},{9,1},... | collective-permute-start | bytes 196616 | tf_op jit(solution)/shard_map/ppermute | solution.py:30
  183.1 5.3 %all-to-all-done.2 = bf16[8,8,4096]{2,1,0:T(8,128)(2,1)S(1)} async-done(((bf16[8,8,4096]{2,1,0:T(8,128)(2,1)}), bf16[8,8,4096]{2,1,0:T(8,128)(2,1)S(1)}, u32[]{:S(2)}, u32[]{:S(2)}) %all-to-all-start.2) | async-done | bytes 524320 | tf_op jit(solution)/shard_map/all_to_all | solution.py:225
  189.3 20.3 %all_to_all.20 = bf16[16,8,2048]{2,1,0:T(8,128)(2,1)S(1)} all-to-all(bf16[16,8,2048]{2,1,0:T(8,128)(2,1)S(1)} %constant_dynamic-update-slice_fusion), channel_id=1, replica_groups={{0,32,64,96,128,160,192,224,256,288,320,352,384,416,448,480},{16,48,80,..., dimensions={0} | all-to-all | bytes 1048576 | tf_op jit(solution)/shard_map/all_to_all | solution.py:246
  209.6 3.8 %collective-permute-start.24 = (bf16[16,8,2048]{2,1,0:T(8,128)(2,1)S(1)}, bf16[16,8,2048]{2,1,0:T(8,128)(2,1)S(1)}, u32[]{:S(2)}, u32[]{:S(2)}) collective-permute-start(bf16[16,8,2048]{2,1,0:T(8,128)(2,1)S(1)} %all_to_all.20), channel_id=1, source_target_pairs={{0,16},{1,17},{2,18},{3,19},{4,20},{5,21},{6,22},{7,23},{8,24},{9,... | collective-permute-start | bytes 1572872 | tf_op jit(solution)/shard_map/ppermute | solution.py:30
  218.4 3.4 %collective-permute-start.25 = (f32[256,256]{1,0:T(8,128)S(1)}, f32[256,256]{1,0:T(8,128)S(1)}, u32[]{:S(2)}, u32[]{:S(2)}) collective-permute-start(f32[256,256]{1,0:T(8,128)S(1)} %get-tuple-element.60), channel_id=1, source_target_pairs={{0,256},{1,257},{2,258},{3,259},{4,260},{5,261},{6,262},{7,263},{8... | collective-permute-start | bytes 786440 | tf_op jit(solution)/shard_map/ppermute | solution.py:30
  224.0 3.4 %collective-permute-start.27 = (f32[256,256]{1,0:T(8,128)S(1)}, f32[256,256]{1,0:T(8,128)S(1)}, u32[]{:S(2)}, u32[]{:S(2)}) collective-permute-start(f32[256,256]{1,0:T(8,128)S(1)} %get-tuple-element.62), channel_id=1, source_target_pairs={{0,384},{1,385},{2,386},{3,387},{4,388},{5,389},{6,390},{7,391},{8... | collective-permute-start | bytes 786440 | tf_op jit(solution)/shard_map/ppermute | solution.py:30
  229.7 4.4 %collective-permute-done.26.refs_2_ = f32[256,256]{1,0:T(8,128)S(1)} collective-permute-done((f32[256,256]{1,0:T(8,128)S(1)}, f32[256,256]{1,0:T(8,128)S(1)}, u32[]{:S(2)}, u32[]{:S(2)}) %collective-permute-start.26) | collective-permute-done | bytes 262176 | tf_op jit(solution)/shard_map/ppermute | solution.py:30
  (127 shorter events, 83.8 us)
Async XLA Ops:
  6.5 12.6 %collective-permute-start = (bf16[256,256]{1,0:T(8,128)(2,1)}, bf16[256,256]{1,0:T(8,128)(2,1)S(1)}, u32[]{:S(2)}, u32[]{:S(2)}) collective-permute-start(bf16[256,256]{1,0:T(8,128)(2,1)} %param.8), channel_id=1, source_target_pairs={{0,96},{1,97},{2,98},{3,99},{4,100},{5,101},{6,102},{7,103},{8,104... | collective-permute-start | bytes 393224 | tf_op jit(solution)/shard_map/ppermute | solution.py:30
  15.0 10.9 %collective-permute-start.1 = (bf16[256,256]{1,0:T(8,128)(2,1)}, bf16[256,256]{1,0:T(8,128)(2,1)S(1)}, u32[]{:S(2)}, u32[]{:S(2)}) collective-permute-start(bf16[256,256]{1,0:T(8,128)(2,1)} %param.8), channel_id=1, source_target_pairs={{0,64},{1,65},{2,66},{3,67},{4,68},{5,69},{6,70},{7,71},{8,72},{9,... | collective-permute-start | bytes 393224 | tf_op jit(solution)/shard_map/ppermute | solution.py:30
  26.9 15.3 %collective-permute-start.6 = (bf16[4,256,256]{2,1,0:T(8,128)(2,1)S(1)}, bf16[4,256,256]{2,1,0:T(8,128)(2,1)S(1)}, u32[]{:S(2)}, u32[]{:S(2)}) collective-permute-start(bf16[4,256,256]{2,1,0:T(8,128)(2,1)S(1)} %get-tuple-element.68), channel_id=1, source_target_pairs={{0,256},{1,257},{2,258},{3,259},{4,260},{5,261},{6,262},{7,263},{8... | collective-permute-start | bytes 1572872 | tf_op jit(solution)/shard_map/ppermute | solution.py:30
  32.0 22.1 %collective-permute-start.3 = (bf16[4,256,256]{2,1,0:T(8,128)(2,1)S(1)}, bf16[4,256,256]{2,1,0:T(8,128)(2,1)S(1)}, u32[]{:S(2)}, u32[]{:S(2)}) collective-permute-start(bf16[4,256,256]{2,1,0:T(8,128)(2,1)S(1)} %get-tuple-element.68), channel_id=1, source_target_pairs={{0,128},{1,129},{2,130},{3,131},{4,132},{5,133},{6,134},{7,135},{8... | collective-permute-start | bytes 1572872 | tf_op jit(solution)/shard_map/ppermute | solution.py:30
  34.2 21.3 %collective-permute-start.4 = (bf16[4,256,256]{2,1,0:T(8,128)(2,1)S(1)}, bf16[4,256,256]{2,1,0:T(8,128)(2,1)S(1)}, u32[]{:S(2)}, u32[]{:S(2)}) collective-permute-start(bf16[4,256,256]{2,1,0:T(8,128)(2,1)S(1)} %get-tuple-element.68), channel_id=1, source_target_pairs={{0,384},{1,385},{2,386},{3,387},{4,388},{5,389},{6,390},{7,391},{8... | collective-permute-start | bytes 1572872 | tf_op jit(solution)/shard_map/ppermute | solution.py:30
  42.3 16.2 %collective-permute-start.7 = (bf16[2,4,256,256]{3,2,1,0:T(8,128)(2,1)S(1)}, bf16[2,4,256,256]{3,2,1,0:T(8,128)(2,1)S(1)}, u32[]{:S(2)}, u32[]{:S(2)}) collective-permute-start(bf16[2,4,256,256]{3,2,1,0:T(8,128)(2,1)S(1)} %pad_maximum_fusion.1), channel_id=1, source_target_pairs={{0,16},{1,17},{2,18},{3,19},{4,20},{5,21},{6,22},{7,23},{8,24},{9,... | collective-permute-start | bytes 3145736 | tf_op jit(solution)/shard_map/ppermute | solution.py:30
  64.7 17.4 %all-to-all-start = ((f32[32,8,256]{2,1,0:T(8,128)}), f32[32,8,256]{2,1,0:T(8,128)S(1)}, u32[]{:S(2)}, u32[]{:S(2)}) async-start(f32[32,8,256]{2,1,0:T(8,128)} %bitcast.13), calls=%async_computation | async-start | bytes 524288 | tf_op jit(solution)/shard_map/all_to_all | solution.py:170
  70.9 59.5 %all-gather.5.cloned.1.call-start = ((), (), s32[]{:S(2)}) async-start(), calls=%async_computation.4 | async-start | bytes 1179648 | tf_op jit(solution)/shard_map/all_gather | solution.py:186
  88.9 34.0 %all-to-all-start.1 = ((bf16[8,32,1024]{2,1,0:T(8,128)(2,1)}), bf16[8,32,1024]{2,1,0:T(8,128)(2,1)S(1)}, u32[]{:S(2)}, u32[]{:S(2)}) async-start(bf16[8,32,1024]{2,1,0:T(8,128)(2,1)} %reshape.125), calls=%async_computation.1 | async-start | bytes 1048576 | tf_op jit(solution)/shard_map/all_to_all | solution.py:183
  93.1 116.5 %all-gather.7.cloned.1.call-start = ((), (), s32[]{:S(2)}) async-start(), calls=%async_computation.5 | async-start | bytes 4718592 | tf_op jit(solution)/shard_map/all_gather | solution.py:190
  93.1 18.4 %collective-permute-start.9 = (bf16[8,4096]{1,0:T(8,128)(2,1)S(1)}, bf16[8,4096]{1,0:T(8,128)(2,1)S(1)}, u32[]{:S(2)}, u32[]{:S(2)}) collective-permute-start(bf16[8,4096]{1,0:T(8,128)(2,1)S(1)} %get-tuple-element.34), channel_id=1, source_target_pairs={{0,8},{1,9},{2,10},{3,11},{4,12},{5,13},{6,14},{7,15},{8,0},{9,1},... | collective-permute-start | bytes 196616 | tf_op jit(solution)/shard_map/ppermute | solution.py:30
  101.1 12.2 %collective-permute-start.10 = (bf16[8,4096]{1,0:T(8,128)(2,1)S(1)}, bf16[8,4096]{1,0:T(8,128)(2,1)S(1)}, u32[]{:S(2)}, u32[]{:S(2)}) collective-permute-start(bf16[8,4096]{1,0:T(8,128)(2,1)S(1)} %get-tuple-element.34), channel_id=1, source_target_pairs={{0,64},{1,65},{2,66},{3,67},{4,68},{5,69},{6,70},{7,71},{8,72},{9,... | collective-permute-start | bytes 196616 | tf_op jit(solution)/shard_map/ppermute | solution.py:30
  113.3 9.5 %collective-permute-start.12 = (bf16[4,8,4096]{2,1,0:T(8,128)(2,1)S(1)}, bf16[4,8,4096]{2,1,0:T(8,128)(2,1)S(1)}, u32[]{:S(2)}, u32[]{:S(2)}) collective-permute-start(bf16[4,8,4096]{2,1,0:T(8,128)(2,1)S(1)} %get-tuple-element.76), channel_id=1, source_target_pairs={{0,256},{1,257},{2,258},{3,259},{4,260},{5,261},{6,262},{7,263},{8... | collective-permute-start | bytes 786440 | tf_op jit(solution)/shard_map/ppermute | solution.py:30
  116.4 10.8 %collective-permute-start.13 = (bf16[4,8,4096]{2,1,0:T(8,128)(2,1)S(1)}, bf16[4,8,4096]{2,1,0:T(8,128)(2,1)S(1)}, u32[]{:S(2)}, u32[]{:S(2)}) collective-permute-start(bf16[4,8,4096]{2,1,0:T(8,128)(2,1)S(1)} %get-tuple-element.76), channel_id=1, source_target_pairs={{0,128},{1,129},{2,130},{3,131},{4,132},{5,133},{6,134},{7,135},{8... | collective-permute-start | bytes 786440 | tf_op jit(solution)/shard_map/ppermute | solution.py:30
  118.7 11.4 %collective-permute-start.14 = (bf16[4,8,4096]{2,1,0:T(8,128)(2,1)S(1)}, bf16[4,8,4096]{2,1,0:T(8,128)(2,1)S(1)}, u32[]{:S(2)}, u32[]{:S(2)}) collective-permute-start(bf16[4,8,4096]{2,1,0:T(8,128)(2,1)S(1)} %get-tuple-element.76), channel_id=1, source_target_pairs={{0,384},{1,385},{2,386},{3,387},{4,388},{5,389},{6,390},{7,391},{8... | collective-permute-start | bytes 786440 | tf_op jit(solution)/shard_map/ppermute | solution.py:30
  141.6 15.8 %collective-permute-start.23 = (bf16[64,4096]{1,0:T(8,128)(2,1)}, bf16[64,4096]{1,0:T(8,128)(2,1)S(1)}, u32[]{:S(2)}, u32[]{:S(2)}) collective-permute-start(bf16[64,4096]{1,0:T(8,128)(2,1)} %fusion.5), channel_id=1, source_target_pairs={{0,32},{1,33},{2,34},{3,35},{4,36},{5,37},{6,38},{7,39},{8,40},{9,... | collective-permute-start | bytes 1572872 | tf_op jit(solution)/shard_map/ppermute | solution.py:30
  147.7 17.8 %collective-permute-start.17 = (bf16[4,8,4096]{2,1,0:T(8,128)(2,1)}, bf16[4,8,4096]{2,1,0:T(8,128)(2,1)S(1)}, u32[]{:S(2)}, u32[]{:S(2)}) collective-permute-start(bf16[4,8,4096]{2,1,0:T(8,128)(2,1)} %get-tuple-element.65), channel_id=1, source_target_pairs={{0,256},{1,257},{2,258},{3,259},{4,260},{5,261},{6,262},{7,263},{8... | collective-permute-start | bytes 786440 | tf_op jit(solution)/shard_map/ppermute | solution.py:30
  151.0 14.5 %collective-permute-start.18 = (bf16[4,8,4096]{2,1,0:T(8,128)(2,1)S(1)}, bf16[4,8,4096]{2,1,0:T(8,128)(2,1)}, u32[]{:S(2)}, u32[]{:S(2)}) collective-permute-start(bf16[4,8,4096]{2,1,0:T(8,128)(2,1)S(1)} %get-tuple-element.64), channel_id=1, source_target_pairs={{0,128},{1,129},{2,130},{3,131},{4,132},{5,133},{6,134},{7,135},{8... | collective-permute-start | bytes 786440 | tf_op jit(solution)/shard_map/ppermute | solution.py:30
  153.4 12.1 %collective-permute-start.19 = (bf16[4,8,4096]{2,1,0:T(8,128)(2,1)S(1)}, bf16[4,8,4096]{2,1,0:T(8,128)(2,1)}, u32[]{:S(2)}, u32[]{:S(2)}) collective-permute-start(bf16[4,8,4096]{2,1,0:T(8,128)(2,1)S(1)} %get-tuple-element.63), channel_id=1, source_target_pairs={{0,384},{1,385},{2,386},{3,387},{4,388},{5,389},{6,390},{7,391},{8... | collective-permute-start | bytes 786440 | tf_op jit(solution)/shard_map/ppermute | solution.py:30
  158.5 30.0 %all-to-all-start.2 = ((bf16[8,8,4096]{2,1,0:T(8,128)(2,1)}), bf16[8,8,4096]{2,1,0:T(8,128)(2,1)S(1)}, u32[]{:S(2)}, u32[]{:S(2)}) async-start(bf16[8,8,4096]{2,1,0:T(8,128)(2,1)} %fusion.6), calls=%async_computation.2 | async-start | bytes 1048576 | tf_op jit(solution)/shard_map/all_to_all | solution.py:225
  166.7 11.4 %collective-permute-start.20 = (bf16[8,4096]{1,0:T(8,128)(2,1)S(1)}, bf16[8,4096]{1,0:T(8,128)(2,1)S(1)}, u32[]{:S(2)}, u32[]{:S(2)}) collective-permute-start(bf16[8,4096]{1,0:T(8,128)(2,1)S(1)} %get-tuple-element.73), channel_id=1, source_target_pairs={{0,8},{1,9},{2,10},{3,11},{4,12},{5,13},{6,14},{7,15},{8,0},{9,1},... | collective-permute-start | bytes 196616 | tf_op jit(solution)/shard_map/ppermute | solution.py:30
  218.4 11.3 %collective-permute-start.25 = (f32[256,256]{1,0:T(8,128)S(1)}, f32[256,256]{1,0:T(8,128)S(1)}, u32[]{:S(2)}, u32[]{:S(2)}) collective-permute-start(f32[256,256]{1,0:T(8,128)S(1)} %get-tuple-element.60), channel_id=1, source_target_pairs={{0,256},{1,257},{2,258},{3,259},{4,260},{5,261},{6,262},{7,263},{8... | collective-permute-start | bytes 786440 | tf_op jit(solution)/shard_map/ppermute | solution.py:30
  221.7 12.4 %collective-permute-start.26 = (f32[256,256]{1,0:T(8,128)S(1)}, f32[256,256]{1,0:T(8,128)S(1)}, u32[]{:S(2)}, u32[]{:S(2)}) collective-permute-start(f32[256,256]{1,0:T(8,128)S(1)} %get-tuple-element.61), channel_id=1, source_target_pairs={{0,128},{1,129},{2,130},{3,131},{4,132},{5,133},{6,134},{7,135},{8... | collective-permute-start | bytes 786440 | tf_op jit(solution)/shard_map/ppermute | solution.py:30
  224.0 11.1 %collective-permute-start.27 = (f32[256,256]{1,0:T(8,128)S(1)}, f32[256,256]{1,0:T(8,128)S(1)}, u32[]{:S(2)}, u32[]{:S(2)}) collective-permute-start(f32[256,256]{1,0:T(8,128)S(1)} %get-tuple-element.62), channel_id=1, source_target_pairs={{0,384},{1,385},{2,386},{3,387},{4,388},{5,389},{6,390},{7,391},{8... | collective-permute-start | bytes 786440 | tf_op jit(solution)/shard_map/ppermute | solution.py:30
  (18 other events, 158.7 us)
Sparse Core Ops, SparseCore 0:
  89.0 37.1 all-gather.4
  141.7 67.8 all-gather.6

commit v19 on v18

--- a/solution.py
+++ b/solution.py
@@ -58,7 +58,15 @@
                 inputs_ref[:, pl.ds(start, depth)], weight_ref[k], preferred_element_type=jnp.float32
             )
             result = part if result is None else result + part
-    out_ref[...] = result.T if last else result
+    if not last:
+        out_ref[...] = result
+        return
+    features = result.T
+    rows = features.shape[1]
+    out_ref[:, :rows] = features
+    for j in range(DP):
+        k = 8 * (j ^ 2)
+        out_ref[8 * j : 8 * j + 8, rows:] = features[k : k + 8, rows // 2 :]
 
 
 def project(order, inputs, own, other, *before):
@@ -68,7 +76,7 @@
         functools.partial(project_kernel, bool(before)),
         in_specs=[pl.BlockSpec(memory_space=pltpu.SMEM)] + [vmem] * (3 + len(before)),
         out_specs=vmem,
-        out_shape=jax.ShapeDtypeStruct((feat, rows) if before else (rows, feat), jnp.float32),
+        out_shape=jax.ShapeDtypeStruct((feat, rows // 2 * 3) if before else (rows, feat), jnp.float32),
         compiler_params=pltpu.CompilerParams(vmem_limit_bytes=16 * 1024 * 1024),
         cost_estimate=pl.CostEstimate(
             flops=4 * rows * feat * own.shape[0] * own.shape[1],
@@ -158,7 +166,7 @@
     parts = [along_z] + [swap(along_z, *mask) for mask in ALONG_X]
     projected = ()
     for k in (0, 2):
-        weight_own = jnp.stack(parts[k : k + 2])
+        weight_own, pieces = lax.optimization_barrier((jnp.stack(parts[k : k + 2]), pieces))
         weight_other = swap(weight_own, 1)
         blocks = np.concatenate([4 * k + np.arange(8), 16 + 4 * k + np.arange(8)])
         half = (DP // 4, rows, feat)
@@ -168,18 +176,16 @@
     projected = projected[0]
 
     own = lax.all_to_all(
-        projected.reshape(DP, block, views * images), "dp", split_axis=0, concat_axis=0
-    ).reshape(DP, block, views, images)
+        projected.reshape(DP, block, (views + 1) * images), "dp", split_axis=0, concat_axis=0
+    ).reshape(DP, block, views + 1, images)
     average = jnp.sum(own, axis=(0, 3), keepdims=True) / total
     centered = own - average
     variance = jnp.sum(centered * centered, axis=(0, 3), keepdims=True) / total
     inverse = lax.rsqrt(variance + epsilon)
-    normed = (centered * inverse).astype(jnp.bfloat16).transpose(2, 1, 0, 3).reshape(views, block, total)
-    inverse = inverse.reshape(block, views).T[:, :, None]
-
-    second = normed[1]
-    pair = jnp.stack([second, partner(second)])
-    first, pair, pieces = lax.optimization_barrier((normed[0], pair, pieces))
+    normed = (centered * inverse).astype(jnp.bfloat16).transpose(2, 1, 0, 3).reshape(views + 1, block, total)
+    inverse = inverse.reshape(block, views + 1).T[:views, :, None]
+
+    first, pair, pieces = lax.optimization_barrier((normed[0], normed[1:], pieces))
     slices = lax.all_to_all(
         pieces, "dp", split_axis=0, concat_axis=0, axis_index_groups=SAME_X
     )
@@ -233,7 +239,7 @@
     along_x = add(both, ALONG_X)[0].astype(jnp.bfloat16)
     grad_a, terms_b = add(along_x, STRIDED_Z, terms_b)
     grads = jnp.stack([grad_a, jnp.sum(terms_b.astype(jnp.float32), axis=0)])
-    wide = normed.astype(jnp.float32)
+    wide = normed[:views].astype(jnp.float32)
     grad_mean = jnp.sum(grads, axis=2, keepdims=True) / total
     cross_mean = jnp.sum(grads * wide, axis=2, keepdims=True) / total
     grad_proj = ((grads - grad_mean - wide * cross_mean) * inverse).astype(jnp.bfloat16)

time: 245 us -> 241 us (0.984)
  blocking collectives: 20.3 us -> 39.8 us
  waiting for transfers between devices: 63.4 us -> 48.8 us
  starting transfers between devices: 117 us -> 108 us
    all_to_all x0 -> x1, blocking collectives: none -> 20 us  [per_device(): lax.all_to_all(projected.reshape(DP, block, (views + 1) * images), 'dp',...]
    all_to_all x1 -> x0, waiting for transfers between devices: 11.2 us -> none  [per_device(): lax.all_to_all(projected.reshape(DP, block, views * images), 'dp', split_...]
    all_to_all x1 -> x0, starting transfers between devices: 6.13 us -> none  [per_device(): lax.all_to_all(projected.reshape(DP, block, views * images), 'dp', split_...]
    ppermute x28 -> x27, waiting for transfers between devices: 46.7 us -> 42.9 us  [swap(): lax.ppermute(array, ('dp', 'mp'), [(i, i ^ mask) for i in range(DP * MP)])]
    ppermute x28 -> x27, starting transfers between devices: 99.6 us -> 97.8 us  [swap(): lax.ppermute(array, ('dp', 'mp'), [(i, i ^ mask) for i in range(DP * MP)])]
  transfers between devices with their start and end apart: 33 -> 31, of which waited for: 20 -> 18; matrix products, arithmetic and copies ran while one was open for 4% -> 5% of each run, Pallas kernels for 1% -> 1%
where the time goes in v19:
time: 241 us; the launch traced here: 240 us
  starting transfers between devices  108 us (45%)
  waiting for transfers between devices  48.8 us (20%)
  blocking collectives  39.8 us (17%)
  between operations  14.1 us (6%)
  local copies, waits for them, and re-layouts  7.73 us (3%)
  Pallas kernels  7.39 us (3%)
  matrix products  6.95 us (3%)
  other arithmetic  6.88 us (3%)
    ppermute x27, starting transfers between devices, swap(): lax.ppermute(array, ('dp', 'mp'), [(i, i ^ mask) for i in range(DP * MP)])  97.8 us
    ppermute x27, waiting for transfers between devices, swap(): lax.ppermute(array, ('dp', 'mp'), [(i, i ^ mask) for i in range(DP * MP)])  42.9 us
    all_to_all x1, blocking collectives, per_device(): lax.all_to_all(projected.reshape(DP, block, (views + 1) * images), 'dp',...  20 us
    all_to_all x1, blocking collectives, per_device(): lax.all_to_all(jnp.stack([part for part in blocks for _ in range(DP // X...  19.8 us
    all_to_all x1, starting transfers between devices, per_device(): lax.all_to_all(terms_b.reshape(Y, block, total), 'mp', split_axis=0, conc...  6.97 us
    all_to_all x1, waiting for transfers between devices, per_device(): lax.all_to_all(terms_b.reshape(Y, block, total), 'mp', split_axis=0, conc...  5.72 us
  transfers between devices with their start and end apart: 31, of which 18 were waited for; matrix products, arithmetic and copies ran while one was open for 5% of the time, Pallas kernels for 1%

profile of v19, /device:TPU:1, one launch (start us, length us, event | category | flops | bytes accessed | tf_op | source)
XLA Modules:
  0.0 239.9 jit_solution(2049316280969175708)
XLA Ops:
  6.5 8.4 %collective-permute-start = (bf16[256,256]{1,0:T(8,128)(2,1)}, bf16[256,256]{1,0:T(8,128)(2,1)S(1)}, u32[]{:S(2)}, u32[]{:S(2)}) collective-permute-start(bf16[256,256]{1,0:T(8,128)(2,1)} %param.8), channel_id=1, source_target_pairs={{0,96},{1,97},{2,98},{3,99},{4,100},{5,101},{6,102},{7,103},{8,104... | collective-permute-start | bytes 393224 | tf_op jit(solution)/shard_map/ppermute | solution.py:30
  19.1 6.7 %collective-permute-done.1 = bf16[256,256]{1,0:T(8,128)(2,1)S(1)} collective-permute-done((bf16[256,256]{1,0:T(8,128)(2,1)}, bf16[256,256]{1,0:T(8,128)(2,1)S(1)}, u32[]{:S(2)}, u32[]{:S(2)}) %collective-permute-start.1) | collective-permute-done | bytes 131104 | tf_op jit(solution)/shard_map/ppermute | solution.py:30
  26.9 5.1 %collective-permute-start.5 = (bf16[4,256,256]{2,1,0:T(8,128)(2,1)S(1)}, bf16[4,256,256]{2,1,0:T(8,128)(2,1)S(1)}, u32[]{:S(2)}, u32[]{:S(2)}) collective-permute-start(bf16[4,256,256]{2,1,0:T(8,128)(2,1)S(1)} %get-tuple-element.76), channel_id=1, source_target_pairs={{0,256},{1,257},{2,258},{3,259},{4,260},{5,261},{6,262},{7,263},{8... | collective-permute-start | bytes 1572872 | tf_op jit(solution)/shard_map/ppermute | solution.py:30
  42.3 6.9 %collective-permute-start.7 = (bf16[2,4,256,256]{3,2,1,0:T(8,128)(2,1)S(1)}, bf16[2,4,256,256]{3,2,1,0:T(8,128)(2,1)S(1)}, u32[]{:S(2)}, u32[]{:S(2)}) collective-permute-start(bf16[2,4,256,256]{3,2,1,0:T(8,128)(2,1)S(1)} %pad_maximum_fusion.1), channel_id=1, source_target_pairs={{0,16},{1,17},{2,18},{3,19},{4,20},{5,21},{6,22},{7,23},{8,24},{9,... | collective-permute-start | bytes 3145736 | tf_op jit(solution)/shard_map/ppermute | solution.py:30
  49.2 5.0 %collective-permute-done.3 = bf16[4,256,256]{2,1,0:T(8,128)(2,1)} collective-permute-done((bf16[4,256,256]{2,1,0:T(8,128)(2,1)S(1)}, bf16[4,256,256]{2,1,0:T(8,128)(2,1)}, u32[]{:S(2)}, u32[]{:S(2)}) %collective-permute-start.3) | collective-permute-done | bytes 524320 | tf_op jit(solution)/shard_map/ppermute | solution.py:30
  65.3 20.0 %all_to_all.20 = f32[32,8,384]{2,1,0:T(8,128)S(1)} all-to-all(f32[32,8,384]{2,1,0:T(8,128)S(1)} %bitcast.217), channel_id=1, replica_groups=mesh['dp'=32,'mp'=16] {'dp'}, dimensions={0} | all-to-all | bytes 786432 | tf_op jit(solution)/shard_map/all_to_all | solution.py:178
  86.5 3.5 %all-to-all-start.1 = ((bf16[8,32,1024]{2,1,0:T(8,128)(2,1)}), bf16[8,32,1024]{2,1,0:T(8,128)(2,1)S(1)}, u32[]{:S(2)}, u32[]{:S(2)}) async-start(bf16[8,32,1024]{2,1,0:T(8,128)(2,1)} %reshape.119), calls=%async_computation.1 | async-start | bytes 1048576 | tf_op jit(solution)/shard_map/all_to_all | solution.py:189
  90.0 7.9 %collective-permute-start.8 = (bf16[8,4096]{1,0:T(8,128)(2,1)S(1)}, bf16[8,4096]{1,0:T(8,128)(2,1)S(1)}, u32[]{:S(2)}, u32[]{:S(2)}) collective-permute-start(bf16[8,4096]{1,0:T(8,128)(2,1)S(1)} %slice_bitcast_fusion.13), channel_id=1, source_target_pairs={{0,8},{1,9},{2,10},{3,11},{4,12},{5,13},{6,14},{7,15},{8,0},{9,1},... | collective-permute-start | bytes 196616 | tf_op jit(solution)/shard_map/ppermute | solution.py:30
  97.9 4.2 %collective-permute-start.9 = (bf16[8,4096]{1,0:T(8,128)(2,1)S(1)}, bf16[8,4096]{1,0:T(8,128)(2,1)S(1)}, u32[]{:S(2)}, u32[]{:S(2)}) collective-permute-start(bf16[8,4096]{1,0:T(8,128)(2,1)S(1)} %slice_bitcast_fusion.13), channel_id=1, source_target_pairs={{0,64},{1,65},{2,66},{3,67},{4,68},{5,69},{6,70},{7,71},{8,72},{9,... | collective-permute-start | bytes 196616 | tf_op jit(solution)/shard_map/ppermute | solution.py:30
  104.1 4.3 %collective-permute-done.8 = bf16[8,4096]{1,0:T(8,128)(2,1)S(1)} collective-permute-done((bf16[8,4096]{1,0:T(8,128)(2,1)S(1)}, bf16[8,4096]{1,0:T(8,128)(2,1)S(1)}, u32[]{:S(2)}, u32[]{:S(2)}) %collective-permute-start.8) | collective-permute-done | bytes 65568 | tf_op jit(solution)/shard_map/ppermute | solution.py:30
  115.2 4.0 %collective-permute-start.13 = (bf16[4,8,4096]{2,1,0:T(8,128)(2,1)S(1)}, bf16[4,8,4096]{2,1,0:T(8,128)(2,1)S(1)}, u32[]{:S(2)}, u32[]{:S(2)}) collective-permute-start(bf16[4,8,4096]{2,1,0:T(8,128)(2,1)S(1)} %get-tuple-element.84), channel_id=1, source_target_pairs={{0,384},{1,385},{2,386},{3,387},{4,388},{5,389},{6,390},{7,391},{8... | collective-permute-start | bytes 786440 | tf_op jit(solution)/shard_map/ppermute | solution.py:30
  119.7 4.1 %collective-permute-done.12 = bf16[4,8,4096]{2,1,0:T(8,128)(2,1)S(1)} collective-permute-done((bf16[4,8,4096]{2,1,0:T(8,128)(2,1)S(1)}, bf16[4,8,4096]{2,1,0:T(8,128)(2,1)S(1)}, u32[]{:S(2)}, u32[]{:S(2)}) %collective-permute-start.12) | collective-permute-done | bytes 262176 | tf_op jit(solution)/shard_map/ppermute | solution.py:30
  127.2 3.5 %collective-permute-start.14 = (bf16[4,4,8,4096]{3,2,1,0:T(8,128)(2,1)S(1)}, bf16[4,4,8,4096]{3,2,1,0:T(8,128)(2,1)S(1)}, u32[]{:S(2)}, u32[]{:S(2)}) collective-permute-start(bf16[4,4,8,4096]{3,2,1,0:T(8,128)(2,1)S(1)} %pad_maximum_fusion.2), channel_id=1, source_target_pairs={{0,16},{1,17},{2,18},{3,19},{4,20},{5,21},{6,22},{7,23},{8,24},{9,... | collective-permute-start | bytes 3145736 | tf_op jit(solution)/shard_map/ppermute | solution.py:30
  138.3 3.8 %collective-permute-start.22 = (bf16[64,4096]{1,0:T(8,128)(2,1)}, bf16[64,4096]{1,0:T(8,128)(2,1)S(1)}, u32[]{:S(2)}, u32[]{:S(2)}) collective-permute-start(bf16[64,4096]{1,0:T(8,128)(2,1)} %fusion.5), channel_id=1, source_target_pairs={{0,32},{1,33},{2,34},{3,35},{4,36},{5,37},{6,38},{7,39},{8,40},{9,... | collective-permute-start | bytes 1572872 | tf_op jit(solution)/shard_map/ppermute | solution.py:30
  144.7 3.2 %collective-permute-start.16 = (bf16[4,8,4096]{2,1,0:T(8,128)(2,1)}, bf16[4,8,4096]{2,1,0:T(8,128)(2,1)S(1)}, u32[]{:S(2)}, u32[]{:S(2)}) collective-permute-start(bf16[4,8,4096]{2,1,0:T(8,128)(2,1)} %get-tuple-element.73), channel_id=1, source_target_pairs={{0,256},{1,257},{2,258},{3,259},{4,260},{5,261},{6,262},{7,263},{8... | collective-permute-start | bytes 786440 | tf_op jit(solution)/shard_map/ppermute | solution.py:30
  150.2 3.5 %collective-permute-start.18 = (bf16[4,8,4096]{2,1,0:T(8,128)(2,1)S(1)}, bf16[4,8,4096]{2,1,0:T(8,128)(2,1)}, u32[]{:S(2)}, u32[]{:S(2)}) collective-permute-start(bf16[4,8,4096]{2,1,0:T(8,128)(2,1)S(1)} %get-tuple-element.71), channel_id=1, source_target_pairs={{0,384},{1,385},{2,386},{3,387},{4,388},{5,389},{6,390},{7,391},{8... | collective-permute-start | bytes 786440 | tf_op jit(solution)/shard_map/ppermute | solution.py:30
  155.6 7.0 %all-to-all-start.2 = ((bf16[8,8,4096]{2,1,0:T(8,128)(2,1)}), bf16[8,8,4096]{2,1,0:T(8,128)(2,1)S(1)}, u32[]{:S(2)}, u32[]{:S(2)}) async-start(bf16[8,8,4096]{2,1,0:T(8,128)(2,1)} %fusion.6), calls=%async_computation.2 | async-start | bytes 1048576 | tf_op jit(solution)/shard_map/all_to_all | solution.py:231
  163.8 6.7 %collective-permute-start.19 = (bf16[8,4096]{1,0:T(8,128)(2,1)S(1)}, bf16[8,4096]{1,0:T(8,128)(2,1)S(1)}, u32[]{:S(2)}, u32[]{:S(2)}) collective-permute-start(bf16[8,4096]{1,0:T(8,128)(2,1)S(1)} %get-tuple-element.81), channel_id=1, source_target_pairs={{0,8},{1,9},{2,10},{3,11},{4,12},{5,13},{6,14},{7,15},{8,0},{9,1},... | collective-permute-start | bytes 196616 | tf_op jit(solution)/shard_map/ppermute | solution.py:30
  179.9 5.7 %all-to-all-done.2 = bf16[8,8,4096]{2,1,0:T(8,128)(2,1)S(1)} async-done(((bf16[8,8,4096]{2,1,0:T(8,128)(2,1)}), bf16[8,8,4096]{2,1,0:T(8,128)(2,1)S(1)}, u32[]{:S(2)}, u32[]{:S(2)}) %all-to-all-start.2) | async-done | bytes 524320 | tf_op jit(solution)/shard_map/all_to_all | solution.py:231
  186.4 19.8 %all_to_all.21 = bf16[16,8,2048]{2,1,0:T(8,128)(2,1)S(1)} all-to-all(bf16[16,8,2048]{2,1,0:T(8,128)(2,1)S(1)} %constant_dynamic-update-slice_fusion), channel_id=1, replica_groups={{0,32,64,96,128,160,192,224,256,288,320,352,384,416,448,480},{16,48,80,..., dimensions={0} | all-to-all | bytes 1048576 | tf_op jit(solution)/shard_map/all_to_all | solution.py:252
  206.3 3.7 %collective-permute-start.23 = (bf16[16,8,2048]{2,1,0:T(8,128)(2,1)S(1)}, bf16[16,8,2048]{2,1,0:T(8,128)(2,1)S(1)}, u32[]{:S(2)}, u32[]{:S(2)}) collective-permute-start(bf16[16,8,2048]{2,1,0:T(8,128)(2,1)S(1)} %all_to_all.21), channel_id=1, source_target_pairs={{0,16},{1,17},{2,18},{3,19},{4,20},{5,21},{6,22},{7,23},{8,24},{9,... | collective-permute-start | bytes 1572872 | tf_op jit(solution)/shard_map/ppermute | solution.py:30
  215.0 3.5 %collective-permute-start.24 = (f32[256,256]{1,0:T(8,128)S(1)}, f32[256,256]{1,0:T(8,128)S(1)}, u32[]{:S(2)}, u32[]{:S(2)}) collective-permute-start(f32[256,256]{1,0:T(8,128)S(1)} %get-tuple-element.68), channel_id=1, source_target_pairs={{0,256},{1,257},{2,258},{3,259},{4,260},{5,261},{6,262},{7,263},{8... | collective-permute-start | bytes 786440 | tf_op jit(solution)/shard_map/ppermute | solution.py:30
  220.7 3.3 %collective-permute-start.26 = (f32[256,256]{1,0:T(8,128)S(1)}, f32[256,256]{1,0:T(8,128)S(1)}, u32[]{:S(2)}, u32[]{:S(2)}) collective-permute-start(f32[256,256]{1,0:T(8,128)S(1)} %get-tuple-element.70), channel_id=1, source_target_pairs={{0,384},{1,385},{2,386},{3,387},{4,388},{5,389},{6,390},{7,391},{8... | collective-permute-start | bytes 786440 | tf_op jit(solution)/shard_map/ppermute | solution.py:30
  226.3 4.5 %collective-permute-done.25.refs_2_ = f32[256,256]{1,0:T(8,128)S(1)} collective-permute-done((f32[256,256]{1,0:T(8,128)S(1)}, f32[256,256]{1,0:T(8,128)S(1)}, u32[]{:S(2)}, u32[]{:S(2)}) %collective-permute-start.25) | collective-permute-done | bytes 262176 | tf_op jit(solution)/shard_map/ppermute | solution.py:30
  (125 shorter events, 77.4 us)
Async XLA Ops:
  6.5 120.6 %all-gather.5.cloned.1.call-start = ((), (), s32[]{:S(2)}) async-start(), calls=%async_computation.4 | async-start | bytes 1179648 | tf_op jit(solution)/shard_map/all_gather | solution.py:192
  6.5 12.6 %collective-permute-start = (bf16[256,256]{1,0:T(8,128)(2,1)}, bf16[256,256]{1,0:T(8,128)(2,1)S(1)}, u32[]{:S(2)}, u32[]{:S(2)}) collective-permute-start(bf16[256,256]{1,0:T(8,128)(2,1)} %param.8), channel_id=1, source_target_pairs={{0,96},{1,97},{2,98},{3,99},{4,100},{5,101},{6,102},{7,103},{8,104... | collective-permute-start | bytes 393224 | tf_op jit(solution)/shard_map/ppermute | solution.py:30
  15.0 10.9 %collective-permute-start.1 = (bf16[256,256]{1,0:T(8,128)(2,1)}, bf16[256,256]{1,0:T(8,128)(2,1)S(1)}, u32[]{:S(2)}, u32[]{:S(2)}) collective-permute-start(bf16[256,256]{1,0:T(8,128)(2,1)} %param.8), channel_id=1, source_target_pairs={{0,64},{1,65},{2,66},{3,67},{4,68},{5,69},{6,70},{7,71},{8,72},{9,... | collective-permute-start | bytes 393224 | tf_op jit(solution)/shard_map/ppermute | solution.py:30
  16.9 9.0 %collective-permute-start.2 = (bf16[256,256]{1,0:T(8,128)(2,1)}, bf16[256,256]{1,0:T(8,128)(2,1)S(1)}, u32[]{:S(2)}, u32[]{:S(2)}) collective-permute-start(bf16[256,256]{1,0:T(8,128)(2,1)} %param.8), channel_id=1, source_target_pairs={{0,32},{1,33},{2,34},{3,35},{4,36},{5,37},{6,38},{7,39},{8,40},{9,... | collective-permute-start | bytes 393224 | tf_op jit(solution)/shard_map/ppermute | solution.py:30
  26.9 15.3 %collective-permute-start.5 = (bf16[4,256,256]{2,1,0:T(8,128)(2,1)S(1)}, bf16[4,256,256]{2,1,0:T(8,128)(2,1)S(1)}, u32[]{:S(2)}, u32[]{:S(2)}) collective-permute-start(bf16[4,256,256]{2,1,0:T(8,128)(2,1)S(1)} %get-tuple-element.76), channel_id=1, source_target_pairs={{0,256},{1,257},{2,258},{3,259},{4,260},{5,261},{6,262},{7,263},{8... | collective-permute-start | bytes 1572872 | tf_op jit(solution)/shard_map/ppermute | solution.py:30
  32.0 22.2 %collective-permute-start.3 = (bf16[4,256,256]{2,1,0:T(8,128)(2,1)S(1)}, bf16[4,256,256]{2,1,0:T(8,128)(2,1)}, u32[]{:S(2)}, u32[]{:S(2)}) collective-permute-start(bf16[4,256,256]{2,1,0:T(8,128)(2,1)S(1)} %get-tuple-element.76), channel_id=1, source_target_pairs={{0,128},{1,129},{2,130},{3,131},{4,132},{5,133},{6,134},{7,135},{8... | collective-permute-start | bytes 1572872 | tf_op jit(solution)/shard_map/ppermute | solution.py:30
  34.2 21.4 %collective-permute-start.4 = (bf16[4,256,256]{2,1,0:T(8,128)(2,1)S(1)}, bf16[4,256,256]{2,1,0:T(8,128)(2,1)}, u32[]{:S(2)}, u32[]{:S(2)}) collective-permute-start(bf16[4,256,256]{2,1,0:T(8,128)(2,1)S(1)} %get-tuple-element.76), channel_id=1, source_target_pairs={{0,384},{1,385},{2,386},{3,387},{4,388},{5,389},{6,390},{7,391},{8... | collective-permute-start | bytes 1572872 | tf_op jit(solution)/shard_map/ppermute | solution.py:30
  42.3 17.5 %collective-permute-start.7 = (bf16[2,4,256,256]{3,2,1,0:T(8,128)(2,1)S(1)}, bf16[2,4,256,256]{3,2,1,0:T(8,128)(2,1)S(1)}, u32[]{:S(2)}, u32[]{:S(2)}) collective-permute-start(bf16[2,4,256,256]{3,2,1,0:T(8,128)(2,1)S(1)} %pad_maximum_fusion.1), channel_id=1, source_target_pairs={{0,16},{1,17},{2,18},{3,19},{4,20},{5,21},{6,22},{7,23},{8,24},{9,... | collective-permute-start | bytes 3145736 | tf_op jit(solution)/shard_map/ppermute | solution.py:30
  86.5 33.3 %all-to-all-start.1 = ((bf16[8,32,1024]{2,1,0:T(8,128)(2,1)}), bf16[8,32,1024]{2,1,0:T(8,128)(2,1)S(1)}, u32[]{:S(2)}, u32[]{:S(2)}) async-start(bf16[8,32,1024]{2,1,0:T(8,128)(2,1)} %reshape.119), calls=%async_computation.1 | async-start | bytes 1048576 | tf_op jit(solution)/shard_map/all_to_all | solution.py:189
  90.0 116.3 %all-gather.7.cloned.1.call-start = ((), (), s32[]{:S(2)}) async-start(), calls=%async_computation.5 | async-start | bytes 4718592 | tf_op jit(solution)/shard_map/all_gather | solution.py:196
  90.0 18.4 %collective-permute-start.8 = (bf16[8,4096]{1,0:T(8,128)(2,1)S(1)}, bf16[8,4096]{1,0:T(8,128)(2,1)S(1)}, u32[]{:S(2)}, u32[]{:S(2)}) collective-permute-start(bf16[8,4096]{1,0:T(8,128)(2,1)S(1)} %slice_bitcast_fusion.13), channel_id=1, source_target_pairs={{0,8},{1,9},{2,10},{3,11},{4,12},{5,13},{6,14},{7,15},{8,0},{9,1},... | collective-permute-start | bytes 196616 | tf_op jit(solution)/shard_map/ppermute | solution.py:30
  97.9 12.2 %collective-permute-start.9 = (bf16[8,4096]{1,0:T(8,128)(2,1)S(1)}, bf16[8,4096]{1,0:T(8,128)(2,1)S(1)}, u32[]{:S(2)}, u32[]{:S(2)}) collective-permute-start(bf16[8,4096]{1,0:T(8,128)(2,1)S(1)} %slice_bitcast_fusion.13), channel_id=1, source_target_pairs={{0,64},{1,65},{2,66},{3,67},{4,68},{5,69},{6,70},{7,71},{8,72},{9,... | collective-permute-start | bytes 196616 | tf_op jit(solution)/shard_map/ppermute | solution.py:30
  110.2 9.5 %collective-permute-start.11 = (bf16[4,8,4096]{2,1,0:T(8,128)(2,1)S(1)}, bf16[4,8,4096]{2,1,0:T(8,128)(2,1)S(1)}, u32[]{:S(2)}, u32[]{:S(2)}) collective-permute-start(bf16[4,8,4096]{2,1,0:T(8,128)(2,1)S(1)} %get-tuple-element.84), channel_id=1, source_target_pairs={{0,256},{1,257},{2,258},{3,259},{4,260},{5,261},{6,262},{7,263},{8... | collective-permute-start | bytes 786440 | tf_op jit(solution)/shard_map/ppermute | solution.py:30
  112.7 11.1 %collective-permute-start.12 = (bf16[4,8,4096]{2,1,0:T(8,128)(2,1)S(1)}, bf16[4,8,4096]{2,1,0:T(8,128)(2,1)S(1)}, u32[]{:S(2)}, u32[]{:S(2)}) collective-permute-start(bf16[4,8,4096]{2,1,0:T(8,128)(2,1)S(1)} %get-tuple-element.84), channel_id=1, source_target_pairs={{0,128},{1,129},{2,130},{3,131},{4,132},{5,133},{6,134},{7,135},{8... | collective-permute-start | bytes 786440 | tf_op jit(solution)/shard_map/ppermute | solution.py:30
  115.2 11.7 %collective-permute-start.13 = (bf16[4,8,4096]{2,1,0:T(8,128)(2,1)S(1)}, bf16[4,8,4096]{2,1,0:T(8,128)(2,1)S(1)}, u32[]{:S(2)}, u32[]{:S(2)}) collective-permute-start(bf16[4,8,4096]{2,1,0:T(8,128)(2,1)S(1)} %get-tuple-element.84), channel_id=1, source_target_pairs={{0,384},{1,385},{2,386},{3,387},{4,388},{5,389},{6,390},{7,391},{8... | collective-permute-start | bytes 786440 | tf_op jit(solution)/shard_map/ppermute | solution.py:30
  138.3 16.2 %collective-permute-start.22 = (bf16[64,4096]{1,0:T(8,128)(2,1)}, bf16[64,4096]{1,0:T(8,128)(2,1)S(1)}, u32[]{:S(2)}, u32[]{:S(2)}) collective-permute-start(bf16[64,4096]{1,0:T(8,128)(2,1)} %fusion.5), channel_id=1, source_target_pairs={{0,32},{1,33},{2,34},{3,35},{4,36},{5,37},{6,38},{7,39},{8,40},{9,... | collective-permute-start | bytes 1572872 | tf_op jit(solution)/shard_map/ppermute | solution.py:30
  144.7 17.9 %collective-permute-start.16 = (bf16[4,8,4096]{2,1,0:T(8,128)(2,1)}, bf16[4,8,4096]{2,1,0:T(8,128)(2,1)S(1)}, u32[]{:S(2)}, u32[]{:S(2)}) collective-permute-start(bf16[4,8,4096]{2,1,0:T(8,128)(2,1)} %get-tuple-element.73), channel_id=1, source_target_pairs={{0,256},{1,257},{2,258},{3,259},{4,260},{5,261},{6,262},{7,263},{8... | collective-permute-start | bytes 786440 | tf_op jit(solution)/shard_map/ppermute | solution.py:30
  148.0 14.7 %collective-permute-start.17 = (bf16[4,8,4096]{2,1,0:T(8,128)(2,1)S(1)}, bf16[4,8,4096]{2,1,0:T(8,128)(2,1)}, u32[]{:S(2)}, u32[]{:S(2)}) collective-permute-start(bf16[4,8,4096]{2,1,0:T(8,128)(2,1)S(1)} %get-tuple-element.72), channel_id=1, source_target_pairs={{0,128},{1,129},{2,130},{3,131},{4,132},{5,133},{6,134},{7,135},{8... | collective-permute-start | bytes 786440 | tf_op jit(solution)/shard_map/ppermute | solution.py:30
  150.2 12.4 %collective-permute-start.18 = (bf16[4,8,4096]{2,1,0:T(8,128)(2,1)S(1)}, bf16[4,8,4096]{2,1,0:T(8,128)(2,1)}, u32[]{:S(2)}, u32[]{:S(2)}) collective-permute-start(bf16[4,8,4096]{2,1,0:T(8,128)(2,1)S(1)} %get-tuple-element.71), channel_id=1, source_target_pairs={{0,384},{1,385},{2,386},{3,387},{4,388},{5,389},{6,390},{7,391},{8... | collective-permute-start | bytes 786440 | tf_op jit(solution)/shard_map/ppermute | solution.py:30
  155.6 30.0 %all-to-all-start.2 = ((bf16[8,8,4096]{2,1,0:T(8,128)(2,1)}), bf16[8,8,4096]{2,1,0:T(8,128)(2,1)S(1)}, u32[]{:S(2)}, u32[]{:S(2)}) async-start(bf16[8,8,4096]{2,1,0:T(8,128)(2,1)} %fusion.6), calls=%async_computation.2 | async-start | bytes 1048576 | tf_op jit(solution)/shard_map/all_to_all | solution.py:231
  163.8 11.4 %collective-permute-start.19 = (bf16[8,4096]{1,0:T(8,128)(2,1)S(1)}, bf16[8,4096]{1,0:T(8,128)(2,1)S(1)}, u32[]{:S(2)}, u32[]{:S(2)}) collective-permute-start(bf16[8,4096]{1,0:T(8,128)(2,1)S(1)} %get-tuple-element.81), channel_id=1, source_target_pairs={{0,8},{1,9},{2,10},{3,11},{4,12},{5,13},{6,14},{7,15},{8,0},{9,1},... | collective-permute-start | bytes 196616 | tf_op jit(solution)/shard_map/ppermute | solution.py:30
  215.0 11.3 %collective-permute-start.24 = (f32[256,256]{1,0:T(8,128)S(1)}, f32[256,256]{1,0:T(8,128)S(1)}, u32[]{:S(2)}, u32[]{:S(2)}) collective-permute-start(f32[256,256]{1,0:T(8,128)S(1)} %get-tuple-element.68), channel_id=1, source_target_pairs={{0,256},{1,257},{2,258},{3,259},{4,260},{5,261},{6,262},{7,263},{8... | collective-permute-start | bytes 786440 | tf_op jit(solution)/shard_map/ppermute | solution.py:30
  218.5 12.4 %collective-permute-start.25 = (f32[256,256]{1,0:T(8,128)S(1)}, f32[256,256]{1,0:T(8,128)S(1)}, u32[]{:S(2)}, u32[]{:S(2)}) collective-permute-start(f32[256,256]{1,0:T(8,128)S(1)} %get-tuple-element.69), channel_id=1, source_target_pairs={{0,128},{1,129},{2,130},{3,131},{4,132},{5,133},{6,134},{7,135},{8... | collective-permute-start | bytes 786440 | tf_op jit(solution)/shard_map/ppermute | solution.py:30
  220.7 11.0 %collective-permute-start.26 = (f32[256,256]{1,0:T(8,128)S(1)}, f32[256,256]{1,0:T(8,128)S(1)}, u32[]{:S(2)}, u32[]{:S(2)}) collective-permute-start(f32[256,256]{1,0:T(8,128)S(1)} %get-tuple-element.70), channel_id=1, source_target_pairs={{0,384},{1,385},{2,386},{3,387},{4,388},{5,389},{6,390},{7,391},{8... | collective-permute-start | bytes 786440 | tf_op jit(solution)/shard_map/ppermute | solution.py:30
  (16 other events, 146.1 us)
Sparse Core Ops, SparseCore 0:
  86.6 36.1 all-gather.4
  138.4 67.8 all-gather.6

commit v20 on v19

--- a/solution.py
+++ b/solution.py
@@ -17,7 +17,6 @@
 X = 4
 GROUPS = [list(range(Y)), list(range(Y, MP))]
 SAME_CORE = [list(range(core, DP, 2)) for core in range(2)]
-SAME_X = [list(range(x * DP // X, (x + 1) * DP // X)) for x in range(X)]
 X_SLOTS = np.array([0, 2, 1, 3])
 Z_SLOTS = np.array([0, 3, 2, 1])
 ALONG_X = [(8 * int(k),) for k in X_SLOTS[1:]]
@@ -32,6 +31,16 @@
 
 def partner(array):
     return swap(array, 2)
+
+
+def along_ring(array, step):
+    pairs = []
+    for i in range(DP * MP):
+        data, model = divmod(i, MP)
+        z = (model // Y * 4 + data // 2 % 4 + step) % 8
+        target = (data // 8 * 8 + z % 4 * 2 + data % 2) * MP + z // 4 * Y + model % Y
+        pairs.append((i, target))
+    return lax.ppermute(array, ("dp", "mp"), pairs)
 
 
 def gather(block, masks, *later):
@@ -86,21 +95,27 @@
     )(order, inputs, own, other, *before)
 
 
-def weight_kernel(targets_ref, grad_ref, columns_ref, *refs):
+def weight_kernel(targets_ref, sources_ref, grad_ref, own_ref, other_ref, *refs):
     before, outs = refs[:-X], refs[-X:]
-    slices, devices, share, wide = columns_ref.shape
-    rows = wide // X
-    half = slices // 2
-    features = grad_ref.shape[0]
+    features, depth = grad_ref.shape
+    places, share, wide = own_ref.shape
+    rows, images = wide // X, share // 2
+    pieces = []
+    for view in range(2):
+        for k in range(2 * places):
+            start = view * (depth // 2) + sources_ref[k] * images
+            pieces.append(grad_ref[:, pl.ds(pl.multiple_of(start, images), images)])
+    grad = jnp.concatenate(pieces, axis=1)
     for k in range(X):
         target = pl.ds(pl.multiple_of(targets_ref[k] * rows, rows), rows)
         pieces = [
-            columns_ref[half * view : half * (view + 1), d, :, target].reshape(half * share, rows)
+            ref[place, images * view : images * (view + 1), target]
             for view in range(2)
-            for d in range(devices)
+            for ref in (own_ref, other_ref)
+            for place in range(places)
         ]
         columns = jnp.concatenate(pieces, axis=0)
-        result = jnp.dot(grad_ref[...], columns, preferred_element_type=jnp.float32)
+        result = jnp.dot(grad, columns, preferred_element_type=jnp.float32)
         if before:
             outs[k][:features] = before[k][...]
             outs[k][features:] = result
@@ -108,21 +123,21 @@
             outs[k][...] = result
 
 
-def weight_half(targets, grad, columns, *before):
+def weight_half(targets, grad, sources, own, other, *before):
     half, depth = grad.shape
-    wide = columns.shape[3]
+    wide = own.shape[2]
     features = 2 * half if before else half
-    vmem = pl.BlockSpec(memory_space=pltpu.VMEM)
+    smem, vmem = pl.BlockSpec(memory_space=pltpu.SMEM), pl.BlockSpec(memory_space=pltpu.VMEM)
     return pl.pallas_call(
         weight_kernel,
-        in_specs=[pl.BlockSpec(memory_space=pltpu.SMEM)] + [vmem] * (2 + len(before)),
+        in_specs=[smem, smem] + [vmem] * (3 + len(before)),
         out_specs=[vmem] * X,
         out_shape=[jax.ShapeDtypeStruct((features, wide // X), jnp.float32)] * X,
         compiler_params=pltpu.CompilerParams(vmem_limit_bytes=16 * 1024 * 1024),
         cost_estimate=pl.CostEstimate(
             flops=2 * half * depth * wide, bytes_accessed=5 * 1024 * 1024, transcendentals=0
         ),
-    )(targets, grad, columns, *before)
+    )(targets, sources, grad, own, other, *before)
 
 
 def finish_kernel(position_ref, *refs):
@@ -159,14 +174,26 @@
     distance = place >> 4 | X_SLOTS[place >> 2 & 3] << 3 | Z_SLOTS[place & 3] << 1
     position = (data_index & 1 ^ jnp.asarray(place & 1, jnp.int32)) << 4 | jnp.asarray(place >> 1, jnp.int32)
 
-    share = views * images // Y
-    mine = lax.dynamic_slice_in_dim(flat, lax.rem(model_index, Y) * share, share, axis=0)
-    pieces = mine.reshape(share, X, DP // X, rows).transpose(2, 0, 1, 3).reshape(DP // X, share, X * rows)
+    core, z = data_index & 1, data_index >> 1 & 3
+    by_place = flat.reshape(views * images, X, 4, 2, rows)
+
+    def piece(step, other):
+        start = (0, 0, z + step & 3, core ^ other, 0)
+        taken = lax.dynamic_slice(by_place, start, (views * images, X, 1, 1, rows))
+        return taken.reshape(views * images, X * rows)
+
+    steps = (0, 2, 1, -1)
+    columns = [jnp.stack([piece(step, other) for other in (0, 1)]) for step in steps]
+    sources = jnp.stack([(z - step & 3) * 2 + (core ^ other) for other in (0, 1) for step in steps])
+
     along_z = gather(weight, ALONG_Z)[0]
     parts = [along_z] + [swap(along_z, *mask) for mask in ALONG_X]
     projected = ()
     for k in (0, 2):
-        weight_own, pieces = lax.optimization_barrier((jnp.stack(parts[k : k + 2]), pieces))
+        weight_own = jnp.stack(parts[k : k + 2])
+        if k == 0:
+            weight_own, columns = lax.optimization_barrier((weight_own, columns))
+            columns[1] = along_ring(columns[1], steps[1])
         weight_other = swap(weight_own, 1)
         blocks = np.concatenate([4 * k + np.arange(8), 16 + 4 * k + np.arange(8)])
         half = (DP // 4, rows, feat)
@@ -185,15 +212,13 @@
     normed = (centered * inverse).astype(jnp.bfloat16).transpose(2, 1, 0, 3).reshape(views + 1, block, total)
     inverse = inverse.reshape(block, views + 1).T[:views, :, None]
 
-    first, pair, pieces = lax.optimization_barrier((normed[0], normed[1:], pieces))
-    slices = lax.all_to_all(
-        pieces, "dp", split_axis=0, concat_axis=0, axis_index_groups=SAME_X
-    )
-    columns_b = lax.all_gather(pair, "mp", axis=0, axis_index_groups=GROUPS)
+    first, pair, columns = lax.optimization_barrier((normed[0], normed[1:], columns))
+    columns[2:] = [along_ring(part, step) for part, step in zip(columns[2:], steps[2:])]
+    copies = jnp.broadcast_to(pair[None], (Y,) + pair.shape)
+    columns_b = lax.all_to_all(copies, "mp", split_axis=0, concat_axis=0, axis_index_groups=GROUPS)
     columns_b = columns_b.reshape(MP * block, total)
-    rows_own, slices = gather(gather(first, STRIDED_Z)[0], ALONG_X, slices)
+    rows_own = gather(gather(first, STRIDED_Z)[0], ALONG_X)[0]
     rows_own, columns_b = lax.optimization_barrier((rows_own, columns_b))
-    columns = lax.all_gather(slices, "mp", axis=0, axis_index_groups=GROUPS)
     rows_other = swap(rows_own, 1).reshape(feat // 2, total)
     rows_own = rows_own.reshape(feat // 2, total)
 
@@ -237,7 +262,12 @@
     terms_own, terms_other = terms_own.reshape(shape), swap(terms_other.reshape(shape), 1)
     both = [(terms_own[k] + terms_other[k].astype(jnp.float32)).astype(jnp.bfloat16) for k in range(X)]
     along_x = add(both, ALONG_X)[0].astype(jnp.bfloat16)
-    grad_a, terms_b = add(along_x, STRIDED_Z, terms_b)
+    along_x, columns = lax.optimization_barrier((along_x, columns))
+    columns_own = jnp.stack([part[0] for part in columns])
+    columns_other = swap(jnp.stack([part[1] for part in columns]), 1)
+    grad_a, terms_b, columns_own, columns_other = add(
+        along_x, STRIDED_Z, terms_b, columns_own, columns_other
+    )
     grads = jnp.stack([grad_a, jnp.sum(terms_b.astype(jnp.float32), axis=0)])
     wide = normed[:views].astype(jnp.float32)
     grad_mean = jnp.sum(grads, axis=2, keepdims=True) / total
@@ -256,11 +286,11 @@
         concat_axis=0,
         axis_index_groups=SAME_CORE,
     )
-    grad_own, columns = lax.optimization_barrier((grad_own, columns))
     grad_other = swap(grad_own, 1)
     targets = data_index >> 3 ^ jnp.asarray(X_SLOTS, jnp.int32)
-    terms = weight_half(targets, grad_own.reshape(feat // 2, depth), columns)
-    terms = weight_half(targets, grad_other.reshape(feat // 2, depth), columns, *terms)
+    columns = (sources, columns_own, columns_other)
+    terms = weight_half(targets, grad_own.reshape(feat // 2, depth), *columns)
+    terms = weight_half(targets, grad_other.reshape(feat // 2, depth), *columns, *terms)
     return finish(position, [terms[0]] + [swap(terms[k + 1], *mask) for k, mask in enumerate(ALONG_X)])
 
 

time: 241 us -> 343 us (1.42)
  waiting for transfers between devices: 48.8 us -> 101 us
  local copies, waits for them, and re-layouts: 7.73 us -> 51.7 us
  starting transfers between devices: 108 us -> 143 us
  blocking collectives: 39.8 us -> 18.9 us
  between operations: 14.1 us -> 0.95 us
  other arithmetic: 6.88 us -> 12.6 us
    ppermute x0 -> x3, waiting for transfers between devices: none -> 48.8 us  [along_ring(): return lax.ppermute(array, ('dp', 'mp'), pairs)]
    dynamic_slice x1, local copies, waits for them, and re-layouts: 1.08 us -> 28.6 us  [piece(): taken = lax.dynamic_slice(by_place, start, (views * images, X, 1, 1, rows))]
    all_to_all x1 -> x0, blocking collectives: 20 us -> none  [per_device(): lax.all_to_all(projected.reshape(DP, block, (views + 1) * images), 'dp',...]
    another operation x0 -> x10, local copies, waits for them, and re-layouts: none -> 18.5 us  [the longest x8 10.6 us: per_device(): jnp.stack([piece(step, other) for other in (0, 1)])]
    ppermute x27 -> x28, starting transfers between devices: 97.8 us -> 113 us  [swap(): lax.ppermute(array, ('dp', 'mp'), [(i, i ^ mask) for i in range(DP * MP)])]
    ppermute x0 -> x3, starting transfers between devices: none -> 11.8 us  [along_ring(): return lax.ppermute(array, ('dp', 'mp'), pairs)]
    all_to_all x1 -> x2, waiting for transfers between devices: 0.01 us -> 9.84 us  [the longest x1 9.84 us: per_device(): lax.all_to_all(projected.reshape(DP, block, (views + 1) * images), 'dp',...]
    all_to_all x1 -> x2, starting transfers between devices: 3.51 us -> 11.5 us  [the longest x1 6.85 us: per_device(): lax.all_to_all(copies, 'mp', split_axis=0, concat_axis=0, axis_index_grou...]
  transfers between devices with their start and end apart: 31 -> 34, of which waited for: 18 -> 17; matrix products, arithmetic and copies ran while one was open for 5% -> 17% of each run, Pallas kernels for 1% -> 1%
where the time goes in v20:
time: 343 us; the launch traced here: 342 us
  starting transfers between devices  143 us (42%)
  waiting for transfers between devices  101 us (29%)
  local copies, waits for them, and re-layouts  51.7 us (15%)
  blocking collectives  18.9 us (6%)
  other arithmetic  12.6 us (4%)
  Pallas kernels  9.75 us (3%)
  matrix products  3.8 us (1%)
    ppermute x28, starting transfers between devices, swap(): lax.ppermute(array, ('dp', 'mp'), [(i, i ^ mask) for i in range(DP * MP)])  113 us
    ppermute x3, waiting for transfers between devices, along_ring(): return lax.ppermute(array, ('dp', 'mp'), pairs)  48.8 us
    ppermute x28, waiting for transfers between devices, swap(): lax.ppermute(array, ('dp', 'mp'), [(i, i ^ mask) for i in range(DP * MP)])  39.7 us
    dynamic_slice x1, local copies, waits for them, and re-layouts, piece(): taken = lax.dynamic_slice(by_place, start, (views * images, X, 1, 1, rows))  28.6 us
    all_to_all x1, blocking collectives, per_device(): lax.all_to_all(jnp.stack([part for part in blocks for _ in range(DP // X...  18.9 us
    ppermute x3, starting transfers between devices, along_ring(): return lax.ppermute(array, ('dp', 'mp'), pairs)  11.8 us
    another operation x8, local copies, waits for them, and re-layouts, per_device(): jnp.stack([piece(step, other) for other in (0, 1)])  10.6 us
    all_to_all x1, waiting for transfers between devices, per_device(): lax.all_to_all(projected.reshape(DP, block, (views + 1) * images), 'dp',...  9.84 us
  transfers between devices with their start and end apart: 34, of which 17 were waited for; matrix products, arithmetic and copies ran while one was open for 17% of the time, Pallas kernels for 1%

profile of v20, /device:TPU:1, one launch (start us, length us, event | category | flops | bytes accessed | tf_op | source)
XLA Modules:
  0.0 341.6 jit_solution(5008961348767183311)
XLA Ops:
  0.0 8.4 %collective-permute-start = (bf16[256,256]{1,0:T(8,128)(2,1)}, bf16[256,256]{1,0:T(8,128)(2,1)S(1)}, u32[]{:S(2)}, u32[]{:S(2)}) collective-permute-start(bf16[256,256]{1,0:T(8,128)(2,1)} %param.8), channel_id=1, source_target_pairs={{0,96},{1,97},{2,98},{3,99},{4,100},{5,101},{6,102},{7,103},{8,104... | collective-permute-start | bytes 393224 | tf_op jit(solution)/shard_map/ppermute | solution.py:29
  12.6 7.8 %reshape_reshape.3 = bf16[256,4,4,2,256]{4,3,2,1,0:T(2,128)(2,1)} reshape(bf16[2,128,8192]{2,1,0:T(8,128)(2,1)} %param.7) | data formatting | bytes 8388608 | tf_op jit(solution)/shard_map/reshape;reshape | solution.py:178
  21.5 4.6 %collective-permute-start.6 = (bf16[4,256,256]{2,1,0:T(8,128)(2,1)}, bf16[4,256,256]{2,1,0:T(8,128)(2,1)}, u32[]{:S(2)}, u32[]{:S(2)}) collective-permute-start(bf16[4,256,256]{2,1,0:T(8,128)(2,1)} %get-tuple-element.106), channel_id=1, source_target_pairs={{0,256},{1,257},{2,258},{3,259},{4,260},{5,261},{6,262},{7,263},{8... | collective-permute-start | bytes 1572872 | tf_op jit(solution)/shard_map/ppermute | solution.py:29
  30.9 28.6 %dynamic-slice_reduce_fusion.1 = (bf16[256,4,256]{2,1,0:T(4,128)(2,1)S(1)}, bf16[256,4,256]{2,1,0:T(4,128)(2,1)}, bf16[256,4,256]{2,1,0:T(4,128)(2,1)}, bf16[256...) fusion(bf16[256,4,4,2,256]{4,3,2,1,0:T(2,128)(2,1)} %reshape_re, ...), kind=kLoop, calls=%fused_computation.24 | loop fusion | bytes 8388632 | tf_op jit(solution)/shard_map/dynamic_slice | solution.py:182
  74.6 6.9 %collective-permute-start.7 = (bf16[2,4,256,256]{3,2,1,0:T(8,128)(2,1)S(1)}, bf16[2,4,256,256]{3,2,1,0:T(8,128)(2,1)S(1)}, u32[]{:S(2)}, u32[]{:S(2)}) collective-permute-start(bf16[2,4,256,256]{3,2,1,0:T(8,128)(2,1)S(1)} %pad_maximum_fusion.3), channel_id=1, source_target_pairs={{0,16},{1,17},{2,18},{3,19},{4,20},{5,21},{6,22},{7,23},{8,24},{9,... | collective-permute-start | bytes 3145736 | tf_op jit(solution)/shard_map/ppermute | solution.py:29
  89.5 4.7 %all-to-all-start = ((f32[32,8,384]{2,1,0:T(8,128)}), f32[32,8,384]{2,1,0:T(8,128)S(1)}, u32[]{:S(2)}, u32[]{:S(2)}) async-start(f32[32,8,384]{2,1,0:T(8,128)} %bitcast.21), calls=%async_computation | async-start | bytes 786432 | tf_op jit(solution)/shard_map/all_to_all | solution.py:205
  94.2 4.2 %collective-permute-start.8 = (bf16[2,256,1024]{2,1,0:T(8,128)(2,1)S(1)}, bf16[2,256,1024]{2,1,0:T(8,128)(2,1)S(1)}, u32[]{:S(2)}, u32[]{:S(2)}) collective-permute-start(bf16[2,256,1024]{2,1,0:T(8,128)(2,1)S(1)} %get-tuple-element.47), channel_id=1, source_target_pairs={{0,64},{1,65},{2,66},{3,67},{4,68},{5,69},{6,70},{7,71},{8,72},{9,... | collective-permute-start | bytes 3145736 | tf_op jit(solution)/shard_map/ppermute | solution.py:43
  98.4 9.8 %all-to-all-done = f32[32,8,384]{2,1,0:T(8,128)S(1)} async-done(((f32[32,8,384]{2,1,0:T(8,128)}), f32[32,8,384]{2,1,0:T(8,128)S(1)}, u32[]{:S(2)}, u32[]{:S(2)}) %all-to-all-start) | async-done | bytes 393248 | tf_op jit(solution)/shard_map/all_to_all | solution.py:205
  108.8 26.7 %collective-permute-done.8 = bf16[2,256,1024]{2,1,0:T(8,128)(2,1)S(1)} collective-permute-done((bf16[2,256,1024]{2,1,0:T(8,128)(2,1)S(1)}, bf16[2,256,1024]{2,1,0:T(8,128)(2,1)S(1)}, u32[]{:S(2)}, u32[]{:S(2)}) %collective-permute-start.8) | collective-permute-done | bytes 1048608 | tf_op jit(solution)/shard_map/ppermute | solution.py:43
  136.7 6.8 %all-to-all-start.1 = ((bf16[8,2,8,4096]{3,2,1,0:T(8,128)(2,1)}), bf16[8,2,8,4096]{3,2,1,0:T(8,128)(2,1)S(1)}, u32[]{:S(2)}, u32[]{:S(2)}) async-start(bf16[8,2,8,4096]{3,2,1,0:T(8,128)(2,1)} %broadcast_in_dim.2), calls=%async_computation.1 | async-start | bytes 2097152 | tf_op jit(solution)/shard_map/all_to_all | solution.py:218
  143.5 18.2 %collective-permute-start.9 = (bf16[8,4096]{1,0:T(8,128)(2,1)S(1)}, bf16[8,4096]{1,0:T(8,128)(2,1)S(1)}, u32[]{:S(2)}, u32[]{:S(2)}) collective-permute-start(bf16[8,4096]{1,0:T(8,128)(2,1)S(1)} %slice_bitcast_fusion.9), channel_id=1, source_target_pairs={{0,8},{1,9},{2,10},{3,11},{4,12},{5,13},{6,14},{7,15},{8,0},{9,1},... | collective-permute-start | bytes 196616 | tf_op jit(solution)/shard_map/ppermute | solution.py:29
  161.8 5.0 %collective-permute-start.10 = (bf16[8,4096]{1,0:T(8,128)(2,1)S(1)}, bf16[8,4096]{1,0:T(8,128)(2,1)S(1)}, u32[]{:S(2)}, u32[]{:S(2)}) collective-permute-start(bf16[8,4096]{1,0:T(8,128)(2,1)S(1)} %slice_bitcast_fusion.9), channel_id=1, source_target_pairs={{0,64},{1,65},{2,66},{3,67},{4,68},{5,69},{6,70},{7,71},{8,72},{9,... | collective-permute-start | bytes 196616 | tf_op jit(solution)/shard_map/ppermute | solution.py:29
  168.7 5.2 %collective-permute-done.11 = bf16[8,4096]{1,0:T(8,128)(2,1)S(1)} collective-permute-done((bf16[8,4096]{1,0:T(8,128)(2,1)S(1)}, bf16[8,4096]{1,0:T(8,128)(2,1)S(1)}, u32[]{:S(2)}, u32[]{:S(2)}) %collective-permute-start.11) | collective-permute-done | bytes 65568 | tf_op jit(solution)/shard_map/ppermute | solution.py:29
  173.9 4.9 %collective-permute-start.12 = (bf16[4,8,4096]{2,1,0:T(8,128)(2,1)S(1)}, bf16[4,8,4096]{2,1,0:T(8,128)(2,1)S(1)}, u32[]{:S(2)}, u32[]{:S(2)}) collective-permute-start(bf16[4,8,4096]{2,1,0:T(8,128)(2,1)S(1)} %get-tuple-element.114), channel_id=1, source_target_pairs={{0,256},{1,257},{2,258},{3,259},{4,260},{5,261},{6,262},{7,263},{8... | collective-permute-start | bytes 786440 | tf_op jit(solution)/shard_map/ppermute | solution.py:29
  183.6 5.1 %collective-permute-done.13 = bf16[4,8,4096]{2,1,0:T(8,128)(2,1)S(1)} collective-permute-done((bf16[4,8,4096]{2,1,0:T(8,128)(2,1)S(1)}, bf16[4,8,4096]{2,1,0:T(8,128)(2,1)S(1)}, u32[]{:S(2)}, u32[]{:S(2)}) %collective-permute-start.13) | collective-permute-done | bytes 262176 | tf_op jit(solution)/shard_map/ppermute | solution.py:29
  190.3 5.7 %collective-permute-start.15 = (bf16[4,4,8,4096]{3,2,1,0:T(8,128)(2,1)S(1)}, bf16[4,4,8,4096]{3,2,1,0:T(8,128)(2,1)S(1)}, u32[]{:S(2)}, u32[]{:S(2)}) collective-permute-start(bf16[4,4,8,4096]{3,2,1,0:T(8,128)(2,1)S(1)} %pad_maximum_fusion.8), channel_id=1, source_target_pairs={{0,16},{1,17},{2,18},{3,19},{4,20},{5,21},{6,22},{7,23},{8,24},{9,... | collective-permute-start | bytes 3145736 | tf_op jit(solution)/shard_map/ppermute | solution.py:29
  213.2 5.4 %collective-permute-start.20 = (bf16[2,256,1024]{2,1,0:T(8,128)(2,1)S(1)}, bf16[2,256,1024]{2,1,0:T(8,128)(2,1)S(1)}, u32[]{:S(2)}, u32[]{:S(2)}) collective-permute-start(bf16[2,256,1024]{2,1,0:T(8,128)(2,1)S(1)} %copy-done.14), channel_id=1, source_target_pairs={{0,32},{1,33},{2,34},{3,35},{4,36},{5,37},{6,38},{7,39},{8,40},{9,... | collective-permute-start | bytes 3145736 | tf_op jit(solution)/shard_map/ppermute | solution.py:43
  221.7 18.3 %collective-permute-done.20 = bf16[2,256,1024]{2,1,0:T(8,128)(2,1)S(1)} collective-permute-done((bf16[2,256,1024]{2,1,0:T(8,128)(2,1)S(1)}, bf16[2,256,1024]{2,1,0:T(8,128)(2,1)S(1)}, u32[]{:S(2)}, u32[]{:S(2)}) %collective-permute-start.20) | collective-permute-done | bytes 1048608 | tf_op jit(solution)/shard_map/ppermute | solution.py:43
  248.1 4.1 %collective-permute-start.26 = (bf16[4,256,1024]{2,1,0:T(8,128)(2,1)}, bf16[4,256,1024]{2,1,0:T(8,128)(2,1)}, u32[]{:S(2)}, u32[]{:S(2)}) collective-permute-start(bf16[4,256,1024]{2,1,0:T(8,128)(2,1)} %pad_maximum_fusion.1), channel_id=1, source_target_pairs={{0,16},{1,17},{2,18},{3,19},{4,20},{5,21},{6,22},{7,23},{8,24},{9,... | collective-permute-start | bytes 6291464 | tf_op jit(solution)/shard_map/ppermute | solution.py:29
  254.5 13.2 %collective-permute-done.25 = bf16[64,4096]{1,0:T(8,128)(2,1)S(1)} collective-permute-done((bf16[64,4096]{1,0:T(8,128)(2,1)S(1)}, bf16[64,4096]{1,0:T(8,128)(2,1)S(1)}, u32[]{:S(2)}, u32[]{:S(2)}) %collective-permute-start.25) | collective-permute-done | bytes 524320 | tf_op jit(solution)/shard_map/ppermute | solution.py:29
  268.8 7.0 %all-to-all-start.2 = ((bf16[8,8,4096]{2,1,0:T(8,128)(2,1)}), bf16[8,8,4096]{2,1,0:T(8,128)(2,1)S(1)}, u32[]{:S(2)}, u32[]{:S(2)}) async-start(bf16[8,8,4096]{2,1,0:T(8,128)(2,1)} %fusion.6), calls=%async_computation.2 | async-start | bytes 1048576 | tf_op jit(solution)/shard_map/all_to_all | solution.py:256
  277.8 5.1 %collective-permute-start.23 = (bf16[8,4096]{1,0:T(8,128)(2,1)S(1)}, bf16[8,4096]{1,0:T(8,128)(2,1)S(1)}, u32[]{:S(2)}, u32[]{:S(2)}) collective-permute-start(bf16[8,4096]{1,0:T(8,128)(2,1)S(1)} %get-tuple-element.110), channel_id=1, source_target_pairs={{0,64},{1,65},{2,66},{3,67},{4,68},{5,69},{6,70},{7,71},{8,72},{9,... | collective-permute-start | bytes 196616 | tf_op jit(solution)/shard_map/ppermute | solution.py:29
  282.9 4.3 %collective-permute-start.24 = (bf16[8,4096]{1,0:T(8,128)(2,1)S(1)}, bf16[8,4096]{1,0:T(8,128)(2,1)}, u32[]{:S(2)}, u32[]{:S(2)}) collective-permute-start(bf16[8,4096]{1,0:T(8,128)(2,1)S(1)} %get-tuple-element.109), channel_id=1, source_target_pairs={{0,72},{1,73},{2,74},{3,75},{4,76},{5,77},{6,78},{7,79},{8,64},{9,... | collective-permute-start | bytes 196616 | tf_op jit(solution)/shard_map/ppermute | solution.py:29
  295.3 18.9 %all_to_all.20 = bf16[16,8,2048]{2,1,0:T(8,128)(2,1)S(1)} all-to-all(bf16[16,8,2048]{2,1,0:T(8,128)(2,1)S(1)} %constant_dynamic-update-slice_fusion), channel_id=1, replica_groups={{0,32,64,96,128,160,192,224,256,288,320,352,384,416,448,480},{16,48,80,..., dimensions={0} | all-to-all | bytes 1048576 | tf_op jit(solution)/shard_map/all_to_all | solution.py:282
  (169 shorter events, 111.4 us)
Async XLA Ops:
  0.0 20.4 %collective-permute-start = (bf16[256,256]{1,0:T(8,128)(2,1)}, bf16[256,256]{1,0:T(8,128)(2,1)S(1)}, u32[]{:S(2)}, u32[]{:S(2)}) collective-permute-start(bf16[256,256]{1,0:T(8,128)(2,1)} %param.8), channel_id=1, source_target_pairs={{0,96},{1,97},{2,98},{3,99},{4,100},{5,101},{6,102},{7,103},{8,104... | collective-permute-start | bytes 393224 | tf_op jit(solution)/shard_map/ppermute | solution.py:29
  8.4 12.0 %collective-permute-start.1 = (bf16[256,256]{1,0:T(8,128)(2,1)}, bf16[256,256]{1,0:T(8,128)(2,1)S(1)}, u32[]{:S(2)}, u32[]{:S(2)}) collective-permute-start(bf16[256,256]{1,0:T(8,128)(2,1)} %param.8), channel_id=1, source_target_pairs={{0,64},{1,65},{2,66},{3,67},{4,68},{5,69},{6,70},{7,71},{8,72},{9,... | collective-permute-start | bytes 393224 | tf_op jit(solution)/shard_map/ppermute | solution.py:29
  10.4 10.1 %collective-permute-start.2 = (bf16[256,256]{1,0:T(8,128)(2,1)}, bf16[256,256]{1,0:T(8,128)(2,1)S(1)}, u32[]{:S(2)}, u32[]{:S(2)}) collective-permute-start(bf16[256,256]{1,0:T(8,128)(2,1)} %param.8), channel_id=1, source_target_pairs={{0,32},{1,33},{2,34},{3,35},{4,36},{5,37},{6,38},{7,39},{8,40},{9,... | collective-permute-start | bytes 393224 | tf_op jit(solution)/shard_map/ppermute | solution.py:29
  21.5 51.8 %collective-permute-start.6 = (bf16[4,256,256]{2,1,0:T(8,128)(2,1)}, bf16[4,256,256]{2,1,0:T(8,128)(2,1)}, u32[]{:S(2)}, u32[]{:S(2)}) collective-permute-start(bf16[4,256,256]{2,1,0:T(8,128)(2,1)} %get-tuple-element.106), channel_id=1, source_target_pairs={{0,256},{1,257},{2,258},{3,259},{4,260},{5,261},{6,262},{7,263},{8... | collective-permute-start | bytes 1572872 | tf_op jit(solution)/shard_map/ppermute | solution.py:29
  26.2 55.4 %collective-permute-start.3 = (bf16[4,256,256]{2,1,0:T(8,128)(2,1)}, bf16[4,256,256]{2,1,0:T(8,128)(2,1)}, u32[]{:S(2)}, u32[]{:S(2)}) collective-permute-start(bf16[4,256,256]{2,1,0:T(8,128)(2,1)} %get-tuple-element.106), channel_id=1, source_target_pairs={{0,128},{1,129},{2,130},{3,131},{4,132},{5,133},{6,134},{7,135},{8... | collective-permute-start | bytes 1572872 | tf_op jit(solution)/shard_map/ppermute | solution.py:29
  28.4 53.2 %collective-permute-start.4 = (bf16[4,256,256]{2,1,0:T(8,128)(2,1)}, bf16[4,256,256]{2,1,0:T(8,128)(2,1)}, u32[]{:S(2)}, u32[]{:S(2)}) collective-permute-start(bf16[4,256,256]{2,1,0:T(8,128)(2,1)} %get-tuple-element.106), channel_id=1, source_target_pairs={{0,384},{1,385},{2,386},{3,387},{4,388},{5,389},{6,390},{7,391},{8... | collective-permute-start | bytes 1572872 | tf_op jit(solution)/shard_map/ppermute | solution.py:29
  74.6 10.3 %collective-permute-start.7 = (bf16[2,4,256,256]{3,2,1,0:T(8,128)(2,1)S(1)}, bf16[2,4,256,256]{3,2,1,0:T(8,128)(2,1)S(1)}, u32[]{:S(2)}, u32[]{:S(2)}) collective-permute-start(bf16[2,4,256,256]{3,2,1,0:T(8,128)(2,1)S(1)} %pad_maximum_fusion.3), channel_id=1, source_target_pairs={{0,16},{1,17},{2,18},{3,19},{4,20},{5,21},{6,22},{7,23},{8,24},{9,... | collective-permute-start | bytes 3145736 | tf_op jit(solution)/shard_map/ppermute | solution.py:29
  89.5 18.7 %all-to-all-start = ((f32[32,8,384]{2,1,0:T(8,128)}), f32[32,8,384]{2,1,0:T(8,128)S(1)}, u32[]{:S(2)}, u32[]{:S(2)}) async-start(f32[32,8,384]{2,1,0:T(8,128)} %bitcast.21), calls=%async_computation | async-start | bytes 786432 | tf_op jit(solution)/shard_map/all_to_all | solution.py:205
  94.2 41.2 %collective-permute-start.8 = (bf16[2,256,1024]{2,1,0:T(8,128)(2,1)S(1)}, bf16[2,256,1024]{2,1,0:T(8,128)(2,1)S(1)}, u32[]{:S(2)}, u32[]{:S(2)}) collective-permute-start(bf16[2,256,1024]{2,1,0:T(8,128)(2,1)S(1)} %get-tuple-element.47), channel_id=1, source_target_pairs={{0,64},{1,65},{2,66},{3,67},{4,68},{5,69},{6,70},{7,71},{8,72},{9,... | collective-permute-start | bytes 3145736 | tf_op jit(solution)/shard_map/ppermute | solution.py:43
  136.7 53.6 %all-to-all-start.1 = ((bf16[8,2,8,4096]{3,2,1,0:T(8,128)(2,1)}), bf16[8,2,8,4096]{3,2,1,0:T(8,128)(2,1)S(1)}, u32[]{:S(2)}, u32[]{:S(2)}) async-start(bf16[8,2,8,4096]{3,2,1,0:T(8,128)(2,1)} %broadcast_in_dim.2), calls=%async_computation.1 | async-start | bytes 2097152 | tf_op jit(solution)/shard_map/all_to_all | solution.py:218
  143.5 25.2 %collective-permute-start.9 = (bf16[8,4096]{1,0:T(8,128)(2,1)S(1)}, bf16[8,4096]{1,0:T(8,128)(2,1)S(1)}, u32[]{:S(2)}, u32[]{:S(2)}) collective-permute-start(bf16[8,4096]{1,0:T(8,128)(2,1)S(1)} %slice_bitcast_fusion.9), channel_id=1, source_target_pairs={{0,8},{1,9},{2,10},{3,11},{4,12},{5,13},{6,14},{7,15},{8,0},{9,1},... | collective-permute-start | bytes 196616 | tf_op jit(solution)/shard_map/ppermute | solution.py:29
  204.2 16.6 %collective-permute-start.17 = (bf16[4,8,4096]{2,1,0:T(8,128)(2,1)S(1)}, bf16[4,8,4096]{2,1,0:T(8,128)(2,1)S(1)}, u32[]{:S(2)}, u32[]{:S(2)}) collective-permute-start(bf16[4,8,4096]{2,1,0:T(8,128)(2,1)S(1)} %get-tuple-element.95), channel_id=1, source_target_pairs={{0,256},{1,257},{2,258},{3,259},{4,260},{5,261},{6,262},{7,263},{8... | collective-permute-start | bytes 786440 | tf_op jit(solution)/shard_map/ppermute | solution.py:29
  207.9 12.9 %collective-permute-start.18 = (bf16[4,8,4096]{2,1,0:T(8,128)(2,1)S(1)}, bf16[4,8,4096]{2,1,0:T(8,128)(2,1)S(1)}, u32[]{:S(2)}, u32[]{:S(2)}) collective-permute-start(bf16[4,8,4096]{2,1,0:T(8,128)(2,1)S(1)} %get-tuple-element.94), channel_id=1, source_target_pairs={{0,128},{1,129},{2,130},{3,131},{4,132},{5,133},{6,134},{7,135},{8... | collective-permute-start | bytes 786440 | tf_op jit(solution)/shard_map/ppermute | solution.py:29
  210.3 10.6 %collective-permute-start.19 = (bf16[4,8,4096]{2,1,0:T(8,128)(2,1)S(1)}, bf16[4,8,4096]{2,1,0:T(8,128)(2,1)S(1)}, u32[]{:S(2)}, u32[]{:S(2)}) collective-permute-start(bf16[4,8,4096]{2,1,0:T(8,128)(2,1)S(1)} %get-tuple-element.93), channel_id=1, source_target_pairs={{0,384},{1,385},{2,386},{3,387},{4,388},{5,389},{6,390},{7,391},{8... | collective-permute-start | bytes 786440 | tf_op jit(solution)/shard_map/ppermute | solution.py:29
  213.2 26.8 %collective-permute-start.20 = (bf16[2,256,1024]{2,1,0:T(8,128)(2,1)S(1)}, bf16[2,256,1024]{2,1,0:T(8,128)(2,1)S(1)}, u32[]{:S(2)}, u32[]{:S(2)}) collective-permute-start(bf16[2,256,1024]{2,1,0:T(8,128)(2,1)S(1)} %copy-done.14), channel_id=1, source_target_pairs={{0,32},{1,33},{2,34},{3,35},{4,36},{5,37},{6,38},{7,39},{8,40},{9,... | collective-permute-start | bytes 3145736 | tf_op jit(solution)/shard_map/ppermute | solution.py:43
  218.6 25.2 %collective-permute-start.21 = (bf16[2,256,1024]{2,1,0:T(8,128)(2,1)S(1)}, bf16[2,256,1024]{2,1,0:T(8,128)(2,1)S(1)}, u32[]{:S(2)}, u32[]{:S(2)}) collective-permute-start(bf16[2,256,1024]{2,1,0:T(8,128)(2,1)S(1)} %copy-done.13), channel_id=1, source_target_pairs={{0,104},{1,105},{2,106},{3,107},{4,108},{5,109},{6,110},{7,111},{8... | collective-permute-start | bytes 3145736 | tf_op jit(solution)/shard_map/ppermute | solution.py:43
  248.1 45.6 %collective-permute-start.26 = (bf16[4,256,1024]{2,1,0:T(8,128)(2,1)}, bf16[4,256,1024]{2,1,0:T(8,128)(2,1)}, u32[]{:S(2)}, u32[]{:S(2)}) collective-permute-start(bf16[4,256,1024]{2,1,0:T(8,128)(2,1)} %pad_maximum_fusion.1), channel_id=1, source_target_pairs={{0,16},{1,17},{2,18},{3,19},{4,20},{5,21},{6,22},{7,23},{8,24},{9,... | collective-permute-start | bytes 6291464 | tf_op jit(solution)/shard_map/ppermute | solution.py:29
  252.3 15.4 %collective-permute-start.25 = (bf16[64,4096]{1,0:T(8,128)(2,1)S(1)}, bf16[64,4096]{1,0:T(8,128)(2,1)S(1)}, u32[]{:S(2)}, u32[]{:S(2)}) collective-permute-start(bf16[64,4096]{1,0:T(8,128)(2,1)S(1)} %fusion.5), channel_id=1, source_target_pairs={{0,32},{1,33},{2,34},{3,35},{4,36},{5,37},{6,38},{7,39},{8,40},{9,... | collective-permute-start | bytes 1572872 | tf_op jit(solution)/shard_map/ppermute | solution.py:29
  268.8 24.9 %all-to-all-start.2 = ((bf16[8,8,4096]{2,1,0:T(8,128)(2,1)}), bf16[8,8,4096]{2,1,0:T(8,128)(2,1)S(1)}, u32[]{:S(2)}, u32[]{:S(2)}) async-start(bf16[8,8,4096]{2,1,0:T(8,128)(2,1)} %fusion.6), calls=%async_computation.2 | async-start | bytes 1048576 | tf_op jit(solution)/shard_map/all_to_all | solution.py:256
  275.9 13.0 %collective-permute-start.22 = (bf16[8,4096]{1,0:T(8,128)(2,1)S(1)}, bf16[8,4096]{1,0:T(8,128)(2,1)S(1)}, u32[]{:S(2)}, u32[]{:S(2)}) collective-permute-start(bf16[8,4096]{1,0:T(8,128)(2,1)S(1)} %get-tuple-element.111), channel_id=1, source_target_pairs={{0,8},{1,9},{2,10},{3,11},{4,12},{5,13},{6,14},{7,15},{8,0},{9,1},... | collective-permute-start | bytes 196616 | tf_op jit(solution)/shard_map/ppermute | solution.py:29
  277.8 11.1 %collective-permute-start.23 = (bf16[8,4096]{1,0:T(8,128)(2,1)S(1)}, bf16[8,4096]{1,0:T(8,128)(2,1)S(1)}, u32[]{:S(2)}, u32[]{:S(2)}) collective-permute-start(bf16[8,4096]{1,0:T(8,128)(2,1)S(1)} %get-tuple-element.110), channel_id=1, source_target_pairs={{0,64},{1,65},{2,66},{3,67},{4,68},{5,69},{6,70},{7,71},{8,72},{9,... | collective-permute-start | bytes 196616 | tf_op jit(solution)/shard_map/ppermute | solution.py:29
  323.0 11.3 %collective-permute-start.28 = (f32[256,256]{1,0:T(8,128)S(1)}, f32[256,256]{1,0:T(8,128)S(1)}, u32[]{:S(2)}, u32[]{:S(2)}) collective-permute-start(f32[256,256]{1,0:T(8,128)S(1)} %get-tuple-element.82), channel_id=1, source_target_pairs={{0,256},{1,257},{2,258},{3,259},{4,260},{5,261},{6,262},{7,263},{8... | collective-permute-start | bytes 786440 | tf_op jit(solution)/shard_map/ppermute | solution.py:29
  325.6 12.5 %collective-permute-start.29 = (f32[256,256]{1,0:T(8,128)S(1)}, f32[256,256]{1,0:T(8,128)S(1)}, u32[]{:S(2)}, u32[]{:S(2)}) collective-permute-start(f32[256,256]{1,0:T(8,128)S(1)} %get-tuple-element.83), channel_id=1, source_target_pairs={{0,128},{1,129},{2,130},{3,131},{4,132},{5,133},{6,134},{7,135},{8... | collective-permute-start | bytes 786440 | tf_op jit(solution)/shard_map/ppermute | solution.py:29
  328.0 12.1 %collective-permute-start.30 = (f32[256,256]{1,0:T(8,128)S(1)}, f32[256,256]{1,0:T(8,128)S(1)}, u32[]{:S(2)}, u32[]{:S(2)}) collective-permute-start(f32[256,256]{1,0:T(8,128)S(1)} %get-tuple-element.84), channel_id=1, source_target_pairs={{0,384},{1,385},{2,386},{3,387},{4,388},{5,389},{6,390},{7,391},{8... | collective-permute-start | bytes 786440 | tf_op jit(solution)/shard_map/ppermute | solution.py:29
  (31 other events, 310.3 us)

commit v21 on v19

--- a/solution.py
+++ b/solution.py
@@ -162,11 +162,16 @@
     share = views * images // Y
     mine = lax.dynamic_slice_in_dim(flat, lax.rem(model_index, Y) * share, share, axis=0)
     pieces = mine.reshape(share, X, DP // X, rows).transpose(2, 0, 1, 3).reshape(DP // X, share, X * rows)
-    along_z = gather(weight, ALONG_Z)[0]
+    along_z, pieces = gather(weight, ALONG_Z, pieces)
+    slices = lax.all_to_all(
+        pieces, "dp", split_axis=0, concat_axis=0, axis_index_groups=SAME_X
+    )
     parts = [along_z] + [swap(along_z, *mask) for mask in ALONG_X]
     projected = ()
     for k in (0, 2):
-        weight_own, pieces = lax.optimization_barrier((jnp.stack(parts[k : k + 2]), pieces))
+        weight_own = jnp.stack(parts[k : k + 2])
+        if k == 0:
+            weight_own, slices = lax.optimization_barrier((weight_own, slices))
         weight_other = swap(weight_own, 1)
         blocks = np.concatenate([4 * k + np.arange(8), 16 + 4 * k + np.arange(8)])
         half = (DP // 4, rows, feat)
@@ -185,14 +190,11 @@
     normed = (centered * inverse).astype(jnp.bfloat16).transpose(2, 1, 0, 3).reshape(views + 1, block, total)
     inverse = inverse.reshape(block, views + 1).T[:views, :, None]
 
-    first, pair, pieces = lax.optimization_barrier((normed[0], normed[1:], pieces))
-    slices = lax.all_to_all(
-        pieces, "dp", split_axis=0, concat_axis=0, axis_index_groups=SAME_X
-    )
-    columns_b = lax.all_gather(pair, "mp", axis=0, axis_index_groups=GROUPS)
+    first, pair = lax.optimization_barrier((normed[0], normed[1:]))
+    copies = jnp.broadcast_to(pair[None], (Y,) + pair.shape)
+    columns_b = lax.all_to_all(copies, "mp", split_axis=0, concat_axis=0, axis_index_groups=GROUPS)
     columns_b = columns_b.reshape(MP * block, total)
-    rows_own, slices = gather(gather(first, STRIDED_Z)[0], ALONG_X, slices)
-    rows_own, columns_b = lax.optimization_barrier((rows_own, columns_b))
+    rows_own, columns_b = gather(gather(first, STRIDED_Z)[0], ALONG_X, columns_b)
     columns = lax.all_gather(slices, "mp", axis=0, axis_index_groups=GROUPS)
     rows_other = swap(rows_own, 1).reshape(feat // 2, total)
     rows_own = rows_own.reshape(feat // 2, total)
@@ -226,7 +228,9 @@
         for k in (0, 1)
     ]
     away = terms_b[1].astype(jnp.bfloat16)
-    corr_own, corr_other, away = lax.optimization_barrier((corr_own, corr_other, away))
+    corr_own, corr_other, away, columns = lax.optimization_barrier(
+        (corr_own, corr_other, away, columns)
+    )
     terms_b = (terms_b[0] + partner(away).astype(jnp.float32)).astype(jnp.bfloat16)
     terms_b = lax.all_to_all(
         terms_b.reshape(Y, block, total), "mp", split_axis=0, concat_axis=0, axis_index_groups=GROUPS
@@ -250,13 +254,14 @@
         for x in range(X)
     ]
     grad_own = lax.all_to_all(
-        jnp.stack([part for part in blocks for _ in range(DP // X // 2)]),
+        jnp.broadcast_to(jnp.stack(blocks)[:, None], (X, DP // X // 2, block, depth)).reshape(
+            DP // 2, block, depth
+        ),
         "dp",
         split_axis=0,
         concat_axis=0,
         axis_index_groups=SAME_CORE,
     )
-    grad_own, columns = lax.optimization_barrier((grad_own, columns))
     grad_other = swap(grad_own, 1)
     targets = data_index >> 3 ^ jnp.asarray(X_SLOTS, jnp.int32)
     terms = weight_half(targets, grad_own.reshape(feat // 2, depth), columns)

time: 241 us -> 260 us (1.079)
  waiting for transfers between devices: 48.8 us -> 79.1 us
  blocking collectives: 39.8 us -> 21.5 us
  starting transfers between devices: 108 us -> 116 us
    all_to_all x0 -> x2, waiting for transfers between devices: none -> 26.6 us  [the longest x1 13.3 us: per_device(): lax.all_to_all(projected.reshape(DP, block, (views + 1) * images), 'dp',...]
    all_to_all x2 -> x1, blocking collectives: 39.8 us -> 21.5 us  [per_device(): lax.all_to_all(jnp.broadcast_to(jnp.stack(blocks)[:, None], (X, DP // X /...]
    all_to_all x0 -> x2, starting transfers between devices: none -> 12.8 us  [the longest x1 6.84 us: per_device(): lax.all_to_all(copies, 'mp', split_axis=0, concat_axis=0, axis_index_grou...]
    all_gather x1, waiting for transfers between devices: 0.19 us -> 12.9 us  [per_device(): columns = lax.all_gather(slices, 'mp', axis=0, axis_index_groups=GROUPS)]
    ppermute x27, starting transfers between devices: 97.8 us -> 91 us  [swap(): lax.ppermute(array, ('dp', 'mp'), [(i, i ^ mask) for i in range(DP * MP)])]
    all_to_all x1, waiting for transfers between devices: 5.72 us -> 0.01 us  [per_device(): lax.all_to_all(terms_b.reshape(Y, block, total), 'mp', split_axis=0, conc...]
    all_to_all x1, starting transfers between devices: 3.51 us -> 7.83 us  [per_device(): lax.all_to_all(pieces, 'dp', split_axis=0, concat_axis=0, axis_index_grou...]
    ppermute x27, waiting for transfers between devices: 42.9 us -> 38.9 us  [swap(): lax.ppermute(array, ('dp', 'mp'), [(i, i ^ mask) for i in range(DP * MP)])]
  transfers between devices with their start and end apart: 31 -> 32, of which waited for: 18 -> 18; matrix products, arithmetic and copies ran while one was open for 5% -> 5% of each run, Pallas kernels for 1% -> 1%
where the time goes in v21:
time: 260 us; the launch traced here: 258 us
  starting transfers between devices  116 us (45%)
  waiting for transfers between devices  79.1 us (30%)
  blocking collectives  21.5 us (8%)
  between operations  14.1 us (5%)
  local copies, waits for them, and re-layouts  8.25 us (3%)
  Pallas kernels  8.18 us (3%)
  other arithmetic  6.55 us (3%)
  matrix products  4.61 us (2%)
    ppermute x27, starting transfers between devices, swap(): lax.ppermute(array, ('dp', 'mp'), [(i, i ^ mask) for i in range(DP * MP)])  91 us
    ppermute x27, waiting for transfers between devices, swap(): lax.ppermute(array, ('dp', 'mp'), [(i, i ^ mask) for i in range(DP * MP)])  38.9 us
    all_to_all x1, blocking collectives, per_device(): lax.all_to_all(jnp.broadcast_to(jnp.stack(blocks)[:, None], (X, DP // X /...  21.5 us
    all_to_all x1, waiting for transfers between devices, per_device(): lax.all_to_all(projected.reshape(DP, block, (views + 1) * images), 'dp',...  13.3 us
    all_to_all x1, waiting for transfers between devices, per_device(): lax.all_to_all(copies, 'mp', split_axis=0, concat_axis=0, axis_index_grou...  13.3 us
    all_gather x1, waiting for transfers between devices, per_device(): columns = lax.all_gather(slices, 'mp', axis=0, axis_index_groups=GROUPS)  12.9 us
    all_to_all x1, starting transfers between devices, per_device(): lax.all_to_all(pieces, 'dp', split_axis=0, concat_axis=0, axis_index_grou...  7.83 us
    all_to_all x1, starting transfers between devices, per_device(): lax.all_to_all(copies, 'mp', split_axis=0, concat_axis=0, axis_index_grou...  6.84 us
  transfers between devices with their start and end apart: 32, of which 18 were waited for; matrix products, arithmetic and copies ran while one was open for 5% of the time, Pallas kernels for 1%

profile of v21, /device:TPU:1, one launch (start us, length us, event | category | flops | bytes accessed | tf_op | source)
XLA Modules:
  0.0 258.2 jit_solution(656245909443898145)
XLA Ops:
  6.5 8.4 %collective-permute-start = (bf16[256,256]{1,0:T(8,128)(2,1)}, bf16[256,256]{1,0:T(8,128)(2,1)S(1)}, u32[]{:S(2)}, u32[]{:S(2)}) collective-permute-start(bf16[256,256]{1,0:T(8,128)(2,1)} %param.8), channel_id=1, source_target_pairs={{0,96},{1,97},{2,98},{3,99},{4,100},{5,101},{6,102},{7,103},{8,104... | collective-permute-start | bytes 393224 | tf_op jit(solution)/shard_map/ppermute | solution.py:30
  21.7 7.8 %all-to-all-start = ((bf16[8,32,1024]{2,1,0:T(8,128)(2,1)}), bf16[8,32,1024]{2,1,0:T(8,128)(2,1)S(1)}, u32[]{:S(2)}, u32[]{:S(2)}) async-start(bf16[8,32,1024]{2,1,0:T(8,128)(2,1)} %reshape.124), calls=%async_computation | async-start | bytes 1048576 | tf_op jit(solution)/shard_map/all_to_all | solution.py:166
  29.7 3.1 %collective-permute-start.6 = (bf16[4,256,256]{2,1,0:T(8,128)(2,1)S(1)}, bf16[4,256,256]{2,1,0:T(8,128)(2,1)S(1)}, u32[]{:S(2)}, u32[]{:S(2)}) collective-permute-start(bf16[4,256,256]{2,1,0:T(8,128)(2,1)S(1)} %get-tuple-element.68), channel_id=1, source_target_pairs={{0,256},{1,257},{2,258},{3,259},{4,260},{5,261},{6,262},{7,263},{8... | collective-permute-start | bytes 1572872 | tf_op jit(solution)/shard_map/ppermute | solution.py:30
  35.0 3.6 %collective-permute-start.4 = (bf16[4,256,256]{2,1,0:T(8,128)(2,1)S(1)}, bf16[4,256,256]{2,1,0:T(8,128)(2,1)}, u32[]{:S(2)}, u32[]{:S(2)}) collective-permute-start(bf16[4,256,256]{2,1,0:T(8,128)(2,1)S(1)} %get-tuple-element.68), channel_id=1, source_target_pairs={{0,384},{1,385},{2,386},{3,387},{4,388},{5,389},{6,390},{7,391},{8... | collective-permute-start | bytes 1572872 | tf_op jit(solution)/shard_map/ppermute | solution.py:30
  38.7 7.8 %collective-permute-done.6 = bf16[4,256,256]{2,1,0:T(8,128)(2,1)S(1)} collective-permute-done((bf16[4,256,256]{2,1,0:T(8,128)(2,1)S(1)}, bf16[4,256,256]{2,1,0:T(8,128)(2,1)S(1)}, u32[]{:S(2)}, u32[]{:S(2)}) %collective-permute-start.6) | collective-permute-done | bytes 524320 | tf_op jit(solution)/shard_map/ppermute | solution.py:30
  46.6 3.4 %collective-permute-start.7 = (bf16[2,4,256,256]{3,2,1,0:T(8,128)(2,1)S(1)}, bf16[2,4,256,256]{3,2,1,0:T(8,128)(2,1)S(1)}, u32[]{:S(2)}, u32[]{:S(2)}) collective-permute-start(bf16[2,4,256,256]{3,2,1,0:T(8,128)(2,1)S(1)} %pad_maximum_fusion.1), channel_id=1, source_target_pairs={{0,16},{1,17},{2,18},{3,19},{4,20},{5,21},{6,22},{7,23},{8,24},{9,... | collective-permute-start | bytes 3145736 | tf_op jit(solution)/shard_map/ppermute | solution.py:30
  50.0 6.5 %collective-permute-done.3 = bf16[4,256,256]{2,1,0:T(8,128)(2,1)} collective-permute-done((bf16[4,256,256]{2,1,0:T(8,128)(2,1)S(1)}, bf16[4,256,256]{2,1,0:T(8,128)(2,1)}, u32[]{:S(2)}, u32[]{:S(2)}) %collective-permute-start.3) | collective-permute-done | bytes 524320 | tf_op jit(solution)/shard_map/ppermute | solution.py:30
  68.3 6.0 %all-to-all-start.1 = ((f32[32,8,384]{2,1,0:T(8,128)}), f32[32,8,384]{2,1,0:T(8,128)S(1)}, u32[]{:S(2)}, u32[]{:S(2)}) async-start(f32[32,8,384]{2,1,0:T(8,128)} %bitcast.14), calls=%async_computation.1 | async-start | bytes 786432 | tf_op jit(solution)/shard_map/all_to_all | solution.py:183
  75.0 13.3 %all-to-all-done.1 = f32[32,8,384]{2,1,0:T(8,128)S(1)} async-done(((f32[32,8,384]{2,1,0:T(8,128)}), f32[32,8,384]{2,1,0:T(8,128)S(1)}, u32[]{:S(2)}, u32[]{:S(2)}) %all-to-all-start.1) | async-done | bytes 393248 | tf_op jit(solution)/shard_map/all_to_all | solution.py:183
  90.7 6.8 %all-to-all-start.2 = ((bf16[8,2,8,4096]{3,2,1,0:T(8,128)(2,1)}), bf16[8,2,8,4096]{3,2,1,0:T(8,128)(2,1)S(1)}, u32[]{:S(2)}, u32[]{:S(2)}) async-start(bf16[8,2,8,4096]{3,2,1,0:T(8,128)(2,1)} %broadcast_in_dim.4), calls=%async_computation.2 | async-start | bytes 2097152 | tf_op jit(solution)/shard_map/all_to_all | solution.py:195
  97.5 8.1 %collective-permute-start.8 = (bf16[8,4096]{1,0:T(8,128)(2,1)S(1)}, bf16[8,4096]{1,0:T(8,128)(2,1)S(1)}, u32[]{:S(2)}, u32[]{:S(2)}) collective-permute-start(bf16[8,4096]{1,0:T(8,128)(2,1)S(1)} %slice_bitcast_fusion.13), channel_id=1, source_target_pairs={{0,8},{1,9},{2,10},{3,11},{4,12},{5,13},{6,14},{7,15},{8,0},{9,1},... | collective-permute-start | bytes 196616 | tf_op jit(solution)/shard_map/ppermute | solution.py:30
  111.9 3.0 %collective-permute-done.10 = bf16[8,4096]{1,0:T(8,128)(2,1)S(1)} collective-permute-done((bf16[8,4096]{1,0:T(8,128)(2,1)S(1)}, bf16[8,4096]{1,0:T(8,128)(2,1)S(1)}, u32[]{:S(2)}, u32[]{:S(2)}) %collective-permute-start.10) | collective-permute-done | bytes 65568 | tf_op jit(solution)/shard_map/ppermute | solution.py:30
  115.0 3.0 %collective-permute-start.11 = (bf16[4,8,4096]{2,1,0:T(8,128)(2,1)S(1)}, bf16[4,8,4096]{2,1,0:T(8,128)(2,1)S(1)}, u32[]{:S(2)}, u32[]{:S(2)}) collective-permute-start(bf16[4,8,4096]{2,1,0:T(8,128)(2,1)S(1)} %get-tuple-element.76), channel_id=1, source_target_pairs={{0,256},{1,257},{2,258},{3,259},{4,260},{5,261},{6,262},{7,263},{8... | collective-permute-start | bytes 786440 | tf_op jit(solution)/shard_map/ppermute | solution.py:30
  120.3 3.7 %collective-permute-start.13 = (bf16[4,8,4096]{2,1,0:T(8,128)(2,1)S(1)}, bf16[4,8,4096]{2,1,0:T(8,128)(2,1)}, u32[]{:S(2)}, u32[]{:S(2)}) collective-permute-start(bf16[4,8,4096]{2,1,0:T(8,128)(2,1)S(1)} %get-tuple-element.76), channel_id=1, source_target_pairs={{0,384},{1,385},{2,386},{3,387},{4,388},{5,389},{6,390},{7,391},{8... | collective-permute-start | bytes 786440 | tf_op jit(solution)/shard_map/ppermute | solution.py:30
  124.5 13.3 %all-to-all-done.2 = bf16[8,2,8,4096]{3,2,1,0:T(8,128)(2,1)S(1)} async-done(((bf16[8,2,8,4096]{3,2,1,0:T(8,128)(2,1)}), bf16[8,2,8,4096]{3,2,1,0:T(8,128)(2,1)S(1)}, u32[]{:S(2)}, u32[]{:S(2)}) %all-to-all-start.2) | async-done | bytes 1048608 | tf_op jit(solution)/shard_map/all_to_all | solution.py:195
  145.9 12.9 %all-gather.3.cloned.1.call-done = bf16[64,32,1024]{2,1,0:T(8,128)(2,1)} async-done(((bf16[8,32,1024]{2,1,0:T(8,128)(2,1)}), bf16[64,32,1024]{2,1,0:T(8,128)(2,1)}) %all-gather.3.cloned.1.call-update) | async-done | bytes 4194320 | tf_op jit(solution)/shard_map/all_gather | solution.py:198
  161.8 3.3 %collective-permute-start.22 = (bf16[64,4096]{1,0:T(8,128)(2,1)S(1)}, bf16[64,4096]{1,0:T(8,128)(2,1)S(1)}, u32[]{:S(2)}, u32[]{:S(2)}) collective-permute-start(bf16[64,4096]{1,0:T(8,128)(2,1)S(1)} %copy-done.4), channel_id=1, source_target_pairs={{0,32},{1,33},{2,34},{3,35},{4,36},{5,37},{6,38},{7,39},{8,40},{9,... | collective-permute-start | bytes 1572872 | tf_op jit(solution)/shard_map/ppermute | solution.py:30
  166.6 4.6 %collective-permute-start.16 = (bf16[4,8,4096]{2,1,0:T(8,128)(2,1)}, bf16[4,8,4096]{2,1,0:T(8,128)(2,1)}, u32[]{:S(2)}, u32[]{:S(2)}) collective-permute-start(bf16[4,8,4096]{2,1,0:T(8,128)(2,1)} %get-tuple-element.65), channel_id=1, source_target_pairs={{0,256},{1,257},{2,258},{3,259},{4,260},{5,261},{6,262},{7,263},{8... | collective-permute-start | bytes 786440 | tf_op jit(solution)/shard_map/ppermute | solution.py:30
  178.5 4.2 %all-to-all-start.3 = ((bf16[8,8,4096]{2,1,0:T(8,128)(2,1)}), bf16[8,8,4096]{2,1,0:T(8,128)(2,1)S(1)}, u32[]{:S(2)}, u32[]{:S(2)}) async-start(bf16[8,8,4096]{2,1,0:T(8,128)(2,1)} %fusion.6), calls=%async_computation.3 | async-start | bytes 1048576 | tf_op jit(solution)/shard_map/all_to_all | solution.py:235
  185.0 6.8 %collective-permute-start.19 = (bf16[8,4096]{1,0:T(8,128)(2,1)S(1)}, bf16[8,4096]{1,0:T(8,128)(2,1)S(1)}, u32[]{:S(2)}, u32[]{:S(2)}) collective-permute-start(bf16[8,4096]{1,0:T(8,128)(2,1)S(1)} %get-tuple-element.73), channel_id=1, source_target_pairs={{0,8},{1,9},{2,10},{3,11},{4,12},{5,13},{6,14},{7,15},{8,0},{9,1},... | collective-permute-start | bytes 196616 | tf_op jit(solution)/shard_map/ppermute | solution.py:30
  202.3 21.5 %all_to_all.25 = bf16[16,8,2048]{2,1,0:T(8,128)(2,1)S(1)} all-to-all(bf16[16,8,2048]{2,1,0:T(8,128)(2,1)S(1)} %bitcast.209), channel_id=1, replica_groups={{0,32,64,96,128,160,192,224,256,288,320,352,384,416,448,480},{16,48,80,..., dimensions={0} | all-to-all | bytes 1048576 | tf_op jit(solution)/shard_map/all_to_all | solution.py:256
  223.9 4.0 %collective-permute-start.23 = (bf16[16,8,2048]{2,1,0:T(8,128)(2,1)S(1)}, bf16[16,8,2048]{2,1,0:T(8,128)(2,1)S(1)}, u32[]{:S(2)}, u32[]{:S(2)}) collective-permute-start(bf16[16,8,2048]{2,1,0:T(8,128)(2,1)S(1)} %all_to_all.25), channel_id=1, source_target_pairs={{0,16},{1,17},{2,18},{3,19},{4,20},{5,21},{6,22},{7,23},{8,24},{9,... | collective-permute-start | bytes 1572872 | tf_op jit(solution)/shard_map/ppermute | solution.py:30
  237.8 4.0 %collective-permute-start.26 = (f32[256,256]{1,0:T(8,128)S(1)}, f32[256,256]{1,0:T(8,128)S(1)}, u32[]{:S(2)}, u32[]{:S(2)}) collective-permute-start(f32[256,256]{1,0:T(8,128)S(1)} %get-tuple-element.62), channel_id=1, source_target_pairs={{0,384},{1,385},{2,386},{3,387},{4,388},{5,389},{6,390},{7,391},{8... | collective-permute-start | bytes 786440 | tf_op jit(solution)/shard_map/ppermute | solution.py:30
  244.1 3.8 %collective-permute-done.25.refs_2_ = f32[256,256]{1,0:T(8,128)S(1)} collective-permute-done((f32[256,256]{1,0:T(8,128)S(1)}, f32[256,256]{1,0:T(8,128)S(1)}, u32[]{:S(2)}, u32[]{:S(2)}) %collective-permute-start.25) | collective-permute-done | bytes 262176 | tf_op jit(solution)/shard_map/ppermute | solution.py:30
  (121 shorter events, 80.9 us)
Async XLA Ops:
  6.5 15.2 %collective-permute-start = (bf16[256,256]{1,0:T(8,128)(2,1)}, bf16[256,256]{1,0:T(8,128)(2,1)S(1)}, u32[]{:S(2)}, u32[]{:S(2)}) collective-permute-start(bf16[256,256]{1,0:T(8,128)(2,1)} %param.8), channel_id=1, source_target_pairs={{0,96},{1,97},{2,98},{3,99},{4,100},{5,101},{6,102},{7,103},{8,104... | collective-permute-start | bytes 393224 | tf_op jit(solution)/shard_map/ppermute | solution.py:30
  15.0 14.6 %collective-permute-start.1 = (bf16[256,256]{1,0:T(8,128)(2,1)}, bf16[256,256]{1,0:T(8,128)(2,1)S(1)}, u32[]{:S(2)}, u32[]{:S(2)}) collective-permute-start(bf16[256,256]{1,0:T(8,128)(2,1)} %param.8), channel_id=1, source_target_pairs={{0,64},{1,65},{2,66},{3,67},{4,68},{5,69},{6,70},{7,71},{8,72},{9,... | collective-permute-start | bytes 393224 | tf_op jit(solution)/shard_map/ppermute | solution.py:30
  16.9 12.6 %collective-permute-start.2 = (bf16[256,256]{1,0:T(8,128)(2,1)}, bf16[256,256]{1,0:T(8,128)(2,1)S(1)}, u32[]{:S(2)}, u32[]{:S(2)}) collective-permute-start(bf16[256,256]{1,0:T(8,128)(2,1)} %param.8), channel_id=1, source_target_pairs={{0,32},{1,33},{2,34},{3,35},{4,36},{5,37},{6,38},{7,39},{8,40},{9,... | collective-permute-start | bytes 393224 | tf_op jit(solution)/shard_map/ppermute | solution.py:30
  21.7 24.9 %all-to-all-start = ((bf16[8,32,1024]{2,1,0:T(8,128)(2,1)}), bf16[8,32,1024]{2,1,0:T(8,128)(2,1)S(1)}, u32[]{:S(2)}, u32[]{:S(2)}) async-start(bf16[8,32,1024]{2,1,0:T(8,128)(2,1)} %reshape.124), calls=%async_computation | async-start | bytes 1048576 | tf_op jit(solution)/shard_map/all_to_all | solution.py:166
  29.7 16.8 %collective-permute-start.6 = (bf16[4,256,256]{2,1,0:T(8,128)(2,1)S(1)}, bf16[4,256,256]{2,1,0:T(8,128)(2,1)S(1)}, u32[]{:S(2)}, u32[]{:S(2)}) collective-permute-start(bf16[4,256,256]{2,1,0:T(8,128)(2,1)S(1)} %get-tuple-element.68), channel_id=1, source_target_pairs={{0,256},{1,257},{2,258},{3,259},{4,260},{5,261},{6,262},{7,263},{8... | collective-permute-start | bytes 1572872 | tf_op jit(solution)/shard_map/ppermute | solution.py:30
  32.8 23.8 %collective-permute-start.3 = (bf16[4,256,256]{2,1,0:T(8,128)(2,1)S(1)}, bf16[4,256,256]{2,1,0:T(8,128)(2,1)}, u32[]{:S(2)}, u32[]{:S(2)}) collective-permute-start(bf16[4,256,256]{2,1,0:T(8,128)(2,1)S(1)} %get-tuple-element.68), channel_id=1, source_target_pairs={{0,128},{1,129},{2,130},{3,131},{4,132},{5,133},{6,134},{7,135},{8... | collective-permute-start | bytes 1572872 | tf_op jit(solution)/shard_map/ppermute | solution.py:30
  35.0 23.2 %collective-permute-start.4 = (bf16[4,256,256]{2,1,0:T(8,128)(2,1)S(1)}, bf16[4,256,256]{2,1,0:T(8,128)(2,1)}, u32[]{:S(2)}, u32[]{:S(2)}) collective-permute-start(bf16[4,256,256]{2,1,0:T(8,128)(2,1)S(1)} %get-tuple-element.68), channel_id=1, source_target_pairs={{0,384},{1,385},{2,386},{3,387},{4,388},{5,389},{6,390},{7,391},{8... | collective-permute-start | bytes 1572872 | tf_op jit(solution)/shard_map/ppermute | solution.py:30
  46.6 15.4 %collective-permute-start.7 = (bf16[2,4,256,256]{3,2,1,0:T(8,128)(2,1)S(1)}, bf16[2,4,256,256]{3,2,1,0:T(8,128)(2,1)S(1)}, u32[]{:S(2)}, u32[]{:S(2)}) collective-permute-start(bf16[2,4,256,256]{3,2,1,0:T(8,128)(2,1)S(1)} %pad_maximum_fusion.1), channel_id=1, source_target_pairs={{0,16},{1,17},{2,18},{3,19},{4,20},{5,21},{6,22},{7,23},{8,24},{9,... | collective-permute-start | bytes 3145736 | tf_op jit(solution)/shard_map/ppermute | solution.py:30
  68.3 20.0 %all-to-all-start.1 = ((f32[32,8,384]{2,1,0:T(8,128)}), f32[32,8,384]{2,1,0:T(8,128)S(1)}, u32[]{:S(2)}, u32[]{:S(2)}) async-start(f32[32,8,384]{2,1,0:T(8,128)} %bitcast.14), calls=%async_computation.1 | async-start | bytes 786432 | tf_op jit(solution)/shard_map/all_to_all | solution.py:183
  74.3 84.5 %all-gather.3.cloned.1.call-start = ((), (), s32[]{:S(2)}) async-start(), calls=%async_computation.5 | async-start | bytes 4718592 | tf_op jit(solution)/shard_map/all_gather | solution.py:198
  90.7 47.1 %all-to-all-start.2 = ((bf16[8,2,8,4096]{3,2,1,0:T(8,128)(2,1)}), bf16[8,2,8,4096]{3,2,1,0:T(8,128)(2,1)S(1)}, u32[]{:S(2)}, u32[]{:S(2)}) async-start(bf16[8,2,8,4096]{3,2,1,0:T(8,128)(2,1)} %broadcast_in_dim.4), calls=%async_computation.2 | async-start | bytes 2097152 | tf_op jit(solution)/shard_map/all_to_all | solution.py:195
  97.5 12.2 %collective-permute-start.8 = (bf16[8,4096]{1,0:T(8,128)(2,1)S(1)}, bf16[8,4096]{1,0:T(8,128)(2,1)S(1)}, u32[]{:S(2)}, u32[]{:S(2)}) collective-permute-start(bf16[8,4096]{1,0:T(8,128)(2,1)S(1)} %slice_bitcast_fusion.13), channel_id=1, source_target_pairs={{0,8},{1,9},{2,10},{3,11},{4,12},{5,13},{6,14},{7,15},{8,0},{9,1},... | collective-permute-start | bytes 196616 | tf_op jit(solution)/shard_map/ppermute | solution.py:30
  115.0 9.4 %collective-permute-start.11 = (bf16[4,8,4096]{2,1,0:T(8,128)(2,1)S(1)}, bf16[4,8,4096]{2,1,0:T(8,128)(2,1)S(1)}, u32[]{:S(2)}, u32[]{:S(2)}) collective-permute-start(bf16[4,8,4096]{2,1,0:T(8,128)(2,1)S(1)} %get-tuple-element.76), channel_id=1, source_target_pairs={{0,256},{1,257},{2,258},{3,259},{4,260},{5,261},{6,262},{7,263},{8... | collective-permute-start | bytes 786440 | tf_op jit(solution)/shard_map/ppermute | solution.py:30
  118.0 19.7 %collective-permute-start.12 = (bf16[4,8,4096]{2,1,0:T(8,128)(2,1)S(1)}, bf16[4,8,4096]{2,1,0:T(8,128)(2,1)S(1)}, u32[]{:S(2)}, u32[]{:S(2)}) collective-permute-start(bf16[4,8,4096]{2,1,0:T(8,128)(2,1)S(1)} %get-tuple-element.76), channel_id=1, source_target_pairs={{0,128},{1,129},{2,130},{3,131},{4,132},{5,133},{6,134},{7,135},{8... | collective-permute-start | bytes 786440 | tf_op jit(solution)/shard_map/ppermute | solution.py:30
  120.3 17.5 %collective-permute-start.13 = (bf16[4,8,4096]{2,1,0:T(8,128)(2,1)S(1)}, bf16[4,8,4096]{2,1,0:T(8,128)(2,1)}, u32[]{:S(2)}, u32[]{:S(2)}) collective-permute-start(bf16[4,8,4096]{2,1,0:T(8,128)(2,1)S(1)} %get-tuple-element.76), channel_id=1, source_target_pairs={{0,384},{1,385},{2,386},{3,387},{4,388},{5,389},{6,390},{7,391},{8... | collective-permute-start | bytes 786440 | tf_op jit(solution)/shard_map/ppermute | solution.py:30
  161.8 15.5 %collective-permute-start.22 = (bf16[64,4096]{1,0:T(8,128)(2,1)S(1)}, bf16[64,4096]{1,0:T(8,128)(2,1)S(1)}, u32[]{:S(2)}, u32[]{:S(2)}) collective-permute-start(bf16[64,4096]{1,0:T(8,128)(2,1)S(1)} %copy-done.4), channel_id=1, source_target_pairs={{0,32},{1,33},{2,34},{3,35},{4,36},{5,37},{6,38},{7,39},{8,40},{9,... | collective-permute-start | bytes 1572872 | tf_op jit(solution)/shard_map/ppermute | solution.py:30
  166.6 16.1 %collective-permute-start.16 = (bf16[4,8,4096]{2,1,0:T(8,128)(2,1)}, bf16[4,8,4096]{2,1,0:T(8,128)(2,1)}, u32[]{:S(2)}, u32[]{:S(2)}) collective-permute-start(bf16[4,8,4096]{2,1,0:T(8,128)(2,1)} %get-tuple-element.65), channel_id=1, source_target_pairs={{0,256},{1,257},{2,258},{3,259},{4,260},{5,261},{6,262},{7,263},{8... | collective-permute-start | bytes 786440 | tf_op jit(solution)/shard_map/ppermute | solution.py:30
  171.2 12.4 %collective-permute-start.17 = (bf16[4,8,4096]{2,1,0:T(8,128)(2,1)}, bf16[4,8,4096]{2,1,0:T(8,128)(2,1)}, u32[]{:S(2)}, u32[]{:S(2)}) collective-permute-start(bf16[4,8,4096]{2,1,0:T(8,128)(2,1)} %get-tuple-element.64), channel_id=1, source_target_pairs={{0,128},{1,129},{2,130},{3,131},{4,132},{5,133},{6,134},{7,135},{8... | collective-permute-start | bytes 786440 | tf_op jit(solution)/shard_map/ppermute | solution.py:30
  173.4 10.4 %collective-permute-start.18 = (bf16[4,8,4096]{2,1,0:T(8,128)(2,1)}, bf16[4,8,4096]{2,1,0:T(8,128)(2,1)}, u32[]{:S(2)}, u32[]{:S(2)}) collective-permute-start(bf16[4,8,4096]{2,1,0:T(8,128)(2,1)} %get-tuple-element.63), channel_id=1, source_target_pairs={{0,384},{1,385},{2,386},{3,387},{4,388},{5,389},{6,390},{7,391},{8... | collective-permute-start | bytes 786440 | tf_op jit(solution)/shard_map/ppermute | solution.py:30
  178.5 23.2 %all-to-all-start.3 = ((bf16[8,8,4096]{2,1,0:T(8,128)(2,1)}), bf16[8,8,4096]{2,1,0:T(8,128)(2,1)S(1)}, u32[]{:S(2)}, u32[]{:S(2)}) async-start(bf16[8,8,4096]{2,1,0:T(8,128)(2,1)} %fusion.6), calls=%async_computation.3 | async-start | bytes 1048576 | tf_op jit(solution)/shard_map/all_to_all | solution.py:235
  185.0 11.5 %collective-permute-start.19 = (bf16[8,4096]{1,0:T(8,128)(2,1)S(1)}, bf16[8,4096]{1,0:T(8,128)(2,1)S(1)}, u32[]{:S(2)}, u32[]{:S(2)}) collective-permute-start(bf16[8,4096]{1,0:T(8,128)(2,1)S(1)} %get-tuple-element.73), channel_id=1, source_target_pairs={{0,8},{1,9},{2,10},{3,11},{4,12},{5,13},{6,14},{7,15},{8,0},{9,1},... | collective-permute-start | bytes 196616 | tf_op jit(solution)/shard_map/ppermute | solution.py:30
  232.8 11.3 %collective-permute-start.24 = (f32[256,256]{1,0:T(8,128)S(1)}, f32[256,256]{1,0:T(8,128)S(1)}, u32[]{:S(2)}, u32[]{:S(2)}) collective-permute-start(f32[256,256]{1,0:T(8,128)S(1)} %get-tuple-element.60), channel_id=1, source_target_pairs={{0,256},{1,257},{2,258},{3,259},{4,260},{5,261},{6,262},{7,263},{8... | collective-permute-start | bytes 786440 | tf_op jit(solution)/shard_map/ppermute | solution.py:30
  235.3 12.6 %collective-permute-start.25 = (f32[256,256]{1,0:T(8,128)S(1)}, f32[256,256]{1,0:T(8,128)S(1)}, u32[]{:S(2)}, u32[]{:S(2)}) collective-permute-start(f32[256,256]{1,0:T(8,128)S(1)} %get-tuple-element.61), channel_id=1, source_target_pairs={{0,128},{1,129},{2,130},{3,131},{4,132},{5,133},{6,134},{7,135},{8... | collective-permute-start | bytes 786440 | tf_op jit(solution)/shard_map/ppermute | solution.py:30
  237.8 12.1 %collective-permute-start.26 = (f32[256,256]{1,0:T(8,128)S(1)}, f32[256,256]{1,0:T(8,128)S(1)}, u32[]{:S(2)}, u32[]{:S(2)}) collective-permute-start(f32[256,256]{1,0:T(8,128)S(1)} %get-tuple-element.62), channel_id=1, source_target_pairs={{0,384},{1,385},{2,386},{3,387},{4,388},{5,389},{6,390},{7,391},{8... | collective-permute-start | bytes 786440 | tf_op jit(solution)/shard_map/ppermute | solution.py:30
  (19 other events, 179.0 us)
Sparse Core Ops, SparseCore 0:
  77.2 81.5 all-gather.2

commit v22 on v19

--- a/solution.py
+++ b/solution.py
@@ -47,13 +47,15 @@
     return sum(part.astype(jnp.float32) for part in parts), *later
 
 
-def project_kernel(last, order_ref, inputs_ref, own_ref, other_ref, *refs):
-    out_ref = refs[-1]
-    blocks, depth, _ = own_ref.shape
-    result = refs[0][...] if last else None
-    for core, weight_ref in enumerate((own_ref, other_ref)):
+def project_kernel(last, order_ref, inputs_ref, *refs):
+    *weight_refs, out_ref = refs
+    result = weight_refs.pop()[...] if last else None
+    place = 0
+    for weight_ref in weight_refs:
+        blocks, depth, _ = weight_ref.shape
         for k in range(blocks):
-            start = pl.multiple_of(order_ref[core * blocks + k] * depth, depth)
+            start = pl.multiple_of(order_ref[place] * depth, depth)
+            place += 1
             part = jnp.dot(
                 inputs_ref[:, pl.ds(start, depth)], weight_ref[k], preferred_element_type=jnp.float32
             )
@@ -69,21 +71,21 @@
         out_ref[8 * j : 8 * j + 8, rows:] = features[k : k + 8, rows // 2 :]
 
 
-def project(order, inputs, own, other, *before):
-    rows, feat = inputs.shape[0], own.shape[2]
+def project(order, inputs, weights, *before):
+    rows, feat = inputs.shape[0], weights[0].shape[2]
     vmem = pl.BlockSpec(memory_space=pltpu.VMEM)
     return pl.pallas_call(
         functools.partial(project_kernel, bool(before)),
-        in_specs=[pl.BlockSpec(memory_space=pltpu.SMEM)] + [vmem] * (3 + len(before)),
+        in_specs=[pl.BlockSpec(memory_space=pltpu.SMEM)] + [vmem] * (1 + len(weights) + len(before)),
         out_specs=vmem,
         out_shape=jax.ShapeDtypeStruct((feat, rows // 2 * 3) if before else (rows, feat), jnp.float32),
         compiler_params=pltpu.CompilerParams(vmem_limit_bytes=16 * 1024 * 1024),
         cost_estimate=pl.CostEstimate(
-            flops=4 * rows * feat * own.shape[0] * own.shape[1],
+            flops=2 * rows * feat * order.shape[0] * feat,
             bytes_accessed=6 * 1024 * 1024,
             transcendentals=0,
         ),
-    )(order, inputs, own, other, *before)
+    )(order, inputs, *weights, *before)
 
 
 def weight_kernel(targets_ref, grad_ref, columns_ref, *refs):
@@ -164,16 +166,15 @@
     pieces = mine.reshape(share, X, DP // X, rows).transpose(2, 0, 1, 3).reshape(DP // X, share, X * rows)
     along_z = gather(weight, ALONG_Z)[0]
     parts = [along_z] + [swap(along_z, *mask) for mask in ALONG_X]
-    projected = ()
-    for k in (0, 2):
-        weight_own, pieces = lax.optimization_barrier((jnp.stack(parts[k : k + 2]), pieces))
-        weight_other = swap(weight_own, 1)
-        blocks = np.concatenate([4 * k + np.arange(8), 16 + 4 * k + np.arange(8)])
-        half = (DP // 4, rows, feat)
-        order = data_index ^ jnp.asarray(distance[blocks], jnp.int32)
-        halves = weight_own.reshape(half), weight_other.reshape(half)
-        projected = (project(order, flat, *halves, *projected),)
-    projected = projected[0]
+    early, pieces = lax.optimization_barrier((parts[:2], pieces))
+    late = jnp.stack(parts[2:]).reshape(DP // 4, rows, feat)
+
+    def order(first):
+        blocks = np.concatenate([first + np.arange(8), 16 + first + np.arange(8)])
+        return data_index ^ jnp.asarray(distance[blocks], jnp.int32)
+
+    projected = project(order(0), flat, early + [swap(part, 1) for part in early])
+    projected = project(order(8), flat, [late, swap(late, 1)], projected)
 
     own = lax.all_to_all(
         projected.reshape(DP, block, (views + 1) * images), "dp", split_axis=0, concat_axis=0

time: 241 us -> 254 us (1.054)
  waiting for transfers between devices: 48.8 us -> 59.3 us
  local copies, waits for them, and re-layouts: 7.73 us -> 10.8 us
    ppermute x27 -> x28, waiting for transfers between devices: 42.9 us -> 53.3 us  [swap(): lax.ppermute(array, ('dp', 'mp'), [(i, i ^ mask) for i in range(DP * MP)])]
    unnamed x19 -> x23, local copies, waits for them, and re-layouts: 4.51 us -> 5.77 us
    ppermute x27 -> x28, starting transfers between devices: 97.8 us -> 98.5 us  [swap(): lax.ppermute(array, ('dp', 'mp'), [(i, i ^ mask) for i in range(DP * MP)])]
  transfers between devices with their start and end apart: 31 -> 32, of which waited for: 18 -> 18; matrix products, arithmetic and copies ran while one was open for 5% -> 5% of each run, Pallas kernels for 1% -> 1%
where the time goes in v22:
time: 254 us; the launch traced here: 252 us
  starting transfers between devices  109 us (43%)
  waiting for transfers between devices  59.3 us (23%)
  blocking collectives  39.3 us (15%)
  between operations  14.1 us (6%)
  local copies, waits for them, and re-layouts  10.8 us (4%)
  Pallas kernels  7.51 us (3%)
  matrix products  6.93 us (3%)
  other arithmetic  5.57 us (2%)
    ppermute x28, starting transfers between devices, swap(): lax.ppermute(array, ('dp', 'mp'), [(i, i ^ mask) for i in range(DP * MP)])  98.5 us
    ppermute x28, waiting for transfers between devices, swap(): lax.ppermute(array, ('dp', 'mp'), [(i, i ^ mask) for i in range(DP * MP)])  53.3 us
    all_to_all x1, blocking collectives, per_device(): lax.all_to_all(jnp.stack([part for part in blocks for _ in range(DP // X...  19.8 us
    all_to_all x1, blocking collectives, per_device(): lax.all_to_all(projected.reshape(DP, block, (views + 1) * images), 'dp',...  19.4 us
    all_to_all x1, starting transfers between devices, per_device(): lax.all_to_all(terms_b.reshape(Y, block, total), 'mp', split_axis=0, conc...  6.93 us
    unnamed x23, local copies, waits for them, and re-layouts  5.77 us
    all_to_all x1, waiting for transfers between devices, per_device(): lax.all_to_all(terms_b.reshape(Y, block, total), 'mp', split_axis=0, conc...  5.71 us
  transfers between devices with their start and end apart: 32, of which 18 were waited for; matrix products, arithmetic and copies ran while one was open for 5% of the time, Pallas kernels for 1%

profile of v22, /device:TPU:1, one launch (start us, length us, event | category | flops | bytes accessed | tf_op | source)
XLA Modules:
  0.0 252.5 jit_solution(5171438311183578755)
XLA Ops:
  6.5 8.4 %collective-permute-start = (bf16[256,256]{1,0:T(8,128)(2,1)}, bf16[256,256]{1,0:T(8,128)(2,1)S(1)}, u32[]{:S(2)}, u32[]{:S(2)}) collective-permute-start(bf16[256,256]{1,0:T(8,128)(2,1)} %param.8), channel_id=1, source_target_pairs={{0,96},{1,97},{2,98},{3,99},{4,100},{5,101},{6,102},{7,103},{8,104... | collective-permute-start | bytes 393224 | tf_op jit(solution)/shard_map/ppermute | solution.py:30
  19.1 6.7 %collective-permute-done.1 = bf16[256,256]{1,0:T(8,128)(2,1)S(1)} collective-permute-done((bf16[256,256]{1,0:T(8,128)(2,1)}, bf16[256,256]{1,0:T(8,128)(2,1)S(1)}, u32[]{:S(2)}, u32[]{:S(2)}) %collective-permute-start.1) | collective-permute-done | bytes 131104 | tf_op jit(solution)/shard_map/ppermute | solution.py:30
  26.8 3.6 %collective-permute-start.3 = (bf16[4,256,256]{2,1,0:T(8,128)(2,1)S(1)}, bf16[4,256,256]{2,1,0:T(8,128)(2,1)S(1)}, u32[]{:S(2)}, u32[]{:S(2)}) collective-permute-start(bf16[4,256,256]{2,1,0:T(8,128)(2,1)S(1)} %pad_maximum_fusion.2.refs_0_), channel_id=1, source_target_pairs={{0,128},{1,129},{2,130},{3,131},{4,132},{5,133},{6,134},{7,135},{8... | collective-permute-start | bytes 1572872 | tf_op jit(solution)/shard_map/ppermute | solution.py:30
  30.4 3.7 %collective-permute-start.4 = (bf16[4,256,256]{2,1,0:T(8,128)(2,1)S(1)}, bf16[4,256,256]{2,1,0:T(8,128)(2,1)S(1)}, u32[]{:S(2)}, u32[]{:S(2)}) collective-permute-start(bf16[4,256,256]{2,1,0:T(8,128)(2,1)S(1)} %pad_maximum_fusion.2.refs_0_), channel_id=1, source_target_pairs={{0,384},{1,385},{2,386},{3,387},{4,388},{5,389},{6,390},{7,391},{8... | collective-permute-start | bytes 1572872 | tf_op jit(solution)/shard_map/ppermute | solution.py:30
  36.7 3.8 %collective-permute-done.3 = bf16[4,256,256]{2,1,0:T(8,128)(2,1)S(1)} collective-permute-done((bf16[4,256,256]{2,1,0:T(8,128)(2,1)S(1)}, bf16[4,256,256]{2,1,0:T(8,128)(2,1)S(1)}, u32[]{:S(2)}, u32[]{:S(2)}) %collective-permute-start.3) | collective-permute-done | bytes 524320 | tf_op jit(solution)/shard_map/ppermute | solution.py:30
  40.6 14.3 %collective-permute-done.4 = bf16[4,256,256]{2,1,0:T(8,128)(2,1)S(1)} collective-permute-done((bf16[4,256,256]{2,1,0:T(8,128)(2,1)S(1)}, bf16[4,256,256]{2,1,0:T(8,128)(2,1)S(1)}, u32[]{:S(2)}, u32[]{:S(2)}) %collective-permute-start.4) | collective-permute-done | bytes 524320 | tf_op jit(solution)/shard_map/ppermute | solution.py:30
  55.0 6.1 %collective-permute-start.5 = (bf16[8,256,256]{2,1,0:T(8,128)(2,1)S(1)}, bf16[8,256,256]{2,1,0:T(8,128)(2,1)S(1)}, u32[]{:S(2)}, u32[]{:S(2)}) collective-permute-start(bf16[8,256,256]{2,1,0:T(8,128)(2,1)S(1)} %bitcast.208), channel_id=1, source_target_pairs={{0,16},{1,17},{2,18},{3,19},{4,20},{5,21},{6,22},{7,23},{8,24},{9,... | collective-permute-start | bytes 3145736 | tf_op jit(solution)/shard_map/ppermute | solution.py:30
  77.6 19.4 %all_to_all.20 = f32[32,8,384]{2,1,0:T(8,128)S(1)} all-to-all(f32[32,8,384]{2,1,0:T(8,128)S(1)} %bitcast.211), channel_id=1, replica_groups=mesh['dp'=32,'mp'=16] {'dp'}, dimensions={0} | all-to-all | bytes 786432 | tf_op jit(solution)/shard_map/all_to_all | solution.py:179
  98.2 3.5 %all-to-all-start.1 = ((bf16[8,32,1024]{2,1,0:T(8,128)(2,1)}), bf16[8,32,1024]{2,1,0:T(8,128)(2,1)S(1)}, u32[]{:S(2)}, u32[]{:S(2)}) async-start(bf16[8,32,1024]{2,1,0:T(8,128)(2,1)} %reshape.111), calls=%async_computation.1 | async-start | bytes 1048576 | tf_op jit(solution)/shard_map/all_to_all | solution.py:190
  101.7 7.9 %collective-permute-start.9 = (bf16[8,4096]{1,0:T(8,128)(2,1)S(1)}, bf16[8,4096]{1,0:T(8,128)(2,1)S(1)}, u32[]{:S(2)}, u32[]{:S(2)}) collective-permute-start(bf16[8,4096]{1,0:T(8,128)(2,1)S(1)} %slice_bitcast_fusion.13), channel_id=1, source_target_pairs={{0,8},{1,9},{2,10},{3,11},{4,12},{5,13},{6,14},{7,15},{8,0},{9,1},... | collective-permute-start | bytes 196616 | tf_op jit(solution)/shard_map/ppermute | solution.py:30
  109.7 4.2 %collective-permute-start.10 = (bf16[8,4096]{1,0:T(8,128)(2,1)S(1)}, bf16[8,4096]{1,0:T(8,128)(2,1)S(1)}, u32[]{:S(2)}, u32[]{:S(2)}) collective-permute-start(bf16[8,4096]{1,0:T(8,128)(2,1)S(1)} %slice_bitcast_fusion.13), channel_id=1, source_target_pairs={{0,64},{1,65},{2,66},{3,67},{4,68},{5,69},{6,70},{7,71},{8,72},{9,... | collective-permute-start | bytes 196616 | tf_op jit(solution)/shard_map/ppermute | solution.py:30
  115.8 4.3 %collective-permute-done.9 = bf16[8,4096]{1,0:T(8,128)(2,1)S(1)} collective-permute-done((bf16[8,4096]{1,0:T(8,128)(2,1)S(1)}, bf16[8,4096]{1,0:T(8,128)(2,1)S(1)}, u32[]{:S(2)}, u32[]{:S(2)}) %collective-permute-start.9) | collective-permute-done | bytes 65568 | tf_op jit(solution)/shard_map/ppermute | solution.py:30
  127.0 4.0 %collective-permute-start.14 = (bf16[4,8,4096]{2,1,0:T(8,128)(2,1)S(1)}, bf16[4,8,4096]{2,1,0:T(8,128)(2,1)S(1)}, u32[]{:S(2)}, u32[]{:S(2)}) collective-permute-start(bf16[4,8,4096]{2,1,0:T(8,128)(2,1)S(1)} %get-tuple-element.80), channel_id=1, source_target_pairs={{0,384},{1,385},{2,386},{3,387},{4,388},{5,389},{6,390},{7,391},{8... | collective-permute-start | bytes 786440 | tf_op jit(solution)/shard_map/ppermute | solution.py:30
  131.4 4.1 %collective-permute-done.13 = bf16[4,8,4096]{2,1,0:T(8,128)(2,1)S(1)} collective-permute-done((bf16[4,8,4096]{2,1,0:T(8,128)(2,1)S(1)}, bf16[4,8,4096]{2,1,0:T(8,128)(2,1)S(1)}, u32[]{:S(2)}, u32[]{:S(2)}) %collective-permute-start.13) | collective-permute-done | bytes 262176 | tf_op jit(solution)/shard_map/ppermute | solution.py:30
  138.9 3.5 %collective-permute-start.15 = (bf16[4,4,8,4096]{3,2,1,0:T(8,128)(2,1)S(1)}, bf16[4,4,8,4096]{3,2,1,0:T(8,128)(2,1)S(1)}, u32[]{:S(2)}, u32[]{:S(2)}) collective-permute-start(bf16[4,4,8,4096]{3,2,1,0:T(8,128)(2,1)S(1)} %pad_maximum_fusion.1), channel_id=1, source_target_pairs={{0,16},{1,17},{2,18},{3,19},{4,20},{5,21},{6,22},{7,23},{8,24},{9,... | collective-permute-start | bytes 3145736 | tf_op jit(solution)/shard_map/ppermute | solution.py:30
  150.0 3.8 %collective-permute-start.23 = (bf16[64,4096]{1,0:T(8,128)(2,1)}, bf16[64,4096]{1,0:T(8,128)(2,1)S(1)}, u32[]{:S(2)}, u32[]{:S(2)}) collective-permute-start(bf16[64,4096]{1,0:T(8,128)(2,1)} %fusion.5), channel_id=1, source_target_pairs={{0,32},{1,33},{2,34},{3,35},{4,36},{5,37},{6,38},{7,39},{8,40},{9,... | collective-permute-start | bytes 1572872 | tf_op jit(solution)/shard_map/ppermute | solution.py:30
  161.9 3.5 %collective-permute-start.19 = (bf16[4,8,4096]{2,1,0:T(8,128)(2,1)S(1)}, bf16[4,8,4096]{2,1,0:T(8,128)(2,1)}, u32[]{:S(2)}, u32[]{:S(2)}) collective-permute-start(bf16[4,8,4096]{2,1,0:T(8,128)(2,1)S(1)} %get-tuple-element.69), channel_id=1, source_target_pairs={{0,384},{1,385},{2,386},{3,387},{4,388},{5,389},{6,390},{7,391},{8... | collective-permute-start | bytes 786440 | tf_op jit(solution)/shard_map/ppermute | solution.py:30
  167.3 6.9 %all-to-all-start.2 = ((bf16[8,8,4096]{2,1,0:T(8,128)(2,1)}), bf16[8,8,4096]{2,1,0:T(8,128)(2,1)S(1)}, u32[]{:S(2)}, u32[]{:S(2)}) async-start(bf16[8,8,4096]{2,1,0:T(8,128)(2,1)} %fusion.6), calls=%async_computation.2 | async-start | bytes 1048576 | tf_op jit(solution)/shard_map/all_to_all | solution.py:232
  175.5 6.7 %collective-permute-start.20 = (bf16[8,4096]{1,0:T(8,128)(2,1)S(1)}, bf16[8,4096]{1,0:T(8,128)(2,1)S(1)}, u32[]{:S(2)}, u32[]{:S(2)}) collective-permute-start(bf16[8,4096]{1,0:T(8,128)(2,1)S(1)} %get-tuple-element.77), channel_id=1, source_target_pairs={{0,8},{1,9},{2,10},{3,11},{4,12},{5,13},{6,14},{7,15},{8,0},{9,1},... | collective-permute-start | bytes 196616 | tf_op jit(solution)/shard_map/ppermute | solution.py:30
  191.6 5.7 %all-to-all-done.2 = bf16[8,8,4096]{2,1,0:T(8,128)(2,1)S(1)} async-done(((bf16[8,8,4096]{2,1,0:T(8,128)(2,1)}), bf16[8,8,4096]{2,1,0:T(8,128)(2,1)S(1)}, u32[]{:S(2)}, u32[]{:S(2)}) %all-to-all-start.2) | async-done | bytes 524320 | tf_op jit(solution)/shard_map/all_to_all | solution.py:232
  198.0 19.8 %all_to_all.21 = bf16[16,8,2048]{2,1,0:T(8,128)(2,1)S(1)} all-to-all(bf16[16,8,2048]{2,1,0:T(8,128)(2,1)S(1)} %constant_dynamic-update-slice_fusion), channel_id=1, replica_groups={{0,32,64,96,128,160,192,224,256,288,320,352,384,416,448,480},{16,48,80,..., dimensions={0} | all-to-all | bytes 1048576 | tf_op jit(solution)/shard_map/all_to_all | solution.py:253
  218.0 3.7 %collective-permute-start.24 = (bf16[16,8,2048]{2,1,0:T(8,128)(2,1)S(1)}, bf16[16,8,2048]{2,1,0:T(8,128)(2,1)S(1)}, u32[]{:S(2)}, u32[]{:S(2)}) collective-permute-start(bf16[16,8,2048]{2,1,0:T(8,128)(2,1)S(1)} %all_to_all.21), channel_id=1, source_target_pairs={{0,16},{1,17},{2,18},{3,19},{4,20},{5,21},{6,22},{7,23},{8,24},{9,... | collective-permute-start | bytes 1572872 | tf_op jit(solution)/shard_map/ppermute | solution.py:30
  227.5 3.5 %collective-permute-start.25 = (f32[256,256]{1,0:T(8,128)S(1)}, f32[256,256]{1,0:T(8,128)S(1)}, u32[]{:S(2)}, u32[]{:S(2)}) collective-permute-start(f32[256,256]{1,0:T(8,128)S(1)} %get-tuple-element.66), channel_id=1, source_target_pairs={{0,256},{1,257},{2,258},{3,259},{4,260},{5,261},{6,262},{7,263},{8... | collective-permute-start | bytes 786440 | tf_op jit(solution)/shard_map/ppermute | solution.py:30
  238.8 4.5 %collective-permute-done.26.refs_2_ = f32[256,256]{1,0:T(8,128)S(1)} collective-permute-done((f32[256,256]{1,0:T(8,128)S(1)}, f32[256,256]{1,0:T(8,128)S(1)}, u32[]{:S(2)}, u32[]{:S(2)}) %collective-permute-start.26) | collective-permute-done | bytes 262176 | tf_op jit(solution)/shard_map/ppermute | solution.py:30
  (130 shorter events, 82.3 us)
Async XLA Ops:
  6.5 132.3 %all-gather.5.cloned.1.call-start = ((), (), s32[]{:S(2)}) async-start(), calls=%async_computation.4 | async-start | bytes 1179648 | tf_op jit(solution)/shard_map/all_gather | solution.py:193
  6.5 12.6 %collective-permute-start = (bf16[256,256]{1,0:T(8,128)(2,1)}, bf16[256,256]{1,0:T(8,128)(2,1)S(1)}, u32[]{:S(2)}, u32[]{:S(2)}) collective-permute-start(bf16[256,256]{1,0:T(8,128)(2,1)} %param.8), channel_id=1, source_target_pairs={{0,96},{1,97},{2,98},{3,99},{4,100},{5,101},{6,102},{7,103},{8,104... | collective-permute-start | bytes 393224 | tf_op jit(solution)/shard_map/ppermute | solution.py:30
  15.0 10.9 %collective-permute-start.1 = (bf16[256,256]{1,0:T(8,128)(2,1)}, bf16[256,256]{1,0:T(8,128)(2,1)S(1)}, u32[]{:S(2)}, u32[]{:S(2)}) collective-permute-start(bf16[256,256]{1,0:T(8,128)(2,1)} %param.8), channel_id=1, source_target_pairs={{0,64},{1,65},{2,66},{3,67},{4,68},{5,69},{6,70},{7,71},{8,72},{9,... | collective-permute-start | bytes 393224 | tf_op jit(solution)/shard_map/ppermute | solution.py:30
  16.9 9.0 %collective-permute-start.2 = (bf16[256,256]{1,0:T(8,128)(2,1)}, bf16[256,256]{1,0:T(8,128)(2,1)S(1)}, u32[]{:S(2)}, u32[]{:S(2)}) collective-permute-start(bf16[256,256]{1,0:T(8,128)(2,1)} %param.8), channel_id=1, source_target_pairs={{0,32},{1,33},{2,34},{3,35},{4,36},{5,37},{6,38},{7,39},{8,40},{9,... | collective-permute-start | bytes 393224 | tf_op jit(solution)/shard_map/ppermute | solution.py:30
  26.8 13.7 %collective-permute-start.3 = (bf16[4,256,256]{2,1,0:T(8,128)(2,1)S(1)}, bf16[4,256,256]{2,1,0:T(8,128)(2,1)S(1)}, u32[]{:S(2)}, u32[]{:S(2)}) collective-permute-start(bf16[4,256,256]{2,1,0:T(8,128)(2,1)S(1)} %pad_maximum_fusion.2.refs_0_), channel_id=1, source_target_pairs={{0,128},{1,129},{2,130},{3,131},{4,132},{5,133},{6,134},{7,135},{8... | collective-permute-start | bytes 1572872 | tf_op jit(solution)/shard_map/ppermute | solution.py:30
  30.4 24.5 %collective-permute-start.4 = (bf16[4,256,256]{2,1,0:T(8,128)(2,1)S(1)}, bf16[4,256,256]{2,1,0:T(8,128)(2,1)S(1)}, u32[]{:S(2)}, u32[]{:S(2)}) collective-permute-start(bf16[4,256,256]{2,1,0:T(8,128)(2,1)S(1)} %pad_maximum_fusion.2.refs_0_), channel_id=1, source_target_pairs={{0,384},{1,385},{2,386},{3,387},{4,388},{5,389},{6,390},{7,391},{8... | collective-permute-start | bytes 1572872 | tf_op jit(solution)/shard_map/ppermute | solution.py:30
  34.2 31.4 %collective-permute-start.6 = (bf16[4,256,256]{2,1,0:T(8,128)(2,1)S(1)}, bf16[4,256,256]{2,1,0:T(8,128)(2,1)S(1)}, u32[]{:S(2)}, u32[]{:S(2)}) collective-permute-start(bf16[4,256,256]{2,1,0:T(8,128)(2,1)S(1)} %pad_maximum_fusion.2.refs_0_), channel_id=1, source_target_pairs={{0,256},{1,257},{2,258},{3,259},{4,260},{5,261},{6,262},{7,263},{8... | collective-permute-start | bytes 1572872 | tf_op jit(solution)/shard_map/ppermute | solution.py:30
  55.0 20.8 %collective-permute-start.5 = (bf16[8,256,256]{2,1,0:T(8,128)(2,1)S(1)}, bf16[8,256,256]{2,1,0:T(8,128)(2,1)S(1)}, u32[]{:S(2)}, u32[]{:S(2)}) collective-permute-start(bf16[8,256,256]{2,1,0:T(8,128)(2,1)S(1)} %bitcast.208), channel_id=1, source_target_pairs={{0,16},{1,17},{2,18},{3,19},{4,20},{5,21},{6,22},{7,23},{8,24},{9,... | collective-permute-start | bytes 3145736 | tf_op jit(solution)/shard_map/ppermute | solution.py:30
  98.2 33.3 %all-to-all-start.1 = ((bf16[8,32,1024]{2,1,0:T(8,128)(2,1)}), bf16[8,32,1024]{2,1,0:T(8,128)(2,1)S(1)}, u32[]{:S(2)}, u32[]{:S(2)}) async-start(bf16[8,32,1024]{2,1,0:T(8,128)(2,1)} %reshape.111), calls=%async_computation.1 | async-start | bytes 1048576 | tf_op jit(solution)/shard_map/all_to_all | solution.py:190
  101.7 116.3 %all-gather.7.cloned.1.call-start = ((), (), s32[]{:S(2)}) async-start(), calls=%async_computation.5 | async-start | bytes 4718592 | tf_op jit(solution)/shard_map/all_gather | solution.py:197
  101.7 18.4 %collective-permute-start.9 = (bf16[8,4096]{1,0:T(8,128)(2,1)S(1)}, bf16[8,4096]{1,0:T(8,128)(2,1)S(1)}, u32[]{:S(2)}, u32[]{:S(2)}) collective-permute-start(bf16[8,4096]{1,0:T(8,128)(2,1)S(1)} %slice_bitcast_fusion.13), channel_id=1, source_target_pairs={{0,8},{1,9},{2,10},{3,11},{4,12},{5,13},{6,14},{7,15},{8,0},{9,1},... | collective-permute-start | bytes 196616 | tf_op jit(solution)/shard_map/ppermute | solution.py:30
  109.7 12.2 %collective-permute-start.10 = (bf16[8,4096]{1,0:T(8,128)(2,1)S(1)}, bf16[8,4096]{1,0:T(8,128)(2,1)S(1)}, u32[]{:S(2)}, u32[]{:S(2)}) collective-permute-start(bf16[8,4096]{1,0:T(8,128)(2,1)S(1)} %slice_bitcast_fusion.13), channel_id=1, source_target_pairs={{0,64},{1,65},{2,66},{3,67},{4,68},{5,69},{6,70},{7,71},{8,72},{9,... | collective-permute-start | bytes 196616 | tf_op jit(solution)/shard_map/ppermute | solution.py:30
  121.9 9.5 %collective-permute-start.12 = (bf16[4,8,4096]{2,1,0:T(8,128)(2,1)S(1)}, bf16[4,8,4096]{2,1,0:T(8,128)(2,1)S(1)}, u32[]{:S(2)}, u32[]{:S(2)}) collective-permute-start(bf16[4,8,4096]{2,1,0:T(8,128)(2,1)S(1)} %get-tuple-element.80), channel_id=1, source_target_pairs={{0,256},{1,257},{2,258},{3,259},{4,260},{5,261},{6,262},{7,263},{8... | collective-permute-start | bytes 786440 | tf_op jit(solution)/shard_map/ppermute | solution.py:30
  124.5 11.1 %collective-permute-start.13 = (bf16[4,8,4096]{2,1,0:T(8,128)(2,1)S(1)}, bf16[4,8,4096]{2,1,0:T(8,128)(2,1)S(1)}, u32[]{:S(2)}, u32[]{:S(2)}) collective-permute-start(bf16[4,8,4096]{2,1,0:T(8,128)(2,1)S(1)} %get-tuple-element.80), channel_id=1, source_target_pairs={{0,128},{1,129},{2,130},{3,131},{4,132},{5,133},{6,134},{7,135},{8... | collective-permute-start | bytes 786440 | tf_op jit(solution)/shard_map/ppermute | solution.py:30
  127.0 11.7 %collective-permute-start.14 = (bf16[4,8,4096]{2,1,0:T(8,128)(2,1)S(1)}, bf16[4,8,4096]{2,1,0:T(8,128)(2,1)S(1)}, u32[]{:S(2)}, u32[]{:S(2)}) collective-permute-start(bf16[4,8,4096]{2,1,0:T(8,128)(2,1)S(1)} %get-tuple-element.80), channel_id=1, source_target_pairs={{0,384},{1,385},{2,386},{3,387},{4,388},{5,389},{6,390},{7,391},{8... | collective-permute-start | bytes 786440 | tf_op jit(solution)/shard_map/ppermute | solution.py:30
  150.0 16.2 %collective-permute-start.23 = (bf16[64,4096]{1,0:T(8,128)(2,1)}, bf16[64,4096]{1,0:T(8,128)(2,1)S(1)}, u32[]{:S(2)}, u32[]{:S(2)}) collective-permute-start(bf16[64,4096]{1,0:T(8,128)(2,1)} %fusion.5), channel_id=1, source_target_pairs={{0,32},{1,33},{2,34},{3,35},{4,36},{5,37},{6,38},{7,39},{8,40},{9,... | collective-permute-start | bytes 1572872 | tf_op jit(solution)/shard_map/ppermute | solution.py:30
  156.4 17.8 %collective-permute-start.17 = (bf16[4,8,4096]{2,1,0:T(8,128)(2,1)}, bf16[4,8,4096]{2,1,0:T(8,128)(2,1)S(1)}, u32[]{:S(2)}, u32[]{:S(2)}) collective-permute-start(bf16[4,8,4096]{2,1,0:T(8,128)(2,1)} %get-tuple-element.71), channel_id=1, source_target_pairs={{0,256},{1,257},{2,258},{3,259},{4,260},{5,261},{6,262},{7,263},{8... | collective-permute-start | bytes 786440 | tf_op jit(solution)/shard_map/ppermute | solution.py:30
  159.6 14.6 %collective-permute-start.18 = (bf16[4,8,4096]{2,1,0:T(8,128)(2,1)S(1)}, bf16[4,8,4096]{2,1,0:T(8,128)(2,1)}, u32[]{:S(2)}, u32[]{:S(2)}) collective-permute-start(bf16[4,8,4096]{2,1,0:T(8,128)(2,1)S(1)} %get-tuple-element.70), channel_id=1, source_target_pairs={{0,128},{1,129},{2,130},{3,131},{4,132},{5,133},{6,134},{7,135},{8... | collective-permute-start | bytes 786440 | tf_op jit(solution)/shard_map/ppermute | solution.py:30
  161.9 12.4 %collective-permute-start.19 = (bf16[4,8,4096]{2,1,0:T(8,128)(2,1)S(1)}, bf16[4,8,4096]{2,1,0:T(8,128)(2,1)}, u32[]{:S(2)}, u32[]{:S(2)}) collective-permute-start(bf16[4,8,4096]{2,1,0:T(8,128)(2,1)S(1)} %get-tuple-element.69), channel_id=1, source_target_pairs={{0,384},{1,385},{2,386},{3,387},{4,388},{5,389},{6,390},{7,391},{8... | collective-permute-start | bytes 786440 | tf_op jit(solution)/shard_map/ppermute | solution.py:30
  167.3 29.9 %all-to-all-start.2 = ((bf16[8,8,4096]{2,1,0:T(8,128)(2,1)}), bf16[8,8,4096]{2,1,0:T(8,128)(2,1)S(1)}, u32[]{:S(2)}, u32[]{:S(2)}) async-start(bf16[8,8,4096]{2,1,0:T(8,128)(2,1)} %fusion.6), calls=%async_computation.2 | async-start | bytes 1048576 | tf_op jit(solution)/shard_map/all_to_all | solution.py:232
  175.5 11.4 %collective-permute-start.20 = (bf16[8,4096]{1,0:T(8,128)(2,1)S(1)}, bf16[8,4096]{1,0:T(8,128)(2,1)S(1)}, u32[]{:S(2)}, u32[]{:S(2)}) collective-permute-start(bf16[8,4096]{1,0:T(8,128)(2,1)S(1)} %get-tuple-element.77), channel_id=1, source_target_pairs={{0,8},{1,9},{2,10},{3,11},{4,12},{5,13},{6,14},{7,15},{8,0},{9,1},... | collective-permute-start | bytes 196616 | tf_op jit(solution)/shard_map/ppermute | solution.py:30
  227.5 11.3 %collective-permute-start.25 = (f32[256,256]{1,0:T(8,128)S(1)}, f32[256,256]{1,0:T(8,128)S(1)}, u32[]{:S(2)}, u32[]{:S(2)}) collective-permute-start(f32[256,256]{1,0:T(8,128)S(1)} %get-tuple-element.66), channel_id=1, source_target_pairs={{0,256},{1,257},{2,258},{3,259},{4,260},{5,261},{6,262},{7,263},{8... | collective-permute-start | bytes 786440 | tf_op jit(solution)/shard_map/ppermute | solution.py:30
  231.0 12.3 %collective-permute-start.26 = (f32[256,256]{1,0:T(8,128)S(1)}, f32[256,256]{1,0:T(8,128)S(1)}, u32[]{:S(2)}, u32[]{:S(2)}) collective-permute-start(f32[256,256]{1,0:T(8,128)S(1)} %get-tuple-element.67), channel_id=1, source_target_pairs={{0,128},{1,129},{2,130},{3,131},{4,132},{5,133},{6,134},{7,135},{8... | collective-permute-start | bytes 786440 | tf_op jit(solution)/shard_map/ppermute | solution.py:30
  233.2 11.0 %collective-permute-start.27 = (f32[256,256]{1,0:T(8,128)S(1)}, f32[256,256]{1,0:T(8,128)S(1)}, u32[]{:S(2)}, u32[]{:S(2)}) collective-permute-start(f32[256,256]{1,0:T(8,128)S(1)} %get-tuple-element.68), channel_id=1, source_target_pairs={{0,384},{1,385},{2,386},{3,387},{4,388},{5,389},{6,390},{7,391},{8... | collective-permute-start | bytes 786440 | tf_op jit(solution)/shard_map/ppermute | solution.py:30
  (19 other events, 135.3 us)
Sparse Core Ops, SparseCore 0:
  98.3 36.1 all-gather.4
  150.1 67.9 all-gather.6

commit v23 on v19

--- a/solution.py
+++ b/solution.py
@@ -18,7 +18,7 @@
 GROUPS = [list(range(Y)), list(range(Y, MP))]
 SAME_CORE = [list(range(core, DP, 2)) for core in range(2)]
 SAME_X = [list(range(x * DP // X, (x + 1) * DP // X)) for x in range(X)]
-X_SLOTS = np.array([0, 2, 1, 3])
+X_SLOTS = np.array([0, 2, 3, 1])
 Z_SLOTS = np.array([0, 3, 2, 1])
 ALONG_X = [(8 * int(k),) for k in X_SLOTS[1:]]
 ALONG_Z = [(2 * int(k),) for k in Z_SLOTS[1:]]

time: 241 us -> 241 us (level)
  starting transfers between devices: 108 us -> 105 us
  waiting for transfers between devices: 48.8 us -> 51.5 us
    ppermute x27, waiting for transfers between devices: 42.9 us -> 46.2 us  [swap(): lax.ppermute(array, ('dp', 'mp'), [(i, i ^ mask) for i in range(DP * MP)])]
    ppermute x27, starting transfers between devices: 97.8 us -> 95 us  [swap(): lax.ppermute(array, ('dp', 'mp'), [(i, i ^ mask) for i in range(DP * MP)])]
  transfers between devices with their start and end apart: 31 -> 31, of which waited for: 18 -> 15; matrix products, arithmetic and copies ran while one was open for 5% -> 5% of each run, Pallas kernels for 1% -> 1%
where the time goes in v23:
time: 241 us; the launch traced here: 239 us
  starting transfers between devices  105 us (44%)
  waiting for transfers between devices  51.5 us (21%)
  blocking collectives  39.4 us (16%)
  between operations  14.1 us (6%)
  local copies, waits for them, and re-layouts  7.73 us (3%)
  Pallas kernels  7.41 us (3%)
  matrix products  6.96 us (3%)
  other arithmetic  6.88 us (3%)
    ppermute x27, starting transfers between devices, swap(): lax.ppermute(array, ('dp', 'mp'), [(i, i ^ mask) for i in range(DP * MP)])  95 us
    ppermute x27, waiting for transfers between devices, swap(): lax.ppermute(array, ('dp', 'mp'), [(i, i ^ mask) for i in range(DP * MP)])  46.2 us
    all_to_all x1, blocking collectives, per_device(): lax.all_to_all(projected.reshape(DP, block, (views + 1) * images), 'dp',...  20 us
    all_to_all x1, blocking collectives, per_device(): lax.all_to_all(jnp.stack([part for part in blocks for _ in range(DP // X...  19.4 us
    all_to_all x1, starting transfers between devices, per_device(): lax.all_to_all(terms_b.reshape(Y, block, total), 'mp', split_axis=0, conc...  6.81 us
    all_to_all x1, waiting for transfers between devices, per_device(): lax.all_to_all(terms_b.reshape(Y, block, total), 'mp', split_axis=0, conc...  4.97 us
  transfers between devices with their start and end apart: 31, of which 15 were waited for; matrix products, arithmetic and copies ran while one was open for 5% of the time, Pallas kernels for 1%

profile of v23, /device:TPU:1, one launch (start us, length us, event | category | flops | bytes accessed | tf_op | source)
XLA Modules:
  0.0 239.4 jit_solution(16249677281579408827)
XLA Ops:
  6.5 8.4 %collective-permute-start = (bf16[256,256]{1,0:T(8,128)(2,1)}, bf16[256,256]{1,0:T(8,128)(2,1)S(1)}, u32[]{:S(2)}, u32[]{:S(2)}) collective-permute-start(bf16[256,256]{1,0:T(8,128)(2,1)} %param.8), channel_id=1, source_target_pairs={{0,96},{1,97},{2,98},{3,99},{4,100},{5,101},{6,102},{7,103},{8,104... | collective-permute-start | bytes 393224 | tf_op jit(solution)/shard_map/ppermute | solution.py:30
  19.1 6.7 %collective-permute-done.1 = bf16[256,256]{1,0:T(8,128)(2,1)S(1)} collective-permute-done((bf16[256,256]{1,0:T(8,128)(2,1)}, bf16[256,256]{1,0:T(8,128)(2,1)S(1)}, u32[]{:S(2)}, u32[]{:S(2)}) %collective-permute-start.1) | collective-permute-done | bytes 131104 | tf_op jit(solution)/shard_map/ppermute | solution.py:30
  26.9 5.1 %collective-permute-start.5 = (bf16[4,256,256]{2,1,0:T(8,128)(2,1)S(1)}, bf16[4,256,256]{2,1,0:T(8,128)(2,1)S(1)}, u32[]{:S(2)}, u32[]{:S(2)}) collective-permute-start(bf16[4,256,256]{2,1,0:T(8,128)(2,1)S(1)} %get-tuple-element.76), channel_id=1, source_target_pairs={{0,256},{1,257},{2,258},{3,259},{4,260},{5,261},{6,262},{7,263},{8... | collective-permute-start | bytes 1572872 | tf_op jit(solution)/shard_map/ppermute | solution.py:30
  39.3 2.9 %collective-permute-done.5 = bf16[4,256,256]{2,1,0:T(8,128)(2,1)S(1)} collective-permute-done((bf16[4,256,256]{2,1,0:T(8,128)(2,1)S(1)}, bf16[4,256,256]{2,1,0:T(8,128)(2,1)S(1)}, u32[]{:S(2)}, u32[]{:S(2)}) %collective-permute-start.5) | collective-permute-done | bytes 524320 | tf_op jit(solution)/shard_map/ppermute | solution.py:30
  42.3 6.9 %collective-permute-start.7 = (bf16[2,4,256,256]{3,2,1,0:T(8,128)(2,1)S(1)}, bf16[2,4,256,256]{3,2,1,0:T(8,128)(2,1)S(1)}, u32[]{:S(2)}, u32[]{:S(2)}) collective-permute-start(bf16[2,4,256,256]{3,2,1,0:T(8,128)(2,1)S(1)} %pad_maximum_fusion.1), channel_id=1, source_target_pairs={{0,16},{1,17},{2,18},{3,19},{4,20},{5,21},{6,22},{7,23},{8,24},{9,... | collective-permute-start | bytes 3145736 | tf_op jit(solution)/shard_map/ppermute | solution.py:30
  49.2 6.5 %collective-permute-done.3 = bf16[4,256,256]{2,1,0:T(8,128)(2,1)} collective-permute-done((bf16[4,256,256]{2,1,0:T(8,128)(2,1)S(1)}, bf16[4,256,256]{2,1,0:T(8,128)(2,1)}, u32[]{:S(2)}, u32[]{:S(2)}) %collective-permute-start.3) | collective-permute-done | bytes 524320 | tf_op jit(solution)/shard_map/ppermute | solution.py:30
  65.3 20.0 %all_to_all.20 = f32[32,8,384]{2,1,0:T(8,128)S(1)} all-to-all(f32[32,8,384]{2,1,0:T(8,128)S(1)} %bitcast.217), channel_id=1, replica_groups=mesh['dp'=32,'mp'=16] {'dp'}, dimensions={0} | all-to-all | bytes 786432 | tf_op jit(solution)/shard_map/all_to_all | solution.py:178
  86.5 3.5 %all-to-all-start.1 = ((bf16[8,32,1024]{2,1,0:T(8,128)(2,1)}), bf16[8,32,1024]{2,1,0:T(8,128)(2,1)S(1)}, u32[]{:S(2)}, u32[]{:S(2)}) async-start(bf16[8,32,1024]{2,1,0:T(8,128)(2,1)} %reshape.119), calls=%async_computation.1 | async-start | bytes 1048576 | tf_op jit(solution)/shard_map/all_to_all | solution.py:189
  90.0 7.9 %collective-permute-start.8 = (bf16[8,4096]{1,0:T(8,128)(2,1)S(1)}, bf16[8,4096]{1,0:T(8,128)(2,1)S(1)}, u32[]{:S(2)}, u32[]{:S(2)}) collective-permute-start(bf16[8,4096]{1,0:T(8,128)(2,1)S(1)} %slice_bitcast_fusion.13), channel_id=1, source_target_pairs={{0,8},{1,9},{2,10},{3,11},{4,12},{5,13},{6,14},{7,15},{8,0},{9,1},... | collective-permute-start | bytes 196616 | tf_op jit(solution)/shard_map/ppermute | solution.py:30
  97.9 4.2 %collective-permute-start.9 = (bf16[8,4096]{1,0:T(8,128)(2,1)S(1)}, bf16[8,4096]{1,0:T(8,128)(2,1)S(1)}, u32[]{:S(2)}, u32[]{:S(2)}) collective-permute-start(bf16[8,4096]{1,0:T(8,128)(2,1)S(1)} %slice_bitcast_fusion.13), channel_id=1, source_target_pairs={{0,64},{1,65},{2,66},{3,67},{4,68},{5,69},{6,70},{7,71},{8,72},{9,... | collective-permute-start | bytes 196616 | tf_op jit(solution)/shard_map/ppermute | solution.py:30
  104.1 4.3 %collective-permute-done.8 = bf16[8,4096]{1,0:T(8,128)(2,1)S(1)} collective-permute-done((bf16[8,4096]{1,0:T(8,128)(2,1)S(1)}, bf16[8,4096]{1,0:T(8,128)(2,1)S(1)}, u32[]{:S(2)}, u32[]{:S(2)}) %collective-permute-start.8) | collective-permute-done | bytes 65568 | tf_op jit(solution)/shard_map/ppermute | solution.py:30
  112.7 3.3 %collective-permute-start.12 = (bf16[4,8,4096]{2,1,0:T(8,128)(2,1)S(1)}, bf16[4,8,4096]{2,1,0:T(8,128)(2,1)S(1)}, u32[]{:S(2)}, u32[]{:S(2)}) collective-permute-start(bf16[4,8,4096]{2,1,0:T(8,128)(2,1)S(1)} %get-tuple-element.84), channel_id=1, source_target_pairs={{0,384},{1,385},{2,386},{3,387},{4,388},{5,389},{6,390},{7,391},{8... | collective-permute-start | bytes 786440 | tf_op jit(solution)/shard_map/ppermute | solution.py:30
  119.7 7.7 %collective-permute-done.12 = bf16[4,8,4096]{2,1,0:T(8,128)(2,1)S(1)} collective-permute-done((bf16[4,8,4096]{2,1,0:T(8,128)(2,1)S(1)}, bf16[4,8,4096]{2,1,0:T(8,128)(2,1)S(1)}, u32[]{:S(2)}, u32[]{:S(2)}) %collective-permute-start.12) | collective-permute-done | bytes 262176 | tf_op jit(solution)/shard_map/ppermute | solution.py:30
  137.6 3.7 %collective-permute-start.22 = (bf16[64,4096]{1,0:T(8,128)(2,1)}, bf16[64,4096]{1,0:T(8,128)(2,1)S(1)}, u32[]{:S(2)}, u32[]{:S(2)}) collective-permute-start(bf16[64,4096]{1,0:T(8,128)(2,1)} %fusion.5), channel_id=1, source_target_pairs={{0,32},{1,33},{2,34},{3,35},{4,36},{5,37},{6,38},{7,39},{8,40},{9,... | collective-permute-start | bytes 1572872 | tf_op jit(solution)/shard_map/ppermute | solution.py:30
  144.0 4.0 %collective-permute-start.16 = (bf16[4,8,4096]{2,1,0:T(8,128)(2,1)}, bf16[4,8,4096]{2,1,0:T(8,128)(2,1)S(1)}, u32[]{:S(2)}, u32[]{:S(2)}) collective-permute-start(bf16[4,8,4096]{2,1,0:T(8,128)(2,1)} %get-tuple-element.73), channel_id=1, source_target_pairs={{0,256},{1,257},{2,258},{3,259},{4,260},{5,261},{6,262},{7,263},{8... | collective-permute-start | bytes 786440 | tf_op jit(solution)/shard_map/ppermute | solution.py:30
  155.0 6.8 %all-to-all-start.2 = ((bf16[8,8,4096]{2,1,0:T(8,128)(2,1)}), bf16[8,8,4096]{2,1,0:T(8,128)(2,1)S(1)}, u32[]{:S(2)}, u32[]{:S(2)}) async-start(bf16[8,8,4096]{2,1,0:T(8,128)(2,1)} %fusion.6), calls=%async_computation.2 | async-start | bytes 1048576 | tf_op jit(solution)/shard_map/all_to_all | solution.py:231
  163.0 7.3 %collective-permute-start.19 = (bf16[8,4096]{1,0:T(8,128)(2,1)S(1)}, bf16[8,4096]{1,0:T(8,128)(2,1)S(1)}, u32[]{:S(2)}, u32[]{:S(2)}) collective-permute-start(bf16[8,4096]{1,0:T(8,128)(2,1)S(1)} %get-tuple-element.81), channel_id=1, source_target_pairs={{0,8},{1,9},{2,10},{3,11},{4,12},{5,13},{6,14},{7,15},{8,0},{9,1},... | collective-permute-start | bytes 196616 | tf_op jit(solution)/shard_map/ppermute | solution.py:30
  179.9 5.0 %all-to-all-done.2 = bf16[8,8,4096]{2,1,0:T(8,128)(2,1)S(1)} async-done(((bf16[8,8,4096]{2,1,0:T(8,128)(2,1)}), bf16[8,8,4096]{2,1,0:T(8,128)(2,1)S(1)}, u32[]{:S(2)}, u32[]{:S(2)}) %all-to-all-start.2) | async-done | bytes 524320 | tf_op jit(solution)/shard_map/all_to_all | solution.py:231
  185.6 19.4 %all_to_all.21 = bf16[16,8,2048]{2,1,0:T(8,128)(2,1)S(1)} all-to-all(bf16[16,8,2048]{2,1,0:T(8,128)(2,1)S(1)} %constant_dynamic-update-slice_fusion), channel_id=1, replica_groups={{0,32,64,96,128,160,192,224,256,288,320,352,384,416,448,480},{16,48,80,..., dimensions={0} | all-to-all | bytes 1048576 | tf_op jit(solution)/shard_map/all_to_all | solution.py:252
  205.3 3.6 %collective-permute-start.23 = (bf16[16,8,2048]{2,1,0:T(8,128)(2,1)S(1)}, bf16[16,8,2048]{2,1,0:T(8,128)(2,1)S(1)}, u32[]{:S(2)}, u32[]{:S(2)}) collective-permute-start(bf16[16,8,2048]{2,1,0:T(8,128)(2,1)S(1)} %all_to_all.21), channel_id=1, source_target_pairs={{0,16},{1,17},{2,18},{3,19},{4,20},{5,21},{6,22},{7,23},{8,24},{9,... | collective-permute-start | bytes 1572872 | tf_op jit(solution)/shard_map/ppermute | solution.py:30
  213.8 3.6 %collective-permute-start.24 = (f32[256,256]{1,0:T(8,128)S(1)}, f32[256,256]{1,0:T(8,128)S(1)}, u32[]{:S(2)}, u32[]{:S(2)}) collective-permute-start(f32[256,256]{1,0:T(8,128)S(1)} %get-tuple-element.68), channel_id=1, source_target_pairs={{0,256},{1,257},{2,258},{3,259},{4,260},{5,261},{6,262},{7,263},{8... | collective-permute-start | bytes 786440 | tf_op jit(solution)/shard_map/ppermute | solution.py:30
  217.5 2.8 %collective-permute-start.25 = (f32[256,256]{1,0:T(8,128)S(1)}, f32[256,256]{1,0:T(8,128)S(1)}, u32[]{:S(2)}, u32[]{:S(2)}) collective-permute-start(f32[256,256]{1,0:T(8,128)S(1)} %get-tuple-element.69), channel_id=1, source_target_pairs={{0,384},{1,385},{2,386},{3,387},{4,388},{5,389},{6,390},{7,391},{8... | collective-permute-start | bytes 786440 | tf_op jit(solution)/shard_map/ppermute | solution.py:30
  222.3 2.9 %collective-permute-done.24.refs_1_ = f32[256,256]{1,0:T(8,128)S(1)} collective-permute-done((f32[256,256]{1,0:T(8,128)S(1)}, f32[256,256]{1,0:T(8,128)S(1)}, u32[]{:S(2)}, u32[]{:S(2)}) %collective-permute-start.24) | collective-permute-done | bytes 262176 | tf_op jit(solution)/shard_map/ppermute | solution.py:30
  225.2 5.9 %collective-permute-done.25.refs_2_ = f32[256,256]{1,0:T(8,128)S(1)} collective-permute-done((f32[256,256]{1,0:T(8,128)S(1)}, f32[256,256]{1,0:T(8,128)S(1)}, u32[]{:S(2)}, u32[]{:S(2)}) %collective-permute-start.25) | collective-permute-done | bytes 262176 | tf_op jit(solution)/shard_map/ppermute | solution.py:30
  (125 shorter events, 72.7 us)
Async XLA Ops:
  6.5 121.1 %all-gather.5.cloned.1.call-start = ((), (), s32[]{:S(2)}) async-start(), calls=%async_computation.4 | async-start | bytes 1179648 | tf_op jit(solution)/shard_map/all_gather | solution.py:192
  6.5 12.6 %collective-permute-start = (bf16[256,256]{1,0:T(8,128)(2,1)}, bf16[256,256]{1,0:T(8,128)(2,1)S(1)}, u32[]{:S(2)}, u32[]{:S(2)}) collective-permute-start(bf16[256,256]{1,0:T(8,128)(2,1)} %param.8), channel_id=1, source_target_pairs={{0,96},{1,97},{2,98},{3,99},{4,100},{5,101},{6,102},{7,103},{8,104... | collective-permute-start | bytes 393224 | tf_op jit(solution)/shard_map/ppermute | solution.py:30
  15.0 10.9 %collective-permute-start.1 = (bf16[256,256]{1,0:T(8,128)(2,1)}, bf16[256,256]{1,0:T(8,128)(2,1)S(1)}, u32[]{:S(2)}, u32[]{:S(2)}) collective-permute-start(bf16[256,256]{1,0:T(8,128)(2,1)} %param.8), channel_id=1, source_target_pairs={{0,64},{1,65},{2,66},{3,67},{4,68},{5,69},{6,70},{7,71},{8,72},{9,... | collective-permute-start | bytes 393224 | tf_op jit(solution)/shard_map/ppermute | solution.py:30
  16.9 9.0 %collective-permute-start.2 = (bf16[256,256]{1,0:T(8,128)(2,1)}, bf16[256,256]{1,0:T(8,128)(2,1)S(1)}, u32[]{:S(2)}, u32[]{:S(2)}) collective-permute-start(bf16[256,256]{1,0:T(8,128)(2,1)} %param.8), channel_id=1, source_target_pairs={{0,32},{1,33},{2,34},{3,35},{4,36},{5,37},{6,38},{7,39},{8,40},{9,... | collective-permute-start | bytes 393224 | tf_op jit(solution)/shard_map/ppermute | solution.py:30
  26.9 15.3 %collective-permute-start.5 = (bf16[4,256,256]{2,1,0:T(8,128)(2,1)S(1)}, bf16[4,256,256]{2,1,0:T(8,128)(2,1)S(1)}, u32[]{:S(2)}, u32[]{:S(2)}) collective-permute-start(bf16[4,256,256]{2,1,0:T(8,128)(2,1)S(1)} %get-tuple-element.76), channel_id=1, source_target_pairs={{0,256},{1,257},{2,258},{3,259},{4,260},{5,261},{6,262},{7,263},{8... | collective-permute-start | bytes 1572872 | tf_op jit(solution)/shard_map/ppermute | solution.py:30
  32.0 23.7 %collective-permute-start.3 = (bf16[4,256,256]{2,1,0:T(8,128)(2,1)S(1)}, bf16[4,256,256]{2,1,0:T(8,128)(2,1)}, u32[]{:S(2)}, u32[]{:S(2)}) collective-permute-start(bf16[4,256,256]{2,1,0:T(8,128)(2,1)S(1)} %get-tuple-element.76), channel_id=1, source_target_pairs={{0,384},{1,385},{2,386},{3,387},{4,388},{5,389},{6,390},{7,391},{8... | collective-permute-start | bytes 1572872 | tf_op jit(solution)/shard_map/ppermute | solution.py:30
  34.8 20.9 %collective-permute-start.4 = (bf16[4,256,256]{2,1,0:T(8,128)(2,1)S(1)}, bf16[4,256,256]{2,1,0:T(8,128)(2,1)}, u32[]{:S(2)}, u32[]{:S(2)}) collective-permute-start(bf16[4,256,256]{2,1,0:T(8,128)(2,1)S(1)} %get-tuple-element.76), channel_id=1, source_target_pairs={{0,128},{1,129},{2,130},{3,131},{4,132},{5,133},{6,134},{7,135},{8... | collective-permute-start | bytes 1572872 | tf_op jit(solution)/shard_map/ppermute | solution.py:30
  42.3 17.5 %collective-permute-start.7 = (bf16[2,4,256,256]{3,2,1,0:T(8,128)(2,1)S(1)}, bf16[2,4,256,256]{3,2,1,0:T(8,128)(2,1)S(1)}, u32[]{:S(2)}, u32[]{:S(2)}) collective-permute-start(bf16[2,4,256,256]{3,2,1,0:T(8,128)(2,1)S(1)} %pad_maximum_fusion.1), channel_id=1, source_target_pairs={{0,16},{1,17},{2,18},{3,19},{4,20},{5,21},{6,22},{7,23},{8,24},{9,... | collective-permute-start | bytes 3145736 | tf_op jit(solution)/shard_map/ppermute | solution.py:30
  86.5 33.3 %all-to-all-start.1 = ((bf16[8,32,1024]{2,1,0:T(8,128)(2,1)}), bf16[8,32,1024]{2,1,0:T(8,128)(2,1)S(1)}, u32[]{:S(2)}, u32[]{:S(2)}) async-start(bf16[8,32,1024]{2,1,0:T(8,128)(2,1)} %reshape.119), calls=%async_computation.1 | async-start | bytes 1048576 | tf_op jit(solution)/shard_map/all_to_all | solution.py:189
  90.0 115.3 %all-gather.7.cloned.1.call-start = ((), (), s32[]{:S(2)}) async-start(), calls=%async_computation.5 | async-start | bytes 4718592 | tf_op jit(solution)/shard_map/all_gather | solution.py:196
  90.0 18.4 %collective-permute-start.8 = (bf16[8,4096]{1,0:T(8,128)(2,1)S(1)}, bf16[8,4096]{1,0:T(8,128)(2,1)S(1)}, u32[]{:S(2)}, u32[]{:S(2)}) collective-permute-start(bf16[8,4096]{1,0:T(8,128)(2,1)S(1)} %slice_bitcast_fusion.13), channel_id=1, source_target_pairs={{0,8},{1,9},{2,10},{3,11},{4,12},{5,13},{6,14},{7,15},{8,0},{9,1},... | collective-permute-start | bytes 196616 | tf_op jit(solution)/shard_map/ppermute | solution.py:30
  97.9 12.2 %collective-permute-start.9 = (bf16[8,4096]{1,0:T(8,128)(2,1)S(1)}, bf16[8,4096]{1,0:T(8,128)(2,1)S(1)}, u32[]{:S(2)}, u32[]{:S(2)}) collective-permute-start(bf16[8,4096]{1,0:T(8,128)(2,1)S(1)} %slice_bitcast_fusion.13), channel_id=1, source_target_pairs={{0,64},{1,65},{2,66},{3,67},{4,68},{5,69},{6,70},{7,71},{8,72},{9,... | collective-permute-start | bytes 196616 | tf_op jit(solution)/shard_map/ppermute | solution.py:30
  110.2 9.5 %collective-permute-start.11 = (bf16[4,8,4096]{2,1,0:T(8,128)(2,1)S(1)}, bf16[4,8,4096]{2,1,0:T(8,128)(2,1)S(1)}, u32[]{:S(2)}, u32[]{:S(2)}) collective-permute-start(bf16[4,8,4096]{2,1,0:T(8,128)(2,1)S(1)} %get-tuple-element.84), channel_id=1, source_target_pairs={{0,256},{1,257},{2,258},{3,259},{4,260},{5,261},{6,262},{7,263},{8... | collective-permute-start | bytes 786440 | tf_op jit(solution)/shard_map/ppermute | solution.py:30
  112.7 14.7 %collective-permute-start.12 = (bf16[4,8,4096]{2,1,0:T(8,128)(2,1)S(1)}, bf16[4,8,4096]{2,1,0:T(8,128)(2,1)S(1)}, u32[]{:S(2)}, u32[]{:S(2)}) collective-permute-start(bf16[4,8,4096]{2,1,0:T(8,128)(2,1)S(1)} %get-tuple-element.84), channel_id=1, source_target_pairs={{0,384},{1,385},{2,386},{3,387},{4,388},{5,389},{6,390},{7,391},{8... | collective-permute-start | bytes 786440 | tf_op jit(solution)/shard_map/ppermute | solution.py:30
  116.1 11.4 %collective-permute-start.13 = (bf16[4,8,4096]{2,1,0:T(8,128)(2,1)S(1)}, bf16[4,8,4096]{2,1,0:T(8,128)(2,1)S(1)}, u32[]{:S(2)}, u32[]{:S(2)}) collective-permute-start(bf16[4,8,4096]{2,1,0:T(8,128)(2,1)S(1)} %get-tuple-element.84), channel_id=1, source_target_pairs={{0,128},{1,129},{2,130},{3,131},{4,132},{5,133},{6,134},{7,135},{8... | collective-permute-start | bytes 786440 | tf_op jit(solution)/shard_map/ppermute | solution.py:30
  137.6 16.2 %collective-permute-start.22 = (bf16[64,4096]{1,0:T(8,128)(2,1)}, bf16[64,4096]{1,0:T(8,128)(2,1)S(1)}, u32[]{:S(2)}, u32[]{:S(2)}) collective-permute-start(bf16[64,4096]{1,0:T(8,128)(2,1)} %fusion.5), channel_id=1, source_target_pairs={{0,32},{1,33},{2,34},{3,35},{4,36},{5,37},{6,38},{7,39},{8,40},{9,... | collective-permute-start | bytes 1572872 | tf_op jit(solution)/shard_map/ppermute | solution.py:30
  144.0 17.8 %collective-permute-start.16 = (bf16[4,8,4096]{2,1,0:T(8,128)(2,1)}, bf16[4,8,4096]{2,1,0:T(8,128)(2,1)S(1)}, u32[]{:S(2)}, u32[]{:S(2)}) collective-permute-start(bf16[4,8,4096]{2,1,0:T(8,128)(2,1)} %get-tuple-element.73), channel_id=1, source_target_pairs={{0,256},{1,257},{2,258},{3,259},{4,260},{5,261},{6,262},{7,263},{8... | collective-permute-start | bytes 786440 | tf_op jit(solution)/shard_map/ppermute | solution.py:30
  148.0 13.8 %collective-permute-start.17 = (bf16[4,8,4096]{2,1,0:T(8,128)(2,1)S(1)}, bf16[4,8,4096]{2,1,0:T(8,128)(2,1)}, u32[]{:S(2)}, u32[]{:S(2)}) collective-permute-start(bf16[4,8,4096]{2,1,0:T(8,128)(2,1)S(1)} %get-tuple-element.72), channel_id=1, source_target_pairs={{0,384},{1,385},{2,386},{3,387},{4,388},{5,389},{6,390},{7,391},{8... | collective-permute-start | bytes 786440 | tf_op jit(solution)/shard_map/ppermute | solution.py:30
  150.8 11.1 %collective-permute-start.18 = (bf16[4,8,4096]{2,1,0:T(8,128)(2,1)S(1)}, bf16[4,8,4096]{2,1,0:T(8,128)(2,1)}, u32[]{:S(2)}, u32[]{:S(2)}) collective-permute-start(bf16[4,8,4096]{2,1,0:T(8,128)(2,1)S(1)} %get-tuple-element.71), channel_id=1, source_target_pairs={{0,128},{1,129},{2,130},{3,131},{4,132},{5,133},{6,134},{7,135},{8... | collective-permute-start | bytes 786440 | tf_op jit(solution)/shard_map/ppermute | solution.py:30
  155.0 29.9 %all-to-all-start.2 = ((bf16[8,8,4096]{2,1,0:T(8,128)(2,1)}), bf16[8,8,4096]{2,1,0:T(8,128)(2,1)S(1)}, u32[]{:S(2)}, u32[]{:S(2)}) async-start(bf16[8,8,4096]{2,1,0:T(8,128)(2,1)} %fusion.6), calls=%async_computation.2 | async-start | bytes 1048576 | tf_op jit(solution)/shard_map/all_to_all | solution.py:231
  163.0 11.6 %collective-permute-start.19 = (bf16[8,4096]{1,0:T(8,128)(2,1)S(1)}, bf16[8,4096]{1,0:T(8,128)(2,1)S(1)}, u32[]{:S(2)}, u32[]{:S(2)}) collective-permute-start(bf16[8,4096]{1,0:T(8,128)(2,1)S(1)} %get-tuple-element.81), channel_id=1, source_target_pairs={{0,8},{1,9},{2,10},{3,11},{4,12},{5,13},{6,14},{7,15},{8,0},{9,1},... | collective-permute-start | bytes 196616 | tf_op jit(solution)/shard_map/ppermute | solution.py:30
  213.8 11.4 %collective-permute-start.24 = (f32[256,256]{1,0:T(8,128)S(1)}, f32[256,256]{1,0:T(8,128)S(1)}, u32[]{:S(2)}, u32[]{:S(2)}) collective-permute-start(f32[256,256]{1,0:T(8,128)S(1)} %get-tuple-element.68), channel_id=1, source_target_pairs={{0,256},{1,257},{2,258},{3,259},{4,260},{5,261},{6,262},{7,263},{8... | collective-permute-start | bytes 786440 | tf_op jit(solution)/shard_map/ppermute | solution.py:30
  217.5 13.7 %collective-permute-start.25 = (f32[256,256]{1,0:T(8,128)S(1)}, f32[256,256]{1,0:T(8,128)S(1)}, u32[]{:S(2)}, u32[]{:S(2)}) collective-permute-start(f32[256,256]{1,0:T(8,128)S(1)} %get-tuple-element.69), channel_id=1, source_target_pairs={{0,384},{1,385},{2,386},{3,387},{4,388},{5,389},{6,390},{7,391},{8... | collective-permute-start | bytes 786440 | tf_op jit(solution)/shard_map/ppermute | solution.py:30
  220.3 10.9 %collective-permute-start.26 = (f32[256,256]{1,0:T(8,128)S(1)}, f32[256,256]{1,0:T(8,128)S(1)}, u32[]{:S(2)}, u32[]{:S(2)}) collective-permute-start(f32[256,256]{1,0:T(8,128)S(1)} %get-tuple-element.70), channel_id=1, source_target_pairs={{0,128},{1,129},{2,130},{3,131},{4,132},{5,133},{6,134},{7,135},{8... | collective-permute-start | bytes 786440 | tf_op jit(solution)/shard_map/ppermute | solution.py:30
  (16 other events, 142.5 us)
Sparse Core Ops, SparseCore 0:
  86.6 36.1 all-gather.4
  137.8 67.5 all-gather.6

commit v24 on v23

--- a/solution.py
+++ b/solution.py
@@ -216,6 +216,8 @@
     def times(lhs, rhs, dims):
         return lax.dot_general(lhs, rhs, (dims, ((), ())), preferred_element_type=jnp.float32) / total
 
+    terms_other = times(corr_other, columns_b, ((1,), (0,))).astype(jnp.bfloat16)
+    corr_other, terms_other = lax.optimization_barrier((corr_other, terms_other))
     half = (feat // 2, Y, 2, block)
     sides = [
         corr.reshape(half).transpose(2, 0, 1, 3).reshape(2, feat // 2, Y * block)
@@ -231,7 +233,6 @@
     terms_b = lax.all_to_all(
         terms_b.reshape(Y, block, total), "mp", split_axis=0, concat_axis=0, axis_index_groups=GROUPS
     )
-    terms_other = times(corr_other, columns_b, ((1,), (0,))).astype(jnp.bfloat16)
     terms_own = times(corr_own, columns_b, ((1,), (0,)))
     shape = (4, 4, block, total)
     terms_own, terms_other = terms_own.reshape(shape), swap(terms_other.reshape(shape), 1)
@@ -250,7 +251,9 @@
         for x in range(X)
     ]
     grad_own = lax.all_to_all(
-        jnp.stack([part for part in blocks for _ in range(DP // X // 2)]),
+        jnp.broadcast_to(jnp.stack(blocks)[:, None], (X, DP // X // 2, block, depth)).reshape(
+            DP // 2, block, depth
+        ),
         "dp",
         split_axis=0,
         concat_axis=0,

time: 241 us -> 245 us (1.017)
  transfers between devices with their start and end apart: 31 -> 31, of which waited for: 15 -> 14; matrix products, arithmetic and copies ran while one was open for 5% -> 7% of each run, Pallas kernels for 1% -> 1%
where the time goes in v24:
time: 245 us; the launch traced here: 244 us
  starting transfers between devices  106 us (43%)
  waiting for transfers between devices  52.9 us (22%)
  blocking collectives  39.6 us (16%)
  between operations  14.1 us (6%)
  matrix products  8.2 us (3%)
  local copies, waits for them, and re-layouts  7.88 us (3%)
  other arithmetic  7.68 us (3%)
  Pallas kernels  7.41 us (3%)
    ppermute x27, starting transfers between devices, swap(): lax.ppermute(array, ('dp', 'mp'), [(i, i ^ mask) for i in range(DP * MP)])  95.4 us
    ppermute x27, waiting for transfers between devices, swap(): lax.ppermute(array, ('dp', 'mp'), [(i, i ^ mask) for i in range(DP * MP)])  48 us
    all_to_all x1, blocking collectives, per_device(): lax.all_to_all(projected.reshape(DP, block, (views + 1) * images), 'dp',...  20 us
    all_to_all x1, blocking collectives, per_device(): lax.all_to_all(jnp.broadcast_to(jnp.stack(blocks)[:, None], (X, DP // X /...  19.7 us
    all_to_all x1, starting transfers between devices, per_device(): lax.all_to_all(terms_b.reshape(Y, block, total), 'mp', split_axis=0, conc...  6.81 us
    dot_general x6, matrix products, times(): lax.dot_general(lhs, rhs, (dims, ((), ())), preferred_element_type=jnp.fl...  6.1 us
  transfers between devices with their start and end apart: 31, of which 14 were waited for; matrix products, arithmetic and copies ran while one was open for 7% of the time, Pallas kernels for 1%

profile of v24, /device:TPU:1, one launch (start us, length us, event | category | flops | bytes accessed | tf_op | source)
XLA Modules:
  0.0 243.5 jit_solution(11006722593990057154)
XLA Ops:
  6.5 8.4 %collective-permute-start = (bf16[256,256]{1,0:T(8,128)(2,1)}, bf16[256,256]{1,0:T(8,128)(2,1)S(1)}, u32[]{:S(2)}, u32[]{:S(2)}) collective-permute-start(bf16[256,256]{1,0:T(8,128)(2,1)} %param.8), channel_id=1, source_target_pairs={{0,96},{1,97},{2,98},{3,99},{4,100},{5,101},{6,102},{7,103},{8,104... | collective-permute-start | bytes 393224 | tf_op jit(solution)/shard_map/ppermute | solution.py:30
  19.1 6.7 %collective-permute-done.1 = bf16[256,256]{1,0:T(8,128)(2,1)S(1)} collective-permute-done((bf16[256,256]{1,0:T(8,128)(2,1)}, bf16[256,256]{1,0:T(8,128)(2,1)S(1)}, u32[]{:S(2)}, u32[]{:S(2)}) %collective-permute-start.1) | collective-permute-done | bytes 131104 | tf_op jit(solution)/shard_map/ppermute | solution.py:30
  26.9 5.1 %collective-permute-start.5 = (bf16[4,256,256]{2,1,0:T(8,128)(2,1)S(1)}, bf16[4,256,256]{2,1,0:T(8,128)(2,1)S(1)}, u32[]{:S(2)}, u32[]{:S(2)}) collective-permute-start(bf16[4,256,256]{2,1,0:T(8,128)(2,1)S(1)} %get-tuple-element.78), channel_id=1, source_target_pairs={{0,256},{1,257},{2,258},{3,259},{4,260},{5,261},{6,262},{7,263},{8... | collective-permute-start | bytes 1572872 | tf_op jit(solution)/shard_map/ppermute | solution.py:30
  39.3 2.9 %collective-permute-done.5 = bf16[4,256,256]{2,1,0:T(8,128)(2,1)S(1)} collective-permute-done((bf16[4,256,256]{2,1,0:T(8,128)(2,1)S(1)}, bf16[4,256,256]{2,1,0:T(8,128)(2,1)S(1)}, u32[]{:S(2)}, u32[]{:S(2)}) %collective-permute-start.5) | collective-permute-done | bytes 524320 | tf_op jit(solution)/shard_map/ppermute | solution.py:30
  42.3 6.9 %collective-permute-start.7 = (bf16[2,4,256,256]{3,2,1,0:T(8,128)(2,1)S(1)}, bf16[2,4,256,256]{3,2,1,0:T(8,128)(2,1)S(1)}, u32[]{:S(2)}, u32[]{:S(2)}) collective-permute-start(bf16[2,4,256,256]{3,2,1,0:T(8,128)(2,1)S(1)} %pad_maximum_fusion.1), channel_id=1, source_target_pairs={{0,16},{1,17},{2,18},{3,19},{4,20},{5,21},{6,22},{7,23},{8,24},{9,... | collective-permute-start | bytes 3145736 | tf_op jit(solution)/shard_map/ppermute | solution.py:30
  49.2 6.5 %collective-permute-done.3 = bf16[4,256,256]{2,1,0:T(8,128)(2,1)} collective-permute-done((bf16[4,256,256]{2,1,0:T(8,128)(2,1)S(1)}, bf16[4,256,256]{2,1,0:T(8,128)(2,1)}, u32[]{:S(2)}, u32[]{:S(2)}) %collective-permute-start.3) | collective-permute-done | bytes 524320 | tf_op jit(solution)/shard_map/ppermute | solution.py:30
  65.3 20.0 %all_to_all.20 = f32[32,8,384]{2,1,0:T(8,128)S(1)} all-to-all(f32[32,8,384]{2,1,0:T(8,128)S(1)} %bitcast.194), channel_id=1, replica_groups=mesh['dp'=32,'mp'=16] {'dp'}, dimensions={0} | all-to-all | bytes 786432 | tf_op jit(solution)/shard_map/all_to_all | solution.py:178
  87.2 3.5 %all-to-all-start.1 = ((bf16[8,32,1024]{2,1,0:T(8,128)(2,1)}), bf16[8,32,1024]{2,1,0:T(8,128)(2,1)S(1)}, u32[]{:S(2)}, u32[]{:S(2)}) async-start(bf16[8,32,1024]{2,1,0:T(8,128)(2,1)} %reshape.123), calls=%async_computation.1 | async-start | bytes 1048576 | tf_op jit(solution)/shard_map/all_to_all | solution.py:189
  90.7 7.9 %collective-permute-start.8 = (bf16[8,4096]{1,0:T(8,128)(2,1)S(1)}, bf16[8,4096]{1,0:T(8,128)(2,1)S(1)}, u32[]{:S(2)}, u32[]{:S(2)}) collective-permute-start(bf16[8,4096]{1,0:T(8,128)(2,1)S(1)} %slice_bitcast_fusion.13), channel_id=1, source_target_pairs={{0,8},{1,9},{2,10},{3,11},{4,12},{5,13},{6,14},{7,15},{8,0},{9,1},... | collective-permute-start | bytes 196616 | tf_op jit(solution)/shard_map/ppermute | solution.py:30
  98.7 4.2 %collective-permute-start.9 = (bf16[8,4096]{1,0:T(8,128)(2,1)S(1)}, bf16[8,4096]{1,0:T(8,128)(2,1)S(1)}, u32[]{:S(2)}, u32[]{:S(2)}) collective-permute-start(bf16[8,4096]{1,0:T(8,128)(2,1)S(1)} %slice_bitcast_fusion.13), channel_id=1, source_target_pairs={{0,64},{1,65},{2,66},{3,67},{4,68},{5,69},{6,70},{7,71},{8,72},{9,... | collective-permute-start | bytes 196616 | tf_op jit(solution)/shard_map/ppermute | solution.py:30
  104.8 4.3 %collective-permute-done.8 = bf16[8,4096]{1,0:T(8,128)(2,1)S(1)} collective-permute-done((bf16[8,4096]{1,0:T(8,128)(2,1)S(1)}, bf16[8,4096]{1,0:T(8,128)(2,1)S(1)}, u32[]{:S(2)}, u32[]{:S(2)}) %collective-permute-start.8) | collective-permute-done | bytes 65568 | tf_op jit(solution)/shard_map/ppermute | solution.py:30
  113.5 3.3 %collective-permute-start.12 = (bf16[4,8,4096]{2,1,0:T(8,128)(2,1)S(1)}, bf16[4,8,4096]{2,1,0:T(8,128)(2,1)S(1)}, u32[]{:S(2)}, u32[]{:S(2)}) collective-permute-start(bf16[4,8,4096]{2,1,0:T(8,128)(2,1)S(1)} %get-tuple-element.86), channel_id=1, source_target_pairs={{0,384},{1,385},{2,386},{3,387},{4,388},{5,389},{6,390},{7,391},{8... | collective-permute-start | bytes 786440 | tf_op jit(solution)/shard_map/ppermute | solution.py:30
  120.5 7.7 %collective-permute-done.12 = bf16[4,8,4096]{2,1,0:T(8,128)(2,1)S(1)} collective-permute-done((bf16[4,8,4096]{2,1,0:T(8,128)(2,1)S(1)}, bf16[4,8,4096]{2,1,0:T(8,128)(2,1)S(1)}, u32[]{:S(2)}, u32[]{:S(2)}) %collective-permute-start.12) | collective-permute-done | bytes 262176 | tf_op jit(solution)/shard_map/ppermute | solution.py:30
  141.9 3.7 %collective-permute-start.22 = (bf16[64,4096]{1,0:T(8,128)(2,1)S(1)}, bf16[64,4096]{1,0:T(8,128)(2,1)S(1)}, u32[]{:S(2)}, u32[]{:S(2)}) collective-permute-start(bf16[64,4096]{1,0:T(8,128)(2,1)S(1)} %fusion.5), channel_id=1, source_target_pairs={{0,32},{1,33},{2,34},{3,35},{4,36},{5,37},{6,38},{7,39},{8,40},{9,... | collective-permute-start | bytes 1572872 | tf_op jit(solution)/shard_map/ppermute | solution.py:30
  148.3 4.0 %collective-permute-start.16 = (bf16[4,8,4096]{2,1,0:T(8,128)(2,1)}, bf16[4,8,4096]{2,1,0:T(8,128)(2,1)S(1)}, u32[]{:S(2)}, u32[]{:S(2)}) collective-permute-start(bf16[4,8,4096]{2,1,0:T(8,128)(2,1)} %get-tuple-element.75), channel_id=1, source_target_pairs={{0,256},{1,257},{2,258},{3,259},{4,260},{5,261},{6,262},{7,263},{8... | collective-permute-start | bytes 786440 | tf_op jit(solution)/shard_map/ppermute | solution.py:30
  159.0 6.8 %all-to-all-start.2 = ((bf16[8,8,4096]{2,1,0:T(8,128)(2,1)}), bf16[8,8,4096]{2,1,0:T(8,128)(2,1)S(1)}, u32[]{:S(2)}, u32[]{:S(2)}) async-start(bf16[8,8,4096]{2,1,0:T(8,128)(2,1)} %fusion.6), calls=%async_computation.2 | async-start | bytes 1048576 | tf_op jit(solution)/shard_map/all_to_all | solution.py:233
  167.1 7.3 %collective-permute-start.19 = (bf16[8,4096]{1,0:T(8,128)(2,1)S(1)}, bf16[8,4096]{1,0:T(8,128)(2,1)S(1)}, u32[]{:S(2)}, u32[]{:S(2)}) collective-permute-start(bf16[8,4096]{1,0:T(8,128)(2,1)S(1)} %get-tuple-element.83), channel_id=1, source_target_pairs={{0,8},{1,9},{2,10},{3,11},{4,12},{5,13},{6,14},{7,15},{8,0},{9,1},... | collective-permute-start | bytes 196616 | tf_op jit(solution)/shard_map/ppermute | solution.py:30
  184.0 4.9 %all-to-all-done.2 = bf16[8,8,4096]{2,1,0:T(8,128)(2,1)S(1)} async-done(((bf16[8,8,4096]{2,1,0:T(8,128)(2,1)}), bf16[8,8,4096]{2,1,0:T(8,128)(2,1)S(1)}, u32[]{:S(2)}, u32[]{:S(2)}) %all-to-all-start.2) | async-done | bytes 524320 | tf_op jit(solution)/shard_map/all_to_all | solution.py:233
  189.6 19.7 %all_to_all.21 = bf16[16,8,2048]{2,1,0:T(8,128)(2,1)S(1)} all-to-all(bf16[16,8,2048]{2,1,0:T(8,128)(2,1)S(1)} %bitcast.210), channel_id=1, replica_groups={{0,32,64,96,128,160,192,224,256,288,320,352,384,416,448,480},{16,48,80,..., dimensions={0} | all-to-all | bytes 1048576 | tf_op jit(solution)/shard_map/all_to_all | solution.py:253
  209.2 3.8 %collective-permute-start.23 = (bf16[16,8,2048]{2,1,0:T(8,128)(2,1)S(1)}, bf16[16,8,2048]{2,1,0:T(8,128)(2,1)S(1)}, u32[]{:S(2)}, u32[]{:S(2)}) collective-permute-start(bf16[16,8,2048]{2,1,0:T(8,128)(2,1)S(1)} %all_to_all.21), channel_id=1, source_target_pairs={{0,16},{1,17},{2,18},{3,19},{4,20},{5,21},{6,22},{7,23},{8,24},{9,... | collective-permute-start | bytes 1572872 | tf_op jit(solution)/shard_map/ppermute | solution.py:30
  220.4 2.8 %collective-permute-start.25 = (f32[256,256]{1,0:T(8,128)S(1)}, f32[256,256]{1,0:T(8,128)S(1)}, u32[]{:S(2)}, u32[]{:S(2)}) collective-permute-start(f32[256,256]{1,0:T(8,128)S(1)} %get-tuple-element.71), channel_id=1, source_target_pairs={{0,384},{1,385},{2,386},{3,387},{4,388},{5,389},{6,390},{7,391},{8... | collective-permute-start | bytes 786440 | tf_op jit(solution)/shard_map/ppermute | solution.py:30
  223.3 3.1 %collective-permute-start.26 = (f32[256,256]{1,0:T(8,128)S(1)}, f32[256,256]{1,0:T(8,128)S(1)}, u32[]{:S(2)}, u32[]{:S(2)}) collective-permute-start(f32[256,256]{1,0:T(8,128)S(1)} %get-tuple-element.72), channel_id=1, source_target_pairs={{0,128},{1,129},{2,130},{3,131},{4,132},{5,133},{6,134},{7,135},{8... | collective-permute-start | bytes 786440 | tf_op jit(solution)/shard_map/ppermute | solution.py:30
  226.4 2.9 %collective-permute-done.24.refs_1_ = f32[256,256]{1,0:T(8,128)S(1)} collective-permute-done((f32[256,256]{1,0:T(8,128)S(1)}, f32[256,256]{1,0:T(8,128)S(1)}, u32[]{:S(2)}, u32[]{:S(2)}) %collective-permute-start.24) | collective-permute-done | bytes 262176 | tf_op jit(solution)/shard_map/ppermute | solution.py:30
  229.3 5.9 %collective-permute-done.25.refs_2_ = f32[256,256]{1,0:T(8,128)S(1)} collective-permute-done((f32[256,256]{1,0:T(8,128)S(1)}, f32[256,256]{1,0:T(8,128)S(1)}, u32[]{:S(2)}, u32[]{:S(2)}) %collective-permute-start.25) | collective-permute-done | bytes 262176 | tf_op jit(solution)/shard_map/ppermute | solution.py:30
  (119 shorter events, 77.0 us)
Async XLA Ops:
  6.5 121.8 %all-gather.5.cloned.1.call-start = ((), (), s32[]{:S(2)}) async-start(), calls=%async_computation.4 | async-start | bytes 1179648 | tf_op jit(solution)/shard_map/all_gather | solution.py:192
  6.5 12.6 %collective-permute-start = (bf16[256,256]{1,0:T(8,128)(2,1)}, bf16[256,256]{1,0:T(8,128)(2,1)S(1)}, u32[]{:S(2)}, u32[]{:S(2)}) collective-permute-start(bf16[256,256]{1,0:T(8,128)(2,1)} %param.8), channel_id=1, source_target_pairs={{0,96},{1,97},{2,98},{3,99},{4,100},{5,101},{6,102},{7,103},{8,104... | collective-permute-start | bytes 393224 | tf_op jit(solution)/shard_map/ppermute | solution.py:30
  15.0 10.9 %collective-permute-start.1 = (bf16[256,256]{1,0:T(8,128)(2,1)}, bf16[256,256]{1,0:T(8,128)(2,1)S(1)}, u32[]{:S(2)}, u32[]{:S(2)}) collective-permute-start(bf16[256,256]{1,0:T(8,128)(2,1)} %param.8), channel_id=1, source_target_pairs={{0,64},{1,65},{2,66},{3,67},{4,68},{5,69},{6,70},{7,71},{8,72},{9,... | collective-permute-start | bytes 393224 | tf_op jit(solution)/shard_map/ppermute | solution.py:30
  26.9 15.3 %collective-permute-start.5 = (bf16[4,256,256]{2,1,0:T(8,128)(2,1)S(1)}, bf16[4,256,256]{2,1,0:T(8,128)(2,1)S(1)}, u32[]{:S(2)}, u32[]{:S(2)}) collective-permute-start(bf16[4,256,256]{2,1,0:T(8,128)(2,1)S(1)} %get-tuple-element.78), channel_id=1, source_target_pairs={{0,256},{1,257},{2,258},{3,259},{4,260},{5,261},{6,262},{7,263},{8... | collective-permute-start | bytes 1572872 | tf_op jit(solution)/shard_map/ppermute | solution.py:30
  32.0 23.7 %collective-permute-start.3 = (bf16[4,256,256]{2,1,0:T(8,128)(2,1)S(1)}, bf16[4,256,256]{2,1,0:T(8,128)(2,1)}, u32[]{:S(2)}, u32[]{:S(2)}) collective-permute-start(bf16[4,256,256]{2,1,0:T(8,128)(2,1)S(1)} %get-tuple-element.78), channel_id=1, source_target_pairs={{0,384},{1,385},{2,386},{3,387},{4,388},{5,389},{6,390},{7,391},{8... | collective-permute-start | bytes 1572872 | tf_op jit(solution)/shard_map/ppermute | solution.py:30
  34.8 20.9 %collective-permute-start.4 = (bf16[4,256,256]{2,1,0:T(8,128)(2,1)S(1)}, bf16[4,256,256]{2,1,0:T(8,128)(2,1)}, u32[]{:S(2)}, u32[]{:S(2)}) collective-permute-start(bf16[4,256,256]{2,1,0:T(8,128)(2,1)S(1)} %get-tuple-element.78), channel_id=1, source_target_pairs={{0,128},{1,129},{2,130},{3,131},{4,132},{5,133},{6,134},{7,135},{8... | collective-permute-start | bytes 1572872 | tf_op jit(solution)/shard_map/ppermute | solution.py:30
  42.3 17.5 %collective-permute-start.7 = (bf16[2,4,256,256]{3,2,1,0:T(8,128)(2,1)S(1)}, bf16[2,4,256,256]{3,2,1,0:T(8,128)(2,1)S(1)}, u32[]{:S(2)}, u32[]{:S(2)}) collective-permute-start(bf16[2,4,256,256]{3,2,1,0:T(8,128)(2,1)S(1)} %pad_maximum_fusion.1), channel_id=1, source_target_pairs={{0,16},{1,17},{2,18},{3,19},{4,20},{5,21},{6,22},{7,23},{8,24},{9,... | collective-permute-start | bytes 3145736 | tf_op jit(solution)/shard_map/ppermute | solution.py:30
  87.2 33.3 %all-to-all-start.1 = ((bf16[8,32,1024]{2,1,0:T(8,128)(2,1)}), bf16[8,32,1024]{2,1,0:T(8,128)(2,1)S(1)}, u32[]{:S(2)}, u32[]{:S(2)}) async-start(bf16[8,32,1024]{2,1,0:T(8,128)(2,1)} %reshape.123), calls=%async_computation.1 | async-start | bytes 1048576 | tf_op jit(solution)/shard_map/all_to_all | solution.py:189
  90.7 118.5 %all-gather.7.cloned.1.call-start = ((), (), s32[]{:S(2)}) async-start(), calls=%async_computation.5 | async-start | bytes 4718592 | tf_op jit(solution)/shard_map/all_gather | solution.py:196
  90.7 18.4 %collective-permute-start.8 = (bf16[8,4096]{1,0:T(8,128)(2,1)S(1)}, bf16[8,4096]{1,0:T(8,128)(2,1)S(1)}, u32[]{:S(2)}, u32[]{:S(2)}) collective-permute-start(bf16[8,4096]{1,0:T(8,128)(2,1)S(1)} %slice_bitcast_fusion.13), channel_id=1, source_target_pairs={{0,8},{1,9},{2,10},{3,11},{4,12},{5,13},{6,14},{7,15},{8,0},{9,1},... | collective-permute-start | bytes 196616 | tf_op jit(solution)/shard_map/ppermute | solution.py:30
  98.7 12.2 %collective-permute-start.9 = (bf16[8,4096]{1,0:T(8,128)(2,1)S(1)}, bf16[8,4096]{1,0:T(8,128)(2,1)S(1)}, u32[]{:S(2)}, u32[]{:S(2)}) collective-permute-start(bf16[8,4096]{1,0:T(8,128)(2,1)S(1)} %slice_bitcast_fusion.13), channel_id=1, source_target_pairs={{0,64},{1,65},{2,66},{3,67},{4,68},{5,69},{6,70},{7,71},{8,72},{9,... | collective-permute-start | bytes 196616 | tf_op jit(solution)/shard_map/ppermute | solution.py:30
  110.9 9.5 %collective-permute-start.11 = (bf16[4,8,4096]{2,1,0:T(8,128)(2,1)S(1)}, bf16[4,8,4096]{2,1,0:T(8,128)(2,1)S(1)}, u32[]{:S(2)}, u32[]{:S(2)}) collective-permute-start(bf16[4,8,4096]{2,1,0:T(8,128)(2,1)S(1)} %get-tuple-element.86), channel_id=1, source_target_pairs={{0,256},{1,257},{2,258},{3,259},{4,260},{5,261},{6,262},{7,263},{8... | collective-permute-start | bytes 786440 | tf_op jit(solution)/shard_map/ppermute | solution.py:30
  113.5 14.7 %collective-permute-start.12 = (bf16[4,8,4096]{2,1,0:T(8,128)(2,1)S(1)}, bf16[4,8,4096]{2,1,0:T(8,128)(2,1)S(1)}, u32[]{:S(2)}, u32[]{:S(2)}) collective-permute-start(bf16[4,8,4096]{2,1,0:T(8,128)(2,1)S(1)} %get-tuple-element.86), channel_id=1, source_target_pairs={{0,384},{1,385},{2,386},{3,387},{4,388},{5,389},{6,390},{7,391},{8... | collective-permute-start | bytes 786440 | tf_op jit(solution)/shard_map/ppermute | solution.py:30
  116.8 11.4 %collective-permute-start.13 = (bf16[4,8,4096]{2,1,0:T(8,128)(2,1)S(1)}, bf16[4,8,4096]{2,1,0:T(8,128)(2,1)S(1)}, u32[]{:S(2)}, u32[]{:S(2)}) collective-permute-start(bf16[4,8,4096]{2,1,0:T(8,128)(2,1)S(1)} %get-tuple-element.86), channel_id=1, source_target_pairs={{0,128},{1,129},{2,130},{3,131},{4,132},{5,133},{6,134},{7,135},{8... | collective-permute-start | bytes 786440 | tf_op jit(solution)/shard_map/ppermute | solution.py:30
  136.3 9.8 %collective-permute-start.15 = (bf16[4,4,8,4096]{3,2,1,0:T(8,128)(2,1)}, bf16[4,4,8,4096]{3,2,1,0:T(8,128)(2,1)}, u32[]{:S(2)}, u32[]{:S(2)}) collective-permute-start(bf16[4,4,8,4096]{3,2,1,0:T(8,128)(2,1)} %bitcast.39), channel_id=1, source_target_pairs={{0,16},{1,17},{2,18},{3,19},{4,20},{5,21},{6,22},{7,23},{8,24},{9,... | collective-permute-start | bytes 3145736 | tf_op jit(solution)/shard_map/ppermute | solution.py:30
  141.9 16.0 %collective-permute-start.22 = (bf16[64,4096]{1,0:T(8,128)(2,1)S(1)}, bf16[64,4096]{1,0:T(8,128)(2,1)S(1)}, u32[]{:S(2)}, u32[]{:S(2)}) collective-permute-start(bf16[64,4096]{1,0:T(8,128)(2,1)S(1)} %fusion.5), channel_id=1, source_target_pairs={{0,32},{1,33},{2,34},{3,35},{4,36},{5,37},{6,38},{7,39},{8,40},{9,... | collective-permute-start | bytes 1572872 | tf_op jit(solution)/shard_map/ppermute | solution.py:30
  148.3 17.5 %collective-permute-start.16 = (bf16[4,8,4096]{2,1,0:T(8,128)(2,1)}, bf16[4,8,4096]{2,1,0:T(8,128)(2,1)S(1)}, u32[]{:S(2)}, u32[]{:S(2)}) collective-permute-start(bf16[4,8,4096]{2,1,0:T(8,128)(2,1)} %get-tuple-element.75), channel_id=1, source_target_pairs={{0,256},{1,257},{2,258},{3,259},{4,260},{5,261},{6,262},{7,263},{8... | collective-permute-start | bytes 786440 | tf_op jit(solution)/shard_map/ppermute | solution.py:30
  152.3 13.6 %collective-permute-start.17 = (bf16[4,8,4096]{2,1,0:T(8,128)(2,1)}, bf16[4,8,4096]{2,1,0:T(8,128)(2,1)}, u32[]{:S(2)}, u32[]{:S(2)}) collective-permute-start(bf16[4,8,4096]{2,1,0:T(8,128)(2,1)} %get-tuple-element.74), channel_id=1, source_target_pairs={{0,384},{1,385},{2,386},{3,387},{4,388},{5,389},{6,390},{7,391},{8... | collective-permute-start | bytes 786440 | tf_op jit(solution)/shard_map/ppermute | solution.py:30
  155.1 10.8 %collective-permute-start.18 = (bf16[4,8,4096]{2,1,0:T(8,128)(2,1)S(1)}, bf16[4,8,4096]{2,1,0:T(8,128)(2,1)}, u32[]{:S(2)}, u32[]{:S(2)}) collective-permute-start(bf16[4,8,4096]{2,1,0:T(8,128)(2,1)S(1)} %get-tuple-element.73), channel_id=1, source_target_pairs={{0,128},{1,129},{2,130},{3,131},{4,132},{5,133},{6,134},{7,135},{8... | collective-permute-start | bytes 786440 | tf_op jit(solution)/shard_map/ppermute | solution.py:30
  159.0 29.9 %all-to-all-start.2 = ((bf16[8,8,4096]{2,1,0:T(8,128)(2,1)}), bf16[8,8,4096]{2,1,0:T(8,128)(2,1)S(1)}, u32[]{:S(2)}, u32[]{:S(2)}) async-start(bf16[8,8,4096]{2,1,0:T(8,128)(2,1)} %fusion.6), calls=%async_computation.2 | async-start | bytes 1048576 | tf_op jit(solution)/shard_map/all_to_all | solution.py:233
  167.1 11.6 %collective-permute-start.19 = (bf16[8,4096]{1,0:T(8,128)(2,1)S(1)}, bf16[8,4096]{1,0:T(8,128)(2,1)S(1)}, u32[]{:S(2)}, u32[]{:S(2)}) collective-permute-start(bf16[8,4096]{1,0:T(8,128)(2,1)S(1)} %get-tuple-element.83), channel_id=1, source_target_pairs={{0,8},{1,9},{2,10},{3,11},{4,12},{5,13},{6,14},{7,15},{8,0},{9,1},... | collective-permute-start | bytes 196616 | tf_op jit(solution)/shard_map/ppermute | solution.py:30
  218.0 11.4 %collective-permute-start.24 = (f32[256,256]{1,0:T(8,128)S(1)}, f32[256,256]{1,0:T(8,128)S(1)}, u32[]{:S(2)}, u32[]{:S(2)}) collective-permute-start(f32[256,256]{1,0:T(8,128)S(1)} %get-tuple-element.70), channel_id=1, source_target_pairs={{0,256},{1,257},{2,258},{3,259},{4,260},{5,261},{6,262},{7,263},{8... | collective-permute-start | bytes 786440 | tf_op jit(solution)/shard_map/ppermute | solution.py:30
  220.4 14.8 %collective-permute-start.25 = (f32[256,256]{1,0:T(8,128)S(1)}, f32[256,256]{1,0:T(8,128)S(1)}, u32[]{:S(2)}, u32[]{:S(2)}) collective-permute-start(f32[256,256]{1,0:T(8,128)S(1)} %get-tuple-element.71), channel_id=1, source_target_pairs={{0,384},{1,385},{2,386},{3,387},{4,388},{5,389},{6,390},{7,391},{8... | collective-permute-start | bytes 786440 | tf_op jit(solution)/shard_map/ppermute | solution.py:30
  223.3 12.0 %collective-permute-start.26 = (f32[256,256]{1,0:T(8,128)S(1)}, f32[256,256]{1,0:T(8,128)S(1)}, u32[]{:S(2)}, u32[]{:S(2)}) collective-permute-start(f32[256,256]{1,0:T(8,128)S(1)} %get-tuple-element.72), channel_id=1, source_target_pairs={{0,128},{1,129},{2,130},{3,131},{4,132},{5,133},{6,134},{7,135},{8... | collective-permute-start | bytes 786440 | tf_op jit(solution)/shard_map/ppermute | solution.py:30
  (17 other events, 170.4 us)
Sparse Core Ops, SparseCore 0:
  87.3 36.1 all-gather.4
  131.1 67.5 all-gather.6
